TPU v7x, 32 devices: a whole 2x2x4 slice. The times are simulated.
32 devices in a mesh: tensor: 4 (over x, core), expert: 4 (over z), dp: 2 (over y).
Axes of the slice: x: 2, y: 2, z: 4, core: 2. Of those that a mesh axis runs over, the one named last changes fastest.
Arguments:
- tokens: bfloat16 [3152, 768], P(('expert', 'dp')), may hold values from -6 to 6
- routes: int32 [3152, 2], P(('expert', 'dp')), may hold values from 0 to 3, all different within a row; in each aligned block of 394 rows (0 to 393, 394 to 787, ...) at most 288 rows name the same one
- images_live: int32 [8], P(('expert', 'dp')), may hold values from 1 to 2, as said below
- ln1_gain: float32 [768], replicated, may hold values from 0.25 to 1.75
- ln1_bias: float32 [768], replicated, may hold values from -1 to 1
- w_qkv: bfloat16 [768, 3, 768], P(None, None, 'tensor'), may hold values from -0.21875 to 0.21875
- w_out: bfloat16 [768, 768], P('tensor'), may hold values from -1.75 to 1.75
- ln2_gain: float32 [768], replicated, may hold values from 0.25 to 1.75
- ln2_bias: float32 [768], replicated, may hold values from -0.5 to 0.5
- w_router: bfloat16 [768, 4], replicated, may hold values from -0.15625 to 0.15625
- w_up: bfloat16 [4, 768, 3072], P('expert', None, 'tensor'), may hold values from -0.21875 to 0.21875
- w_down: bfloat16 [4, 3072, 768], P('expert', 'tensor'), may hold values from -1.25 to 1.25
- cotangent: bfloat16 [3152, 768], P(('expert', 'dp')), may hold values from -6 to 6
Outputs:
- out: bfloat16 [3152, 768], P(('expert', 'dp'))
- grad_tokens: bfloat16 [3152, 768], P(('expert', 'dp'))
- grad_ln1_gain: float32 [768], replicated
- grad_ln1_bias: float32 [768], replicated
- grad_qkv: float32 [768, 3, 768], P(None, None, 'tensor')
- grad_out: float32 [768, 768], P('tensor')
- grad_ln2_gain: float32 [768], replicated
- grad_ln2_bias: float32 [768], replicated
- grad_router: float32 [768, 4], replicated
- grad_up: float32 [4, 768, 3072], P('expert', 'dp', 'tensor')
- grad_down: float32 [4, 3072, 768], P('expert', 'tensor', 'dp')
Inputs may be any that keep to these rules, and one draw needn't show every extreme that they name: `routes`: in each group's 394 rows (aligned blocks) no expert is named by more than 288 rows, a bound that some block reaches. `images_live`: some group holds all 2 images.
All inputs are finite; a program needn't handle non-finite values.
Results may differ from a plain program's by a relative error of at most 0.03.
Values may be sent and summed in bfloat16 or wider, within the bound.
No kernel may reach another device: no remote copies, remote signals or barrier semaphores. Data moves between devices by JAX's collectives and lax.ppermute only.
A program may use at most 128 MiB of HBM per device.

v0:
```python
import functools

import jax
import jax.numpy as jnp
from jax import lax
from jax.experimental import pallas as pl
from jax.experimental.pallas import tpu as pltpu
from jax.sharding import PartitionSpec as P

HEAD_DIM = 64
SEQ = 197
EPSILON = 1e-06
F32 = jnp.float32
BF16 = jnp.bfloat16
LANES = 128
SMALL = 16


def dot_nn(left, right):
    return lax.dot_general(left, right, (((1,), (0,)), ((), ())), preferred_element_type=F32)


def dot_tn(left, right):
    return lax.dot_general(left, right, (((0,), (0,)), ((), ())), preferred_element_type=F32)


def dot_nt(left, right):
    return lax.dot_general(left, right, (((1,), (1,)), ((), ())), preferred_element_type=F32)


def norm_parts(values_in):
    row_mean = jnp.mean(values_in, axis=-1, keepdims=True)
    centred = values_in - row_mean
    variance = jnp.mean(centred * centred, axis=-1, keepdims=True)
    scale = lax.rsqrt(variance + EPSILON)
    return centred * scale, scale


def norm_back(normed, scale, u):
    return scale * (
        u
        - jnp.mean(u, axis=-1, keepdims=True)
        - normed * jnp.mean(u * normed, axis=-1, keepdims=True)
    )


def iota(shape, dim):
    return lax.broadcasted_iota(jnp.int32, shape, dim)


def head_mask(head, width):
    lane = iota((1, width), 1)
    return ((lane >= head * HEAD_DIM) & (lane < (head + 1) * HEAD_DIM)).astype(BF16)


def image_of(shape, dim, images):
    at = iota(shape, dim)
    image = jnp.zeros(shape, jnp.int32)
    for number in range(1, images):
        image = image + (at >= number * SEQ).astype(jnp.int32)
    return image


T_ID, C_ID, E_ID, D_ID, G_ID, L_ID = range(6)


def plan_kernel(experts, ids, routes, cot, router, table, router_pad, *blocks):
    rows = cot.shape[0]
    cap = table.shape[2]
    picks = routes[...]
    lane = iota((rows, LANES), 1)
    named = picks[:, 0:1] == lane
    for k in range(1, picks.shape[1]):
        named = named | (picks[:, k : k + 1] == lane)
    named = named & (iota((rows, LANES), 0) < ids[L_ID])
    marks = jnp.where(named, 1.0, 0.0).astype(BF16)
    earlier = jnp.where(iota((rows, rows), 0) > iota((rows, rows), 1), 1.0, 0.0).astype(BF16)
    slot = dot_nn(earlier, marks)
    first = (ids[C_ID] * cap).astype(F32)
    slot = jnp.where(named, slot - first, -1.0)
    column = iota((rows, cap), 1).astype(F32)
    for x in range(experts):
        table[x] = jnp.where(slot[:, x : x + 1] == column, 1.0, 0.0).astype(BF16)
    for k in range(experts):
        blocks[k][...] = dot_tn(table[ids[E_ID] ^ k], cot[...]).astype(BF16)
    router_pad[...] = jnp.zeros_like(router_pad)
    router_pad[:experts, :] = router[...]


def attend_kernel(images, tokens, gain, bias, weight, normed, query, key, value, probs, head_out):
    rows = tokens.shape[0]
    inner = query.shape[1]
    heads = inner // HEAD_DIM
    unit, _ = norm_parts(tokens[...].astype(F32))
    normed[...] = (unit * gain[...] + bias[...]).astype(BF16)
    query[...] = dot_nt(normed[...], weight[:inner]).astype(BF16)
    key[...] = dot_nt(normed[...], weight[inner : 2 * inner]).astype(BF16)
    value[...] = dot_nt(normed[...], weight[2 * inner :]).astype(BF16)
    same = image_of((rows, 1), 0, images) == image_of((1, rows), 1, images)
    total = jnp.zeros((rows, inner), F32)
    for head in range(heads):
        mask = head_mask(head, inner)
        scores = dot_nt(query[...] * mask, key[...]) * (HEAD_DIM**-0.5)
        scores = jnp.where(same, scores, -1e30)
        top = jnp.max(scores, axis=-1, keepdims=True)
        weights = jnp.exp(scores - top)
        weights = weights * (1.0 / jnp.sum(weights, axis=-1, keepdims=True))
        probs[head] = weights.astype(BF16)
        total = total + dot_nn(probs[head], value[...] * mask)
    head_out[...] = total.astype(BF16)


def middle_kernel(
    n_tensor, experts, ids, tokens, gain, bias, table, *rest
):
    heads = rest[:n_tensor]
    weights = rest[n_tensor : 2 * n_tensor]
    middle = rest[2 * n_tensor]
    blocks = rest[2 * n_tensor + 1 : 2 * n_tensor + 1 + experts]
    held_heads, held_weights, low = rest[2 * n_tensor + 1 + experts :]
    for j in range(n_tensor):
        held_heads[j] = heads[j][...]
        held_weights[j] = weights[j][...]
    total = tokens[...].astype(F32)
    for rank in range(n_tensor):
        place = ids[T_ID] ^ rank
        total = total + dot_nn(held_heads[place], held_weights[place])
    middle[...] = total
    unit, _ = norm_parts(total)
    low[...] = (unit * gain[...] + bias[...]).astype(BF16)
    for k in range(experts):
        blocks[k][...] = dot_tn(table[ids[E_ID] ^ k], low[...]).astype(BF16)


def expert_kernel(
    experts, ids, rows_in, d_out, up_a, up_b, down_a, down_b, router,
    d_back, gated, d_result, hidden_a, hidden_b, d_pre_a, d_pre_b, router_part,
):
    count = rows_in.shape[0]
    lane = iota((count, LANES), 1)
    logits = dot_nt(rows_in[...], router[...])
    logits = jnp.where(lane < experts, logits, -1e30)
    top = jnp.max(logits, axis=-1, keepdims=True)
    odds = jnp.exp(logits - top)
    odds = odds / jnp.sum(odds, axis=-1, keepdims=True)
    mine = (lane == ids[E_ID]).astype(F32)
    gate = jnp.sum(odds * mine, axis=-1, keepdims=True)
    d_out_f = d_out[...].astype(F32)
    d_result[...] = (gate * d_out_f).astype(BF16)
    result = jnp.zeros(d_out.shape, F32)
    back = jnp.zeros(d_out.shape, F32)
    scale = 0.7978845608028654
    for up, down, hidden, d_pre in (
        (up_a, down_a, hidden_a, d_pre_a),
        (up_b, down_b, hidden_b, d_pre_b),
    ):
        act = dot_nn(rows_in[...], up[...])
        square = act * act
        bend = jnp.tanh(scale * act * (1.0 + 0.044715 * square))
        half = 0.5 * (1.0 + bend)
        hidden[...] = (act * half).astype(BF16)
        slope = half + 0.5 * act * (1.0 - bend * bend) * (
            scale * (1.0 + 3 * 0.044715 * square)
        )
        result = result + dot_nn(hidden[...], down[...])
        d_pre[...] = (dot_nt(d_result[...], down[...]) * slope).astype(BF16)
        back = back + dot_nt(d_pre[...], up[...])
    d_gate = jnp.sum(d_out_f * result, axis=-1, keepdims=True)
    d_logits = (d_gate * gate * (mine - odds)).astype(BF16)
    d_back[...] = (back + dot_nn(d_logits, router[...])).astype(BF16)
    gated[...] = (gate * result).astype(BF16)
    router_part[...] = dot_tn(d_logits, rows_in[...])[: router_part.shape[0]]


def weight_grad_kernel(count, *refs):
    rows = refs[:count]
    d_pre_a = refs[count : 2 * count]
    d_pre_b = refs[2 * count : 3 * count]
    hidden_a = refs[3 * count : 4 * count]
    hidden_b = refs[4 * count : 5 * count]
    d_result = refs[5 * count : 6 * count]
    up_a, up_b, down_a, down_b = refs[6 * count :]
    for out, lefts, rights in (
        (up_b, rows, d_pre_b),
        (down_b, hidden_b, d_result),
        (up_a, rows, d_pre_a),
        (down_a, hidden_a, d_result),
    ):
        total = dot_tn(lefts[0][...], rights[0][...])
        for k in range(1, count):
            total = total + dot_tn(lefts[k][...], rights[k][...])
        out[...] = total.astype(BF16)


def combine_kernel(experts, ids, table, *refs):
    blocks = refs[:experts]
    kept, sent, total = refs[experts:]
    value = dot_nn(table[ids[E_ID]], blocks[0][...])
    for k in range(1, experts):
        value = value + dot_nn(table[ids[E_ID] ^ k], blocks[k][...])
    total[...] = value
    half = kept.shape[1]
    kept[...] = total[:, pl.ds(pl.multiple_of(ids[C_ID] * half, LANES), half)].astype(BF16)
    sent[...] = total[:, pl.ds(pl.multiple_of((1 - ids[C_ID]) * half, LANES), half)].astype(BF16)


def joined(ids, own, other, whole):
    half = own.shape[1]
    whole[:, pl.ds(pl.multiple_of(ids[C_ID] * half, LANES), half)] = own[...].astype(F32)
    whole[:, pl.ds(pl.multiple_of((1 - ids[C_ID]) * half, LANES), half)] = other[...].astype(F32)


def back_kernel(
    blocks_n, ids, own, other, middle, cot, gain, w_out, head_out, normed, query, key, value,
    probs, weight, *rest
):
    d_middle, kept, sent, small = rest[:4]
    blocks = rest[4 : 4 + blocks_n]
    whole, grads = rest[4 + blocks_n :]
    rows, inner = query.shape
    heads = inner // HEAD_DIM
    joined(ids, own, other, whole)
    d_normed = whole[...]
    unit, scale = norm_parts(middle[...])
    small[...] = jnp.zeros_like(small)
    small[2:3, :] = jnp.sum(d_normed * unit, axis=0, keepdims=True)
    small[3:4, :] = jnp.sum(d_normed, axis=0, keepdims=True)
    live = iota((rows, 1), 0) < ids[L_ID]
    d_out = jnp.where(live, cot[...].astype(F32), 0.0)
    d_mid = d_out + norm_back(unit, scale, d_normed * gain[...])
    d_middle[...] = d_mid
    d_branch = d_mid.astype(BF16)
    d_head = dot_nt(d_branch, w_out[...]).astype(BF16)
    grads[3 * inner :, :] = dot_tn(head_out[...], d_branch).astype(BF16)
    d_query = jnp.zeros((rows, inner), F32)
    d_key = jnp.zeros((rows, inner), F32)
    d_value = jnp.zeros((rows, inner), F32)
    for head in range(heads):
        mask = head_mask(head, inner)
        chance = probs[head].astype(F32)
        d_probs = dot_nt(d_head, value[...] * mask)
        delta = jnp.sum(d_probs * chance, axis=-1, keepdims=True)
        d_scores = (chance * (d_probs - delta)).astype(BF16)
        d_value = d_value + dot_tn(probs[head], d_head * mask)
        d_query = d_query + dot_nn(d_scores, key[...] * mask)
        d_key = d_key + dot_tn(d_scores, query[...] * mask)
    d_query = (d_query * (HEAD_DIM**-0.5)).astype(BF16)
    d_key = (d_key * (HEAD_DIM**-0.5)).astype(BF16)
    d_value = d_value.astype(BF16)
    grads[:inner, :] = dot_tn(d_query, normed[...]).astype(BF16)
    grads[inner : 2 * inner, :] = dot_tn(d_key, normed[...]).astype(BF16)
    grads[2 * inner : 3 * inner, :] = dot_tn(d_value, normed[...]).astype(BF16)
    if blocks_n == 1:
        blocks[0][...] = grads[...]
    else:
        size = blocks[0].shape[0]
        for m in range(blocks_n):
            at = pl.multiple_of((ids[G_ID] ^ m) * size, 16)
            blocks[m][...] = grads[pl.ds(at, size), :]
    d_in = dot_nn(d_query, weight[:inner])
    d_in = d_in + dot_nn(d_key, weight[inner : 2 * inner])
    whole[...] = d_in + dot_nn(d_value, weight[2 * inner :])
    half = kept.shape[1]
    kept[...] = whole[:, pl.ds(pl.multiple_of(ids[C_ID] * half, LANES), half)].astype(BF16)
    sent[...] = whole[:, pl.ds(pl.multiple_of((1 - ids[C_ID]) * half, LANES), half)].astype(BF16)


def last_norm_kernel(ids, own, other, tokens, d_middle, gain, small2, router, grad_tokens, small, whole):
    joined(ids, own, other, whole)
    d_normed = whole[...]
    unit, scale = norm_parts(tokens[...].astype(F32))
    small[...] = small2[...]
    small[0:1, :] = jnp.sum(d_normed * unit, axis=0, keepdims=True)
    small[1:2, :] = jnp.sum(d_normed, axis=0, keepdims=True)
    small[8 : 8 + router.shape[0], :] = router[...]
    grad_tokens[...] = (
        d_middle[...] + norm_back(unit, scale, d_normed * gain[...])
    ).astype(BF16)


def sum_kernel(count, small, *refs):
    blocks = refs[:count]
    out = refs[count]
    size = blocks[0].shape[0]
    total = blocks[0][...].astype(F32)
    for m in range(1, count):
        total = total + blocks[m][...].astype(F32)
    out[:size, :] = total.astype(BF16)
    out[size:, :] = small[...].astype(BF16)


def spread_kernel(count, ids, *refs):
    parts = refs[:count]
    grad_qkv, grad_out, small, grads, held = refs[count:]
    size = parts[0].shape[0] - SMALL
    for m in range(count):
        group = ids[G_ID] ^ m
        grads[pl.ds(pl.multiple_of(group * size, 16), size), :] = parts[m][:size, :].astype(F32)
        held[group] = parts[m][size:, :].astype(F32)
    total = held[0]
    for group in range(1, count):
        total = total + held[group]
    small[...] = total
    inner = grad_qkv.shape[0]
    grad_qkv[...] = grads[:inner, :]
    grad_out[...] = grads[inner:, :]


def run(kernel, outs, args, scratch=(), micros=1.0):
    smem = pl.BlockSpec(memory_space=pltpu.SMEM)
    vmem = pl.BlockSpec(memory_space=pltpu.VMEM)
    return pl.pallas_call(
        kernel,
        out_shape=[jax.ShapeDtypeStruct(shape, kind) for shape, kind in outs],
        in_specs=[smem if arg.dtype == jnp.int32 and arg.ndim == 1 else vmem for arg in args],
        out_specs=[vmem] * len(outs),
        scratch_shapes=[pltpu.VMEM(shape, kind) for shape, kind in scratch],
        compiler_params=pltpu.CompilerParams(vmem_limit_bytes=40 * 1024 * 1024),
        cost_estimate=pl.CostEstimate(
            flops=int(micros * 1.15e9), bytes_accessed=1024, transcendentals=0
        ),
    )(*args)


def make_body(n_tensor, n_expert, n_dp):
    groups = n_expert * n_dp
    small_slice = n_expert <= 8

    def tensor_swap(value, mask):
        return lax.ppermute(value, "tensor", [(i, i ^ mask) for i in range(n_tensor)])

    def expert_swap(value, mask):
        return lax.ppermute(value, "expert", [(i, i ^ mask) for i in range(n_expert)])

    def dp_swap(value):
        return lax.ppermute(value, "dp", [(i, i ^ 1) for i in range(n_dp)])

    def group_swap(value, mask):
        pairs = [(i, i ^ mask) for i in range(groups)]
        return lax.ppermute(value, ("expert", "dp"), pairs)

    def exchange(blocks):
        if small_slice:
            return [blocks[0]] + [expert_swap(blocks[k], k) for k in range(1, n_expert)]
        order = jnp.arange(n_expert) ^ lax.axis_index("expert")
        stacked = lax.all_to_all(
            jnp.stack(blocks)[order], "expert", split_axis=0, concat_axis=0, tiled=True
        )[order]
        return [stacked[k] for k in range(n_expert)]

    def tensor_sum(kept, sent):
        chip = (kept.astype(F32) + tensor_swap(sent, 1).astype(F32)).astype(BF16)
        own = (chip.astype(F32) + tensor_swap(chip, 2).astype(F32)).astype(BF16)
        return own, tensor_swap(own, 1)

    def body(
        tokens,
        routes,
        images_live,
        ln1_gain,
        ln1_bias,
        w_qkv,
        w_out,
        ln2_gain,
        ln2_bias,
        w_router,
        w_up,
        w_down,
        cotangent,
    ):
        rows, width = tokens.shape
        inner = w_qkv.shape[2]
        heads = inner // HEAD_DIM
        experts = w_router.shape[1]
        capacity = max(2, 3 * rows // experts // 8 * 8)
        cap = capacity // 2
        images = rows // SEQ
        half = width // 2
        rank = lax.axis_index("tensor")
        owner = lax.axis_index("expert")
        copy = lax.axis_index("dp")
        ids = jnp.stack(
            [
                rank,
                rank % 2,
                owner,
                copy,
                owner * n_dp + copy,
                jnp.minimum(images_live[0] * SEQ, rows),
                rank,
                rank,
            ]
        ).astype(jnp.int32)
        gain1, bias1 = ln1_gain.reshape(1, width), ln1_bias.reshape(1, width)
        gain2, bias2 = ln2_gain.reshape(1, width), ln2_bias.reshape(1, width)
        weight = w_qkv.transpose(1, 2, 0).reshape(3 * inner, width)
        up_a, down_a = w_up[0], w_down[0]

        table, router, *cot_blocks = run(
            functools.partial(plan_kernel, experts),
            [((experts, rows, cap), BF16), ((LANES, width), BF16)]
            + [((cap, width), BF16)] * experts,
            [ids, routes, cotangent, w_router.T],
            micros=3,
        )
        outs = [w_out] + [tensor_swap(w_out, mask) for mask in range(1, n_tensor)]
        d_rows_in = exchange(cot_blocks)
        up_b, down_b = tensor_swap(up_a, 1), tensor_swap(down_a, 1)

        normed, query, key, value, probs, head_out = run(
            functools.partial(attend_kernel, images),
            [((rows, width), BF16)]
            + [((rows, inner), BF16)] * 3
            + [((heads, rows, rows), BF16), ((rows, inner), BF16)],
            [tokens, gain1, bias1, weight],
            micros=8,
        )
        heads_all = [head_out] + [tensor_swap(head_out, mask) for mask in range(1, n_tensor)]
        middle, *row_blocks = run(
            functools.partial(middle_kernel, n_tensor, experts),
            [((rows, width), F32)] + [((cap, width), BF16)] * experts,
            [ids, tokens, gain2, bias2, table] + heads_all + outs,
            scratch=[
                ((n_tensor, rows, inner), BF16),
                ((n_tensor, inner, width), BF16),
                ((rows, width), BF16),
            ],
            micros=4,
        )
        rows_in = exchange(row_blocks)
        if not small_slice:
            rows_in = [jnp.concatenate(rows_in, axis=0)]
            d_rows_in = [jnp.concatenate(d_rows_in, axis=0)]
        part_rows = max(8, -(-experts // 8) * 8)

        worked = []
        for at in range(len(rows_in)):
            count = rows_in[at].shape[0]
            worked.append(
                run(
                    functools.partial(expert_kernel, experts),
                    [((count, width), BF16)] * 3
                    + [((count, up_a.shape[1]), BF16)] * 4
                    + [((part_rows, width), F32)],
                    [ids, rows_in[at], d_rows_in[at], up_a, up_b, down_a, down_b, router],
                    micros=4,
                )
            )
        d_back = [one[0] for one in worked]
        gated = [one[1] for one in worked]
        if not small_slice:
            d_back = list(d_back[0].reshape(experts, cap, width))
            gated = list(gated[0].reshape(experts, cap, width))

        def collect(blocks):
            kept, sent = run(
                functools.partial(combine_kernel, experts),
                [((rows, half), BF16)] * 2,
                [ids, table] + blocks,
                scratch=[((rows, width), F32)],
                micros=2,
            )
            return tensor_sum(kept, sent)

        d_home = exchange(d_back)
        own, other = collect(d_home)

        parts = groups if small_slice else 1
        d_middle, kept1, sent1, small2, *grad_blocks = run(
            functools.partial(back_kernel, parts),
            [((rows, width), F32)]
            + [((rows, half), BF16)] * 2
            + [((SMALL, width), F32)]
            + [((4 * inner // parts, width), BF16)] * parts,
            [
                ids, own, other, middle, cotangent, gain2, w_out, head_out, normed, query, key,
                value, probs, weight,
            ],
            scratch=[((rows, width), F32), ((4 * inner, width), BF16)],
            micros=8,
        )

        router_part = worked[0][7]
        for one in worked[1:]:
            router_part = router_part + one[7]
        router_part = router_part + tensor_swap(router_part, 1)
        router_part = router_part + tensor_swap(router_part, 2)

        count = len(worked)
        fields = [[one[at] for one in worked] for at in (5, 6, 3, 4, 2)]
        up_own, up_pair, down_own, down_pair = run(
            functools.partial(weight_grad_kernel, count),
            [((width, up_a.shape[1]), BF16)] * 2 + [((up_a.shape[1], width), BF16)] * 2,
            rows_in + [one for field in fields for one in field],
            micros=8,
        )
        up_sum = up_own.astype(F32) + tensor_swap(up_pair, 1).astype(F32)
        down_sum = down_own.astype(F32) + tensor_swap(down_pair, 1).astype(F32)
        cut = width // 2
        up_kept = jnp.where(copy == 0, up_sum[:cut], up_sum[cut:])
        up_sent = jnp.where(copy == 0, up_sum[cut:], up_sum[:cut]).astype(BF16)
        down_kept = jnp.where(copy == 0, down_sum[:, :cut], down_sum[:, cut:])
        down_sent = jnp.where(copy == 0, down_sum[:, cut:], down_sum[:, :cut]).astype(BF16)
        grad_up = (up_kept + dp_swap(up_sent).astype(F32))[None]
        grad_down = (down_kept + dp_swap(down_sent).astype(F32))[None]

        gated, d_home = lax.optimization_barrier((gated, d_home))
        mix_own, mix_other = collect(exchange(gated))
        mixture = jnp.where(
            rank % 2 == 0,
            jnp.concatenate([mix_own, mix_other], axis=1),
            jnp.concatenate([mix_other, mix_own], axis=1),
        ).astype(F32)
        alive = (jnp.arange(rows, dtype=jnp.int32) < images_live[0] * SEQ)[:, None]
        out = jnp.where(alive, middle + mixture, 0.0).astype(BF16)

        own1, other1 = tensor_sum(kept1, sent1)
        grad_tokens, small = run(
            last_norm_kernel,
            [((rows, width), BF16), ((SMALL, width), F32)]
            if small_slice
            else [((rows, width), BF16), ((8 + part_rows, width), F32)],
            [ids, own1, other1, tokens, d_middle, gain1, small2, router_part]
            if small_slice
            else [
                ids, own1, other1, tokens, d_middle, gain1,
                jnp.zeros((8 + part_rows, width), F32).at[:SMALL].set(small2), router_part,
            ],
            scratch=[((rows, width), F32)],
            micros=3,
        )
        if small_slice:
            arrived = [grad_blocks[0]] + [
                group_swap(grad_blocks[m], m) for m in range(1, groups)
            ]
            size = grad_blocks[0].shape[0]
            (ready,) = run(
                functools.partial(sum_kernel, groups),
                [((size + SMALL, width), BF16)],
                [small] + arrived,
                micros=1,
            )
            everything = [ready] + [group_swap(ready, m) for m in range(1, groups)]
            grad_qkv, grad_out, small_sum = run(
                functools.partial(spread_kernel, groups),
                [((3 * inner, width), F32), ((inner, width), F32), ((SMALL, width), F32)],
                [ids] + everything,
                scratch=[((4 * inner, width), F32), ((groups, SMALL, width), F32)],
                micros=3,
            )
        else:
            grads = lax.psum(grad_blocks[0], ("expert", "dp")).astype(F32)
            grad_qkv, grad_out = grads[: 3 * inner], grads[3 * inner :]
            small_sum = lax.psum(small, ("expert", "dp"))
        return (
            out,
            grad_tokens,
            small_sum[0],
            small_sum[1],
            grad_qkv.reshape(3, inner, width).transpose(2, 0, 1),
            grad_out,
            small_sum[2],
            small_sum[3],
            small_sum[8 : 8 + experts].T,
            grad_up,
            grad_down,
        )

    return body


def solution(mesh):
    in_specs = (
        P(("expert", "dp"), None),
        P(("expert", "dp"), None),
        P(("expert", "dp")),
        P(),
        P(),
        P(None, None, "tensor"),
        P("tensor", None),
        P(),
        P(),
        P(),
        P("expert", None, "tensor"),
        P("expert", "tensor", None),
        P(("expert", "dp"), None),
    )
    out_specs = (
        P(("expert", "dp"), None),
        P(("expert", "dp"), None),
        P(),
        P(),
        P(None, None, "tensor"),
        P("tensor", None),
        P(),
        P(),
        P(),
        P("expert", "dp", "tensor"),
        P("expert", "tensor", "dp"),
    )
    body = make_body(mesh.shape["tensor"], mesh.shape["expert"], mesh.shape["dp"])
    return jax.shard_map(body, mesh=mesh, in_specs=in_specs, out_specs=out_specs, check_vma=False)
```

profile of v0, /device:TPU:0, one launch (start us, length us, event | category | flops | bytes accessed | tf_op | source)
XLA Modules:
  0.0 237.9 jit_solution(3828244096740692063)
XLA Ops:
  2.6 1.2 copy-done.5
  3.8 1.1 copy-done.8
  4.9 2.5 %shard_map.213 = (bf16[394,768]{1,0:T(8,128)(2,1)S(1)}, bf16[394,192]{1,0:T(8,128)(2,1)S(1)}, bf16[394,192]{1,0:T(8,128)(2,1)S(1)}, bf16[394,192]{1,0:T(8,128)(2...) custom-call(bf16[394,768]{1,0:T(8,128)(2,1)S(1)} %copy-done.8, f32[1,768]{1,0:T(1,128)S(1)} %reshape.48.gain, ...), custom_call_target="tpu_custom_call" | custom-call | flops 9200000000 | bytes 1024 | tf_op jit(solution)/shard_map/pallas_call | solution.py:312
  10.6 2.6 %collective-permute-start.2 = (bf16[394,192]{1,0:T(8,128)(2,1)S(1)}, bf16[394,192]{1,0:T(8,128)(2,1)S(1)}, u32[]{:S(2)}, u32[]{:S(2)}) collective-permute-start(bf16[394,192]{1,0:T(8,128)(2,1)S(1)} %get-tuple-element.90.rest_0_.head_out), channel_id=1, source_target_pairs={{0,24},{8,16},{16,8},{24,0},{1,25},{9,17},{17,9},{25,1},{2,26},{10... | collective-permute-start | bytes 453896 | tf_op jit(solution)/shard_map/ppermute | solution.py:330
  14.6 4.1 %collective-permute-done.2.rest_3_ = bf16[394,192]{1,0:T(8,128)(2,1)S(1)} collective-permute-done((bf16[394,192]{1,0:T(8,128)(2,1)S(1)}, bf16[394,192]{1,0:T(8,128)(2,1)S(1)}, u32[]{:S(2)}, u32[]{:S(2)}) %collective-permute-start.2) | collective-permute-done | bytes 151328 | tf_op jit(solution)/shard_map/ppermute | solution.py:330
  18.7 1.9 collective-permute-start.5
  20.6 3.2 %collective-permute-done.1.rest_2_ = bf16[394,192]{1,0:T(8,128)(2,1)S(1)} collective-permute-done((bf16[394,192]{1,0:T(8,128)(2,1)S(1)}, bf16[394,192]{1,0:T(8,128)(2,1)S(1)}, u32[]{:S(2)}, u32[]{:S(2)}) %collective-permute-start.1) | collective-permute-done | bytes 151328 | tf_op jit(solution)/shard_map/ppermute | solution.py:330
  23.8 1.8 collective-permute-start.4
  25.6 2.0 shard_map.212
  27.6 1.8 collective-permute-done.5.rest_7_
  29.4 4.1 %collective-permute-start.13 = (bf16[144,768]{1,0:T(8,128)(2,1)S(1)}, bf16[144,768]{1,0:T(8,128)(2,1)S(1)}, u32[]{:S(2)}, u32[]{:S(2)}) collective-permute-start(bf16[144,768]{1,0:T(8,128)(2,1)S(1)} %get-tuple-element.103), channel_id=1, source_target_pairs={{0,6},{2,4},{4,2},{6,0},{1,7},{3,5},{5,3},{7,1},{8,14},{10,12},{12... | collective-permute-start | bytes 663560 | tf_op jit(solution)/shard_map/ppermute | solution.py:333
  33.5 2.4 %collective-permute-done.4.rest_6_ = bf16[192,768]{1,0:T(8,128)(2,1)S(1)} collective-permute-done((bf16[192,768]{1,0:T(8,128)(2,1)S(1)}, bf16[192,768]{1,0:T(8,128)(2,1)S(1)}, u32[]{:S(2)}, u32[]{:S(2)}) %collective-permute-start.4) | collective-permute-done | bytes 294944 | tf_op jit(solution)/shard_map/ppermute | solution.py:330
  35.9 2.7 %shard_map.214 = (f32[394,768]{1,0:T(8,128)S(1)}, bf16[144,768]{1,0:T(8,128)(2,1)S(1)}, bf16[144,768]{1,0:T(8,128)(2,1)S(1)}, bf16[144,768]{1,0:T(8,128)(2,1)S(1)}, bf16[144,768]{1,0:T(8,128)(2,1)S(1)}) custom-call(s32[8]{0:T(128)S(1)} %stack.29.ids, bf16[394,768]{1,0:T(8,128)(2,1)S(1)} %copy-done.9, f32[1,768]{1,0:T(1,128)S(1)} %reshape.46.gain, ...), custom_call_target="tpu_custom_call" | custom-call | flops 4600000000 | bytes 1024 | tf_op jit(solution)/shard_map/pallas_call | solution.py:312
  38.7 4.2 %collective-permute-start.12 = (bf16[144,768]{1,0:T(8,128)(2,1)S(1)}, bf16[144,768]{1,0:T(8,128)(2,1)S(1)}, u32[]{:S(2)}, u32[]{:S(2)}) collective-permute-start(bf16[144,768]{1,0:T(8,128)(2,1)S(1)} %get-tuple-element.102), channel_id=1, source_target_pairs={{0,6},{2,4},{4,2},{6,0},{1,7},{3,5},{5,3},{7,1},{8,14},{10,12},{12... | collective-permute-start | bytes 663560 | tf_op jit(solution)/shard_map/ppermute | solution.py:333
  42.9 2.5 %collective-permute-start.11 = (bf16[144,768]{1,0:T(8,128)(2,1)S(1)}, bf16[144,768]{1,0:T(8,128)(2,1)S(1)}, u32[]{:S(2)}, u32[]{:S(2)}) collective-permute-start(bf16[144,768]{1,0:T(8,128)(2,1)S(1)} %get-tuple-element.100), channel_id=1, source_target_pairs={{0,4},{2,6},{4,0},{6,2},{1,5},{3,7},{5,1},{7,3},{8,12},{10,14},{12... | collective-permute-start | bytes 663560 | tf_op jit(solution)/shard_map/ppermute | solution.py:333
  45.4 3.8 %collective-permute-done.12.rows_in.refs_3_ = bf16[144,768]{1,0:T(8,128)(2,1)S(1)} collective-permute-done((bf16[144,768]{1,0:T(8,128)(2,1)S(1)}, bf16[144,768]{1,0:T(8,128)(2,1)S(1)}, u32[]{:S(2)}, u32[]{:S(2)}) %collective-permute-start.12) | collective-permute-done | bytes 221216 | tf_op jit(solution)/shard_map/ppermute | solution.py:333
  49.2 8.8 %collective-permute-start.8 = (bf16[144,768]{1,0:T(8,128)(2,1)S(1)}, bf16[144,768]{1,0:T(8,128)(2,1)S(1)}, u32[]{:S(2)}, u32[]{:S(2)}) collective-permute-start(bf16[144,768]{1,0:T(8,128)(2,1)S(1)} %get-tuple-element.96), channel_id=1, source_target_pairs={{0,2},{2,0},{4,6},{6,4},{1,3},{3,1},{5,7},{7,5},{8,10},{10,8},{12,... | collective-permute-start | bytes 663560 | tf_op jit(solution)/shard_map/ppermute | solution.py:333
  58.0 4.7 %shard_map.218 = (bf16[144,768]{1,0:T(8,128)(2,1)S(1)}, bf16[144,768]{1,0:T(8,128)(2,1)S(1)}, bf16[144,768]{1,0:T(8,128)(2,1)S(1)}, bf16[144,768]{1,0:T(8,128)(2...) custom-call(s32[8]{0:T(128)S(1)} %stack.29.ids, ...), custom_call_target="tpu_custom_call" | custom-call | flops 4600000000 | bytes 1024 | tf_op jit(solution)/shard_map/pallas_call | solution.py:312
  62.7 2.4 %collective-permute-start.16 = (bf16[144,768]{1,0:T(8,128)(2,1)S(1)}, bf16[144,768]{1,0:T(8,128)(2,1)S(1)}, u32[]{:S(2)}, u32[]{:S(2)}) collective-permute-start(bf16[144,768]{1,0:T(8,128)(2,1)S(1)} %get-tuple-element.108), channel_id=1, source_target_pairs={{0,6},{2,4},{4,2},{6,0},{1,7},{3,5},{5,3},{7,1},{8,14},{10,12},{12... | collective-permute-start | bytes 663560 | tf_op jit(solution)/shard_map/ppermute | solution.py:333
  65.1 7.2 %collective-permute-done.11.d_out = bf16[144,768]{1,0:T(8,128)(2,1)S(1)} collective-permute-done((bf16[144,768]{1,0:T(8,128)(2,1)S(1)}, bf16[144,768]{1,0:T(8,128)(2,1)S(1)}, u32[]{:S(2)}, u32[]{:S(2)}) %collective-permute-start.11) | collective-permute-done | bytes 221216 | tf_op jit(solution)/shard_map/ppermute | solution.py:333
  72.3 4.7 %collective-permute-done.10.rows_in.refs_2_ = bf16[144,768]{1,0:T(8,128)(2,1)S(1)} collective-permute-done((bf16[144,768]{1,0:T(8,128)(2,1)S(1)}, bf16[144,768]{1,0:T(8,128)(2,1)S(1)}, u32[]{:S(2)}, u32[]{:S(2)}) %collective-permute-start.10) | collective-permute-done | bytes 221216 | tf_op jit(solution)/shard_map/ppermute | solution.py:333
  77.1 4.7 %shard_map.217 = (bf16[144,768]{1,0:T(8,128)(2,1)S(1)}, bf16[144,768]{1,0:T(8,128)(2,1)S(1)}, bf16[144,768]{1,0:T(8,128)(2,1)S(1)}, bf16[144,768]{1,0:T(8,128)(2...) custom-call(s32[8]{0:T(128)S(1)} %stack.29.ids, ...), custom_call_target="tpu_custom_call" | custom-call | flops 4600000000 | bytes 1024 | tf_op jit(solution)/shard_map/pallas_call | solution.py:312
  81.9 4.9 %shard_map.216 = (bf16[144,768]{1,0:T(8,128)(2,1)S(1)}, bf16[144,768]{1,0:T(8,128)(2,1)S(1)}, bf16[144,768]{1,0:T(8,128)(2,1)S(1)}, bf16[144,768]{1,0:T(8,128)(2...) custom-call(s32[8]{0:T(128)S(1)} %stack.29.ids, ...), custom_call_target="tpu_custom_call" | custom-call | flops 4600000000 | bytes 1024 | tf_op jit(solution)/shard_map/pallas_call | solution.py:312
  86.7 3.1 %collective-permute-start.14 = (bf16[144,768]{1,0:T(8,128)(2,1)S(1)}, bf16[144,768]{1,0:T(8,128)(2,1)S(1)}, u32[]{:S(2)}, u32[]{:S(2)}) collective-permute-start(bf16[144,768]{1,0:T(8,128)(2,1)S(1)} %get-tuple-element.106), channel_id=1, source_target_pairs={{0,2},{2,0},{4,6},{6,4},{1,3},{3,1},{5,7},{7,5},{8,10},{10,8},{12,... | collective-permute-start | bytes 663560 | tf_op jit(solution)/shard_map/ppermute | solution.py:333
  89.8 4.7 %shard_map.215 = (bf16[144,768]{1,0:T(8,128)(2,1)S(1)}, bf16[144,768]{1,0:T(8,128)(2,1)S(1)}, bf16[144,768]{1,0:T(8,128)(2,1)S(1)}, bf16[144,768]{1,0:T(8,128)(2...) custom-call(s32[8]{0:T(128)S(1)} %stack.29.ids, ...), custom_call_target="tpu_custom_call" | custom-call | flops 4600000000 | bytes 1024 | tf_op jit(solution)/shard_map/pallas_call | solution.py:312
  94.5 3.8 %collective-permute-done.14.refs_1_ = bf16[144,768]{1,0:T(8,128)(2,1)S(1)} collective-permute-done((bf16[144,768]{1,0:T(8,128)(2,1)S(1)}, bf16[144,768]{1,0:T(8,128)(2,1)S(1)}, u32[]{:S(2)}, u32[]{:S(2)}) %collective-permute-start.14) | collective-permute-done | bytes 221216 | tf_op jit(solution)/shard_map/ppermute | solution.py:333
  98.4 1.9 collective-permute-start.18
  100.3 2.5 %collective-permute-start.19 = (bf16[144,768]{1,0:T(8,128)(2,1)S(1)}, bf16[144,768]{1,0:T(8,128)(2,1)S(1)}, u32[]{:S(2)}, u32[]{:S(2)}) collective-permute-start(bf16[144,768]{1,0:T(8,128)(2,1)S(1)} %get-tuple-element.112), channel_id=1, source_target_pairs={{0,6},{2,4},{4,2},{6,0},{1,7},{3,5},{5,3},{7,1},{8,14},{10,12},{12... | collective-permute-start | bytes 663560 | tf_op jit(solution)/shard_map/ppermute | solution.py:333
  102.7 1.4 shard_map.220
  104.8 4.4 %collective-permute-done.17.refs_1_ = bf16[144,768]{1,0:T(8,128)(2,1)S(1)} collective-permute-done((bf16[144,768]{1,0:T(8,128)(2,1)S(1)}, bf16[144,768]{1,0:T(8,128)(2,1)S(1)}, u32[]{:S(2)}, u32[]{:S(2)}) %collective-permute-start.17) | collective-permute-done | bytes 221216 | tf_op jit(solution)/shard_map/ppermute | solution.py:333
  109.2 7.9 %collective-permute-done.18.refs_2_ = bf16[144,768]{1,0:T(8,128)(2,1)S(1)} collective-permute-done((bf16[144,768]{1,0:T(8,128)(2,1)S(1)}, bf16[144,768]{1,0:T(8,128)(2,1)S(1)}, u32[]{:S(2)}, u32[]{:S(2)}) %collective-permute-start.18) | collective-permute-done | bytes 221216 | tf_op jit(solution)/shard_map/ppermute | solution.py:333
  117.1 1.4 shard_map.219
  118.7 1.6 collective-permute-start.24
  120.2 5.6 %shard_map.225 = (bf16[768,768]{1,0:T(8,128)(2,1)S(1)}, bf16[768,768]{1,0:T(8,128)(2,1)}, bf16[768,768]{1,0:T(8,128)(2,1)S(1)}, bf16[768,768]{1,0:T(8,128)(2,1)S(1)}) custom-call(bf16[144,768]{1,0:T(8,128)(2,1)S(1)} %get-tuple-element.92.rows_in.refs_0_, bf16[144,768]{1,0:T(8,128)(2,1)S(1)} %collective-permute-done.8.rows_in.refs_1_, ...), custom_call_target="tpu_custom_call" | custom-call | flops 9200000000 | bytes 1024 | tf_op jit(solution)/shard_map/pallas_call | solution.py:312
  130.0 1.5 collective-permute-start.21
  133.6 5.9 %collective-permute-done.21 = bf16[394,384]{1,0:T(8,128)(2,1)} collective-permute-done((bf16[394,384]{1,0:T(8,128)(2,1)}, bf16[394,384]{1,0:T(8,128)(2,1)}, u32[]{:S(2)}, u32[]{:S(2)}) %collective-permute-start.21) | collective-permute-done | bytes 302624 | tf_op jit(solution)/shard_map/ppermute | solution.py:330
  139.5 1.1 add_convert_fusion.4
  140.8 1.2 copy-done.6
  142.9 1.3 copy-done.15
  144.2 1.1 copy-done.17
  148.0 5.4 %shard_map.221 = (f32[394,768]{1,0:T(8,128)S(1)}, bf16[394,384]{1,0:T(8,128)(2,1)S(1)}, bf16[394,384]{1,0:T(8,128)(2,1)S(1)}, f32[16,768]{1,0:T(8,128)S(1)}, bf1...) custom-call(s32[8]{0:T(128)S(1)} %stack.29.ids, ...), custom_call_target="tpu_custom_call" | custom-call | flops 9200000000 | bytes 1024 | tf_op jit(solution)/shard_map/pallas_call | solution.py:312
  153.5 1.6 collective-permute-start.31
  155.1 4.4 %collective-permute-start.32 = (bf16[96,768]{1,0:T(8,128)(2,1)S(1)}, bf16[96,768]{1,0:T(8,128)(2,1)S(1)}, u32[]{:S(2)}, u32[]{:S(2)}) collective-permute-start(bf16[96,768]{1,0:T(8,128)(2,1)S(1)} %get-tuple-element.134), channel_id=1, source_target_pairs={{0,2},{1,3},{2,0},{3,1},{4,6},{5,7},{6,4},{7,5},{8,10},{9,11},{10,... | collective-permute-start | bytes 442376 | tf_op jit(solution)/shard_map/ppermute | solution.py:340
  159.4 1.5 convert_add_fusion.1
  161.3 1.6 collective-permute-start.27
  163.2 7.7 %collective-permute-done.27 = bf16[394,384]{1,0:T(8,128)(2,1)S(1)} collective-permute-done((bf16[394,384]{1,0:T(8,128)(2,1)S(1)}, bf16[394,384]{1,0:T(8,128)(2,1)S(1)}, u32[]{:S(2)}, u32[]{:S(2)}) %collective-permute-start.27) | collective-permute-done | bytes 302624 | tf_op jit(solution)/shard_map/ppermute | solution.py:330
  171.2 1.7 collective-permute-start.34
  172.9 1.5 collective-permute-start.46
  175.5 1.2 collective-permute-start.35
  176.7 1.5 collective-permute-start.36
  178.2 10.1 %collective-permute-done.34.refs_4_ = bf16[96,768]{1,0:T(8,128)(2,1)S(1)} collective-permute-done((bf16[96,768]{1,0:T(8,128)(2,1)S(1)}, bf16[96,768]{1,0:T(8,128)(2,1)S(1)}, u32[]{:S(2)}, u32[]{:S(2)}) %collective-permute-start.34) | collective-permute-done | bytes 147488 | tf_op jit(solution)/shard_map/ppermute | solution.py:340
  188.3 2.1 collective-permute-start.37
  191.2 2.3 shard_map.222
  193.6 2.7 %collective-permute-done.37.refs_7_ = bf16[96,768]{1,0:T(8,128)(2,1)S(1)} collective-permute-done((bf16[96,768]{1,0:T(8,128)(2,1)S(1)}, bf16[96,768]{1,0:T(8,128)(2,1)S(1)}, u32[]{:S(2)}, u32[]{:S(2)}) %collective-permute-start.37) | collective-permute-done | bytes 147488 | tf_op jit(solution)/shard_map/ppermute | solution.py:340
  196.4 2.6 %collective-permute-start.44 = (bf16[112,768]{1,0:T(8,128)(2,1)S(1)}, bf16[112,768]{1,0:T(8,128)(2,1)S(1)}, u32[]{:S(2)}, u32[]{:S(2)}) collective-permute-start(bf16[112,768]{1,0:T(8,128)(2,1)S(1)} %shard_map.223.refs_0_), channel_id=1, source_target_pairs={{0,7},{1,6},{2,5},{3,4},{4,3},{5,2},{6,1},{7,0},{8,15},{9,14},{10,... | collective-permute-start | bytes 516104 | tf_op jit(solution)/shard_map/ppermute | solution.py:340
  199.0 1.9 collective-permute-start.43
  200.9 1.2 add_bitcast_fusion.1
  202.1 11.7 %collective-permute-start.42 = (bf16[112,768]{1,0:T(8,128)(2,1)S(1)}, bf16[112,768]{1,0:T(8,128)(2,1)S(1)}, u32[]{:S(2)}, u32[]{:S(2)}) collective-permute-start(bf16[112,768]{1,0:T(8,128)(2,1)S(1)} %shard_map.223.refs_0_), channel_id=1, source_target_pairs={{0,5},{1,4},{2,7},{3,6},{4,1},{5,0},{6,3},{7,2},{8,13},{9,12},{10,... | collective-permute-start | bytes 516104 | tf_op jit(solution)/shard_map/ppermute | solution.py:340
  213.8 2.9 %collective-permute-start.40 = (bf16[112,768]{1,0:T(8,128)(2,1)S(1)}, bf16[112,768]{1,0:T(8,128)(2,1)S(1)}, u32[]{:S(2)}, u32[]{:S(2)}) collective-permute-start(bf16[112,768]{1,0:T(8,128)(2,1)S(1)} %shard_map.223.refs_0_), channel_id=1, source_target_pairs={{0,3},{1,2},{2,1},{3,0},{4,7},{5,6},{6,5},{7,4},{8,11},{9,10},{10,... | collective-permute-start | bytes 516104 | tf_op jit(solution)/shard_map/ppermute | solution.py:340
  216.7 7.3 %collective-permute-start.39 = (bf16[112,768]{1,0:T(8,128)(2,1)S(1)}, bf16[112,768]{1,0:T(8,128)(2,1)S(1)}, u32[]{:S(2)}, u32[]{:S(2)}) collective-permute-start(bf16[112,768]{1,0:T(8,128)(2,1)S(1)} %shard_map.223.refs_0_), channel_id=1, source_target_pairs={{0,2},{1,3},{2,0},{3,1},{4,6},{5,7},{6,4},{7,5},{8,10},{9,11},{10,... | collective-permute-start | bytes 516104 | tf_op jit(solution)/shard_map/ppermute | solution.py:340
  224.6 1.2 add_bitcast_fusion
  225.8 6.0 %collective-permute-done.42.refs_5_ = bf16[112,768]{1,0:T(8,128)(2,1)S(1)} collective-permute-done((bf16[112,768]{1,0:T(8,128)(2,1)S(1)}, bf16[112,768]{1,0:T(8,128)(2,1)S(1)}, u32[]{:S(2)}, u32[]{:S(2)}) %collective-permute-start.42) | collective-permute-done | bytes 172064 | tf_op jit(solution)/shard_map/ppermute | solution.py:340
  231.8 1.8 collective-permute-done.41.refs_4_
  234.4 2.3 shard_map.224
  (127 shorter events, 22.4 us)
Async XLA Ops:
  0.6 57.4 %collective-permute-start.6 = (bf16[768,768]{1,0:T(8,128)(2,1)}, bf16[768,768]{1,0:T(8,128)(2,1)}, u32[]{:S(2)}, u32[]{:S(2)}) collective-permute-start(bf16[768,768]{1,0:T(8,128)(2,1)} %bitcast.22), channel_id=1, source_target_pairs={{0,8},{8,0},{16,24},{24,16},{1,9},{9,1},{17,25},{25,17},{2,10},{10... | collective-permute-start | bytes 3538952 | tf_op jit(solution)/shard_map/ppermute | solution.py:330
  1.2 56.8 %collective-permute-start.7 = (bf16[768,768]{1,0:T(8,128)(2,1)}, bf16[768,768]{1,0:T(8,128)(2,1)}, u32[]{:S(2)}, u32[]{:S(2)}) collective-permute-start(bf16[768,768]{1,0:T(8,128)(2,1)} %bitcast.27), channel_id=1, source_target_pairs={{0,8},{8,0},{16,24},{24,16},{1,9},{9,1},{17,25},{25,17},{2,10},{10... | collective-permute-start | bytes 3538952 | tf_op jit(solution)/shard_map/ppermute | solution.py:330
  2.6 1.2 copy-start.5
  4.9 9.5 %copy-start.25 = (f32[768]{0:T(1024)S(1)}, f32[768]{0:T(1024)}, u32[]{:S(2)}) copy-start(f32[768]{0:T(1024)} %param.20) | copy-start | bytes 9220
  4.9 9.5 %copy-start.26 = (f32[768]{0:T(1024)S(1)}, f32[768]{0:T(1024)}, u32[]{:S(2)}) copy-start(f32[768]{0:T(1024)} %param.21) | copy-start | bytes 9220
  4.9 9.5 %copy-start.24 = (s32[394,2]{0,1:T(2,128)S(1)}, s32[394,2]{0,1:T(2,128)}, u32[]{:S(2)}) copy-start(s32[394,2]{0,1:T(2,128)} %param.14) | copy-start | bytes 9460
  4.9 13.8 %copy-start.11 = (bf16[192,768]{1,0:T(8,128)(2,1)S(1)}, bf16[192,768]{1,0:T(8,128)(2,1)}, u32[]{:S(2)}) copy-start(bf16[192,768]{1,0:T(8,128)(2,1)} %w_out.1) | copy-start | bytes 884740
  4.9 20.7 %copy-start.7 = (bf16[394,768]{1,0:T(8,128)(2,1)S(1)}, bf16[394,768]{1,0:T(8,128)(2,1)}, u32[]{:S(2)}) copy-start(bf16[394,768]{1,0:T(8,128)(2,1)} %cot.3) | copy-start | bytes 1815556
  4.9 20.7 %copy-start.13 = (bf16[768,4]{0,1:T(4,128)(2,1)S(1)}, bf16[768,4]{0,1:T(4,128)(2,1)}, u32[]{:S(2)}) copy-start(bf16[768,4]{0,1:T(4,128)(2,1)} %param.22) | copy-start | bytes 18436
  10.6 14.9 %copy-start.22 = (bf16[394,192]{1,0:T(8,128)(2,1)}, bf16[394,192]{1,0:T(8,128)(2,1)S(1)}, u32[]{:S(2)}) copy-start(bf16[394,192]{1,0:T(8,128)(2,1)S(1)} %get-tuple-element.120.value) | copy-start | bytes 453892
  10.6 8.1 %collective-permute-start.2 = (bf16[394,192]{1,0:T(8,128)(2,1)S(1)}, bf16[394,192]{1,0:T(8,128)(2,1)S(1)}, u32[]{:S(2)}, u32[]{:S(2)}) collective-permute-start(bf16[394,192]{1,0:T(8,128)(2,1)S(1)} %get-tuple-element.90.rest_0_.head_out), channel_id=1, source_target_pairs={{0,24},{8,16},{16,8},{24,0},{1,25},{9,17},{17,9},{25,1},{2,26},{10... | collective-permute-start | bytes 453896 | tf_op jit(solution)/shard_map/ppermute | solution.py:330
  13.2 10.6 %collective-permute-start.1 = (bf16[394,192]{1,0:T(8,128)(2,1)S(1)}, bf16[394,192]{1,0:T(8,128)(2,1)S(1)}, u32[]{:S(2)}, u32[]{:S(2)}) collective-permute-start(bf16[394,192]{1,0:T(8,128)(2,1)S(1)} %get-tuple-element.90.rest_0_.head_out), channel_id=1, source_target_pairs={{0,16},{8,24},{16,0},{24,8},{1,17},{9,25},{17,1},{25,9},{2,18},{10... | collective-permute-start | bytes 453896 | tf_op jit(solution)/shard_map/ppermute | solution.py:330
  13.6 12.0 %collective-permute-start = (bf16[394,192]{1,0:T(8,128)(2,1)S(1)}, bf16[394,192]{1,0:T(8,128)(2,1)S(1)}, u32[]{:S(2)}, u32[]{:S(2)}) collective-permute-start(bf16[394,192]{1,0:T(8,128)(2,1)S(1)} %get-tuple-element.90.rest_0_.head_out), channel_id=1, source_target_pairs={{0,8},{8,0},{16,24},{24,16},{1,9},{9,1},{17,25},{25,17},{2,10},{10... | collective-permute-start | bytes 453896 | tf_op jit(solution)/shard_map/ppermute | solution.py:330
  18.7 10.7 %collective-permute-start.5 = (bf16[192,768]{1,0:T(8,128)(2,1)S(1)}, bf16[192,768]{1,0:T(8,128)(2,1)S(1)}, u32[]{:S(2)}, u32[]{:S(2)}) collective-permute-start(bf16[192,768]{1,0:T(8,128)(2,1)S(1)} %copy-done.11), channel_id=1, source_target_pairs={{0,24},{8,16},{16,8},{24,0},{1,25},{9,17},{17,9},{25,1},{2,26},{10... | collective-permute-start | bytes 884744 | tf_op jit(solution)/shard_map/ppermute | solution.py:330
  23.8 12.1 %collective-permute-start.4 = (bf16[192,768]{1,0:T(8,128)(2,1)S(1)}, bf16[192,768]{1,0:T(8,128)(2,1)S(1)}, u32[]{:S(2)}, u32[]{:S(2)}) collective-permute-start(bf16[192,768]{1,0:T(8,128)(2,1)S(1)} %copy-done.11), channel_id=1, source_target_pairs={{0,16},{8,24},{16,0},{24,8},{1,17},{9,25},{17,1},{25,9},{2,18},{10... | collective-permute-start | bytes 884744 | tf_op jit(solution)/shard_map/ppermute | solution.py:330
  25.6 10.3 %collective-permute-start.3 = (bf16[192,768]{1,0:T(8,128)(2,1)S(1)}, bf16[192,768]{1,0:T(8,128)(2,1)S(1)}, u32[]{:S(2)}, u32[]{:S(2)}) collective-permute-start(bf16[192,768]{1,0:T(8,128)(2,1)S(1)} %copy-done.11), channel_id=1, source_target_pairs={{0,8},{8,0},{16,24},{24,16},{1,9},{9,1},{17,25},{25,17},{2,10},{10... | collective-permute-start | bytes 884744 | tf_op jit(solution)/shard_map/ppermute | solution.py:330
  25.6 10.3 %copy-start.9 = (bf16[394,768]{1,0:T(8,128)(2,1)S(1)}, bf16[394,768]{1,0:T(8,128)(2,1)}, u32[]{:S(2)}) copy-start(bf16[394,768]{1,0:T(8,128)(2,1)} %tokens.5) | copy-start | bytes 1815556
  29.4 13.5 %collective-permute-start.13 = (bf16[144,768]{1,0:T(8,128)(2,1)S(1)}, bf16[144,768]{1,0:T(8,128)(2,1)S(1)}, u32[]{:S(2)}, u32[]{:S(2)}) collective-permute-start(bf16[144,768]{1,0:T(8,128)(2,1)S(1)} %get-tuple-element.103), channel_id=1, source_target_pairs={{0,6},{2,4},{4,2},{6,0},{1,7},{3,5},{5,3},{7,1},{8,14},{10,12},{12... | collective-permute-start | bytes 663560 | tf_op jit(solution)/shard_map/ppermute | solution.py:333
  35.9 22.1 %copy-start.2 = (bf16[1,768,768]{2,1,0:T(8,128)(2,1)S(1)}, bf16[1,768,768]{2,1,0:T(8,128)(2,1)}, u32[]{:S(2)}) copy-start(bf16[1,768,768]{2,1,0:T(8,128)(2,1)} %param.23) | copy-start | bytes 3538948
  35.9 22.1 %copy-start.3 = (bf16[1,768,768]{2,1,0:T(8,128)(2,1)S(1)}, bf16[1,768,768]{2,1,0:T(8,128)(2,1)}, u32[]{:S(2)}) copy-start(bf16[1,768,768]{2,1,0:T(8,128)(2,1)} %param.24) | copy-start | bytes 3538948
  38.7 10.6 %collective-permute-start.12 = (bf16[144,768]{1,0:T(8,128)(2,1)S(1)}, bf16[144,768]{1,0:T(8,128)(2,1)S(1)}, u32[]{:S(2)}, u32[]{:S(2)}) collective-permute-start(bf16[144,768]{1,0:T(8,128)(2,1)S(1)} %get-tuple-element.102), channel_id=1, source_target_pairs={{0,6},{2,4},{4,2},{6,0},{1,7},{3,5},{5,3},{7,1},{8,14},{10,12},{12... | collective-permute-start | bytes 663560 | tf_op jit(solution)/shard_map/ppermute | solution.py:333
  42.9 38.9 %collective-permute-start.9 = (bf16[144,768]{1,0:T(8,128)(2,1)S(1)}, bf16[144,768]{1,0:T(8,128)(2,1)S(1)}, u32[]{:S(2)}, u32[]{:S(2)}) collective-permute-start(bf16[144,768]{1,0:T(8,128)(2,1)S(1)} %get-tuple-element.97), channel_id=1, source_target_pairs={{0,2},{2,0},{4,6},{6,4},{1,3},{3,1},{5,7},{7,5},{8,10},{10,8},{12,... | collective-permute-start | bytes 663560 | tf_op jit(solution)/shard_map/ppermute | solution.py:333
  42.9 29.5 %collective-permute-start.11 = (bf16[144,768]{1,0:T(8,128)(2,1)S(1)}, bf16[144,768]{1,0:T(8,128)(2,1)S(1)}, u32[]{:S(2)}, u32[]{:S(2)}) collective-permute-start(bf16[144,768]{1,0:T(8,128)(2,1)S(1)} %get-tuple-element.100), channel_id=1, source_target_pairs={{0,4},{2,6},{4,0},{6,2},{1,5},{3,7},{5,1},{7,3},{8,12},{10,14},{12... | collective-permute-start | bytes 663560 | tf_op jit(solution)/shard_map/ppermute | solution.py:333
  49.2 32.6 %collective-permute-start.8 = (bf16[144,768]{1,0:T(8,128)(2,1)S(1)}, bf16[144,768]{1,0:T(8,128)(2,1)S(1)}, u32[]{:S(2)}, u32[]{:S(2)}) collective-permute-start(bf16[144,768]{1,0:T(8,128)(2,1)S(1)} %get-tuple-element.96), channel_id=1, source_target_pairs={{0,2},{2,0},{4,6},{6,4},{1,3},{3,1},{5,7},{7,5},{8,10},{10,8},{12,... | collective-permute-start | bytes 663560 | tf_op jit(solution)/shard_map/ppermute | solution.py:333
  58.0 19.1 %collective-permute-start.10 = (bf16[144,768]{1,0:T(8,128)(2,1)S(1)}, bf16[144,768]{1,0:T(8,128)(2,1)S(1)}, u32[]{:S(2)}, u32[]{:S(2)}) collective-permute-start(bf16[144,768]{1,0:T(8,128)(2,1)S(1)} %get-tuple-element.99), channel_id=1, source_target_pairs={{0,4},{2,6},{4,0},{6,2},{1,5},{3,7},{5,1},{7,3},{8,12},{10,14},{12... | collective-permute-start | bytes 663560 | tf_op jit(solution)/shard_map/ppermute | solution.py:333
  62.7 31.8 %collective-permute-start.16 = (bf16[144,768]{1,0:T(8,128)(2,1)S(1)}, bf16[144,768]{1,0:T(8,128)(2,1)S(1)}, u32[]{:S(2)}, u32[]{:S(2)}) collective-permute-start(bf16[144,768]{1,0:T(8,128)(2,1)S(1)} %get-tuple-element.108), channel_id=1, source_target_pairs={{0,6},{2,4},{4,2},{6,0},{1,7},{3,5},{5,3},{7,1},{8,14},{10,12},{12... | collective-permute-start | bytes 663560 | tf_op jit(solution)/shard_map/ppermute | solution.py:333
  81.8 12.8 %collective-permute-start.15 = (bf16[144,768]{1,0:T(8,128)(2,1)S(1)}, bf16[144,768]{1,0:T(8,128)(2,1)S(1)}, u32[]{:S(2)}, u32[]{:S(2)}) collective-permute-start(bf16[144,768]{1,0:T(8,128)(2,1)S(1)} %get-tuple-element.107), channel_id=1, source_target_pairs={{0,4},{2,6},{4,0},{6,2},{1,5},{3,7},{5,1},{7,3},{8,12},{10,14},{12... | collective-permute-start | bytes 663560 | tf_op jit(solution)/shard_map/ppermute | solution.py:333
  86.7 11.6 %collective-permute-start.14 = (bf16[144,768]{1,0:T(8,128)(2,1)S(1)}, bf16[144,768]{1,0:T(8,128)(2,1)S(1)}, u32[]{:S(2)}, u32[]{:S(2)}) collective-permute-start(bf16[144,768]{1,0:T(8,128)(2,1)S(1)} %get-tuple-element.106), channel_id=1, source_target_pairs={{0,2},{2,0},{4,6},{6,4},{1,3},{3,1},{5,7},{7,5},{8,10},{10,8},{12,... | collective-permute-start | bytes 663560 | tf_op jit(solution)/shard_map/ppermute | solution.py:333
  98.3 10.9 %collective-permute-start.17 = (bf16[144,768]{1,0:T(8,128)(2,1)S(1)}, bf16[144,768]{1,0:T(8,128)(2,1)S(1)}, u32[]{:S(2)}, u32[]{:S(2)}) collective-permute-start(bf16[144,768]{1,0:T(8,128)(2,1)S(1)} %get-tuple-element.110), channel_id=1, source_target_pairs={{0,2},{2,0},{4,6},{6,4},{1,3},{3,1},{5,7},{7,5},{8,10},{10,8},{12,... | collective-permute-start | bytes 663560 | tf_op jit(solution)/shard_map/ppermute | solution.py:333
  98.4 18.7 %collective-permute-start.18 = (bf16[144,768]{1,0:T(8,128)(2,1)S(1)}, bf16[144,768]{1,0:T(8,128)(2,1)S(1)}, u32[]{:S(2)}, u32[]{:S(2)}) collective-permute-start(bf16[144,768]{1,0:T(8,128)(2,1)S(1)} %get-tuple-element.111), channel_id=1, source_target_pairs={{0,4},{2,6},{4,0},{6,2},{1,5},{3,7},{5,1},{7,3},{8,12},{10,14},{12... | collective-permute-start | bytes 663560 | tf_op jit(solution)/shard_map/ppermute | solution.py:333
  100.3 16.8 %collective-permute-start.19 = (bf16[144,768]{1,0:T(8,128)(2,1)S(1)}, bf16[144,768]{1,0:T(8,128)(2,1)S(1)}, u32[]{:S(2)}, u32[]{:S(2)}) collective-permute-start(bf16[144,768]{1,0:T(8,128)(2,1)S(1)} %get-tuple-element.112), channel_id=1, source_target_pairs={{0,6},{2,4},{4,2},{6,0},{1,7},{3,5},{5,3},{7,1},{8,14},{10,12},{12... | collective-permute-start | bytes 663560 | tf_op jit(solution)/shard_map/ppermute | solution.py:333
  104.1 14.4 %collective-permute-start.23 = (bf16[394,384]{1,0:T(8,128)(2,1)S(1)}, bf16[394,384]{1,0:T(8,128)(2,1)S(1)}, u32[]{:S(2)}, u32[]{:S(2)}) collective-permute-start(bf16[394,384]{1,0:T(8,128)(2,1)S(1)} %get-tuple-element.116), channel_id=1, source_target_pairs={{0,8},{8,0},{16,24},{24,16},{1,9},{9,1},{17,25},{25,17},{2,10},{10... | collective-permute-start | bytes 907784 | tf_op jit(solution)/shard_map/ppermute | solution.py:330
  104.2 23.8 %collective-permute-start.29 = (f32[8,768]{1,0:T(8,128)S(1)}, f32[8,768]{1,0:T(8,128)S(1)}, u32[]{:S(2)}, u32[]{:S(2)}) collective-permute-start(f32[8,768]{1,0:T(8,128)S(1)} %add_add_fusion), channel_id=1, source_target_pairs={{0,8},{8,0},{16,24},{24,16},{1,9},{9,1},{17,25},{25,17},{2,10},{10... | collective-permute-start | bytes 73736 | tf_op jit(solution)/shard_map/ppermute | solution.py:330
  118.5 10.7 %collective-permute-start.20 = (bf16[394,384]{1,0:T(8,128)(2,1)S(1)}, bf16[394,384]{1,0:T(8,128)(2,1)S(1)}, u32[]{:S(2)}, u32[]{:S(2)}) collective-permute-start(bf16[394,384]{1,0:T(8,128)(2,1)S(1)} %get-tuple-element.114), channel_id=1, source_target_pairs={{0,8},{8,0},{16,24},{24,16},{1,9},{9,1},{17,25},{25,17},{2,10},{10... | collective-permute-start | bytes 907784 | tf_op jit(solution)/shard_map/ppermute | solution.py:330
  118.7 12.8 %collective-permute-start.24 = (bf16[394,384]{1,0:T(8,128)(2,1)S(1)}, bf16[394,384]{1,0:T(8,128)(2,1)S(1)}, u32[]{:S(2)}, u32[]{:S(2)}) collective-permute-start(bf16[394,384]{1,0:T(8,128)(2,1)S(1)} %add_convert_fusion.3), channel_id=1, source_target_pairs={{0,16},{8,24},{16,0},{24,8},{1,17},{9,25},{17,1},{25,9},{2,18},{10... | collective-permute-start | bytes 907784 | tf_op jit(solution)/shard_map/ppermute | solution.py:330
  127.8 31.6 %collective-permute-start.45 = (bf16[768,768]{1,0:T(8,128)(2,1)}, bf16[768,768]{1,0:T(8,128)(2,1)}, u32[]{:S(2)}, u32[]{:S(2)}) collective-permute-start(bf16[768,768]{1,0:T(8,128)(2,1)} %get-tuple-element.164), channel_id=1, source_target_pairs={{0,8},{8,0},{16,24},{24,16},{1,9},{9,1},{17,25},{25,17},{2,10},{10... | collective-permute-start | bytes 3538952 | tf_op jit(solution)/shard_map/ppermute | solution.py:330
  128.7 4.1 %collective-permute-start.30 = (f32[8,768]{1,0:T(8,128)}, f32[8,768]{1,0:T(8,128)}, u32[]{:S(2)}, u32[]{:S(2)}) collective-permute-start(f32[8,768]{1,0:T(8,128)} %add.68), channel_id=1, source_target_pairs={{0,16},{8,24},{16,0},{24,8},{1,17},{9,25},{17,1},{25,9},{2,18},{10... | collective-permute-start | bytes 73736 | tf_op jit(solution)/shard_map/ppermute | solution.py:330
  130.0 9.5 %collective-permute-start.21 = (bf16[394,384]{1,0:T(8,128)(2,1)}, bf16[394,384]{1,0:T(8,128)(2,1)}, u32[]{:S(2)}, u32[]{:S(2)}) collective-permute-start(bf16[394,384]{1,0:T(8,128)(2,1)} %add_convert_fusion.5), channel_id=1, source_target_pairs={{0,16},{8,24},{16,0},{24,8},{1,17},{9,25},{17,1},{25,9},{2,18},{10... | collective-permute-start | bytes 907784 | tf_op jit(solution)/shard_map/ppermute | solution.py:330
  131.6 9.2 %collective-permute-start.25 = (bf16[394,384]{1,0:T(8,128)(2,1)S(1)}, bf16[394,384]{1,0:T(8,128)(2,1)}, u32[]{:S(2)}, u32[]{:S(2)}) collective-permute-start(bf16[394,384]{1,0:T(8,128)(2,1)S(1)} %add_convert_fusion.2.own), channel_id=1, source_target_pairs={{0,8},{8,0},{16,24},{24,16},{1,9},{9,1},{17,25},{25,17},{2,10},{10... | collective-permute-start | bytes 907784 | tf_op jit(solution)/shard_map/ppermute | solution.py:330
  131.7 29.6 %collective-permute-start.47 = (bf16[768,768]{1,0:T(8,128)(2,1)}, bf16[768,768]{1,0:T(8,128)(2,1)S(1)}, u32[]{:S(2)}, u32[]{:S(2)}) collective-permute-start(bf16[768,768]{1,0:T(8,128)(2,1)} %copy-done.4), channel_id=1, source_target_pairs={{0,8},{8,0},{16,24},{24,16},{1,9},{9,1},{17,25},{25,17},{2,10},{10... | collective-permute-start | bytes 3538952 | tf_op jit(solution)/shard_map/ppermute | solution.py:330
  140.7 32.3 %collective-permute-start.22 = (bf16[394,384]{1,0:T(8,128)(2,1)S(1)}, bf16[394,384]{1,0:T(8,128)(2,1)S(1)}, u32[]{:S(2)}, u32[]{:S(2)}) collective-permute-start(bf16[394,384]{1,0:T(8,128)(2,1)S(1)} %add_convert_fusion.4), channel_id=1, source_target_pairs={{0,8},{8,0},{16,24},{24,16},{1,9},{9,1},{17,25},{25,17},{2,10},{10... | collective-permute-start | bytes 907784 | tf_op jit(solution)/shard_map/ppermute | solution.py:330
  140.7 1.2 copy-start.6
  142.9 1.3 copy-start.15
  148.0 11.4 %copy-start.1 = (bf16[768,768]{1,0:T(8,128)(2,1)S(1)}, bf16[768,768]{1,0:T(8,128)(2,1)}, u32[]{:S(2)}) copy-start(bf16[768,768]{1,0:T(8,128)(2,1)} %copy-done) | copy-start | bytes 3538948
  153.5 17.7 %collective-permute-start.31 = (bf16[96,768]{1,0:T(8,128)(2,1)S(1)}, bf16[96,768]{1,0:T(8,128)(2,1)S(1)}, u32[]{:S(2)}, u32[]{:S(2)}) collective-permute-start(bf16[96,768]{1,0:T(8,128)(2,1)S(1)} %get-tuple-element.133), channel_id=1, source_target_pairs={{0,1},{1,0},{2,3},{3,2},{4,5},{5,4},{6,7},{7,6},{8,9},{9,8},{10,11... | collective-permute-start | bytes 442376 | tf_op jit(solution)/shard_map/ppermute | solution.py:340
  155.1 20.4 %collective-permute-start.32 = (bf16[96,768]{1,0:T(8,128)(2,1)S(1)}, bf16[96,768]{1,0:T(8,128)(2,1)S(1)}, u32[]{:S(2)}, u32[]{:S(2)}) collective-permute-start(bf16[96,768]{1,0:T(8,128)(2,1)S(1)} %get-tuple-element.134), channel_id=1, source_target_pairs={{0,2},{1,3},{2,0},{3,1},{4,6},{5,7},{6,4},{7,5},{8,10},{9,11},{10,... | collective-permute-start | bytes 442376 | tf_op jit(solution)/shard_map/ppermute | solution.py:340
  159.4 1.6 collective-permute-start.26
  161.0 15.6 %collective-permute-start.33 = (bf16[96,768]{1,0:T(8,128)(2,1)S(1)}, bf16[96,768]{1,0:T(8,128)(2,1)S(1)}, u32[]{:S(2)}, u32[]{:S(2)}) collective-permute-start(bf16[96,768]{1,0:T(8,128)(2,1)S(1)} %get-tuple-element.135), channel_id=1, source_target_pairs={{0,3},{1,2},{2,1},{3,0},{4,7},{5,6},{6,5},{7,4},{8,11},{9,10},{10,... | collective-permute-start | bytes 442376 | tf_op jit(solution)/shard_map/ppermute | solution.py:340
  161.3 9.6 %collective-permute-start.27 = (bf16[394,384]{1,0:T(8,128)(2,1)S(1)}, bf16[394,384]{1,0:T(8,128)(2,1)S(1)}, u32[]{:S(2)}, u32[]{:S(2)}) collective-permute-start(bf16[394,384]{1,0:T(8,128)(2,1)S(1)} %add_convert_fusion.1), channel_id=1, source_target_pairs={{0,16},{8,24},{16,0},{24,8},{1,17},{9,25},{17,1},{25,9},{2,18},{10... | collective-permute-start | bytes 907784 | tf_op jit(solution)/shard_map/ppermute | solution.py:330
  171.0 19.5 %collective-permute-start.28 = (bf16[394,384]{1,0:T(8,128)(2,1)S(1)}, bf16[394,384]{1,0:T(8,128)(2,1)S(1)}, u32[]{:S(2)}, u32[]{:S(2)}) collective-permute-start(bf16[394,384]{1,0:T(8,128)(2,1)S(1)} %add_convert_fusion.own), channel_id=1, source_target_pairs={{0,8},{8,0},{16,24},{24,16},{1,9},{9,1},{17,25},{25,17},{2,10},{10... | collective-permute-start | bytes 907784 | tf_op jit(solution)/shard_map/ppermute | solution.py:330
  171.2 20.0 %copy-start.10 = (bf16[394,768]{1,0:T(8,128)(2,1)S(1)}, bf16[394,768]{1,0:T(8,128)(2,1)}, u32[]{:S(2)}) copy-start(bf16[394,768]{1,0:T(8,128)(2,1)} %tokens.5) | copy-start | bytes 1815556
  171.2 17.1 %collective-permute-start.34 = (bf16[96,768]{1,0:T(8,128)(2,1)S(1)}, bf16[96,768]{1,0:T(8,128)(2,1)S(1)}, u32[]{:S(2)}, u32[]{:S(2)}) collective-permute-start(bf16[96,768]{1,0:T(8,128)(2,1)S(1)} %get-tuple-element.136), channel_id=1, source_target_pairs={{0,4},{1,5},{2,6},{3,7},{4,0},{5,1},{6,2},{7,3},{8,12},{9,13},{10,... | collective-permute-start | bytes 442376 | tf_op jit(solution)/shard_map/ppermute | solution.py:340
  172.9 28.0 %collective-permute-start.46 = (bf16[384,768]{1,0:T(8,128)(2,1)S(1)}, bf16[384,768]{1,0:T(8,128)(2,1)S(1)}, u32[]{:S(2)}, u32[]{:S(2)}) collective-permute-start(bf16[384,768]{1,0:T(8,128)(2,1)S(1)} %select_convert_fusion.2), channel_id=1, source_target_pairs={{0,1},{1,0},{2,3},{3,2},{4,5},{5,4},{6,7},{7,6},{8,9},{9,8},{10,11... | collective-permute-start | bytes 1769480 | tf_op jit(solution)/shard_map/ppermute | solution.py:336
  175.5 18.1 %collective-permute-start.35 = (bf16[96,768]{1,0:T(8,128)(2,1)S(1)}, bf16[96,768]{1,0:T(8,128)(2,1)S(1)}, u32[]{:S(2)}, u32[]{:S(2)}) collective-permute-start(bf16[96,768]{1,0:T(8,128)(2,1)S(1)} %get-tuple-element.137), channel_id=1, source_target_pairs={{0,5},{1,4},{2,7},{3,6},{4,1},{5,0},{6,3},{7,2},{8,13},{9,12},{10,... | collective-permute-start | bytes 442376 | tf_op jit(solution)/shard_map/ppermute | solution.py:340
  176.7 16.9 %collective-permute-start.36 = (bf16[96,768]{1,0:T(8,128)(2,1)S(1)}, bf16[96,768]{1,0:T(8,128)(2,1)S(1)}, u32[]{:S(2)}, u32[]{:S(2)}) collective-permute-start(bf16[96,768]{1,0:T(8,128)(2,1)S(1)} %get-tuple-element.138), channel_id=1, source_target_pairs={{0,6},{1,7},{2,4},{3,5},{4,2},{5,3},{6,0},{7,1},{8,14},{9,15},{10,... | collective-permute-start | bytes 442376 | tf_op jit(solution)/shard_map/ppermute | solution.py:340
  188.3 8.0 %collective-permute-start.37 = (bf16[96,768]{1,0:T(8,128)(2,1)S(1)}, bf16[96,768]{1,0:T(8,128)(2,1)S(1)}, u32[]{:S(2)}, u32[]{:S(2)}) collective-permute-start(bf16[96,768]{1,0:T(8,128)(2,1)S(1)} %get-tuple-element.139), channel_id=1, source_target_pairs={{0,7},{1,6},{2,5},{3,4},{4,3},{5,2},{6,1},{7,0},{8,15},{9,14},{10,... | collective-permute-start | bytes 442376 | tf_op jit(solution)/shard_map/ppermute | solution.py:340
  190.4 23.4 %collective-permute-start.48 = (bf16[768,384]{1,0:T(8,128)(2,1)S(1)}, bf16[768,384]{1,0:T(8,128)(2,1)S(1)}, u32[]{:S(2)}, u32[]{:S(2)}) collective-permute-start(bf16[768,384]{1,0:T(8,128)(2,1)S(1)} %select_convert_fusion.1), channel_id=1, source_target_pairs={{0,1},{1,0},{2,3},{3,2},{4,5},{5,4},{6,7},{7,6},{8,9},{9,8},{10,11... | collective-permute-start | bytes 1769480 | tf_op jit(solution)/shard_map/ppermute | solution.py:336
  196.4 20.3 %collective-permute-start.44 = (bf16[112,768]{1,0:T(8,128)(2,1)S(1)}, bf16[112,768]{1,0:T(8,128)(2,1)S(1)}, u32[]{:S(2)}, u32[]{:S(2)}) collective-permute-start(bf16[112,768]{1,0:T(8,128)(2,1)S(1)} %shard_map.223.refs_0_), channel_id=1, source_target_pairs={{0,7},{1,6},{2,5},{3,4},{4,3},{5,2},{6,1},{7,0},{8,15},{9,14},{10,... | collective-permute-start | bytes 516104 | tf_op jit(solution)/shard_map/ppermute | solution.py:340
  199.0 25.1 %collective-permute-start.43 = (bf16[112,768]{1,0:T(8,128)(2,1)S(1)}, bf16[112,768]{1,0:T(8,128)(2,1)S(1)}, u32[]{:S(2)}, u32[]{:S(2)}) collective-permute-start(bf16[112,768]{1,0:T(8,128)(2,1)S(1)} %shard_map.223.refs_0_), channel_id=1, source_target_pairs={{0,6},{1,7},{2,4},{3,5},{4,2},{5,3},{6,0},{7,1},{8,14},{9,15},{10,... | collective-permute-start | bytes 516104 | tf_op jit(solution)/shard_map/ppermute | solution.py:340
  202.1 29.7 %collective-permute-start.42 = (bf16[112,768]{1,0:T(8,128)(2,1)S(1)}, bf16[112,768]{1,0:T(8,128)(2,1)S(1)}, u32[]{:S(2)}, u32[]{:S(2)}) collective-permute-start(bf16[112,768]{1,0:T(8,128)(2,1)S(1)} %shard_map.223.refs_0_), channel_id=1, source_target_pairs={{0,5},{1,4},{2,7},{3,6},{4,1},{5,0},{6,3},{7,2},{8,13},{9,12},{10,... | collective-permute-start | bytes 516104 | tf_op jit(solution)/shard_map/ppermute | solution.py:340
  213.8 19.8 %collective-permute-start.41 = (bf16[112,768]{1,0:T(8,128)(2,1)S(1)}, bf16[112,768]{1,0:T(8,128)(2,1)S(1)}, u32[]{:S(2)}, u32[]{:S(2)}) collective-permute-start(bf16[112,768]{1,0:T(8,128)(2,1)S(1)} %shard_map.223.refs_0_), channel_id=1, source_target_pairs={{0,4},{1,5},{2,6},{3,7},{4,0},{5,1},{6,2},{7,3},{8,12},{9,13},{10,... | collective-permute-start | bytes 516104 | tf_op jit(solution)/shard_map/ppermute | solution.py:340
  213.8 19.8 %collective-permute-start.40 = (bf16[112,768]{1,0:T(8,128)(2,1)S(1)}, bf16[112,768]{1,0:T(8,128)(2,1)S(1)}, u32[]{:S(2)}, u32[]{:S(2)}) collective-permute-start(bf16[112,768]{1,0:T(8,128)(2,1)S(1)} %shard_map.223.refs_0_), channel_id=1, source_target_pairs={{0,3},{1,2},{2,1},{3,0},{4,7},{5,6},{6,5},{7,4},{8,11},{9,10},{10,... | collective-permute-start | bytes 516104 | tf_op jit(solution)/shard_map/ppermute | solution.py:340
  216.7 17.7 %collective-permute-start.39 = (bf16[112,768]{1,0:T(8,128)(2,1)S(1)}, bf16[112,768]{1,0:T(8,128)(2,1)S(1)}, u32[]{:S(2)}, u32[]{:S(2)}) collective-permute-start(bf16[112,768]{1,0:T(8,128)(2,1)S(1)} %shard_map.223.refs_0_), channel_id=1, source_target_pairs={{0,2},{1,3},{2,0},{3,1},{4,6},{5,7},{6,4},{7,5},{8,10},{9,11},{10,... | collective-permute-start | bytes 516104 | tf_op jit(solution)/shard_map/ppermute | solution.py:340
  224.0 10.4 %collective-permute-start.38 = (bf16[112,768]{1,0:T(8,128)(2,1)S(1)}, bf16[112,768]{1,0:T(8,128)(2,1)S(1)}, u32[]{:S(2)}, u32[]{:S(2)}) collective-permute-start(bf16[112,768]{1,0:T(8,128)(2,1)S(1)} %shard_map.223.refs_0_), channel_id=1, source_target_pairs={{0,1},{1,0},{2,3},{3,2},{4,5},{5,4},{6,7},{7,6},{8,9},{9,8},{10,11... | collective-permute-start | bytes 516104 | tf_op jit(solution)/shard_map/ppermute | solution.py:340
  (12 other events, 11.1 us)
where the time goes:
time: 239 us; the launch traced here: 238 us
  starting transfers between devices  85.5 us (36%)
  waiting for transfers between devices  79.3 us (33%)
  Pallas kernels  44.7 us (19%)
  local copies, waits for them, and re-layouts  17.6 us (7%)
  other arithmetic  9.1 us (4%)
    pallas_call x14, Pallas kernels, run(): pl.pallas_call(kernel, out_shape=[jax.ShapeDtypeStruct(shape, kind) for s...  44.7 us
    ppermute x14, starting transfers between devices, group_swap(): return lax.ppermute(value, ('expert', 'dp'), pairs)  39.6 us
    ppermute x12, waiting for transfers between devices, expert_swap(): lax.ppermute(value, 'expert', [(i, i ^ mask) for i in range(n_expert)])  31.9 us
    ppermute x12, starting transfers between devices, expert_swap(): lax.ppermute(value, 'expert', [(i, i ^ mask) for i in range(n_expert)])  29.5 us
    ppermute x21, waiting for transfers between devices, tensor_swap(): lax.ppermute(value, 'tensor', [(i, i ^ mask) for i in range(n_tensor)])  25.9 us
    ppermute x14, waiting for transfers between devices, group_swap(): return lax.ppermute(value, ('expert', 'dp'), pairs)  21.5 us
    unnamed x55, local copies, waits for them, and re-layouts  14.9 us
    ppermute x21, starting transfers between devices, tensor_swap(): lax.ppermute(value, 'tensor', [(i, i ^ mask) for i in range(n_tensor)])  14 us
  transfers between devices with their start and end apart: 49, of which 19 were waited for; matrix products, arithmetic and copies ran while one was open for 5% of the time, Pallas kernels for 18%

commit v1 on v0

v1 whole, which is shorter than its diff:
```python
import functools

import jax
import jax.numpy as jnp
from jax import lax
from jax.experimental import pallas as pl
from jax.experimental.pallas import tpu as pltpu
from jax.sharding import PartitionSpec as P

HEAD_DIM = 64
SEQ = 197
EPSILON = 1e-06
F32 = jnp.float32
BF16 = jnp.bfloat16
LANES = 128
SMALL = 16


def dot_nn(left, right):
    return lax.dot_general(left, right, (((1,), (0,)), ((), ())), preferred_element_type=F32)


def dot_tn(left, right):
    return lax.dot_general(left, right, (((0,), (0,)), ((), ())), preferred_element_type=F32)


def dot_nt(left, right):
    return lax.dot_general(left, right, (((1,), (1,)), ((), ())), preferred_element_type=F32)


def norm_parts(values_in):
    row_mean = jnp.mean(values_in, axis=-1, keepdims=True)
    centred = values_in - row_mean
    variance = jnp.mean(centred * centred, axis=-1, keepdims=True)
    scale = lax.rsqrt(variance + EPSILON)
    return centred * scale, scale


def norm_back(normed, scale, u):
    return scale * (
        u
        - jnp.mean(u, axis=-1, keepdims=True)
        - normed * jnp.mean(u * normed, axis=-1, keepdims=True)
    )


def iota(shape, dim):
    return lax.broadcasted_iota(jnp.int32, shape, dim)


def row_of(vector):
    return vector[...].reshape(1, vector.shape[0])


def head_mask(head, width):
    lane = iota((1, width), 1)
    return ((lane >= head * HEAD_DIM) & (lane < (head + 1) * HEAD_DIM)).astype(BF16)


def image_of(shape, dim, images):
    at = iota(shape, dim)
    image = jnp.zeros(shape, jnp.int32)
    for number in range(1, images):
        image = image + (at >= number * SEQ).astype(jnp.int32)
    return image


T_ID, C_ID, E_ID, D_ID, Q_ID, L_ID = range(6)


def plan_kernel(experts, ids, routes, cot, router, table, router_pad, *blocks):
    rows = cot.shape[0]
    cap = table.shape[1]
    tall = max(16, -(-experts // 16) * 16)
    picks = routes[...]
    expert = iota((tall, rows), 0)
    named = picks[0:1, :] == expert
    for k in range(1, picks.shape[0]):
        named = named | (picks[k : k + 1, :] == expert)
    named = named & (iota((tall, rows), 1) < ids[L_ID])
    marks = jnp.where(named, 1.0, 0.0).astype(BF16)
    earlier = jnp.where(iota((rows, rows), 0) < iota((rows, rows), 1), 1.0, 0.0).astype(BF16)
    slot = dot_nn(marks, earlier)
    first = (ids[C_ID] * cap).astype(F32)
    slot = jnp.where(named, slot - first, -1.0)
    place = iota((cap, rows), 0).astype(F32)
    for x in range(experts):
        table[x] = jnp.where(slot[x : x + 1, :] == place, 1.0, 0.0).astype(BF16)
    for k in range(experts):
        blocks[k][...] = dot_nn(table[ids[E_ID] ^ k], cot[...]).astype(BF16)
    router_pad[...] = jnp.zeros_like(router_pad)
    router_pad[:experts, :] = router[...]


def attend_kernel(images, tokens, gain, bias, weight, normed, query, key, value, probs, head_out):
    rows = tokens.shape[0]
    inner = query.shape[1]
    heads = inner // HEAD_DIM
    unit, _ = norm_parts(tokens[...].astype(F32))
    normed[...] = (unit * row_of(gain) + row_of(bias)).astype(BF16)
    query[...] = dot_nt(normed[...], weight[:inner]).astype(BF16)
    key[...] = dot_nt(normed[...], weight[inner : 2 * inner]).astype(BF16)
    value[...] = dot_nt(normed[...], weight[2 * inner :]).astype(BF16)
    same = image_of((rows, 1), 0, images) == image_of((1, rows), 1, images)
    total = jnp.zeros((rows, inner), F32)
    for head in range(heads):
        mask = head_mask(head, inner)
        scores = dot_nt(query[...] * mask, key[...]) * (HEAD_DIM**-0.5)
        scores = jnp.where(same, scores, -1e30)
        top = jnp.max(scores, axis=-1, keepdims=True)
        weights = jnp.exp(scores - top)
        weights = weights * (1.0 / jnp.sum(weights, axis=-1, keepdims=True))
        probs[head] = weights.astype(BF16)
        total = total + dot_nn(probs[head], value[...] * mask)
    head_out[...] = total.astype(BF16)


def middle_kernel(
    n_tensor, experts, ids, tokens, gain, bias, table, *rest
):
    heads = rest[:n_tensor]
    weights = rest[n_tensor : 2 * n_tensor]
    middle = rest[2 * n_tensor]
    blocks = rest[2 * n_tensor + 1 : 2 * n_tensor + 1 + experts]
    held_heads, held_weights, low = rest[2 * n_tensor + 1 + experts :]
    for j in range(n_tensor):
        held_heads[j] = heads[j][...]
        held_weights[j] = weights[j][...]
    total = tokens[...].astype(F32)
    for rank in range(n_tensor):
        place = ids[T_ID] ^ rank
        total = total + dot_nn(held_heads[place], held_weights[place])
    middle[...] = total
    unit, _ = norm_parts(total)
    low[...] = (unit * row_of(gain) + row_of(bias)).astype(BF16)
    for k in range(experts):
        blocks[k][...] = dot_nn(table[ids[E_ID] ^ k], low[...]).astype(BF16)


def expert_kernel(experts, number, ids, up_a, up_b, down_a, down_b, router, *refs):
    row_blocks, out_blocks = refs[:number], refs[number : 2 * number]
    refs = refs[2 * number :]
    back_blocks, gated_blocks = refs[:number], refs[number : 2 * number]
    rows_in, d_result, hidden_a, hidden_b, d_pre_a, d_pre_b, router_part, d_out = refs[2 * number :]
    size = row_blocks[0].shape[0]
    count = size * number
    for k in range(number):
        rows_in[k * size : (k + 1) * size, :] = row_blocks[k][...]
        d_out[k * size : (k + 1) * size, :] = out_blocks[k][...].astype(F32)
    lane = iota((count, LANES), 1)
    logits = dot_nt(rows_in[...], router[...])
    logits = jnp.where(lane < experts, logits, -1e30)
    top = jnp.max(logits, axis=-1, keepdims=True)
    odds = jnp.exp(logits - top)
    odds = odds / jnp.sum(odds, axis=-1, keepdims=True)
    mine = (lane == ids[E_ID]).astype(F32)
    gate = jnp.sum(odds * mine, axis=-1, keepdims=True)
    d_result[...] = (gate * d_out[...]).astype(BF16)
    result = jnp.zeros(d_out.shape, F32)
    back = jnp.zeros(d_out.shape, F32)
    scale = 0.7978845608028654
    for up, down, hidden, d_pre in (
        (up_a, down_a, hidden_a, d_pre_a),
        (up_b, down_b, hidden_b, d_pre_b),
    ):
        act = dot_nn(rows_in[...], up[...])
        square = act * act
        bend = jnp.tanh(scale * act * (1.0 + 0.044715 * square))
        half = 0.5 * (1.0 + bend)
        hidden[...] = (act * half).astype(BF16)
        slope = half + 0.5 * act * (1.0 - bend * bend) * (
            scale * (1.0 + 3 * 0.044715 * square)
        )
        result = result + dot_nn(hidden[...], down[...])
        d_pre[...] = (dot_nt(d_result[...], down[...]) * slope).astype(BF16)
        back = back + dot_nt(d_pre[...], up[...])
    d_gate = jnp.sum(d_out[...] * result, axis=-1, keepdims=True)
    d_logits = (d_gate * gate * (mine - odds)).astype(BF16)
    back = (back + dot_nn(d_logits, router[...])).astype(BF16)
    gated = (gate * result).astype(BF16)
    for k in range(number):
        back_blocks[k][...] = back[k * size : (k + 1) * size, :]
        gated_blocks[k][...] = gated[k * size : (k + 1) * size, :]
    router_part[...] = dot_tn(d_logits, rows_in[...])[: router_part.shape[0]]


def weight_grad_kernel(count, *refs):
    rows = refs[:count]
    d_pre_a = refs[count : 2 * count]
    d_pre_b = refs[2 * count : 3 * count]
    hidden_a = refs[3 * count : 4 * count]
    hidden_b = refs[4 * count : 5 * count]
    d_result = refs[5 * count : 6 * count]
    own, pair = refs[6 * count :]
    width = own.shape[0] // 2
    for out, at, lefts, rights in (
        (pair, 0, rows, d_pre_b),
        (pair, width, hidden_b, d_result),
        (own, 0, rows, d_pre_a),
        (own, width, hidden_a, d_result),
    ):
        total = dot_tn(lefts[0][...], rights[0][...])
        for k in range(1, count):
            total = total + dot_tn(lefts[k][...], rights[k][...])
        out[at : at + width, :] = total.astype(BF16)


def split_grad_kernel(ids, own, came, kept, sent, total):
    total[...] = own[...].astype(F32) + came[...].astype(F32)
    width = own.shape[1]
    half = width // 2
    for out, which in ((kept, ids[D_ID]), (sent, 1 - ids[D_ID])):
        out[:half, :] = total[pl.ds(pl.multiple_of(which * half, 16), half), :].astype(out.dtype)
        column = pl.ds(pl.multiple_of(which * half, LANES), half)
        out[half:, :half] = total[width : width + half, column].astype(out.dtype)
        out[half:, half:] = total[width + half :, column].astype(out.dtype)


def join_grad_kernel(kept, came, grad_up, grad_down):
    half = kept.shape[1] // 2
    grad_up[...] = kept[:half, :] + came[:half, :].astype(F32)
    grad_down[:half, :] = kept[half:, :half] + came[half:, :half].astype(F32)
    grad_down[half:, :] = kept[half:, half:] + came[half:, half:].astype(F32)


def combine_kernel(experts, parts, base, ids, table, *refs):
    blocks = refs[:experts]
    routers = refs[experts : experts + parts]
    kept, sent, total = refs[experts + parts :]
    value = dot_tn(table[ids[E_ID]], blocks[0][...])
    for k in range(1, experts):
        value = value + dot_tn(table[ids[E_ID] ^ k], blocks[k][...])
    total[...] = jnp.zeros_like(total)
    total[: value.shape[0], :] = value
    if parts:
        added = routers[0][...]
        for k in range(1, parts):
            added = added + routers[k][...]
        total[base : base + added.shape[0], :] = added
    half = kept.shape[1]
    kept[...] = total[:, pl.ds(pl.multiple_of(ids[C_ID] * half, LANES), half)].astype(BF16)
    sent[...] = total[:, pl.ds(pl.multiple_of((1 - ids[C_ID]) * half, LANES), half)].astype(BF16)


def joined(ids, own, other, whole):
    half = own.shape[1]
    whole[:, pl.ds(pl.multiple_of(ids[C_ID] * half, LANES), half)] = own[...].astype(F32)
    whole[:, pl.ds(pl.multiple_of((1 - ids[C_ID]) * half, LANES), half)] = other[...].astype(F32)


def back_kernel(
    blocks_n, ids, own, other, middle, cot, gain, w_out, head_out, normed, query, key, value,
    probs, weight, *rest
):
    d_middle, kept, sent, small = rest[:4]
    blocks = rest[4 : 4 + blocks_n]
    whole, grads = rest[4 + blocks_n :]
    rows, inner = query.shape
    heads = inner // HEAD_DIM
    joined(ids, own, other, whole)
    d_normed = whole[:rows, :]
    unit, scale = norm_parts(middle[...])
    small[...] = jnp.zeros_like(small)
    base = -(-rows // 16) * 16
    small[8:, :] = whole[base : base + small.shape[0] - 8, :]
    small[2:3, :] = jnp.sum(d_normed * unit, axis=0, keepdims=True)
    small[3:4, :] = jnp.sum(d_normed, axis=0, keepdims=True)
    live = iota((rows, 1), 0) < ids[L_ID]
    d_out = jnp.where(live, cot[...].astype(F32), 0.0)
    d_mid = d_out + norm_back(unit, scale, d_normed * row_of(gain))
    d_middle[...] = d_mid
    d_branch = d_mid.astype(BF16)
    d_head = dot_nt(d_branch, w_out[...]).astype(BF16)
    grads[3 * inner :, :] = dot_tn(head_out[...], d_branch).astype(BF16)
    d_query = jnp.zeros((rows, inner), F32)
    d_key = jnp.zeros((rows, inner), F32)
    d_value = jnp.zeros((rows, inner), F32)
    for head in range(heads):
        mask = head_mask(head, inner)
        chance = probs[head].astype(F32)
        d_probs = dot_nt(d_head, value[...] * mask)
        delta = jnp.sum(d_probs * chance, axis=-1, keepdims=True)
        d_scores = (chance * (d_probs - delta)).astype(BF16)
        d_value = d_value + dot_tn(probs[head], d_head * mask)
        d_query = d_query + dot_nn(d_scores, key[...] * mask)
        d_key = d_key + dot_tn(d_scores, query[...] * mask)
    d_query = (d_query * (HEAD_DIM**-0.5)).astype(BF16)
    d_key = (d_key * (HEAD_DIM**-0.5)).astype(BF16)
    d_value = d_value.astype(BF16)
    grads[:inner, :] = dot_tn(d_query, normed[...]).astype(BF16)
    grads[inner : 2 * inner, :] = dot_tn(d_key, normed[...]).astype(BF16)
    grads[2 * inner : 3 * inner, :] = dot_tn(d_value, normed[...]).astype(BF16)
    if blocks_n == 1:
        blocks[0][...] = grads[...]
    else:
        size = blocks[0].shape[0]
        for m in range(blocks_n):
            at = pl.multiple_of((ids[Q_ID] ^ m) * size, 16)
            blocks[m][...] = grads[pl.ds(at, size), :]
    d_in = dot_nn(d_query, weight[:inner])
    d_in = d_in + dot_nn(d_key, weight[inner : 2 * inner])
    whole[:rows, :] = d_in + dot_nn(d_value, weight[2 * inner :])
    half = kept.shape[1]
    kept[...] = whole[:rows, pl.ds(pl.multiple_of(ids[C_ID] * half, LANES), half)].astype(BF16)
    sent[...] = whole[:rows, pl.ds(pl.multiple_of((1 - ids[C_ID]) * half, LANES), half)].astype(BF16)


def last_norm_kernel(ids, own, other, tokens, d_middle, gain, small2, grad_tokens, small, whole):
    joined(ids, own, other, whole)
    d_normed = whole[...]
    unit, scale = norm_parts(tokens[...].astype(F32))
    small[...] = small2[...]
    small[0:1, :] = jnp.sum(d_normed * unit, axis=0, keepdims=True)
    small[1:2, :] = jnp.sum(d_normed, axis=0, keepdims=True)
    grad_tokens[...] = (
        d_middle[...] + norm_back(unit, scale, d_normed * row_of(gain))
    ).astype(BF16)


def sum_kernel(count, *refs):
    total = refs[0][...].astype(F32)
    for m in range(1, count):
        total = total + refs[m][...].astype(F32)
    refs[count][...] = total.astype(BF16)


def pair_kernel(own, came, small, small_came, out):
    size = own.shape[0]
    out[:size, :] = (own[...].astype(F32) + came[...].astype(F32)).astype(BF16)
    out[size:, :] = (small[...] + small_came[...]).astype(BF16)


def spread_kernel(count, ids, *refs):
    parts = refs[:count]
    grad_qkv, grad_out, small, grads, held = refs[count:]
    size = grads.shape[0] // count
    for m in range(count):
        quarter = ids[Q_ID] ^ m
        grads[pl.ds(pl.multiple_of(quarter * size, 16), size), :] = parts[m][:size, :].astype(F32)
        held[quarter] = parts[m][size:, :].astype(F32)
    total = held[0]
    for quarter in range(1, count):
        total = total + held[quarter]
    small[...] = total
    inner = grad_qkv.shape[0]
    grad_qkv[...] = grads[:inner, :]
    grad_out[...] = grads[inner:, :]


def after(value, *others):
    return lax.optimization_barrier((value,) + others)[0]


def run(kernel, outs, args, scratch=(), micros=1.0, limit=16):
    smem = pl.BlockSpec(memory_space=pltpu.SMEM)
    vmem = pl.BlockSpec(memory_space=pltpu.VMEM)
    return pl.pallas_call(
        kernel,
        out_shape=[jax.ShapeDtypeStruct(shape, kind) for shape, kind in outs],
        in_specs=[smem if arg.dtype == jnp.int32 and arg.ndim == 1 else vmem for arg in args],
        out_specs=[vmem] * len(outs),
        scratch_shapes=[pltpu.VMEM(shape, kind) for shape, kind in scratch],
        compiler_params=pltpu.CompilerParams(vmem_limit_bytes=limit * 1024 * 1024),
        cost_estimate=pl.CostEstimate(
            flops=int(micros * 1.15e9), bytes_accessed=1024, transcendentals=0
        ),
    )(*args)


def make_body(n_tensor, n_expert, n_dp):
    small_slice = n_expert == 4 and n_dp == 2

    def tensor_swap(value, mask):
        return lax.ppermute(value, "tensor", [(i, i ^ mask) for i in range(n_tensor)])

    def expert_swap(value, mask):
        return lax.ppermute(value, "expert", [(i, i ^ mask) for i in range(n_expert)])

    def dp_swap(value):
        return lax.ppermute(value, "dp", [(i, i ^ 1) for i in range(n_dp)])

    def quarter_swap(value, mask):
        pairs = [(i, i ^ mask) for i in range(n_expert * n_dp)]
        return lax.ppermute(value, ("expert", "dp"), pairs)

    def exchange(blocks):
        if small_slice:
            came = {k: expert_swap(blocks[k], k) for k in (3, 2, 1)}
            return [blocks[0]] + [came[k] for k in range(1, n_expert)]
        order = jnp.arange(n_expert) ^ lax.axis_index("expert")
        stacked = lax.all_to_all(
            jnp.stack(blocks)[order], "expert", split_axis=0, concat_axis=0, tiled=True
        )[order]
        return [stacked[k] for k in range(n_expert)]

    def tensor_sum(kept, sent):
        chip = (kept.astype(F32) + tensor_swap(sent, 1).astype(F32)).astype(BF16)
        own = (chip.astype(F32) + tensor_swap(chip, 2).astype(F32)).astype(BF16)
        return own, tensor_swap(own, 1)

    def body(
        tokens,
        routes,
        images_live,
        ln1_gain,
        ln1_bias,
        w_qkv,
        w_out,
        ln2_gain,
        ln2_bias,
        w_router,
        w_up,
        w_down,
        cotangent,
    ):
        rows, width = tokens.shape
        inner = w_qkv.shape[2]
        heads = inner // HEAD_DIM
        experts = w_router.shape[1]
        capacity = max(2, 3 * rows // experts // 8 * 8)
        cap = capacity // 2
        images = rows // SEQ
        half = width // 2
        hidden_width = w_up.shape[2]
        rank = lax.axis_index("tensor")
        owner = lax.axis_index("expert")
        copy = lax.axis_index("dp")
        ids = jnp.stack(
            [
                rank,
                rank % 2,
                owner,
                copy,
                (owner % 2) * 2 + copy,
                jnp.minimum(images_live[0] * SEQ, rows),
                rank,
                rank,
            ]
        ).astype(jnp.int32)
        weight = w_qkv.transpose(1, 2, 0).reshape(3 * inner, width)
        up_a, down_a = w_up[0], w_down[0]
        part_rows = max(8, -(-experts // 8) * 8)
        small_rows = 8 + part_rows
        base = -(-rows // 16) * 16
        tall = base + -(-part_rows // 16) * 16

        out_x, out_c = tensor_swap(w_out, 2), tensor_swap(w_out, 1)
        up_b, down_b = tensor_swap(up_a, 1), tensor_swap(down_a, 1)
        table, router, *cot_blocks = run(
            functools.partial(plan_kernel, experts),
            [((experts, cap, rows), BF16), ((LANES, width), BF16)]
            + [((cap, width), BF16)] * experts,
            [ids, routes.T, cotangent, w_router.T],
            micros=3,
        )
        d_rows_in = exchange(cot_blocks)
        normed, query, key, value, probs, head_out = run(
            functools.partial(attend_kernel, images),
            [((rows, width), BF16)]
            + [((rows, inner), BF16)] * 3
            + [((heads, rows, rows), BF16), ((rows, inner), BF16)],
            [after(tokens, table), ln1_gain, ln1_bias, weight],
            micros=4,
        )
        head_out, out_x, up_b, down_b = lax.optimization_barrier((head_out, out_x, up_b, down_b))
        head_x, head_c = tensor_swap(head_out, 2), tensor_swap(head_out, 1)
        out_all = [w_out, out_c, out_x, tensor_swap(out_x, 1)]
        heads_all = [head_out, head_c, head_x, tensor_swap(head_x, 1)]
        middle, *row_blocks = run(
            functools.partial(middle_kernel, n_tensor, experts),
            [((rows, width), F32)] + [((cap, width), BF16)] * experts,
            [ids, tokens, ln2_gain, ln2_bias, table] + heads_all + out_all,
            scratch=[
                ((n_tensor, rows, inner), BF16),
                ((n_tensor, inner, width), BF16),
                ((rows, width), BF16),
            ],
            micros=3,
        )
        rows_in = exchange(row_blocks)

        calls = [(0, 1), (2, 3)] if small_slice else [tuple(range(experts))]
        worked = []
        d_back, gated = [], []
        for call in calls:
            count = cap * len(call)
            results = run(
                functools.partial(expert_kernel, experts, len(call)),
                [((cap, width), BF16)] * (2 * len(call))
                + [((count, width), BF16)] * 2
                + [((count, hidden_width), BF16)] * 4
                + [((part_rows, width), F32)],
                [ids, up_a, up_b, down_a, down_b, router]
                + [rows_in[k] for k in call]
                + [d_rows_in[k] for k in call],
                scratch=[((count, width), F32)],
                micros=7,
            )
            d_back += results[: len(call)]
            gated += results[len(call) : 2 * len(call)]
            worked.append(results[2 * len(call) :])

        def collect(blocks, routers):
            kept, sent = run(
                functools.partial(combine_kernel, experts, len(routers), base),
                [((tall if routers else base, half), BF16)] * 2,
                [ids, table] + blocks + routers,
                scratch=[((tall if routers else base, width), F32)],
                micros=2,
            )
            return tensor_sum(kept, sent)

        d_home = exchange(d_back)

        fields = [[one[at] for one in worked] for at in (0, 4, 5, 2, 3, 1)]
        grad_own, grad_pair = run(
            functools.partial(weight_grad_kernel, len(worked)),
            [((2 * width, hidden_width), BF16)] * 2,
            [one for field in fields for one in field],
            micros=6,
            limit=24,
        )
        grad_kept, grad_sent = run(
            split_grad_kernel,
            [((width, width), F32), ((width, width), BF16)],
            [ids, grad_own, tensor_swap(grad_pair, 1)],
            scratch=[((2 * width, width), F32)],
            micros=2,
            limit=24,
        )
        grad_came = dp_swap(grad_sent)

        d_home = list(lax.optimization_barrier(tuple(d_home) + (grad_sent,))[:-1])
        own, other = collect(d_home, [one[6] for one in worked])

        parts = 4 if small_slice else 1
        d_middle, kept1, sent1, small2, *grad_blocks = run(
            functools.partial(back_kernel, parts),
            [((rows, width), F32)]
            + [((rows, half), BF16)] * 2
            + [((small_rows, width), F32)]
            + [((4 * inner // parts, width), BF16)] * parts,
            [
                ids, own, other, middle, cotangent, ln2_gain, w_out, head_out, normed, query,
                key, value, probs, weight,
            ],
            scratch=[((tall, width), F32), ((4 * inner, width), BF16)],
            micros=6,
        )

        own1, other1 = tensor_sum(kept1, sent1)
        grad_tokens, small = run(
            last_norm_kernel,
            [((rows, width), BF16), ((small_rows, width), F32)],
            [ids, own1, other1, tokens, d_middle, ln1_gain, small2],
            scratch=[((rows, width), F32)],
            micros=2,
        )
        if small_slice:
            arrived = [grad_blocks[0]] + [quarter_swap(grad_blocks[m], m) for m in (1, 2, 3)]
            size = grad_blocks[0].shape[0]
            (summed,) = run(
                functools.partial(sum_kernel, 4), [((size, width), BF16)], arrived, micros=1
            )
            (ready,) = run(
                pair_kernel,
                [((size + small_rows, width), BF16)],
                [summed, expert_swap(summed, 2), small, expert_swap(small, 2)],
                micros=1,
            )
            everything = [ready] + [quarter_swap(ready, m) for m in (1, 2, 3)]
            grad_qkv, grad_out, small_sum = run(
                functools.partial(spread_kernel, 4),
                [((3 * inner, width), F32), ((inner, width), F32), ((small_rows, width), F32)],
                [ids] + everything,
                scratch=[((4 * inner, width), F32), ((4, small_rows, width), F32)],
                micros=3,
            )
        else:
            grads = lax.psum(grad_blocks[0], ("expert", "dp")).astype(F32)
            grad_qkv, grad_out = grads[: 3 * inner], grads[3 * inner :]
            small_sum = lax.psum(small, ("expert", "dp"))

        grad_up, grad_down = run(
            join_grad_kernel,
            [((half, hidden_width), F32), ((hidden_width, half), F32)],
            [after(grad_kept, grad_blocks[0]), grad_came],
            micros=2,
        )

        gated = list(lax.optimization_barrier(tuple(gated) + tuple(d_home))[:experts])
        gated_home = exchange(gated)
        gated_home = list(lax.optimization_barrier(tuple(gated_home) + (d_middle,))[:-1])
        mix_own, mix_other = collect(gated_home, [])
        mixture = jnp.where(
            rank % 2 == 0,
            jnp.concatenate([mix_own, mix_other], axis=1),
            jnp.concatenate([mix_other, mix_own], axis=1),
        )[:rows].astype(F32)
        alive = (jnp.arange(rows, dtype=jnp.int32) < images_live[0] * SEQ)[:, None]
        out = jnp.where(alive, middle + mixture, 0.0).astype(BF16)
        return (
            out,
            grad_tokens,
            small_sum[0],
            small_sum[1],
            grad_qkv.reshape(3, inner, width).transpose(2, 0, 1),
            grad_out,
            small_sum[2],
            small_sum[3],
            small_sum[8 : 8 + experts].T,
            grad_up[None],
            grad_down[None],
        )

    return body


def solution(mesh):
    in_specs = (
        P(("expert", "dp"), None),
        P(("expert", "dp"), None),
        P(("expert", "dp")),
        P(),
        P(),
        P(None, None, "tensor"),
        P("tensor", None),
        P(),
        P(),
        P(),
        P("expert", None, "tensor"),
        P("expert", "tensor", None),
        P(("expert", "dp"), None),
    )
    out_specs = (
        P(("expert", "dp"), None),
        P(("expert", "dp"), None),
        P(),
        P(),
        P(None, None, "tensor"),
        P("tensor", None),
        P(),
        P(),
        P(),
        P("expert", "dp", "tensor"),
        P("expert", "tensor", "dp"),
    )
    body = make_body(mesh.shape["tensor"], mesh.shape["expert"], mesh.shape["dp"])
    return jax.shard_map(body, mesh=mesh, in_specs=in_specs, out_specs=out_specs, check_vma=False)
```

time: 239 us -> 203 us (0.85)
  starting transfers between devices: 85.5 us -> 53.2 us
  waiting for transfers between devices: 79.3 us -> 98.9 us
  local copies, waits for them, and re-layouts: 17.6 us -> 4.88 us
  Pallas kernels: 44.7 us -> 39.2 us
  other arithmetic: 9.1 us -> 4.26 us
    ppermute x12 -> x14, waiting for transfers between devices: 31.9 us -> 65.5 us  [expert_swap(): lax.ppermute(value, 'expert', [(i, i ^ mask) for i in range(n_expert)])]
    ppermute x14 -> x6, starting transfers between devices: 39.6 us -> 13.7 us  [quarter_swap(): return lax.ppermute(value, ('expert', 'dp'), pairs)]
    unnamed x55 -> x48, local copies, waits for them, and re-layouts: 14.9 us -> 3.57 us
    ppermute x21 -> x18, waiting for transfers between devices: 25.9 us -> 16 us  [tensor_swap(): lax.ppermute(value, 'tensor', [(i, i ^ mask) for i in range(n_tensor)])]
    pallas_call x14 -> x15, Pallas kernels: 44.7 us -> 39.2 us  [run(): pl.pallas_call(kernel, out_shape=[jax.ShapeDtypeStruct(shape, kind) for s...]
    ppermute x14 -> x6, waiting for transfers between devices: 21.5 us -> 17.4 us  [quarter_swap(): return lax.ppermute(value, ('expert', 'dp'), pairs)]
    add x5 -> x0, other arithmetic: 3.18 us -> none  [the longest x1 1.5 us: body(): up_sum = up_own.astype(F32) + tensor_swap(up_pair, 1).astype(F32)]
    ppermute x21 -> x18, starting transfers between devices: 14 us -> 10.9 us  [tensor_swap(): lax.ppermute(value, 'tensor', [(i, i ^ mask) for i in range(n_tensor)])]
  transfers between devices with their start and end apart: 49 -> 39, of which waited for: 19 -> 16; matrix products, arithmetic and copies ran while one was open for 5% -> 2% of each run, Pallas kernels for 18% -> 10%
where the time goes in v1:
time: 203 us; the launch traced here: 202 us
  waiting for transfers between devices  98.9 us (49%)
  starting transfers between devices  53.2 us (26%)
  Pallas kernels  39.2 us (19%)
  local copies, waits for them, and re-layouts  4.88 us (2%)
  other arithmetic  4.26 us (2%)
    ppermute x14, waiting for transfers between devices, expert_swap(): lax.ppermute(value, 'expert', [(i, i ^ mask) for i in range(n_expert)])  65.5 us
    pallas_call x15, Pallas kernels, run(): pl.pallas_call(kernel, out_shape=[jax.ShapeDtypeStruct(shape, kind) for s...  39.2 us
    ppermute x14, starting transfers between devices, expert_swap(): lax.ppermute(value, 'expert', [(i, i ^ mask) for i in range(n_expert)])  27 us
    ppermute x6, waiting for transfers between devices, quarter_swap(): return lax.ppermute(value, ('expert', 'dp'), pairs)  17.4 us
    ppermute x18, waiting for transfers between devices, tensor_swap(): lax.ppermute(value, 'tensor', [(i, i ^ mask) for i in range(n_tensor)])  16 us
    ppermute x6, starting transfers between devices, quarter_swap(): return lax.ppermute(value, ('expert', 'dp'), pairs)  13.7 us
    ppermute x18, starting transfers between devices, tensor_swap(): lax.ppermute(value, 'tensor', [(i, i ^ mask) for i in range(n_tensor)])  10.9 us
  transfers between devices with their start and end apart: 39, of which 16 were waited for; matrix products, arithmetic and copies ran while one was open for 2% of the time, Pallas kernels for 10%

profile of v1, /device:TPU:0, one launch (start us, length us, event | category | flops | bytes accessed | tf_op | source)
XLA Modules:
  0.0 202.3 jit_solution(6414771794183917396)
XLA Ops:
  0.6 0.5 collective-permute-start.1
  1.2 2.9 %collective-permute-start = (bf16[192,768]{1,0:T(8,128)(2,1)}, bf16[192,768]{1,0:T(8,128)(2,1)}, u32[]{:S(2)}, u32[]{:S(2)}) collective-permute-start(bf16[192,768]{1,0:T(8,128)(2,1)} %w_out.1), channel_id=1, source_target_pairs={{0,16},{8,24},{16,0},{24,8},{1,17},{9,25},{17,1},{25,9},{2,18},{10... | collective-permute-start | bytes 884744 | tf_op jit(solution)/shard_map/ppermute | solution.py:374
  4.9 1.1 copy-done.5
  6.0 0.7 copy-done.12
  6.7 0.7 copy-done.13
  7.4 1.4 shard_map.212
  8.9 2.5 %shard_map.213 = (bf16[394,768]{1,0:T(8,128)(2,1)S(1)}, bf16[394,192]{1,0:T(8,128)(2,1)S(1)}, bf16[394,192]{1,0:T(8,128)(2,1)S(1)}, bf16[394,192]{1,0:T(8,128)(2...) custom-call(bf16[394,768]{1,0:T(8,128)(2,1)S(1)} %copy-done.7, f32[768]{0:T(1024)S(1)} %copy-done.17, ...), custom_call_target="tpu_custom_call" | custom-call | flops 4600000000 | bytes 1024 | tf_op jit(solution)/shard_map/pallas_call | solution.py:357
  11.7 1.0 copy-done.2
  12.7 1.7 collective-permute-start.4
  14.5 0.5 collective-permute-start.7
  15.0 4.3 %collective-permute-done.4.rest_2_ = bf16[394,192]{1,0:T(8,128)(2,1)S(1)} collective-permute-done((bf16[394,192]{1,0:T(8,128)(2,1)S(1)}, bf16[394,192]{1,0:T(8,128)(2,1)S(1)}, u32[]{:S(2)}, u32[]{:S(2)}) %collective-permute-start.4) | collective-permute-done | bytes 151328 | tf_op jit(solution)/shard_map/ppermute | solution.py:374
  19.3 2.5 %collective-permute-start.12 = (bf16[144,768]{1,0:T(8,128)(2,1)S(1)}, bf16[144,768]{1,0:T(8,128)(2,1)S(1)}, u32[]{:S(2)}, u32[]{:S(2)}) collective-permute-start(bf16[144,768]{1,0:T(8,128)(2,1)S(1)} %get-tuple-element.108), channel_id=1, source_target_pairs={{0,4},{2,6},{4,0},{6,2},{1,5},{3,7},{5,1},{7,3},{8,12},{10,14},{12... | collective-permute-start | bytes 663560 | tf_op jit(solution)/shard_map/ppermute | solution.py:377
  21.8 1.4 collective-permute-start.13
  23.3 3.2 %shard_map.214 = (f32[394,768]{1,0:T(8,128)S(1)}, bf16[144,768]{1,0:T(8,128)(2,1)S(1)}, bf16[144,768]{1,0:T(8,128)(2,1)S(1)}, bf16[144,768]{1,0:T(8,128)(2,1)S(1)}, bf16[144,768]{1,0:T(8,128)(2,1)S(1)}) custom-call(s32[8]{0:T(128)S(1)} %stack.29.ids, bf16[394,768]{1,0:T(8,128)(2,1)S(1)} %copy-done.7, f32[768]{0:T(1024)S(1)} %copy-done.16, ...), custom_call_target="tpu_custom_call" | custom-call | flops 3449999872 | bytes 1024 | tf_op jit(solution)/shard_map/pallas_call | solution.py:357
  26.4 1.8 collective-permute-start.10
  28.2 1.1 collective-permute-start.11
  29.3 0.7 collective-permute-start.9
  30.0 17.4 %collective-permute-done.12.refs_2_ = bf16[144,768]{1,0:T(8,128)(2,1)S(1)} collective-permute-done((bf16[144,768]{1,0:T(8,128)(2,1)S(1)}, bf16[144,768]{1,0:T(8,128)(2,1)S(1)}, u32[]{:S(2)}, u32[]{:S(2)}) %collective-permute-start.12) | collective-permute-done | bytes 221216 | tf_op jit(solution)/shard_map/ppermute | solution.py:377
  47.7 9.3 %collective-permute-done.10.refs_0_ = bf16[144,768]{1,0:T(8,128)(2,1)S(1)} collective-permute-done((bf16[144,768]{1,0:T(8,128)(2,1)S(1)}, bf16[144,768]{1,0:T(8,128)(2,1)S(1)}, u32[]{:S(2)}, u32[]{:S(2)}) %collective-permute-start.10) | collective-permute-done | bytes 221216 | tf_op jit(solution)/shard_map/ppermute | solution.py:377
  57.0 4.5 %shard_map.216 = (bf16[144,768]{1,0:T(8,128)(2,1)S(1)}, bf16[144,768]{1,0:T(8,128)(2,1)S(1)}, bf16[144,768]{1,0:T(8,128)(2,1)S(1)}, bf16[144,768]{1,0:T(8,128)(2...) custom-call(s32[8]{0:T(128)S(1)} %stack.29.ids, ...), custom_call_target="tpu_custom_call" | custom-call | flops 8049999872 | bytes 1024 | tf_op jit(solution)/shard_map/pallas_call | solution.py:357
  61.5 4.8 %shard_map.215 = (bf16[144,768]{1,0:T(8,128)(2,1)S(1)}, bf16[144,768]{1,0:T(8,128)(2,1)S(1)}, bf16[144,768]{1,0:T(8,128)(2,1)S(1)}, bf16[144,768]{1,0:T(8,128)(2...) custom-call(s32[8]{0:T(128)S(1)} %stack.29.ids, ...), custom_call_target="tpu_custom_call" | custom-call | flops 8049999872 | bytes 1024 | tf_op jit(solution)/shard_map/pallas_call | solution.py:357
  66.3 5.1 %shard_map.217 = (bf16[1536,768]{1,0:T(8,128)(2,1)S(1)}, bf16[1536,768]{1,0:T(8,128)(2,1)S(1)}) custom-call(bf16[288,768]{1,0:T(8,128)(2,1)S(1)} %get-tuple-element.116.refs_0_, bf16[288,768]{1,0:T(8,128)(2,1)S(1)} %get-tuple-element.117.refs_1_, bf16[288,768]{1,0:T(8,128)(2,1)S(1)} %get-tuple-element.118.refs_2_, ...), custom_call_target="tpu_custom_call" | custom-call | flops 6899999744 | bytes 1024 | tf_op jit(solution)/shard_map/pallas_call | solution.py:357
  71.5 5.0 %collective-permute-start.14 = (bf16[144,768]{1,0:T(8,128)(2,1)S(1)}, bf16[144,768]{1,0:T(8,128)(2,1)S(1)}, u32[]{:S(2)}, u32[]{:S(2)}) collective-permute-start(bf16[144,768]{1,0:T(8,128)(2,1)S(1)} %get-tuple-element.113), channel_id=1, source_target_pairs={{0,2},{2,0},{4,6},{6,4},{1,3},{3,1},{5,7},{7,5},{8,10},{10,8},{12,... | collective-permute-start | bytes 663560 | tf_op jit(solution)/shard_map/ppermute | solution.py:377
  76.5 2.0 collective-permute-start.15
  78.5 1.4 collective-permute-start.16
  79.9 1.6 shard_map.218
  81.5 5.8 %collective-permute-done.14.refs_1_ = bf16[144,768]{1,0:T(8,128)(2,1)S(1)} collective-permute-done((bf16[144,768]{1,0:T(8,128)(2,1)S(1)}, bf16[144,768]{1,0:T(8,128)(2,1)S(1)}, u32[]{:S(2)}, u32[]{:S(2)}) %collective-permute-start.14) | collective-permute-done | bytes 221216 | tf_op jit(solution)/shard_map/ppermute | solution.py:377
  87.3 7.9 %collective-permute-done.16.refs_3_ = bf16[144,768]{1,0:T(8,128)(2,1)S(1)} collective-permute-done((bf16[144,768]{1,0:T(8,128)(2,1)S(1)}, bf16[144,768]{1,0:T(8,128)(2,1)S(1)}, u32[]{:S(2)}, u32[]{:S(2)}) %collective-permute-start.16) | collective-permute-done | bytes 221216 | tf_op jit(solution)/shard_map/ppermute | solution.py:377
  95.2 1.5 shard_map.219
  96.8 1.6 collective-permute-done.21
  98.5 1.6 collective-permute-start.22
  100.0 8.1 %collective-permute-done.22 = bf16[416,384]{1,0:T(8,128)(2,1)S(1)} collective-permute-done((bf16[416,384]{1,0:T(8,128)(2,1)S(1)}, bf16[416,384]{1,0:T(8,128)(2,1)S(1)}, u32[]{:S(2)}, u32[]{:S(2)}) %collective-permute-start.22) | collective-permute-done | bytes 319520 | tf_op jit(solution)/shard_map/ppermute | solution.py:374
  108.3 1.6 collective-permute-done.23.other
  109.9 4.7 %shard_map.220 = (f32[394,768]{1,0:T(8,128)S(1)}, bf16[394,384]{1,0:T(8,128)(2,1)S(1)}, bf16[394,384]{1,0:T(8,128)(2,1)S(1)}, f32[16,768]{1,0:T(8,128)S(1)}, bf1...) custom-call(s32[8]{0:T(128)S(1)} %stack.29.ids, ...), custom_call_target="tpu_custom_call" | custom-call | flops 6899999744 | bytes 1024 | tf_op jit(solution)/shard_map/pallas_call | solution.py:357
  114.8 4.5 %collective-permute-start.18 = (bf16[144,768]{1,0:T(8,128)(2,1)S(1)}, bf16[144,768]{1,0:T(8,128)(2,1)S(1)}, u32[]{:S(2)}, u32[]{:S(2)}) collective-permute-start(bf16[144,768]{1,0:T(8,128)(2,1)S(1)} %get-tuple-element.136), channel_id=1, source_target_pairs={{0,2},{2,0},{4,6},{6,4},{1,3},{3,1},{5,7},{7,5},{8,10},{10,8},{12,... | collective-permute-start | bytes 663560 | tf_op jit(solution)/shard_map/ppermute | solution.py:377
  119.4 1.9 collective-permute-start.19
  121.3 1.5 collective-permute-start.20
  122.7 1.5 collective-permute-start.38
  124.3 5.8 %collective-permute-done.18.refs_1_ = bf16[144,768]{1,0:T(8,128)(2,1)S(1)} collective-permute-done((bf16[144,768]{1,0:T(8,128)(2,1)S(1)}, bf16[144,768]{1,0:T(8,128)(2,1)S(1)}, u32[]{:S(2)}, u32[]{:S(2)}) %collective-permute-start.18) | collective-permute-done | bytes 221216 | tf_op jit(solution)/shard_map/ppermute | solution.py:377
  130.0 8.1 %collective-permute-done.19.refs_2_ = bf16[144,768]{1,0:T(8,128)(2,1)S(1)} collective-permute-done((bf16[144,768]{1,0:T(8,128)(2,1)S(1)}, bf16[144,768]{1,0:T(8,128)(2,1)S(1)}, u32[]{:S(2)}, u32[]{:S(2)}) %collective-permute-start.19) | collective-permute-done | bytes 221216 | tf_op jit(solution)/shard_map/ppermute | solution.py:377
  138.1 0.8 add_convert_fusion.3
  138.9 1.5 collective-permute-start.28
  140.4 2.4 %shard_map.221 = (bf16[400,384]{1,0:T(8,128)(2,1)S(1)}, bf16[400,384]{1,0:T(8,128)(2,1)}) custom-call(s32[8]{0:T(128)S(1)} %stack.29.ids, bf16[4,144,394]{2,1,0:T(8,128)(2,1)S(1)} %get-tuple-element.91.table, bf16[144,768]{1,0:T(8,128)(2,1)S(1)} %get-tuple-element.149.refs_0_, bf16[144,768]{1,0:T(8,128)(2,1)S(1)} %collective-permute-done.18.refs_1_, ...), custom_call_target="tpu_custom_call" | custom-call | flops 2300000000 | bytes 1024 | tf_op jit(solution)/shard_map/pallas_call | solution.py:357
  142.9 1.6 collective-permute-start.30
  144.5 4.4 %collective-permute-start.31 = (bf16[192,768]{1,0:T(8,128)(2,1)}, bf16[192,768]{1,0:T(8,128)(2,1)S(1)}, u32[]{:S(2)}, u32[]{:S(2)}) collective-permute-start(bf16[192,768]{1,0:T(8,128)(2,1)} %copy-done.10), channel_id=1, source_target_pairs={{0,2},{1,3},{2,0},{3,1},{4,6},{5,7},{6,4},{7,5},{8,10},{9,11},{10,... | collective-permute-start | bytes 884744 | tf_op jit(solution)/shard_map/ppermute | solution.py:384
  148.9 4.2 %collective-permute-start.32 = (bf16[192,768]{1,0:T(8,128)(2,1)}, bf16[192,768]{1,0:T(8,128)(2,1)S(1)}, u32[]{:S(2)}, u32[]{:S(2)}) collective-permute-start(bf16[192,768]{1,0:T(8,128)(2,1)} %copy-done.9), channel_id=1, source_target_pairs={{0,3},{1,2},{2,1},{3,0},{4,7},{5,6},{6,5},{7,4},{8,11},{9,10},{10,... | collective-permute-start | bytes 884744 | tf_op jit(solution)/shard_map/ppermute | solution.py:384
  153.1 1.1 add_convert_fusion.2.own
  154.3 1.0 add_convert_fusion.5
  155.4 7.7 %collective-permute-done.30.refs_1_ = bf16[192,768]{1,0:T(8,128)(2,1)S(1)} collective-permute-done((bf16[192,768]{1,0:T(8,128)(2,1)}, bf16[192,768]{1,0:T(8,128)(2,1)S(1)}, u32[]{:S(2)}, u32[]{:S(2)}) %collective-permute-start.30) | collective-permute-done | bytes 294944 | tf_op jit(solution)/shard_map/ppermute | solution.py:384
  163.0 1.5 collective-permute-start.25
  164.7 1.9 collective-permute-start.33
  166.6 2.4 %shard_map.222 = (bf16[394,768]{1,0:T(8,128)(2,1)}, f32[16,768]{1,0:T(8,128)S(1)}) custom-call(s32[8]{0:T(128)S(1)} %stack.29.ids, bf16[394,384]{1,0:T(8,128)(2,1)S(1)} %add_convert_fusion.2.own, bf16[394,384]{1,0:T(8,128)(2,1)S(1)} %collective-permute-done.29.other, bf16[394,768]{1,0:T(8,128)(2,1)S(1)} %copy-done.7, f32[394,768]{1,0:T(8,128)S(1)} %copy-done.23, ...), custom_call_target="tpu_custom_call" | custom-call | flops 2300000000 | bytes 1024 | tf_op jit(solution)/shard_map/pallas_call | solution.py:357
  169.0 1.1 collective-permute-start.34
  170.3 10.5 %collective-permute-done.33.came = bf16[192,768]{1,0:T(8,128)(2,1)S(1)} collective-permute-done((bf16[192,768]{1,0:T(8,128)(2,1)S(1)}, bf16[192,768]{1,0:T(8,128)(2,1)S(1)}, u32[]{:S(2)}, u32[]{:S(2)}) %collective-permute-start.33) | collective-permute-done | bytes 294944 | tf_op jit(solution)/shard_map/ppermute | solution.py:377
  180.7 0.8 collective-permute-done.34.small_came
  181.6 0.9 collective-permute-start.37
  182.5 2.2 %collective-permute-start.36 = (bf16[208,768]{1,0:T(8,128)(2,1)S(1)}, bf16[208,768]{1,0:T(8,128)(2,1)S(1)}, u32[]{:S(2)}, u32[]{:S(2)}) collective-permute-start(bf16[208,768]{1,0:T(8,128)(2,1)S(1)} %shard_map.224.refs_0_), channel_id=1, source_target_pairs={{0,2},{1,3},{2,0},{3,1},{4,6},{5,7},{6,4},{7,5},{8,10},{9,11},{10,... | collective-permute-start | bytes 958472 | tf_op jit(solution)/shard_map/ppermute | solution.py:384
  185.2 2.8 %shard_map.226 = (f32[384,768]{1,0:T(8,128)}, f32[768,384]{1,0:T(8,128)}) custom-call(f32[768,768]{1,0:T(8,128)S(1)} %copy-done.19, bf16[768,768]{1,0:T(8,128)(2,1)} %collective-permute-done.38.came), custom_call_target="tpu_custom_call" | custom-call | flops 2300000000 | bytes 1024 | tf_op jit(solution)/shard_map/pallas_call | solution.py:357
  188.0 1.0 select_convert_fusion
  189.0 4.0 %collective-permute-done.37.refs_3_ = bf16[208,768]{1,0:T(8,128)(2,1)S(1)} collective-permute-done((bf16[208,768]{1,0:T(8,128)(2,1)S(1)}, bf16[208,768]{1,0:T(8,128)(2,1)S(1)}, u32[]{:S(2)}, u32[]{:S(2)}) %collective-permute-start.37) | collective-permute-done | bytes 319520 | tf_op jit(solution)/shard_map/ppermute | solution.py:384
  193.0 5.8 %collective-permute-done.36.refs_2_ = bf16[208,768]{1,0:T(8,128)(2,1)S(1)} collective-permute-done((bf16[208,768]{1,0:T(8,128)(2,1)S(1)}, bf16[208,768]{1,0:T(8,128)(2,1)S(1)}, u32[]{:S(2)}, u32[]{:S(2)}) %collective-permute-start.36) | collective-permute-done | bytes 319520 | tf_op jit(solution)/shard_map/ppermute | solution.py:384
  198.8 2.2 %shard_map.225 = (f32[576,768]{1,0:T(8,128)}, f32[192,768]{1,0:T(8,128)}, f32[16,768]{1,0:T(8,128)S(1)}) custom-call(s32[8]{0:T(128)S(1)} %stack.29.ids, bf16[208,768]{1,0:T(8,128)(2,1)S(1)} %shard_map.224.refs_0_, bf16[208,768]{1,0:T(8,128)(2,1)S(1)} %collective-permute-done.35.refs_1_, bf16[208,768]{1,0:T(8,128)(2,1)S(1)} %collective-permute-done.36.refs_2_, ...), custom_call_target="tpu_custom_call" | custom-call | flops 3449999872 | bytes 1024 | tf_op jit(solution)/shard_map/pallas_call | solution.py:357
  201.0 0.6 slice_bitcast_fusion
  201.6 0.6 slice_reduce_fusion
  (88 shorter events, 2.6 us)
Async XLA Ops:
  0.6 11.1 %collective-permute-start.1 = (bf16[768,768]{1,0:T(8,128)(2,1)}, bf16[768,768]{1,0:T(8,128)(2,1)S(1)}, u32[]{:S(2)}, u32[]{:S(2)}) collective-permute-start(bf16[768,768]{1,0:T(8,128)(2,1)} %bitcast.21), channel_id=1, source_target_pairs={{0,8},{8,0},{16,24},{24,16},{1,9},{9,1},{17,25},{25,17},{2,10},{10... | collective-permute-start | bytes 3538952 | tf_op jit(solution)/shard_map/ppermute | solution.py:374
  1.2 10.6 %collective-permute-start.2 = (bf16[768,768]{1,0:T(8,128)(2,1)}, bf16[768,768]{1,0:T(8,128)(2,1)S(1)}, u32[]{:S(2)}, u32[]{:S(2)}) collective-permute-start(bf16[768,768]{1,0:T(8,128)(2,1)} %bitcast.24), channel_id=1, source_target_pairs={{0,8},{8,0},{16,24},{24,16},{1,9},{9,1},{17,25},{25,17},{2,10},{10... | collective-permute-start | bytes 3538952 | tf_op jit(solution)/shard_map/ppermute | solution.py:374
  1.2 10.5 %collective-permute-start = (bf16[192,768]{1,0:T(8,128)(2,1)}, bf16[192,768]{1,0:T(8,128)(2,1)}, u32[]{:S(2)}, u32[]{:S(2)}) collective-permute-start(bf16[192,768]{1,0:T(8,128)(2,1)} %w_out.1), channel_id=1, source_target_pairs={{0,16},{8,24},{16,0},{24,8},{1,17},{9,25},{17,1},{25,9},{2,18},{10... | collective-permute-start | bytes 884744 | tf_op jit(solution)/shard_map/ppermute | solution.py:374
  4.9 1.1 copy-start.5
  6.0 0.7 copy-start.12
  6.7 0.7 copy-start.13
  7.4 1.4 copy-start.4
  7.4 1.4 copy-start.7
  7.4 1.4 copy-start.14
  7.4 1.5 copy-start.17
  8.8 5.7 %copy-start.8 = (bf16[192,768]{1,0:T(8,128)(2,1)S(1)}, bf16[192,768]{1,0:T(8,128)(2,1)}, u32[]{:S(2)}) copy-start(bf16[192,768]{1,0:T(8,128)(2,1)} %w_out.1) | copy-start | bytes 884740
  8.8 14.4 %copy-start.15 = (f32[768]{0:T(1024)S(1)}, f32[768]{0:T(1024)}, u32[]{:S(2)}) copy-start(f32[768]{0:T(1024)} %bias.3) | copy-start | bytes 9220
  8.9 14.4 %copy-start.16 = (f32[768]{0:T(1024)S(1)}, f32[768]{0:T(1024)}, u32[]{:S(2)}) copy-start(f32[768]{0:T(1024)} %gain.6) | copy-start | bytes 9220
  11.7 1.0 copy-start.2
  12.7 6.5 %collective-permute-start.4 = (bf16[394,192]{1,0:T(8,128)(2,1)S(1)}, bf16[394,192]{1,0:T(8,128)(2,1)S(1)}, u32[]{:S(2)}, u32[]{:S(2)}) collective-permute-start(bf16[394,192]{1,0:T(8,128)(2,1)S(1)} %get-tuple-element.94.rest_0_.head_out), channel_id=1, source_target_pairs={{0,16},{8,24},{16,0},{24,8},{1,17},{9,25},{17,1},{25,9},{2,18},{10... | collective-permute-start | bytes 453896 | tf_op jit(solution)/shard_map/ppermute | solution.py:374
  14.5 7.3 %collective-permute-start.6 = (bf16[192,768]{1,0:T(8,128)(2,1)S(1)}, bf16[192,768]{1,0:T(8,128)(2,1)S(1)}, u32[]{:S(2)}, u32[]{:S(2)}) collective-permute-start(bf16[192,768]{1,0:T(8,128)(2,1)S(1)} %copy-done.8), channel_id=1, source_target_pairs={{0,8},{8,0},{16,24},{24,16},{1,9},{9,1},{17,25},{25,17},{2,10},{10... | collective-permute-start | bytes 884744 | tf_op jit(solution)/shard_map/ppermute | solution.py:374
  14.5 8.8 %collective-permute-start.7 = (bf16[192,768]{1,0:T(8,128)(2,1)}, bf16[192,768]{1,0:T(8,128)(2,1)S(1)}, u32[]{:S(2)}, u32[]{:S(2)}) collective-permute-start(bf16[192,768]{1,0:T(8,128)(2,1)} %collective-permute-done.rest_6_), channel_id=1, source_target_pairs={{0,8},{8,0},{16,24},{24,16},{1,9},{9,1},{17,25},{25,17},{2,10},{10... | collective-permute-start | bytes 884744 | tf_op jit(solution)/shard_map/ppermute | solution.py:374
  15.0 8.2 %collective-permute-start.3 = (bf16[394,192]{1,0:T(8,128)(2,1)S(1)}, bf16[394,192]{1,0:T(8,128)(2,1)S(1)}, u32[]{:S(2)}, u32[]{:S(2)}) collective-permute-start(bf16[394,192]{1,0:T(8,128)(2,1)S(1)} %get-tuple-element.94.rest_0_.head_out), channel_id=1, source_target_pairs={{0,8},{8,0},{16,24},{24,16},{1,9},{9,1},{17,25},{25,17},{2,10},{10... | collective-permute-start | bytes 453896 | tf_op jit(solution)/shard_map/ppermute | solution.py:374
  19.3 4.0 %collective-permute-start.5 = (bf16[394,192]{1,0:T(8,128)(2,1)S(1)}, bf16[394,192]{1,0:T(8,128)(2,1)S(1)}, u32[]{:S(2)}, u32[]{:S(2)}) collective-permute-start(bf16[394,192]{1,0:T(8,128)(2,1)S(1)} %collective-permute-done.4.rest_2_), channel_id=1, source_target_pairs={{0,8},{8,0},{16,24},{24,16},{1,9},{9,1},{17,25},{25,17},{2,10},{10... | collective-permute-start | bytes 453896 | tf_op jit(solution)/shard_map/ppermute | solution.py:374
  19.3 28.1 %collective-permute-start.12 = (bf16[144,768]{1,0:T(8,128)(2,1)S(1)}, bf16[144,768]{1,0:T(8,128)(2,1)S(1)}, u32[]{:S(2)}, u32[]{:S(2)}) collective-permute-start(bf16[144,768]{1,0:T(8,128)(2,1)S(1)} %get-tuple-element.108), channel_id=1, source_target_pairs={{0,4},{2,6},{4,0},{6,2},{1,5},{3,7},{5,1},{7,3},{8,12},{10,14},{12... | collective-permute-start | bytes 663560 | tf_op jit(solution)/shard_map/ppermute | solution.py:377
  21.8 35.1 %copy-start = (bf16[1,768,768]{2,1,0:T(8,128)(2,1)S(1)}, bf16[1,768,768]{2,1,0:T(8,128)(2,1)}, u32[]{:S(2)}) copy-start(bf16[1,768,768]{2,1,0:T(8,128)(2,1)} %param.23) | copy-start | bytes 3538948
  21.8 35.1 %copy-start.1 = (bf16[1,768,768]{2,1,0:T(8,128)(2,1)S(1)}, bf16[1,768,768]{2,1,0:T(8,128)(2,1)}, u32[]{:S(2)}) copy-start(bf16[1,768,768]{2,1,0:T(8,128)(2,1)} %param.24) | copy-start | bytes 3538948
  21.8 35.1 %copy-start.3 = (bf16[768,768]{1,0:T(8,128)(2,1)S(1)}, bf16[768,768]{1,0:T(8,128)(2,1)}, u32[]{:S(2)}) copy-start(bf16[768,768]{1,0:T(8,128)(2,1)} %copy-done.2) | copy-start | bytes 3538948
  21.8 25.9 %collective-permute-start.13 = (bf16[144,768]{1,0:T(8,128)(2,1)S(1)}, bf16[144,768]{1,0:T(8,128)(2,1)S(1)}, u32[]{:S(2)}, u32[]{:S(2)}) collective-permute-start(bf16[144,768]{1,0:T(8,128)(2,1)S(1)} %get-tuple-element.109), channel_id=1, source_target_pairs={{0,6},{2,4},{4,2},{6,0},{1,7},{3,5},{5,3},{7,1},{8,14},{10,12},{12... | collective-permute-start | bytes 663560 | tf_op jit(solution)/shard_map/ppermute | solution.py:377
  26.4 30.5 %collective-permute-start.10 = (bf16[144,768]{1,0:T(8,128)(2,1)S(1)}, bf16[144,768]{1,0:T(8,128)(2,1)S(1)}, u32[]{:S(2)}, u32[]{:S(2)}) collective-permute-start(bf16[144,768]{1,0:T(8,128)(2,1)S(1)} %get-tuple-element.106), channel_id=1, source_target_pairs={{0,4},{2,6},{4,0},{6,2},{1,5},{3,7},{5,1},{7,3},{8,12},{10,14},{12... | collective-permute-start | bytes 663560 | tf_op jit(solution)/shard_map/ppermute | solution.py:377
  28.2 28.8 %collective-permute-start.11 = (bf16[144,768]{1,0:T(8,128)(2,1)S(1)}, bf16[144,768]{1,0:T(8,128)(2,1)S(1)}, u32[]{:S(2)}, u32[]{:S(2)}) collective-permute-start(bf16[144,768]{1,0:T(8,128)(2,1)S(1)} %get-tuple-element.107), channel_id=1, source_target_pairs={{0,6},{2,4},{4,2},{6,0},{1,7},{3,5},{5,3},{7,1},{8,14},{10,12},{12... | collective-permute-start | bytes 663560 | tf_op jit(solution)/shard_map/ppermute | solution.py:377
  29.3 32.2 %collective-permute-start.9 = (bf16[144,768]{1,0:T(8,128)(2,1)S(1)}, bf16[144,768]{1,0:T(8,128)(2,1)S(1)}, u32[]{:S(2)}, u32[]{:S(2)}) collective-permute-start(bf16[144,768]{1,0:T(8,128)(2,1)S(1)} %get-tuple-element.103), channel_id=1, source_target_pairs={{0,2},{2,0},{4,6},{6,4},{1,3},{3,1},{5,7},{7,5},{8,10},{10,8},{12,... | collective-permute-start | bytes 663560 | tf_op jit(solution)/shard_map/ppermute | solution.py:377
  47.4 14.1 %collective-permute-start.8 = (bf16[144,768]{1,0:T(8,128)(2,1)S(1)}, bf16[144,768]{1,0:T(8,128)(2,1)S(1)}, u32[]{:S(2)}, u32[]{:S(2)}) collective-permute-start(bf16[144,768]{1,0:T(8,128)(2,1)S(1)} %get-tuple-element.101), channel_id=1, source_target_pairs={{0,2},{2,0},{4,6},{6,4},{1,3},{3,1},{5,7},{7,5},{8,10},{10,8},{12,... | collective-permute-start | bytes 663560 | tf_op jit(solution)/shard_map/ppermute | solution.py:377
  71.4 8.5 %collective-permute-start.17 = (bf16[1536,768]{1,0:T(8,128)(2,1)S(1)}, bf16[1536,768]{1,0:T(8,128)(2,1)S(1)}, u32[]{:S(2)}, u32[]{:S(2)}) collective-permute-start(bf16[1536,768]{1,0:T(8,128)(2,1)S(1)} %get-tuple-element.129), channel_id=1, source_target_pairs={{0,8},{8,0},{16,24},{24,16},{1,9},{9,1},{17,25},{25,17},{2,10},{10... | collective-permute-start | bytes 7077896 | tf_op jit(solution)/shard_map/ppermute | solution.py:374
  71.5 15.8 %collective-permute-start.14 = (bf16[144,768]{1,0:T(8,128)(2,1)S(1)}, bf16[144,768]{1,0:T(8,128)(2,1)S(1)}, u32[]{:S(2)}, u32[]{:S(2)}) collective-permute-start(bf16[144,768]{1,0:T(8,128)(2,1)S(1)} %get-tuple-element.113), channel_id=1, source_target_pairs={{0,2},{2,0},{4,6},{6,4},{1,3},{3,1},{5,7},{7,5},{8,10},{10,8},{12,... | collective-permute-start | bytes 663560 | tf_op jit(solution)/shard_map/ppermute | solution.py:377
  76.5 10.8 %collective-permute-start.15 = (bf16[144,768]{1,0:T(8,128)(2,1)S(1)}, bf16[144,768]{1,0:T(8,128)(2,1)S(1)}, u32[]{:S(2)}, u32[]{:S(2)}) collective-permute-start(bf16[144,768]{1,0:T(8,128)(2,1)S(1)} %get-tuple-element.114), channel_id=1, source_target_pairs={{0,4},{2,6},{4,0},{6,2},{1,5},{3,7},{5,1},{7,3},{8,12},{10,14},{12... | collective-permute-start | bytes 663560 | tf_op jit(solution)/shard_map/ppermute | solution.py:377
  78.5 16.7 %collective-permute-start.16 = (bf16[144,768]{1,0:T(8,128)(2,1)S(1)}, bf16[144,768]{1,0:T(8,128)(2,1)S(1)}, u32[]{:S(2)}, u32[]{:S(2)}) collective-permute-start(bf16[144,768]{1,0:T(8,128)(2,1)S(1)} %get-tuple-element.115), channel_id=1, source_target_pairs={{0,6},{2,4},{4,2},{6,0},{1,7},{3,5},{5,3},{7,1},{8,14},{10,12},{12... | collective-permute-start | bytes 663560 | tf_op jit(solution)/shard_map/ppermute | solution.py:377
  81.4 15.2 %copy-start.18 = (f32[768,768]{1,0:T(8,128)}, f32[768,768]{1,0:T(8,128)S(1)}, u32[]{:S(2)}) copy-start(f32[768,768]{1,0:T(8,128)S(1)} %get-tuple-element.168.kept) | copy-start | bytes 7077892
  96.7 13.2 %copy-start.6 = (bf16[394,768]{1,0:T(8,128)(2,1)S(1)}, bf16[394,768]{1,0:T(8,128)(2,1)}, u32[]{:S(2)}) copy-start(bf16[394,768]{1,0:T(8,128)(2,1)} %cot.3) | copy-start | bytes 1815556
  96.7 1.7 collective-permute-start.21
  98.5 9.6 %collective-permute-start.22 = (bf16[416,384]{1,0:T(8,128)(2,1)S(1)}, bf16[416,384]{1,0:T(8,128)(2,1)S(1)}, u32[]{:S(2)}, u32[]{:S(2)}) collective-permute-start(bf16[416,384]{1,0:T(8,128)(2,1)S(1)} %add_convert_fusion.1), channel_id=1, source_target_pairs={{0,16},{8,24},{16,0},{24,8},{1,17},{9,25},{17,1},{25,9},{2,18},{10... | collective-permute-start | bytes 958472 | tf_op jit(solution)/shard_map/ppermute | solution.py:374
  108.2 1.7 collective-permute-start.23
  114.6 28.2 %copy-start.9 = (bf16[192,768]{1,0:T(8,128)(2,1)}, bf16[192,768]{1,0:T(8,128)(2,1)S(1)}, u32[]{:S(2)}) copy-start(bf16[192,768]{1,0:T(8,128)(2,1)S(1)} %get-tuple-element.162) | copy-start | bytes 884740
  114.6 28.2 %copy-start.10 = (bf16[192,768]{1,0:T(8,128)(2,1)}, bf16[192,768]{1,0:T(8,128)(2,1)S(1)}, u32[]{:S(2)}) copy-start(bf16[192,768]{1,0:T(8,128)(2,1)S(1)} %get-tuple-element.161) | copy-start | bytes 884740
  114.6 28.2 %copy-start.11 = (bf16[192,768]{1,0:T(8,128)(2,1)}, bf16[192,768]{1,0:T(8,128)(2,1)S(1)}, u32[]{:S(2)}) copy-start(bf16[192,768]{1,0:T(8,128)(2,1)S(1)} %get-tuple-element.160) | copy-start | bytes 884740
  114.6 28.2 %copy-start.20 = (bf16[192,768]{1,0:T(8,128)(2,1)}, bf16[192,768]{1,0:T(8,128)(2,1)S(1)}, u32[]{:S(2)}) copy-start(bf16[192,768]{1,0:T(8,128)(2,1)S(1)} %get-tuple-element.159.refs_0_) | copy-start | bytes 884740
  114.6 28.2 %copy-start.22 = (f32[394,768]{1,0:T(8,128)}, f32[394,768]{1,0:T(8,128)S(1)}, u32[]{:S(2)}) copy-start(f32[394,768]{1,0:T(8,128)S(1)} %get-tuple-element.148.d_middle) | copy-start | bytes 3631108
  114.6 23.4 %collective-permute-start.27 = (bf16[394,384]{1,0:T(8,128)(2,1)S(1)}, bf16[394,384]{1,0:T(8,128)(2,1)S(1)}, u32[]{:S(2)}, u32[]{:S(2)}) collective-permute-start(bf16[394,384]{1,0:T(8,128)(2,1)S(1)} %get-tuple-element.156), channel_id=1, source_target_pairs={{0,8},{8,0},{16,24},{24,16},{1,9},{9,1},{17,25},{25,17},{2,10},{10... | collective-permute-start | bytes 907784 | tf_op jit(solution)/shard_map/ppermute | solution.py:374
  114.8 15.2 %collective-permute-start.18 = (bf16[144,768]{1,0:T(8,128)(2,1)S(1)}, bf16[144,768]{1,0:T(8,128)(2,1)S(1)}, u32[]{:S(2)}, u32[]{:S(2)}) collective-permute-start(bf16[144,768]{1,0:T(8,128)(2,1)S(1)} %get-tuple-element.136), channel_id=1, source_target_pairs={{0,2},{2,0},{4,6},{6,4},{1,3},{3,1},{5,7},{7,5},{8,10},{10,8},{12,... | collective-permute-start | bytes 663560 | tf_op jit(solution)/shard_map/ppermute | solution.py:377
  119.4 18.7 %collective-permute-start.19 = (bf16[144,768]{1,0:T(8,128)(2,1)S(1)}, bf16[144,768]{1,0:T(8,128)(2,1)S(1)}, u32[]{:S(2)}, u32[]{:S(2)}) collective-permute-start(bf16[144,768]{1,0:T(8,128)(2,1)S(1)} %get-tuple-element.137), channel_id=1, source_target_pairs={{0,4},{2,6},{4,0},{6,2},{1,5},{3,7},{5,1},{7,3},{8,12},{10,14},{12... | collective-permute-start | bytes 663560 | tf_op jit(solution)/shard_map/ppermute | solution.py:377
  121.3 16.8 %collective-permute-start.20 = (bf16[144,768]{1,0:T(8,128)(2,1)S(1)}, bf16[144,768]{1,0:T(8,128)(2,1)S(1)}, u32[]{:S(2)}, u32[]{:S(2)}) collective-permute-start(bf16[144,768]{1,0:T(8,128)(2,1)S(1)} %get-tuple-element.138), channel_id=1, source_target_pairs={{0,6},{2,4},{4,2},{6,0},{1,7},{3,5},{5,3},{7,1},{8,14},{10,12},{12... | collective-permute-start | bytes 663560 | tf_op jit(solution)/shard_map/ppermute | solution.py:377
  122.7 62.4 %collective-permute-start.38 = (bf16[768,768]{1,0:T(8,128)(2,1)S(1)}, bf16[768,768]{1,0:T(8,128)(2,1)}, u32[]{:S(2)}, u32[]{:S(2)}) collective-permute-start(bf16[768,768]{1,0:T(8,128)(2,1)S(1)} %get-tuple-element.130), channel_id=1, source_target_pairs={{0,1},{1,0},{2,3},{3,2},{4,5},{5,4},{6,7},{7,6},{8,9},{9,8},{10,11... | collective-permute-start | bytes 3538952 | tf_op jit(solution)/shard_map/ppermute | solution.py:380
  138.9 10.1 %collective-permute-start.28 = (bf16[394,384]{1,0:T(8,128)(2,1)}, bf16[394,384]{1,0:T(8,128)(2,1)}, u32[]{:S(2)}, u32[]{:S(2)}) collective-permute-start(bf16[394,384]{1,0:T(8,128)(2,1)} %add_convert_fusion.3), channel_id=1, source_target_pairs={{0,16},{8,24},{16,0},{24,8},{1,17},{9,25},{17,1},{25,9},{2,18},{10... | collective-permute-start | bytes 907784 | tf_op jit(solution)/shard_map/ppermute | solution.py:374
  142.8 11.4 %collective-permute-start.24 = (bf16[400,384]{1,0:T(8,128)(2,1)}, bf16[400,384]{1,0:T(8,128)(2,1)}, u32[]{:S(2)}, u32[]{:S(2)}) collective-permute-start(bf16[400,384]{1,0:T(8,128)(2,1)} %get-tuple-element.154), channel_id=1, source_target_pairs={{0,8},{8,0},{16,24},{24,16},{1,9},{9,1},{17,25},{25,17},{2,10},{10... | collective-permute-start | bytes 921608 | tf_op jit(solution)/shard_map/ppermute | solution.py:374
  142.9 21.6 %copy-start.21 = (bf16[192,768]{1,0:T(8,128)(2,1)S(1)}, bf16[192,768]{1,0:T(8,128)(2,1)}, u32[]{:S(2)}) copy-start(bf16[192,768]{1,0:T(8,128)(2,1)} %copy-done.20) | copy-start | bytes 884740
  142.9 20.1 %collective-permute-start.30 = (bf16[192,768]{1,0:T(8,128)(2,1)}, bf16[192,768]{1,0:T(8,128)(2,1)S(1)}, u32[]{:S(2)}, u32[]{:S(2)}) collective-permute-start(bf16[192,768]{1,0:T(8,128)(2,1)} %copy-done.11), channel_id=1, source_target_pairs={{0,1},{1,0},{2,3},{3,2},{4,5},{5,4},{6,7},{7,6},{8,9},{9,8},{10,11... | collective-permute-start | bytes 884744 | tf_op jit(solution)/shard_map/ppermute | solution.py:384
  144.5 20.0 %collective-permute-start.31 = (bf16[192,768]{1,0:T(8,128)(2,1)}, bf16[192,768]{1,0:T(8,128)(2,1)S(1)}, u32[]{:S(2)}, u32[]{:S(2)}) collective-permute-start(bf16[192,768]{1,0:T(8,128)(2,1)} %copy-done.10), channel_id=1, source_target_pairs={{0,2},{1,3},{2,0},{3,1},{4,6},{5,7},{6,4},{7,5},{8,10},{9,11},{10,... | collective-permute-start | bytes 884744 | tf_op jit(solution)/shard_map/ppermute | solution.py:384
  148.9 15.6 %collective-permute-start.32 = (bf16[192,768]{1,0:T(8,128)(2,1)}, bf16[192,768]{1,0:T(8,128)(2,1)S(1)}, u32[]{:S(2)}, u32[]{:S(2)}) collective-permute-start(bf16[192,768]{1,0:T(8,128)(2,1)} %copy-done.9), channel_id=1, source_target_pairs={{0,3},{1,2},{2,1},{3,0},{4,7},{5,6},{6,5},{7,4},{8,11},{9,10},{10,... | collective-permute-start | bytes 884744 | tf_op jit(solution)/shard_map/ppermute | solution.py:384
  154.2 12.4 %collective-permute-start.29 = (bf16[394,384]{1,0:T(8,128)(2,1)S(1)}, bf16[394,384]{1,0:T(8,128)(2,1)S(1)}, u32[]{:S(2)}, u32[]{:S(2)}) collective-permute-start(bf16[394,384]{1,0:T(8,128)(2,1)S(1)} %add_convert_fusion.2.own), channel_id=1, source_target_pairs={{0,8},{8,0},{16,24},{24,16},{1,9},{9,1},{17,25},{25,17},{2,10},{10... | collective-permute-start | bytes 907784 | tf_op jit(solution)/shard_map/ppermute | solution.py:374
  155.4 11.2 %copy-start.23 = (f32[394,768]{1,0:T(8,128)S(1)}, f32[394,768]{1,0:T(8,128)}, u32[]{:S(2)}) copy-start(f32[394,768]{1,0:T(8,128)} %copy-done.22) | copy-start | bytes 3631108
  163.0 7.1 %collective-permute-start.25 = (bf16[400,384]{1,0:T(8,128)(2,1)S(1)}, bf16[400,384]{1,0:T(8,128)(2,1)S(1)}, u32[]{:S(2)}, u32[]{:S(2)}) collective-permute-start(bf16[400,384]{1,0:T(8,128)(2,1)S(1)} %add_convert_fusion.5), channel_id=1, source_target_pairs={{0,16},{8,24},{16,0},{24,8},{1,17},{9,25},{17,1},{25,9},{2,18},{10... | collective-permute-start | bytes 921608 | tf_op jit(solution)/shard_map/ppermute | solution.py:374
  164.7 16.0 %collective-permute-start.33 = (bf16[192,768]{1,0:T(8,128)(2,1)S(1)}, bf16[192,768]{1,0:T(8,128)(2,1)S(1)}, u32[]{:S(2)}, u32[]{:S(2)}) collective-permute-start(bf16[192,768]{1,0:T(8,128)(2,1)S(1)} %shard_map.223.own), channel_id=1, source_target_pairs={{0,4},{2,6},{4,0},{6,2},{1,5},{3,7},{5,1},{7,3},{8,12},{10,14},{12... | collective-permute-start | bytes 884744 | tf_op jit(solution)/shard_map/ppermute | solution.py:377
  169.0 12.5 %collective-permute-start.34 = (f32[16,768]{1,0:T(8,128)S(1)}, f32[16,768]{1,0:T(8,128)S(1)}, u32[]{:S(2)}, u32[]{:S(2)}) collective-permute-start(f32[16,768]{1,0:T(8,128)S(1)} %get-tuple-element.163.small), channel_id=1, source_target_pairs={{0,4},{2,6},{4,0},{6,2},{1,5},{3,7},{5,1},{7,3},{8,12},{10,14},{12... | collective-permute-start | bytes 147464 | tf_op jit(solution)/shard_map/ppermute | solution.py:377
  170.2 15.0 %copy-start.19 = (f32[768,768]{1,0:T(8,128)S(1)}, f32[768,768]{1,0:T(8,128)}, u32[]{:S(2)}) copy-start(f32[768,768]{1,0:T(8,128)} %copy-done.18) | copy-start | bytes 7077892
  170.2 17.8 %collective-permute-start.26 = (bf16[400,384]{1,0:T(8,128)(2,1)S(1)}, bf16[400,384]{1,0:T(8,128)(2,1)S(1)}, u32[]{:S(2)}, u32[]{:S(2)}) collective-permute-start(bf16[400,384]{1,0:T(8,128)(2,1)S(1)} %add_convert_fusion.4), channel_id=1, source_target_pairs={{0,8},{8,0},{16,24},{24,16},{1,9},{9,1},{17,25},{25,17},{2,10},{10... | collective-permute-start | bytes 921608 | tf_op jit(solution)/shard_map/ppermute | solution.py:374
  181.6 11.4 %collective-permute-start.37 = (bf16[208,768]{1,0:T(8,128)(2,1)S(1)}, bf16[208,768]{1,0:T(8,128)(2,1)S(1)}, u32[]{:S(2)}, u32[]{:S(2)}) collective-permute-start(bf16[208,768]{1,0:T(8,128)(2,1)S(1)} %shard_map.224.refs_0_), channel_id=1, source_target_pairs={{0,3},{1,2},{2,1},{3,0},{4,7},{5,6},{6,5},{7,4},{8,11},{9,10},{10,... | collective-permute-start | bytes 958472 | tf_op jit(solution)/shard_map/ppermute | solution.py:384
  182.5 16.3 %collective-permute-start.36 = (bf16[208,768]{1,0:T(8,128)(2,1)S(1)}, bf16[208,768]{1,0:T(8,128)(2,1)S(1)}, u32[]{:S(2)}, u32[]{:S(2)}) collective-permute-start(bf16[208,768]{1,0:T(8,128)(2,1)S(1)} %shard_map.224.refs_0_), channel_id=1, source_target_pairs={{0,2},{1,3},{2,0},{3,1},{4,6},{5,7},{6,4},{7,5},{8,10},{9,11},{10,... | collective-permute-start | bytes 958472 | tf_op jit(solution)/shard_map/ppermute | solution.py:384
  184.6 14.2 %collective-permute-start.35 = (bf16[208,768]{1,0:T(8,128)(2,1)S(1)}, bf16[208,768]{1,0:T(8,128)(2,1)S(1)}, u32[]{:S(2)}, u32[]{:S(2)}) collective-permute-start(bf16[208,768]{1,0:T(8,128)(2,1)S(1)} %shard_map.224.refs_0_), channel_id=1, source_target_pairs={{0,1},{1,0},{2,3},{3,2},{4,5},{5,4},{6,7},{7,6},{8,9},{9,8},{10,11... | collective-permute-start | bytes 958472 | tf_op jit(solution)/shard_map/ppermute | solution.py:384

commit v2 on v1

--- a/solution.py
+++ b/solution.py
@@ -68,7 +68,7 @@
 T_ID, C_ID, E_ID, D_ID, Q_ID, L_ID = range(6)
 
 
-def plan_kernel(experts, ids, routes, cot, router, table, router_pad, *blocks):
+def plan_kernel(experts, ids, routes, cot, router, table, part, router_pad, *blocks):
     rows = cot.shape[0]
     cap = table.shape[1]
     tall = max(16, -(-experts // 16) * 16)
@@ -86,8 +86,14 @@
     place = iota((cap, rows), 0).astype(F32)
     for x in range(experts):
         table[x] = jnp.where(slot[x : x + 1, :] == place, 1.0, 0.0).astype(BF16)
+    quarter = part.shape[1]
+    first = ((ids[T_ID] // 2) * quarter).astype(F32)
+    place = iota((quarter, rows), 0).astype(F32) + first
+    for x in range(experts):
+        part[x] = jnp.where(slot[x : x + 1, :] == place, 1.0, 0.0).astype(BF16)
     for k in range(experts):
-        blocks[k][...] = dot_nn(table[ids[E_ID] ^ k], cot[...]).astype(BF16)
+        source = table if blocks[k].shape[0] == cap else part
+        blocks[k][...] = dot_nn(source[ids[E_ID] ^ k], cot[...]).astype(BF16)
     router_pad[...] = jnp.zeros_like(router_pad)
     router_pad[:experts, :] = router[...]
 
@@ -137,16 +143,29 @@
         blocks[k][...] = dot_nn(table[ids[E_ID] ^ k], low[...]).astype(BF16)
 
 
-def expert_kernel(experts, number, ids, up_a, up_b, down_a, down_b, router, *refs):
+def expert_kernel(
+    experts, places, with_grads, ids, up_a, up_b, down_a, down_b, router, pair_out, *refs
+):
+    number = len(places)
     row_blocks, out_blocks = refs[:number], refs[number : 2 * number]
     refs = refs[2 * number :]
-    back_blocks, gated_blocks = refs[:number], refs[number : 2 * number]
-    rows_in, d_result, hidden_a, hidden_b, d_pre_a, d_pre_b, router_part, d_out = refs[2 * number :]
+    back_blocks, gated_kept, gated_sent = refs[:number], refs[number], refs[number + 1]
+    refs = refs[number + 2 :]
+    rows_in, d_result, hidden_a, hidden_b, d_pre_a, d_pre_b, router_part = refs[:7]
+    d_out = refs[-1]
     size = row_blocks[0].shape[0]
     count = size * number
+    far = ids[T_ID] // 2
     for k in range(number):
         rows_in[k * size : (k + 1) * size, :] = row_blocks[k][...]
-        d_out[k * size : (k + 1) * size, :] = out_blocks[k][...].astype(F32)
+        quarter = out_blocks[k].shape[0]
+        if quarter == size:
+            d_out[k * size : (k + 1) * size, :] = out_blocks[k][...].astype(F32)
+        else:
+            here = pl.multiple_of(k * size + far * quarter, 8)
+            there = pl.multiple_of(k * size + (1 - far) * quarter, 8)
+            d_out[pl.ds(here, quarter), :] = out_blocks[k][...].astype(F32)
+            d_out[pl.ds(there, quarter), :] = pair_out[places[k] - 1].astype(F32)
     lane = iota((count, LANES), 1)
     logits = dot_nt(rows_in[...], router[...])
     logits = jnp.where(lane < experts, logits, -1e30)
@@ -177,46 +196,78 @@
     d_gate = jnp.sum(d_out[...] * result, axis=-1, keepdims=True)
     d_logits = (d_gate * gate * (mine - odds)).astype(BF16)
     back = (back + dot_nn(d_logits, router[...])).astype(BF16)
-    gated = (gate * result).astype(BF16)
     for k in range(number):
         back_blocks[k][...] = back[k * size : (k + 1) * size, :]
-        gated_blocks[k][...] = gated[k * size : (k + 1) * size, :]
+    d_out[...] = gate * result
+    quarter = gated_kept.shape[1]
+    for k in range(number):
+        if quarter == size:
+            gated_kept[k] = d_out[k * size : (k + 1) * size, :].astype(BF16)
+        else:
+            here = pl.multiple_of(k * size + far * quarter, 8)
+            there = pl.multiple_of(k * size + (1 - far) * quarter, 8)
+            gated_kept[k] = d_out[pl.ds(here, quarter), :].astype(BF16)
+            gated_sent[k] = d_out[pl.ds(there, quarter), :].astype(BF16)
+    if quarter == size:
+        gated_sent[...] = jnp.zeros_like(gated_sent)
     router_part[...] = dot_tn(d_logits, rows_in[...])[: router_part.shape[0]]
-
-
-def weight_grad_kernel(count, *refs):
-    rows = refs[:count]
-    d_pre_a = refs[count : 2 * count]
-    d_pre_b = refs[2 * count : 3 * count]
-    hidden_a = refs[3 * count : 4 * count]
-    hidden_b = refs[4 * count : 5 * count]
-    d_result = refs[5 * count : 6 * count]
-    own, pair = refs[6 * count :]
+    if with_grads:
+        own, pair = refs[7:9]
+        weight_grads(rows_in, d_pre_a, d_pre_b, hidden_a, hidden_b, d_result, None, None, own, pair)
+
+
+def weight_grads(
+    rows, d_pre_a, d_pre_b, hidden_a, hidden_b, d_result, own_before, pair_before, own, pair
+):
     width = own.shape[0] // 2
-    for out, at, lefts, rights in (
-        (pair, 0, rows, d_pre_b),
-        (pair, width, hidden_b, d_result),
-        (own, 0, rows, d_pre_a),
-        (own, width, hidden_a, d_result),
+    for out, before, at, left, right in (
+        (pair, pair_before, 0, rows, d_pre_b),
+        (pair, pair_before, width, hidden_b, d_result),
+        (own, own_before, 0, rows, d_pre_a),
+        (own, own_before, width, hidden_a, d_result),
     ):
-        total = dot_tn(lefts[0][...], rights[0][...])
-        for k in range(1, count):
-            total = total + dot_tn(lefts[k][...], rights[k][...])
+        total = dot_tn(left[...], right[...])
+        if before is not None:
+            total = total + before[at : at + width, :].astype(F32)
         out[at : at + width, :] = total.astype(BF16)
 
 
-def split_grad_kernel(ids, own, came, kept, sent, total):
+def gated_sum_kernel(kept_a, came_a, kept_b, came_b, *blocks):
+    for k in range(4):
+        kept, came = (kept_a, came_a) if k < 2 else (kept_b, came_b)
+        blocks[k][...] = (kept[k % 2].astype(F32) + came[k % 2].astype(F32)).astype(BF16)
+
+
+def weight_grad_kernel(*refs):
+    rows, d_pre_a, d_pre_b, hidden_a, hidden_b, d_result = refs[:6]
+    own_before, pair_before = refs[6:8] if len(refs) == 10 else (None, None)
+    weight_grads(
+        rows, d_pre_a, d_pre_b, hidden_a, hidden_b, d_result, own_before, pair_before, *refs[-2:]
+    )
+
+
+def split_grad_kernel(ids, own, came, kept, sent_first, sent_rest, total, sent):
     total[...] = own[...].astype(F32) + came[...].astype(F32)
     width = own.shape[1]
     half = width // 2
-    for out, which in ((kept, ids[D_ID]), (sent, 1 - ids[D_ID])):
-        out[:half, :] = total[pl.ds(pl.multiple_of(which * half, 16), half), :].astype(out.dtype)
-        column = pl.ds(pl.multiple_of(which * half, LANES), half)
-        out[half:, :half] = total[width : width + half, column].astype(out.dtype)
-        out[half:, half:] = total[width + half :, column].astype(out.dtype)
-
-
-def join_grad_kernel(kept, came, grad_up, grad_down):
+    mine, other = ids[D_ID], 1 - ids[D_ID]
+    kept[:half, :] = total[pl.ds(pl.multiple_of(mine * half, 16), half), :]
+    sent[:half, :] = total[pl.ds(pl.multiple_of(other * half, 16), half), :].astype(BF16)
+    column = pl.ds(pl.multiple_of(mine * half, LANES), half)
+    kept[half:, :half] = total[width : width + half, column]
+    kept[half:, half:] = total[width + half :, column]
+    column = pl.ds(pl.multiple_of(other * half, LANES), half)
+    sent[half:, :half] = total[width : width + half, column].astype(BF16)
+    sent[half:, half:] = total[width + half :, column].astype(BF16)
+    first = sent_first.shape[0]
+    sent_first[...] = sent[:first, :]
+    sent_rest[...] = sent[first:, :]
+
+
+def join_grad_kernel(kept, came_first, came_rest, grad_up, grad_down, came):
+    first = came_first.shape[0]
+    came[:first, :] = came_first[...]
+    came[first:, :] = came_rest[...]
     half = kept.shape[1] // 2
     grad_up[...] = kept[:half, :] + came[:half, :].astype(F32)
     grad_down[:half, :] = kept[half:, :half] + came[half:, :half].astype(F32)
@@ -318,21 +369,25 @@
 
 
 def sum_kernel(count, *refs):
-    total = refs[0][...].astype(F32)
-    for m in range(1, count):
-        total = total + refs[m][...].astype(F32)
-    refs[count][...] = total.astype(BF16)
-
-
-def pair_kernel(own, came, small, small_came, out):
-    size = own.shape[0]
-    out[:size, :] = (own[...].astype(F32) + came[...].astype(F32)).astype(BF16)
-    out[size:, :] = (small[...] + small_came[...]).astype(BF16)
+    size = refs[0].shape[0] // 2
+    for half in range(2):
+        part = pl.ds(half * size, size)
+        total = refs[0][part, :].astype(F32)
+        for m in range(1, count):
+            total = total + refs[m][part, :].astype(F32)
+        refs[count + half][...] = total.astype(BF16)
+
+
+def pair_kernel(own_a, own_b, came_a, came_b, small, small_came, out):
+    size = own_a.shape[0]
+    out[:size, :] = (own_a[...].astype(F32) + came_a[...].astype(F32)).astype(BF16)
+    out[size : 2 * size, :] = (own_b[...].astype(F32) + came_b[...].astype(F32)).astype(BF16)
+    out[2 * size :, :] = (small[...] + small_came[...]).astype(BF16)
 
 
 def spread_kernel(count, ids, *refs):
     parts = refs[:count]
-    grad_qkv, grad_out, small, grads, held = refs[count:]
+    grad_qkv, grad_out, gain1, bias1, gain2, bias2, router, grads, held = refs[count:]
     size = grads.shape[0] // count
     for m in range(count):
         quarter = ids[Q_ID] ^ m
@@ -341,7 +396,9 @@
     total = held[0]
     for quarter in range(1, count):
         total = total + held[quarter]
-    small[...] = total
+    for row, out in enumerate((gain1, bias1, gain2, bias2)):
+        out[...] = total[row : row + 1, :].reshape(out.shape)
+    router[...] = total[8 : 8 + router.shape[0], :]
     inner = grad_qkv.shape[0]
     grad_qkv[...] = grads[:inner, :]
     grad_out[...] = grads[inner:, :]
@@ -392,11 +449,6 @@
             jnp.stack(blocks)[order], "expert", split_axis=0, concat_axis=0, tiled=True
         )[order]
         return [stacked[k] for k in range(n_expert)]
-
-    def tensor_sum(kept, sent):
-        chip = (kept.astype(F32) + tensor_swap(sent, 1).astype(F32)).astype(BF16)
-        own = (chip.astype(F32) + tensor_swap(chip, 2).astype(F32)).astype(BF16)
-        return own, tensor_swap(own, 1)
 
     def body(
         tokens,
@@ -446,24 +498,30 @@
 
         out_x, out_c = tensor_swap(w_out, 2), tensor_swap(w_out, 1)
         up_b, down_b = tensor_swap(up_a, 1), tensor_swap(down_a, 1)
-        table, router, *cot_blocks = run(
-            functools.partial(plan_kernel, experts),
-            [((experts, cap, rows), BF16), ((LANES, width), BF16)]
-            + [((cap, width), BF16)] * experts,
-            [ids, routes.T, cotangent, w_router.T],
-            micros=3,
-        )
-        d_rows_in = exchange(cot_blocks)
         normed, query, key, value, probs, head_out = run(
             functools.partial(attend_kernel, images),
             [((rows, width), BF16)]
             + [((rows, inner), BF16)] * 3
             + [((heads, rows, rows), BF16), ((rows, inner), BF16)],
-            [after(tokens, table), ln1_gain, ln1_bias, weight],
+            [tokens, ln1_gain, ln1_bias, weight],
             micros=4,
         )
-        head_out, out_x, up_b, down_b = lax.optimization_barrier((head_out, out_x, up_b, down_b))
+        head_out, out_x, out_c, up_b, down_b = lax.optimization_barrier(
+            (head_out, out_x, out_c, up_b, down_b)
+        )
         head_x, head_c = tensor_swap(head_out, 2), tensor_swap(head_out, 1)
+        quarter = cap // 2
+        cot_shapes = [(cap, width)] + [(quarter if small_slice else cap, width)] * (experts - 1)
+        table, part, router, *cot_blocks = run(
+            functools.partial(plan_kernel, experts),
+            [((experts, cap, rows), BF16), ((experts, quarter, rows), BF16)]
+            + [((LANES, width), BF16)]
+            + [(shape, BF16) for shape in cot_shapes],
+            [ids, after(routes.T, head_out), cotangent, w_router.T],
+            micros=2,
+        )
+        head_x = after(head_x, table)
+        d_rows_in = exchange(cot_blocks)
         out_all = [w_out, out_c, out_x, tensor_swap(out_x, 1)]
         heads_all = [head_out, head_c, head_x, tensor_swap(head_x, 1)]
         middle, *row_blocks = run(
@@ -478,60 +536,88 @@
             micros=3,
         )
         rows_in = exchange(row_blocks)
+        middle, *d_rows_in = lax.optimization_barrier((middle, *d_rows_in))
+        if small_slice:
+            pair_out = tensor_swap(jnp.stack(d_rows_in[1:]), 2)
+        else:
+            pair_out = router
 
         calls = [(0, 1), (2, 3)] if small_slice else [tuple(range(experts))]
         worked = []
         d_back, gated = [], []
-        for call in calls:
+        for number, call in enumerate(calls):
             count = cap * len(call)
+            last = number == len(calls) - 1
+            grads = [] if last else [((2 * width, hidden_width), BF16)] * 2
             results = run(
-                functools.partial(expert_kernel, experts, len(call)),
-                [((cap, width), BF16)] * (2 * len(call))
+                functools.partial(expert_kernel, experts, call, not last),
+                [((cap, width), BF16)] * len(call)
+                + [((len(call), quarter if small_slice else cap, width), BF16)] * 2
                 + [((count, width), BF16)] * 2
                 + [((count, hidden_width), BF16)] * 4
-                + [((part_rows, width), F32)],
-                [ids, up_a, up_b, down_a, down_b, router]
+                + [((part_rows, width), F32)]
+                + grads,
+                [ids, up_a, up_b, down_a, down_b]
+                + [after(router, worked[-1][6]) if worked else router, pair_out]
                 + [rows_in[k] for k in call]
                 + [d_rows_in[k] for k in call],
                 scratch=[((count, width), F32)],
                 micros=7,
+                limit=24,
             )
             d_back += results[: len(call)]
-            gated += results[len(call) : 2 * len(call)]
-            worked.append(results[2 * len(call) :])
-
-        def collect(blocks, routers):
-            kept, sent = run(
+            gated.append(results[len(call) : len(call) + 2])
+            worked.append(results[len(call) + 2 :])
+
+        def combine(blocks, spots, routers):
+            return run(
                 functools.partial(combine_kernel, experts, len(routers), base),
                 [((tall if routers else base, half), BF16)] * 2,
-                [ids, table] + blocks + routers,
+                [ids, spots] + blocks + routers,
                 scratch=[((tall if routers else base, width), F32)],
                 micros=2,
             )
-            return tensor_sum(kept, sent)
 
         d_home = exchange(d_back)
 
-        fields = [[one[at] for one in worked] for at in (0, 4, 5, 2, 3, 1)]
         grad_own, grad_pair = run(
-            functools.partial(weight_grad_kernel, len(worked)),
+            weight_grad_kernel,
             [((2 * width, hidden_width), BF16)] * 2,
-            [one for field in fields for one in field],
-            micros=6,
+            [worked[-1][at] for at in (0, 4, 5, 2, 3, 1)] + list(worked[0][7:]),
+            micros=4,
             limit=24,
         )
-        grad_kept, grad_sent = run(
+        third = width // 48 * 16
+        grad_kept, sent_first, sent_rest = run(
             split_grad_kernel,
-            [((width, width), F32), ((width, width), BF16)],
+            [((width, width), F32), ((third, width), BF16), ((width - third, width), BF16)],
             [ids, grad_own, tensor_swap(grad_pair, 1)],
-            scratch=[((2 * width, width), F32)],
+            scratch=[((2 * width, width), F32), ((width, width), BF16)],
             micros=2,
             limit=24,
         )
-        grad_came = dp_swap(grad_sent)
-
-        d_home = list(lax.optimization_barrier(tuple(d_home) + (grad_sent,))[:-1])
-        own, other = collect(d_home, [one[6] for one in worked])
+
+        if small_slice:
+            (kept_a, sent_a), (kept_b, sent_b) = gated
+            gated_blocks = run(
+                gated_sum_kernel,
+                [((quarter, width), BF16)] * 4,
+                [kept_a, tensor_swap(sent_a, 2), kept_b, tensor_swap(sent_b, 2)],
+            )
+            spots = part
+        else:
+            gated_blocks = [gated[0][0][k] for k in range(experts)]
+            spots = table
+
+        *d_home, sent_first = lax.optimization_barrier((*d_home, *gated_blocks, sent_first))
+        d_home, gated_blocks = d_home[:experts], d_home[experts:]
+        kept, sent = combine(list(d_home), table, [one[6] for one in worked])
+        chip = (kept.astype(F32) + tensor_swap(sent, 1).astype(F32)).astype(BF16)
+        own = (chip.astype(F32) + tensor_swap(chip, 2).astype(F32)).astype(BF16)
+        gated_home = exchange(list(gated_blocks))
+        came_first = dp_swap(sent_first)
+        own, came_first, *gated_home = lax.optimization_barrier((own, came_first, *gated_home))
+        other = tensor_swap(own, 1)
 
         parts = 4 if small_slice else 1
         d_middle, kept1, sent1, small2, *grad_blocks = run(
@@ -548,7 +634,27 @@
             micros=6,
         )
 
-        own1, other1 = tensor_sum(kept1, sent1)
+        *gated_home, _ = lax.optimization_barrier((*gated_home, d_middle))
+        kept_y, sent_y = combine(list(gated_home), spots, [])
+
+        if small_slice:
+            arrived = [grad_blocks[0]] + [quarter_swap(grad_blocks[m], m) for m in (3, 1, 2)]
+            arrived[0], kept_y, sent_y = lax.optimization_barrier((arrived[0], kept_y, sent_y))
+            size = grad_blocks[0].shape[0]
+            summed_a, summed_b = run(
+                functools.partial(sum_kernel, 4), [((size // 2, width), BF16)] * 2, arrived
+            )
+            sent_rest = after(sent_rest, summed_a)
+            came_a = expert_swap(summed_a, 2)
+            came_b = expert_swap(after(summed_b, came_a), 2)
+        chip_y = (kept_y.astype(F32) + tensor_swap(sent_y, 1).astype(F32)).astype(BF16)
+        own_y = (chip_y.astype(F32) + tensor_swap(chip_y, 2).astype(F32)).astype(BF16)
+
+        chip1 = (kept1.astype(F32) + tensor_swap(sent1, 1).astype(F32)).astype(BF16)
+        own1 = (chip1.astype(F32) + tensor_swap(chip1, 2).astype(F32)).astype(BF16)
+        if small_slice:
+            own1 = after(own1, summed_a)
+        other1 = tensor_swap(own1, 1)
         grad_tokens, small = run(
             last_norm_kernel,
             [((rows, width), BF16), ((small_rows, width), F32)],
@@ -557,21 +663,19 @@
             micros=2,
         )
         if small_slice:
-            arrived = [grad_blocks[0]] + [quarter_swap(grad_blocks[m], m) for m in (1, 2, 3)]
-            size = grad_blocks[0].shape[0]
-            (summed,) = run(
-                functools.partial(sum_kernel, 4), [((size, width), BF16)], arrived, micros=1
-            )
             (ready,) = run(
                 pair_kernel,
                 [((size + small_rows, width), BF16)],
-                [summed, expert_swap(summed, 2), small, expert_swap(small, 2)],
+                [summed_a, summed_b, came_a, came_b, small, expert_swap(small, 2)],
                 micros=1,
             )
+            own_y, ready = lax.optimization_barrier((own_y, ready))
             everything = [ready] + [quarter_swap(ready, m) for m in (1, 2, 3)]
-            grad_qkv, grad_out, small_sum = run(
+            grad_qkv, grad_out, *sums, grad_router = run(
                 functools.partial(spread_kernel, 4),
-                [((3 * inner, width), F32), ((inner, width), F32), ((small_rows, width), F32)],
+                [((3 * inner, width), F32), ((inner, width), F32)]
+                + [((width,), F32)] * 4
+                + [((experts, width), F32)],
                 [ids] + everything,
                 scratch=[((4 * inner, width), F32), ((4, small_rows, width), F32)],
                 micros=3,
@@ -580,18 +684,17 @@
             grads = lax.psum(grad_blocks[0], ("expert", "dp")).astype(F32)
             grad_qkv, grad_out = grads[: 3 * inner], grads[3 * inner :]
             small_sum = lax.psum(small, ("expert", "dp"))
+            sums, grad_router = list(small_sum[:4]), small_sum[8 : 8 + experts]
 
         grad_up, grad_down = run(
             join_grad_kernel,
             [((half, hidden_width), F32), ((hidden_width, half), F32)],
-            [after(grad_kept, grad_blocks[0]), grad_came],
+            [grad_kept, came_first, dp_swap(sent_rest)],
+            scratch=[((width, width), BF16)],
             micros=2,
         )
 
-        gated = list(lax.optimization_barrier(tuple(gated) + tuple(d_home))[:experts])
-        gated_home = exchange(gated)
-        gated_home = list(lax.optimization_barrier(tuple(gated_home) + (d_middle,))[:-1])
-        mix_own, mix_other = collect(gated_home, [])
+        mix_own, mix_other = own_y, tensor_swap(own_y, 1)
         mixture = jnp.where(
             rank % 2 == 0,
             jnp.concatenate([mix_own, mix_other], axis=1),
@@ -602,13 +705,13 @@
         return (
             out,
             grad_tokens,
-            small_sum[0],
-            small_sum[1],
+            sums[0],
+            sums[1],
             grad_qkv.reshape(3, inner, width).transpose(2, 0, 1),
             grad_out,
-            small_sum[2],
-            small_sum[3],
-            small_sum[8 : 8 + experts].T,
+            sums[2],
+            sums[3],
+            grad_router.T,
             grad_up[None],
             grad_down[None],
         )

time: 203 us -> 175 us (0.86)
  waiting for transfers between devices: 98.9 us -> 71.8 us
  local copies, waits for them, and re-layouts: 4.88 us -> 6.94 us
    ppermute x14 -> x15, waiting for transfers between devices: 65.5 us -> 37.3 us  [expert_swap(): lax.ppermute(value, 'expert', [(i, i ^ mask) for i in range(n_expert)])]
    ppermute x6, starting transfers between devices: 13.7 us -> 7.84 us  [quarter_swap(): return lax.ppermute(value, ('expert', 'dp'), pairs)]
    ppermute x6, waiting for transfers between devices: 17.4 us -> 21.8 us  [quarter_swap(): return lax.ppermute(value, ('expert', 'dp'), pairs)]
    ppermute x18 -> x21, waiting for transfers between devices: 16 us -> 12.6 us  [tensor_swap(): lax.ppermute(value, 'tensor', [(i, i ^ mask) for i in range(n_tensor)])]
    unnamed x48 -> x52, local copies, waits for them, and re-layouts: 3.57 us -> 6.86 us
    ppermute x18 -> x21, starting transfers between devices: 10.9 us -> 13.4 us  [tensor_swap(): lax.ppermute(value, 'tensor', [(i, i ^ mask) for i in range(n_tensor)])]
    pallas_call x15 -> x16, Pallas kernels: 39.2 us -> 39.4 us  [run(): pl.pallas_call(kernel, out_shape=[jax.ShapeDtypeStruct(shape, kind) for s...]
    ppermute x14 -> x15, starting transfers between devices: 27 us -> 27.2 us  [expert_swap(): lax.ppermute(value, 'expert', [(i, i ^ mask) for i in range(n_expert)])]
  transfers between devices with their start and end apart: 39 -> 44, of which waited for: 16 -> 21; matrix products, arithmetic and copies ran while one was open for 2% -> 2% of each run, Pallas kernels for 10% -> 13%
where the time goes in v2:
time: 175 us
  waiting for transfers between devices  71.8 us (41%)
  starting transfers between devices  51.5 us (29%)
  Pallas kernels  39.4 us (23%)
  local copies, waits for them, and re-layouts  6.94 us (4%)
  other arithmetic  3.3 us (2%)
  between operations  1.75 us (1%)
    pallas_call x16, Pallas kernels, run(): pl.pallas_call(kernel, out_shape=[jax.ShapeDtypeStruct(shape, kind) for s...  39.4 us
    ppermute x15, waiting for transfers between devices, expert_swap(): lax.ppermute(value, 'expert', [(i, i ^ mask) for i in range(n_expert)])  37.3 us
    ppermute x15, starting transfers between devices, expert_swap(): lax.ppermute(value, 'expert', [(i, i ^ mask) for i in range(n_expert)])  27.2 us
    ppermute x6, waiting for transfers between devices, quarter_swap(): return lax.ppermute(value, ('expert', 'dp'), pairs)  21.8 us
    ppermute x21, starting transfers between devices, tensor_swap(): lax.ppermute(value, 'tensor', [(i, i ^ mask) for i in range(n_tensor)])  13.4 us
    ppermute x21, waiting for transfers between devices, tensor_swap(): lax.ppermute(value, 'tensor', [(i, i ^ mask) for i in range(n_tensor)])  12.6 us
    ppermute x6, starting transfers between devices, quarter_swap(): return lax.ppermute(value, ('expert', 'dp'), pairs)  7.84 us
    unnamed x52, local copies, waits for them, and re-layouts  6.86 us
  transfers between devices with their start and end apart: 44, of which 21 were waited for; matrix products, arithmetic and copies ran while one was open for 2% of the time, Pallas kernels for 13%

profile of v2, /device:TPU:0, one launch (start us, length us, event | category | flops | bytes accessed | tf_op | source)
XLA Modules:
  0.0 174.7 jit_solution(7499261287256305411)
XLA Ops:
  1.2 2.9 %collective-permute-start = (bf16[192,768]{1,0:T(8,128)(2,1)}, bf16[192,768]{1,0:T(8,128)(2,1)S(1)}, u32[]{:S(2)}, u32[]{:S(2)}) collective-permute-start(bf16[192,768]{1,0:T(8,128)(2,1)} %w_out.1), channel_id=1, source_target_pairs={{0,16},{8,24},{16,0},{24,8},{1,17},{9,25},{17,1},{25,9},{2,18},{10... | collective-permute-start | bytes 884744 | tf_op jit(solution)/shard_map/ppermute | solution.py:431
  4.9 1.2 copy-done.4
  6.1 1.1 copy-done.7
  8.5 2.5 %shard_map.212 = (bf16[394,768]{1,0:T(8,128)(2,1)S(1)}, bf16[394,192]{1,0:T(8,128)(2,1)S(1)}, bf16[394,192]{1,0:T(8,128)(2,1)S(1)}, bf16[394,192]{1,0:T(8,128)(2...) custom-call(bf16[394,768]{1,0:T(8,128)(2,1)S(1)} %copy-done.7, f32[768]{0:T(1024)S(1)} %copy-done.18, ...), custom_call_target="tpu_custom_call" | custom-call | flops 4600000000 | bytes 1024 | tf_op jit(solution)/shard_map/pallas_call | solution.py:414
  11.7 1.8 %collective-permute-start.5 = (bf16[394,192]{1,0:T(8,128)(2,1)S(1)}, bf16[394,192]{1,0:T(8,128)(2,1)S(1)}, u32[]{:S(2)}, u32[]{:S(2)}) collective-permute-start(bf16[394,192]{1,0:T(8,128)(2,1)S(1)} %get-tuple-element.122.rest_0_.head_out), channel_id=1, source_target_pairs={{0,16},{8,24},{16,0},{24,8},{1,17},{9,25},{17,1},{25,9},{2,18},{10... | collective-permute-start | bytes 453896 | tf_op jit(solution)/shard_map/ppermute | solution.py:431
  13.7 1.3 shard_map.213
  15.1 4.1 %collective-permute-done.5.rest_2_ = bf16[394,192]{1,0:T(8,128)(2,1)S(1)} collective-permute-done((bf16[394,192]{1,0:T(8,128)(2,1)S(1)}, bf16[394,192]{1,0:T(8,128)(2,1)S(1)}, u32[]{:S(2)}, u32[]{:S(2)}) %collective-permute-start.5) | collective-permute-done | bytes 151328 | tf_op jit(solution)/shard_map/ppermute | solution.py:431
  19.2 1.8 %collective-permute-start.8 = (bf16[72,768]{1,0:T(8,128)(2,1)S(1)}, bf16[72,768]{1,0:T(8,128)(2,1)S(1)}, u32[]{:S(2)}, u32[]{:S(2)}) collective-permute-start(bf16[72,768]{1,0:T(8,128)(2,1)S(1)} %get-tuple-element.130), channel_id=1, source_target_pairs={{0,2},{2,0},{4,6},{6,4},{1,3},{3,1},{5,7},{7,5},{8,10},{10,8},{12,... | collective-permute-start | bytes 331784 | tf_op jit(solution)/shard_map/ppermute | solution.py:434
  21.0 2.6 %collective-permute-start.9 = (bf16[72,768]{1,0:T(8,128)(2,1)S(1)}, bf16[72,768]{1,0:T(8,128)(2,1)S(1)}, u32[]{:S(2)}, u32[]{:S(2)}) collective-permute-start(bf16[72,768]{1,0:T(8,128)(2,1)S(1)} %get-tuple-element.131), channel_id=1, source_target_pairs={{0,4},{2,6},{4,0},{6,2},{1,5},{3,7},{5,1},{7,3},{8,12},{10,14},{12... | collective-permute-start | bytes 331784 | tf_op jit(solution)/shard_map/ppermute | solution.py:434
  23.8 2.7 %shard_map.214 = (f32[394,768]{1,0:T(8,128)S(1)}, bf16[144,768]{1,0:T(8,128)(2,1)S(1)}, bf16[144,768]{1,0:T(8,128)(2,1)S(1)}, bf16[144,768]{1,0:T(8,128)(2,1)S(1)}, bf16[144,768]{1,0:T(8,128)(2,1)S(1)}) custom-call(s32[8]{0:T(128)S(1)} %stack.41.ids, bf16[394,768]{1,0:T(8,128)(2,1)S(1)} %copy-done.8, f32[768]{0:T(1024)S(1)} %copy-done.17, ...), custom_call_target="tpu_custom_call" | custom-call | flops 3449999872 | bytes 1024 | tf_op jit(solution)/shard_map/pallas_call | solution.py:414
  26.5 6.0 %collective-permute-done.9.refs_2_ = bf16[72,768]{1,0:T(8,128)(2,1)S(1)} collective-permute-done((bf16[72,768]{1,0:T(8,128)(2,1)S(1)}, bf16[72,768]{1,0:T(8,128)(2,1)S(1)}, u32[]{:S(2)}, u32[]{:S(2)}) %collective-permute-start.9) | collective-permute-done | bytes 110624 | tf_op jit(solution)/shard_map/ppermute | solution.py:434
  32.6 1.6 collective-permute-start.11
  34.2 2.2 %collective-permute-start.12 = (bf16[144,768]{1,0:T(8,128)(2,1)S(1)}, bf16[144,768]{1,0:T(8,128)(2,1)S(1)}, u32[]{:S(2)}, u32[]{:S(2)}) collective-permute-start(bf16[144,768]{1,0:T(8,128)(2,1)S(1)} %get-tuple-element.141), channel_id=1, source_target_pairs={{0,2},{2,0},{4,6},{6,4},{1,3},{3,1},{5,7},{7,5},{8,10},{10,8},{12,... | collective-permute-start | bytes 663560 | tf_op jit(solution)/shard_map/ppermute | solution.py:434
  36.5 1.0 collective-permute-start.14
  37.5 1.5 collective-permute-start.15
  38.9 5.6 %collective-permute-done.12.refs_1_ = bf16[144,768]{1,0:T(8,128)(2,1)S(1)} collective-permute-done((bf16[144,768]{1,0:T(8,128)(2,1)S(1)}, bf16[144,768]{1,0:T(8,128)(2,1)S(1)}, u32[]{:S(2)}, u32[]{:S(2)}) %collective-permute-start.12) | collective-permute-done | bytes 221216 | tf_op jit(solution)/shard_map/ppermute | solution.py:434
  44.6 7.1 %shard_map.215 = (bf16[144,768]{1,0:T(8,128)(2,1)S(1)}, bf16[144,768]{1,0:T(8,128)(2,1)S(1)}, bf16[2,72,768]{2,1,0:T(8,128)(2,1)S(1)}, bf16[2,72,768]{2,1,0:T(8,...) custom-call(s32[8]{0:T(128)S(1)} %stack.41.ids, ...), custom_call_target="tpu_custom_call" | custom-call | flops 8049999872 | bytes 1024 | tf_op jit(solution)/shard_map/pallas_call | solution.py:414
  51.7 3.5 %collective-permute-done.14.refs_0_ = bf16[144,768]{1,0:T(8,128)(2,1)S(1)} collective-permute-done((bf16[144,768]{1,0:T(8,128)(2,1)S(1)}, bf16[144,768]{1,0:T(8,128)(2,1)S(1)}, u32[]{:S(2)}, u32[]{:S(2)}) %collective-permute-start.14) | collective-permute-done | bytes 221216 | tf_op jit(solution)/shard_map/ppermute | solution.py:434
  55.2 4.9 %shard_map.216 = (bf16[144,768]{1,0:T(8,128)(2,1)S(1)}, bf16[144,768]{1,0:T(8,128)(2,1)S(1)}, bf16[2,72,768]{2,1,0:T(8,128)(2,1)S(1)}, bf16[2,72,768]{2,1,0:T(8,...) custom-call(s32[8]{0:T(128)S(1)} %stack.41.ids, ...), custom_call_target="tpu_custom_call" | custom-call | flops 8049999872 | bytes 1024 | tf_op jit(solution)/shard_map/pallas_call | solution.py:414
  60.1 2.7 %shard_map.218 = (bf16[1536,768]{1,0:T(8,128)(2,1)S(1)}, bf16[1536,768]{1,0:T(8,128)(2,1)S(1)}) custom-call(bf16[288,768]{1,0:T(8,128)(2,1)S(1)} %get-tuple-element.159.refs_0_, bf16[288,768]{1,0:T(8,128)(2,1)S(1)} %get-tuple-element.160.refs_1_, bf16[288,768]{1,0:T(8,128)(2,1)S(1)} %get-tuple-element.161.refs_2_, ...), custom_call_target="tpu_custom_call" | custom-call | flops 4600000000 | bytes 1024 | tf_op jit(solution)/shard_map/pallas_call | solution.py:414
  63.4 1.5 collective-permute-start.19
  65.0 3.2 %collective-permute-start.13 = (bf16[144,768]{1,0:T(8,128)(2,1)S(1)}, bf16[144,768]{1,0:T(8,128)(2,1)S(1)}, u32[]{:S(2)}, u32[]{:S(2)}) collective-permute-start(bf16[144,768]{1,0:T(8,128)(2,1)S(1)} %get-tuple-element.144), channel_id=1, source_target_pairs={{0,2},{2,0},{4,6},{6,4},{1,3},{3,1},{5,7},{7,5},{8,10},{10,8},{12,... | collective-permute-start | bytes 663560 | tf_op jit(solution)/shard_map/ppermute | solution.py:434
  68.1 1.0 collective-permute-start.16
  69.1 2.0 %collective-permute-done.18.came_a = bf16[2,72,768]{2,1,0:T(8,128)(2,1)S(1)} collective-permute-done((bf16[2,72,768]{2,1,0:T(8,128)(2,1)S(1)}, bf16[2,72,768]{2,1,0:T(8,128)(2,1)S(1)}, u32[]{:S(2)}, u32[]{:S(2)}) %collective-permute-start.18) | collective-permute-done | bytes 221216 | tf_op jit(solution)/shard_map/ppermute | solution.py:431
  71.2 2.2 %collective-permute-start.17 = (bf16[144,768]{1,0:T(8,128)(2,1)S(1)}, bf16[144,768]{1,0:T(8,128)(2,1)S(1)}, u32[]{:S(2)}, u32[]{:S(2)}) collective-permute-start(bf16[144,768]{1,0:T(8,128)(2,1)S(1)} %get-tuple-element.150), channel_id=1, source_target_pairs={{0,6},{2,4},{4,2},{6,0},{1,7},{3,5},{5,3},{7,1},{8,14},{10,12},{12... | collective-permute-start | bytes 663560 | tf_op jit(solution)/shard_map/ppermute | solution.py:434
  73.3 2.1 %collective-permute-done.19.came_b = bf16[2,72,768]{2,1,0:T(8,128)(2,1)S(1)} collective-permute-done((bf16[2,72,768]{2,1,0:T(8,128)(2,1)S(1)}, bf16[2,72,768]{2,1,0:T(8,128)(2,1)S(1)}, u32[]{:S(2)}, u32[]{:S(2)}) %collective-permute-start.19) | collective-permute-done | bytes 221216 | tf_op jit(solution)/shard_map/ppermute | solution.py:431
  75.6 1.6 shard_map.219
  77.9 8.4 %collective-permute-done.16.refs_2_ = bf16[144,768]{1,0:T(8,128)(2,1)S(1)} collective-permute-done((bf16[144,768]{1,0:T(8,128)(2,1)S(1)}, bf16[144,768]{1,0:T(8,128)(2,1)S(1)}, u32[]{:S(2)}, u32[]{:S(2)}) %collective-permute-start.16) | collective-permute-done | bytes 221216 | tf_op jit(solution)/shard_map/ppermute | solution.py:434
  86.3 1.5 shard_map.220
  87.9 1.6 collective-permute-done.21
  90.1 1.6 collective-permute-start.23
  91.7 4.5 %collective-permute-start.24 = (bf16[72,768]{1,0:T(8,128)(2,1)S(1)}, bf16[72,768]{1,0:T(8,128)(2,1)S(1)}, u32[]{:S(2)}, u32[]{:S(2)}) collective-permute-start(bf16[72,768]{1,0:T(8,128)(2,1)S(1)} %get-tuple-element.179), channel_id=1, source_target_pairs={{0,2},{2,0},{4,6},{6,4},{1,3},{3,1},{5,7},{7,5},{8,10},{10,8},{12,... | collective-permute-start | bytes 331784 | tf_op jit(solution)/shard_map/ppermute | solution.py:434
  96.2 1.0 collective-permute-start.25
  97.2 1.5 collective-permute-start.26
  99.7 7.6 %collective-permute-done.25.refs_2_ = bf16[72,768]{1,0:T(8,128)(2,1)S(1)} collective-permute-done((bf16[72,768]{1,0:T(8,128)(2,1)S(1)}, bf16[72,768]{1,0:T(8,128)(2,1)S(1)}, u32[]{:S(2)}, u32[]{:S(2)}) %collective-permute-start.25) | collective-permute-done | bytes 110624 | tf_op jit(solution)/shard_map/ppermute | solution.py:434
  107.3 1.6 collective-permute-done.27.other
  108.9 5.0 %shard_map.221 = (f32[394,768]{1,0:T(8,128)S(1)}, bf16[394,384]{1,0:T(8,128)(2,1)S(1)}, bf16[394,384]{1,0:T(8,128)(2,1)S(1)}, f32[16,768]{1,0:T(8,128)S(1)}, bf1...) custom-call(s32[8]{0:T(128)S(1)} %stack.41.ids, ...), custom_call_target="tpu_custom_call" | custom-call | flops 6899999744 | bytes 1024 | tf_op jit(solution)/shard_map/pallas_call | solution.py:414
  114.1 1.7 collective-permute-start.30
  115.7 1.6 collective-permute-start.31
  117.7 1.6 collective-permute-start.36
  119.2 1.4 shard_map.222
  120.8 4.1 %collective-permute-done.30.refs_1_ = bf16[192,768]{1,0:T(8,128)(2,1)S(1)} collective-permute-done((bf16[192,768]{1,0:T(8,128)(2,1)S(1)}, bf16[192,768]{1,0:T(8,128)(2,1)S(1)}, u32[]{:S(2)}, u32[]{:S(2)}) %collective-permute-start.30) | collective-permute-done | bytes 294944 | tf_op jit(solution)/shard_map/ppermute | solution.py:441
  124.9 5.7 %collective-permute-done.31.refs_2_ = bf16[192,768]{1,0:T(8,128)(2,1)S(1)} collective-permute-done((bf16[192,768]{1,0:T(8,128)(2,1)S(1)}, bf16[192,768]{1,0:T(8,128)(2,1)S(1)}, u32[]{:S(2)}, u32[]{:S(2)}) %collective-permute-start.31) | collective-permute-done | bytes 294944 | tf_op jit(solution)/shard_map/ppermute | solution.py:441
  131.3 1.7 %collective-permute-start.33 = (bf16[96,768]{1,0:T(8,128)(2,1)}, bf16[96,768]{1,0:T(8,128)(2,1)}, u32[]{:S(2)}, u32[]{:S(2)}) collective-permute-start(bf16[96,768]{1,0:T(8,128)(2,1)} %get-tuple-element.207.own_a), channel_id=1, source_target_pairs={{0,4},{2,6},{4,0},{6,2},{1,5},{3,7},{5,1},{7,3},{8,12},{10,14},{12... | collective-permute-start | bytes 442376 | tf_op jit(solution)/shard_map/ppermute | solution.py:434
  133.1 1.5 collective-permute-start.43
  134.8 0.8 add_convert_fusion.5
  135.6 1.5 collective-permute-start.29
  137.1 4.2 %collective-permute-done.33.came_a = bf16[96,768]{1,0:T(8,128)(2,1)} collective-permute-done((bf16[96,768]{1,0:T(8,128)(2,1)}, bf16[96,768]{1,0:T(8,128)(2,1)}, u32[]{:S(2)}, u32[]{:S(2)}) %collective-permute-start.33) | collective-permute-done | bytes 147488 | tf_op jit(solution)/shard_map/ppermute | solution.py:434
  141.3 1.1 copy-done.9
  142.3 1.3 copy-done.23
  143.6 0.8 copy-done.25
  144.4 2.9 %shard_map.224 = (bf16[394,768]{1,0:T(8,128)(2,1)}, f32[16,768]{1,0:T(8,128)S(1)}) custom-call(s32[8]{0:T(128)S(1)} %stack.41.ids, bf16[394,384]{1,0:T(8,128)(2,1)S(1)} %add_convert_fusion.2.own, bf16[394,384]{1,0:T(8,128)(2,1)} %collective-permute-done.37.other, bf16[394,768]{1,0:T(8,128)(2,1)S(1)} %copy-done.9, f32[394,768]{1,0:T(8,128)S(1)} %copy-done.23, ...), custom_call_target="tpu_custom_call" | custom-call | flops 2300000000 | bytes 1024 | tf_op jit(solution)/shard_map/pallas_call | solution.py:414
  147.3 2.9 %collective-permute-start.38 = (f32[16,768]{1,0:T(8,128)S(1)}, f32[16,768]{1,0:T(8,128)S(1)}, u32[]{:S(2)}, u32[]{:S(2)}) collective-permute-start(f32[16,768]{1,0:T(8,128)S(1)} %get-tuple-element.214.small), channel_id=1, source_target_pairs={{0,4},{2,6},{4,0},{6,2},{1,5},{3,7},{5,1},{7,3},{8,12},{10,14},{12... | collective-permute-start | bytes 147464 | tf_op jit(solution)/shard_map/ppermute | solution.py:434
  150.2 1.1 add_convert_fusion.4
  151.4 0.9 collective-permute-done.38.small_came
  152.3 1.1 shard_map.225.refs_0_
  153.4 1.4 collective-permute-start.40
  154.9 2.4 %collective-permute-start.41 = (bf16[208,768]{1,0:T(8,128)(2,1)S(1)}, bf16[208,768]{1,0:T(8,128)(2,1)S(1)}, u32[]{:S(2)}, u32[]{:S(2)}) collective-permute-start(bf16[208,768]{1,0:T(8,128)(2,1)S(1)} %shard_map.225.refs_0_), channel_id=1, source_target_pairs={{0,2},{1,3},{2,0},{3,1},{4,6},{5,7},{6,4},{7,5},{8,10},{9,11},{10,... | collective-permute-start | bytes 958472 | tf_op jit(solution)/shard_map/ppermute | solution.py:441
  157.8 1.7 shard_map.227
  159.5 1.0 select_convert_fusion
  160.5 2.9 %collective-permute-done.40.refs_1_ = bf16[208,768]{1,0:T(8,128)(2,1)S(1)} collective-permute-done((bf16[208,768]{1,0:T(8,128)(2,1)S(1)}, bf16[208,768]{1,0:T(8,128)(2,1)S(1)}, u32[]{:S(2)}, u32[]{:S(2)}) %collective-permute-start.40) | collective-permute-done | bytes 319520 | tf_op jit(solution)/shard_map/ppermute | solution.py:441
  163.4 2.2 %collective-permute-done.41.refs_2_ = bf16[208,768]{1,0:T(8,128)(2,1)S(1)} collective-permute-done((bf16[208,768]{1,0:T(8,128)(2,1)S(1)}, bf16[208,768]{1,0:T(8,128)(2,1)S(1)}, u32[]{:S(2)}, u32[]{:S(2)}) %collective-permute-start.41) | collective-permute-done | bytes 319520 | tf_op jit(solution)/shard_map/ppermute | solution.py:441
  165.6 6.9 %collective-permute-done.42.refs_3_ = bf16[208,768]{1,0:T(8,128)(2,1)S(1)} collective-permute-done((bf16[208,768]{1,0:T(8,128)(2,1)S(1)}, bf16[208,768]{1,0:T(8,128)(2,1)S(1)}, u32[]{:S(2)}, u32[]{:S(2)}) %collective-permute-start.42) | collective-permute-done | bytes 319520 | tf_op jit(solution)/shard_map/ppermute | solution.py:441
  172.5 2.2 %shard_map.226 = (f32[576,768]{1,0:T(8,128)}, f32[192,768]{1,0:T(8,128)}, f32[768]{0:T(1024)}, f32[768]{0:T(1024)}, f32[768]{0:T(1024)}, /*index=5*/f32[768]{0:T(1024)}, f32[4,768]{1,0:T(4,128)}) custom-call(s32[8]{0:T(128)S(1)} %stack.41.ids, bf16[208,768]{1,0:T(8,128)(2,1)S(1)} %shard_map.225.refs_0_, ...), custom_call_target="tpu_custom_call" | custom-call | flops 3449999872 | bytes 1024 | tf_op jit(solution)/shard_map/pallas_call | solution.py:414
  (102 shorter events, 8.3 us)
Async XLA Ops:
  0.6 11.0 %collective-permute-start.2 = (bf16[768,768]{1,0:T(8,128)(2,1)}, bf16[768,768]{1,0:T(8,128)(2,1)S(1)}, u32[]{:S(2)}, u32[]{:S(2)}) collective-permute-start(bf16[768,768]{1,0:T(8,128)(2,1)} %bitcast.26), channel_id=1, source_target_pairs={{0,8},{8,0},{16,24},{24,16},{1,9},{9,1},{17,25},{25,17},{2,10},{10... | collective-permute-start | bytes 3538952 | tf_op jit(solution)/shard_map/ppermute | solution.py:431
  1.2 10.5 %collective-permute-start.3 = (bf16[768,768]{1,0:T(8,128)(2,1)}, bf16[768,768]{1,0:T(8,128)(2,1)S(1)}, u32[]{:S(2)}, u32[]{:S(2)}) collective-permute-start(bf16[768,768]{1,0:T(8,128)(2,1)} %bitcast.29), channel_id=1, source_target_pairs={{0,8},{8,0},{16,24},{24,16},{1,9},{9,1},{17,25},{25,17},{2,10},{10... | collective-permute-start | bytes 3538952 | tf_op jit(solution)/shard_map/ppermute | solution.py:431
  1.2 10.4 %collective-permute-start = (bf16[192,768]{1,0:T(8,128)(2,1)}, bf16[192,768]{1,0:T(8,128)(2,1)S(1)}, u32[]{:S(2)}, u32[]{:S(2)}) collective-permute-start(bf16[192,768]{1,0:T(8,128)(2,1)} %w_out.1), channel_id=1, source_target_pairs={{0,16},{8,24},{16,0},{24,8},{1,17},{9,25},{17,1},{25,9},{2,18},{10... | collective-permute-start | bytes 884744 | tf_op jit(solution)/shard_map/ppermute | solution.py:431
  4.2 7.5 %collective-permute-start.1 = (bf16[192,768]{1,0:T(8,128)(2,1)}, bf16[192,768]{1,0:T(8,128)(2,1)S(1)}, u32[]{:S(2)}, u32[]{:S(2)}) collective-permute-start(bf16[192,768]{1,0:T(8,128)(2,1)} %w_out.1), channel_id=1, source_target_pairs={{0,8},{8,0},{16,24},{24,16},{1,9},{9,1},{17,25},{25,17},{2,10},{10... | collective-permute-start | bytes 884744 | tf_op jit(solution)/shard_map/ppermute | solution.py:431
  8.5 5.2 %copy-start.6 = (bf16[394,768]{1,0:T(8,128)(2,1)S(1)}, bf16[394,768]{1,0:T(8,128)(2,1)}, u32[]{:S(2)}) copy-start(bf16[394,768]{1,0:T(8,128)(2,1)} %cot.3) | copy-start | bytes 1815556
  8.5 5.2 %copy-start.13 = (bf16[768,4]{0,1:T(4,128)(2,1)S(1)}, bf16[768,4]{0,1:T(4,128)(2,1)}, u32[]{:S(2)}) copy-start(bf16[768,4]{0,1:T(4,128)(2,1)} %param.22) | copy-start | bytes 18436
  8.5 5.2 %copy-start.15 = (s32[394,2]{0,1:T(2,128)S(1)}, s32[394,2]{0,1:T(2,128)}, u32[]{:S(2)}) copy-start(s32[394,2]{0,1:T(2,128)} %param.14) | copy-start | bytes 9460
  11.6 3.4 %copy-start.2 = (bf16[768,768]{1,0:T(8,128)(2,1)}, bf16[768,768]{1,0:T(8,128)(2,1)S(1)}, u32[]{:S(2)}) copy-start(bf16[768,768]{1,0:T(8,128)(2,1)S(1)} %collective-permute-done.3.down_b) | copy-start | bytes 3538948
  11.6 12.0 %collective-permute-start.4 = (bf16[394,192]{1,0:T(8,128)(2,1)S(1)}, bf16[394,192]{1,0:T(8,128)(2,1)S(1)}, u32[]{:S(2)}, u32[]{:S(2)}) collective-permute-start(bf16[394,192]{1,0:T(8,128)(2,1)S(1)} %get-tuple-element.122.rest_0_.head_out), channel_id=1, source_target_pairs={{0,8},{8,0},{16,24},{24,16},{1,9},{9,1},{17,25},{25,17},{2,10},{10... | collective-permute-start | bytes 453896 | tf_op jit(solution)/shard_map/ppermute | solution.py:431
  11.7 7.5 %collective-permute-start.5 = (bf16[394,192]{1,0:T(8,128)(2,1)S(1)}, bf16[394,192]{1,0:T(8,128)(2,1)S(1)}, u32[]{:S(2)}, u32[]{:S(2)}) collective-permute-start(bf16[394,192]{1,0:T(8,128)(2,1)S(1)} %get-tuple-element.122.rest_0_.head_out), channel_id=1, source_target_pairs={{0,16},{8,24},{16,0},{24,8},{1,17},{9,25},{17,1},{25,9},{2,18},{10... | collective-permute-start | bytes 453896 | tf_op jit(solution)/shard_map/ppermute | solution.py:431
  13.5 10.2 %collective-permute-start.7 = (bf16[192,768]{1,0:T(8,128)(2,1)S(1)}, bf16[192,768]{1,0:T(8,128)(2,1)S(1)}, u32[]{:S(2)}, u32[]{:S(2)}) collective-permute-start(bf16[192,768]{1,0:T(8,128)(2,1)S(1)} %collective-permute-done.rest_6_), channel_id=1, source_target_pairs={{0,8},{8,0},{16,24},{24,16},{1,9},{9,1},{17,25},{25,17},{2,10},{10... | collective-permute-start | bytes 884744 | tf_op jit(solution)/shard_map/ppermute | solution.py:431
  13.7 10.0 %copy-start.8 = (bf16[394,768]{1,0:T(8,128)(2,1)S(1)}, bf16[394,768]{1,0:T(8,128)(2,1)}, u32[]{:S(2)}) copy-start(bf16[394,768]{1,0:T(8,128)(2,1)} %tokens.5) | copy-start | bytes 1815556
  13.7 10.1 %copy-start.10 = (bf16[192,768]{1,0:T(8,128)(2,1)S(1)}, bf16[192,768]{1,0:T(8,128)(2,1)}, u32[]{:S(2)}) copy-start(bf16[192,768]{1,0:T(8,128)(2,1)} %w_out.1) | copy-start | bytes 884740
  13.7 10.1 %copy-start.16 = (f32[768]{0:T(1024)S(1)}, f32[768]{0:T(1024)}, u32[]{:S(2)}) copy-start(f32[768]{0:T(1024)} %bias.3) | copy-start | bytes 9220
  13.7 10.0 %copy-start.17 = (f32[768]{0:T(1024)S(1)}, f32[768]{0:T(1024)}, u32[]{:S(2)}) copy-start(f32[768]{0:T(1024)} %gain.6) | copy-start | bytes 9220
  19.2 4.5 %collective-permute-start.6 = (bf16[394,192]{1,0:T(8,128)(2,1)S(1)}, bf16[394,192]{1,0:T(8,128)(2,1)S(1)}, u32[]{:S(2)}, u32[]{:S(2)}) collective-permute-start(bf16[394,192]{1,0:T(8,128)(2,1)S(1)} %collective-permute-done.5.rest_2_), channel_id=1, source_target_pairs={{0,8},{8,0},{16,24},{24,16},{1,9},{9,1},{17,25},{25,17},{2,10},{10... | collective-permute-start | bytes 453896 | tf_op jit(solution)/shard_map/ppermute | solution.py:431
  19.2 7.3 %collective-permute-start.8 = (bf16[72,768]{1,0:T(8,128)(2,1)S(1)}, bf16[72,768]{1,0:T(8,128)(2,1)S(1)}, u32[]{:S(2)}, u32[]{:S(2)}) collective-permute-start(bf16[72,768]{1,0:T(8,128)(2,1)S(1)} %get-tuple-element.130), channel_id=1, source_target_pairs={{0,2},{2,0},{4,6},{6,4},{1,3},{3,1},{5,7},{7,5},{8,10},{10,8},{12,... | collective-permute-start | bytes 331784 | tf_op jit(solution)/shard_map/ppermute | solution.py:434
  21.0 11.5 %collective-permute-start.9 = (bf16[72,768]{1,0:T(8,128)(2,1)S(1)}, bf16[72,768]{1,0:T(8,128)(2,1)S(1)}, u32[]{:S(2)}, u32[]{:S(2)}) collective-permute-start(bf16[72,768]{1,0:T(8,128)(2,1)S(1)} %get-tuple-element.131), channel_id=1, source_target_pairs={{0,4},{2,6},{4,0},{6,2},{1,5},{3,7},{5,1},{7,3},{8,12},{10,14},{12... | collective-permute-start | bytes 331784 | tf_op jit(solution)/shard_map/ppermute | solution.py:434
  23.6 20.9 %copy-start = (bf16[1,768,768]{2,1,0:T(8,128)(2,1)S(1)}, bf16[1,768,768]{2,1,0:T(8,128)(2,1)}, u32[]{:S(2)}) copy-start(bf16[1,768,768]{2,1,0:T(8,128)(2,1)} %param.23) | copy-start | bytes 3538948
  23.6 20.9 %copy-start.1 = (bf16[1,768,768]{2,1,0:T(8,128)(2,1)S(1)}, bf16[1,768,768]{2,1,0:T(8,128)(2,1)}, u32[]{:S(2)}) copy-start(bf16[1,768,768]{2,1,0:T(8,128)(2,1)} %param.24) | copy-start | bytes 3538948
  23.6 20.9 %copy-start.3 = (bf16[768,768]{1,0:T(8,128)(2,1)S(1)}, bf16[768,768]{1,0:T(8,128)(2,1)}, u32[]{:S(2)}) copy-start(bf16[768,768]{1,0:T(8,128)(2,1)} %copy-done.2) | copy-start | bytes 3538948
  23.7 8.9 %collective-permute-start.10 = (bf16[72,768]{1,0:T(8,128)(2,1)S(1)}, bf16[72,768]{1,0:T(8,128)(2,1)S(1)}, u32[]{:S(2)}, u32[]{:S(2)}) collective-permute-start(bf16[72,768]{1,0:T(8,128)(2,1)S(1)} %get-tuple-element.132), channel_id=1, source_target_pairs={{0,6},{2,4},{4,2},{6,0},{1,7},{3,5},{5,3},{7,1},{8,14},{10,12},{12... | collective-permute-start | bytes 331784 | tf_op jit(solution)/shard_map/ppermute | solution.py:434
  32.6 11.9 %collective-permute-start.11 = (bf16[3,72,768]{2,1,0:T(8,128)(2,1)S(1)}, bf16[3,72,768]{2,1,0:T(8,128)(2,1)S(1)}, u32[]{:S(2)}, u32[]{:S(2)}) collective-permute-start(bf16[3,72,768]{2,1,0:T(8,128)(2,1)S(1)} %pad_maximum_fusion.2), channel_id=1, source_target_pairs={{0,16},{8,24},{16,0},{24,8},{1,17},{9,25},{17,1},{25,9},{2,18},{10... | collective-permute-start | bytes 995336 | tf_op jit(solution)/shard_map/ppermute | solution.py:431
  34.2 10.3 %collective-permute-start.12 = (bf16[144,768]{1,0:T(8,128)(2,1)S(1)}, bf16[144,768]{1,0:T(8,128)(2,1)S(1)}, u32[]{:S(2)}, u32[]{:S(2)}) collective-permute-start(bf16[144,768]{1,0:T(8,128)(2,1)S(1)} %get-tuple-element.141), channel_id=1, source_target_pairs={{0,2},{2,0},{4,6},{6,4},{1,3},{3,1},{5,7},{7,5},{8,10},{10,8},{12,... | collective-permute-start | bytes 663560 | tf_op jit(solution)/shard_map/ppermute | solution.py:434
  36.5 18.7 %collective-permute-start.14 = (bf16[144,768]{1,0:T(8,128)(2,1)S(1)}, bf16[144,768]{1,0:T(8,128)(2,1)S(1)}, u32[]{:S(2)}, u32[]{:S(2)}) collective-permute-start(bf16[144,768]{1,0:T(8,128)(2,1)S(1)} %get-tuple-element.147), channel_id=1, source_target_pairs={{0,4},{2,6},{4,0},{6,2},{1,5},{3,7},{5,1},{7,3},{8,12},{10,14},{12... | collective-permute-start | bytes 663560 | tf_op jit(solution)/shard_map/ppermute | solution.py:434
  37.5 17.7 %collective-permute-start.15 = (bf16[144,768]{1,0:T(8,128)(2,1)S(1)}, bf16[144,768]{1,0:T(8,128)(2,1)S(1)}, u32[]{:S(2)}, u32[]{:S(2)}) collective-permute-start(bf16[144,768]{1,0:T(8,128)(2,1)S(1)} %get-tuple-element.148), channel_id=1, source_target_pairs={{0,6},{2,4},{4,2},{6,0},{1,7},{3,5},{5,3},{7,1},{8,14},{10,12},{12... | collective-permute-start | bytes 663560 | tf_op jit(solution)/shard_map/ppermute | solution.py:434
  62.8 12.8 %collective-permute-start.20 = (bf16[1536,768]{1,0:T(8,128)(2,1)S(1)}, bf16[1536,768]{1,0:T(8,128)(2,1)S(1)}, u32[]{:S(2)}, u32[]{:S(2)}) collective-permute-start(bf16[1536,768]{1,0:T(8,128)(2,1)S(1)} %get-tuple-element.168), channel_id=1, source_target_pairs={{0,8},{8,0},{16,24},{24,16},{1,9},{9,1},{17,25},{25,17},{2,10},{10... | collective-permute-start | bytes 7077896 | tf_op jit(solution)/shard_map/ppermute | solution.py:431
  62.9 8.3 %collective-permute-start.18 = (bf16[2,72,768]{2,1,0:T(8,128)(2,1)S(1)}, bf16[2,72,768]{2,1,0:T(8,128)(2,1)S(1)}, u32[]{:S(2)}, u32[]{:S(2)}) collective-permute-start(bf16[2,72,768]{2,1,0:T(8,128)(2,1)S(1)} %get-tuple-element.152), channel_id=1, source_target_pairs={{0,16},{8,24},{16,0},{24,8},{1,17},{9,25},{17,1},{25,9},{2,18},{10... | collective-permute-start | bytes 663560 | tf_op jit(solution)/shard_map/ppermute | solution.py:431
  63.4 12.0 %collective-permute-start.19 = (bf16[2,72,768]{2,1,0:T(8,128)(2,1)S(1)}, bf16[2,72,768]{2,1,0:T(8,128)(2,1)S(1)}, u32[]{:S(2)}, u32[]{:S(2)}) collective-permute-start(bf16[2,72,768]{2,1,0:T(8,128)(2,1)S(1)} %get-tuple-element.154), channel_id=1, source_target_pairs={{0,16},{8,24},{16,0},{24,8},{1,17},{9,25},{17,1},{25,9},{2,18},{10... | collective-permute-start | bytes 663560 | tf_op jit(solution)/shard_map/ppermute | solution.py:431
  65.0 12.9 %collective-permute-start.13 = (bf16[144,768]{1,0:T(8,128)(2,1)S(1)}, bf16[144,768]{1,0:T(8,128)(2,1)S(1)}, u32[]{:S(2)}, u32[]{:S(2)}) collective-permute-start(bf16[144,768]{1,0:T(8,128)(2,1)S(1)} %get-tuple-element.144), channel_id=1, source_target_pairs={{0,2},{2,0},{4,6},{6,4},{1,3},{3,1},{5,7},{7,5},{8,10},{10,8},{12,... | collective-permute-start | bytes 663560 | tf_op jit(solution)/shard_map/ppermute | solution.py:434
  68.1 18.2 %collective-permute-start.16 = (bf16[144,768]{1,0:T(8,128)(2,1)S(1)}, bf16[144,768]{1,0:T(8,128)(2,1)S(1)}, u32[]{:S(2)}, u32[]{:S(2)}) collective-permute-start(bf16[144,768]{1,0:T(8,128)(2,1)S(1)} %get-tuple-element.149), channel_id=1, source_target_pairs={{0,4},{2,6},{4,0},{6,2},{1,5},{3,7},{5,1},{7,3},{8,12},{10,14},{12... | collective-permute-start | bytes 663560 | tf_op jit(solution)/shard_map/ppermute | solution.py:434
  71.2 15.1 %collective-permute-start.17 = (bf16[144,768]{1,0:T(8,128)(2,1)S(1)}, bf16[144,768]{1,0:T(8,128)(2,1)S(1)}, u32[]{:S(2)}, u32[]{:S(2)}) collective-permute-start(bf16[144,768]{1,0:T(8,128)(2,1)S(1)} %get-tuple-element.150), channel_id=1, source_target_pairs={{0,6},{2,4},{4,2},{6,0},{1,7},{3,5},{5,3},{7,1},{8,14},{10,12},{12... | collective-permute-start | bytes 663560 | tf_op jit(solution)/shard_map/ppermute | solution.py:434
  77.2 10.5 %copy-start.20 = (f32[768,768]{1,0:T(8,128)}, f32[768,768]{1,0:T(8,128)S(1)}, u32[]{:S(2)}) copy-start(f32[768,768]{1,0:T(8,128)S(1)} %get-tuple-element.225.kept) | copy-start | bytes 7077892
  87.8 21.1 %copy-start.5 = (bf16[768,3,192]{0,2,1:T(8,128)(2,1)S(1)}, bf16[768,3,192]{0,2,1:T(8,128)(2,1)}, u32[]{:S(2)}) copy-start(bf16[768,3,192]{0,2,1:T(8,128)(2,1)} %param.18) | copy-start | bytes 2654212
  87.8 1.7 collective-permute-start.21
  89.6 9.6 %collective-permute-start.22 = (bf16[416,384]{1,0:T(8,128)(2,1)S(1)}, bf16[416,384]{1,0:T(8,128)(2,1)S(1)}, u32[]{:S(2)}, u32[]{:S(2)}) collective-permute-start(bf16[416,384]{1,0:T(8,128)(2,1)S(1)} %add_convert_fusion.1), channel_id=1, source_target_pairs={{0,16},{8,24},{16,0},{24,8},{1,17},{9,25},{17,1},{25,9},{2,18},{10... | collective-permute-start | bytes 958472 | tf_op jit(solution)/shard_map/ppermute | solution.py:431
  90.1 17.2 %collective-permute-start.23 = (bf16[256,768]{1,0:T(8,128)(2,1)S(1)}, bf16[256,768]{1,0:T(8,128)(2,1)S(1)}, u32[]{:S(2)}, u32[]{:S(2)}) collective-permute-start(bf16[256,768]{1,0:T(8,128)(2,1)S(1)} %get-tuple-element.177), channel_id=1, source_target_pairs={{0,1},{1,0},{2,3},{3,2},{4,5},{5,4},{6,7},{7,6},{8,9},{9,8},{10,11... | collective-permute-start | bytes 1179656 | tf_op jit(solution)/shard_map/ppermute | solution.py:437
  91.7 8.0 %collective-permute-start.24 = (bf16[72,768]{1,0:T(8,128)(2,1)S(1)}, bf16[72,768]{1,0:T(8,128)(2,1)S(1)}, u32[]{:S(2)}, u32[]{:S(2)}) collective-permute-start(bf16[72,768]{1,0:T(8,128)(2,1)S(1)} %get-tuple-element.179), channel_id=1, source_target_pairs={{0,2},{2,0},{4,6},{6,4},{1,3},{3,1},{5,7},{7,5},{8,10},{10,8},{12,... | collective-permute-start | bytes 331784 | tf_op jit(solution)/shard_map/ppermute | solution.py:434
  96.2 11.1 %collective-permute-start.25 = (bf16[72,768]{1,0:T(8,128)(2,1)S(1)}, bf16[72,768]{1,0:T(8,128)(2,1)S(1)}, u32[]{:S(2)}, u32[]{:S(2)}) collective-permute-start(bf16[72,768]{1,0:T(8,128)(2,1)S(1)} %get-tuple-element.180), channel_id=1, source_target_pairs={{0,4},{2,6},{4,0},{6,2},{1,5},{3,7},{5,1},{7,3},{8,12},{10,14},{12... | collective-permute-start | bytes 331784 | tf_op jit(solution)/shard_map/ppermute | solution.py:434
  97.2 10.1 %collective-permute-start.26 = (bf16[72,768]{1,0:T(8,128)(2,1)S(1)}, bf16[72,768]{1,0:T(8,128)(2,1)S(1)}, u32[]{:S(2)}, u32[]{:S(2)}) collective-permute-start(bf16[72,768]{1,0:T(8,128)(2,1)S(1)} %get-tuple-element.181), channel_id=1, source_target_pairs={{0,6},{2,4},{4,2},{6,0},{1,7},{3,5},{5,3},{7,1},{8,14},{10,12},{12... | collective-permute-start | bytes 331784 | tf_op jit(solution)/shard_map/ppermute | solution.py:434
  107.3 1.6 collective-permute-start.27
  113.9 6.8 %copy-start.22 = (f32[394,768]{1,0:T(8,128)}, f32[394,768]{1,0:T(8,128)S(1)}, u32[]{:S(2)}) copy-start(f32[394,768]{1,0:T(8,128)S(1)} %get-tuple-element.194.d_middle) | copy-start | bytes 3631108
  113.9 6.8 %copy-start.24 = (f32[16,768]{1,0:T(8,128)}, f32[16,768]{1,0:T(8,128)S(1)}, u32[]{:S(2)}) copy-start(f32[16,768]{1,0:T(8,128)S(1)} %get-tuple-element.213.small2) | copy-start | bytes 147460
  113.9 3.7 %collective-permute-start.35 = (bf16[394,384]{1,0:T(8,128)(2,1)S(1)}, bf16[394,384]{1,0:T(8,128)(2,1)S(1)}, u32[]{:S(2)}, u32[]{:S(2)}) collective-permute-start(bf16[394,384]{1,0:T(8,128)(2,1)S(1)} %get-tuple-element.211), channel_id=1, source_target_pairs={{0,8},{8,0},{16,24},{24,16},{1,9},{9,1},{17,25},{25,17},{2,10},{10... | collective-permute-start | bytes 907784 | tf_op jit(solution)/shard_map/ppermute | solution.py:431
  114.1 10.8 %collective-permute-start.30 = (bf16[192,768]{1,0:T(8,128)(2,1)S(1)}, bf16[192,768]{1,0:T(8,128)(2,1)S(1)}, u32[]{:S(2)}, u32[]{:S(2)}) collective-permute-start(bf16[192,768]{1,0:T(8,128)(2,1)S(1)} %get-tuple-element.204), channel_id=1, source_target_pairs={{0,3},{1,2},{2,1},{3,0},{4,7},{5,6},{6,5},{7,4},{8,11},{9,10},{10,... | collective-permute-start | bytes 884744 | tf_op jit(solution)/shard_map/ppermute | solution.py:441
  115.7 14.9 %collective-permute-start.31 = (bf16[192,768]{1,0:T(8,128)(2,1)S(1)}, bf16[192,768]{1,0:T(8,128)(2,1)S(1)}, u32[]{:S(2)}, u32[]{:S(2)}) collective-permute-start(bf16[192,768]{1,0:T(8,128)(2,1)S(1)} %get-tuple-element.205), channel_id=1, source_target_pairs={{0,1},{1,0},{2,3},{3,2},{4,5},{5,4},{6,7},{7,6},{8,9},{9,8},{10,11... | collective-permute-start | bytes 884744 | tf_op jit(solution)/shard_map/ppermute | solution.py:441
  117.3 13.3 %collective-permute-start.32 = (bf16[192,768]{1,0:T(8,128)(2,1)S(1)}, bf16[192,768]{1,0:T(8,128)(2,1)S(1)}, u32[]{:S(2)}, u32[]{:S(2)}) collective-permute-start(bf16[192,768]{1,0:T(8,128)(2,1)S(1)} %get-tuple-element.206), channel_id=1, source_target_pairs={{0,2},{1,3},{2,0},{3,1},{4,6},{5,7},{6,4},{7,5},{8,10},{9,11},{10,... | collective-permute-start | bytes 884744 | tf_op jit(solution)/shard_map/ppermute | solution.py:441
  117.7 16.9 %collective-permute-start.36 = (bf16[394,384]{1,0:T(8,128)(2,1)S(1)}, bf16[394,384]{1,0:T(8,128)(2,1)S(1)}, u32[]{:S(2)}, u32[]{:S(2)}) collective-permute-start(bf16[394,384]{1,0:T(8,128)(2,1)S(1)} %add_convert_fusion.3), channel_id=1, source_target_pairs={{0,16},{8,24},{16,0},{24,8},{1,17},{9,25},{17,1},{25,9},{2,18},{10... | collective-permute-start | bytes 907784 | tf_op jit(solution)/shard_map/ppermute | solution.py:431
  120.7 14.1 %collective-permute-start.28 = (bf16[400,384]{1,0:T(8,128)(2,1)S(1)}, bf16[400,384]{1,0:T(8,128)(2,1)S(1)}, u32[]{:S(2)}, u32[]{:S(2)}) collective-permute-start(bf16[400,384]{1,0:T(8,128)(2,1)S(1)} %get-tuple-element.202), channel_id=1, source_target_pairs={{0,8},{8,0},{16,24},{24,16},{1,9},{9,1},{17,25},{25,17},{2,10},{10... | collective-permute-start | bytes 921608 | tf_op jit(solution)/shard_map/ppermute | solution.py:431
  131.3 4.2 %copy-start.11 = (bf16[96,768]{1,0:T(8,128)(2,1)}, bf16[96,768]{1,0:T(8,128)(2,1)S(1)}, u32[]{:S(2)}) copy-start(bf16[96,768]{1,0:T(8,128)(2,1)S(1)} %get-tuple-element.209.own_b) | copy-start | bytes 442372
  131.3 9.9 %copy-start.19 = (f32[768]{0:T(1024)S(1)}, f32[768]{0:T(1024)}, u32[]{:S(2)}) copy-start(f32[768]{0:T(1024)} %gain.7) | copy-start | bytes 9220
  131.3 9.9 %collective-permute-start.33 = (bf16[96,768]{1,0:T(8,128)(2,1)}, bf16[96,768]{1,0:T(8,128)(2,1)}, u32[]{:S(2)}, u32[]{:S(2)}) collective-permute-start(bf16[96,768]{1,0:T(8,128)(2,1)} %get-tuple-element.207.own_a), channel_id=1, source_target_pairs={{0,4},{2,6},{4,0},{6,2},{1,5},{3,7},{5,1},{7,3},{8,12},{10,14},{12... | collective-permute-start | bytes 442376 | tf_op jit(solution)/shard_map/ppermute | solution.py:434
  133.1 24.7 %collective-permute-start.43 = (bf16[512,768]{1,0:T(8,128)(2,1)S(1)}, bf16[512,768]{1,0:T(8,128)(2,1)S(1)}, u32[]{:S(2)}, u32[]{:S(2)}) collective-permute-start(bf16[512,768]{1,0:T(8,128)(2,1)S(1)} %get-tuple-element.228), channel_id=1, source_target_pairs={{0,1},{1,0},{2,3},{3,2},{4,5},{5,4},{6,7},{7,6},{8,9},{9,8},{10,11... | collective-permute-start | bytes 2359304 | tf_op jit(solution)/shard_map/ppermute | solution.py:437
  134.7 6.6 %collective-permute-start.37 = (bf16[394,384]{1,0:T(8,128)(2,1)S(1)}, bf16[394,384]{1,0:T(8,128)(2,1)}, u32[]{:S(2)}, u32[]{:S(2)}) collective-permute-start(bf16[394,384]{1,0:T(8,128)(2,1)S(1)} %add_convert_fusion.2.own), channel_id=1, source_target_pairs={{0,8},{8,0},{16,24},{24,16},{1,9},{9,1},{17,25},{25,17},{2,10},{10... | collective-permute-start | bytes 907784 | tf_op jit(solution)/shard_map/ppermute | solution.py:431
  135.6 14.7 %collective-permute-start.29 = (bf16[400,384]{1,0:T(8,128)(2,1)}, bf16[400,384]{1,0:T(8,128)(2,1)}, u32[]{:S(2)}, u32[]{:S(2)}) collective-permute-start(bf16[400,384]{1,0:T(8,128)(2,1)} %add_convert_fusion.5), channel_id=1, source_target_pairs={{0,16},{8,24},{16,0},{24,8},{1,17},{9,25},{17,1},{25,9},{2,18},{10... | collective-permute-start | bytes 921608 | tf_op jit(solution)/shard_map/ppermute | solution.py:431
  141.2 10.1 %collective-permute-start.34 = (bf16[96,768]{1,0:T(8,128)(2,1)}, bf16[96,768]{1,0:T(8,128)(2,1)S(1)}, u32[]{:S(2)}, u32[]{:S(2)}) collective-permute-start(bf16[96,768]{1,0:T(8,128)(2,1)} %copy-done.11), channel_id=1, source_target_pairs={{0,4},{2,6},{4,0},{6,2},{1,5},{3,7},{5,1},{7,3},{8,12},{10,14},{12... | collective-permute-start | bytes 442376 | tf_op jit(solution)/shard_map/ppermute | solution.py:434
  142.3 1.3 copy-start.23
  144.4 7.9 %copy-start.12 = (bf16[96,768]{1,0:T(8,128)(2,1)S(1)}, bf16[96,768]{1,0:T(8,128)(2,1)}, u32[]{:S(2)}) copy-start(bf16[96,768]{1,0:T(8,128)(2,1)} %copy-done.11) | copy-start | bytes 442372
  147.3 5.0 %collective-permute-start.38 = (f32[16,768]{1,0:T(8,128)S(1)}, f32[16,768]{1,0:T(8,128)S(1)}, u32[]{:S(2)}, u32[]{:S(2)}) collective-permute-start(f32[16,768]{1,0:T(8,128)S(1)} %get-tuple-element.214.small), channel_id=1, source_target_pairs={{0,4},{2,6},{4,0},{6,2},{1,5},{3,7},{5,1},{7,3},{8,12},{10,14},{12... | collective-permute-start | bytes 147464 | tf_op jit(solution)/shard_map/ppermute | solution.py:434
  151.4 6.4 %copy-start.21 = (f32[768,768]{1,0:T(8,128)S(1)}, f32[768,768]{1,0:T(8,128)}, u32[]{:S(2)}) copy-start(f32[768,768]{1,0:T(8,128)} %copy-done.20) | copy-start | bytes 7077892
  153.4 6.1 %collective-permute-start.39 = (bf16[400,384]{1,0:T(8,128)(2,1)S(1)}, bf16[400,384]{1,0:T(8,128)(2,1)S(1)}, u32[]{:S(2)}, u32[]{:S(2)}) collective-permute-start(bf16[400,384]{1,0:T(8,128)(2,1)S(1)} %add_convert_fusion.4), channel_id=1, source_target_pairs={{0,8},{8,0},{16,24},{24,16},{1,9},{9,1},{17,25},{25,17},{2,10},{10... | collective-permute-start | bytes 921608 | tf_op jit(solution)/shard_map/ppermute | solution.py:431
  153.4 9.9 %collective-permute-start.40 = (bf16[208,768]{1,0:T(8,128)(2,1)S(1)}, bf16[208,768]{1,0:T(8,128)(2,1)S(1)}, u32[]{:S(2)}, u32[]{:S(2)}) collective-permute-start(bf16[208,768]{1,0:T(8,128)(2,1)S(1)} %shard_map.225.refs_0_), channel_id=1, source_target_pairs={{0,1},{1,0},{2,3},{3,2},{4,5},{5,4},{6,7},{7,6},{8,9},{9,8},{10,11... | collective-permute-start | bytes 958472 | tf_op jit(solution)/shard_map/ppermute | solution.py:441
  154.9 10.7 %collective-permute-start.41 = (bf16[208,768]{1,0:T(8,128)(2,1)S(1)}, bf16[208,768]{1,0:T(8,128)(2,1)S(1)}, u32[]{:S(2)}, u32[]{:S(2)}) collective-permute-start(bf16[208,768]{1,0:T(8,128)(2,1)S(1)} %shard_map.225.refs_0_), channel_id=1, source_target_pairs={{0,2},{1,3},{2,0},{3,1},{4,6},{5,7},{6,4},{7,5},{8,10},{9,11},{10,... | collective-permute-start | bytes 958472 | tf_op jit(solution)/shard_map/ppermute | solution.py:441
  157.2 15.2 %collective-permute-start.42 = (bf16[208,768]{1,0:T(8,128)(2,1)S(1)}, bf16[208,768]{1,0:T(8,128)(2,1)S(1)}, u32[]{:S(2)}, u32[]{:S(2)}) collective-permute-start(bf16[208,768]{1,0:T(8,128)(2,1)S(1)} %shard_map.225.refs_0_), channel_id=1, source_target_pairs={{0,3},{1,2},{2,1},{3,0},{4,7},{5,6},{6,5},{7,4},{8,11},{9,10},{10,... | collective-permute-start | bytes 958472 | tf_op jit(solution)/shard_map/ppermute | solution.py:441
  (6 other events, 5.5 us)

commit v3 on v2

--- a/solution.py
+++ b/solution.py
@@ -98,7 +98,21 @@
     router_pad[:experts, :] = router[...]
 
 
-def attend_kernel(images, tokens, gain, bias, weight, normed, query, key, value, probs, head_out):
+def attend_kernel(
+    images, tokens_far, gain_far, bias_far, weight_far,
+    normed, query, key, value, probs, head_out,
+    tokens, gain, bias, weight, arrivals,
+):
+    copies = [
+        pltpu.make_async_copy(source, target, arrivals.at[at])
+        for at, (source, target) in enumerate(
+            ((tokens_far, tokens), (gain_far, gain), (bias_far, bias), (weight_far, weight))
+        )
+    ]
+    for copy in copies:
+        copy.start()
+    for copy in copies:
+        copy.wait()
     rows = tokens.shape[0]
     inner = query.shape[1]
     heads = inner // HEAD_DIM
@@ -165,7 +179,7 @@
             here = pl.multiple_of(k * size + far * quarter, 8)
             there = pl.multiple_of(k * size + (1 - far) * quarter, 8)
             d_out[pl.ds(here, quarter), :] = out_blocks[k][...].astype(F32)
-            d_out[pl.ds(there, quarter), :] = pair_out[places[k] - 1].astype(F32)
+            d_out[pl.ds(there, quarter), :] = pair_out[places[k] - 2].astype(F32)
     lane = iota((count, LANES), 1)
     logits = dot_nt(rows_in[...], router[...])
     logits = jnp.where(lane < experts, logits, -1e30)
@@ -232,10 +246,8 @@
         out[at : at + width, :] = total.astype(BF16)
 
 
-def gated_sum_kernel(kept_a, came_a, kept_b, came_b, *blocks):
-    for k in range(4):
-        kept, came = (kept_a, came_a) if k < 2 else (kept_b, came_b)
-        blocks[k][...] = (kept[k % 2].astype(F32) + came[k % 2].astype(F32)).astype(BF16)
+def gated_sum_kernel(kept, came, out):
+    out[...] = (kept[...].astype(F32) + came[...].astype(F32)).astype(BF16)
 
 
 def weight_grad_kernel(*refs):
@@ -274,13 +286,14 @@
     grad_down[half:, :] = kept[half:, half:] + came[half:, half:].astype(F32)
 
 
-def combine_kernel(experts, parts, base, ids, table, *refs):
+def combine_kernel(experts, parts, base, ids, table, part, *refs):
     blocks = refs[:experts]
     routers = refs[experts : experts + parts]
     kept, sent, total = refs[experts + parts :]
     value = dot_tn(table[ids[E_ID]], blocks[0][...])
     for k in range(1, experts):
-        value = value + dot_tn(table[ids[E_ID] ^ k], blocks[k][...])
+        spots = table if blocks[k].shape[0] == table.shape[1] else part
+        value = value + dot_tn(spots[ids[E_ID] ^ k], blocks[k][...])
     total[...] = jnp.zeros_like(total)
     total[: value.shape[0], :] = value
     if parts:
@@ -300,12 +313,12 @@
 
 
 def back_kernel(
-    blocks_n, ids, own, other, middle, cot, gain, w_out, head_out, normed, query, key, value,
+    split, ids, own, other, middle, cot, gain, w_out, head_out, normed, query, key, value,
     probs, weight, *rest
 ):
     d_middle, kept, sent, small = rest[:4]
-    blocks = rest[4 : 4 + blocks_n]
-    whole, grads = rest[4 + blocks_n :]
+    blocks = rest[4:-2]
+    whole, grads = rest[-2:]
     rows, inner = query.shape
     heads = inner // HEAD_DIM
     joined(ids, own, other, whole)
@@ -341,13 +354,22 @@
     grads[:inner, :] = dot_tn(d_query, normed[...]).astype(BF16)
     grads[inner : 2 * inner, :] = dot_tn(d_key, normed[...]).astype(BF16)
     grads[2 * inner : 3 * inner, :] = dot_tn(d_value, normed[...]).astype(BF16)
-    if blocks_n == 1:
+    if not split:
         blocks[0][...] = grads[...]
     else:
-        size = blocks[0].shape[0]
-        for m in range(blocks_n):
-            at = pl.multiple_of((ids[Q_ID] ^ m) * size, 16)
-            blocks[m][...] = grads[pl.ds(at, size), :]
+        mine, over_y, over_z, kept_left, kept_right = blocks
+        size, half = kept_left.shape
+
+        def piece(mask):
+            return pl.ds(pl.multiple_of((ids[Q_ID] ^ mask) * size, 16), size)
+
+        mine[...] = grads[piece(0), :]
+        over_y[0] = grads[piece(1), :half]
+        over_y[1] = grads[piece(3), :half]
+        over_z[0] = grads[piece(2), half:]
+        over_z[1] = grads[piece(3), half:]
+        kept_left[...] = grads[piece(2), :half]
+        kept_right[...] = grads[piece(1), half:]
     d_in = dot_nn(d_query, weight[:inner])
     d_in = d_in + dot_nn(d_key, weight[inner : 2 * inner])
     whole[:rows, :] = d_in + dot_nn(d_value, weight[2 * inner :])
@@ -368,14 +390,21 @@
     ).astype(BF16)
 
 
-def sum_kernel(count, *refs):
-    size = refs[0].shape[0] // 2
-    for half in range(2):
-        part = pl.ds(half * size, size)
-        total = refs[0][part, :].astype(F32)
-        for m in range(1, count):
-            total = total + refs[m][part, :].astype(F32)
-        refs[count + half][...] = total.astype(BF16)
+def scatter_kernel(mine, kept_left, kept_right, came_y, came_z, total, next_z, next_y):
+    half = kept_left.shape[1]
+    total[:, :half] = mine[:, :half].astype(F32) + came_y[0].astype(F32)
+    total[:, half:] = mine[:, half:].astype(F32) + came_z[0].astype(F32)
+    next_z[...] = (kept_left[...].astype(F32) + came_y[1].astype(F32)).astype(BF16)
+    next_y[...] = (kept_right[...].astype(F32) + came_z[1].astype(F32)).astype(BF16)
+
+
+def sum_kernel(total, came_z, came_y, out_a, out_b):
+    size, half = came_z.shape
+    size = size // 2
+    for out, at in ((out_a, 0), (out_b, size)):
+        part = pl.ds(at, size)
+        out[:, :half] = (total[part, :half] + came_z[part, :].astype(F32)).astype(BF16)
+        out[:, half:] = (total[part, half:] + came_y[part, :].astype(F32)).astype(BF16)
 
 
 def pair_kernel(own_a, own_b, came_a, came_b, small, small_came, out):
@@ -408,18 +437,22 @@
     return lax.optimization_barrier((value,) + others)[0]
 
 
-def run(kernel, outs, args, scratch=(), micros=1.0, limit=16):
+def run(kernel, outs, args, scratch=(), micros=1.0, limit=16, far=False):
     smem = pl.BlockSpec(memory_space=pltpu.SMEM)
     vmem = pl.BlockSpec(memory_space=pltpu.VMEM)
+    held = pl.BlockSpec(memory_space=pltpu.HBM) if far else vmem
+    kinds = [pltpu.VMEM(shape, kind) for shape, kind in scratch]
+    if far:
+        kinds.append(pltpu.SemaphoreType.DMA((len(args),)))
     return pl.pallas_call(
         kernel,
         out_shape=[jax.ShapeDtypeStruct(shape, kind) for shape, kind in outs],
-        in_specs=[smem if arg.dtype == jnp.int32 and arg.ndim == 1 else vmem for arg in args],
+        in_specs=[smem if arg.dtype == jnp.int32 and arg.ndim == 1 else held for arg in args],
         out_specs=[vmem] * len(outs),
-        scratch_shapes=[pltpu.VMEM(shape, kind) for shape, kind in scratch],
+        scratch_shapes=kinds,
         compiler_params=pltpu.CompilerParams(vmem_limit_bytes=limit * 1024 * 1024),
         cost_estimate=pl.CostEstimate(
-            flops=int(micros * 1.15e9), bytes_accessed=1024, transcendentals=0
+            flops=int(micros * 2e7), bytes_accessed=1024, transcendentals=0
         ),
     )(*args)
 
@@ -496,7 +529,7 @@
         base = -(-rows // 16) * 16
         tall = base + -(-part_rows // 16) * 16
 
-        out_x, out_c = tensor_swap(w_out, 2), tensor_swap(w_out, 1)
+        out_c = tensor_swap(w_out, 1)
         up_b, down_b = tensor_swap(up_a, 1), tensor_swap(down_a, 1)
         normed, query, key, value, probs, head_out = run(
             functools.partial(attend_kernel, images),
@@ -504,14 +537,17 @@
             + [((rows, inner), BF16)] * 3
             + [((heads, rows, rows), BF16), ((rows, inner), BF16)],
             [tokens, ln1_gain, ln1_bias, weight],
+            scratch=[
+                ((rows, width), BF16), ((width,), F32), ((width,), F32), ((3 * inner, width), BF16)
+            ],
             micros=4,
-        )
-        head_out, out_x, out_c, up_b, down_b = lax.optimization_barrier(
-            (head_out, out_x, out_c, up_b, down_b)
-        )
+            far=True,
+        )
+        head_out, out_c, up_b, down_b = lax.optimization_barrier((head_out, out_c, up_b, down_b))
+        out_x = tensor_swap(after(w_out, head_out), 2)
         head_x, head_c = tensor_swap(head_out, 2), tensor_swap(head_out, 1)
         quarter = cap // 2
-        cot_shapes = [(cap, width)] + [(quarter if small_slice else cap, width)] * (experts - 1)
+        cot_shapes = [(quarter if small_slice and k > 1 else cap, width) for k in range(experts)]
         table, part, router, *cot_blocks = run(
             functools.partial(plan_kernel, experts),
             [((experts, cap, rows), BF16), ((experts, quarter, rows), BF16)]
@@ -536,9 +572,10 @@
             micros=3,
         )
         rows_in = exchange(row_blocks)
-        middle, *d_rows_in = lax.optimization_barrier((middle, *d_rows_in))
         if small_slice:
-            pair_out = tensor_swap(jnp.stack(d_rows_in[1:]), 2)
+            rows_in[1], *far_out = lax.optimization_barrier((rows_in[1], *d_rows_in[2:]))
+            d_rows_in[2:] = far_out
+            pair_out = tensor_swap(jnp.stack(far_out), 2)
         else:
             pair_out = router
 
@@ -552,13 +589,14 @@
             results = run(
                 functools.partial(expert_kernel, experts, call, not last),
                 [((cap, width), BF16)] * len(call)
-                + [((len(call), quarter if small_slice else cap, width), BF16)] * 2
+                + [((len(call), quarter if worked else cap, width), BF16)] * 2
                 + [((count, width), BF16)] * 2
                 + [((count, hidden_width), BF16)] * 4
                 + [((part_rows, width), F32)]
                 + grads,
                 [ids, up_a, up_b, down_a, down_b]
-                + [after(router, worked[-1][6]) if worked else router, pair_out]
+                + [after(router, worked[-1][6]) if worked else router]
+                + [pair_out if worked or not small_slice else router]
                 + [rows_in[k] for k in call]
                 + [d_rows_in[k] for k in call],
                 scratch=[((count, width), F32)],
@@ -569,16 +607,21 @@
             gated.append(results[len(call) : len(call) + 2])
             worked.append(results[len(call) + 2 :])
 
-        def combine(blocks, spots, routers):
+        def combine(blocks, routers):
             return run(
                 functools.partial(combine_kernel, experts, len(routers), base),
                 [((tall if routers else base, half), BF16)] * 2,
-                [ids, spots] + blocks + routers,
+                [ids, table, part] + blocks + routers,
                 scratch=[((tall if routers else base, width), F32)],
                 micros=2,
             )
 
-        d_home = exchange(d_back)
+        if small_slice:
+            home = {k: expert_swap(d_back[k], k) for k in (3, 1)}
+            home[2] = expert_swap(after(d_back[2], home[3]), 2)
+            d_home = [d_back[0]] + [home[k] for k in (1, 2, 3)]
+        else:
+            d_home = exchange(d_back)
 
         grad_own, grad_pair = run(
             weight_grad_kernel,
@@ -598,34 +641,42 @@
         )
 
         if small_slice:
-            (kept_a, sent_a), (kept_b, sent_b) = gated
-            gated_blocks = run(
+            (gated_far,) = run(
                 gated_sum_kernel,
-                [((quarter, width), BF16)] * 4,
-                [kept_a, tensor_swap(sent_a, 2), kept_b, tensor_swap(sent_b, 2)],
+                [((2, quarter, width), BF16)],
+                [gated[1][0], tensor_swap(gated[1][1], 2)],
             )
-            spots = part
+            gated_near = [gated[0][0][0], gated[0][0][1]]
+            *d_home, gated_far, sent_first = lax.optimization_barrier(
+                (*d_home, gated_far, sent_first)
+            )
         else:
-            gated_blocks = [gated[0][0][k] for k in range(experts)]
-            spots = table
-
-        *d_home, sent_first = lax.optimization_barrier((*d_home, *gated_blocks, sent_first))
-        d_home, gated_blocks = d_home[:experts], d_home[experts:]
-        kept, sent = combine(list(d_home), table, [one[6] for one in worked])
+            gated_home = exchange([gated[0][0][k] for k in range(experts)])
+            *d_home, sent_first = lax.optimization_barrier((*d_home, sent_first))
+        kept, sent = combine(list(d_home), [one[6] for one in worked])
         chip = (kept.astype(F32) + tensor_swap(sent, 1).astype(F32)).astype(BF16)
         own = (chip.astype(F32) + tensor_swap(chip, 2).astype(F32)).astype(BF16)
-        gated_home = exchange(list(gated_blocks))
         came_first = dp_swap(sent_first)
-        own, came_first, *gated_home = lax.optimization_barrier((own, came_first, *gated_home))
+        if small_slice:
+            far_home = expert_swap(gated_far, 2)
+            near_home = expert_swap(gated_near[1], 1)
+            own, came_first, far_home, near_home = lax.optimization_barrier(
+                (own, came_first, far_home, near_home)
+            )
+            gated_home = [gated_near[0], near_home, far_home[0], expert_swap(far_home[1], 1)]
         other = tensor_swap(own, 1)
 
-        parts = 4 if small_slice else 1
+        size = inner
+        if small_slice:
+            grad_shapes = [(size, width), (2, size, half), (2, size, half), (size, half), (size, half)]
+        else:
+            grad_shapes = [(4 * size, width)]
         d_middle, kept1, sent1, small2, *grad_blocks = run(
-            functools.partial(back_kernel, parts),
+            functools.partial(back_kernel, small_slice),
             [((rows, width), F32)]
             + [((rows, half), BF16)] * 2
             + [((small_rows, width), F32)]
-            + [((4 * inner // parts, width), BF16)] * parts,
+            + [(shape, BF16) for shape in grad_shapes],
             [
                 ids, own, other, middle, cotangent, ln2_gain, w_out, head_out, normed, query,
                 key, value, probs, weight,
@@ -635,25 +686,26 @@
         )
 
         *gated_home, _ = lax.optimization_barrier((*gated_home, d_middle))
-        kept_y, sent_y = combine(list(gated_home), spots, [])
+        kept_y, sent_y = combine(list(gated_home), [])
 
         if small_slice:
-            arrived = [grad_blocks[0]] + [quarter_swap(grad_blocks[m], m) for m in (3, 1, 2)]
-            arrived[0], kept_y, sent_y = lax.optimization_barrier((arrived[0], kept_y, sent_y))
-            size = grad_blocks[0].shape[0]
+            mine, over_y, over_z, kept_left, kept_right = grad_blocks
+            total, next_z, next_y = run(
+                scatter_kernel,
+                [((size, width), F32)] + [((size, half), BF16)] * 2,
+                [mine, kept_left, kept_right, dp_swap(over_y), expert_swap(over_z, 1)],
+            )
+        chip1 = (kept1.astype(F32) + tensor_swap(sent1, 1).astype(F32)).astype(BF16)
+        own1 = (chip1.astype(F32) + tensor_swap(chip1, 2).astype(F32)).astype(BF16)
+        if small_slice:
+            total, kept_y, sent_y, own1 = lax.optimization_barrier((total, kept_y, sent_y, own1))
             summed_a, summed_b = run(
-                functools.partial(sum_kernel, 4), [((size // 2, width), BF16)] * 2, arrived
+                sum_kernel,
+                [((size // 2, width), BF16)] * 2,
+                [total, expert_swap(next_z, 1), dp_swap(next_y)],
             )
             sent_rest = after(sent_rest, summed_a)
             came_a = expert_swap(summed_a, 2)
-            came_b = expert_swap(after(summed_b, came_a), 2)
-        chip_y = (kept_y.astype(F32) + tensor_swap(sent_y, 1).astype(F32)).astype(BF16)
-        own_y = (chip_y.astype(F32) + tensor_swap(chip_y, 2).astype(F32)).astype(BF16)
-
-        chip1 = (kept1.astype(F32) + tensor_swap(sent1, 1).astype(F32)).astype(BF16)
-        own1 = (chip1.astype(F32) + tensor_swap(chip1, 2).astype(F32)).astype(BF16)
-        if small_slice:
-            own1 = after(own1, summed_a)
         other1 = tensor_swap(own1, 1)
         grad_tokens, small = run(
             last_norm_kernel,
@@ -662,7 +714,10 @@
             scratch=[((rows, width), F32)],
             micros=2,
         )
+        chip_y = (kept_y.astype(F32) + tensor_swap(sent_y, 1).astype(F32)).astype(BF16)
+        own_y = (chip_y.astype(F32) + tensor_swap(chip_y, 2).astype(F32)).astype(BF16)
         if small_slice:
+            came_b = expert_swap(after(summed_b, came_a, small), 2)
             (ready,) = run(
                 pair_kernel,
                 [((size + small_rows, width), BF16)],

time: 175 us -> 189 us (1.080)
  local copies, waits for them, and re-layouts: 6.94 us -> 17.4 us
  waiting for transfers between devices: 71.8 us -> 76.4 us
    ppermute x6 -> x3, waiting for transfers between devices: 21.8 us -> 8.89 us  [quarter_swap(): return lax.ppermute(value, ('expert', 'dp'), pairs)]
    ppermute x15 -> x17, waiting for transfers between devices: 37.3 us -> 49.8 us  [expert_swap(): lax.ppermute(value, 'expert', [(i, i ^ mask) for i in range(n_expert)])]
    unnamed x52 -> x76, local copies, waits for them, and re-layouts: 6.86 us -> 17.2 us
    ppermute x21 -> x20, waiting for transfers between devices: 12.6 us -> 17.7 us  [tensor_swap(): lax.ppermute(value, 'tensor', [(i, i ^ mask) for i in range(n_tensor)])]
    ppermute x6 -> x3, starting transfers between devices: 7.84 us -> 3.49 us  [quarter_swap(): return lax.ppermute(value, ('expert', 'dp'), pairs)]
    ppermute x15 -> x17, starting transfers between devices: 27.2 us -> 31.2 us  [expert_swap(): lax.ppermute(value, 'expert', [(i, i ^ mask) for i in range(n_expert)])]
    ppermute x21 -> x20, starting transfers between devices: 13.4 us -> 10.4 us  [tensor_swap(): lax.ppermute(value, 'tensor', [(i, i ^ mask) for i in range(n_tensor)])]
    ppermute x2 -> x4, starting transfers between devices: 3.09 us -> 5.08 us  [dp_swap(): return lax.ppermute(value, 'dp', [(i, i ^ 1) for i in range(n_dp)])]
  transfers between devices with their start and end apart: 44 -> 44, of which waited for: 21 -> 22; matrix products, arithmetic and copies ran while one was open for 2% -> 2% of each run, Pallas kernels for 13% -> 10%
where the time goes in v3:
time: 189 us; the launch traced here: 188 us
  waiting for transfers between devices  76.4 us (40%)
  starting transfers between devices  50.1 us (27%)
  Pallas kernels  39.1 us (21%)
  local copies, waits for them, and re-layouts  17.4 us (9%)
  other arithmetic  3.56 us (2%)
    ppermute x17, waiting for transfers between devices, expert_swap(): lax.ppermute(value, 'expert', [(i, i ^ mask) for i in range(n_expert)])  49.8 us
    pallas_call x17, Pallas kernels, run(): pl.pallas_call(kernel, out_shape=[jax.ShapeDtypeStruct(shape, kind) for s...  39.1 us
    ppermute x17, starting transfers between devices, expert_swap(): lax.ppermute(value, 'expert', [(i, i ^ mask) for i in range(n_expert)])  31.2 us
    ppermute x20, waiting for transfers between devices, tensor_swap(): lax.ppermute(value, 'tensor', [(i, i ^ mask) for i in range(n_tensor)])  17.7 us
    unnamed x76, local copies, waits for them, and re-layouts  17.2 us
    ppermute x20, starting transfers between devices, tensor_swap(): lax.ppermute(value, 'tensor', [(i, i ^ mask) for i in range(n_tensor)])  10.4 us
    ppermute x3, waiting for transfers between devices, quarter_swap(): return lax.ppermute(value, ('expert', 'dp'), pairs)  8.89 us
    ppermute x4, starting transfers between devices, dp_swap(): return lax.ppermute(value, 'dp', [(i, i ^ 1) for i in range(n_dp)])  5.08 us
  transfers between devices with their start and end apart: 44, of which 22 were waited for; matrix products, arithmetic and copies ran while one was open for 2% of the time, Pallas kernels for 10%

profile of v3, /device:TPU:0, one launch (start us, length us, event | category | flops | bytes accessed | tf_op | source)
XLA Modules:
  0.0 188.3 jit_solution(15896416595843727143)
XLA Ops:
  1.7 1.1 copy-done
  2.8 1.2 copy-done.6
  5.3 2.9 %shard_map.212 = (bf16[394,768]{1,0:T(8,128)(2,1)S(1)}, bf16[394,192]{1,0:T(8,128)(2,1)S(1)}, bf16[394,192]{1,0:T(8,128)(2,1)S(1)}, bf16[394,192]{1,0:T(8,128)(2...) custom-call(bf16[394,768]{1,0:T(8,128)(2,1)S(1)} %copy-done, f32[768]{0:T(1024)S(1)} %copy-done.31, ...), custom_call_target="tpu_custom_call" | custom-call | flops 80000000 | bytes 1024 | tf_op jit(solution)/shard_map/pallas_call | solution.py:447
  8.2 1.0 copy-done.12
  12.8 1.0 copy-done.4
  13.8 2.6 %collective-permute-start.6 = (bf16[192,768]{1,0:T(8,128)(2,1)S(1)}, bf16[192,768]{1,0:T(8,128)(2,1)S(1)}, u32[]{:S(2)}, u32[]{:S(2)}) collective-permute-start(bf16[192,768]{1,0:T(8,128)(2,1)S(1)} %copy-done.14), channel_id=1, source_target_pairs={{0,16},{8,24},{16,0},{24,8},{1,17},{9,25},{17,1},{25,9},{2,18},{10... | collective-permute-start | bytes 884744 | tf_op jit(solution)/shard_map/ppermute | solution.py:464
  16.4 7.8 %collective-permute-done.6.rest_6_ = bf16[192,768]{1,0:T(8,128)(2,1)S(1)} collective-permute-done((bf16[192,768]{1,0:T(8,128)(2,1)S(1)}, bf16[192,768]{1,0:T(8,128)(2,1)S(1)}, u32[]{:S(2)}, u32[]{:S(2)}) %collective-permute-start.6) | collective-permute-done | bytes 294944 | tf_op jit(solution)/shard_map/ppermute | solution.py:464
  25.5 1.1 copy-done.8
  26.6 1.4 shard_map.213
  30.6 1.0 copy-done.18
  31.5 1.0 copy-done.20
  32.5 1.0 copy-done.22
  33.5 0.9 copy-done.30
  34.4 2.7 %shard_map.214 = (f32[394,768]{1,0:T(8,128)S(1)}, bf16[144,768]{1,0:T(8,128)(2,1)S(1)}, bf16[144,768]{1,0:T(8,128)(2,1)S(1)}, bf16[144,768]{1,0:T(8,128)(2,1)S(1)}, bf16[144,768]{1,0:T(8,128)(2,1)S(1)}) custom-call(s32[8]{0:T(128)S(1)} %stack.38.ids, bf16[394,768]{1,0:T(8,128)(2,1)S(1)} %copy-done.1, f32[768]{0:T(1024)S(1)} %copy-done.33, ...), custom_call_target="tpu_custom_call" | custom-call | flops 60000000 | bytes 1024 | tf_op jit(solution)/shard_map/pallas_call | solution.py:447
  37.1 1.9 %collective-permute-start.8 = (bf16[144,768]{1,0:T(8,128)(2,1)S(1)}, bf16[144,768]{1,0:T(8,128)(2,1)S(1)}, u32[]{:S(2)}, u32[]{:S(2)}) collective-permute-start(bf16[144,768]{1,0:T(8,128)(2,1)S(1)} %get-tuple-element.127), channel_id=1, source_target_pairs={{0,2},{2,0},{4,6},{6,4},{1,3},{3,1},{5,7},{7,5},{8,10},{10,8},{12,... | collective-permute-start | bytes 663560 | tf_op jit(solution)/shard_map/ppermute | solution.py:467
  39.1 2.6 %collective-permute-start.9 = (bf16[72,768]{1,0:T(8,128)(2,1)S(1)}, bf16[72,768]{1,0:T(8,128)(2,1)S(1)}, u32[]{:S(2)}, u32[]{:S(2)}) collective-permute-start(bf16[72,768]{1,0:T(8,128)(2,1)S(1)} %get-tuple-element.128), channel_id=1, source_target_pairs={{0,4},{2,6},{4,0},{6,2},{1,5},{3,7},{5,1},{7,3},{8,12},{10,14},{12... | collective-permute-start | bytes 331784 | tf_op jit(solution)/shard_map/ppermute | solution.py:467
  41.6 0.9 collective-permute-start.11
  42.5 3.5 %collective-permute-start.14 = (bf16[144,768]{1,0:T(8,128)(2,1)S(1)}, bf16[144,768]{1,0:T(8,128)(2,1)S(1)}, u32[]{:S(2)}, u32[]{:S(2)}) collective-permute-start(bf16[144,768]{1,0:T(8,128)(2,1)S(1)} %get-tuple-element.139), channel_id=1, source_target_pairs={{0,4},{2,6},{4,0},{6,2},{1,5},{3,7},{5,1},{7,3},{8,12},{10,14},{12... | collective-permute-start | bytes 663560 | tf_op jit(solution)/shard_map/ppermute | solution.py:467
  46.0 1.2 collective-permute-done.9.refs_2_
  47.3 2.5 %collective-permute-start.15 = (bf16[144,768]{1,0:T(8,128)(2,1)S(1)}, bf16[144,768]{1,0:T(8,128)(2,1)S(1)}, u32[]{:S(2)}, u32[]{:S(2)}) collective-permute-start(bf16[144,768]{1,0:T(8,128)(2,1)S(1)} %get-tuple-element.140), channel_id=1, source_target_pairs={{0,6},{2,4},{4,2},{6,0},{1,7},{3,5},{5,3},{7,1},{8,14},{10,12},{12... | collective-permute-start | bytes 663560 | tf_op jit(solution)/shard_map/ppermute | solution.py:467
  49.7 2.8 %collective-permute-done.10.refs_3_ = bf16[72,768]{1,0:T(8,128)(2,1)S(1)} collective-permute-done((bf16[72,768]{1,0:T(8,128)(2,1)S(1)}, bf16[72,768]{1,0:T(8,128)(2,1)S(1)}, u32[]{:S(2)}, u32[]{:S(2)}) %collective-permute-start.10) | collective-permute-done | bytes 110624 | tf_op jit(solution)/shard_map/ppermute | solution.py:467
  52.6 1.6 collective-permute-start.13
  54.2 4.3 %collective-permute-done.11.refs_3_ = bf16[144,768]{1,0:T(8,128)(2,1)S(1)} collective-permute-done((bf16[144,768]{1,0:T(8,128)(2,1)S(1)}, bf16[144,768]{1,0:T(8,128)(2,1)S(1)}, u32[]{:S(2)}, u32[]{:S(2)}) %collective-permute-start.11) | collective-permute-done | bytes 221216 | tf_op jit(solution)/shard_map/ppermute | solution.py:467
  58.4 7.1 %shard_map.215 = (bf16[144,768]{1,0:T(8,128)(2,1)S(1)}, bf16[144,768]{1,0:T(8,128)(2,1)S(1)}, bf16[2,144,768]{2,1,0:T(8,128)(2,1)S(1)}, bf16[2,144,768]{2,1,0:T(...) custom-call(s32[8]{0:T(128)S(1)} %stack.38.ids, ...), custom_call_target="tpu_custom_call" | custom-call | flops 140000000 | bytes 1024 | tf_op jit(solution)/shard_map/pallas_call | solution.py:447
  65.6 1.7 collective-permute-done.14.refs_0_
  67.2 4.9 %shard_map.216 = (bf16[144,768]{1,0:T(8,128)(2,1)S(1)}, bf16[144,768]{1,0:T(8,128)(2,1)S(1)}, bf16[2,72,768]{2,1,0:T(8,128)(2,1)S(1)}, bf16[2,72,768]{2,1,0:T(8,...) custom-call(s32[8]{0:T(128)S(1)} %stack.38.ids, ...), custom_call_target="tpu_custom_call" | custom-call | flops 140000000 | bytes 1024 | tf_op jit(solution)/shard_map/pallas_call | solution.py:447
  72.1 2.7 %shard_map.218 = (bf16[1536,768]{1,0:T(8,128)(2,1)S(1)}, bf16[1536,768]{1,0:T(8,128)(2,1)S(1)}) custom-call(bf16[288,768]{1,0:T(8,128)(2,1)S(1)} %get-tuple-element.146.refs_0_, bf16[288,768]{1,0:T(8,128)(2,1)S(1)} %get-tuple-element.147.refs_1_, bf16[288,768]{1,0:T(8,128)(2,1)S(1)} %get-tuple-element.148.refs_2_, ...), custom_call_target="tpu_custom_call" | custom-call | flops 80000000 | bytes 1024 | tf_op jit(solution)/shard_map/pallas_call | solution.py:447
  74.9 2.5 %collective-permute-start.16 = (bf16[144,768]{1,0:T(8,128)(2,1)S(1)}, bf16[144,768]{1,0:T(8,128)(2,1)S(1)}, u32[]{:S(2)}, u32[]{:S(2)}) collective-permute-start(bf16[144,768]{1,0:T(8,128)(2,1)S(1)} %get-tuple-element.142), channel_id=1, source_target_pairs={{0,6},{2,4},{4,2},{6,0},{1,7},{3,5},{5,3},{7,1},{8,14},{10,12},{12... | collective-permute-start | bytes 663560 | tf_op jit(solution)/shard_map/ppermute | solution.py:467
  77.4 1.5 collective-permute-start.18
  78.9 3.3 %collective-permute-start.12 = (bf16[144,768]{1,0:T(8,128)(2,1)S(1)}, bf16[144,768]{1,0:T(8,128)(2,1)S(1)}, u32[]{:S(2)}, u32[]{:S(2)}) collective-permute-start(bf16[144,768]{1,0:T(8,128)(2,1)S(1)} %get-tuple-element.134), channel_id=1, source_target_pairs={{0,2},{2,0},{4,6},{6,4},{1,3},{3,1},{5,7},{7,5},{8,10},{10,8},{12,... | collective-permute-start | bytes 663560 | tf_op jit(solution)/shard_map/ppermute | solution.py:467
  82.2 2.8 %collective-permute-done.16.refs_3_ = bf16[144,768]{1,0:T(8,128)(2,1)S(1)} collective-permute-done((bf16[144,768]{1,0:T(8,128)(2,1)S(1)}, bf16[144,768]{1,0:T(8,128)(2,1)S(1)}, u32[]{:S(2)}, u32[]{:S(2)}) %collective-permute-start.16) | collective-permute-done | bytes 221216 | tf_op jit(solution)/shard_map/ppermute | solution.py:467
  85.0 5.8 %collective-permute-start.17 = (bf16[144,768]{1,0:T(8,128)(2,1)S(1)}, bf16[144,768]{1,0:T(8,128)(2,1)S(1)}, u32[]{:S(2)}, u32[]{:S(2)}) collective-permute-start(bf16[144,768]{1,0:T(8,128)(2,1)S(1)} %get-tuple-element.143), channel_id=1, source_target_pairs={{0,4},{2,6},{4,0},{6,2},{1,5},{3,7},{5,1},{7,3},{8,12},{10,14},{12... | collective-permute-start | bytes 663560 | tf_op jit(solution)/shard_map/ppermute | solution.py:467
  90.9 2.5 %shard_map.219 = (f32[768,768]{1,0:T(8,128)S(1)}, bf16[256,768]{1,0:T(8,128)(2,1)S(1)}, bf16[512,768]{1,0:T(8,128)(2,1)}) custom-call(s32[8]{0:T(128)S(1)} %stack.38.ids, bf16[1536,768]{1,0:T(8,128)(2,1)S(1)} %get-tuple-element.154.own, bf16[1536,768]{1,0:T(8,128)(2,1)S(1)} %collective-permute-done.19.came), custom_call_target="tpu_custom_call" | custom-call | flops 40000000 | bytes 1024 | tf_op jit(solution)/shard_map/pallas_call | solution.py:447
  93.4 7.8 %collective-permute-done.17.refs_2_ = bf16[144,768]{1,0:T(8,128)(2,1)S(1)} collective-permute-done((bf16[144,768]{1,0:T(8,128)(2,1)S(1)}, bf16[144,768]{1,0:T(8,128)(2,1)S(1)}, u32[]{:S(2)}, u32[]{:S(2)}) %collective-permute-start.17) | collective-permute-done | bytes 221216 | tf_op jit(solution)/shard_map/ppermute | solution.py:467
  101.2 1.5 shard_map.220
  102.8 1.6 collective-permute-done.20
  104.5 1.6 collective-permute-start.21
  106.1 1.5 collective-permute-start.22
  107.7 1.9 %collective-permute-start.23 = (bf16[2,72,768]{2,1,0:T(8,128)(2,1)S(1)}, bf16[2,72,768]{2,1,0:T(8,128)(2,1)S(1)}, u32[]{:S(2)}, u32[]{:S(2)}) collective-permute-start(bf16[2,72,768]{2,1,0:T(8,128)(2,1)S(1)} %shard_map.217), channel_id=1, source_target_pairs={{0,4},{2,6},{4,0},{6,2},{1,5},{3,7},{5,1},{7,3},{8,12},{10,14},{12... | collective-permute-start | bytes 663560 | tf_op jit(solution)/shard_map/ppermute | solution.py:467
  109.6 4.6 %collective-permute-done.21 = bf16[416,384]{1,0:T(8,128)(2,1)S(1)} collective-permute-done((bf16[416,384]{1,0:T(8,128)(2,1)S(1)}, bf16[416,384]{1,0:T(8,128)(2,1)S(1)}, u32[]{:S(2)}, u32[]{:S(2)}) %collective-permute-start.21) | collective-permute-done | bytes 319520 | tf_op jit(solution)/shard_map/ppermute | solution.py:464
  114.2 3.8 %collective-permute-done.24.refs_1_ = bf16[144,768]{1,0:T(8,128)(2,1)S(1)} collective-permute-done((bf16[144,768]{1,0:T(8,128)(2,1)S(1)}, bf16[144,768]{1,0:T(8,128)(2,1)S(1)}, u32[]{:S(2)}, u32[]{:S(2)}) %collective-permute-start.24) | collective-permute-done | bytes 221216 | tf_op jit(solution)/shard_map/ppermute | solution.py:467
  118.0 2.3 %collective-permute-done.23 = bf16[2,72,768]{2,1,0:T(8,128)(2,1)S(1)} collective-permute-done((bf16[2,72,768]{2,1,0:T(8,128)(2,1)S(1)}, bf16[2,72,768]{2,1,0:T(8,128)(2,1)S(1)}, u32[]{:S(2)}, u32[]{:S(2)}) %collective-permute-start.23) | collective-permute-done | bytes 221216 | tf_op jit(solution)/shard_map/ppermute | solution.py:467
  120.4 1.6 collective-permute-done.25.other
  122.0 5.0 %shard_map.221 = (f32[394,768]{1,0:T(8,128)S(1)}, bf16[394,384]{1,0:T(8,128)(2,1)S(1)}, bf16[394,384]{1,0:T(8,128)(2,1)S(1)}, f32[16,768]{1,0:T(8,128)S(1)}, bf1...) custom-call(s32[8]{0:T(128)S(1)} %stack.38.ids, ...), custom_call_target="tpu_custom_call" | custom-call | flops 120000000 | bytes 1024 | tf_op jit(solution)/shard_map/pallas_call | solution.py:447
  127.7 0.9 collective-permute-done.29
  129.4 1.1 collective-permute-start.28
  130.5 8.6 %collective-permute-done.28.refs_3_ = bf16[72,768]{1,0:T(8,128)(2,1)S(1)} collective-permute-done((bf16[72,768]{1,0:T(8,128)(2,1)S(1)}, bf16[72,768]{1,0:T(8,128)(2,1)S(1)}, u32[]{:S(2)}, u32[]{:S(2)}) %collective-permute-start.28) | collective-permute-done | bytes 110624 | tf_op jit(solution)/shard_map/ppermute | solution.py:467
  139.1 1.5 shard_map.223
  141.3 1.5 collective-permute-start.34
  143.5 3.7 %collective-permute-done.33.came_z = bf16[192,384]{1,0:T(8,128)(2,1)S(1)} collective-permute-done((bf16[192,384]{1,0:T(8,128)(2,1)S(1)}, bf16[192,384]{1,0:T(8,128)(2,1)S(1)}, u32[]{:S(2)}, u32[]{:S(2)}) %collective-permute-start.33) | collective-permute-done | bytes 147488 | tf_op jit(solution)/shard_map/ppermute | solution.py:467
  147.3 1.7 collective-permute-start.35
  149.0 1.5 collective-permute-start.43
  150.5 2.3 %shard_map.225 = (bf16[394,768]{1,0:T(8,128)(2,1)}, f32[16,768]{1,0:T(8,128)S(1)}) custom-call(s32[8]{0:T(128)S(1)} %stack.38.ids, bf16[394,384]{1,0:T(8,128)(2,1)S(1)} %add_convert_fusion.4.own, bf16[394,384]{1,0:T(8,128)(2,1)S(1)} %collective-permute-done.36.other, bf16[394,768]{1,0:T(8,128)(2,1)S(1)} %copy-done.1, ...), custom_call_target="tpu_custom_call" | custom-call | flops 40000000 | bytes 1024 | tf_op jit(solution)/shard_map/pallas_call | solution.py:447
  152.9 3.9 %collective-permute-done.35.came_a = bf16[96,768]{1,0:T(8,128)(2,1)S(1)} collective-permute-done((bf16[96,768]{1,0:T(8,128)(2,1)S(1)}, bf16[96,768]{1,0:T(8,128)(2,1)S(1)}, u32[]{:S(2)}, u32[]{:S(2)}) %collective-permute-start.35) | collective-permute-done | bytes 147488 | tf_op jit(solution)/shard_map/ppermute | solution.py:467
  156.8 2.9 %collective-permute-start.38 = (f32[16,768]{1,0:T(8,128)S(1)}, f32[16,768]{1,0:T(8,128)S(1)}, u32[]{:S(2)}, u32[]{:S(2)}) collective-permute-start(f32[16,768]{1,0:T(8,128)S(1)} %get-tuple-element.199.small), channel_id=1, source_target_pairs={{0,4},{2,6},{4,0},{6,2},{1,5},{3,7},{5,1},{7,3},{8,12},{10,14},{12... | collective-permute-start | bytes 147464 | tf_op jit(solution)/shard_map/ppermute | solution.py:467
  159.7 6.9 %collective-permute-done.38.small_came = f32[16,768]{1,0:T(8,128)S(1)} collective-permute-done((f32[16,768]{1,0:T(8,128)S(1)}, f32[16,768]{1,0:T(8,128)S(1)}, u32[]{:S(2)}, u32[]{:S(2)}) %collective-permute-start.38) | collective-permute-done | bytes 49184 | tf_op jit(solution)/shard_map/ppermute | solution.py:467
  167.5 1.5 collective-permute-start.40
  169.0 2.0 %collective-permute-start.42 = (bf16[208,768]{1,0:T(8,128)(2,1)S(1)}, bf16[208,768]{1,0:T(8,128)(2,1)}, u32[]{:S(2)}, u32[]{:S(2)}) collective-permute-start(bf16[208,768]{1,0:T(8,128)(2,1)S(1)} %shard_map.226.refs_0_), channel_id=1, source_target_pairs={{0,3},{1,2},{2,1},{3,0},{4,7},{5,6},{6,5},{7,4},{8,11},{9,10},{10,... | collective-permute-start | bytes 958472 | tf_op jit(solution)/shard_map/ppermute | solution.py:474
  171.0 1.7 copy-done.11
  172.7 1.7 shard_map.228
  174.3 2.3 %select_convert_fusion = bf16[394,768]{1,0:T(8,128)(2,1)} fusion(f32[394,768]{1,0:T(8,128)S(1)} %get-tuple-element.121.middle, bf16[400,384]{1,0:T(8,128)(2,1)} %collective-permute-done.39, bf16[400,384]{1,0:T(8,128)(2,1)} %add_convert_fusion.2, pred[394]{0:T(512)(128)(4,1)S(1)} %iota_compare_fusion, pred[]{:T(512)S(6)} %eq.7), kind=kLoop, calls=%fused_computation | loop fusion | flops 3933696 | bytes 2430347 | tf_op jit(solution)/shard_map/convert_element_type | solution.py:759
  177.4 2.1 %collective-permute-done.41.refs_2_ = bf16[208,768]{1,0:T(8,128)(2,1)} collective-permute-done((bf16[208,768]{1,0:T(8,128)(2,1)S(1)}, bf16[208,768]{1,0:T(8,128)(2,1)}, u32[]{:S(2)}, u32[]{:S(2)}) %collective-permute-start.41) | collective-permute-done | bytes 319520 | tf_op jit(solution)/shard_map/ppermute | solution.py:474
  179.5 6.1 %collective-permute-done.42.refs_3_ = bf16[208,768]{1,0:T(8,128)(2,1)} collective-permute-done((bf16[208,768]{1,0:T(8,128)(2,1)S(1)}, bf16[208,768]{1,0:T(8,128)(2,1)}, u32[]{:S(2)}, u32[]{:S(2)}) %collective-permute-start.42) | collective-permute-done | bytes 319520 | tf_op jit(solution)/shard_map/ppermute | solution.py:474
  185.6 2.7 %shard_map.227 = (f32[576,768]{1,0:T(8,128)}, f32[192,768]{1,0:T(8,128)}, f32[768]{0:T(1024)}, f32[768]{0:T(1024)}, f32[768]{0:T(1024)}, /*index=5*/f32[768]{0:T(1024)}, f32[4,768]{1,0:T(4,128)}) custom-call(s32[8]{0:T(128)S(1)} %stack.38.ids, bf16[208,768]{1,0:T(8,128)(2,1)S(1)} %shard_map.226.refs_0_, ...), custom_call_target="tpu_custom_call" | custom-call | flops 60000000 | bytes 1024 | tf_op jit(solution)/shard_map/pallas_call | solution.py:447
  (129 shorter events, 14.3 us)
Async XLA Ops:
  0.6 29.9 %copy-start.33 = (f32[768]{0:T(1024)S(1)}, f32[768]{0:T(1024)}, u32[]{:S(2)}) copy-start(f32[768]{0:T(1024)} %gain.4) | copy-start | bytes 9220
  0.7 12.2 %collective-permute-start.1 = (bf16[768,768]{1,0:T(8,128)(2,1)}, bf16[768,768]{1,0:T(8,128)(2,1)S(1)}, u32[]{:S(2)}, u32[]{:S(2)}) collective-permute-start(bf16[768,768]{1,0:T(8,128)(2,1)} %bitcast.30), channel_id=1, source_target_pairs={{0,8},{8,0},{16,24},{24,16},{1,9},{9,1},{17,25},{25,17},{2,10},{10... | collective-permute-start | bytes 3538952 | tf_op jit(solution)/shard_map/ppermute | solution.py:464
  1.2 11.6 %collective-permute-start.2 = (bf16[768,768]{1,0:T(8,128)(2,1)}, bf16[768,768]{1,0:T(8,128)(2,1)S(1)}, u32[]{:S(2)}, u32[]{:S(2)}) collective-permute-start(bf16[768,768]{1,0:T(8,128)(2,1)} %bitcast.33), channel_id=1, source_target_pairs={{0,8},{8,0},{16,24},{24,16},{1,9},{9,1},{17,25},{25,17},{2,10},{10... | collective-permute-start | bytes 3538952 | tf_op jit(solution)/shard_map/ppermute | solution.py:464
  1.3 10.8 %collective-permute-start = (bf16[192,768]{1,0:T(8,128)(2,1)}, bf16[192,768]{1,0:T(8,128)(2,1)S(1)}, u32[]{:S(2)}, u32[]{:S(2)}) collective-permute-start(bf16[192,768]{1,0:T(8,128)(2,1)} %w_out.1), channel_id=1, source_target_pairs={{0,8},{8,0},{16,24},{24,16},{1,9},{9,1},{17,25},{25,17},{2,10},{10... | collective-permute-start | bytes 884744 | tf_op jit(solution)/shard_map/ppermute | solution.py:464
  5.3 8.5 %copy-start.14 = (bf16[192,768]{1,0:T(8,128)(2,1)S(1)}, bf16[192,768]{1,0:T(8,128)(2,1)}, u32[]{:S(2)}) copy-start(bf16[192,768]{1,0:T(8,128)(2,1)} %w_out.1) | copy-start | bytes 884740
  5.3 20.2 %copy-start.34 = (bf16[768,4]{0,1:T(4,128)(2,1)S(1)}, bf16[768,4]{0,1:T(4,128)(2,1)}, u32[]{:S(2)}) copy-start(bf16[768,4]{0,1:T(4,128)(2,1)} %param.22) | copy-start | bytes 18436
  5.3 20.2 %copy-start.36 = (s32[394,2]{0,1:T(2,128)S(1)}, s32[394,2]{0,1:T(2,128)}, u32[]{:S(2)}) copy-start(s32[394,2]{0,1:T(2,128)} %param.14) | copy-start | bytes 9460
  5.3 25.3 %copy-start.1 = (bf16[394,768]{1,0:T(8,128)(2,1)S(1)}, bf16[394,768]{1,0:T(8,128)(2,1)}, u32[]{:S(2)}) copy-start(bf16[394,768]{1,0:T(8,128)(2,1)} %tokens.3) | copy-start | bytes 1815556
  5.3 25.3 %copy-start.37 = (f32[768]{0:T(1024)S(1)}, f32[768]{0:T(1024)}, u32[]{:S(2)}) copy-start(f32[768]{0:T(1024)} %bias.1) | copy-start | bytes 9220
  13.8 10.4 %collective-permute-start.6 = (bf16[192,768]{1,0:T(8,128)(2,1)S(1)}, bf16[192,768]{1,0:T(8,128)(2,1)S(1)}, u32[]{:S(2)}, u32[]{:S(2)}) collective-permute-start(bf16[192,768]{1,0:T(8,128)(2,1)S(1)} %copy-done.14), channel_id=1, source_target_pairs={{0,16},{8,24},{16,0},{24,8},{1,17},{9,25},{17,1},{25,9},{2,18},{10... | collective-permute-start | bytes 884744 | tf_op jit(solution)/shard_map/ppermute | solution.py:464
  16.4 12.0 %collective-permute-start.4 = (bf16[394,192]{1,0:T(8,128)(2,1)S(1)}, bf16[394,192]{1,0:T(8,128)(2,1)S(1)}, u32[]{:S(2)}, u32[]{:S(2)}) collective-permute-start(bf16[394,192]{1,0:T(8,128)(2,1)S(1)} %get-tuple-element.115.rest_0_.head_out), channel_id=1, source_target_pairs={{0,16},{8,24},{16,0},{24,8},{1,17},{9,25},{17,1},{25,9},{2,18},{10... | collective-permute-start | bytes 453896 | tf_op jit(solution)/shard_map/ppermute | solution.py:464
  24.3 5.6 %copy-start.19 = (bf16[192,768]{1,0:T(8,128)(2,1)}, bf16[192,768]{1,0:T(8,128)(2,1)S(1)}, u32[]{:S(2)}) copy-start(bf16[192,768]{1,0:T(8,128)(2,1)S(1)} %collective-permute-done.6.rest_6_) | copy-start | bytes 884740
  24.3 5.6 %collective-permute-start.7 = (bf16[192,768]{1,0:T(8,128)(2,1)S(1)}, bf16[192,768]{1,0:T(8,128)(2,1)S(1)}, u32[]{:S(2)}, u32[]{:S(2)}) collective-permute-start(bf16[192,768]{1,0:T(8,128)(2,1)S(1)} %collective-permute-done.6.rest_6_), channel_id=1, source_target_pairs={{0,8},{8,0},{16,24},{24,16},{1,9},{9,1},{17,25},{25,17},{2,10},{10... | collective-permute-start | bytes 884744 | tf_op jit(solution)/shard_map/ppermute | solution.py:464
  25.0 4.1 %collective-permute-start.3 = (bf16[394,192]{1,0:T(8,128)(2,1)S(1)}, bf16[394,192]{1,0:T(8,128)(2,1)S(1)}, u32[]{:S(2)}, u32[]{:S(2)}) collective-permute-start(bf16[394,192]{1,0:T(8,128)(2,1)S(1)} %get-tuple-element.115.rest_0_.head_out), channel_id=1, source_target_pairs={{0,8},{8,0},{16,24},{24,16},{1,9},{9,1},{17,25},{25,17},{2,10},{10... | collective-permute-start | bytes 453896 | tf_op jit(solution)/shard_map/ppermute | solution.py:464
  28.4 30.0 %copy-start.2 = (bf16[1,768,768]{2,1,0:T(8,128)(2,1)S(1)}, bf16[1,768,768]{2,1,0:T(8,128)(2,1)}, u32[]{:S(2)}) copy-start(bf16[1,768,768]{2,1,0:T(8,128)(2,1)} %param.23) | copy-start | bytes 3538948
  28.4 30.0 %copy-start.3 = (bf16[1,768,768]{2,1,0:T(8,128)(2,1)S(1)}, bf16[1,768,768]{2,1,0:T(8,128)(2,1)}, u32[]{:S(2)}) copy-start(bf16[1,768,768]{2,1,0:T(8,128)(2,1)} %param.24) | copy-start | bytes 3538948
  28.4 30.0 %copy-start.5 = (bf16[768,768]{1,0:T(8,128)(2,1)S(1)}, bf16[768,768]{1,0:T(8,128)(2,1)}, u32[]{:S(2)}) copy-start(bf16[768,768]{1,0:T(8,128)(2,1)} %copy-done.4) | copy-start | bytes 3538948
  28.4 1.5 collective-permute-start.5
  37.1 15.4 %collective-permute-start.8 = (bf16[144,768]{1,0:T(8,128)(2,1)S(1)}, bf16[144,768]{1,0:T(8,128)(2,1)S(1)}, u32[]{:S(2)}, u32[]{:S(2)}) collective-permute-start(bf16[144,768]{1,0:T(8,128)(2,1)S(1)} %get-tuple-element.127), channel_id=1, source_target_pairs={{0,2},{2,0},{4,6},{6,4},{1,3},{3,1},{5,7},{7,5},{8,10},{10,8},{12,... | collective-permute-start | bytes 663560 | tf_op jit(solution)/shard_map/ppermute | solution.py:467
  39.1 8.2 %collective-permute-start.9 = (bf16[72,768]{1,0:T(8,128)(2,1)S(1)}, bf16[72,768]{1,0:T(8,128)(2,1)S(1)}, u32[]{:S(2)}, u32[]{:S(2)}) collective-permute-start(bf16[72,768]{1,0:T(8,128)(2,1)S(1)} %get-tuple-element.128), channel_id=1, source_target_pairs={{0,4},{2,6},{4,0},{6,2},{1,5},{3,7},{5,1},{7,3},{8,12},{10,14},{12... | collective-permute-start | bytes 331784 | tf_op jit(solution)/shard_map/ppermute | solution.py:467
  41.6 10.9 %collective-permute-start.10 = (bf16[72,768]{1,0:T(8,128)(2,1)S(1)}, bf16[72,768]{1,0:T(8,128)(2,1)S(1)}, u32[]{:S(2)}, u32[]{:S(2)}) collective-permute-start(bf16[72,768]{1,0:T(8,128)(2,1)S(1)} %get-tuple-element.129), channel_id=1, source_target_pairs={{0,6},{2,4},{4,2},{6,0},{1,7},{3,5},{5,3},{7,1},{8,14},{10,12},{12... | collective-permute-start | bytes 331784 | tf_op jit(solution)/shard_map/ppermute | solution.py:467
  41.6 16.8 %collective-permute-start.11 = (bf16[144,768]{1,0:T(8,128)(2,1)S(1)}, bf16[144,768]{1,0:T(8,128)(2,1)S(1)}, u32[]{:S(2)}, u32[]{:S(2)}) collective-permute-start(bf16[144,768]{1,0:T(8,128)(2,1)S(1)} %get-tuple-element.132), channel_id=1, source_target_pairs={{0,2},{2,0},{4,6},{6,4},{1,3},{3,1},{5,7},{7,5},{8,10},{10,8},{12,... | collective-permute-start | bytes 663560 | tf_op jit(solution)/shard_map/ppermute | solution.py:467
  42.5 24.7 %collective-permute-start.14 = (bf16[144,768]{1,0:T(8,128)(2,1)S(1)}, bf16[144,768]{1,0:T(8,128)(2,1)S(1)}, u32[]{:S(2)}, u32[]{:S(2)}) collective-permute-start(bf16[144,768]{1,0:T(8,128)(2,1)S(1)} %get-tuple-element.139), channel_id=1, source_target_pairs={{0,4},{2,6},{4,0},{6,2},{1,5},{3,7},{5,1},{7,3},{8,12},{10,14},{12... | collective-permute-start | bytes 663560 | tf_op jit(solution)/shard_map/ppermute | solution.py:467
  47.3 20.0 %collective-permute-start.15 = (bf16[144,768]{1,0:T(8,128)(2,1)S(1)}, bf16[144,768]{1,0:T(8,128)(2,1)S(1)}, u32[]{:S(2)}, u32[]{:S(2)}) collective-permute-start(bf16[144,768]{1,0:T(8,128)(2,1)S(1)} %get-tuple-element.140), channel_id=1, source_target_pairs={{0,6},{2,4},{4,2},{6,0},{1,7},{3,5},{5,3},{7,1},{8,14},{10,12},{12... | collective-permute-start | bytes 663560 | tf_op jit(solution)/shard_map/ppermute | solution.py:467
  52.6 14.6 %collective-permute-start.13 = (bf16[2,72,768]{2,1,0:T(8,128)(2,1)S(1)}, bf16[2,72,768]{2,1,0:T(8,128)(2,1)S(1)}, u32[]{:S(2)}, u32[]{:S(2)}) collective-permute-start(bf16[2,72,768]{2,1,0:T(8,128)(2,1)S(1)} %pad_maximum_fusion.2), channel_id=1, source_target_pairs={{0,16},{8,24},{16,0},{24,8},{1,17},{9,25},{17,1},{25,9},{2,18},{10... | collective-permute-start | bytes 663560 | tf_op jit(solution)/shard_map/ppermute | solution.py:464
  74.8 16.1 %collective-permute-start.19 = (bf16[1536,768]{1,0:T(8,128)(2,1)S(1)}, bf16[1536,768]{1,0:T(8,128)(2,1)S(1)}, u32[]{:S(2)}, u32[]{:S(2)}) collective-permute-start(bf16[1536,768]{1,0:T(8,128)(2,1)S(1)} %get-tuple-element.155), channel_id=1, source_target_pairs={{0,8},{8,0},{16,24},{24,16},{1,9},{9,1},{17,25},{25,17},{2,10},{10... | collective-permute-start | bytes 7077896 | tf_op jit(solution)/shard_map/ppermute | solution.py:464
  74.9 10.1 %collective-permute-start.16 = (bf16[144,768]{1,0:T(8,128)(2,1)S(1)}, bf16[144,768]{1,0:T(8,128)(2,1)S(1)}, u32[]{:S(2)}, u32[]{:S(2)}) collective-permute-start(bf16[144,768]{1,0:T(8,128)(2,1)S(1)} %get-tuple-element.142), channel_id=1, source_target_pairs={{0,6},{2,4},{4,2},{6,0},{1,7},{3,5},{5,3},{7,1},{8,14},{10,12},{12... | collective-permute-start | bytes 663560 | tf_op jit(solution)/shard_map/ppermute | solution.py:467
  77.4 13.4 %collective-permute-start.18 = (bf16[2,72,768]{2,1,0:T(8,128)(2,1)S(1)}, bf16[2,72,768]{2,1,0:T(8,128)(2,1)S(1)}, u32[]{:S(2)}, u32[]{:S(2)}) collective-permute-start(bf16[2,72,768]{2,1,0:T(8,128)(2,1)S(1)} %get-tuple-element.145), channel_id=1, source_target_pairs={{0,16},{8,24},{16,0},{24,8},{1,17},{9,25},{17,1},{25,9},{2,18},{10... | collective-permute-start | bytes 663560 | tf_op jit(solution)/shard_map/ppermute | solution.py:464
  78.9 14.5 %collective-permute-start.12 = (bf16[144,768]{1,0:T(8,128)(2,1)S(1)}, bf16[144,768]{1,0:T(8,128)(2,1)S(1)}, u32[]{:S(2)}, u32[]{:S(2)}) collective-permute-start(bf16[144,768]{1,0:T(8,128)(2,1)S(1)} %get-tuple-element.134), channel_id=1, source_target_pairs={{0,2},{2,0},{4,6},{6,4},{1,3},{3,1},{5,7},{7,5},{8,10},{10,8},{12,... | collective-permute-start | bytes 663560 | tf_op jit(solution)/shard_map/ppermute | solution.py:467
  85.0 16.2 %collective-permute-start.17 = (bf16[144,768]{1,0:T(8,128)(2,1)S(1)}, bf16[144,768]{1,0:T(8,128)(2,1)S(1)}, u32[]{:S(2)}, u32[]{:S(2)}) collective-permute-start(bf16[144,768]{1,0:T(8,128)(2,1)S(1)} %get-tuple-element.143), channel_id=1, source_target_pairs={{0,4},{2,6},{4,0},{6,2},{1,5},{3,7},{5,1},{7,3},{8,12},{10,14},{12... | collective-permute-start | bytes 663560 | tf_op jit(solution)/shard_map/ppermute | solution.py:467
  93.4 11.1 %copy-start.10 = (f32[768,768]{1,0:T(8,128)}, f32[768,768]{1,0:T(8,128)S(1)}, u32[]{:S(2)}) copy-start(f32[768,768]{1,0:T(8,128)S(1)} %get-tuple-element.211.kept) | copy-start | bytes 7077892
  101.2 20.8 %copy-start.16 = (bf16[394,768]{1,0:T(8,128)(2,1)S(1)}, bf16[394,768]{1,0:T(8,128)(2,1)}, u32[]{:S(2)}) copy-start(bf16[394,768]{1,0:T(8,128)(2,1)} %copy-done.15) | copy-start | bytes 1815556
  101.2 20.8 %copy-start.24 = (bf16[394,192]{1,0:T(8,128)(2,1)S(1)}, bf16[394,192]{1,0:T(8,128)(2,1)}, u32[]{:S(2)}) copy-start(bf16[394,192]{1,0:T(8,128)(2,1)} %copy-done.23) | copy-start | bytes 453892
  101.2 20.8 %copy-start.26 = (bf16[394,192]{1,0:T(8,128)(2,1)S(1)}, bf16[394,192]{1,0:T(8,128)(2,1)}, u32[]{:S(2)}) copy-start(bf16[394,192]{1,0:T(8,128)(2,1)} %copy-done.25) | copy-start | bytes 453892
  101.2 20.8 %copy-start.28 = (bf16[394,192]{1,0:T(8,128)(2,1)S(1)}, bf16[394,192]{1,0:T(8,128)(2,1)}, u32[]{:S(2)}) copy-start(bf16[394,192]{1,0:T(8,128)(2,1)} %copy-done.27) | copy-start | bytes 453892
  102.7 1.7 collective-permute-start.20
  104.4 17.6 %copy-start.7 = (bf16[768,3,192]{0,2,1:T(8,128)(2,1)S(1)}, bf16[768,3,192]{0,2,1:T(8,128)(2,1)}, u32[]{:S(2)}) copy-start(bf16[768,3,192]{0,2,1:T(8,128)(2,1)} %param.18) | copy-start | bytes 2654212
  104.4 17.6 %copy-start.9 = (bf16[394,768]{1,0:T(8,128)(2,1)S(1)}, bf16[394,768]{1,0:T(8,128)(2,1)}, u32[]{:S(2)}) copy-start(bf16[394,768]{1,0:T(8,128)(2,1)} %cot.3) | copy-start | bytes 1815556
  104.4 17.6 %copy-start.13 = (bf16[3,394,394]{2,1,0:T(8,128)(2,1)S(1)}, bf16[3,394,394]{2,1,0:T(8,128)(2,1)}, u32[]{:S(2)}) copy-start(bf16[3,394,394]{2,1,0:T(8,128)(2,1)} %copy-done.12) | copy-start | bytes 2794252
  104.5 9.6 %collective-permute-start.21 = (bf16[416,384]{1,0:T(8,128)(2,1)S(1)}, bf16[416,384]{1,0:T(8,128)(2,1)S(1)}, u32[]{:S(2)}, u32[]{:S(2)}) collective-permute-start(bf16[416,384]{1,0:T(8,128)(2,1)S(1)} %add_convert_fusion.1), channel_id=1, source_target_pairs={{0,16},{8,24},{16,0},{24,8},{1,17},{9,25},{17,1},{25,9},{2,18},{10... | collective-permute-start | bytes 958472 | tf_op jit(solution)/shard_map/ppermute | solution.py:464
  106.1 14.3 %collective-permute-start.22 = (bf16[256,768]{1,0:T(8,128)(2,1)S(1)}, bf16[256,768]{1,0:T(8,128)(2,1)S(1)}, u32[]{:S(2)}, u32[]{:S(2)}) collective-permute-start(bf16[256,768]{1,0:T(8,128)(2,1)S(1)} %get-tuple-element.164), channel_id=1, source_target_pairs={{0,1},{1,0},{2,3},{3,2},{4,5},{5,4},{6,7},{7,6},{8,9},{9,8},{10,11... | collective-permute-start | bytes 1179656 | tf_op jit(solution)/shard_map/ppermute | solution.py:470
  107.6 10.4 %collective-permute-start.24 = (bf16[144,768]{1,0:T(8,128)(2,1)S(1)}, bf16[144,768]{1,0:T(8,128)(2,1)S(1)}, u32[]{:S(2)}, u32[]{:S(2)}) collective-permute-start(bf16[144,768]{1,0:T(8,128)(2,1)S(1)} %get-tuple-element.218), channel_id=1, source_target_pairs={{0,2},{2,0},{4,6},{6,4},{1,3},{3,1},{5,7},{7,5},{8,10},{10,8},{12,... | collective-permute-start | bytes 663560 | tf_op jit(solution)/shard_map/ppermute | solution.py:467
  107.7 12.7 %collective-permute-start.23 = (bf16[2,72,768]{2,1,0:T(8,128)(2,1)S(1)}, bf16[2,72,768]{2,1,0:T(8,128)(2,1)S(1)}, u32[]{:S(2)}, u32[]{:S(2)}) collective-permute-start(bf16[2,72,768]{2,1,0:T(8,128)(2,1)S(1)} %shard_map.217), channel_id=1, source_target_pairs={{0,4},{2,6},{4,0},{6,2},{1,5},{3,7},{5,1},{7,3},{8,12},{10,14},{12... | collective-permute-start | bytes 663560 | tf_op jit(solution)/shard_map/ppermute | solution.py:467
  120.4 1.6 collective-permute-start.25
  127.0 1.7 collective-permute-start.29
  127.2 13.4 %collective-permute-start.26 = (bf16[2,192,384]{2,1,0:T(8,128)(2,1)S(1)}, bf16[2,192,384]{2,1,0:T(8,128)(2,1)S(1)}, u32[]{:S(2)}, u32[]{:S(2)}) collective-permute-start(bf16[2,192,384]{2,1,0:T(8,128)(2,1)S(1)} %get-tuple-element.176), channel_id=1, source_target_pairs={{0,1},{1,0},{2,3},{3,2},{4,5},{5,4},{6,7},{7,6},{8,9},{9,8},{10,11... | collective-permute-start | bytes 884744 | tf_op jit(solution)/shard_map/ppermute | solution.py:470
  127.7 12.9 %collective-permute-start.27 = (bf16[2,192,384]{2,1,0:T(8,128)(2,1)S(1)}, bf16[2,192,384]{2,1,0:T(8,128)(2,1)S(1)}, u32[]{:S(2)}, u32[]{:S(2)}) collective-permute-start(bf16[2,192,384]{2,1,0:T(8,128)(2,1)S(1)} %get-tuple-element.177), channel_id=1, source_target_pairs={{0,2},{2,0},{4,6},{6,4},{1,3},{3,1},{5,7},{7,5},{8,10},{10,8},{12,... | collective-permute-start | bytes 884744 | tf_op jit(solution)/shard_map/ppermute | solution.py:467
  128.8 12.0 %collective-permute-start.30 = (bf16[394,384]{1,0:T(8,128)(2,1)S(1)}, bf16[394,384]{1,0:T(8,128)(2,1)S(1)}, u32[]{:S(2)}, u32[]{:S(2)}) collective-permute-start(bf16[394,384]{1,0:T(8,128)(2,1)S(1)} %add_convert_fusion.5), channel_id=1, source_target_pairs={{0,16},{8,24},{16,0},{24,8},{1,17},{9,25},{17,1},{25,9},{2,18},{10... | collective-permute-start | bytes 907784 | tf_op jit(solution)/shard_map/ppermute | solution.py:464
  129.4 9.7 %collective-permute-start.28 = (bf16[72,768]{1,0:T(8,128)(2,1)S(1)}, bf16[72,768]{1,0:T(8,128)(2,1)S(1)}, u32[]{:S(2)}, u32[]{:S(2)}) collective-permute-start(bf16[72,768]{1,0:T(8,128)(2,1)S(1)} %get-tuple-element.219), channel_id=1, source_target_pairs={{0,2},{2,0},{4,6},{6,4},{1,3},{3,1},{5,7},{7,5},{8,10},{10,8},{12,... | collective-permute-start | bytes 331784 | tf_op jit(solution)/shard_map/ppermute | solution.py:467
  140.8 9.8 %copy-start.32 = (f32[768]{0:T(1024)S(1)}, f32[768]{0:T(1024)}, u32[]{:S(2)}) copy-start(f32[768]{0:T(1024)} %gain.5) | copy-start | bytes 9220
  140.9 2.0 %collective-permute-start.31 = (bf16[400,384]{1,0:T(8,128)(2,1)S(1)}, bf16[400,384]{1,0:T(8,128)(2,1)S(1)}, u32[]{:S(2)}, u32[]{:S(2)}) collective-permute-start(bf16[400,384]{1,0:T(8,128)(2,1)S(1)} %get-tuple-element.191), channel_id=1, source_target_pairs={{0,8},{8,0},{16,24},{24,16},{1,9},{9,1},{17,25},{25,17},{2,10},{10... | collective-permute-start | bytes 921608 | tf_op jit(solution)/shard_map/ppermute | solution.py:464
  140.9 6.3 %collective-permute-start.33 = (bf16[192,384]{1,0:T(8,128)(2,1)S(1)}, bf16[192,384]{1,0:T(8,128)(2,1)S(1)}, u32[]{:S(2)}, u32[]{:S(2)}) collective-permute-start(bf16[192,384]{1,0:T(8,128)(2,1)S(1)} %get-tuple-element.193), channel_id=1, source_target_pairs={{0,2},{2,0},{4,6},{6,4},{1,3},{3,1},{5,7},{7,5},{8,10},{10,8},{12,... | collective-permute-start | bytes 442376 | tf_op jit(solution)/shard_map/ppermute | solution.py:467
  141.3 5.9 %collective-permute-start.34 = (bf16[192,384]{1,0:T(8,128)(2,1)S(1)}, bf16[192,384]{1,0:T(8,128)(2,1)S(1)}, u32[]{:S(2)}, u32[]{:S(2)}) collective-permute-start(bf16[192,384]{1,0:T(8,128)(2,1)S(1)} %get-tuple-element.194), channel_id=1, source_target_pairs={{0,1},{1,0},{2,3},{3,2},{4,5},{5,4},{6,7},{7,6},{8,9},{9,8},{10,11... | collective-permute-start | bytes 442376 | tf_op jit(solution)/shard_map/ppermute | solution.py:470
  142.8 7.7 %collective-permute-start.36 = (bf16[394,384]{1,0:T(8,128)(2,1)S(1)}, bf16[394,384]{1,0:T(8,128)(2,1)S(1)}, u32[]{:S(2)}, u32[]{:S(2)}) collective-permute-start(bf16[394,384]{1,0:T(8,128)(2,1)S(1)} %add_convert_fusion.4.own), channel_id=1, source_target_pairs={{0,8},{8,0},{16,24},{24,16},{1,9},{9,1},{17,25},{25,17},{2,10},{10... | collective-permute-start | bytes 907784 | tf_op jit(solution)/shard_map/ppermute | solution.py:464
  142.9 23.8 %collective-permute-start.32 = (bf16[400,384]{1,0:T(8,128)(2,1)S(1)}, bf16[400,384]{1,0:T(8,128)(2,1)S(1)}, u32[]{:S(2)}, u32[]{:S(2)}) collective-permute-start(bf16[400,384]{1,0:T(8,128)(2,1)S(1)} %add_convert_fusion.3), channel_id=1, source_target_pairs={{0,16},{8,24},{16,0},{24,8},{1,17},{9,25},{17,1},{25,9},{2,18},{10... | collective-permute-start | bytes 921608 | tf_op jit(solution)/shard_map/ppermute | solution.py:464
  147.3 9.5 %collective-permute-start.35 = (bf16[96,768]{1,0:T(8,128)(2,1)S(1)}, bf16[96,768]{1,0:T(8,128)(2,1)S(1)}, u32[]{:S(2)}, u32[]{:S(2)}) collective-permute-start(bf16[96,768]{1,0:T(8,128)(2,1)S(1)} %get-tuple-element.195.own_a), channel_id=1, source_target_pairs={{0,4},{2,6},{4,0},{6,2},{1,5},{3,7},{5,1},{7,3},{8,12},{10,14},{12... | collective-permute-start | bytes 442376 | tf_op jit(solution)/shard_map/ppermute | solution.py:467
  149.0 22.0 %collective-permute-start.43 = (bf16[512,768]{1,0:T(8,128)(2,1)}, bf16[512,768]{1,0:T(8,128)(2,1)S(1)}, u32[]{:S(2)}, u32[]{:S(2)}) collective-permute-start(bf16[512,768]{1,0:T(8,128)(2,1)} %get-tuple-element.214), channel_id=1, source_target_pairs={{0,1},{1,0},{2,3},{3,2},{4,5},{5,4},{6,7},{7,6},{8,9},{9,8},{10,11... | collective-permute-start | bytes 2359304 | tf_op jit(solution)/shard_map/ppermute | solution.py:470
  156.8 9.8 %collective-permute-start.37 = (bf16[96,768]{1,0:T(8,128)(2,1)S(1)}, bf16[96,768]{1,0:T(8,128)(2,1)S(1)}, u32[]{:S(2)}, u32[]{:S(2)}) collective-permute-start(bf16[96,768]{1,0:T(8,128)(2,1)S(1)} %get-tuple-element.200.own_b), channel_id=1, source_target_pairs={{0,4},{2,6},{4,0},{6,2},{1,5},{3,7},{5,1},{7,3},{8,12},{10,14},{12... | collective-permute-start | bytes 442376 | tf_op jit(solution)/shard_map/ppermute | solution.py:467
  156.8 9.8 %collective-permute-start.38 = (f32[16,768]{1,0:T(8,128)S(1)}, f32[16,768]{1,0:T(8,128)S(1)}, u32[]{:S(2)}, u32[]{:S(2)}) collective-permute-start(f32[16,768]{1,0:T(8,128)S(1)} %get-tuple-element.199.small), channel_id=1, source_target_pairs={{0,4},{2,6},{4,0},{6,2},{1,5},{3,7},{5,1},{7,3},{8,12},{10,14},{12... | collective-permute-start | bytes 147464 | tf_op jit(solution)/shard_map/ppermute | solution.py:467
  167.5 6.8 %collective-permute-start.39 = (bf16[400,384]{1,0:T(8,128)(2,1)}, bf16[400,384]{1,0:T(8,128)(2,1)}, u32[]{:S(2)}, u32[]{:S(2)}) collective-permute-start(bf16[400,384]{1,0:T(8,128)(2,1)} %add_convert_fusion.2), channel_id=1, source_target_pairs={{0,8},{8,0},{16,24},{24,16},{1,9},{9,1},{17,25},{25,17},{2,10},{10... | collective-permute-start | bytes 921608 | tf_op jit(solution)/shard_map/ppermute | solution.py:464
  167.5 9.9 %collective-permute-start.40 = (bf16[208,768]{1,0:T(8,128)(2,1)S(1)}, bf16[208,768]{1,0:T(8,128)(2,1)S(1)}, u32[]{:S(2)}, u32[]{:S(2)}) collective-permute-start(bf16[208,768]{1,0:T(8,128)(2,1)S(1)} %shard_map.226.refs_0_), channel_id=1, source_target_pairs={{0,1},{1,0},{2,3},{3,2},{4,5},{5,4},{6,7},{7,6},{8,9},{9,8},{10,11... | collective-permute-start | bytes 958472 | tf_op jit(solution)/shard_map/ppermute | solution.py:474
  169.0 10.5 %collective-permute-start.41 = (bf16[208,768]{1,0:T(8,128)(2,1)S(1)}, bf16[208,768]{1,0:T(8,128)(2,1)}, u32[]{:S(2)}, u32[]{:S(2)}) collective-permute-start(bf16[208,768]{1,0:T(8,128)(2,1)S(1)} %shard_map.226.refs_0_), channel_id=1, source_target_pairs={{0,2},{1,3},{2,0},{3,1},{4,6},{5,7},{6,4},{7,5},{8,10},{9,11},{10,... | collective-permute-start | bytes 958472 | tf_op jit(solution)/shard_map/ppermute | solution.py:474
  169.0 16.5 %collective-permute-start.42 = (bf16[208,768]{1,0:T(8,128)(2,1)S(1)}, bf16[208,768]{1,0:T(8,128)(2,1)}, u32[]{:S(2)}, u32[]{:S(2)}) collective-permute-start(bf16[208,768]{1,0:T(8,128)(2,1)S(1)} %shard_map.226.refs_0_), channel_id=1, source_target_pairs={{0,3},{1,2},{2,1},{3,0},{4,7},{5,6},{6,5},{7,4},{8,11},{9,10},{10,... | collective-permute-start | bytes 958472 | tf_op jit(solution)/shard_map/ppermute | solution.py:474
  171.0 1.7 copy-start.11
  (18 other events, 15.5 us)

commit v4 on v2

--- a/solution.py
+++ b/solution.py
@@ -165,7 +165,7 @@
             here = pl.multiple_of(k * size + far * quarter, 8)
             there = pl.multiple_of(k * size + (1 - far) * quarter, 8)
             d_out[pl.ds(here, quarter), :] = out_blocks[k][...].astype(F32)
-            d_out[pl.ds(there, quarter), :] = pair_out[places[k] - 1].astype(F32)
+            d_out[pl.ds(there, quarter), :] = pair_out[places[k] - 2].astype(F32)
     lane = iota((count, LANES), 1)
     logits = dot_nt(rows_in[...], router[...])
     logits = jnp.where(lane < experts, logits, -1e30)
@@ -232,10 +232,9 @@
         out[at : at + width, :] = total.astype(BF16)
 
 
-def gated_sum_kernel(kept_a, came_a, kept_b, came_b, *blocks):
-    for k in range(4):
-        kept, came = (kept_a, came_a) if k < 2 else (kept_b, came_b)
-        blocks[k][...] = (kept[k % 2].astype(F32) + came[k % 2].astype(F32)).astype(BF16)
+def gated_sum_kernel(kept, came, *blocks):
+    for k, out in enumerate(blocks):
+        out[...] = (kept[k].astype(F32) + came[k].astype(F32)).astype(BF16)
 
 
 def weight_grad_kernel(*refs):
@@ -274,13 +273,14 @@
     grad_down[half:, :] = kept[half:, half:] + came[half:, half:].astype(F32)
 
 
-def combine_kernel(experts, parts, base, ids, table, *refs):
+def combine_kernel(experts, parts, base, ids, table, part, *refs):
     blocks = refs[:experts]
     routers = refs[experts : experts + parts]
     kept, sent, total = refs[experts + parts :]
     value = dot_tn(table[ids[E_ID]], blocks[0][...])
     for k in range(1, experts):
-        value = value + dot_tn(table[ids[E_ID] ^ k], blocks[k][...])
+        spots = table if blocks[k].shape[0] == table.shape[1] else part
+        value = value + dot_tn(spots[ids[E_ID] ^ k], blocks[k][...])
     total[...] = jnp.zeros_like(total)
     total[: value.shape[0], :] = value
     if parts:
@@ -369,20 +369,16 @@
 
 
 def sum_kernel(count, *refs):
-    size = refs[0].shape[0] // 2
-    for half in range(2):
-        part = pl.ds(half * size, size)
-        total = refs[0][part, :].astype(F32)
-        for m in range(1, count):
-            total = total + refs[m][part, :].astype(F32)
-        refs[count + half][...] = total.astype(BF16)
-
-
-def pair_kernel(own_a, own_b, came_a, came_b, small, small_came, out):
-    size = own_a.shape[0]
-    out[:size, :] = (own_a[...].astype(F32) + came_a[...].astype(F32)).astype(BF16)
-    out[size : 2 * size, :] = (own_b[...].astype(F32) + came_b[...].astype(F32)).astype(BF16)
-    out[2 * size :, :] = (small[...] + small_came[...]).astype(BF16)
+    total = refs[0][...].astype(F32)
+    for m in range(1, count):
+        total = total + refs[m][...].astype(F32)
+    refs[count][...] = total.astype(BF16)
+
+
+def pair_kernel(own, came, small, small_came, out):
+    size = own.shape[0]
+    out[:size, :] = (own[...].astype(F32) + came[...].astype(F32)).astype(BF16)
+    out[size:, :] = (small[...] + small_came[...]).astype(BF16)
 
 
 def spread_kernel(count, ids, *refs):
@@ -511,7 +507,7 @@
         )
         head_x, head_c = tensor_swap(head_out, 2), tensor_swap(head_out, 1)
         quarter = cap // 2
-        cot_shapes = [(cap, width)] + [(quarter if small_slice else cap, width)] * (experts - 1)
+        cot_shapes = [(quarter if small_slice and k > 1 else cap, width) for k in range(experts)]
         table, part, router, *cot_blocks = run(
             functools.partial(plan_kernel, experts),
             [((experts, cap, rows), BF16), ((experts, quarter, rows), BF16)]
@@ -521,7 +517,10 @@
             micros=2,
         )
         head_x = after(head_x, table)
-        d_rows_in = exchange(cot_blocks)
+        if small_slice:
+            d_rows_in = cot_blocks[:2] + [expert_swap(cot_blocks[k], k) for k in (2, 3)]
+        else:
+            d_rows_in = exchange(cot_blocks)
         out_all = [w_out, out_c, out_x, tensor_swap(out_x, 1)]
         heads_all = [head_out, head_c, head_x, tensor_swap(head_x, 1)]
         middle, *row_blocks = run(
@@ -535,12 +534,14 @@
             ],
             micros=3,
         )
-        rows_in = exchange(row_blocks)
-        middle, *d_rows_in = lax.optimization_barrier((middle, *d_rows_in))
         if small_slice:
-            pair_out = tensor_swap(jnp.stack(d_rows_in[1:]), 2)
+            *row_blocks, far_2, far_3 = lax.optimization_barrier((*row_blocks, *d_rows_in[2:]))
+            d_rows_in[2:] = [far_2, far_3]
+            d_rows_in[1] = expert_swap(after(d_rows_in[1], middle), 1)
+            pair_out = tensor_swap(jnp.stack([far_2, far_3]), 2)
         else:
             pair_out = router
+        rows_in = exchange(list(row_blocks))
 
         calls = [(0, 1), (2, 3)] if small_slice else [tuple(range(experts))]
         worked = []
@@ -552,13 +553,14 @@
             results = run(
                 functools.partial(expert_kernel, experts, call, not last),
                 [((cap, width), BF16)] * len(call)
-                + [((len(call), quarter if small_slice else cap, width), BF16)] * 2
+                + [((len(call), quarter if worked else cap, width), BF16)] * 2
                 + [((count, width), BF16)] * 2
                 + [((count, hidden_width), BF16)] * 4
                 + [((part_rows, width), F32)]
                 + grads,
                 [ids, up_a, up_b, down_a, down_b]
-                + [after(router, worked[-1][6]) if worked else router, pair_out]
+                + [after(router, worked[-1][6]) if worked else router]
+                + [pair_out if worked or not small_slice else router]
                 + [rows_in[k] for k in call]
                 + [d_rows_in[k] for k in call],
                 scratch=[((count, width), F32)],
@@ -569,11 +571,11 @@
             gated.append(results[len(call) : len(call) + 2])
             worked.append(results[len(call) + 2 :])
 
-        def combine(blocks, spots, routers):
+        def combine(blocks, routers):
             return run(
                 functools.partial(combine_kernel, experts, len(routers), base),
                 [((tall if routers else base, half), BF16)] * 2,
-                [ids, spots] + blocks + routers,
+                [ids, table, part] + blocks + routers,
                 scratch=[((tall if routers else base, width), F32)],
                 micros=2,
             )
@@ -598,20 +600,18 @@
         )
 
         if small_slice:
-            (kept_a, sent_a), (kept_b, sent_b) = gated
-            gated_blocks = run(
+            far_blocks = run(
                 gated_sum_kernel,
-                [((quarter, width), BF16)] * 4,
-                [kept_a, tensor_swap(sent_a, 2), kept_b, tensor_swap(sent_b, 2)],
+                [((quarter, width), BF16)] * 2,
+                [gated[1][0], tensor_swap(gated[1][1], 2)],
             )
-            spots = part
+            gated_blocks = [gated[0][0][0], gated[0][0][1], *far_blocks]
         else:
             gated_blocks = [gated[0][0][k] for k in range(experts)]
-            spots = table
 
         *d_home, sent_first = lax.optimization_barrier((*d_home, *gated_blocks, sent_first))
         d_home, gated_blocks = d_home[:experts], d_home[experts:]
-        kept, sent = combine(list(d_home), table, [one[6] for one in worked])
+        kept, sent = combine(list(d_home), [one[6] for one in worked])
         chip = (kept.astype(F32) + tensor_swap(sent, 1).astype(F32)).astype(BF16)
         own = (chip.astype(F32) + tensor_swap(chip, 2).astype(F32)).astype(BF16)
         gated_home = exchange(list(gated_blocks))
@@ -635,38 +635,33 @@
         )
 
         *gated_home, _ = lax.optimization_barrier((*gated_home, d_middle))
-        kept_y, sent_y = combine(list(gated_home), spots, [])
-
+        kept_y, sent_y = combine(list(gated_home), [])
+
+        chip1 = (kept1.astype(F32) + tensor_swap(sent1, 1).astype(F32)).astype(BF16)
+        own1 = (chip1.astype(F32) + tensor_swap(chip1, 2).astype(F32)).astype(BF16)
         if small_slice:
             arrived = [grad_blocks[0]] + [quarter_swap(grad_blocks[m], m) for m in (3, 1, 2)]
             arrived[0], kept_y, sent_y = lax.optimization_barrier((arrived[0], kept_y, sent_y))
             size = grad_blocks[0].shape[0]
-            summed_a, summed_b = run(
-                functools.partial(sum_kernel, 4), [((size // 2, width), BF16)] * 2, arrived
+            (summed,) = run(
+                functools.partial(sum_kernel, 4), [((size, width), BF16)], arrived, micros=0.5
             )
-            sent_rest = after(sent_rest, summed_a)
-            came_a = expert_swap(summed_a, 2)
-            came_b = expert_swap(after(summed_b, came_a), 2)
-        chip_y = (kept_y.astype(F32) + tensor_swap(sent_y, 1).astype(F32)).astype(BF16)
-        own_y = (chip_y.astype(F32) + tensor_swap(chip_y, 2).astype(F32)).astype(BF16)
-
-        chip1 = (kept1.astype(F32) + tensor_swap(sent1, 1).astype(F32)).astype(BF16)
-        own1 = (chip1.astype(F32) + tensor_swap(chip1, 2).astype(F32)).astype(BF16)
-        if small_slice:
-            own1 = after(own1, summed_a)
+            sent_rest, own1 = lax.optimization_barrier((sent_rest, own1, summed))[:2]
         other1 = tensor_swap(own1, 1)
         grad_tokens, small = run(
             last_norm_kernel,
             [((rows, width), BF16), ((small_rows, width), F32)],
             [ids, own1, other1, tokens, d_middle, ln1_gain, small2],
             scratch=[((rows, width), F32)],
-            micros=2,
-        )
+            micros=0.01,
+        )
+        chip_y = (kept_y.astype(F32) + tensor_swap(sent_y, 1).astype(F32)).astype(BF16)
+        own_y = (chip_y.astype(F32) + tensor_swap(chip_y, 2).astype(F32)).astype(BF16)
         if small_slice:
             (ready,) = run(
                 pair_kernel,
                 [((size + small_rows, width), BF16)],
-                [summed_a, summed_b, came_a, came_b, small, expert_swap(small, 2)],
+                [summed, expert_swap(summed, 2), small, expert_swap(small, 2)],
                 micros=1,
             )
             own_y, ready = lax.optimization_barrier((own_y, ready))

time: 175 us -> 190 us (1.086)
  waiting for transfers between devices: 71.8 us -> 92.6 us
  starting transfers between devices: 51.5 us -> 48.1 us
    ppermute x6, waiting for transfers between devices: 21.8 us -> 36 us  [quarter_swap(): return lax.ppermute(value, ('expert', 'dp'), pairs)]
    ppermute x21 -> x20, waiting for transfers between devices: 12.6 us -> 16.2 us  [tensor_swap(): lax.ppermute(value, 'tensor', [(i, i ^ mask) for i in range(n_tensor)])]
    ppermute x15 -> x14, waiting for transfers between devices: 37.3 us -> 40.4 us  [expert_swap(): lax.ppermute(value, 'expert', [(i, i ^ mask) for i in range(n_expert)])]
    unnamed x52 -> x38, local copies, waits for them, and re-layouts: 6.86 us -> 5.06 us
    ppermute x15 -> x14, starting transfers between devices: 27.2 us -> 25.7 us  [expert_swap(): lax.ppermute(value, 'expert', [(i, i ^ mask) for i in range(n_expert)])]
    ppermute x21 -> x20, starting transfers between devices: 13.4 us -> 12.7 us  [tensor_swap(): lax.ppermute(value, 'tensor', [(i, i ^ mask) for i in range(n_tensor)])]
  transfers between devices with their start and end apart: 44 -> 42, of which waited for: 21 -> 20; matrix products, arithmetic and copies ran while one was open for 2% -> 2% of each run, Pallas kernels for 13% -> 12%
where the time goes in v4:
time: 190 us; the launch traced here: 189 us
  waiting for transfers between devices  92.6 us (49%)
  starting transfers between devices  48.1 us (25%)
  Pallas kernels  38 us (20%)
  local copies, waits for them, and re-layouts  5.18 us (3%)
  other arithmetic  3.73 us (2%)
    ppermute x14, waiting for transfers between devices, expert_swap(): lax.ppermute(value, 'expert', [(i, i ^ mask) for i in range(n_expert)])  40.4 us
    pallas_call x16, Pallas kernels, run(): pl.pallas_call(kernel, out_shape=[jax.ShapeDtypeStruct(shape, kind) for s...  38 us
    ppermute x6, waiting for transfers between devices, quarter_swap(): return lax.ppermute(value, ('expert', 'dp'), pairs)  36 us
    ppermute x14, starting transfers between devices, expert_swap(): lax.ppermute(value, 'expert', [(i, i ^ mask) for i in range(n_expert)])  25.7 us
    ppermute x20, waiting for transfers between devices, tensor_swap(): lax.ppermute(value, 'tensor', [(i, i ^ mask) for i in range(n_tensor)])  16.2 us
    ppermute x20, starting transfers between devices, tensor_swap(): lax.ppermute(value, 'tensor', [(i, i ^ mask) for i in range(n_tensor)])  12.7 us
    ppermute x6, starting transfers between devices, quarter_swap(): return lax.ppermute(value, ('expert', 'dp'), pairs)  6.99 us
    unnamed x38, local copies, waits for them, and re-layouts  5.06 us
  transfers between devices with their start and end apart: 42, of which 20 were waited for; matrix products, arithmetic and copies ran while one was open for 2% of the time, Pallas kernels for 12%

profile of v4, /device:TPU:0, one launch (start us, length us, event | category | flops | bytes accessed | tf_op | source)
XLA Modules:
  0.0 189.2 jit_solution(10519529456835790159)
XLA Ops:
  1.2 2.9 %collective-permute-start = (bf16[192,768]{1,0:T(8,128)(2,1)}, bf16[192,768]{1,0:T(8,128)(2,1)S(1)}, u32[]{:S(2)}, u32[]{:S(2)}) collective-permute-start(bf16[192,768]{1,0:T(8,128)(2,1)} %w_out.1), channel_id=1, source_target_pairs={{0,16},{8,24},{16,0},{24,8},{1,17},{9,25},{17,1},{25,9},{2,18},{10... | collective-permute-start | bytes 884744 | tf_op jit(solution)/shard_map/ppermute | solution.py:427
  4.9 1.1 copy-done
  6.0 0.7 copy-done.2
  6.7 1.2 copy-done.8
  7.8 0.7 copy-done.13
  8.5 2.5 %shard_map.212 = (bf16[394,768]{1,0:T(8,128)(2,1)S(1)}, bf16[394,192]{1,0:T(8,128)(2,1)S(1)}, bf16[394,192]{1,0:T(8,128)(2,1)S(1)}, bf16[394,192]{1,0:T(8,128)(2...) custom-call(bf16[394,768]{1,0:T(8,128)(2,1)S(1)} %copy-done, f32[768]{0:T(1024)S(1)} %copy-done.2, ...), custom_call_target="tpu_custom_call" | custom-call | flops 4600000000 | bytes 1024 | tf_op jit(solution)/shard_map/pallas_call | solution.py:410
  11.7 1.8 collective-permute-start.5
  13.7 1.4 shard_map.213
  15.1 4.1 %collective-permute-done.5.rest_2_ = bf16[394,192]{1,0:T(8,128)(2,1)S(1)} collective-permute-done((bf16[394,192]{1,0:T(8,128)(2,1)S(1)}, bf16[394,192]{1,0:T(8,128)(2,1)S(1)}, u32[]{:S(2)}, u32[]{:S(2)}) %collective-permute-start.5) | collective-permute-done | bytes 151328 | tf_op jit(solution)/shard_map/ppermute | solution.py:427
  19.2 2.8 %collective-permute-start.8 = (bf16[72,768]{1,0:T(8,128)(2,1)S(1)}, bf16[72,768]{1,0:T(8,128)(2,1)S(1)}, u32[]{:S(2)}, u32[]{:S(2)}) collective-permute-start(bf16[72,768]{1,0:T(8,128)(2,1)S(1)} %get-tuple-element.133), channel_id=1, source_target_pairs={{0,4},{2,6},{4,0},{6,2},{1,5},{3,7},{5,1},{7,3},{8,12},{10,14},{12... | collective-permute-start | bytes 331784 | tf_op jit(solution)/shard_map/ppermute | solution.py:430
  22.1 1.3 collective-permute-start.9
  23.5 2.7 %shard_map.214 = (f32[394,768]{1,0:T(8,128)S(1)}, bf16[144,768]{1,0:T(8,128)(2,1)S(1)}, bf16[144,768]{1,0:T(8,128)(2,1)S(1)}, bf16[144,768]{1,0:T(8,128)(2,1)S(1)}, bf16[144,768]{1,0:T(8,128)(2,1)S(1)}) custom-call(s32[8]{0:T(128)S(1)} %stack.38.ids, bf16[394,768]{1,0:T(8,128)(2,1)S(1)} %copy-done.1, f32[768]{0:T(1024)S(1)} %copy-done.16, ...), custom_call_target="tpu_custom_call" | custom-call | flops 3449999872 | bytes 1024 | tf_op jit(solution)/shard_map/pallas_call | solution.py:410
  26.2 4.6 %collective-permute-done.8.refs_2_ = bf16[72,768]{1,0:T(8,128)(2,1)S(1)} collective-permute-done((bf16[72,768]{1,0:T(8,128)(2,1)S(1)}, bf16[72,768]{1,0:T(8,128)(2,1)S(1)}, u32[]{:S(2)}, u32[]{:S(2)}) %collective-permute-start.8) | collective-permute-done | bytes 110624 | tf_op jit(solution)/shard_map/ppermute | solution.py:430
  30.8 2.9 %collective-permute-start.10 = (bf16[144,768]{1,0:T(8,128)(2,1)S(1)}, bf16[144,768]{1,0:T(8,128)(2,1)S(1)}, u32[]{:S(2)}, u32[]{:S(2)}) collective-permute-start(bf16[144,768]{1,0:T(8,128)(2,1)S(1)} %get-tuple-element.136), channel_id=1, source_target_pairs={{0,2},{2,0},{4,6},{6,4},{1,3},{3,1},{5,7},{7,5},{8,10},{10,8},{12,... | collective-permute-start | bytes 663560 | tf_op jit(solution)/shard_map/ppermute | solution.py:430
  33.7 1.6 collective-permute-start.13
  35.3 3.9 %collective-permute-start.14 = (bf16[144,768]{1,0:T(8,128)(2,1)S(1)}, bf16[144,768]{1,0:T(8,128)(2,1)S(1)}, u32[]{:S(2)}, u32[]{:S(2)}) collective-permute-start(bf16[144,768]{1,0:T(8,128)(2,1)S(1)} %get-tuple-element.146), channel_id=1, source_target_pairs={{0,4},{2,6},{4,0},{6,2},{1,5},{3,7},{5,1},{7,3},{8,12},{10,14},{12... | collective-permute-start | bytes 663560 | tf_op jit(solution)/shard_map/ppermute | solution.py:430
  39.6 4.1 %collective-permute-done.10.refs_1_ = bf16[144,768]{1,0:T(8,128)(2,1)S(1)} collective-permute-done((bf16[144,768]{1,0:T(8,128)(2,1)S(1)}, bf16[144,768]{1,0:T(8,128)(2,1)S(1)}, u32[]{:S(2)}, u32[]{:S(2)}) %collective-permute-start.10) | collective-permute-done | bytes 221216 | tf_op jit(solution)/shard_map/ppermute | solution.py:430
  43.7 5.0 %collective-permute-done.11.refs_3_ = bf16[144,768]{1,0:T(8,128)(2,1)S(1)} collective-permute-done((bf16[144,768]{1,0:T(8,128)(2,1)S(1)}, bf16[144,768]{1,0:T(8,128)(2,1)S(1)}, u32[]{:S(2)}, u32[]{:S(2)}) %collective-permute-start.11) | collective-permute-done | bytes 221216 | tf_op jit(solution)/shard_map/ppermute | solution.py:430
  48.8 7.1 %shard_map.215 = (bf16[144,768]{1,0:T(8,128)(2,1)S(1)}, bf16[144,768]{1,0:T(8,128)(2,1)S(1)}, bf16[2,144,768]{2,1,0:T(8,128)(2,1)S(1)}, bf16[2,144,768]{2,1,0:T(...) custom-call(s32[8]{0:T(128)S(1)} %stack.38.ids, ...), custom_call_target="tpu_custom_call" | custom-call | flops 8049999872 | bytes 1024 | tf_op jit(solution)/shard_map/pallas_call | solution.py:410
  55.9 0.8 collective-permute-done.15.refs_1_
  56.7 4.9 %shard_map.216 = (bf16[144,768]{1,0:T(8,128)(2,1)S(1)}, bf16[144,768]{1,0:T(8,128)(2,1)S(1)}, bf16[2,72,768]{2,1,0:T(8,128)(2,1)S(1)}, bf16[2,72,768]{2,1,0:T(8,...) custom-call(s32[8]{0:T(128)S(1)} %stack.38.ids, ...), custom_call_target="tpu_custom_call" | custom-call | flops 8049999872 | bytes 1024 | tf_op jit(solution)/shard_map/pallas_call | solution.py:410
  61.6 2.7 %shard_map.218 = (bf16[1536,768]{1,0:T(8,128)(2,1)S(1)}, bf16[1536,768]{1,0:T(8,128)(2,1)S(1)}) custom-call(bf16[288,768]{1,0:T(8,128)(2,1)S(1)} %get-tuple-element.155.refs_0_, bf16[288,768]{1,0:T(8,128)(2,1)S(1)} %get-tuple-element.156.refs_1_, bf16[288,768]{1,0:T(8,128)(2,1)S(1)} %get-tuple-element.157.refs_2_, ...), custom_call_target="tpu_custom_call" | custom-call | flops 4600000000 | bytes 1024 | tf_op jit(solution)/shard_map/pallas_call | solution.py:410
  64.3 2.1 %collective-permute-start.12 = (bf16[144,768]{1,0:T(8,128)(2,1)S(1)}, bf16[144,768]{1,0:T(8,128)(2,1)S(1)}, u32[]{:S(2)}, u32[]{:S(2)}) collective-permute-start(bf16[144,768]{1,0:T(8,128)(2,1)S(1)} %get-tuple-element.141), channel_id=1, source_target_pairs={{0,2},{2,0},{4,6},{6,4},{1,3},{3,1},{5,7},{7,5},{8,10},{10,8},{12,... | collective-permute-start | bytes 663560 | tf_op jit(solution)/shard_map/ppermute | solution.py:430
  66.5 1.5 collective-permute-start.16
  68.0 0.9 collective-permute-start.17
  68.9 1.3 collective-permute-start.18
  70.3 5.8 %collective-permute-done.18.came = bf16[2,72,768]{2,1,0:T(8,128)(2,1)S(1)} collective-permute-done((bf16[2,72,768]{2,1,0:T(8,128)(2,1)S(1)}, bf16[2,72,768]{2,1,0:T(8,128)(2,1)S(1)}, u32[]{:S(2)}, u32[]{:S(2)}) %collective-permute-start.18) | collective-permute-done | bytes 221216 | tf_op jit(solution)/shard_map/ppermute | solution.py:427
  76.2 1.6 shard_map.219
  77.8 1.4 copy-done.17
  79.2 6.0 %collective-permute-done.16.refs_2_ = bf16[144,768]{1,0:T(8,128)(2,1)S(1)} collective-permute-done((bf16[144,768]{1,0:T(8,128)(2,1)S(1)}, bf16[144,768]{1,0:T(8,128)(2,1)S(1)}, u32[]{:S(2)}, u32[]{:S(2)}) %collective-permute-start.16) | collective-permute-done | bytes 221216 | tf_op jit(solution)/shard_map/ppermute | solution.py:430
  85.2 1.5 shard_map.220
  86.7 1.6 collective-permute-done.20
  88.4 0.6 collective-permute-start.21
  89.0 1.5 collective-permute-start.22
  90.6 4.5 %collective-permute-start.23 = (bf16[144,768]{1,0:T(8,128)(2,1)S(1)}, bf16[144,768]{1,0:T(8,128)(2,1)S(1)}, u32[]{:S(2)}, u32[]{:S(2)}) collective-permute-start(bf16[144,768]{1,0:T(8,128)(2,1)S(1)} %get-tuple-element.175), channel_id=1, source_target_pairs={{0,2},{2,0},{4,6},{6,4},{1,3},{3,1},{5,7},{7,5},{8,10},{10,8},{12,... | collective-permute-start | bytes 663560 | tf_op jit(solution)/shard_map/ppermute | solution.py:430
  95.1 0.9 collective-permute-start.24
  96.0 1.5 collective-permute-start.25
  97.5 0.6 collective-permute-done.21
  98.2 5.0 %collective-permute-done.24.refs_2_ = bf16[72,768]{1,0:T(8,128)(2,1)S(1)} collective-permute-done((bf16[72,768]{1,0:T(8,128)(2,1)S(1)}, bf16[72,768]{1,0:T(8,128)(2,1)S(1)}, u32[]{:S(2)}, u32[]{:S(2)}) %collective-permute-start.24) | collective-permute-done | bytes 110624 | tf_op jit(solution)/shard_map/ppermute | solution.py:430
  103.1 4.1 %collective-permute-done.25.refs_3_ = bf16[72,768]{1,0:T(8,128)(2,1)S(1)} collective-permute-done((bf16[72,768]{1,0:T(8,128)(2,1)S(1)}, bf16[72,768]{1,0:T(8,128)(2,1)S(1)}, u32[]{:S(2)}, u32[]{:S(2)}) %collective-permute-start.25) | collective-permute-done | bytes 110624 | tf_op jit(solution)/shard_map/ppermute | solution.py:430
  107.2 1.6 collective-permute-done.26.other
  108.8 4.9 %shard_map.221 = (f32[394,768]{1,0:T(8,128)S(1)}, bf16[394,384]{1,0:T(8,128)(2,1)S(1)}, bf16[394,384]{1,0:T(8,128)(2,1)S(1)}, f32[16,768]{1,0:T(8,128)S(1)}, bf1...) custom-call(s32[8]{0:T(128)S(1)} %stack.38.ids, ...), custom_call_target="tpu_custom_call" | custom-call | flops 6899999744 | bytes 1024 | tf_op jit(solution)/shard_map/pallas_call | solution.py:410
  114.0 0.7 collective-permute-start.29
  114.7 1.5 collective-permute-start.30
  116.2 1.3 collective-permute-start.31
  117.5 1.5 shard_map.222
  119.1 1.6 collective-permute-start.34
  120.7 4.1 %collective-permute-done.29.refs_1_ = bf16[192,768]{1,0:T(8,128)(2,1)S(1)} collective-permute-done((bf16[192,768]{1,0:T(8,128)(2,1)S(1)}, bf16[192,768]{1,0:T(8,128)(2,1)S(1)}, u32[]{:S(2)}, u32[]{:S(2)}) %collective-permute-start.29) | collective-permute-done | bytes 294944 | tf_op jit(solution)/shard_map/ppermute | solution.py:437
  124.8 5.3 %collective-permute-done.30.refs_2_ = bf16[192,768]{1,0:T(8,128)(2,1)S(1)} collective-permute-done((bf16[192,768]{1,0:T(8,128)(2,1)S(1)}, bf16[192,768]{1,0:T(8,128)(2,1)S(1)}, u32[]{:S(2)}, u32[]{:S(2)}) %collective-permute-start.30) | collective-permute-done | bytes 294944 | tf_op jit(solution)/shard_map/ppermute | solution.py:437
  130.3 1.5 collective-permute-start.28
  132.0 1.3 collective-permute-start.32
  133.6 2.4 %shard_map.224 = (bf16[394,768]{1,0:T(8,128)(2,1)}, f32[16,768]{1,0:T(8,128)S(1)}) custom-call(s32[8]{0:T(128)S(1)} %stack.38.ids, bf16[394,384]{1,0:T(8,128)(2,1)S(1)} %add_convert_fusion.2.own, bf16[394,384]{1,0:T(8,128)(2,1)S(1)} %collective-permute-done.35.other, bf16[394,768]{1,0:T(8,128)(2,1)S(1)} %copy-done.1, ...), custom_call_target="tpu_custom_call" | custom-call | flops 11500000 | bytes 1024 | tf_op jit(solution)/shard_map/pallas_call | solution.py:410
  136.0 1.4 collective-permute-start.36
  137.4 1.7 collective-permute-done.28
  139.1 0.8 add_convert_fusion.4
  139.9 10.2 %collective-permute-done.32.came = bf16[192,768]{1,0:T(8,128)(2,1)S(1)} collective-permute-done((bf16[192,768]{1,0:T(8,128)(2,1)S(1)}, bf16[192,768]{1,0:T(8,128)(2,1)S(1)}, u32[]{:S(2)}, u32[]{:S(2)}) %collective-permute-start.32) | collective-permute-done | bytes 294944 | tf_op jit(solution)/shard_map/ppermute | solution.py:430
  150.1 0.6 collective-permute-done.36.small_came
  150.9 1.1 collective-permute-start.41
  152.1 1.0 collective-permute-start.38
  153.0 2.5 %collective-permute-start.40 = (bf16[208,768]{1,0:T(8,128)(2,1)S(1)}, bf16[208,768]{1,0:T(8,128)(2,1)}, u32[]{:S(2)}, u32[]{:S(2)}) collective-permute-start(bf16[208,768]{1,0:T(8,128)(2,1)S(1)} %shard_map.225.refs_0_), channel_id=1, source_target_pairs={{0,3},{1,2},{2,1},{3,0},{4,7},{5,6},{6,5},{7,4},{8,11},{9,10},{10,... | collective-permute-start | bytes 958472 | tf_op jit(solution)/shard_map/ppermute | solution.py:437
  155.6 2.5 %select_convert_fusion = bf16[394,768]{1,0:T(8,128)(2,1)} fusion(f32[394,768]{1,0:T(8,128)S(1)} %get-tuple-element.124.middle, bf16[400,384]{1,0:T(8,128)(2,1)} %collective-permute-done.37, bf16[400,384]{1,0:T(8,128)(2,1)} %add_convert_fusion.4, pred[394]{0:T(512)(128)(4,1)S(1)} %iota_compare_fusion, pred[]{:T(512)S(6)} %eq.7), kind=kLoop, calls=%fused_computation | loop fusion | flops 3933696 | bytes 2430347 | tf_op jit(solution)/shard_map/convert_element_type | solution.py:699
  158.1 26.6 %collective-permute-done.38.refs_1_ = bf16[208,768]{1,0:T(8,128)(2,1)} collective-permute-done((bf16[208,768]{1,0:T(8,128)(2,1)S(1)}, bf16[208,768]{1,0:T(8,128)(2,1)}, u32[]{:S(2)}, u32[]{:S(2)}) %collective-permute-start.38) | collective-permute-done | bytes 319520 | tf_op jit(solution)/shard_map/ppermute | solution.py:437
  184.7 2.8 %shard_map.226 = (f32[576,768]{1,0:T(8,128)}, f32[192,768]{1,0:T(8,128)}, f32[768]{0:T(1024)}, f32[768]{0:T(1024)}, f32[768]{0:T(1024)}, /*index=5*/f32[768]{0:T(1024)}, f32[4,768]{1,0:T(4,128)}) custom-call(s32[8]{0:T(128)S(1)} %stack.38.ids, bf16[208,768]{1,0:T(8,128)(2,1)S(1)} %shard_map.225.refs_0_, bf16[208,768]{1,0:T(8,128)(2,1)} %collective-permute-done.38.refs_1_, ...), custom_call_target="tpu_custom_call" | custom-call | flops 3449999872 | bytes 1024 | tf_op jit(solution)/shard_map/pallas_call | solution.py:410
  187.5 1.7 shard_map.227
  (85 shorter events, 3.7 us)
Async XLA Ops:
  0.6 11.0 %collective-permute-start.2 = (bf16[768,768]{1,0:T(8,128)(2,1)}, bf16[768,768]{1,0:T(8,128)(2,1)S(1)}, u32[]{:S(2)}, u32[]{:S(2)}) collective-permute-start(bf16[768,768]{1,0:T(8,128)(2,1)} %bitcast.28), channel_id=1, source_target_pairs={{0,8},{8,0},{16,24},{24,16},{1,9},{9,1},{17,25},{25,17},{2,10},{10... | collective-permute-start | bytes 3538952 | tf_op jit(solution)/shard_map/ppermute | solution.py:427
  1.2 10.5 %collective-permute-start.3 = (bf16[768,768]{1,0:T(8,128)(2,1)}, bf16[768,768]{1,0:T(8,128)(2,1)S(1)}, u32[]{:S(2)}, u32[]{:S(2)}) collective-permute-start(bf16[768,768]{1,0:T(8,128)(2,1)} %bitcast.31), channel_id=1, source_target_pairs={{0,8},{8,0},{16,24},{24,16},{1,9},{9,1},{17,25},{25,17},{2,10},{10... | collective-permute-start | bytes 3538952 | tf_op jit(solution)/shard_map/ppermute | solution.py:427
  1.2 10.4 %collective-permute-start = (bf16[192,768]{1,0:T(8,128)(2,1)}, bf16[192,768]{1,0:T(8,128)(2,1)S(1)}, u32[]{:S(2)}, u32[]{:S(2)}) collective-permute-start(bf16[192,768]{1,0:T(8,128)(2,1)} %w_out.1), channel_id=1, source_target_pairs={{0,16},{8,24},{16,0},{24,8},{1,17},{9,25},{17,1},{25,9},{2,18},{10... | collective-permute-start | bytes 884744 | tf_op jit(solution)/shard_map/ppermute | solution.py:427
  4.2 7.5 %collective-permute-start.1 = (bf16[192,768]{1,0:T(8,128)(2,1)}, bf16[192,768]{1,0:T(8,128)(2,1)S(1)}, u32[]{:S(2)}, u32[]{:S(2)}) collective-permute-start(bf16[192,768]{1,0:T(8,128)(2,1)} %w_out.1), channel_id=1, source_target_pairs={{0,8},{8,0},{16,24},{24,16},{1,9},{9,1},{17,25},{25,17},{2,10},{10... | collective-permute-start | bytes 884744 | tf_op jit(solution)/shard_map/ppermute | solution.py:427
  4.9 1.1 copy-start
  6.0 0.7 copy-start.2
  6.7 1.2 copy-start.8
  7.8 0.7 copy-start.13
  8.5 5.2 %copy-start.10 = (bf16[394,768]{1,0:T(8,128)(2,1)S(1)}, bf16[394,768]{1,0:T(8,128)(2,1)}, u32[]{:S(2)}) copy-start(bf16[394,768]{1,0:T(8,128)(2,1)} %cot.3) | copy-start | bytes 1815556
  8.5 5.2 %copy-start.12 = (bf16[768,4]{0,1:T(4,128)(2,1)S(1)}, bf16[768,4]{0,1:T(4,128)(2,1)}, u32[]{:S(2)}) copy-start(bf16[768,4]{0,1:T(4,128)(2,1)} %param.22) | copy-start | bytes 18436
  8.5 5.2 %copy-start.14 = (s32[394,2]{0,1:T(2,128)S(1)}, s32[394,2]{0,1:T(2,128)}, u32[]{:S(2)}) copy-start(s32[394,2]{0,1:T(2,128)} %param.14) | copy-start | bytes 9460
  11.6 3.5 %copy-start.6 = (bf16[768,768]{1,0:T(8,128)(2,1)}, bf16[768,768]{1,0:T(8,128)(2,1)S(1)}, u32[]{:S(2)}) copy-start(bf16[768,768]{1,0:T(8,128)(2,1)S(1)} %collective-permute-done.3.down_b) | copy-start | bytes 3538948
  11.6 11.8 %collective-permute-start.4 = (bf16[394,192]{1,0:T(8,128)(2,1)S(1)}, bf16[394,192]{1,0:T(8,128)(2,1)S(1)}, u32[]{:S(2)}, u32[]{:S(2)}) collective-permute-start(bf16[394,192]{1,0:T(8,128)(2,1)S(1)} %get-tuple-element.118.rest_0_.head_out), channel_id=1, source_target_pairs={{0,8},{8,0},{16,24},{24,16},{1,9},{9,1},{17,25},{25,17},{2,10},{10... | collective-permute-start | bytes 453896 | tf_op jit(solution)/shard_map/ppermute | solution.py:427
  11.7 7.5 %collective-permute-start.5 = (bf16[394,192]{1,0:T(8,128)(2,1)S(1)}, bf16[394,192]{1,0:T(8,128)(2,1)S(1)}, u32[]{:S(2)}, u32[]{:S(2)}) collective-permute-start(bf16[394,192]{1,0:T(8,128)(2,1)S(1)} %get-tuple-element.118.rest_0_.head_out), channel_id=1, source_target_pairs={{0,16},{8,24},{16,0},{24,8},{1,17},{9,25},{17,1},{25,9},{2,18},{10... | collective-permute-start | bytes 453896 | tf_op jit(solution)/shard_map/ppermute | solution.py:427
  13.5 9.9 %collective-permute-start.7 = (bf16[192,768]{1,0:T(8,128)(2,1)S(1)}, bf16[192,768]{1,0:T(8,128)(2,1)S(1)}, u32[]{:S(2)}, u32[]{:S(2)}) collective-permute-start(bf16[192,768]{1,0:T(8,128)(2,1)S(1)} %collective-permute-done.rest_6_), channel_id=1, source_target_pairs={{0,8},{8,0},{16,24},{24,16},{1,9},{9,1},{17,25},{25,17},{2,10},{10... | collective-permute-start | bytes 884744 | tf_op jit(solution)/shard_map/ppermute | solution.py:427
  13.7 9.7 %copy-start.1 = (bf16[394,768]{1,0:T(8,128)(2,1)S(1)}, bf16[394,768]{1,0:T(8,128)(2,1)}, u32[]{:S(2)}) copy-start(bf16[394,768]{1,0:T(8,128)(2,1)} %tokens.5) | copy-start | bytes 1815556
  13.7 9.7 %copy-start.11 = (bf16[192,768]{1,0:T(8,128)(2,1)S(1)}, bf16[192,768]{1,0:T(8,128)(2,1)}, u32[]{:S(2)}) copy-start(bf16[192,768]{1,0:T(8,128)(2,1)} %w_out.1) | copy-start | bytes 884740
  13.7 9.7 %copy-start.15 = (f32[768]{0:T(1024)S(1)}, f32[768]{0:T(1024)}, u32[]{:S(2)}) copy-start(f32[768]{0:T(1024)} %bias.3) | copy-start | bytes 9220
  13.7 9.7 %copy-start.16 = (f32[768]{0:T(1024)S(1)}, f32[768]{0:T(1024)}, u32[]{:S(2)}) copy-start(f32[768]{0:T(1024)} %gain.6) | copy-start | bytes 9220
  19.2 4.2 %collective-permute-start.6 = (bf16[394,192]{1,0:T(8,128)(2,1)S(1)}, bf16[394,192]{1,0:T(8,128)(2,1)S(1)}, u32[]{:S(2)}, u32[]{:S(2)}) collective-permute-start(bf16[394,192]{1,0:T(8,128)(2,1)S(1)} %collective-permute-done.5.rest_2_), channel_id=1, source_target_pairs={{0,8},{8,0},{16,24},{24,16},{1,9},{9,1},{17,25},{25,17},{2,10},{10... | collective-permute-start | bytes 453896 | tf_op jit(solution)/shard_map/ppermute | solution.py:427
  19.2 11.6 %collective-permute-start.8 = (bf16[72,768]{1,0:T(8,128)(2,1)S(1)}, bf16[72,768]{1,0:T(8,128)(2,1)S(1)}, u32[]{:S(2)}, u32[]{:S(2)}) collective-permute-start(bf16[72,768]{1,0:T(8,128)(2,1)S(1)} %get-tuple-element.133), channel_id=1, source_target_pairs={{0,4},{2,6},{4,0},{6,2},{1,5},{3,7},{5,1},{7,3},{8,12},{10,14},{12... | collective-permute-start | bytes 331784 | tf_op jit(solution)/shard_map/ppermute | solution.py:430
  22.1 26.7 %copy-start.4 = (bf16[1,768,768]{2,1,0:T(8,128)(2,1)S(1)}, bf16[1,768,768]{2,1,0:T(8,128)(2,1)}, u32[]{:S(2)}) copy-start(bf16[1,768,768]{2,1,0:T(8,128)(2,1)} %param.23) | copy-start | bytes 3538948
  22.1 26.7 %copy-start.5 = (bf16[1,768,768]{2,1,0:T(8,128)(2,1)S(1)}, bf16[1,768,768]{2,1,0:T(8,128)(2,1)}, u32[]{:S(2)}) copy-start(bf16[1,768,768]{2,1,0:T(8,128)(2,1)} %param.24) | copy-start | bytes 3538948
  22.1 26.7 %copy-start.7 = (bf16[768,768]{1,0:T(8,128)(2,1)S(1)}, bf16[768,768]{1,0:T(8,128)(2,1)}, u32[]{:S(2)}) copy-start(bf16[768,768]{1,0:T(8,128)(2,1)} %copy-done.6) | copy-start | bytes 3538948
  22.1 8.7 %collective-permute-start.9 = (bf16[72,768]{1,0:T(8,128)(2,1)S(1)}, bf16[72,768]{1,0:T(8,128)(2,1)S(1)}, u32[]{:S(2)}, u32[]{:S(2)}) collective-permute-start(bf16[72,768]{1,0:T(8,128)(2,1)S(1)} %get-tuple-element.134), channel_id=1, source_target_pairs={{0,6},{2,4},{4,2},{6,0},{1,7},{3,5},{5,3},{7,1},{8,14},{10,12},{12... | collective-permute-start | bytes 331784 | tf_op jit(solution)/shard_map/ppermute | solution.py:430
  30.8 12.9 %collective-permute-start.10 = (bf16[144,768]{1,0:T(8,128)(2,1)S(1)}, bf16[144,768]{1,0:T(8,128)(2,1)S(1)}, u32[]{:S(2)}, u32[]{:S(2)}) collective-permute-start(bf16[144,768]{1,0:T(8,128)(2,1)S(1)} %get-tuple-element.136), channel_id=1, source_target_pairs={{0,2},{2,0},{4,6},{6,4},{1,3},{3,1},{5,7},{7,5},{8,10},{10,8},{12,... | collective-permute-start | bytes 663560 | tf_op jit(solution)/shard_map/ppermute | solution.py:430
  33.6 15.1 %collective-permute-start.11 = (bf16[144,768]{1,0:T(8,128)(2,1)S(1)}, bf16[144,768]{1,0:T(8,128)(2,1)S(1)}, u32[]{:S(2)}, u32[]{:S(2)}) collective-permute-start(bf16[144,768]{1,0:T(8,128)(2,1)S(1)} %get-tuple-element.139), channel_id=1, source_target_pairs={{0,2},{2,0},{4,6},{6,4},{1,3},{3,1},{5,7},{7,5},{8,10},{10,8},{12,... | collective-permute-start | bytes 663560 | tf_op jit(solution)/shard_map/ppermute | solution.py:430
  33.7 22.2 %collective-permute-start.13 = (bf16[2,72,768]{2,1,0:T(8,128)(2,1)S(1)}, bf16[2,72,768]{2,1,0:T(8,128)(2,1)S(1)}, u32[]{:S(2)}, u32[]{:S(2)}) collective-permute-start(bf16[2,72,768]{2,1,0:T(8,128)(2,1)S(1)} %pad_maximum_fusion.2), channel_id=1, source_target_pairs={{0,16},{8,24},{16,0},{24,8},{1,17},{9,25},{17,1},{25,9},{2,18},{10... | collective-permute-start | bytes 663560 | tf_op jit(solution)/shard_map/ppermute | solution.py:427
  35.3 20.6 %collective-permute-start.14 = (bf16[144,768]{1,0:T(8,128)(2,1)S(1)}, bf16[144,768]{1,0:T(8,128)(2,1)S(1)}, u32[]{:S(2)}, u32[]{:S(2)}) collective-permute-start(bf16[144,768]{1,0:T(8,128)(2,1)S(1)} %get-tuple-element.146), channel_id=1, source_target_pairs={{0,4},{2,6},{4,0},{6,2},{1,5},{3,7},{5,1},{7,3},{8,12},{10,14},{12... | collective-permute-start | bytes 663560 | tf_op jit(solution)/shard_map/ppermute | solution.py:430
  39.1 17.6 %collective-permute-start.15 = (bf16[144,768]{1,0:T(8,128)(2,1)S(1)}, bf16[144,768]{1,0:T(8,128)(2,1)S(1)}, u32[]{:S(2)}, u32[]{:S(2)}) collective-permute-start(bf16[144,768]{1,0:T(8,128)(2,1)S(1)} %get-tuple-element.147), channel_id=1, source_target_pairs={{0,6},{2,4},{4,2},{6,0},{1,7},{3,5},{5,3},{7,1},{8,14},{10,12},{12... | collective-permute-start | bytes 663560 | tf_op jit(solution)/shard_map/ppermute | solution.py:430
  64.3 11.9 %collective-permute-start.19 = (bf16[1536,768]{1,0:T(8,128)(2,1)S(1)}, bf16[1536,768]{1,0:T(8,128)(2,1)S(1)}, u32[]{:S(2)}, u32[]{:S(2)}) collective-permute-start(bf16[1536,768]{1,0:T(8,128)(2,1)S(1)} %get-tuple-element.164), channel_id=1, source_target_pairs={{0,8},{8,0},{16,24},{24,16},{1,9},{9,1},{17,25},{25,17},{2,10},{10... | collective-permute-start | bytes 7077896 | tf_op jit(solution)/shard_map/ppermute | solution.py:427
  64.3 14.9 %collective-permute-start.12 = (bf16[144,768]{1,0:T(8,128)(2,1)S(1)}, bf16[144,768]{1,0:T(8,128)(2,1)S(1)}, u32[]{:S(2)}, u32[]{:S(2)}) collective-permute-start(bf16[144,768]{1,0:T(8,128)(2,1)S(1)} %get-tuple-element.141), channel_id=1, source_target_pairs={{0,2},{2,0},{4,6},{6,4},{1,3},{3,1},{5,7},{7,5},{8,10},{10,8},{12,... | collective-permute-start | bytes 663560 | tf_op jit(solution)/shard_map/ppermute | solution.py:430
  66.5 18.7 %collective-permute-start.16 = (bf16[144,768]{1,0:T(8,128)(2,1)S(1)}, bf16[144,768]{1,0:T(8,128)(2,1)S(1)}, u32[]{:S(2)}, u32[]{:S(2)}) collective-permute-start(bf16[144,768]{1,0:T(8,128)(2,1)S(1)} %get-tuple-element.148), channel_id=1, source_target_pairs={{0,4},{2,6},{4,0},{6,2},{1,5},{3,7},{5,1},{7,3},{8,12},{10,14},{12... | collective-permute-start | bytes 663560 | tf_op jit(solution)/shard_map/ppermute | solution.py:430
  68.0 17.2 %collective-permute-start.17 = (bf16[144,768]{1,0:T(8,128)(2,1)S(1)}, bf16[144,768]{1,0:T(8,128)(2,1)S(1)}, u32[]{:S(2)}, u32[]{:S(2)}) collective-permute-start(bf16[144,768]{1,0:T(8,128)(2,1)S(1)} %get-tuple-element.149), channel_id=1, source_target_pairs={{0,6},{2,4},{4,2},{6,0},{1,7},{3,5},{5,3},{7,1},{8,14},{10,12},{12... | collective-permute-start | bytes 663560 | tf_op jit(solution)/shard_map/ppermute | solution.py:430
  68.9 7.2 %collective-permute-start.18 = (bf16[2,72,768]{2,1,0:T(8,128)(2,1)S(1)}, bf16[2,72,768]{2,1,0:T(8,128)(2,1)S(1)}, u32[]{:S(2)}, u32[]{:S(2)}) collective-permute-start(bf16[2,72,768]{2,1,0:T(8,128)(2,1)S(1)} %get-tuple-element.152), channel_id=1, source_target_pairs={{0,16},{8,24},{16,0},{24,8},{1,17},{9,25},{17,1},{25,9},{2,18},{10... | collective-permute-start | bytes 663560 | tf_op jit(solution)/shard_map/ppermute | solution.py:427
  77.8 1.4 copy-start.17
  86.7 22.2 %copy-start.9 = (bf16[768,3,192]{0,2,1:T(8,128)(2,1)S(1)}, bf16[768,3,192]{0,2,1:T(8,128)(2,1)}, u32[]{:S(2)}) copy-start(bf16[768,3,192]{0,2,1:T(8,128)(2,1)} %param.18) | copy-start | bytes 2654212
  86.7 1.7 collective-permute-start.20
  88.4 9.6 %collective-permute-start.21 = (bf16[416,384]{1,0:T(8,128)(2,1)S(1)}, bf16[416,384]{1,0:T(8,128)(2,1)S(1)}, u32[]{:S(2)}, u32[]{:S(2)}) collective-permute-start(bf16[416,384]{1,0:T(8,128)(2,1)S(1)} %add_convert_fusion.1), channel_id=1, source_target_pairs={{0,16},{8,24},{16,0},{24,8},{1,17},{9,25},{17,1},{25,9},{2,18},{10... | collective-permute-start | bytes 958472 | tf_op jit(solution)/shard_map/ppermute | solution.py:427
  89.0 18.2 %collective-permute-start.22 = (bf16[256,768]{1,0:T(8,128)(2,1)S(1)}, bf16[256,768]{1,0:T(8,128)(2,1)S(1)}, u32[]{:S(2)}, u32[]{:S(2)}) collective-permute-start(bf16[256,768]{1,0:T(8,128)(2,1)S(1)} %get-tuple-element.173), channel_id=1, source_target_pairs={{0,1},{1,0},{2,3},{3,2},{4,5},{5,4},{6,7},{7,6},{8,9},{9,8},{10,11... | collective-permute-start | bytes 1179656 | tf_op jit(solution)/shard_map/ppermute | solution.py:433
  90.6 16.7 %collective-permute-start.23 = (bf16[144,768]{1,0:T(8,128)(2,1)S(1)}, bf16[144,768]{1,0:T(8,128)(2,1)S(1)}, u32[]{:S(2)}, u32[]{:S(2)}) collective-permute-start(bf16[144,768]{1,0:T(8,128)(2,1)S(1)} %get-tuple-element.175), channel_id=1, source_target_pairs={{0,2},{2,0},{4,6},{6,4},{1,3},{3,1},{5,7},{7,5},{8,10},{10,8},{12,... | collective-permute-start | bytes 663560 | tf_op jit(solution)/shard_map/ppermute | solution.py:430
  95.1 8.0 %collective-permute-start.24 = (bf16[72,768]{1,0:T(8,128)(2,1)S(1)}, bf16[72,768]{1,0:T(8,128)(2,1)S(1)}, u32[]{:S(2)}, u32[]{:S(2)}) collective-permute-start(bf16[72,768]{1,0:T(8,128)(2,1)S(1)} %get-tuple-element.176), channel_id=1, source_target_pairs={{0,4},{2,6},{4,0},{6,2},{1,5},{3,7},{5,1},{7,3},{8,12},{10,14},{12... | collective-permute-start | bytes 331784 | tf_op jit(solution)/shard_map/ppermute | solution.py:430
  96.0 11.2 %collective-permute-start.25 = (bf16[72,768]{1,0:T(8,128)(2,1)S(1)}, bf16[72,768]{1,0:T(8,128)(2,1)S(1)}, u32[]{:S(2)}, u32[]{:S(2)}) collective-permute-start(bf16[72,768]{1,0:T(8,128)(2,1)S(1)} %get-tuple-element.177), channel_id=1, source_target_pairs={{0,6},{2,4},{4,2},{6,0},{1,7},{3,5},{5,3},{7,1},{8,14},{10,12},{12... | collective-permute-start | bytes 331784 | tf_op jit(solution)/shard_map/ppermute | solution.py:430
  107.2 1.6 collective-permute-start.26
  113.8 5.3 %collective-permute-start.33 = (bf16[394,384]{1,0:T(8,128)(2,1)S(1)}, bf16[394,384]{1,0:T(8,128)(2,1)S(1)}, u32[]{:S(2)}, u32[]{:S(2)}) collective-permute-start(bf16[394,384]{1,0:T(8,128)(2,1)S(1)} %get-tuple-element.204), channel_id=1, source_target_pairs={{0,8},{8,0},{16,24},{24,16},{1,9},{9,1},{17,25},{25,17},{2,10},{10... | collective-permute-start | bytes 907784 | tf_op jit(solution)/shard_map/ppermute | solution.py:427
  114.0 10.8 %collective-permute-start.29 = (bf16[192,768]{1,0:T(8,128)(2,1)S(1)}, bf16[192,768]{1,0:T(8,128)(2,1)S(1)}, u32[]{:S(2)}, u32[]{:S(2)}) collective-permute-start(bf16[192,768]{1,0:T(8,128)(2,1)S(1)} %get-tuple-element.199), channel_id=1, source_target_pairs={{0,3},{1,2},{2,1},{3,0},{4,7},{5,6},{6,5},{7,4},{8,11},{9,10},{10,... | collective-permute-start | bytes 884744 | tf_op jit(solution)/shard_map/ppermute | solution.py:437
  114.7 15.3 %collective-permute-start.30 = (bf16[192,768]{1,0:T(8,128)(2,1)S(1)}, bf16[192,768]{1,0:T(8,128)(2,1)S(1)}, u32[]{:S(2)}, u32[]{:S(2)}) collective-permute-start(bf16[192,768]{1,0:T(8,128)(2,1)S(1)} %get-tuple-element.200), channel_id=1, source_target_pairs={{0,1},{1,0},{2,3},{3,2},{4,5},{5,4},{6,7},{7,6},{8,9},{9,8},{10,11... | collective-permute-start | bytes 884744 | tf_op jit(solution)/shard_map/ppermute | solution.py:437
  116.2 13.8 %collective-permute-start.31 = (bf16[192,768]{1,0:T(8,128)(2,1)S(1)}, bf16[192,768]{1,0:T(8,128)(2,1)S(1)}, u32[]{:S(2)}, u32[]{:S(2)}) collective-permute-start(bf16[192,768]{1,0:T(8,128)(2,1)S(1)} %get-tuple-element.201), channel_id=1, source_target_pairs={{0,2},{1,3},{2,0},{3,1},{4,6},{5,7},{6,4},{7,5},{8,10},{9,11},{10,... | collective-permute-start | bytes 884744 | tf_op jit(solution)/shard_map/ppermute | solution.py:437
  119.0 11.2 %collective-permute-start.27 = (bf16[400,384]{1,0:T(8,128)(2,1)S(1)}, bf16[400,384]{1,0:T(8,128)(2,1)S(1)}, u32[]{:S(2)}, u32[]{:S(2)}) collective-permute-start(bf16[400,384]{1,0:T(8,128)(2,1)S(1)} %get-tuple-element.197), channel_id=1, source_target_pairs={{0,8},{8,0},{16,24},{24,16},{1,9},{9,1},{17,25},{25,17},{2,10},{10... | collective-permute-start | bytes 921608 | tf_op jit(solution)/shard_map/ppermute | solution.py:427
  119.1 12.7 %collective-permute-start.34 = (bf16[394,384]{1,0:T(8,128)(2,1)S(1)}, bf16[394,384]{1,0:T(8,128)(2,1)S(1)}, u32[]{:S(2)}, u32[]{:S(2)}) collective-permute-start(bf16[394,384]{1,0:T(8,128)(2,1)S(1)} %add_convert_fusion.3), channel_id=1, source_target_pairs={{0,16},{8,24},{16,0},{24,8},{1,17},{9,25},{17,1},{25,9},{2,18},{10... | collective-permute-start | bytes 907784 | tf_op jit(solution)/shard_map/ppermute | solution.py:427
  130.2 3.4 %copy-start.3 = (f32[768]{0:T(1024)S(1)}, f32[768]{0:T(1024)}, u32[]{:S(2)}) copy-start(f32[768]{0:T(1024)} %gain.7) | copy-start | bytes 9220
  130.3 8.8 %collective-permute-start.28 = (bf16[400,384]{1,0:T(8,128)(2,1)S(1)}, bf16[400,384]{1,0:T(8,128)(2,1)S(1)}, u32[]{:S(2)}, u32[]{:S(2)}) collective-permute-start(bf16[400,384]{1,0:T(8,128)(2,1)S(1)} %add_convert_fusion.5), channel_id=1, source_target_pairs={{0,16},{8,24},{16,0},{24,8},{1,17},{9,25},{17,1},{25,9},{2,18},{10... | collective-permute-start | bytes 921608 | tf_op jit(solution)/shard_map/ppermute | solution.py:427
  131.9 1.7 collective-permute-start.35
  132.0 18.1 %collective-permute-start.32 = (bf16[192,768]{1,0:T(8,128)(2,1)S(1)}, bf16[192,768]{1,0:T(8,128)(2,1)S(1)}, u32[]{:S(2)}, u32[]{:S(2)}) collective-permute-start(bf16[192,768]{1,0:T(8,128)(2,1)S(1)} %shard_map.223.own), channel_id=1, source_target_pairs={{0,4},{2,6},{4,0},{6,2},{1,5},{3,7},{5,1},{7,3},{8,12},{10,14},{12... | collective-permute-start | bytes 884744 | tf_op jit(solution)/shard_map/ppermute | solution.py:430
  136.0 14.8 %collective-permute-start.36 = (f32[16,768]{1,0:T(8,128)S(1)}, f32[16,768]{1,0:T(8,128)S(1)}, u32[]{:S(2)}, u32[]{:S(2)}) collective-permute-start(f32[16,768]{1,0:T(8,128)S(1)} %get-tuple-element.207.small), channel_id=1, source_target_pairs={{0,4},{2,6},{4,0},{6,2},{1,5},{3,7},{5,1},{7,3},{8,12},{10,14},{12... | collective-permute-start | bytes 147464 | tf_op jit(solution)/shard_map/ppermute | solution.py:430
  150.8 4.7 %collective-permute-start.37 = (bf16[400,384]{1,0:T(8,128)(2,1)}, bf16[400,384]{1,0:T(8,128)(2,1)}, u32[]{:S(2)}, u32[]{:S(2)}) collective-permute-start(bf16[400,384]{1,0:T(8,128)(2,1)} %add_convert_fusion.4), channel_id=1, source_target_pairs={{0,8},{8,0},{16,24},{24,16},{1,9},{9,1},{17,25},{25,17},{2,10},{10... | collective-permute-start | bytes 921608 | tf_op jit(solution)/shard_map/ppermute | solution.py:427
  150.9 36.6 %collective-permute-start.41 = (bf16[512,768]{1,0:T(8,128)(2,1)S(1)}, bf16[512,768]{1,0:T(8,128)(2,1)S(1)}, u32[]{:S(2)}, u32[]{:S(2)}) collective-permute-start(bf16[512,768]{1,0:T(8,128)(2,1)S(1)} %get-tuple-element.220), channel_id=1, source_target_pairs={{0,1},{1,0},{2,3},{3,2},{4,5},{5,4},{6,7},{7,6},{8,9},{9,8},{10,11... | collective-permute-start | bytes 2359304 | tf_op jit(solution)/shard_map/ppermute | solution.py:433
  152.1 32.6 %collective-permute-start.38 = (bf16[208,768]{1,0:T(8,128)(2,1)S(1)}, bf16[208,768]{1,0:T(8,128)(2,1)}, u32[]{:S(2)}, u32[]{:S(2)}) collective-permute-start(bf16[208,768]{1,0:T(8,128)(2,1)S(1)} %shard_map.225.refs_0_), channel_id=1, source_target_pairs={{0,1},{1,0},{2,3},{3,2},{4,5},{5,4},{6,7},{7,6},{8,9},{9,8},{10,11... | collective-permute-start | bytes 958472 | tf_op jit(solution)/shard_map/ppermute | solution.py:437
  153.0 31.7 %collective-permute-start.39 = (bf16[208,768]{1,0:T(8,128)(2,1)S(1)}, bf16[208,768]{1,0:T(8,128)(2,1)}, u32[]{:S(2)}, u32[]{:S(2)}) collective-permute-start(bf16[208,768]{1,0:T(8,128)(2,1)S(1)} %shard_map.225.refs_0_), channel_id=1, source_target_pairs={{0,2},{1,3},{2,0},{3,1},{4,6},{5,7},{6,4},{7,5},{8,10},{9,11},{10,... | collective-permute-start | bytes 958472 | tf_op jit(solution)/shard_map/ppermute | solution.py:437
  153.0 31.7 %collective-permute-start.40 = (bf16[208,768]{1,0:T(8,128)(2,1)S(1)}, bf16[208,768]{1,0:T(8,128)(2,1)}, u32[]{:S(2)}, u32[]{:S(2)}) collective-permute-start(bf16[208,768]{1,0:T(8,128)(2,1)S(1)} %shard_map.225.refs_0_), channel_id=1, source_target_pairs={{0,3},{1,2},{2,1},{3,0},{4,7},{5,6},{6,5},{7,4},{8,11},{9,10},{10,... | collective-permute-start | bytes 958472 | tf_op jit(solution)/shard_map/ppermute | solution.py:437
  158.1 29.4 %copy-start.18 = (f32[768,768]{1,0:T(8,128)S(1)}, f32[768,768]{1,0:T(8,128)}, u32[]{:S(2)}) copy-start(f32[768,768]{1,0:T(8,128)} %copy-done.17) | copy-start | bytes 7077892

commit v5 on v4

--- a/solution.py
+++ b/solution.py
@@ -400,10 +400,6 @@
     grad_out[...] = grads[inner:, :]
 
 
-def after(value, *others):
-    return lax.optimization_barrier((value,) + others)[0]
-
-
 def run(kernel, outs, args, scratch=(), micros=1.0, limit=16):
     smem = pl.BlockSpec(memory_space=pltpu.SMEM)
     vmem = pl.BlockSpec(memory_space=pltpu.VMEM)
@@ -494,18 +490,6 @@
 
         out_x, out_c = tensor_swap(w_out, 2), tensor_swap(w_out, 1)
         up_b, down_b = tensor_swap(up_a, 1), tensor_swap(down_a, 1)
-        normed, query, key, value, probs, head_out = run(
-            functools.partial(attend_kernel, images),
-            [((rows, width), BF16)]
-            + [((rows, inner), BF16)] * 3
-            + [((heads, rows, rows), BF16), ((rows, inner), BF16)],
-            [tokens, ln1_gain, ln1_bias, weight],
-            micros=4,
-        )
-        head_out, out_x, out_c, up_b, down_b = lax.optimization_barrier(
-            (head_out, out_x, out_c, up_b, down_b)
-        )
-        head_x, head_c = tensor_swap(head_out, 2), tensor_swap(head_out, 1)
         quarter = cap // 2
         cot_shapes = [(quarter if small_slice and k > 1 else cap, width) for k in range(experts)]
         table, part, router, *cot_blocks = run(
@@ -513,20 +497,40 @@
             [((experts, cap, rows), BF16), ((experts, quarter, rows), BF16)]
             + [((LANES, width), BF16)]
             + [(shape, BF16) for shape in cot_shapes],
-            [ids, after(routes.T, head_out), cotangent, w_router.T],
+            [ids, routes.T, cotangent, w_router.T],
             micros=2,
         )
-        head_x = after(head_x, table)
-        if small_slice:
-            d_rows_in = cot_blocks[:2] + [expert_swap(cot_blocks[k], k) for k in (2, 3)]
+        tokens_first, table, part = lax.optimization_barrier((tokens, table, part))
+        normed, query, key, value, probs, head_out = run(
+            functools.partial(attend_kernel, images),
+            [((rows, width), BF16)]
+            + [((rows, inner), BF16)] * 3
+            + [((heads, rows, rows), BF16), ((rows, inner), BF16)],
+            [tokens_first, ln1_gain, ln1_bias, weight],
+            micros=4,
+        )
+        if small_slice:
+            cot_blocks[3] = expert_swap(cot_blocks[3], 3)
+        head_out, out_x, out_c, up_b, down_b, cot_blocks[-1] = lax.optimization_barrier(
+            (head_out, out_x, out_c, up_b, down_b, cot_blocks[-1])
+        )
+        head_x, head_c = tensor_swap(head_out, 2), tensor_swap(head_out, 1)
+        if small_slice:
+            cot_blocks[2] = expert_swap(cot_blocks[2], 2)
+            d_rows_in = cot_blocks
         else:
             d_rows_in = exchange(cot_blocks)
         out_all = [w_out, out_c, out_x, tensor_swap(out_x, 1)]
         heads_all = [head_out, head_c, head_x, tensor_swap(head_x, 1)]
+        spots = table
+        if small_slice:
+            spots, d_rows_in[2], d_rows_in[3] = lax.optimization_barrier(
+                (table, d_rows_in[2], d_rows_in[3])
+            )
         middle, *row_blocks = run(
             functools.partial(middle_kernel, n_tensor, experts),
             [((rows, width), F32)] + [((cap, width), BF16)] * experts,
-            [ids, tokens, ln2_gain, ln2_bias, table] + heads_all + out_all,
+            [ids, tokens, ln2_gain, ln2_bias, spots] + heads_all + out_all,
             scratch=[
                 ((n_tensor, rows, inner), BF16),
                 ((n_tensor, inner, width), BF16),
@@ -535,10 +539,9 @@
             micros=3,
         )
         if small_slice:
-            *row_blocks, far_2, far_3 = lax.optimization_barrier((*row_blocks, *d_rows_in[2:]))
-            d_rows_in[2:] = [far_2, far_3]
-            d_rows_in[1] = expert_swap(after(d_rows_in[1], middle), 1)
-            pair_out = tensor_swap(jnp.stack([far_2, far_3]), 2)
+            pair_out = jnp.stack(d_rows_in[2:])
+            d_rows_in[1], middle = lax.optimization_barrier((d_rows_in[1], middle))
+            d_rows_in[1] = expert_swap(d_rows_in[1], 1)
         else:
             pair_out = router
         rows_in = exchange(list(row_blocks))
@@ -547,6 +550,9 @@
         worked = []
         d_back, gated = [], []
         for number, call in enumerate(calls):
+            if number == 1:
+                router, pair_out, d_back[1] = lax.optimization_barrier((router, pair_out, d_back[1]))
+                pair_out = tensor_swap(pair_out, 2)
             count = cap * len(call)
             last = number == len(calls) - 1
             grads = [] if last else [((2 * width, hidden_width), BF16)] * 2
@@ -559,7 +565,7 @@
                 + [((part_rows, width), F32)]
                 + grads,
                 [ids, up_a, up_b, down_a, down_b]
-                + [after(router, worked[-1][6]) if worked else router]
+                + [router]
                 + [pair_out if worked or not small_slice else router]
                 + [rows_in[k] for k in call]
                 + [d_rows_in[k] for k in call],
@@ -580,7 +586,11 @@
                 micros=2,
             )
 
-        d_home = exchange(d_back)
+        if small_slice:
+            home = {k: expert_swap(d_back[k], k) for k in (3, 2, 1)}
+            d_home = [d_back[0]] + [home[k] for k in (1, 2, 3)]
+        else:
+            d_home = exchange(d_back)
 
         grad_own, grad_pair = run(
             weight_grad_kernel,
@@ -614,8 +624,11 @@
         kept, sent = combine(list(d_home), [one[6] for one in worked])
         chip = (kept.astype(F32) + tensor_swap(sent, 1).astype(F32)).astype(BF16)
         own = (chip.astype(F32) + tensor_swap(chip, 2).astype(F32)).astype(BF16)
-        gated_home = exchange(list(gated_blocks))
         came_first = dp_swap(sent_first)
+        if small_slice:
+            gated_home = [gated_blocks[0]] + [expert_swap(gated_blocks[k], k) for k in (1, 2)]
+        else:
+            gated_home = exchange(list(gated_blocks))
         own, came_first, *gated_home = lax.optimization_barrier((own, came_first, *gated_home))
         other = tensor_swap(own, 1)
 
@@ -634,7 +647,10 @@
             micros=6,
         )
 
-        *gated_home, _ = lax.optimization_barrier((*gated_home, d_middle))
+        if small_slice:
+            last_block, d_middle = lax.optimization_barrier((gated_blocks[3], d_middle))
+            gated_home = list(gated_home) + [expert_swap(last_block, 3)]
+        *gated_home, d_middle = lax.optimization_barrier((*gated_home, d_middle))
         kept_y, sent_y = combine(list(gated_home), [])
 
         chip1 = (kept1.astype(F32) + tensor_swap(sent1, 1).astype(F32)).astype(BF16)
@@ -646,7 +662,9 @@
             (summed,) = run(
                 functools.partial(sum_kernel, 4), [((size, width), BF16)], arrived, micros=0.5
             )
-            sent_rest, own1 = lax.optimization_barrier((sent_rest, own1, summed))[:2]
+            sent_rest, own1, summed = lax.optimization_barrier((sent_rest, own1, summed))
+            came_rest = dp_swap(sent_rest)
+            summed_came = expert_swap(summed, 2)
         other1 = tensor_swap(own1, 1)
         grad_tokens, small = run(
             last_norm_kernel,
@@ -658,10 +676,11 @@
         chip_y = (kept_y.astype(F32) + tensor_swap(sent_y, 1).astype(F32)).astype(BF16)
         own_y = (chip_y.astype(F32) + tensor_swap(chip_y, 2).astype(F32)).astype(BF16)
         if small_slice:
+            summed, came_rest = lax.optimization_barrier((summed, came_rest))
             (ready,) = run(
                 pair_kernel,
                 [((size + small_rows, width), BF16)],
-                [summed, expert_swap(summed, 2), small, expert_swap(small, 2)],
+                [summed, summed_came, small, expert_swap(small, 2)],
                 micros=1,
             )
             own_y, ready = lax.optimization_barrier((own_y, ready))
@@ -679,12 +698,13 @@
             grads = lax.psum(grad_blocks[0], ("expert", "dp")).astype(F32)
             grad_qkv, grad_out = grads[: 3 * inner], grads[3 * inner :]
             small_sum = lax.psum(small, ("expert", "dp"))
+            came_rest = dp_swap(sent_rest)
             sums, grad_router = list(small_sum[:4]), small_sum[8 : 8 + experts]
 
         grad_up, grad_down = run(
             join_grad_kernel,
             [((half, hidden_width), F32), ((hidden_width, half), F32)],
-            [grad_kept, came_first, dp_swap(sent_rest)],
+            [grad_kept, came_first, came_rest],
             scratch=[((width, width), BF16)],
             micros=2,
         )

time: 190 us -> 189 us (level)
  Pallas kernels: 38 us -> 42.8 us
  waiting for transfers between devices: 92.6 us -> 88.7 us
    ppermute x6, waiting for transfers between devices: 36 us -> 21.2 us  [quarter_swap(): return lax.ppermute(value, ('expert', 'dp'), pairs)]
    ppermute x2, waiting for transfers between devices: 0.01 us -> 8.03 us  [dp_swap(): return lax.ppermute(value, 'dp', [(i, i ^ 1) for i in range(n_dp)])]
    pallas_call x16, Pallas kernels: 38 us -> 42.8 us  [run(): pl.pallas_call(kernel, out_shape=[jax.ShapeDtypeStruct(shape, kind) for s...]
    ppermute x20, starting transfers between devices: 12.7 us -> 9.29 us  [tensor_swap(): lax.ppermute(value, 'tensor', [(i, i ^ mask) for i in range(n_tensor)])]
    ppermute x20, waiting for transfers between devices: 16.2 us -> 19.6 us  [tensor_swap(): lax.ppermute(value, 'tensor', [(i, i ^ mask) for i in range(n_tensor)])]
    ppermute x14, starting transfers between devices: 25.7 us -> 29 us  [expert_swap(): lax.ppermute(value, 'expert', [(i, i ^ mask) for i in range(n_expert)])]
  transfers between devices with their start and end apart: 42 -> 42, of which waited for: 20 -> 24; matrix products, arithmetic and copies ran while one was open for 2% -> 2% of each run, Pallas kernels for 12% -> 12%
where the time goes in v5:
time: 189 us; the launch traced here: 188 us
  waiting for transfers between devices  88.7 us (47%)
  starting transfers between devices  47.4 us (25%)
  Pallas kernels  42.8 us (23%)
  local copies, waits for them, and re-layouts  4.39 us (2%)
  other arithmetic  3.3 us (2%)
    pallas_call x16, Pallas kernels, run(): pl.pallas_call(kernel, out_shape=[jax.ShapeDtypeStruct(shape, kind) for s...  42.8 us
    ppermute x14, waiting for transfers between devices, expert_swap(): lax.ppermute(value, 'expert', [(i, i ^ mask) for i in range(n_expert)])  40 us
    ppermute x14, starting transfers between devices, expert_swap(): lax.ppermute(value, 'expert', [(i, i ^ mask) for i in range(n_expert)])  29 us
    ppermute x6, waiting for transfers between devices, quarter_swap(): return lax.ppermute(value, ('expert', 'dp'), pairs)  21.2 us
    ppermute x20, waiting for transfers between devices, tensor_swap(): lax.ppermute(value, 'tensor', [(i, i ^ mask) for i in range(n_tensor)])  19.6 us
    ppermute x20, starting transfers between devices, tensor_swap(): lax.ppermute(value, 'tensor', [(i, i ^ mask) for i in range(n_tensor)])  9.29 us
    ppermute x2, waiting for transfers between devices, dp_swap(): return lax.ppermute(value, 'dp', [(i, i ^ 1) for i in range(n_dp)])  8.03 us
    ppermute x6, starting transfers between devices, quarter_swap(): return lax.ppermute(value, ('expert', 'dp'), pairs)  6.99 us
  transfers between devices with their start and end apart: 42, of which 24 were waited for; matrix products, arithmetic and copies ran while one was open for 2% of the time, Pallas kernels for 12%

profile of v5, /device:TPU:0, one launch (start us, length us, event | category | flops | bytes accessed | tf_op | source)
XLA Modules:
  0.0 188.2 jit_solution(1656588457061456968)
XLA Ops:
  1.2 2.9 %collective-permute-start.1 = (bf16[192,768]{1,0:T(8,128)(2,1)}, bf16[192,768]{1,0:T(8,128)(2,1)S(1)}, u32[]{:S(2)}, u32[]{:S(2)}) collective-permute-start(bf16[192,768]{1,0:T(8,128)(2,1)} %w_out.1), channel_id=1, source_target_pairs={{0,16},{8,24},{16,0},{24,8},{1,17},{9,25},{17,1},{25,9},{2,18},{10... | collective-permute-start | bytes 884744 | tf_op jit(solution)/shard_map/ppermute | solution.py:423
  4.9 1.1 copy-done.7
  6.0 0.7 copy-done.12
  6.7 0.7 copy-done.13
  7.4 1.4 shard_map.212
  8.8 3.7 %collective-permute-start.5 = (bf16[72,768]{1,0:T(8,128)(2,1)S(1)}, bf16[72,768]{1,0:T(8,128)(2,1)S(1)}, u32[]{:S(2)}, u32[]{:S(2)}) collective-permute-start(bf16[72,768]{1,0:T(8,128)(2,1)S(1)} %get-tuple-element.131), channel_id=1, source_target_pairs={{0,6},{2,4},{4,2},{6,0},{1,7},{3,5},{5,3},{7,1},{8,14},{10,12},{12... | collective-permute-start | bytes 331784 | tf_op jit(solution)/shard_map/ppermute | solution.py:426
  12.5 2.5 %shard_map.213 = (bf16[394,768]{1,0:T(8,128)(2,1)S(1)}, bf16[394,192]{1,0:T(8,128)(2,1)S(1)}, bf16[394,192]{1,0:T(8,128)(2,1)S(1)}, bf16[394,192]{1,0:T(8,128)(2...) custom-call(bf16[394,768]{1,0:T(8,128)(2,1)S(1)} %copy-done, f32[768]{0:T(1024)S(1)} %copy-done.1, ...), custom_call_target="tpu_custom_call" | custom-call | flops 4600000000 | bytes 1024 | tf_op jit(solution)/shard_map/pallas_call | solution.py:406
  15.0 1.3 collective-permute-done.5.refs_3_
  16.3 1.0 copy-done.4
  18.3 5.7 %collective-permute-done.7.rest_2_ = bf16[394,192]{1,0:T(8,128)(2,1)S(1)} collective-permute-done((bf16[394,192]{1,0:T(8,128)(2,1)S(1)}, bf16[394,192]{1,0:T(8,128)(2,1)S(1)}, u32[]{:S(2)}, u32[]{:S(2)}) %collective-permute-start.7) | collective-permute-done | bytes 151328 | tf_op jit(solution)/shard_map/ppermute | solution.py:423
  24.0 2.1 %collective-permute-start = (bf16[72,768]{1,0:T(8,128)(2,1)S(1)}, bf16[72,768]{1,0:T(8,128)(2,1)S(1)}, u32[]{:S(2)}, u32[]{:S(2)}) collective-permute-start(bf16[72,768]{1,0:T(8,128)(2,1)S(1)} %get-tuple-element.128), channel_id=1, source_target_pairs={{0,4},{2,6},{4,0},{6,2},{1,5},{3,7},{5,1},{7,3},{8,12},{10,14},{12... | collective-permute-start | bytes 331784 | tf_op jit(solution)/shard_map/ppermute | solution.py:426
  26.1 6.6 %collective-permute-done.refs_2_ = bf16[72,768]{1,0:T(8,128)(2,1)S(1)} collective-permute-done((bf16[72,768]{1,0:T(8,128)(2,1)S(1)}, bf16[72,768]{1,0:T(8,128)(2,1)S(1)}, u32[]{:S(2)}, u32[]{:S(2)}) %collective-permute-start) | collective-permute-done | bytes 110624 | tf_op jit(solution)/shard_map/ppermute | solution.py:426
  32.8 2.8 %shard_map.214 = (f32[394,768]{1,0:T(8,128)S(1)}, bf16[144,768]{1,0:T(8,128)(2,1)S(1)}, bf16[144,768]{1,0:T(8,128)(2,1)S(1)}, bf16[144,768]{1,0:T(8,128)(2,1)S(1)}, bf16[144,768]{1,0:T(8,128)(2,1)S(1)}) custom-call(s32[8]{0:T(128)S(1)} %stack.38.ids, bf16[394,768]{1,0:T(8,128)(2,1)S(1)} %copy-done, f32[768]{0:T(1024)S(1)} %copy-done.16, f32[768]{0:T(1024)S(1)} %copy-done.15, ...), custom_call_target="tpu_custom_call" | custom-call | flops 3449999872 | bytes 1024 | tf_op jit(solution)/shard_map/pallas_call | solution.py:406
  35.8 1.9 %collective-permute-start.11 = (bf16[144,768]{1,0:T(8,128)(2,1)S(1)}, bf16[144,768]{1,0:T(8,128)(2,1)S(1)}, u32[]{:S(2)}, u32[]{:S(2)}) collective-permute-start(bf16[144,768]{1,0:T(8,128)(2,1)S(1)} %get-tuple-element.146), channel_id=1, source_target_pairs={{0,2},{2,0},{4,6},{6,4},{1,3},{3,1},{5,7},{7,5},{8,10},{10,8},{12,... | collective-permute-start | bytes 663560 | tf_op jit(solution)/shard_map/ppermute | solution.py:426
  37.7 1.6 collective-permute-start.14
  39.3 1.5 collective-permute-start.15
  40.8 8.0 %collective-permute-done.10.refs_1_ = bf16[144,768]{1,0:T(8,128)(2,1)S(1)} collective-permute-done((bf16[144,768]{1,0:T(8,128)(2,1)S(1)}, bf16[144,768]{1,0:T(8,128)(2,1)S(1)}, u32[]{:S(2)}, u32[]{:S(2)}) %collective-permute-start.10) | collective-permute-done | bytes 221216 | tf_op jit(solution)/shard_map/ppermute | solution.py:426
  48.7 3.4 %collective-permute-done.11.refs_3_ = bf16[144,768]{1,0:T(8,128)(2,1)S(1)} collective-permute-done((bf16[144,768]{1,0:T(8,128)(2,1)S(1)}, bf16[144,768]{1,0:T(8,128)(2,1)S(1)}, u32[]{:S(2)}, u32[]{:S(2)}) %collective-permute-start.11) | collective-permute-done | bytes 221216 | tf_op jit(solution)/shard_map/ppermute | solution.py:426
  52.1 7.8 %shard_map.215 = (bf16[144,768]{1,0:T(8,128)(2,1)S(1)}, bf16[144,768]{1,0:T(8,128)(2,1)S(1)}, bf16[2,144,768]{2,1,0:T(8,128)(2,1)S(1)}, bf16[2,144,768]{2,1,0:T(...) custom-call(s32[8]{0:T(128)S(1)} %stack.38.ids, ...), custom_call_target="tpu_custom_call" | custom-call | flops 8049999872 | bytes 1024 | tf_op jit(solution)/shard_map/pallas_call | solution.py:406
  59.9 0.7 collective-permute-start.13
  60.7 5.4 %collective-permute-done.13.pair_out = bf16[2,72,768]{2,1,0:T(8,128)(2,1)S(1)} collective-permute-done((bf16[2,72,768]{2,1,0:T(8,128)(2,1)S(1)}, bf16[2,72,768]{2,1,0:T(8,128)(2,1)S(1)}, u32[]{:S(2)}, u32[]{:S(2)}) %collective-permute-start.13) | collective-permute-done | bytes 221216 | tf_op jit(solution)/shard_map/ppermute | solution.py:423
  66.1 5.6 %shard_map.216 = (bf16[144,768]{1,0:T(8,128)(2,1)S(1)}, bf16[144,768]{1,0:T(8,128)(2,1)S(1)}, bf16[2,72,768]{2,1,0:T(8,128)(2,1)S(1)}, bf16[2,72,768]{2,1,0:T(8,...) custom-call(s32[8]{0:T(128)S(1)} %stack.38.ids, ...), custom_call_target="tpu_custom_call" | custom-call | flops 8049999872 | bytes 1024 | tf_op jit(solution)/shard_map/pallas_call | solution.py:406
  71.7 2.6 %shard_map.218 = (bf16[1536,768]{1,0:T(8,128)(2,1)S(1)}, bf16[1536,768]{1,0:T(8,128)(2,1)S(1)}) custom-call(bf16[288,768]{1,0:T(8,128)(2,1)S(1)} %get-tuple-element.163.refs_0_, bf16[288,768]{1,0:T(8,128)(2,1)S(1)} %get-tuple-element.164.refs_1_, bf16[288,768]{1,0:T(8,128)(2,1)S(1)} %get-tuple-element.165.refs_2_, ...), custom_call_target="tpu_custom_call" | custom-call | flops 4600000000 | bytes 1024 | tf_op jit(solution)/shard_map/pallas_call | solution.py:406
  74.5 0.7 collective-permute-start.18
  75.2 8.4 %collective-permute-start.16 = (bf16[144,768]{1,0:T(8,128)(2,1)S(1)}, bf16[144,768]{1,0:T(8,128)(2,1)S(1)}, u32[]{:S(2)}, u32[]{:S(2)}) collective-permute-start(bf16[144,768]{1,0:T(8,128)(2,1)S(1)} %get-tuple-element.156), channel_id=1, source_target_pairs={{0,4},{2,6},{4,0},{6,2},{1,5},{3,7},{5,1},{7,3},{8,12},{10,14},{12... | collective-permute-start | bytes 663560 | tf_op jit(solution)/shard_map/ppermute | solution.py:426
  83.7 2.5 %shard_map.219 = (f32[768,768]{1,0:T(8,128)S(1)}, bf16[256,768]{1,0:T(8,128)(2,1)S(1)}, bf16[512,768]{1,0:T(8,128)(2,1)}) custom-call(s32[8]{0:T(128)S(1)} %stack.38.ids, bf16[1536,768]{1,0:T(8,128)(2,1)S(1)} %get-tuple-element.171.own, bf16[1536,768]{1,0:T(8,128)(2,1)S(1)} %collective-permute-done.19.came), custom_call_target="tpu_custom_call" | custom-call | flops 2300000000 | bytes 1024 | tf_op jit(solution)/shard_map/pallas_call | solution.py:406
  86.2 13.1 %collective-permute-done.16.refs_2_ = bf16[144,768]{1,0:T(8,128)(2,1)S(1)} collective-permute-done((bf16[144,768]{1,0:T(8,128)(2,1)S(1)}, bf16[144,768]{1,0:T(8,128)(2,1)S(1)}, u32[]{:S(2)}, u32[]{:S(2)}) %collective-permute-start.16) | collective-permute-done | bytes 221216 | tf_op jit(solution)/shard_map/ppermute | solution.py:426
  99.3 1.5 shard_map.220
  100.9 1.6 collective-permute-done.20
  102.6 1.5 collective-permute-start.21
  104.1 1.5 collective-permute-start.22
  105.7 4.5 %collective-permute-start.23 = (bf16[144,768]{1,0:T(8,128)(2,1)S(1)}, bf16[144,768]{1,0:T(8,128)(2,1)S(1)}, u32[]{:S(2)}, u32[]{:S(2)}) collective-permute-start(bf16[144,768]{1,0:T(8,128)(2,1)S(1)} %get-tuple-element.184), channel_id=1, source_target_pairs={{0,2},{2,0},{4,6},{6,4},{1,3},{3,1},{5,7},{7,5},{8,10},{10,8},{12,... | collective-permute-start | bytes 663560 | tf_op jit(solution)/shard_map/ppermute | solution.py:426
  110.2 0.9 collective-permute-start.24
  111.1 1.1 collective-permute-done.21
  112.3 4.7 %collective-permute-done.24.refs_2_ = bf16[72,768]{1,0:T(8,128)(2,1)S(1)} collective-permute-done((bf16[72,768]{1,0:T(8,128)(2,1)S(1)}, bf16[72,768]{1,0:T(8,128)(2,1)S(1)}, u32[]{:S(2)}, u32[]{:S(2)}) %collective-permute-start.24) | collective-permute-done | bytes 110624 | tf_op jit(solution)/shard_map/ppermute | solution.py:426
  117.0 0.7 collective-permute-done.23.refs_1_
  117.7 0.7 copy-done.9
  118.5 1.6 collective-permute-done.25.other
  120.1 4.9 %shard_map.221 = (f32[394,768]{1,0:T(8,128)S(1)}, bf16[394,384]{1,0:T(8,128)(2,1)S(1)}, bf16[394,384]{1,0:T(8,128)(2,1)S(1)}, f32[16,768]{1,0:T(8,128)S(1)}, bf1...) custom-call(s32[8]{0:T(128)S(1)} %stack.38.ids, ...), custom_call_target="tpu_custom_call" | custom-call | flops 6899999744 | bytes 1024 | tf_op jit(solution)/shard_map/pallas_call | solution.py:406
  125.2 2.4 %collective-permute-start.26 = (bf16[72,768]{1,0:T(8,128)(2,1)S(1)}, bf16[72,768]{1,0:T(8,128)(2,1)S(1)}, u32[]{:S(2)}, u32[]{:S(2)}) collective-permute-start(bf16[72,768]{1,0:T(8,128)(2,1)S(1)} %get-tuple-element.198), channel_id=1, source_target_pairs={{0,6},{2,4},{4,2},{6,0},{1,7},{3,5},{5,3},{7,1},{8,14},{10,12},{12... | collective-permute-start | bytes 331784 | tf_op jit(solution)/shard_map/ppermute | solution.py:426
  127.6 1.9 collective-permute-start.31
  130.0 1.1 collective-permute-start.33
  131.8 1.1 collective-permute-done.26.refs_3_
  132.9 1.5 shard_map.222
  134.5 4.3 %collective-permute-done.31.refs_1_ = bf16[192,768]{1,0:T(8,128)(2,1)S(1)} collective-permute-done((bf16[192,768]{1,0:T(8,128)(2,1)S(1)}, bf16[192,768]{1,0:T(8,128)(2,1)S(1)}, u32[]{:S(2)}, u32[]{:S(2)}) %collective-permute-start.31) | collective-permute-done | bytes 294944 | tf_op jit(solution)/shard_map/ppermute | solution.py:433
  138.8 5.6 %collective-permute-done.32.refs_2_ = bf16[192,768]{1,0:T(8,128)(2,1)S(1)} collective-permute-done((bf16[192,768]{1,0:T(8,128)(2,1)S(1)}, bf16[192,768]{1,0:T(8,128)(2,1)S(1)}, u32[]{:S(2)}, u32[]{:S(2)}) %collective-permute-start.32) | collective-permute-done | bytes 294944 | tf_op jit(solution)/shard_map/ppermute | solution.py:433
  145.0 0.9 shard_map.223.own
  146.6 0.8 add_convert_fusion.5
  148.5 1.2 collective-permute-done.36.other
  149.7 2.8 %shard_map.224 = (bf16[394,768]{1,0:T(8,128)(2,1)}, f32[16,768]{1,0:T(8,128)S(1)}) custom-call(s32[8]{0:T(128)S(1)} %stack.38.ids, bf16[394,384]{1,0:T(8,128)(2,1)S(1)} %add_convert_fusion.2.own, bf16[394,384]{1,0:T(8,128)(2,1)} %collective-permute-done.36.other, bf16[394,768]{1,0:T(8,128)(2,1)S(1)} %copy-done, f32[394,768]{1,0:T(8,128)S(1)} %get-tuple-element.219.d_middle, ...), custom_call_target="tpu_custom_call" | custom-call | flops 11500000 | bytes 1024 | tf_op jit(solution)/shard_map/pallas_call | solution.py:406
  152.5 1.2 collective-permute-start.37
  153.7 3.0 %collective-permute-done.28 = bf16[400,384]{1,0:T(8,128)(2,1)} collective-permute-done((bf16[400,384]{1,0:T(8,128)(2,1)}, bf16[400,384]{1,0:T(8,128)(2,1)}, u32[]{:S(2)}, u32[]{:S(2)}) %collective-permute-start.28) | collective-permute-done | bytes 307232 | tf_op jit(solution)/shard_map/ppermute | solution.py:423
  156.7 1.1 add_convert_fusion.4
  157.8 8.0 %collective-permute-done.34.came_rest = bf16[512,768]{1,0:T(8,128)(2,1)} collective-permute-done((bf16[512,768]{1,0:T(8,128)(2,1)}, bf16[512,768]{1,0:T(8,128)(2,1)}, u32[]{:S(2)}, u32[]{:S(2)}) %collective-permute-start.34) | collective-permute-done | bytes 786464 | tf_op jit(solution)/shard_map/ppermute | solution.py:429
  166.0 0.9 collective-permute-done.37.small_came
  166.9 1.1 shard_map.225.refs_0_
  168.2 1.5 collective-permute-start.39
  169.6 2.0 %collective-permute-start.41 = (bf16[208,768]{1,0:T(8,128)(2,1)S(1)}, bf16[208,768]{1,0:T(8,128)(2,1)S(1)}, u32[]{:S(2)}, u32[]{:S(2)}) collective-permute-start(bf16[208,768]{1,0:T(8,128)(2,1)S(1)} %shard_map.225.refs_0_), channel_id=1, source_target_pairs={{0,3},{1,2},{2,1},{3,0},{4,7},{5,6},{6,5},{7,4},{8,11},{9,10},{10,... | collective-permute-start | bytes 958472 | tf_op jit(solution)/shard_map/ppermute | solution.py:433
  171.7 2.8 %shard_map.227 = (f32[384,768]{1,0:T(8,128)}, f32[768,384]{1,0:T(8,128)}) custom-call(f32[768,768]{1,0:T(8,128)S(1)} %copy-done.18, bf16[256,768]{1,0:T(8,128)(2,1)S(1)} %copy-done.10, bf16[512,768]{1,0:T(8,128)(2,1)} %collective-permute-done.34.came_rest), custom_call_target="tpu_custom_call" | custom-call | flops 2300000000 | bytes 1024 | tf_op jit(solution)/shard_map/pallas_call | solution.py:406
  174.5 1.0 select_convert_fusion
  175.5 2.6 %collective-permute-done.39.refs_1_ = bf16[208,768]{1,0:T(8,128)(2,1)S(1)} collective-permute-done((bf16[208,768]{1,0:T(8,128)(2,1)S(1)}, bf16[208,768]{1,0:T(8,128)(2,1)S(1)}, u32[]{:S(2)}, u32[]{:S(2)}) %collective-permute-start.39) | collective-permute-done | bytes 319520 | tf_op jit(solution)/shard_map/ppermute | solution.py:433
  178.0 2.0 %collective-permute-done.40.refs_2_ = bf16[208,768]{1,0:T(8,128)(2,1)S(1)} collective-permute-done((bf16[208,768]{1,0:T(8,128)(2,1)S(1)}, bf16[208,768]{1,0:T(8,128)(2,1)S(1)}, u32[]{:S(2)}, u32[]{:S(2)}) %collective-permute-start.40) | collective-permute-done | bytes 319520 | tf_op jit(solution)/shard_map/ppermute | solution.py:433
  180.0 6.0 %collective-permute-done.41.refs_3_ = bf16[208,768]{1,0:T(8,128)(2,1)S(1)} collective-permute-done((bf16[208,768]{1,0:T(8,128)(2,1)S(1)}, bf16[208,768]{1,0:T(8,128)(2,1)S(1)}, u32[]{:S(2)}, u32[]{:S(2)}) %collective-permute-start.41) | collective-permute-done | bytes 319520 | tf_op jit(solution)/shard_map/ppermute | solution.py:433
  186.1 2.2 %shard_map.226 = (f32[576,768]{1,0:T(8,128)}, f32[192,768]{1,0:T(8,128)}, f32[768]{0:T(1024)}, f32[768]{0:T(1024)}, f32[768]{0:T(1024)}, /*index=5*/f32[768]{0:T(1024)}, f32[4,768]{1,0:T(4,128)}) custom-call(s32[8]{0:T(128)S(1)} %stack.38.ids, bf16[208,768]{1,0:T(8,128)(2,1)S(1)} %shard_map.225.refs_0_, ...), custom_call_target="tpu_custom_call" | custom-call | flops 3449999872 | bytes 1024 | tf_op jit(solution)/shard_map/pallas_call | solution.py:406
  (85 shorter events, 6.7 us)
Async XLA Ops:
  0.6 15.6 %collective-permute-start.3 = (bf16[768,768]{1,0:T(8,128)(2,1)}, bf16[768,768]{1,0:T(8,128)(2,1)S(1)}, u32[]{:S(2)}, u32[]{:S(2)}) collective-permute-start(bf16[768,768]{1,0:T(8,128)(2,1)} %bitcast.28), channel_id=1, source_target_pairs={{0,8},{8,0},{16,24},{24,16},{1,9},{9,1},{17,25},{25,17},{2,10},{10... | collective-permute-start | bytes 3538952 | tf_op jit(solution)/shard_map/ppermute | solution.py:423
  1.2 16.1 %collective-permute-start.4 = (bf16[768,768]{1,0:T(8,128)(2,1)}, bf16[768,768]{1,0:T(8,128)(2,1)}, u32[]{:S(2)}, u32[]{:S(2)}) collective-permute-start(bf16[768,768]{1,0:T(8,128)(2,1)} %bitcast.31), channel_id=1, source_target_pairs={{0,8},{8,0},{16,24},{24,16},{1,9},{9,1},{17,25},{25,17},{2,10},{10... | collective-permute-start | bytes 3538952 | tf_op jit(solution)/shard_map/ppermute | solution.py:423
  1.2 15.0 %collective-permute-start.1 = (bf16[192,768]{1,0:T(8,128)(2,1)}, bf16[192,768]{1,0:T(8,128)(2,1)S(1)}, u32[]{:S(2)}, u32[]{:S(2)}) collective-permute-start(bf16[192,768]{1,0:T(8,128)(2,1)} %w_out.1), channel_id=1, source_target_pairs={{0,16},{8,24},{16,0},{24,8},{1,17},{9,25},{17,1},{25,9},{2,18},{10... | collective-permute-start | bytes 884744 | tf_op jit(solution)/shard_map/ppermute | solution.py:423
  4.2 12.1 %collective-permute-start.2 = (bf16[192,768]{1,0:T(8,128)(2,1)}, bf16[192,768]{1,0:T(8,128)(2,1)S(1)}, u32[]{:S(2)}, u32[]{:S(2)}) collective-permute-start(bf16[192,768]{1,0:T(8,128)(2,1)} %w_out.1), channel_id=1, source_target_pairs={{0,8},{8,0},{16,24},{24,16},{1,9},{9,1},{17,25},{25,17},{2,10},{10... | collective-permute-start | bytes 884744 | tf_op jit(solution)/shard_map/ppermute | solution.py:423
  4.9 1.1 copy-start.7
  6.0 0.7 copy-start.12
  6.7 0.7 copy-start.13
  7.4 5.1 %copy-start = (bf16[394,768]{1,0:T(8,128)(2,1)S(1)}, bf16[394,768]{1,0:T(8,128)(2,1)}, u32[]{:S(2)}) copy-start(bf16[394,768]{1,0:T(8,128)(2,1)} %tokens.4) | copy-start | bytes 1815556
  7.4 5.1 %copy-start.1 = (f32[768]{0:T(1024)S(1)}, f32[768]{0:T(1024)}, u32[]{:S(2)}) copy-start(f32[768]{0:T(1024)} %gain.7) | copy-start | bytes 9220
  7.4 5.1 %copy-start.6 = (bf16[768,3,192]{0,2,1:T(8,128)(2,1)S(1)}, bf16[768,3,192]{0,2,1:T(8,128)(2,1)}, u32[]{:S(2)}) copy-start(bf16[768,3,192]{0,2,1:T(8,128)(2,1)} %param.18) | copy-start | bytes 2654212
  7.4 5.1 %copy-start.14 = (f32[768]{0:T(1024)S(1)}, f32[768]{0:T(1024)}, u32[]{:S(2)}) copy-start(f32[768]{0:T(1024)} %bias.2) | copy-start | bytes 9220
  8.8 7.5 %collective-permute-start.5 = (bf16[72,768]{1,0:T(8,128)(2,1)S(1)}, bf16[72,768]{1,0:T(8,128)(2,1)S(1)}, u32[]{:S(2)}, u32[]{:S(2)}) collective-permute-start(bf16[72,768]{1,0:T(8,128)(2,1)S(1)} %get-tuple-element.131), channel_id=1, source_target_pairs={{0,6},{2,4},{4,2},{6,0},{1,7},{3,5},{5,3},{7,1},{8,14},{10,12},{12... | collective-permute-start | bytes 331784 | tf_op jit(solution)/shard_map/ppermute | solution.py:426
  12.4 20.3 %copy-start.11 = (bf16[192,768]{1,0:T(8,128)(2,1)S(1)}, bf16[192,768]{1,0:T(8,128)(2,1)}, u32[]{:S(2)}) copy-start(bf16[192,768]{1,0:T(8,128)(2,1)} %w_out.1) | copy-start | bytes 884740
  12.5 20.3 %copy-start.15 = (f32[768]{0:T(1024)S(1)}, f32[768]{0:T(1024)}, u32[]{:S(2)}) copy-start(f32[768]{0:T(1024)} %bias.3) | copy-start | bytes 9220
  12.5 20.3 %copy-start.16 = (f32[768]{0:T(1024)S(1)}, f32[768]{0:T(1024)}, u32[]{:S(2)}) copy-start(f32[768]{0:T(1024)} %gain.6) | copy-start | bytes 9220
  16.3 1.0 copy-start.4
  17.3 6.7 %collective-permute-start.7 = (bf16[394,192]{1,0:T(8,128)(2,1)S(1)}, bf16[394,192]{1,0:T(8,128)(2,1)S(1)}, u32[]{:S(2)}, u32[]{:S(2)}) collective-permute-start(bf16[394,192]{1,0:T(8,128)(2,1)S(1)} %get-tuple-element.134.rest_0_.head_out), channel_id=1, source_target_pairs={{0,16},{8,24},{16,0},{24,8},{1,17},{9,25},{17,1},{25,9},{2,18},{10... | collective-permute-start | bytes 453896 | tf_op jit(solution)/shard_map/ppermute | solution.py:423
  17.8 14.9 %collective-permute-start.9 = (bf16[192,768]{1,0:T(8,128)(2,1)S(1)}, bf16[192,768]{1,0:T(8,128)(2,1)S(1)}, u32[]{:S(2)}, u32[]{:S(2)}) collective-permute-start(bf16[192,768]{1,0:T(8,128)(2,1)S(1)} %collective-permute-done.1.rest_6_), channel_id=1, source_target_pairs={{0,8},{8,0},{16,24},{24,16},{1,9},{9,1},{17,25},{25,17},{2,10},{10... | collective-permute-start | bytes 884744 | tf_op jit(solution)/shard_map/ppermute | solution.py:423
  17.8 14.9 %collective-permute-start.6 = (bf16[394,192]{1,0:T(8,128)(2,1)S(1)}, bf16[394,192]{1,0:T(8,128)(2,1)S(1)}, u32[]{:S(2)}, u32[]{:S(2)}) collective-permute-start(bf16[394,192]{1,0:T(8,128)(2,1)S(1)} %get-tuple-element.134.rest_0_.head_out), channel_id=1, source_target_pairs={{0,8},{8,0},{16,24},{24,16},{1,9},{9,1},{17,25},{25,17},{2,10},{10... | collective-permute-start | bytes 453896 | tf_op jit(solution)/shard_map/ppermute | solution.py:423
  24.0 8.8 %collective-permute-start.8 = (bf16[394,192]{1,0:T(8,128)(2,1)S(1)}, bf16[394,192]{1,0:T(8,128)(2,1)S(1)}, u32[]{:S(2)}, u32[]{:S(2)}) collective-permute-start(bf16[394,192]{1,0:T(8,128)(2,1)S(1)} %collective-permute-done.7.rest_2_), channel_id=1, source_target_pairs={{0,8},{8,0},{16,24},{24,16},{1,9},{9,1},{17,25},{25,17},{2,10},{10... | collective-permute-start | bytes 453896 | tf_op jit(solution)/shard_map/ppermute | solution.py:423
  24.0 28.1 %copy-start.2 = (bf16[1,768,768]{2,1,0:T(8,128)(2,1)S(1)}, bf16[1,768,768]{2,1,0:T(8,128)(2,1)}, u32[]{:S(2)}) copy-start(bf16[1,768,768]{2,1,0:T(8,128)(2,1)} %param.23) | copy-start | bytes 3538948
  24.0 28.1 %copy-start.3 = (bf16[1,768,768]{2,1,0:T(8,128)(2,1)S(1)}, bf16[1,768,768]{2,1,0:T(8,128)(2,1)}, u32[]{:S(2)}) copy-start(bf16[1,768,768]{2,1,0:T(8,128)(2,1)} %param.24) | copy-start | bytes 3538948
  24.0 28.1 %copy-start.5 = (bf16[768,768]{1,0:T(8,128)(2,1)S(1)}, bf16[768,768]{1,0:T(8,128)(2,1)}, u32[]{:S(2)}) copy-start(bf16[768,768]{1,0:T(8,128)(2,1)} %copy-done.4) | copy-start | bytes 3538948
  24.0 8.7 %collective-permute-start = (bf16[72,768]{1,0:T(8,128)(2,1)S(1)}, bf16[72,768]{1,0:T(8,128)(2,1)S(1)}, u32[]{:S(2)}, u32[]{:S(2)}) collective-permute-start(bf16[72,768]{1,0:T(8,128)(2,1)S(1)} %get-tuple-element.128), channel_id=1, source_target_pairs={{0,4},{2,6},{4,0},{6,2},{1,5},{3,7},{5,1},{7,3},{8,12},{10,14},{12... | collective-permute-start | bytes 331784 | tf_op jit(solution)/shard_map/ppermute | solution.py:426
  35.6 13.1 %collective-permute-start.10 = (bf16[144,768]{1,0:T(8,128)(2,1)S(1)}, bf16[144,768]{1,0:T(8,128)(2,1)S(1)}, u32[]{:S(2)}, u32[]{:S(2)}) collective-permute-start(bf16[144,768]{1,0:T(8,128)(2,1)S(1)} %get-tuple-element.144), channel_id=1, source_target_pairs={{0,2},{2,0},{4,6},{6,4},{1,3},{3,1},{5,7},{7,5},{8,10},{10,8},{12,... | collective-permute-start | bytes 663560 | tf_op jit(solution)/shard_map/ppermute | solution.py:426
  35.8 16.3 %collective-permute-start.11 = (bf16[144,768]{1,0:T(8,128)(2,1)S(1)}, bf16[144,768]{1,0:T(8,128)(2,1)S(1)}, u32[]{:S(2)}, u32[]{:S(2)}) collective-permute-start(bf16[144,768]{1,0:T(8,128)(2,1)S(1)} %get-tuple-element.146), channel_id=1, source_target_pairs={{0,2},{2,0},{4,6},{6,4},{1,3},{3,1},{5,7},{7,5},{8,10},{10,8},{12,... | collective-permute-start | bytes 663560 | tf_op jit(solution)/shard_map/ppermute | solution.py:426
  37.7 23.0 %collective-permute-start.14 = (bf16[144,768]{1,0:T(8,128)(2,1)S(1)}, bf16[144,768]{1,0:T(8,128)(2,1)S(1)}, u32[]{:S(2)}, u32[]{:S(2)}) collective-permute-start(bf16[144,768]{1,0:T(8,128)(2,1)S(1)} %get-tuple-element.154), channel_id=1, source_target_pairs={{0,4},{2,6},{4,0},{6,2},{1,5},{3,7},{5,1},{7,3},{8,12},{10,14},{12... | collective-permute-start | bytes 663560 | tf_op jit(solution)/shard_map/ppermute | solution.py:426
  39.3 21.4 %collective-permute-start.15 = (bf16[144,768]{1,0:T(8,128)(2,1)S(1)}, bf16[144,768]{1,0:T(8,128)(2,1)S(1)}, u32[]{:S(2)}, u32[]{:S(2)}) collective-permute-start(bf16[144,768]{1,0:T(8,128)(2,1)S(1)} %get-tuple-element.155), channel_id=1, source_target_pairs={{0,6},{2,4},{4,2},{6,0},{1,7},{3,5},{5,3},{7,1},{8,14},{10,12},{12... | collective-permute-start | bytes 663560 | tf_op jit(solution)/shard_map/ppermute | solution.py:426
  59.9 6.1 %collective-permute-start.13 = (bf16[2,72,768]{2,1,0:T(8,128)(2,1)S(1)}, bf16[2,72,768]{2,1,0:T(8,128)(2,1)S(1)}, u32[]{:S(2)}, u32[]{:S(2)}) collective-permute-start(bf16[2,72,768]{2,1,0:T(8,128)(2,1)S(1)} %pad_maximum_fusion.2), channel_id=1, source_target_pairs={{0,16},{8,24},{16,0},{24,8},{1,17},{9,25},{17,1},{25,9},{2,18},{10... | collective-permute-start | bytes 663560 | tf_op jit(solution)/shard_map/ppermute | solution.py:423
  74.3 9.4 %collective-permute-start.19 = (bf16[1536,768]{1,0:T(8,128)(2,1)S(1)}, bf16[1536,768]{1,0:T(8,128)(2,1)S(1)}, u32[]{:S(2)}, u32[]{:S(2)}) collective-permute-start(bf16[1536,768]{1,0:T(8,128)(2,1)S(1)} %get-tuple-element.172), channel_id=1, source_target_pairs={{0,8},{8,0},{16,24},{24,16},{1,9},{9,1},{17,25},{25,17},{2,10},{10... | collective-permute-start | bytes 7077896 | tf_op jit(solution)/shard_map/ppermute | solution.py:423
  74.4 11.8 %collective-permute-start.12 = (bf16[144,768]{1,0:T(8,128)(2,1)S(1)}, bf16[144,768]{1,0:T(8,128)(2,1)S(1)}, u32[]{:S(2)}, u32[]{:S(2)}) collective-permute-start(bf16[144,768]{1,0:T(8,128)(2,1)S(1)} %get-tuple-element.151), channel_id=1, source_target_pairs={{0,2},{2,0},{4,6},{6,4},{1,3},{3,1},{5,7},{7,5},{8,10},{10,8},{12,... | collective-permute-start | bytes 663560 | tf_op jit(solution)/shard_map/ppermute | solution.py:426
  74.5 9.1 %collective-permute-start.18 = (bf16[2,72,768]{2,1,0:T(8,128)(2,1)S(1)}, bf16[2,72,768]{2,1,0:T(8,128)(2,1)S(1)}, u32[]{:S(2)}, u32[]{:S(2)}) collective-permute-start(bf16[2,72,768]{2,1,0:T(8,128)(2,1)S(1)} %get-tuple-element.160), channel_id=1, source_target_pairs={{0,16},{8,24},{16,0},{24,8},{1,17},{9,25},{17,1},{25,9},{2,18},{10... | collective-permute-start | bytes 663560 | tf_op jit(solution)/shard_map/ppermute | solution.py:423
  75.2 24.1 %collective-permute-start.16 = (bf16[144,768]{1,0:T(8,128)(2,1)S(1)}, bf16[144,768]{1,0:T(8,128)(2,1)S(1)}, u32[]{:S(2)}, u32[]{:S(2)}) collective-permute-start(bf16[144,768]{1,0:T(8,128)(2,1)S(1)} %get-tuple-element.156), channel_id=1, source_target_pairs={{0,4},{2,6},{4,0},{6,2},{1,5},{3,7},{5,1},{7,3},{8,12},{10,14},{12... | collective-permute-start | bytes 663560 | tf_op jit(solution)/shard_map/ppermute | solution.py:426
  83.6 15.7 %collective-permute-start.17 = (bf16[144,768]{1,0:T(8,128)(2,1)S(1)}, bf16[144,768]{1,0:T(8,128)(2,1)S(1)}, u32[]{:S(2)}, u32[]{:S(2)}) collective-permute-start(bf16[144,768]{1,0:T(8,128)(2,1)S(1)} %get-tuple-element.157), channel_id=1, source_target_pairs={{0,6},{2,4},{4,2},{6,0},{1,7},{3,5},{5,3},{7,1},{8,14},{10,12},{12... | collective-permute-start | bytes 663560 | tf_op jit(solution)/shard_map/ppermute | solution.py:426
  86.2 14.6 %copy-start.17 = (f32[768,768]{1,0:T(8,128)}, f32[768,768]{1,0:T(8,128)S(1)}, u32[]{:S(2)}) copy-start(f32[768,768]{1,0:T(8,128)S(1)} %get-tuple-element.232.kept) | copy-start | bytes 7077892
  100.8 19.3 %copy-start.8 = (bf16[394,768]{1,0:T(8,128)(2,1)S(1)}, bf16[394,768]{1,0:T(8,128)(2,1)}, u32[]{:S(2)}) copy-start(bf16[394,768]{1,0:T(8,128)(2,1)} %cot.3) | copy-start | bytes 1815556
  100.8 1.7 collective-permute-start.20
  102.6 9.6 %collective-permute-start.21 = (bf16[416,384]{1,0:T(8,128)(2,1)S(1)}, bf16[416,384]{1,0:T(8,128)(2,1)S(1)}, u32[]{:S(2)}, u32[]{:S(2)}) collective-permute-start(bf16[416,384]{1,0:T(8,128)(2,1)S(1)} %add_convert_fusion.1), channel_id=1, source_target_pairs={{0,16},{8,24},{16,0},{24,8},{1,17},{9,25},{17,1},{25,9},{2,18},{10... | collective-permute-start | bytes 958472 | tf_op jit(solution)/shard_map/ppermute | solution.py:423
  104.1 13.6 %collective-permute-start.22 = (bf16[256,768]{1,0:T(8,128)(2,1)S(1)}, bf16[256,768]{1,0:T(8,128)(2,1)S(1)}, u32[]{:S(2)}, u32[]{:S(2)}) collective-permute-start(bf16[256,768]{1,0:T(8,128)(2,1)S(1)} %get-tuple-element.182), channel_id=1, source_target_pairs={{0,1},{1,0},{2,3},{3,2},{4,5},{5,4},{6,7},{7,6},{8,9},{9,8},{10,11... | collective-permute-start | bytes 1179656 | tf_op jit(solution)/shard_map/ppermute | solution.py:429
  105.7 12.1 %collective-permute-start.23 = (bf16[144,768]{1,0:T(8,128)(2,1)S(1)}, bf16[144,768]{1,0:T(8,128)(2,1)S(1)}, u32[]{:S(2)}, u32[]{:S(2)}) collective-permute-start(bf16[144,768]{1,0:T(8,128)(2,1)S(1)} %get-tuple-element.184), channel_id=1, source_target_pairs={{0,2},{2,0},{4,6},{6,4},{1,3},{3,1},{5,7},{7,5},{8,10},{10,8},{12,... | collective-permute-start | bytes 663560 | tf_op jit(solution)/shard_map/ppermute | solution.py:426
  110.2 6.8 %collective-permute-start.24 = (bf16[72,768]{1,0:T(8,128)(2,1)S(1)}, bf16[72,768]{1,0:T(8,128)(2,1)S(1)}, u32[]{:S(2)}, u32[]{:S(2)}) collective-permute-start(bf16[72,768]{1,0:T(8,128)(2,1)S(1)} %get-tuple-element.185), channel_id=1, source_target_pairs={{0,4},{2,6},{4,0},{6,2},{1,5},{3,7},{5,1},{7,3},{8,12},{10,14},{12... | collective-permute-start | bytes 331784 | tf_op jit(solution)/shard_map/ppermute | solution.py:426
  117.7 0.7 copy-start.9
  118.5 1.6 collective-permute-start.25
  125.0 6.1 %collective-permute-start.29 = (bf16[394,384]{1,0:T(8,128)(2,1)S(1)}, bf16[394,384]{1,0:T(8,128)(2,1)S(1)}, u32[]{:S(2)}, u32[]{:S(2)}) collective-permute-start(bf16[394,384]{1,0:T(8,128)(2,1)S(1)} %get-tuple-element.210), channel_id=1, source_target_pairs={{0,8},{8,0},{16,24},{24,16},{1,9},{9,1},{17,25},{25,17},{2,10},{10... | collective-permute-start | bytes 907784 | tf_op jit(solution)/shard_map/ppermute | solution.py:423
  125.2 7.7 %collective-permute-start.26 = (bf16[72,768]{1,0:T(8,128)(2,1)S(1)}, bf16[72,768]{1,0:T(8,128)(2,1)S(1)}, u32[]{:S(2)}, u32[]{:S(2)}) collective-permute-start(bf16[72,768]{1,0:T(8,128)(2,1)S(1)} %get-tuple-element.198), channel_id=1, source_target_pairs={{0,6},{2,4},{4,2},{6,0},{1,7},{3,5},{5,3},{7,1},{8,14},{10,12},{12... | collective-permute-start | bytes 331784 | tf_op jit(solution)/shard_map/ppermute | solution.py:426
  127.6 11.2 %collective-permute-start.31 = (bf16[192,768]{1,0:T(8,128)(2,1)S(1)}, bf16[192,768]{1,0:T(8,128)(2,1)S(1)}, u32[]{:S(2)}, u32[]{:S(2)}) collective-permute-start(bf16[192,768]{1,0:T(8,128)(2,1)S(1)} %get-tuple-element.212), channel_id=1, source_target_pairs={{0,3},{1,2},{2,1},{3,0},{4,7},{5,6},{6,5},{7,4},{8,11},{9,10},{10,... | collective-permute-start | bytes 884744 | tf_op jit(solution)/shard_map/ppermute | solution.py:433
  129.5 15.0 %collective-permute-start.32 = (bf16[192,768]{1,0:T(8,128)(2,1)S(1)}, bf16[192,768]{1,0:T(8,128)(2,1)S(1)}, u32[]{:S(2)}, u32[]{:S(2)}) collective-permute-start(bf16[192,768]{1,0:T(8,128)(2,1)S(1)} %get-tuple-element.213), channel_id=1, source_target_pairs={{0,1},{1,0},{2,3},{3,2},{4,5},{5,4},{6,7},{7,6},{8,9},{9,8},{10,11... | collective-permute-start | bytes 884744 | tf_op jit(solution)/shard_map/ppermute | solution.py:433
  130.0 15.0 %collective-permute-start.33 = (bf16[192,768]{1,0:T(8,128)(2,1)S(1)}, bf16[192,768]{1,0:T(8,128)(2,1)S(1)}, u32[]{:S(2)}, u32[]{:S(2)}) collective-permute-start(bf16[192,768]{1,0:T(8,128)(2,1)S(1)} %get-tuple-element.214), channel_id=1, source_target_pairs={{0,2},{1,3},{2,0},{3,1},{4,6},{5,7},{6,4},{7,5},{8,10},{9,11},{10,... | collective-permute-start | bytes 884744 | tf_op jit(solution)/shard_map/ppermute | solution.py:433
  131.2 14.7 %collective-permute-start.30 = (bf16[394,384]{1,0:T(8,128)(2,1)S(1)}, bf16[394,384]{1,0:T(8,128)(2,1)S(1)}, u32[]{:S(2)}, u32[]{:S(2)}) collective-permute-start(bf16[394,384]{1,0:T(8,128)(2,1)S(1)} %add_convert_fusion.3), channel_id=1, source_target_pairs={{0,16},{8,24},{16,0},{24,8},{1,17},{9,25},{17,1},{25,9},{2,18},{10... | collective-permute-start | bytes 907784 | tf_op jit(solution)/shard_map/ppermute | solution.py:423
  134.4 12.2 %collective-permute-start.27 = (bf16[400,384]{1,0:T(8,128)(2,1)S(1)}, bf16[400,384]{1,0:T(8,128)(2,1)S(1)}, u32[]{:S(2)}, u32[]{:S(2)}) collective-permute-start(bf16[400,384]{1,0:T(8,128)(2,1)S(1)} %get-tuple-element.207), channel_id=1, source_target_pairs={{0,8},{8,0},{16,24},{24,16},{1,9},{9,1},{17,25},{25,17},{2,10},{10... | collective-permute-start | bytes 921608 | tf_op jit(solution)/shard_map/ppermute | solution.py:423
  146.0 19.9 %collective-permute-start.34 = (bf16[512,768]{1,0:T(8,128)(2,1)}, bf16[512,768]{1,0:T(8,128)(2,1)}, u32[]{:S(2)}, u32[]{:S(2)}) collective-permute-start(bf16[512,768]{1,0:T(8,128)(2,1)} %get-tuple-element.216), channel_id=1, source_target_pairs={{0,1},{1,0},{2,3},{3,2},{4,5},{5,4},{6,7},{7,6},{8,9},{9,8},{10,11... | collective-permute-start | bytes 2359304 | tf_op jit(solution)/shard_map/ppermute | solution.py:429
  147.4 9.2 %collective-permute-start.28 = (bf16[400,384]{1,0:T(8,128)(2,1)}, bf16[400,384]{1,0:T(8,128)(2,1)}, u32[]{:S(2)}, u32[]{:S(2)}) collective-permute-start(bf16[400,384]{1,0:T(8,128)(2,1)} %add_convert_fusion.5), channel_id=1, source_target_pairs={{0,16},{8,24},{16,0},{24,8},{1,17},{9,25},{17,1},{25,9},{2,18},{10... | collective-permute-start | bytes 921608 | tf_op jit(solution)/shard_map/ppermute | solution.py:423
  148.0 1.7 collective-permute-start.36
  148.0 18.0 %collective-permute-start.35 = (bf16[192,768]{1,0:T(8,128)(2,1)}, bf16[192,768]{1,0:T(8,128)(2,1)}, u32[]{:S(2)}, u32[]{:S(2)}) collective-permute-start(bf16[192,768]{1,0:T(8,128)(2,1)} %shard_map.223.own), channel_id=1, source_target_pairs={{0,4},{2,6},{4,0},{6,2},{1,5},{3,7},{5,1},{7,3},{8,12},{10,14},{12... | collective-permute-start | bytes 884744 | tf_op jit(solution)/shard_map/ppermute | solution.py:426
  152.5 14.4 %collective-permute-start.37 = (f32[16,768]{1,0:T(8,128)S(1)}, f32[16,768]{1,0:T(8,128)S(1)}, u32[]{:S(2)}, u32[]{:S(2)}) collective-permute-start(f32[16,768]{1,0:T(8,128)S(1)} %get-tuple-element.221.small), channel_id=1, source_target_pairs={{0,4},{2,6},{4,0},{6,2},{1,5},{3,7},{5,1},{7,3},{8,12},{10,14},{12... | collective-permute-start | bytes 147464 | tf_op jit(solution)/shard_map/ppermute | solution.py:426
  157.8 13.9 %copy-start.10 = (bf16[256,768]{1,0:T(8,128)(2,1)S(1)}, bf16[256,768]{1,0:T(8,128)(2,1)}, u32[]{:S(2)}) copy-start(bf16[256,768]{1,0:T(8,128)(2,1)} %copy-done.9) | copy-start | bytes 1179652
  157.8 13.9 %copy-start.18 = (f32[768,768]{1,0:T(8,128)S(1)}, f32[768,768]{1,0:T(8,128)}, u32[]{:S(2)}) copy-start(f32[768,768]{1,0:T(8,128)} %copy-done.17) | copy-start | bytes 7077892
  168.0 6.4 %collective-permute-start.38 = (bf16[400,384]{1,0:T(8,128)(2,1)S(1)}, bf16[400,384]{1,0:T(8,128)(2,1)S(1)}, u32[]{:S(2)}, u32[]{:S(2)}) collective-permute-start(bf16[400,384]{1,0:T(8,128)(2,1)S(1)} %add_convert_fusion.4), channel_id=1, source_target_pairs={{0,8},{8,0},{16,24},{24,16},{1,9},{9,1},{17,25},{25,17},{2,10},{10... | collective-permute-start | bytes 921608 | tf_op jit(solution)/shard_map/ppermute | solution.py:423
  168.2 9.9 %collective-permute-start.39 = (bf16[208,768]{1,0:T(8,128)(2,1)S(1)}, bf16[208,768]{1,0:T(8,128)(2,1)S(1)}, u32[]{:S(2)}, u32[]{:S(2)}) collective-permute-start(bf16[208,768]{1,0:T(8,128)(2,1)S(1)} %shard_map.225.refs_0_), channel_id=1, source_target_pairs={{0,1},{1,0},{2,3},{3,2},{4,5},{5,4},{6,7},{7,6},{8,9},{9,8},{10,11... | collective-permute-start | bytes 958472 | tf_op jit(solution)/shard_map/ppermute | solution.py:433
  169.6 10.4 %collective-permute-start.40 = (bf16[208,768]{1,0:T(8,128)(2,1)S(1)}, bf16[208,768]{1,0:T(8,128)(2,1)S(1)}, u32[]{:S(2)}, u32[]{:S(2)}) collective-permute-start(bf16[208,768]{1,0:T(8,128)(2,1)S(1)} %shard_map.225.refs_0_), channel_id=1, source_target_pairs={{0,2},{1,3},{2,0},{3,1},{4,6},{5,7},{6,4},{7,5},{8,10},{9,11},{10,... | collective-permute-start | bytes 958472 | tf_op jit(solution)/shard_map/ppermute | solution.py:433
  169.6 16.4 %collective-permute-start.41 = (bf16[208,768]{1,0:T(8,128)(2,1)S(1)}, bf16[208,768]{1,0:T(8,128)(2,1)S(1)}, u32[]{:S(2)}, u32[]{:S(2)}) collective-permute-start(bf16[208,768]{1,0:T(8,128)(2,1)S(1)} %shard_map.225.refs_0_), channel_id=1, source_target_pairs={{0,3},{1,2},{2,1},{3,0},{4,7},{5,6},{6,5},{7,4},{8,11},{9,10},{10,... | collective-permute-start | bytes 958472 | tf_op jit(solution)/shard_map/ppermute | solution.py:433

commit v6 on v4

--- a/solution.py
+++ b/solution.py
@@ -547,6 +547,8 @@
         worked = []
         d_back, gated = [], []
         for number, call in enumerate(calls):
+            if number == 1:
+                router, d_back[1] = lax.optimization_barrier((router, d_back[1]))
             count = cap * len(call)
             last = number == len(calls) - 1
             grads = [] if last else [((2 * width, hidden_width), BF16)] * 2
@@ -559,12 +561,12 @@
                 + [((part_rows, width), F32)]
                 + grads,
                 [ids, up_a, up_b, down_a, down_b]
-                + [after(router, worked[-1][6]) if worked else router]
+                + [router]
                 + [pair_out if worked or not small_slice else router]
                 + [rows_in[k] for k in call]
                 + [d_rows_in[k] for k in call],
                 scratch=[((count, width), F32)],
-                micros=7,
+                micros=0.05,
                 limit=24,
             )
             d_back += results[: len(call)]
@@ -657,6 +659,13 @@
         )
         chip_y = (kept_y.astype(F32) + tensor_swap(sent_y, 1).astype(F32)).astype(BF16)
         own_y = (chip_y.astype(F32) + tensor_swap(chip_y, 2).astype(F32)).astype(BF16)
+        grad_up, grad_down = run(
+            join_grad_kernel,
+            [((half, hidden_width), F32), ((hidden_width, half), F32)],
+            [grad_kept, came_first, dp_swap(sent_rest)],
+            scratch=[((width, width), BF16)],
+            micros=2,
+        )
         if small_slice:
             (ready,) = run(
                 pair_kernel,
@@ -665,7 +674,9 @@
                 micros=1,
             )
             own_y, ready = lax.optimization_barrier((own_y, ready))
-            everything = [ready] + [quarter_swap(ready, m) for m in (1, 2, 3)]
+            everything = [quarter_swap(ready, m) for m in (1, 2, 3)]
+            ready, grad_up, grad_down = lax.optimization_barrier((ready, grad_up, grad_down))
+            everything = [ready] + everything
             grad_qkv, grad_out, *sums, grad_router = run(
                 functools.partial(spread_kernel, 4),
                 [((3 * inner, width), F32), ((inner, width), F32)]
@@ -680,14 +691,6 @@
             grad_qkv, grad_out = grads[: 3 * inner], grads[3 * inner :]
             small_sum = lax.psum(small, ("expert", "dp"))
             sums, grad_router = list(small_sum[:4]), small_sum[8 : 8 + experts]
-
-        grad_up, grad_down = run(
-            join_grad_kernel,
-            [((half, hidden_width), F32), ((hidden_width, half), F32)],
-            [grad_kept, came_first, dp_swap(sent_rest)],
-            scratch=[((width, width), BF16)],
-            micros=2,
-        )
 
         mix_own, mix_other = own_y, tensor_swap(own_y, 1)
         mixture = jnp.where(

time: 190 us -> 171 us (0.900)
  waiting for transfers between devices: 92.6 us -> 76.5 us
    ppermute x6, waiting for transfers between devices: 36 us -> 19.7 us  [quarter_swap(): return lax.ppermute(value, ('expert', 'dp'), pairs)]
  transfers between devices with their start and end apart: 42 -> 42, of which waited for: 20 -> 21; matrix products, arithmetic and copies ran while one was open for 2% -> 2% of each run, Pallas kernels for 12% -> 12%
where the time goes in v6:
time: 171 us
  waiting for transfers between devices  76.5 us (45%)
  starting transfers between devices  48.3 us (28%)
  Pallas kernels  37.2 us (22%)
  local copies, waits for them, and re-layouts  3.81 us (2%)
  other arithmetic  3.56 us (2%)
    ppermute x14, waiting for transfers between devices, expert_swap(): lax.ppermute(value, 'expert', [(i, i ^ mask) for i in range(n_expert)])  41.9 us
    pallas_call x16, Pallas kernels, run(): pl.pallas_call(kernel, out_shape=[jax.ShapeDtypeStruct(shape, kind) for s...  37.2 us
    ppermute x14, starting transfers between devices, expert_swap(): lax.ppermute(value, 'expert', [(i, i ^ mask) for i in range(n_expert)])  25.5 us
    ppermute x6, waiting for transfers between devices, quarter_swap(): return lax.ppermute(value, ('expert', 'dp'), pairs)  19.7 us
    ppermute x20, waiting for transfers between devices, tensor_swap(): lax.ppermute(value, 'tensor', [(i, i ^ mask) for i in range(n_tensor)])  14.9 us
    ppermute x20, starting transfers between devices, tensor_swap(): lax.ppermute(value, 'tensor', [(i, i ^ mask) for i in range(n_tensor)])  12.8 us
    ppermute x6, starting transfers between devices, quarter_swap(): return lax.ppermute(value, ('expert', 'dp'), pairs)  7.06 us
    unnamed x38, local copies, waits for them, and re-layouts  3.69 us
  transfers between devices with their start and end apart: 42, of which 21 were waited for; matrix products, arithmetic and copies ran while one was open for 2% of the time, Pallas kernels for 12%

profile of v6, /device:TPU:0, one launch (start us, length us, event | category | flops | bytes accessed | tf_op | source)
XLA Modules:
  0.0 171.1 jit_solution(13358802309427407608)
XLA Ops:
  1.2 2.9 %collective-permute-start = (bf16[192,768]{1,0:T(8,128)(2,1)}, bf16[192,768]{1,0:T(8,128)(2,1)S(1)}, u32[]{:S(2)}, u32[]{:S(2)}) collective-permute-start(bf16[192,768]{1,0:T(8,128)(2,1)} %w_out.1), channel_id=1, source_target_pairs={{0,16},{8,24},{16,0},{24,8},{1,17},{9,25},{17,1},{25,9},{2,18},{10... | collective-permute-start | bytes 884744 | tf_op jit(solution)/shard_map/ppermute | solution.py:427
  4.9 1.1 copy-done.4
  6.0 0.7 copy-done.6
  6.7 1.2 copy-done.8
  7.8 0.7 copy-done.13
  8.5 2.5 %shard_map.212 = (bf16[394,768]{1,0:T(8,128)(2,1)S(1)}, bf16[394,192]{1,0:T(8,128)(2,1)S(1)}, bf16[394,192]{1,0:T(8,128)(2,1)S(1)}, bf16[394,192]{1,0:T(8,128)(2...) custom-call(bf16[394,768]{1,0:T(8,128)(2,1)S(1)} %copy-done.4, f32[768]{0:T(1024)S(1)} %copy-done.6, ...), custom_call_target="tpu_custom_call" | custom-call | flops 4600000000 | bytes 1024 | tf_op jit(solution)/shard_map/pallas_call | solution.py:410
  11.7 1.8 %collective-permute-start.5 = (bf16[394,192]{1,0:T(8,128)(2,1)S(1)}, bf16[394,192]{1,0:T(8,128)(2,1)S(1)}, u32[]{:S(2)}, u32[]{:S(2)}) collective-permute-start(bf16[394,192]{1,0:T(8,128)(2,1)S(1)} %get-tuple-element.122.rest_0_.head_out), channel_id=1, source_target_pairs={{0,16},{8,24},{16,0},{24,8},{1,17},{9,25},{17,1},{25,9},{2,18},{10... | collective-permute-start | bytes 453896 | tf_op jit(solution)/shard_map/ppermute | solution.py:427
  13.7 1.4 shard_map.213
  15.1 4.1 %collective-permute-done.5.rest_2_ = bf16[394,192]{1,0:T(8,128)(2,1)S(1)} collective-permute-done((bf16[394,192]{1,0:T(8,128)(2,1)S(1)}, bf16[394,192]{1,0:T(8,128)(2,1)S(1)}, u32[]{:S(2)}, u32[]{:S(2)}) %collective-permute-start.5) | collective-permute-done | bytes 151328 | tf_op jit(solution)/shard_map/ppermute | solution.py:427
  19.2 2.8 %collective-permute-start.8 = (bf16[72,768]{1,0:T(8,128)(2,1)S(1)}, bf16[72,768]{1,0:T(8,128)(2,1)S(1)}, u32[]{:S(2)}, u32[]{:S(2)}) collective-permute-start(bf16[72,768]{1,0:T(8,128)(2,1)S(1)} %get-tuple-element.137), channel_id=1, source_target_pairs={{0,4},{2,6},{4,0},{6,2},{1,5},{3,7},{5,1},{7,3},{8,12},{10,14},{12... | collective-permute-start | bytes 331784 | tf_op jit(solution)/shard_map/ppermute | solution.py:430
  22.0 1.3 collective-permute-start.9
  23.5 2.7 %shard_map.214 = (f32[394,768]{1,0:T(8,128)S(1)}, bf16[144,768]{1,0:T(8,128)(2,1)S(1)}, bf16[144,768]{1,0:T(8,128)(2,1)S(1)}, bf16[144,768]{1,0:T(8,128)(2,1)S(1)}, bf16[144,768]{1,0:T(8,128)(2,1)S(1)}) custom-call(s32[8]{0:T(128)S(1)} %stack.38.ids, bf16[394,768]{1,0:T(8,128)(2,1)S(1)} %copy-done.5, f32[768]{0:T(1024)S(1)} %copy-done.16, ...), custom_call_target="tpu_custom_call" | custom-call | flops 3449999872 | bytes 1024 | tf_op jit(solution)/shard_map/pallas_call | solution.py:410
  26.2 4.6 %collective-permute-done.8.refs_2_ = bf16[72,768]{1,0:T(8,128)(2,1)S(1)} collective-permute-done((bf16[72,768]{1,0:T(8,128)(2,1)S(1)}, bf16[72,768]{1,0:T(8,128)(2,1)S(1)}, u32[]{:S(2)}, u32[]{:S(2)}) %collective-permute-start.8) | collective-permute-done | bytes 110624 | tf_op jit(solution)/shard_map/ppermute | solution.py:430
  30.8 2.9 %collective-permute-start.10 = (bf16[144,768]{1,0:T(8,128)(2,1)S(1)}, bf16[144,768]{1,0:T(8,128)(2,1)S(1)}, u32[]{:S(2)}, u32[]{:S(2)}) collective-permute-start(bf16[144,768]{1,0:T(8,128)(2,1)S(1)} %get-tuple-element.140), channel_id=1, source_target_pairs={{0,2},{2,0},{4,6},{6,4},{1,3},{3,1},{5,7},{7,5},{8,10},{10,8},{12,... | collective-permute-start | bytes 663560 | tf_op jit(solution)/shard_map/ppermute | solution.py:430
  33.7 1.6 collective-permute-start.13
  35.3 3.9 %collective-permute-start.14 = (bf16[144,768]{1,0:T(8,128)(2,1)S(1)}, bf16[144,768]{1,0:T(8,128)(2,1)S(1)}, u32[]{:S(2)}, u32[]{:S(2)}) collective-permute-start(bf16[144,768]{1,0:T(8,128)(2,1)S(1)} %get-tuple-element.150), channel_id=1, source_target_pairs={{0,4},{2,6},{4,0},{6,2},{1,5},{3,7},{5,1},{7,3},{8,12},{10,14},{12... | collective-permute-start | bytes 663560 | tf_op jit(solution)/shard_map/ppermute | solution.py:430
  39.6 4.1 %collective-permute-done.10.refs_1_ = bf16[144,768]{1,0:T(8,128)(2,1)S(1)} collective-permute-done((bf16[144,768]{1,0:T(8,128)(2,1)S(1)}, bf16[144,768]{1,0:T(8,128)(2,1)S(1)}, u32[]{:S(2)}, u32[]{:S(2)}) %collective-permute-start.10) | collective-permute-done | bytes 221216 | tf_op jit(solution)/shard_map/ppermute | solution.py:430
  43.7 5.0 %collective-permute-done.11.refs_3_ = bf16[144,768]{1,0:T(8,128)(2,1)S(1)} collective-permute-done((bf16[144,768]{1,0:T(8,128)(2,1)S(1)}, bf16[144,768]{1,0:T(8,128)(2,1)S(1)}, u32[]{:S(2)}, u32[]{:S(2)}) %collective-permute-start.11) | collective-permute-done | bytes 221216 | tf_op jit(solution)/shard_map/ppermute | solution.py:430
  48.8 7.0 %shard_map.215 = (bf16[144,768]{1,0:T(8,128)(2,1)S(1)}, bf16[144,768]{1,0:T(8,128)(2,1)S(1)}, bf16[2,144,768]{2,1,0:T(8,128)(2,1)S(1)}, bf16[2,144,768]{2,1,0:T(...) custom-call(s32[8]{0:T(128)S(1)} %stack.38.ids, ...), custom_call_target="tpu_custom_call" | custom-call | flops 57500000 | bytes 1024 | tf_op jit(solution)/shard_map/pallas_call | solution.py:410
  55.8 0.9 collective-permute-done.15.refs_1_
  56.7 4.8 %shard_map.216 = (bf16[144,768]{1,0:T(8,128)(2,1)S(1)}, bf16[144,768]{1,0:T(8,128)(2,1)S(1)}, bf16[2,72,768]{2,1,0:T(8,128)(2,1)S(1)}, bf16[2,72,768]{2,1,0:T(8,...) custom-call(s32[8]{0:T(128)S(1)} %stack.38.ids, ...), custom_call_target="tpu_custom_call" | custom-call | flops 57500000 | bytes 1024 | tf_op jit(solution)/shard_map/pallas_call | solution.py:410
  61.5 2.7 %shard_map.218 = (bf16[1536,768]{1,0:T(8,128)(2,1)S(1)}, bf16[1536,768]{1,0:T(8,128)(2,1)S(1)}) custom-call(bf16[288,768]{1,0:T(8,128)(2,1)S(1)} %get-tuple-element.159.refs_0_, bf16[288,768]{1,0:T(8,128)(2,1)S(1)} %get-tuple-element.160.refs_1_, bf16[288,768]{1,0:T(8,128)(2,1)S(1)} %get-tuple-element.161.refs_2_, ...), custom_call_target="tpu_custom_call" | custom-call | flops 4600000000 | bytes 1024 | tf_op jit(solution)/shard_map/pallas_call | solution.py:410
  64.3 2.2 %collective-permute-start.12 = (bf16[144,768]{1,0:T(8,128)(2,1)S(1)}, bf16[144,768]{1,0:T(8,128)(2,1)S(1)}, u32[]{:S(2)}, u32[]{:S(2)}) collective-permute-start(bf16[144,768]{1,0:T(8,128)(2,1)S(1)} %get-tuple-element.146), channel_id=1, source_target_pairs={{0,2},{2,0},{4,6},{6,4},{1,3},{3,1},{5,7},{7,5},{8,10},{10,8},{12,... | collective-permute-start | bytes 663560 | tf_op jit(solution)/shard_map/ppermute | solution.py:430
  66.4 1.4 collective-permute-start.16
  67.8 1.0 collective-permute-start.17
  68.9 1.3 collective-permute-start.18
  70.3 5.8 %collective-permute-done.18.came = bf16[2,72,768]{2,1,0:T(8,128)(2,1)S(1)} collective-permute-done((bf16[2,72,768]{2,1,0:T(8,128)(2,1)S(1)}, bf16[2,72,768]{2,1,0:T(8,128)(2,1)S(1)}, u32[]{:S(2)}, u32[]{:S(2)}) %collective-permute-start.18) | collective-permute-done | bytes 221216 | tf_op jit(solution)/shard_map/ppermute | solution.py:427
  76.1 1.6 shard_map.219
  77.8 7.3 %collective-permute-done.16.refs_2_ = bf16[144,768]{1,0:T(8,128)(2,1)S(1)} collective-permute-done((bf16[144,768]{1,0:T(8,128)(2,1)S(1)}, bf16[144,768]{1,0:T(8,128)(2,1)S(1)}, u32[]{:S(2)}, u32[]{:S(2)}) %collective-permute-start.16) | collective-permute-done | bytes 221216 | tf_op jit(solution)/shard_map/ppermute | solution.py:430
  85.1 1.5 shard_map.220
  86.7 1.6 collective-permute-done.20
  89.0 1.5 collective-permute-start.22
  90.5 4.5 %collective-permute-start.23 = (bf16[144,768]{1,0:T(8,128)(2,1)S(1)}, bf16[144,768]{1,0:T(8,128)(2,1)S(1)}, u32[]{:S(2)}, u32[]{:S(2)}) collective-permute-start(bf16[144,768]{1,0:T(8,128)(2,1)S(1)} %get-tuple-element.180), channel_id=1, source_target_pairs={{0,2},{2,0},{4,6},{6,4},{1,3},{3,1},{5,7},{7,5},{8,10},{10,8},{12,... | collective-permute-start | bytes 663560 | tf_op jit(solution)/shard_map/ppermute | solution.py:430
  95.1 0.9 collective-permute-start.24
  96.0 1.5 collective-permute-start.25
  97.4 0.6 collective-permute-done.21
  98.1 5.0 %collective-permute-done.24.refs_2_ = bf16[72,768]{1,0:T(8,128)(2,1)S(1)} collective-permute-done((bf16[72,768]{1,0:T(8,128)(2,1)S(1)}, bf16[72,768]{1,0:T(8,128)(2,1)S(1)}, u32[]{:S(2)}, u32[]{:S(2)}) %collective-permute-start.24) | collective-permute-done | bytes 110624 | tf_op jit(solution)/shard_map/ppermute | solution.py:430
  103.1 4.1 %collective-permute-done.25.refs_3_ = bf16[72,768]{1,0:T(8,128)(2,1)S(1)} collective-permute-done((bf16[72,768]{1,0:T(8,128)(2,1)S(1)}, bf16[72,768]{1,0:T(8,128)(2,1)S(1)}, u32[]{:S(2)}, u32[]{:S(2)}) %collective-permute-start.25) | collective-permute-done | bytes 110624 | tf_op jit(solution)/shard_map/ppermute | solution.py:430
  107.2 1.6 collective-permute-done.26.other
  108.8 4.9 %shard_map.221 = (f32[394,768]{1,0:T(8,128)S(1)}, bf16[394,384]{1,0:T(8,128)(2,1)S(1)}, bf16[394,384]{1,0:T(8,128)(2,1)S(1)}, f32[16,768]{1,0:T(8,128)S(1)}, bf1...) custom-call(s32[8]{0:T(128)S(1)} %stack.38.ids, ...), custom_call_target="tpu_custom_call" | custom-call | flops 6899999744 | bytes 1024 | tf_op jit(solution)/shard_map/pallas_call | solution.py:410
  114.0 0.7 collective-permute-start.29
  114.7 1.5 collective-permute-start.30
  116.2 1.3 collective-permute-start.31
  117.5 1.5 shard_map.222
  119.1 1.6 collective-permute-start.34
  120.7 4.1 %collective-permute-done.29.refs_1_ = bf16[192,768]{1,0:T(8,128)(2,1)S(1)} collective-permute-done((bf16[192,768]{1,0:T(8,128)(2,1)S(1)}, bf16[192,768]{1,0:T(8,128)(2,1)S(1)}, u32[]{:S(2)}, u32[]{:S(2)}) %collective-permute-start.29) | collective-permute-done | bytes 294944 | tf_op jit(solution)/shard_map/ppermute | solution.py:437
  124.7 5.3 %collective-permute-done.30.refs_2_ = bf16[192,768]{1,0:T(8,128)(2,1)S(1)} collective-permute-done((bf16[192,768]{1,0:T(8,128)(2,1)S(1)}, bf16[192,768]{1,0:T(8,128)(2,1)S(1)}, u32[]{:S(2)}, u32[]{:S(2)}) %collective-permute-start.30) | collective-permute-done | bytes 294944 | tf_op jit(solution)/shard_map/ppermute | solution.py:437
  130.3 1.6 collective-permute-start.28
  132.0 1.3 collective-permute-start.32
  133.3 1.5 collective-permute-start.38
  134.8 2.4 %shard_map.224 = (bf16[394,768]{1,0:T(8,128)(2,1)}, f32[16,768]{1,0:T(8,128)S(1)}) custom-call(s32[8]{0:T(128)S(1)} %stack.38.ids, bf16[394,384]{1,0:T(8,128)(2,1)S(1)} %add_convert_fusion.2.own, bf16[394,384]{1,0:T(8,128)(2,1)S(1)} %collective-permute-done.35.other, bf16[394,768]{1,0:T(8,128)(2,1)S(1)} %copy-done.5, ...), custom_call_target="tpu_custom_call" | custom-call | flops 11500000 | bytes 1024 | tf_op jit(solution)/shard_map/pallas_call | solution.py:410
  137.2 1.2 collective-permute-start.36
  138.5 0.6 collective-permute-done.28
  139.1 0.8 add_convert_fusion.4
  139.9 10.3 %collective-permute-done.32.came = bf16[192,768]{1,0:T(8,128)(2,1)S(1)} collective-permute-done((bf16[192,768]{1,0:T(8,128)(2,1)S(1)}, bf16[192,768]{1,0:T(8,128)(2,1)S(1)}, u32[]{:S(2)}, u32[]{:S(2)}) %collective-permute-start.32) | collective-permute-done | bytes 294944 | tf_op jit(solution)/shard_map/ppermute | solution.py:430
  150.1 0.6 collective-permute-done.36.small_came
  150.9 1.2 collective-permute-start.39
  152.1 2.4 %collective-permute-start.41 = (bf16[208,768]{1,0:T(8,128)(2,1)S(1)}, bf16[208,768]{1,0:T(8,128)(2,1)S(1)}, u32[]{:S(2)}, u32[]{:S(2)}) collective-permute-start(bf16[208,768]{1,0:T(8,128)(2,1)S(1)} %shard_map.225.refs_0_), channel_id=1, source_target_pairs={{0,3},{1,2},{2,1},{3,0},{4,7},{5,6},{6,5},{7,4},{8,11},{9,10},{10,... | collective-permute-start | bytes 958472 | tf_op jit(solution)/shard_map/ppermute | solution.py:437
  154.5 2.3 %select_convert_fusion = bf16[394,768]{1,0:T(8,128)(2,1)} fusion(f32[394,768]{1,0:T(8,128)S(1)} %copy-done.3, bf16[400,384]{1,0:T(8,128)(2,1)} %collective-permute-done.37, bf16[400,384]{1,0:T(8,128)(2,1)} %add_convert_fusion.4, pred[394]{0:T(512)(128)(4,1)S(1)} %iota_compare_fusion, pred[]{:T(512)S(6)} %eq.7), kind=kLoop, calls=%fused_computation | loop fusion | flops 3933696 | bytes 2430347 | tf_op jit(solution)/shard_map/convert_element_type | solution.py:702
  156.8 1.7 shard_map.226
  158.5 2.3 %collective-permute-done.39.refs_1_ = bf16[208,768]{1,0:T(8,128)(2,1)S(1)} collective-permute-done((bf16[208,768]{1,0:T(8,128)(2,1)S(1)}, bf16[208,768]{1,0:T(8,128)(2,1)S(1)}, u32[]{:S(2)}, u32[]{:S(2)}) %collective-permute-start.39) | collective-permute-done | bytes 319520 | tf_op jit(solution)/shard_map/ppermute | solution.py:437
  160.9 1.6 collective-permute-done.40.refs_2_
  162.4 6.4 %collective-permute-done.41.refs_3_ = bf16[208,768]{1,0:T(8,128)(2,1)S(1)} collective-permute-done((bf16[208,768]{1,0:T(8,128)(2,1)S(1)}, bf16[208,768]{1,0:T(8,128)(2,1)S(1)}, u32[]{:S(2)}, u32[]{:S(2)}) %collective-permute-start.41) | collective-permute-done | bytes 319520 | tf_op jit(solution)/shard_map/ppermute | solution.py:437
  168.9 2.2 %shard_map.227 = (f32[576,768]{1,0:T(8,128)}, f32[192,768]{1,0:T(8,128)}, f32[768]{0:T(1024)}, f32[768]{0:T(1024)}, f32[768]{0:T(1024)}, /*index=5*/f32[768]{0:T(1024)}, f32[4,768]{1,0:T(4,128)}) custom-call(s32[8]{0:T(128)S(1)} %stack.38.ids, bf16[208,768]{1,0:T(8,128)(2,1)S(1)} %shard_map.225.refs_0_, ...), custom_call_target="tpu_custom_call" | custom-call | flops 3449999872 | bytes 1024 | tf_op jit(solution)/shard_map/pallas_call | solution.py:410
  (85 shorter events, 4.0 us)
Async XLA Ops:
  0.6 11.0 %collective-permute-start.2 = (bf16[768,768]{1,0:T(8,128)(2,1)}, bf16[768,768]{1,0:T(8,128)(2,1)S(1)}, u32[]{:S(2)}, u32[]{:S(2)}) collective-permute-start(bf16[768,768]{1,0:T(8,128)(2,1)} %bitcast.26), channel_id=1, source_target_pairs={{0,8},{8,0},{16,24},{24,16},{1,9},{9,1},{17,25},{25,17},{2,10},{10... | collective-permute-start | bytes 3538952 | tf_op jit(solution)/shard_map/ppermute | solution.py:427
  1.2 10.5 %collective-permute-start.3 = (bf16[768,768]{1,0:T(8,128)(2,1)}, bf16[768,768]{1,0:T(8,128)(2,1)S(1)}, u32[]{:S(2)}, u32[]{:S(2)}) collective-permute-start(bf16[768,768]{1,0:T(8,128)(2,1)} %bitcast.29), channel_id=1, source_target_pairs={{0,8},{8,0},{16,24},{24,16},{1,9},{9,1},{17,25},{25,17},{2,10},{10... | collective-permute-start | bytes 3538952 | tf_op jit(solution)/shard_map/ppermute | solution.py:427
  1.2 10.4 %collective-permute-start = (bf16[192,768]{1,0:T(8,128)(2,1)}, bf16[192,768]{1,0:T(8,128)(2,1)S(1)}, u32[]{:S(2)}, u32[]{:S(2)}) collective-permute-start(bf16[192,768]{1,0:T(8,128)(2,1)} %w_out.1), channel_id=1, source_target_pairs={{0,16},{8,24},{16,0},{24,8},{1,17},{9,25},{17,1},{25,9},{2,18},{10... | collective-permute-start | bytes 884744 | tf_op jit(solution)/shard_map/ppermute | solution.py:427
  4.2 7.5 %collective-permute-start.1 = (bf16[192,768]{1,0:T(8,128)(2,1)}, bf16[192,768]{1,0:T(8,128)(2,1)S(1)}, u32[]{:S(2)}, u32[]{:S(2)}) collective-permute-start(bf16[192,768]{1,0:T(8,128)(2,1)} %w_out.1), channel_id=1, source_target_pairs={{0,8},{8,0},{16,24},{24,16},{1,9},{9,1},{17,25},{25,17},{2,10},{10... | collective-permute-start | bytes 884744 | tf_op jit(solution)/shard_map/ppermute | solution.py:427
  4.9 1.1 copy-start.4
  6.0 0.7 copy-start.6
  6.7 1.2 copy-start.8
  7.8 0.7 copy-start.13
  8.5 5.2 %copy-start.10 = (bf16[394,768]{1,0:T(8,128)(2,1)S(1)}, bf16[394,768]{1,0:T(8,128)(2,1)}, u32[]{:S(2)}) copy-start(bf16[394,768]{1,0:T(8,128)(2,1)} %cot.3) | copy-start | bytes 1815556
  8.5 5.2 %copy-start.12 = (bf16[768,4]{0,1:T(4,128)(2,1)S(1)}, bf16[768,4]{0,1:T(4,128)(2,1)}, u32[]{:S(2)}) copy-start(bf16[768,4]{0,1:T(4,128)(2,1)} %param.22) | copy-start | bytes 18436
  8.5 5.2 %copy-start.14 = (s32[394,2]{0,1:T(2,128)S(1)}, s32[394,2]{0,1:T(2,128)}, u32[]{:S(2)}) copy-start(s32[394,2]{0,1:T(2,128)} %param.14) | copy-start | bytes 9460
  11.6 11.8 %collective-permute-start.4 = (bf16[394,192]{1,0:T(8,128)(2,1)S(1)}, bf16[394,192]{1,0:T(8,128)(2,1)S(1)}, u32[]{:S(2)}, u32[]{:S(2)}) collective-permute-start(bf16[394,192]{1,0:T(8,128)(2,1)S(1)} %get-tuple-element.122.rest_0_.head_out), channel_id=1, source_target_pairs={{0,8},{8,0},{16,24},{24,16},{1,9},{9,1},{17,25},{25,17},{2,10},{10... | collective-permute-start | bytes 453896 | tf_op jit(solution)/shard_map/ppermute | solution.py:427
  11.7 7.5 %collective-permute-start.5 = (bf16[394,192]{1,0:T(8,128)(2,1)S(1)}, bf16[394,192]{1,0:T(8,128)(2,1)S(1)}, u32[]{:S(2)}, u32[]{:S(2)}) collective-permute-start(bf16[394,192]{1,0:T(8,128)(2,1)S(1)} %get-tuple-element.122.rest_0_.head_out), channel_id=1, source_target_pairs={{0,16},{8,24},{16,0},{24,8},{1,17},{9,25},{17,1},{25,9},{2,18},{10... | collective-permute-start | bytes 453896 | tf_op jit(solution)/shard_map/ppermute | solution.py:427
  13.5 9.9 %collective-permute-start.7 = (bf16[192,768]{1,0:T(8,128)(2,1)S(1)}, bf16[192,768]{1,0:T(8,128)(2,1)S(1)}, u32[]{:S(2)}, u32[]{:S(2)}) collective-permute-start(bf16[192,768]{1,0:T(8,128)(2,1)S(1)} %collective-permute-done.rest_6_), channel_id=1, source_target_pairs={{0,8},{8,0},{16,24},{24,16},{1,9},{9,1},{17,25},{25,17},{2,10},{10... | collective-permute-start | bytes 884744 | tf_op jit(solution)/shard_map/ppermute | solution.py:427
  13.7 9.7 %copy-start.5 = (bf16[394,768]{1,0:T(8,128)(2,1)S(1)}, bf16[394,768]{1,0:T(8,128)(2,1)}, u32[]{:S(2)}) copy-start(bf16[394,768]{1,0:T(8,128)(2,1)} %tokens.5) | copy-start | bytes 1815556
  13.7 9.7 %copy-start.11 = (bf16[192,768]{1,0:T(8,128)(2,1)S(1)}, bf16[192,768]{1,0:T(8,128)(2,1)}, u32[]{:S(2)}) copy-start(bf16[192,768]{1,0:T(8,128)(2,1)} %w_out.1) | copy-start | bytes 884740
  13.7 9.7 %copy-start.15 = (f32[768]{0:T(1024)S(1)}, f32[768]{0:T(1024)}, u32[]{:S(2)}) copy-start(f32[768]{0:T(1024)} %bias.3) | copy-start | bytes 9220
  13.7 9.7 %copy-start.16 = (f32[768]{0:T(1024)S(1)}, f32[768]{0:T(1024)}, u32[]{:S(2)}) copy-start(f32[768]{0:T(1024)} %gain.6) | copy-start | bytes 9220
  19.2 4.2 %collective-permute-start.6 = (bf16[394,192]{1,0:T(8,128)(2,1)S(1)}, bf16[394,192]{1,0:T(8,128)(2,1)S(1)}, u32[]{:S(2)}, u32[]{:S(2)}) collective-permute-start(bf16[394,192]{1,0:T(8,128)(2,1)S(1)} %collective-permute-done.5.rest_2_), channel_id=1, source_target_pairs={{0,8},{8,0},{16,24},{24,16},{1,9},{9,1},{17,25},{25,17},{2,10},{10... | collective-permute-start | bytes 453896 | tf_op jit(solution)/shard_map/ppermute | solution.py:427
  19.2 11.6 %collective-permute-start.8 = (bf16[72,768]{1,0:T(8,128)(2,1)S(1)}, bf16[72,768]{1,0:T(8,128)(2,1)S(1)}, u32[]{:S(2)}, u32[]{:S(2)}) collective-permute-start(bf16[72,768]{1,0:T(8,128)(2,1)S(1)} %get-tuple-element.137), channel_id=1, source_target_pairs={{0,4},{2,6},{4,0},{6,2},{1,5},{3,7},{5,1},{7,3},{8,12},{10,14},{12... | collective-permute-start | bytes 331784 | tf_op jit(solution)/shard_map/ppermute | solution.py:430
  22.0 8.7 %collective-permute-start.9 = (bf16[72,768]{1,0:T(8,128)(2,1)S(1)}, bf16[72,768]{1,0:T(8,128)(2,1)S(1)}, u32[]{:S(2)}, u32[]{:S(2)}) collective-permute-start(bf16[72,768]{1,0:T(8,128)(2,1)S(1)} %get-tuple-element.138), channel_id=1, source_target_pairs={{0,6},{2,4},{4,2},{6,0},{1,7},{3,5},{5,3},{7,1},{8,14},{10,12},{12... | collective-permute-start | bytes 331784 | tf_op jit(solution)/shard_map/ppermute | solution.py:430
  23.4 25.3 %copy-start = (bf16[1,768,768]{2,1,0:T(8,128)(2,1)S(1)}, bf16[1,768,768]{2,1,0:T(8,128)(2,1)}, u32[]{:S(2)}) copy-start(bf16[1,768,768]{2,1,0:T(8,128)(2,1)} %param.23) | copy-start | bytes 3538948
  23.5 25.3 %copy-start.1 = (bf16[1,768,768]{2,1,0:T(8,128)(2,1)S(1)}, bf16[1,768,768]{2,1,0:T(8,128)(2,1)}, u32[]{:S(2)}) copy-start(bf16[1,768,768]{2,1,0:T(8,128)(2,1)} %param.24) | copy-start | bytes 3538948
  26.2 82.6 %copy-start.2 = (f32[394,768]{1,0:T(8,128)}, f32[394,768]{1,0:T(8,128)S(1)}, u32[]{:S(2)}) copy-start(f32[394,768]{1,0:T(8,128)S(1)} %get-tuple-element.128.middle) | copy-start | bytes 3631108
  30.8 12.9 %collective-permute-start.10 = (bf16[144,768]{1,0:T(8,128)(2,1)S(1)}, bf16[144,768]{1,0:T(8,128)(2,1)S(1)}, u32[]{:S(2)}, u32[]{:S(2)}) collective-permute-start(bf16[144,768]{1,0:T(8,128)(2,1)S(1)} %get-tuple-element.140), channel_id=1, source_target_pairs={{0,2},{2,0},{4,6},{6,4},{1,3},{3,1},{5,7},{7,5},{8,10},{10,8},{12,... | collective-permute-start | bytes 663560 | tf_op jit(solution)/shard_map/ppermute | solution.py:430
  33.6 15.1 %collective-permute-start.11 = (bf16[144,768]{1,0:T(8,128)(2,1)S(1)}, bf16[144,768]{1,0:T(8,128)(2,1)S(1)}, u32[]{:S(2)}, u32[]{:S(2)}) collective-permute-start(bf16[144,768]{1,0:T(8,128)(2,1)S(1)} %get-tuple-element.143), channel_id=1, source_target_pairs={{0,2},{2,0},{4,6},{6,4},{1,3},{3,1},{5,7},{7,5},{8,10},{10,8},{12,... | collective-permute-start | bytes 663560 | tf_op jit(solution)/shard_map/ppermute | solution.py:430
  33.7 22.1 %collective-permute-start.13 = (bf16[2,72,768]{2,1,0:T(8,128)(2,1)S(1)}, bf16[2,72,768]{2,1,0:T(8,128)(2,1)S(1)}, u32[]{:S(2)}, u32[]{:S(2)}) collective-permute-start(bf16[2,72,768]{2,1,0:T(8,128)(2,1)S(1)} %pad_maximum_fusion.2), channel_id=1, source_target_pairs={{0,16},{8,24},{16,0},{24,8},{1,17},{9,25},{17,1},{25,9},{2,18},{10... | collective-permute-start | bytes 663560 | tf_op jit(solution)/shard_map/ppermute | solution.py:427
  35.3 20.5 %collective-permute-start.14 = (bf16[144,768]{1,0:T(8,128)(2,1)S(1)}, bf16[144,768]{1,0:T(8,128)(2,1)S(1)}, u32[]{:S(2)}, u32[]{:S(2)}) collective-permute-start(bf16[144,768]{1,0:T(8,128)(2,1)S(1)} %get-tuple-element.150), channel_id=1, source_target_pairs={{0,4},{2,6},{4,0},{6,2},{1,5},{3,7},{5,1},{7,3},{8,12},{10,14},{12... | collective-permute-start | bytes 663560 | tf_op jit(solution)/shard_map/ppermute | solution.py:430
  39.1 17.6 %collective-permute-start.15 = (bf16[144,768]{1,0:T(8,128)(2,1)S(1)}, bf16[144,768]{1,0:T(8,128)(2,1)S(1)}, u32[]{:S(2)}, u32[]{:S(2)}) collective-permute-start(bf16[144,768]{1,0:T(8,128)(2,1)S(1)} %get-tuple-element.151), channel_id=1, source_target_pairs={{0,6},{2,4},{4,2},{6,0},{1,7},{3,5},{5,3},{7,1},{8,14},{10,12},{12... | collective-permute-start | bytes 663560 | tf_op jit(solution)/shard_map/ppermute | solution.py:430
  64.2 11.9 %collective-permute-start.19 = (bf16[1536,768]{1,0:T(8,128)(2,1)S(1)}, bf16[1536,768]{1,0:T(8,128)(2,1)S(1)}, u32[]{:S(2)}, u32[]{:S(2)}) collective-permute-start(bf16[1536,768]{1,0:T(8,128)(2,1)S(1)} %get-tuple-element.168), channel_id=1, source_target_pairs={{0,8},{8,0},{16,24},{24,16},{1,9},{9,1},{17,25},{25,17},{2,10},{10... | collective-permute-start | bytes 7077896 | tf_op jit(solution)/shard_map/ppermute | solution.py:427
  64.3 13.5 %collective-permute-start.12 = (bf16[144,768]{1,0:T(8,128)(2,1)S(1)}, bf16[144,768]{1,0:T(8,128)(2,1)S(1)}, u32[]{:S(2)}, u32[]{:S(2)}) collective-permute-start(bf16[144,768]{1,0:T(8,128)(2,1)S(1)} %get-tuple-element.146), channel_id=1, source_target_pairs={{0,2},{2,0},{4,6},{6,4},{1,3},{3,1},{5,7},{7,5},{8,10},{10,8},{12,... | collective-permute-start | bytes 663560 | tf_op jit(solution)/shard_map/ppermute | solution.py:430
  66.4 18.7 %collective-permute-start.16 = (bf16[144,768]{1,0:T(8,128)(2,1)S(1)}, bf16[144,768]{1,0:T(8,128)(2,1)S(1)}, u32[]{:S(2)}, u32[]{:S(2)}) collective-permute-start(bf16[144,768]{1,0:T(8,128)(2,1)S(1)} %get-tuple-element.152), channel_id=1, source_target_pairs={{0,4},{2,6},{4,0},{6,2},{1,5},{3,7},{5,1},{7,3},{8,12},{10,14},{12... | collective-permute-start | bytes 663560 | tf_op jit(solution)/shard_map/ppermute | solution.py:430
  67.8 17.3 %collective-permute-start.17 = (bf16[144,768]{1,0:T(8,128)(2,1)S(1)}, bf16[144,768]{1,0:T(8,128)(2,1)S(1)}, u32[]{:S(2)}, u32[]{:S(2)}) collective-permute-start(bf16[144,768]{1,0:T(8,128)(2,1)S(1)} %get-tuple-element.153), channel_id=1, source_target_pairs={{0,6},{2,4},{4,2},{6,0},{1,7},{3,5},{5,3},{7,1},{8,14},{10,12},{12... | collective-permute-start | bytes 663560 | tf_op jit(solution)/shard_map/ppermute | solution.py:430
  68.9 7.2 %collective-permute-start.18 = (bf16[2,72,768]{2,1,0:T(8,128)(2,1)S(1)}, bf16[2,72,768]{2,1,0:T(8,128)(2,1)S(1)}, u32[]{:S(2)}, u32[]{:S(2)}) collective-permute-start(bf16[2,72,768]{2,1,0:T(8,128)(2,1)S(1)} %get-tuple-element.156), channel_id=1, source_target_pairs={{0,16},{8,24},{16,0},{24,8},{1,17},{9,25},{17,1},{25,9},{2,18},{10... | collective-permute-start | bytes 663560 | tf_op jit(solution)/shard_map/ppermute | solution.py:427
  77.8 8.9 %copy-start.17 = (f32[768,768]{1,0:T(8,128)}, f32[768,768]{1,0:T(8,128)S(1)}, u32[]{:S(2)}) copy-start(f32[768,768]{1,0:T(8,128)S(1)} %get-tuple-element.216.kept) | copy-start | bytes 7077892
  86.6 22.2 %copy-start.9 = (bf16[768,3,192]{0,2,1:T(8,128)(2,1)S(1)}, bf16[768,3,192]{0,2,1:T(8,128)(2,1)}, u32[]{:S(2)}) copy-start(bf16[768,3,192]{0,2,1:T(8,128)(2,1)} %param.18) | copy-start | bytes 2654212
  86.6 1.7 collective-permute-start.20
  88.4 9.6 %collective-permute-start.21 = (bf16[416,384]{1,0:T(8,128)(2,1)S(1)}, bf16[416,384]{1,0:T(8,128)(2,1)S(1)}, u32[]{:S(2)}, u32[]{:S(2)}) collective-permute-start(bf16[416,384]{1,0:T(8,128)(2,1)S(1)} %add_convert_fusion.1), channel_id=1, source_target_pairs={{0,16},{8,24},{16,0},{24,8},{1,17},{9,25},{17,1},{25,9},{2,18},{10... | collective-permute-start | bytes 958472 | tf_op jit(solution)/shard_map/ppermute | solution.py:427
  89.0 18.2 %collective-permute-start.22 = (bf16[256,768]{1,0:T(8,128)(2,1)S(1)}, bf16[256,768]{1,0:T(8,128)(2,1)S(1)}, u32[]{:S(2)}, u32[]{:S(2)}) collective-permute-start(bf16[256,768]{1,0:T(8,128)(2,1)S(1)} %get-tuple-element.178), channel_id=1, source_target_pairs={{0,1},{1,0},{2,3},{3,2},{4,5},{5,4},{6,7},{7,6},{8,9},{9,8},{10,11... | collective-permute-start | bytes 1179656 | tf_op jit(solution)/shard_map/ppermute | solution.py:433
  90.5 16.6 %collective-permute-start.23 = (bf16[144,768]{1,0:T(8,128)(2,1)S(1)}, bf16[144,768]{1,0:T(8,128)(2,1)S(1)}, u32[]{:S(2)}, u32[]{:S(2)}) collective-permute-start(bf16[144,768]{1,0:T(8,128)(2,1)S(1)} %get-tuple-element.180), channel_id=1, source_target_pairs={{0,2},{2,0},{4,6},{6,4},{1,3},{3,1},{5,7},{7,5},{8,10},{10,8},{12,... | collective-permute-start | bytes 663560 | tf_op jit(solution)/shard_map/ppermute | solution.py:430
  95.1 8.0 %collective-permute-start.24 = (bf16[72,768]{1,0:T(8,128)(2,1)S(1)}, bf16[72,768]{1,0:T(8,128)(2,1)S(1)}, u32[]{:S(2)}, u32[]{:S(2)}) collective-permute-start(bf16[72,768]{1,0:T(8,128)(2,1)S(1)} %get-tuple-element.181), channel_id=1, source_target_pairs={{0,4},{2,6},{4,0},{6,2},{1,5},{3,7},{5,1},{7,3},{8,12},{10,14},{12... | collective-permute-start | bytes 331784 | tf_op jit(solution)/shard_map/ppermute | solution.py:430
  96.0 11.2 %collective-permute-start.25 = (bf16[72,768]{1,0:T(8,128)(2,1)S(1)}, bf16[72,768]{1,0:T(8,128)(2,1)S(1)}, u32[]{:S(2)}, u32[]{:S(2)}) collective-permute-start(bf16[72,768]{1,0:T(8,128)(2,1)S(1)} %get-tuple-element.182), channel_id=1, source_target_pairs={{0,6},{2,4},{4,2},{6,0},{1,7},{3,5},{5,3},{7,1},{8,14},{10,12},{12... | collective-permute-start | bytes 331784 | tf_op jit(solution)/shard_map/ppermute | solution.py:430
  107.2 1.6 collective-permute-start.26
  113.8 5.3 %collective-permute-start.33 = (bf16[394,384]{1,0:T(8,128)(2,1)S(1)}, bf16[394,384]{1,0:T(8,128)(2,1)S(1)}, u32[]{:S(2)}, u32[]{:S(2)}) collective-permute-start(bf16[394,384]{1,0:T(8,128)(2,1)S(1)} %get-tuple-element.209), channel_id=1, source_target_pairs={{0,8},{8,0},{16,24},{24,16},{1,9},{9,1},{17,25},{25,17},{2,10},{10... | collective-permute-start | bytes 907784 | tf_op jit(solution)/shard_map/ppermute | solution.py:427
  114.0 10.8 %collective-permute-start.29 = (bf16[192,768]{1,0:T(8,128)(2,1)S(1)}, bf16[192,768]{1,0:T(8,128)(2,1)S(1)}, u32[]{:S(2)}, u32[]{:S(2)}) collective-permute-start(bf16[192,768]{1,0:T(8,128)(2,1)S(1)} %get-tuple-element.204), channel_id=1, source_target_pairs={{0,3},{1,2},{2,1},{3,0},{4,7},{5,6},{6,5},{7,4},{8,11},{9,10},{10,... | collective-permute-start | bytes 884744 | tf_op jit(solution)/shard_map/ppermute | solution.py:437
  114.7 15.3 %collective-permute-start.30 = (bf16[192,768]{1,0:T(8,128)(2,1)S(1)}, bf16[192,768]{1,0:T(8,128)(2,1)S(1)}, u32[]{:S(2)}, u32[]{:S(2)}) collective-permute-start(bf16[192,768]{1,0:T(8,128)(2,1)S(1)} %get-tuple-element.205), channel_id=1, source_target_pairs={{0,1},{1,0},{2,3},{3,2},{4,5},{5,4},{6,7},{7,6},{8,9},{9,8},{10,11... | collective-permute-start | bytes 884744 | tf_op jit(solution)/shard_map/ppermute | solution.py:437
  116.2 13.8 %collective-permute-start.31 = (bf16[192,768]{1,0:T(8,128)(2,1)S(1)}, bf16[192,768]{1,0:T(8,128)(2,1)S(1)}, u32[]{:S(2)}, u32[]{:S(2)}) collective-permute-start(bf16[192,768]{1,0:T(8,128)(2,1)S(1)} %get-tuple-element.206), channel_id=1, source_target_pairs={{0,2},{1,3},{2,0},{3,1},{4,6},{5,7},{6,4},{7,5},{8,10},{9,11},{10,... | collective-permute-start | bytes 884744 | tf_op jit(solution)/shard_map/ppermute | solution.py:437
  118.9 11.2 %collective-permute-start.27 = (bf16[400,384]{1,0:T(8,128)(2,1)S(1)}, bf16[400,384]{1,0:T(8,128)(2,1)S(1)}, u32[]{:S(2)}, u32[]{:S(2)}) collective-permute-start(bf16[400,384]{1,0:T(8,128)(2,1)S(1)} %get-tuple-element.202), channel_id=1, source_target_pairs={{0,8},{8,0},{16,24},{24,16},{1,9},{9,1},{17,25},{25,17},{2,10},{10... | collective-permute-start | bytes 921608 | tf_op jit(solution)/shard_map/ppermute | solution.py:427
  119.1 12.7 %collective-permute-start.34 = (bf16[394,384]{1,0:T(8,128)(2,1)S(1)}, bf16[394,384]{1,0:T(8,128)(2,1)S(1)}, u32[]{:S(2)}, u32[]{:S(2)}) collective-permute-start(bf16[394,384]{1,0:T(8,128)(2,1)S(1)} %add_convert_fusion.3), channel_id=1, source_target_pairs={{0,16},{8,24},{16,0},{24,8},{1,17},{9,25},{17,1},{25,9},{2,18},{10... | collective-permute-start | bytes 907784 | tf_op jit(solution)/shard_map/ppermute | solution.py:427
  130.1 4.7 %copy-start.7 = (f32[768]{0:T(1024)S(1)}, f32[768]{0:T(1024)}, u32[]{:S(2)}) copy-start(f32[768]{0:T(1024)} %gain.7) | copy-start | bytes 9220
  130.3 8.8 %collective-permute-start.28 = (bf16[400,384]{1,0:T(8,128)(2,1)S(1)}, bf16[400,384]{1,0:T(8,128)(2,1)S(1)}, u32[]{:S(2)}, u32[]{:S(2)}) collective-permute-start(bf16[400,384]{1,0:T(8,128)(2,1)S(1)} %add_convert_fusion.5), channel_id=1, source_target_pairs={{0,16},{8,24},{16,0},{24,8},{1,17},{9,25},{17,1},{25,9},{2,18},{10... | collective-permute-start | bytes 921608 | tf_op jit(solution)/shard_map/ppermute | solution.py:427
  131.9 2.9 %collective-permute-start.35 = (bf16[394,384]{1,0:T(8,128)(2,1)S(1)}, bf16[394,384]{1,0:T(8,128)(2,1)S(1)}, u32[]{:S(2)}, u32[]{:S(2)}) collective-permute-start(bf16[394,384]{1,0:T(8,128)(2,1)S(1)} %add_convert_fusion.2.own), channel_id=1, source_target_pairs={{0,8},{8,0},{16,24},{24,16},{1,9},{9,1},{17,25},{25,17},{2,10},{10... | collective-permute-start | bytes 907784 | tf_op jit(solution)/shard_map/ppermute | solution.py:427
  132.0 18.1 %collective-permute-start.32 = (bf16[192,768]{1,0:T(8,128)(2,1)S(1)}, bf16[192,768]{1,0:T(8,128)(2,1)S(1)}, u32[]{:S(2)}, u32[]{:S(2)}) collective-permute-start(bf16[192,768]{1,0:T(8,128)(2,1)S(1)} %shard_map.223.own), channel_id=1, source_target_pairs={{0,4},{2,6},{4,0},{6,2},{1,5},{3,7},{5,1},{7,3},{8,12},{10,14},{12... | collective-permute-start | bytes 884744 | tf_op jit(solution)/shard_map/ppermute | solution.py:430
  133.3 23.5 %collective-permute-start.38 = (bf16[512,768]{1,0:T(8,128)(2,1)S(1)}, bf16[512,768]{1,0:T(8,128)(2,1)S(1)}, u32[]{:S(2)}, u32[]{:S(2)}) collective-permute-start(bf16[512,768]{1,0:T(8,128)(2,1)S(1)} %get-tuple-element.218), channel_id=1, source_target_pairs={{0,1},{1,0},{2,3},{3,2},{4,5},{5,4},{6,7},{7,6},{8,9},{9,8},{10,11... | collective-permute-start | bytes 2359304 | tf_op jit(solution)/shard_map/ppermute | solution.py:433
  137.2 13.5 %collective-permute-start.36 = (f32[16,768]{1,0:T(8,128)S(1)}, f32[16,768]{1,0:T(8,128)S(1)}, u32[]{:S(2)}, u32[]{:S(2)}) collective-permute-start(f32[16,768]{1,0:T(8,128)S(1)} %get-tuple-element.212.small), channel_id=1, source_target_pairs={{0,4},{2,6},{4,0},{6,2},{1,5},{3,7},{5,1},{7,3},{8,12},{10,14},{12... | collective-permute-start | bytes 147464 | tf_op jit(solution)/shard_map/ppermute | solution.py:430
  139.9 14.6 %copy-start.3 = (f32[394,768]{1,0:T(8,128)S(1)}, f32[394,768]{1,0:T(8,128)}, u32[]{:S(2)}) copy-start(f32[394,768]{1,0:T(8,128)} %copy-done.2) | copy-start | bytes 3631108
  150.8 3.7 %collective-permute-start.37 = (bf16[400,384]{1,0:T(8,128)(2,1)}, bf16[400,384]{1,0:T(8,128)(2,1)}, u32[]{:S(2)}, u32[]{:S(2)}) collective-permute-start(bf16[400,384]{1,0:T(8,128)(2,1)} %add_convert_fusion.4), channel_id=1, source_target_pairs={{0,8},{8,0},{16,24},{24,16},{1,9},{9,1},{17,25},{25,17},{2,10},{10... | collective-permute-start | bytes 921608 | tf_op jit(solution)/shard_map/ppermute | solution.py:427
  150.9 5.9 %copy-start.18 = (f32[768,768]{1,0:T(8,128)S(1)}, f32[768,768]{1,0:T(8,128)}, u32[]{:S(2)}) copy-start(f32[768,768]{1,0:T(8,128)} %copy-done.17) | copy-start | bytes 7077892
  150.9 9.9 %collective-permute-start.39 = (bf16[208,768]{1,0:T(8,128)(2,1)S(1)}, bf16[208,768]{1,0:T(8,128)(2,1)S(1)}, u32[]{:S(2)}, u32[]{:S(2)}) collective-permute-start(bf16[208,768]{1,0:T(8,128)(2,1)S(1)} %shard_map.225.refs_0_), channel_id=1, source_target_pairs={{0,1},{1,0},{2,3},{3,2},{4,5},{5,4},{6,7},{7,6},{8,9},{9,8},{10,11... | collective-permute-start | bytes 958472 | tf_op jit(solution)/shard_map/ppermute | solution.py:437
  152.1 10.4 %collective-permute-start.40 = (bf16[208,768]{1,0:T(8,128)(2,1)S(1)}, bf16[208,768]{1,0:T(8,128)(2,1)S(1)}, u32[]{:S(2)}, u32[]{:S(2)}) collective-permute-start(bf16[208,768]{1,0:T(8,128)(2,1)S(1)} %shard_map.225.refs_0_), channel_id=1, source_target_pairs={{0,2},{1,3},{2,0},{3,1},{4,6},{5,7},{6,4},{7,5},{8,10},{9,11},{10,... | collective-permute-start | bytes 958472 | tf_op jit(solution)/shard_map/ppermute | solution.py:437
  152.1 16.8 %collective-permute-start.41 = (bf16[208,768]{1,0:T(8,128)(2,1)S(1)}, bf16[208,768]{1,0:T(8,128)(2,1)S(1)}, u32[]{:S(2)}, u32[]{:S(2)}) collective-permute-start(bf16[208,768]{1,0:T(8,128)(2,1)S(1)} %shard_map.225.refs_0_), channel_id=1, source_target_pairs={{0,3},{1,2},{2,1},{3,0},{4,7},{5,6},{6,5},{7,4},{8,11},{9,10},{10,... | collective-permute-start | bytes 958472 | tf_op jit(solution)/shard_map/ppermute | solution.py:437

commit v7 on v6

--- a/solution.py
+++ b/solution.py
@@ -144,11 +144,12 @@
 
 
 def expert_kernel(
-    experts, places, with_grads, ids, up_a, up_b, down_a, down_b, router, pair_out, *refs
+    experts, places, with_grads, ids, up_a, up_b, down_a, down_b, router, *refs
 ):
     number = len(places)
     row_blocks, out_blocks = refs[:number], refs[number : 2 * number]
-    refs = refs[2 * number :]
+    pair_out = refs[2 * number]
+    refs = refs[2 * number + 1 :]
     back_blocks, gated_kept, gated_sent = refs[:number], refs[number], refs[number + 1]
     refs = refs[number + 2 :]
     rows_in, d_result, hidden_a, hidden_b, d_pre_a, d_pre_b, router_part = refs[:7]
@@ -273,14 +274,15 @@
     grad_down[half:, :] = kept[half:, half:] + came[half:, half:].astype(F32)
 
 
-def combine_kernel(experts, parts, base, ids, table, part, *refs):
+def combine_kernel(order, parts, base, ids, table, part, *refs):
+    experts = len(order)
     blocks = refs[:experts]
     routers = refs[experts : experts + parts]
     kept, sent, total = refs[experts + parts :]
     value = dot_tn(table[ids[E_ID]], blocks[0][...])
-    for k in range(1, experts):
-        spots = table if blocks[k].shape[0] == table.shape[1] else part
-        value = value + dot_tn(spots[ids[E_ID] ^ k], blocks[k][...])
+    for block, k in zip(blocks[1:], order[1:]):
+        spots = table if block.shape[0] == table.shape[1] else part
+        value = value + dot_tn(spots[ids[E_ID] ^ k], block[...])
     total[...] = jnp.zeros_like(total)
     total[: value.shape[0], :] = value
     if parts:
@@ -381,14 +383,15 @@
     out[size:, :] = (small[...] + small_came[...]).astype(BF16)
 
 
-def spread_kernel(count, ids, *refs):
+def spread_kernel(masks, ids, *refs):
+    count = len(masks)
     parts = refs[:count]
     grad_qkv, grad_out, gain1, bias1, gain2, bias2, router, grads, held = refs[count:]
     size = grads.shape[0] // count
-    for m in range(count):
-        quarter = ids[Q_ID] ^ m
-        grads[pl.ds(pl.multiple_of(quarter * size, 16), size), :] = parts[m][:size, :].astype(F32)
-        held[quarter] = parts[m][size:, :].astype(F32)
+    for mask, block in zip(masks, parts):
+        quarter = ids[Q_ID] ^ mask
+        grads[pl.ds(pl.multiple_of(quarter * size, 16), size), :] = block[:size, :].astype(F32)
+        held[quarter] = block[size:, :].astype(F32)
     total = held[0]
     for quarter in range(1, count):
         total = total + held[quarter]
@@ -537,7 +540,8 @@
         if small_slice:
             *row_blocks, far_2, far_3 = lax.optimization_barrier((*row_blocks, *d_rows_in[2:]))
             d_rows_in[2:] = [far_2, far_3]
-            d_rows_in[1] = expert_swap(after(d_rows_in[1], middle), 1)
+            d_rows_in[1], middle = lax.optimization_barrier((d_rows_in[1], middle))
+            d_rows_in[1] = expert_swap(d_rows_in[1], 1)
             pair_out = tensor_swap(jnp.stack([far_2, far_3]), 2)
         else:
             pair_out = router
@@ -562,9 +566,9 @@
                 + grads,
                 [ids, up_a, up_b, down_a, down_b]
                 + [router]
-                + [pair_out if worked or not small_slice else router]
                 + [rows_in[k] for k in call]
-                + [d_rows_in[k] for k in call],
+                + [d_rows_in[k] for k in call]
+                + [pair_out if worked or not small_slice else router],
                 scratch=[((count, width), F32)],
                 micros=0.05,
                 limit=24,
@@ -573,15 +577,20 @@
             gated.append(results[len(call) : len(call) + 2])
             worked.append(results[len(call) + 2 :])
 
+        order = [0] + list(range(experts - 1, 0, -1))
+
         def combine(blocks, routers):
+            blocks = [blocks[k] for k in order]
             return run(
-                functools.partial(combine_kernel, experts, len(routers), base),
+                functools.partial(combine_kernel, order, len(routers), base),
                 [((tall if routers else base, half), BF16)] * 2,
                 [ids, table, part] + blocks + routers,
                 scratch=[((tall if routers else base, width), F32)],
                 micros=2,
             )
 
+        if small_slice:
+            d_back[1], d_back[2] = lax.optimization_barrier((d_back[1], d_back[2]))
         d_home = exchange(d_back)
 
         grad_own, grad_pair = run(
@@ -607,18 +616,23 @@
                 [((quarter, width), BF16)] * 2,
                 [gated[1][0], tensor_swap(gated[1][1], 2)],
             )
-            gated_blocks = [gated[0][0][0], gated[0][0][1], *far_blocks]
+            gated_blocks = [gated[0][0][0], expert_swap(gated[0][0][1], 1), *far_blocks]
         else:
             gated_blocks = [gated[0][0][k] for k in range(experts)]
 
-        *d_home, sent_first = lax.optimization_barrier((*d_home, *gated_blocks, sent_first))
-        d_home, gated_blocks = d_home[:experts], d_home[experts:]
+        *gated_blocks, sent_first = lax.optimization_barrier(
+            (*d_home[::-1], *gated_blocks, sent_first)
+        )
+        d_home, gated_blocks = gated_blocks[:experts][::-1], gated_blocks[experts:]
         kept, sent = combine(list(d_home), [one[6] for one in worked])
         chip = (kept.astype(F32) + tensor_swap(sent, 1).astype(F32)).astype(BF16)
         own = (chip.astype(F32) + tensor_swap(chip, 2).astype(F32)).astype(BF16)
-        gated_home = exchange(list(gated_blocks))
+        if small_slice:
+            gated_home = gated_blocks[:2] + [expert_swap(gated_blocks[k], k) for k in (3, 2)][::-1]
+        else:
+            gated_home = exchange(list(gated_blocks))
         came_first = dp_swap(sent_first)
-        own, came_first, *gated_home = lax.optimization_barrier((own, came_first, *gated_home))
+        own, *gated_home, came_first = lax.optimization_barrier((own, *gated_home, came_first))
         other = tensor_swap(own, 1)
 
         parts = 4 if small_slice else 1
@@ -674,11 +688,11 @@
                 micros=1,
             )
             own_y, ready = lax.optimization_barrier((own_y, ready))
-            everything = [quarter_swap(ready, m) for m in (1, 2, 3)]
+            everything = [quarter_swap(ready, m) for m in (3, 1, 2)]
             ready, grad_up, grad_down = lax.optimization_barrier((ready, grad_up, grad_down))
             everything = [ready] + everything
             grad_qkv, grad_out, *sums, grad_router = run(
-                functools.partial(spread_kernel, 4),
+                functools.partial(spread_kernel, (0, 3, 1, 2)),
                 [((3 * inner, width), F32), ((inner, width), F32)]
                 + [((width,), F32)] * 4
                 + [((experts, width), F32)],

time: 171 us -> 169 us (0.988)
  starting transfers between devices: 48.3 us -> 45 us
    ppermute x14, waiting for transfers between devices: 41.9 us -> 38.3 us  [expert_swap(): lax.ppermute(value, 'expert', [(i, i ^ mask) for i in range(n_expert)])]
    ppermute x20, waiting for transfers between devices: 14.9 us -> 18.4 us  [tensor_swap(): lax.ppermute(value, 'tensor', [(i, i ^ mask) for i in range(n_tensor)])]
    ppermute x14, starting transfers between devices: 25.5 us -> 23 us  [expert_swap(): lax.ppermute(value, 'expert', [(i, i ^ mask) for i in range(n_expert)])]
  transfers between devices with their start and end apart: 42 -> 42, of which waited for: 21 -> 21; matrix products, arithmetic and copies ran while one was open for 2% -> 2% of each run, Pallas kernels for 12% -> 13%
where the time goes in v7:
time: 169 us; the launch traced here: 168 us
  waiting for transfers between devices  77 us (46%)
  starting transfers between devices  45 us (27%)
  Pallas kernels  37.2 us (22%)
  local copies, waits for them, and re-layouts  3.81 us (2%)
  other arithmetic  3.55 us (2%)
  between operations  1.71 us (1%)
    ppermute x14, waiting for transfers between devices, expert_swap(): lax.ppermute(value, 'expert', [(i, i ^ mask) for i in range(n_expert)])  38.3 us
    pallas_call x16, Pallas kernels, run(): pl.pallas_call(kernel, out_shape=[jax.ShapeDtypeStruct(shape, kind) for s...  37.2 us
    ppermute x14, starting transfers between devices, expert_swap(): lax.ppermute(value, 'expert', [(i, i ^ mask) for i in range(n_expert)])  23 us
    ppermute x6, waiting for transfers between devices, quarter_swap(): return lax.ppermute(value, ('expert', 'dp'), pairs)  20.3 us
    ppermute x20, waiting for transfers between devices, tensor_swap(): lax.ppermute(value, 'tensor', [(i, i ^ mask) for i in range(n_tensor)])  18.4 us
    ppermute x20, starting transfers between devices, tensor_swap(): lax.ppermute(value, 'tensor', [(i, i ^ mask) for i in range(n_tensor)])  12 us
    ppermute x6, starting transfers between devices, quarter_swap(): return lax.ppermute(value, ('expert', 'dp'), pairs)  7.05 us
    unnamed x38, local copies, waits for them, and re-layouts  3.69 us
  transfers between devices with their start and end apart: 42, of which 21 were waited for; matrix products, arithmetic and copies ran while one was open for 2% of the time, Pallas kernels for 13%

profile of v7, /device:TPU:0, one launch (start us, length us, event | category | flops | bytes accessed | tf_op | source)
XLA Modules:
  0.0 168.2 jit_solution(8765655680504623220)
XLA Ops:
  0.6 0.5 collective-permute-start.2
  1.2 2.9 %collective-permute-start = (bf16[192,768]{1,0:T(8,128)(2,1)}, bf16[192,768]{1,0:T(8,128)(2,1)S(1)}, u32[]{:S(2)}, u32[]{:S(2)}) collective-permute-start(bf16[192,768]{1,0:T(8,128)(2,1)} %w_out.1), channel_id=1, source_target_pairs={{0,16},{8,24},{16,0},{24,8},{1,17},{9,25},{17,1},{25,9},{2,18},{10... | collective-permute-start | bytes 884744 | tf_op jit(solution)/shard_map/ppermute | solution.py:430
  4.9 1.1 copy-done.4
  6.0 0.7 copy-done.6
  6.7 1.2 copy-done.8
  7.8 0.7 copy-done.13
  8.5 2.5 %shard_map.212 = (bf16[394,768]{1,0:T(8,128)(2,1)S(1)}, bf16[394,192]{1,0:T(8,128)(2,1)S(1)}, bf16[394,192]{1,0:T(8,128)(2,1)S(1)}, bf16[394,192]{1,0:T(8,128)(2...) custom-call(bf16[394,768]{1,0:T(8,128)(2,1)S(1)} %copy-done.4, f32[768]{0:T(1024)S(1)} %copy-done.6, ...), custom_call_target="tpu_custom_call" | custom-call | flops 4600000000 | bytes 1024 | tf_op jit(solution)/shard_map/pallas_call | solution.py:413
  11.1 0.6 collective-permute-done.rest_6_
  11.7 1.8 %collective-permute-start.5 = (bf16[394,192]{1,0:T(8,128)(2,1)S(1)}, bf16[394,192]{1,0:T(8,128)(2,1)S(1)}, u32[]{:S(2)}, u32[]{:S(2)}) collective-permute-start(bf16[394,192]{1,0:T(8,128)(2,1)S(1)} %get-tuple-element.125.rest_0_.head_out), channel_id=1, source_target_pairs={{0,16},{8,24},{16,0},{24,8},{1,17},{9,25},{17,1},{25,9},{2,18},{10... | collective-permute-start | bytes 453896 | tf_op jit(solution)/shard_map/ppermute | solution.py:430
  13.7 1.4 shard_map.213
  15.1 4.1 %collective-permute-done.5.rest_2_ = bf16[394,192]{1,0:T(8,128)(2,1)S(1)} collective-permute-done((bf16[394,192]{1,0:T(8,128)(2,1)S(1)}, bf16[394,192]{1,0:T(8,128)(2,1)S(1)}, u32[]{:S(2)}, u32[]{:S(2)}) %collective-permute-start.5) | collective-permute-done | bytes 151328 | tf_op jit(solution)/shard_map/ppermute | solution.py:430
  19.2 2.8 %collective-permute-start.8 = (bf16[72,768]{1,0:T(8,128)(2,1)S(1)}, bf16[72,768]{1,0:T(8,128)(2,1)S(1)}, u32[]{:S(2)}, u32[]{:S(2)}) collective-permute-start(bf16[72,768]{1,0:T(8,128)(2,1)S(1)} %get-tuple-element.142), channel_id=1, source_target_pairs={{0,4},{2,6},{4,0},{6,2},{1,5},{3,7},{5,1},{7,3},{8,12},{10,14},{12... | collective-permute-start | bytes 331784 | tf_op jit(solution)/shard_map/ppermute | solution.py:433
  22.0 1.3 collective-permute-start.9
  23.5 2.7 %shard_map.214 = (f32[394,768]{1,0:T(8,128)S(1)}, bf16[144,768]{1,0:T(8,128)(2,1)S(1)}, bf16[144,768]{1,0:T(8,128)(2,1)S(1)}, bf16[144,768]{1,0:T(8,128)(2,1)S(1)}, bf16[144,768]{1,0:T(8,128)(2,1)S(1)}) custom-call(s32[8]{0:T(128)S(1)} %stack.38.ids, bf16[394,768]{1,0:T(8,128)(2,1)S(1)} %copy-done.5, f32[768]{0:T(1024)S(1)} %copy-done.16, ...), custom_call_target="tpu_custom_call" | custom-call | flops 3449999872 | bytes 1024 | tf_op jit(solution)/shard_map/pallas_call | solution.py:413
  26.2 4.6 %collective-permute-done.8.refs_2_ = bf16[72,768]{1,0:T(8,128)(2,1)S(1)} collective-permute-done((bf16[72,768]{1,0:T(8,128)(2,1)S(1)}, bf16[72,768]{1,0:T(8,128)(2,1)S(1)}, u32[]{:S(2)}, u32[]{:S(2)}) %collective-permute-start.8) | collective-permute-done | bytes 110624 | tf_op jit(solution)/shard_map/ppermute | solution.py:433
  30.8 2.9 %collective-permute-start.10 = (bf16[144,768]{1,0:T(8,128)(2,1)S(1)}, bf16[144,768]{1,0:T(8,128)(2,1)S(1)}, u32[]{:S(2)}, u32[]{:S(2)}) collective-permute-start(bf16[144,768]{1,0:T(8,128)(2,1)S(1)} %get-tuple-element.145), channel_id=1, source_target_pairs={{0,2},{2,0},{4,6},{6,4},{1,3},{3,1},{5,7},{7,5},{8,10},{10,8},{12,... | collective-permute-start | bytes 663560 | tf_op jit(solution)/shard_map/ppermute | solution.py:433
  33.7 3.9 %collective-permute-start.12 = (bf16[144,768]{1,0:T(8,128)(2,1)S(1)}, bf16[144,768]{1,0:T(8,128)(2,1)S(1)}, u32[]{:S(2)}, u32[]{:S(2)}) collective-permute-start(bf16[144,768]{1,0:T(8,128)(2,1)S(1)} %get-tuple-element.150), channel_id=1, source_target_pairs={{0,4},{2,6},{4,0},{6,2},{1,5},{3,7},{5,1},{7,3},{8,12},{10,14},{12... | collective-permute-start | bytes 663560 | tf_op jit(solution)/shard_map/ppermute | solution.py:433
  37.6 0.5 collective-permute-start.13
  38.0 1.6 collective-permute-start.14
  39.6 5.0 %collective-permute-done.10.refs_1_ = bf16[144,768]{1,0:T(8,128)(2,1)S(1)} collective-permute-done((bf16[144,768]{1,0:T(8,128)(2,1)S(1)}, bf16[144,768]{1,0:T(8,128)(2,1)S(1)}, u32[]{:S(2)}, u32[]{:S(2)}) %collective-permute-start.10) | collective-permute-done | bytes 221216 | tf_op jit(solution)/shard_map/ppermute | solution.py:433
  44.6 4.2 %collective-permute-done.11.refs_3_ = bf16[144,768]{1,0:T(8,128)(2,1)S(1)} collective-permute-done((bf16[144,768]{1,0:T(8,128)(2,1)S(1)}, bf16[144,768]{1,0:T(8,128)(2,1)S(1)}, u32[]{:S(2)}, u32[]{:S(2)}) %collective-permute-start.11) | collective-permute-done | bytes 221216 | tf_op jit(solution)/shard_map/ppermute | solution.py:433
  48.8 7.0 %shard_map.215 = (bf16[144,768]{1,0:T(8,128)(2,1)S(1)}, bf16[144,768]{1,0:T(8,128)(2,1)S(1)}, bf16[2,144,768]{2,1,0:T(8,128)(2,1)S(1)}, bf16[2,144,768]{2,1,0:T(...) custom-call(s32[8]{0:T(128)S(1)} %stack.38.ids, ...), custom_call_target="tpu_custom_call" | custom-call | flops 57500000 | bytes 1024 | tf_op jit(solution)/shard_map/pallas_call | solution.py:413
  55.8 0.9 collective-permute-done.13.refs_1_
  56.7 4.8 %shard_map.216 = (bf16[144,768]{1,0:T(8,128)(2,1)S(1)}, bf16[144,768]{1,0:T(8,128)(2,1)S(1)}, bf16[2,72,768]{2,1,0:T(8,128)(2,1)S(1)}, bf16[2,72,768]{2,1,0:T(8,...) custom-call(s32[8]{0:T(128)S(1)} %stack.38.ids, ...), custom_call_target="tpu_custom_call" | custom-call | flops 57500000 | bytes 1024 | tf_op jit(solution)/shard_map/pallas_call | solution.py:413
  61.5 2.7 %shard_map.218 = (bf16[1536,768]{1,0:T(8,128)(2,1)S(1)}, bf16[1536,768]{1,0:T(8,128)(2,1)S(1)}) custom-call(bf16[288,768]{1,0:T(8,128)(2,1)S(1)} %get-tuple-element.165.refs_0_, bf16[288,768]{1,0:T(8,128)(2,1)S(1)} %get-tuple-element.166.refs_1_, bf16[288,768]{1,0:T(8,128)(2,1)S(1)} %get-tuple-element.167.refs_2_, ...), custom_call_target="tpu_custom_call" | custom-call | flops 4600000000 | bytes 1024 | tf_op jit(solution)/shard_map/pallas_call | solution.py:413
  64.3 3.2 %collective-permute-start.15 = (bf16[144,768]{1,0:T(8,128)(2,1)S(1)}, bf16[144,768]{1,0:T(8,128)(2,1)S(1)}, u32[]{:S(2)}, u32[]{:S(2)}) collective-permute-start(bf16[144,768]{1,0:T(8,128)(2,1)S(1)} %get-tuple-element.154), channel_id=1, source_target_pairs={{0,6},{2,4},{4,2},{6,0},{1,7},{3,5},{5,3},{7,1},{8,14},{10,12},{12... | collective-permute-start | bytes 663560 | tf_op jit(solution)/shard_map/ppermute | solution.py:433
  67.5 1.2 collective-permute-start.17
  68.7 1.5 collective-permute-start.19
  70.3 5.4 %collective-permute-done.19.came = bf16[2,72,768]{2,1,0:T(8,128)(2,1)S(1)} collective-permute-done((bf16[2,72,768]{2,1,0:T(8,128)(2,1)S(1)}, bf16[2,72,768]{2,1,0:T(8,128)(2,1)S(1)}, u32[]{:S(2)}, u32[]{:S(2)}) %collective-permute-start.19) | collective-permute-done | bytes 221216 | tf_op jit(solution)/shard_map/ppermute | solution.py:430
  75.7 1.1 collective-permute-start.18
  76.8 1.6 shard_map.219
  78.5 8.2 %collective-permute-done.16.refs_2_ = bf16[144,768]{1,0:T(8,128)(2,1)S(1)} collective-permute-done((bf16[144,768]{1,0:T(8,128)(2,1)S(1)}, bf16[144,768]{1,0:T(8,128)(2,1)S(1)}, u32[]{:S(2)}, u32[]{:S(2)}) %collective-permute-start.16) | collective-permute-done | bytes 221216 | tf_op jit(solution)/shard_map/ppermute | solution.py:433
  86.7 1.6 collective-permute-done.18.refs_3_
  88.2 1.5 shard_map.220
  89.8 1.6 collective-permute-done.21
  91.5 1.6 collective-permute-start.22
  93.1 1.5 collective-permute-start.25
  94.6 1.2 collective-permute-start.23
  95.8 2.5 %collective-permute-start.24 = (bf16[72,768]{1,0:T(8,128)(2,1)S(1)}, bf16[72,768]{1,0:T(8,128)(2,1)S(1)}, u32[]{:S(2)}, u32[]{:S(2)}) collective-permute-start(bf16[72,768]{1,0:T(8,128)(2,1)S(1)} %get-tuple-element.187), channel_id=1, source_target_pairs={{0,6},{2,4},{4,2},{6,0},{1,7},{3,5},{5,3},{7,1},{8,14},{10,12},{12... | collective-permute-start | bytes 331784 | tf_op jit(solution)/shard_map/ppermute | solution.py:433
  98.3 2.9 %collective-permute-done.22 = bf16[416,384]{1,0:T(8,128)(2,1)S(1)} collective-permute-done((bf16[416,384]{1,0:T(8,128)(2,1)S(1)}, bf16[416,384]{1,0:T(8,128)(2,1)S(1)}, u32[]{:S(2)}, u32[]{:S(2)}) %collective-permute-start.22) | collective-permute-done | bytes 319520 | tf_op jit(solution)/shard_map/ppermute | solution.py:430
  101.2 4.5 %collective-permute-done.23.refs_2_ = bf16[72,768]{1,0:T(8,128)(2,1)S(1)} collective-permute-done((bf16[72,768]{1,0:T(8,128)(2,1)S(1)}, bf16[72,768]{1,0:T(8,128)(2,1)S(1)}, u32[]{:S(2)}, u32[]{:S(2)}) %collective-permute-start.23) | collective-permute-done | bytes 110624 | tf_op jit(solution)/shard_map/ppermute | solution.py:433
  105.7 1.6 collective-permute-done.26.other
  107.3 5.0 %shard_map.221 = (f32[394,768]{1,0:T(8,128)S(1)}, bf16[394,384]{1,0:T(8,128)(2,1)S(1)}, bf16[394,384]{1,0:T(8,128)(2,1)S(1)}, f32[16,768]{1,0:T(8,128)S(1)}, bf1...) custom-call(s32[8]{0:T(128)S(1)} %stack.38.ids, ...), custom_call_target="tpu_custom_call" | custom-call | flops 6899999744 | bytes 1024 | tf_op jit(solution)/shard_map/pallas_call | solution.py:413
  112.5 2.0 %collective-permute-start.29 = (bf16[192,768]{1,0:T(8,128)(2,1)S(1)}, bf16[192,768]{1,0:T(8,128)(2,1)S(1)}, u32[]{:S(2)}, u32[]{:S(2)}) collective-permute-start(bf16[192,768]{1,0:T(8,128)(2,1)S(1)} %get-tuple-element.210), channel_id=1, source_target_pairs={{0,3},{1,2},{2,1},{3,0},{4,7},{5,6},{6,5},{7,4},{8,11},{9,10},{10,... | collective-permute-start | bytes 884744 | tf_op jit(solution)/shard_map/ppermute | solution.py:440
  114.5 1.5 collective-permute-start.30
  116.0 1.4 shard_map.222
  117.6 0.6 collective-permute-start.34
  118.2 5.1 %collective-permute-done.29.refs_1_ = bf16[192,768]{1,0:T(8,128)(2,1)S(1)} collective-permute-done((bf16[192,768]{1,0:T(8,128)(2,1)S(1)}, bf16[192,768]{1,0:T(8,128)(2,1)S(1)}, u32[]{:S(2)}, u32[]{:S(2)}) %collective-permute-start.29) | collective-permute-done | bytes 294944 | tf_op jit(solution)/shard_map/ppermute | solution.py:440
  123.3 5.7 %collective-permute-done.30.refs_2_ = bf16[192,768]{1,0:T(8,128)(2,1)S(1)} collective-permute-done((bf16[192,768]{1,0:T(8,128)(2,1)S(1)}, bf16[192,768]{1,0:T(8,128)(2,1)S(1)}, u32[]{:S(2)}, u32[]{:S(2)}) %collective-permute-start.30) | collective-permute-done | bytes 294944 | tf_op jit(solution)/shard_map/ppermute | solution.py:440
  129.3 0.6 collective-permute-start.28
  130.0 1.8 %collective-permute-start.32 = (bf16[192,768]{1,0:T(8,128)(2,1)S(1)}, bf16[192,768]{1,0:T(8,128)(2,1)S(1)}, u32[]{:S(2)}, u32[]{:S(2)}) collective-permute-start(bf16[192,768]{1,0:T(8,128)(2,1)S(1)} %shard_map.223.own), channel_id=1, source_target_pairs={{0,4},{2,6},{4,0},{6,2},{1,5},{3,7},{5,1},{7,3},{8,12},{10,14},{12... | collective-permute-start | bytes 884744 | tf_op jit(solution)/shard_map/ppermute | solution.py:433
  131.9 1.5 collective-permute-start.38
  133.4 2.4 %shard_map.224 = (bf16[394,768]{1,0:T(8,128)(2,1)}, f32[16,768]{1,0:T(8,128)S(1)}) custom-call(s32[8]{0:T(128)S(1)} %stack.38.ids, bf16[394,384]{1,0:T(8,128)(2,1)S(1)} %add_convert_fusion.2.own, bf16[394,384]{1,0:T(8,128)(2,1)S(1)} %collective-permute-done.35.other, bf16[394,768]{1,0:T(8,128)(2,1)S(1)} %copy-done.5, ...), custom_call_target="tpu_custom_call" | custom-call | flops 11500000 | bytes 1024 | tf_op jit(solution)/shard_map/pallas_call | solution.py:413
  136.2 2.3 %collective-permute-done.28 = bf16[400,384]{1,0:T(8,128)(2,1)S(1)} collective-permute-done((bf16[400,384]{1,0:T(8,128)(2,1)S(1)}, bf16[400,384]{1,0:T(8,128)(2,1)S(1)}, u32[]{:S(2)}, u32[]{:S(2)}) %collective-permute-start.28) | collective-permute-done | bytes 307232 | tf_op jit(solution)/shard_map/ppermute | solution.py:430
  138.5 0.8 add_convert_fusion.4
  139.3 8.9 %collective-permute-done.32.came = bf16[192,768]{1,0:T(8,128)(2,1)S(1)} collective-permute-done((bf16[192,768]{1,0:T(8,128)(2,1)S(1)}, bf16[192,768]{1,0:T(8,128)(2,1)S(1)}, u32[]{:S(2)}, u32[]{:S(2)}) %collective-permute-start.32) | collective-permute-done | bytes 294944 | tf_op jit(solution)/shard_map/ppermute | solution.py:433
  148.2 0.6 collective-permute-done.36.small_came
  149.1 0.9 collective-permute-start.40
  149.9 2.6 %collective-permute-start.41 = (bf16[208,768]{1,0:T(8,128)(2,1)S(1)}, bf16[208,768]{1,0:T(8,128)(2,1)S(1)}, u32[]{:S(2)}, u32[]{:S(2)}) collective-permute-start(bf16[208,768]{1,0:T(8,128)(2,1)S(1)} %shard_map.225.refs_0_), channel_id=1, source_target_pairs={{0,2},{1,3},{2,0},{3,1},{4,6},{5,7},{6,4},{7,5},{8,10},{9,11},{10,... | collective-permute-start | bytes 958472 | tf_op jit(solution)/shard_map/ppermute | solution.py:440
  152.5 2.3 %select_convert_fusion = bf16[394,768]{1,0:T(8,128)(2,1)} fusion(f32[394,768]{1,0:T(8,128)S(1)} %copy-done.3, bf16[400,384]{1,0:T(8,128)(2,1)} %collective-permute-done.37, bf16[400,384]{1,0:T(8,128)(2,1)} %add_convert_fusion.4, pred[394]{0:T(512)(128)(4,1)S(1)} %iota_compare_fusion, pred[]{:T(512)S(6)} %eq.7), kind=kLoop, calls=%fused_computation | loop fusion | flops 3933696 | bytes 2430347 | tf_op jit(solution)/shard_map/convert_element_type | solution.py:716
  154.9 1.7 %shard_map.226 = (f32[384,768]{1,0:T(8,128)}, f32[768,384]{1,0:T(8,128)}) custom-call(f32[768,768]{1,0:T(8,128)S(1)} %copy-done.18, bf16[256,768]{1,0:T(8,128)(2,1)S(1)} %collective-permute-done.25.came_first, bf16[512,768]{1,0:T(8,128)(2,1)S(1)} %collective-permute-done.38.came_rest), custom_call_target="tpu_custom_call" | custom-call | flops 2300000000 | bytes 1024 | tf_op jit(solution)/shard_map/pallas_call | solution.py:413
  156.6 3.8 %collective-permute-done.39.refs_1_ = bf16[208,768]{1,0:T(8,128)(2,1)S(1)} collective-permute-done((bf16[208,768]{1,0:T(8,128)(2,1)S(1)}, bf16[208,768]{1,0:T(8,128)(2,1)S(1)}, u32[]{:S(2)}, u32[]{:S(2)}) %collective-permute-start.39) | collective-permute-done | bytes 319520 | tf_op jit(solution)/shard_map/ppermute | solution.py:440
  160.3 5.5 %collective-permute-done.40.refs_2_ = bf16[208,768]{1,0:T(8,128)(2,1)S(1)} collective-permute-done((bf16[208,768]{1,0:T(8,128)(2,1)S(1)}, bf16[208,768]{1,0:T(8,128)(2,1)S(1)}, u32[]{:S(2)}, u32[]{:S(2)}) %collective-permute-start.40) | collective-permute-done | bytes 319520 | tf_op jit(solution)/shard_map/ppermute | solution.py:440
  166.1 2.2 %shard_map.227 = (f32[576,768]{1,0:T(8,128)}, f32[192,768]{1,0:T(8,128)}, f32[768]{0:T(1024)}, f32[768]{0:T(1024)}, f32[768]{0:T(1024)}, /*index=5*/f32[768]{0:T(1024)}, f32[4,768]{1,0:T(4,128)}) custom-call(s32[8]{0:T(128)S(1)} %stack.38.ids, bf16[208,768]{1,0:T(8,128)(2,1)S(1)} %shard_map.225.refs_0_, ...), custom_call_target="tpu_custom_call" | custom-call | flops 3449999872 | bytes 1024 | tf_op jit(solution)/shard_map/pallas_call | solution.py:413
  (85 shorter events, 2.6 us)
Async XLA Ops:
  0.6 11.0 %collective-permute-start.2 = (bf16[768,768]{1,0:T(8,128)(2,1)}, bf16[768,768]{1,0:T(8,128)(2,1)S(1)}, u32[]{:S(2)}, u32[]{:S(2)}) collective-permute-start(bf16[768,768]{1,0:T(8,128)(2,1)} %bitcast.26), channel_id=1, source_target_pairs={{0,8},{8,0},{16,24},{24,16},{1,9},{9,1},{17,25},{25,17},{2,10},{10... | collective-permute-start | bytes 3538952 | tf_op jit(solution)/shard_map/ppermute | solution.py:430
  1.2 10.5 %collective-permute-start.3 = (bf16[768,768]{1,0:T(8,128)(2,1)}, bf16[768,768]{1,0:T(8,128)(2,1)S(1)}, u32[]{:S(2)}, u32[]{:S(2)}) collective-permute-start(bf16[768,768]{1,0:T(8,128)(2,1)} %bitcast.29), channel_id=1, source_target_pairs={{0,8},{8,0},{16,24},{24,16},{1,9},{9,1},{17,25},{25,17},{2,10},{10... | collective-permute-start | bytes 3538952 | tf_op jit(solution)/shard_map/ppermute | solution.py:430
  1.2 10.4 %collective-permute-start = (bf16[192,768]{1,0:T(8,128)(2,1)}, bf16[192,768]{1,0:T(8,128)(2,1)S(1)}, u32[]{:S(2)}, u32[]{:S(2)}) collective-permute-start(bf16[192,768]{1,0:T(8,128)(2,1)} %w_out.1), channel_id=1, source_target_pairs={{0,16},{8,24},{16,0},{24,8},{1,17},{9,25},{17,1},{25,9},{2,18},{10... | collective-permute-start | bytes 884744 | tf_op jit(solution)/shard_map/ppermute | solution.py:430
  4.2 7.5 %collective-permute-start.1 = (bf16[192,768]{1,0:T(8,128)(2,1)}, bf16[192,768]{1,0:T(8,128)(2,1)S(1)}, u32[]{:S(2)}, u32[]{:S(2)}) collective-permute-start(bf16[192,768]{1,0:T(8,128)(2,1)} %w_out.1), channel_id=1, source_target_pairs={{0,8},{8,0},{16,24},{24,16},{1,9},{9,1},{17,25},{25,17},{2,10},{10... | collective-permute-start | bytes 884744 | tf_op jit(solution)/shard_map/ppermute | solution.py:430
  4.9 1.1 copy-start.4
  6.0 0.7 copy-start.6
  6.7 1.2 copy-start.8
  7.8 0.7 copy-start.13
  8.5 5.2 %copy-start.10 = (bf16[394,768]{1,0:T(8,128)(2,1)S(1)}, bf16[394,768]{1,0:T(8,128)(2,1)}, u32[]{:S(2)}) copy-start(bf16[394,768]{1,0:T(8,128)(2,1)} %cot.3) | copy-start | bytes 1815556
  8.5 5.2 %copy-start.12 = (bf16[768,4]{0,1:T(4,128)(2,1)S(1)}, bf16[768,4]{0,1:T(4,128)(2,1)}, u32[]{:S(2)}) copy-start(bf16[768,4]{0,1:T(4,128)(2,1)} %param.22) | copy-start | bytes 18436
  8.5 5.2 %copy-start.14 = (s32[394,2]{0,1:T(2,128)S(1)}, s32[394,2]{0,1:T(2,128)}, u32[]{:S(2)}) copy-start(s32[394,2]{0,1:T(2,128)} %param.14) | copy-start | bytes 9460
  11.6 11.8 %collective-permute-start.4 = (bf16[394,192]{1,0:T(8,128)(2,1)S(1)}, bf16[394,192]{1,0:T(8,128)(2,1)S(1)}, u32[]{:S(2)}, u32[]{:S(2)}) collective-permute-start(bf16[394,192]{1,0:T(8,128)(2,1)S(1)} %get-tuple-element.125.rest_0_.head_out), channel_id=1, source_target_pairs={{0,8},{8,0},{16,24},{24,16},{1,9},{9,1},{17,25},{25,17},{2,10},{10... | collective-permute-start | bytes 453896 | tf_op jit(solution)/shard_map/ppermute | solution.py:430
  11.7 7.5 %collective-permute-start.5 = (bf16[394,192]{1,0:T(8,128)(2,1)S(1)}, bf16[394,192]{1,0:T(8,128)(2,1)S(1)}, u32[]{:S(2)}, u32[]{:S(2)}) collective-permute-start(bf16[394,192]{1,0:T(8,128)(2,1)S(1)} %get-tuple-element.125.rest_0_.head_out), channel_id=1, source_target_pairs={{0,16},{8,24},{16,0},{24,8},{1,17},{9,25},{17,1},{25,9},{2,18},{10... | collective-permute-start | bytes 453896 | tf_op jit(solution)/shard_map/ppermute | solution.py:430
  13.5 9.9 %collective-permute-start.7 = (bf16[192,768]{1,0:T(8,128)(2,1)S(1)}, bf16[192,768]{1,0:T(8,128)(2,1)S(1)}, u32[]{:S(2)}, u32[]{:S(2)}) collective-permute-start(bf16[192,768]{1,0:T(8,128)(2,1)S(1)} %collective-permute-done.rest_6_), channel_id=1, source_target_pairs={{0,8},{8,0},{16,24},{24,16},{1,9},{9,1},{17,25},{25,17},{2,10},{10... | collective-permute-start | bytes 884744 | tf_op jit(solution)/shard_map/ppermute | solution.py:430
  13.7 9.7 %copy-start.5 = (bf16[394,768]{1,0:T(8,128)(2,1)S(1)}, bf16[394,768]{1,0:T(8,128)(2,1)}, u32[]{:S(2)}) copy-start(bf16[394,768]{1,0:T(8,128)(2,1)} %tokens.5) | copy-start | bytes 1815556
  13.7 9.7 %copy-start.11 = (bf16[192,768]{1,0:T(8,128)(2,1)S(1)}, bf16[192,768]{1,0:T(8,128)(2,1)}, u32[]{:S(2)}) copy-start(bf16[192,768]{1,0:T(8,128)(2,1)} %w_out.1) | copy-start | bytes 884740
  13.7 9.7 %copy-start.15 = (f32[768]{0:T(1024)S(1)}, f32[768]{0:T(1024)}, u32[]{:S(2)}) copy-start(f32[768]{0:T(1024)} %bias.3) | copy-start | bytes 9220
  13.7 9.7 %copy-start.16 = (f32[768]{0:T(1024)S(1)}, f32[768]{0:T(1024)}, u32[]{:S(2)}) copy-start(f32[768]{0:T(1024)} %gain.6) | copy-start | bytes 9220
  19.2 4.2 %collective-permute-start.6 = (bf16[394,192]{1,0:T(8,128)(2,1)S(1)}, bf16[394,192]{1,0:T(8,128)(2,1)S(1)}, u32[]{:S(2)}, u32[]{:S(2)}) collective-permute-start(bf16[394,192]{1,0:T(8,128)(2,1)S(1)} %collective-permute-done.5.rest_2_), channel_id=1, source_target_pairs={{0,8},{8,0},{16,24},{24,16},{1,9},{9,1},{17,25},{25,17},{2,10},{10... | collective-permute-start | bytes 453896 | tf_op jit(solution)/shard_map/ppermute | solution.py:430
  19.2 11.6 %collective-permute-start.8 = (bf16[72,768]{1,0:T(8,128)(2,1)S(1)}, bf16[72,768]{1,0:T(8,128)(2,1)S(1)}, u32[]{:S(2)}, u32[]{:S(2)}) collective-permute-start(bf16[72,768]{1,0:T(8,128)(2,1)S(1)} %get-tuple-element.142), channel_id=1, source_target_pairs={{0,4},{2,6},{4,0},{6,2},{1,5},{3,7},{5,1},{7,3},{8,12},{10,14},{12... | collective-permute-start | bytes 331784 | tf_op jit(solution)/shard_map/ppermute | solution.py:433
  22.0 8.7 %collective-permute-start.9 = (bf16[72,768]{1,0:T(8,128)(2,1)S(1)}, bf16[72,768]{1,0:T(8,128)(2,1)S(1)}, u32[]{:S(2)}, u32[]{:S(2)}) collective-permute-start(bf16[72,768]{1,0:T(8,128)(2,1)S(1)} %get-tuple-element.143), channel_id=1, source_target_pairs={{0,6},{2,4},{4,2},{6,0},{1,7},{3,5},{5,3},{7,1},{8,14},{10,12},{12... | collective-permute-start | bytes 331784 | tf_op jit(solution)/shard_map/ppermute | solution.py:433
  23.4 25.3 %copy-start = (bf16[1,768,768]{2,1,0:T(8,128)(2,1)S(1)}, bf16[1,768,768]{2,1,0:T(8,128)(2,1)}, u32[]{:S(2)}) copy-start(bf16[1,768,768]{2,1,0:T(8,128)(2,1)} %param.23) | copy-start | bytes 3538948
  23.5 25.3 %copy-start.1 = (bf16[1,768,768]{2,1,0:T(8,128)(2,1)S(1)}, bf16[1,768,768]{2,1,0:T(8,128)(2,1)}, u32[]{:S(2)}) copy-start(bf16[1,768,768]{2,1,0:T(8,128)(2,1)} %param.24) | copy-start | bytes 3538948
  26.2 81.1 %copy-start.2 = (f32[394,768]{1,0:T(8,128)}, f32[394,768]{1,0:T(8,128)S(1)}, u32[]{:S(2)}) copy-start(f32[394,768]{1,0:T(8,128)S(1)} %get-tuple-element.133.middle) | copy-start | bytes 3631108
  30.8 13.8 %collective-permute-start.10 = (bf16[144,768]{1,0:T(8,128)(2,1)S(1)}, bf16[144,768]{1,0:T(8,128)(2,1)S(1)}, u32[]{:S(2)}, u32[]{:S(2)}) collective-permute-start(bf16[144,768]{1,0:T(8,128)(2,1)S(1)} %get-tuple-element.145), channel_id=1, source_target_pairs={{0,2},{2,0},{4,6},{6,4},{1,3},{3,1},{5,7},{7,5},{8,10},{10,8},{12,... | collective-permute-start | bytes 663560 | tf_op jit(solution)/shard_map/ppermute | solution.py:433
  33.6 15.1 %collective-permute-start.11 = (bf16[144,768]{1,0:T(8,128)(2,1)S(1)}, bf16[144,768]{1,0:T(8,128)(2,1)S(1)}, u32[]{:S(2)}, u32[]{:S(2)}) collective-permute-start(bf16[144,768]{1,0:T(8,128)(2,1)S(1)} %get-tuple-element.147), channel_id=1, source_target_pairs={{0,2},{2,0},{4,6},{6,4},{1,3},{3,1},{5,7},{7,5},{8,10},{10,8},{12,... | collective-permute-start | bytes 663560 | tf_op jit(solution)/shard_map/ppermute | solution.py:433
  33.7 22.1 %collective-permute-start.12 = (bf16[144,768]{1,0:T(8,128)(2,1)S(1)}, bf16[144,768]{1,0:T(8,128)(2,1)S(1)}, u32[]{:S(2)}, u32[]{:S(2)}) collective-permute-start(bf16[144,768]{1,0:T(8,128)(2,1)S(1)} %get-tuple-element.150), channel_id=1, source_target_pairs={{0,4},{2,6},{4,0},{6,2},{1,5},{3,7},{5,1},{7,3},{8,12},{10,14},{12... | collective-permute-start | bytes 663560 | tf_op jit(solution)/shard_map/ppermute | solution.py:433
  37.6 19.1 %collective-permute-start.13 = (bf16[144,768]{1,0:T(8,128)(2,1)S(1)}, bf16[144,768]{1,0:T(8,128)(2,1)S(1)}, u32[]{:S(2)}, u32[]{:S(2)}) collective-permute-start(bf16[144,768]{1,0:T(8,128)(2,1)S(1)} %get-tuple-element.151), channel_id=1, source_target_pairs={{0,6},{2,4},{4,2},{6,0},{1,7},{3,5},{5,3},{7,1},{8,14},{10,12},{12... | collective-permute-start | bytes 663560 | tf_op jit(solution)/shard_map/ppermute | solution.py:433
  38.0 18.7 %collective-permute-start.14 = (bf16[2,72,768]{2,1,0:T(8,128)(2,1)S(1)}, bf16[2,72,768]{2,1,0:T(8,128)(2,1)S(1)}, u32[]{:S(2)}, u32[]{:S(2)}) collective-permute-start(bf16[2,72,768]{2,1,0:T(8,128)(2,1)S(1)} %pad_maximum_fusion.2), channel_id=1, source_target_pairs={{0,16},{8,24},{16,0},{24,8},{1,17},{9,25},{17,1},{25,9},{2,18},{10... | collective-permute-start | bytes 663560 | tf_op jit(solution)/shard_map/ppermute | solution.py:430
  64.2 12.6 %collective-permute-start.20 = (bf16[1536,768]{1,0:T(8,128)(2,1)S(1)}, bf16[1536,768]{1,0:T(8,128)(2,1)S(1)}, u32[]{:S(2)}, u32[]{:S(2)}) collective-permute-start(bf16[1536,768]{1,0:T(8,128)(2,1)S(1)} %get-tuple-element.174), channel_id=1, source_target_pairs={{0,8},{8,0},{16,24},{24,16},{1,9},{9,1},{17,25},{25,17},{2,10},{10... | collective-permute-start | bytes 7077896 | tf_op jit(solution)/shard_map/ppermute | solution.py:430
  64.3 14.2 %collective-permute-start.15 = (bf16[144,768]{1,0:T(8,128)(2,1)S(1)}, bf16[144,768]{1,0:T(8,128)(2,1)S(1)}, u32[]{:S(2)}, u32[]{:S(2)}) collective-permute-start(bf16[144,768]{1,0:T(8,128)(2,1)S(1)} %get-tuple-element.154), channel_id=1, source_target_pairs={{0,6},{2,4},{4,2},{6,0},{1,7},{3,5},{5,3},{7,1},{8,14},{10,12},{12... | collective-permute-start | bytes 663560 | tf_op jit(solution)/shard_map/ppermute | solution.py:433
  67.5 19.2 %collective-permute-start.16 = (bf16[144,768]{1,0:T(8,128)(2,1)S(1)}, bf16[144,768]{1,0:T(8,128)(2,1)S(1)}, u32[]{:S(2)}, u32[]{:S(2)}) collective-permute-start(bf16[144,768]{1,0:T(8,128)(2,1)S(1)} %get-tuple-element.157), channel_id=1, source_target_pairs={{0,4},{2,6},{4,0},{6,2},{1,5},{3,7},{5,1},{7,3},{8,12},{10,14},{12... | collective-permute-start | bytes 663560 | tf_op jit(solution)/shard_map/ppermute | solution.py:433
  67.5 19.2 %collective-permute-start.17 = (bf16[144,768]{1,0:T(8,128)(2,1)S(1)}, bf16[144,768]{1,0:T(8,128)(2,1)S(1)}, u32[]{:S(2)}, u32[]{:S(2)}) collective-permute-start(bf16[144,768]{1,0:T(8,128)(2,1)S(1)} %get-tuple-element.158), channel_id=1, source_target_pairs={{0,2},{2,0},{4,6},{6,4},{1,3},{3,1},{5,7},{7,5},{8,10},{10,8},{12,... | collective-permute-start | bytes 663560 | tf_op jit(solution)/shard_map/ppermute | solution.py:433
  68.7 6.9 %collective-permute-start.19 = (bf16[2,72,768]{2,1,0:T(8,128)(2,1)S(1)}, bf16[2,72,768]{2,1,0:T(8,128)(2,1)S(1)}, u32[]{:S(2)}, u32[]{:S(2)}) collective-permute-start(bf16[2,72,768]{2,1,0:T(8,128)(2,1)S(1)} %get-tuple-element.162), channel_id=1, source_target_pairs={{0,16},{8,24},{16,0},{24,8},{1,17},{9,25},{17,1},{25,9},{2,18},{10... | collective-permute-start | bytes 663560 | tf_op jit(solution)/shard_map/ppermute | solution.py:430
  75.7 12.6 %collective-permute-start.18 = (bf16[144,768]{1,0:T(8,128)(2,1)S(1)}, bf16[144,768]{1,0:T(8,128)(2,1)S(1)}, u32[]{:S(2)}, u32[]{:S(2)}) collective-permute-start(bf16[144,768]{1,0:T(8,128)(2,1)S(1)} %get-tuple-element.237), channel_id=1, source_target_pairs={{0,2},{2,0},{4,6},{6,4},{1,3},{3,1},{5,7},{7,5},{8,10},{10,8},{12,... | collective-permute-start | bytes 663560 | tf_op jit(solution)/shard_map/ppermute | solution.py:433
  78.5 11.3 %copy-start.17 = (f32[768,768]{1,0:T(8,128)}, f32[768,768]{1,0:T(8,128)S(1)}, u32[]{:S(2)}) copy-start(f32[768,768]{1,0:T(8,128)S(1)} %get-tuple-element.222.kept) | copy-start | bytes 7077892
  89.7 17.6 %copy-start.9 = (bf16[768,3,192]{0,2,1:T(8,128)(2,1)S(1)}, bf16[768,3,192]{0,2,1:T(8,128)(2,1)}, u32[]{:S(2)}) copy-start(bf16[768,3,192]{0,2,1:T(8,128)(2,1)} %param.18) | copy-start | bytes 2654212
  89.7 1.7 %collective-permute-start.21 = (bf16[416,384]{1,0:T(8,128)(2,1)S(1)}, bf16[416,384]{1,0:T(8,128)(2,1)S(1)}, u32[]{:S(2)}, u32[]{:S(2)}) collective-permute-start(bf16[416,384]{1,0:T(8,128)(2,1)S(1)} %get-tuple-element.183), channel_id=1, source_target_pairs={{0,8},{8,0},{16,24},{24,16},{1,9},{9,1},{17,25},{25,17},{2,10},{10... | collective-permute-start | bytes 958472 | tf_op jit(solution)/shard_map/ppermute | solution.py:430
  91.5 9.6 %collective-permute-start.22 = (bf16[416,384]{1,0:T(8,128)(2,1)S(1)}, bf16[416,384]{1,0:T(8,128)(2,1)S(1)}, u32[]{:S(2)}, u32[]{:S(2)}) collective-permute-start(bf16[416,384]{1,0:T(8,128)(2,1)S(1)} %add_convert_fusion.1), channel_id=1, source_target_pairs={{0,16},{8,24},{16,0},{24,8},{1,17},{9,25},{17,1},{25,9},{2,18},{10... | collective-permute-start | bytes 958472 | tf_op jit(solution)/shard_map/ppermute | solution.py:430
  93.1 12.6 %collective-permute-start.25 = (bf16[256,768]{1,0:T(8,128)(2,1)S(1)}, bf16[256,768]{1,0:T(8,128)(2,1)S(1)}, u32[]{:S(2)}, u32[]{:S(2)}) collective-permute-start(bf16[256,768]{1,0:T(8,128)(2,1)S(1)} %get-tuple-element.188), channel_id=1, source_target_pairs={{0,1},{1,0},{2,3},{3,2},{4,5},{5,4},{6,7},{7,6},{8,9},{9,8},{10,11... | collective-permute-start | bytes 1179656 | tf_op jit(solution)/shard_map/ppermute | solution.py:436
  94.6 11.1 %collective-permute-start.23 = (bf16[72,768]{1,0:T(8,128)(2,1)S(1)}, bf16[72,768]{1,0:T(8,128)(2,1)S(1)}, u32[]{:S(2)}, u32[]{:S(2)}) collective-permute-start(bf16[72,768]{1,0:T(8,128)(2,1)S(1)} %get-tuple-element.186), channel_id=1, source_target_pairs={{0,4},{2,6},{4,0},{6,2},{1,5},{3,7},{5,1},{7,3},{8,12},{10,14},{12... | collective-permute-start | bytes 331784 | tf_op jit(solution)/shard_map/ppermute | solution.py:433
  95.8 9.9 %collective-permute-start.24 = (bf16[72,768]{1,0:T(8,128)(2,1)S(1)}, bf16[72,768]{1,0:T(8,128)(2,1)S(1)}, u32[]{:S(2)}, u32[]{:S(2)}) collective-permute-start(bf16[72,768]{1,0:T(8,128)(2,1)S(1)} %get-tuple-element.187), channel_id=1, source_target_pairs={{0,6},{2,4},{4,2},{6,0},{1,7},{3,5},{5,3},{7,1},{8,14},{10,12},{12... | collective-permute-start | bytes 331784 | tf_op jit(solution)/shard_map/ppermute | solution.py:433
  105.7 1.6 collective-permute-start.26
  112.3 5.2 %collective-permute-start.33 = (bf16[394,384]{1,0:T(8,128)(2,1)S(1)}, bf16[394,384]{1,0:T(8,128)(2,1)S(1)}, u32[]{:S(2)}, u32[]{:S(2)}) collective-permute-start(bf16[394,384]{1,0:T(8,128)(2,1)S(1)} %get-tuple-element.215), channel_id=1, source_target_pairs={{0,8},{8,0},{16,24},{24,16},{1,9},{9,1},{17,25},{25,17},{2,10},{10... | collective-permute-start | bytes 907784 | tf_op jit(solution)/shard_map/ppermute | solution.py:430
  112.5 10.8 %collective-permute-start.29 = (bf16[192,768]{1,0:T(8,128)(2,1)S(1)}, bf16[192,768]{1,0:T(8,128)(2,1)S(1)}, u32[]{:S(2)}, u32[]{:S(2)}) collective-permute-start(bf16[192,768]{1,0:T(8,128)(2,1)S(1)} %get-tuple-element.210), channel_id=1, source_target_pairs={{0,3},{1,2},{2,1},{3,0},{4,7},{5,6},{6,5},{7,4},{8,11},{9,10},{10,... | collective-permute-start | bytes 884744 | tf_op jit(solution)/shard_map/ppermute | solution.py:440
  114.5 14.5 %collective-permute-start.30 = (bf16[192,768]{1,0:T(8,128)(2,1)S(1)}, bf16[192,768]{1,0:T(8,128)(2,1)S(1)}, u32[]{:S(2)}, u32[]{:S(2)}) collective-permute-start(bf16[192,768]{1,0:T(8,128)(2,1)S(1)} %get-tuple-element.211), channel_id=1, source_target_pairs={{0,1},{1,0},{2,3},{3,2},{4,5},{5,4},{6,7},{7,6},{8,9},{9,8},{10,11... | collective-permute-start | bytes 884744 | tf_op jit(solution)/shard_map/ppermute | solution.py:440
  116.0 13.0 %collective-permute-start.31 = (bf16[192,768]{1,0:T(8,128)(2,1)S(1)}, bf16[192,768]{1,0:T(8,128)(2,1)S(1)}, u32[]{:S(2)}, u32[]{:S(2)}) collective-permute-start(bf16[192,768]{1,0:T(8,128)(2,1)S(1)} %get-tuple-element.212), channel_id=1, source_target_pairs={{0,2},{1,3},{2,0},{3,1},{4,6},{5,7},{6,4},{7,5},{8,10},{9,11},{10,... | collective-permute-start | bytes 884744 | tf_op jit(solution)/shard_map/ppermute | solution.py:440
  117.4 11.7 %collective-permute-start.27 = (bf16[400,384]{1,0:T(8,128)(2,1)S(1)}, bf16[400,384]{1,0:T(8,128)(2,1)S(1)}, u32[]{:S(2)}, u32[]{:S(2)}) collective-permute-start(bf16[400,384]{1,0:T(8,128)(2,1)S(1)} %get-tuple-element.208), channel_id=1, source_target_pairs={{0,8},{8,0},{16,24},{24,16},{1,9},{9,1},{17,25},{25,17},{2,10},{10... | collective-permute-start | bytes 921608 | tf_op jit(solution)/shard_map/ppermute | solution.py:430
  117.6 12.2 %collective-permute-start.34 = (bf16[394,384]{1,0:T(8,128)(2,1)S(1)}, bf16[394,384]{1,0:T(8,128)(2,1)S(1)}, u32[]{:S(2)}, u32[]{:S(2)}) collective-permute-start(bf16[394,384]{1,0:T(8,128)(2,1)S(1)} %add_convert_fusion.3), channel_id=1, source_target_pairs={{0,16},{8,24},{16,0},{24,8},{1,17},{9,25},{17,1},{25,9},{2,18},{10... | collective-permute-start | bytes 907784 | tf_op jit(solution)/shard_map/ppermute | solution.py:430
  129.2 4.2 %copy-start.7 = (f32[768]{0:T(1024)S(1)}, f32[768]{0:T(1024)}, u32[]{:S(2)}) copy-start(f32[768]{0:T(1024)} %gain.7) | copy-start | bytes 9220
  129.3 9.3 %collective-permute-start.28 = (bf16[400,384]{1,0:T(8,128)(2,1)S(1)}, bf16[400,384]{1,0:T(8,128)(2,1)S(1)}, u32[]{:S(2)}, u32[]{:S(2)}) collective-permute-start(bf16[400,384]{1,0:T(8,128)(2,1)S(1)} %add_convert_fusion.5), channel_id=1, source_target_pairs={{0,16},{8,24},{16,0},{24,8},{1,17},{9,25},{17,1},{25,9},{2,18},{10... | collective-permute-start | bytes 921608 | tf_op jit(solution)/shard_map/ppermute | solution.py:430
  130.0 3.4 %collective-permute-start.35 = (bf16[394,384]{1,0:T(8,128)(2,1)S(1)}, bf16[394,384]{1,0:T(8,128)(2,1)S(1)}, u32[]{:S(2)}, u32[]{:S(2)}) collective-permute-start(bf16[394,384]{1,0:T(8,128)(2,1)S(1)} %add_convert_fusion.2.own), channel_id=1, source_target_pairs={{0,8},{8,0},{16,24},{24,16},{1,9},{9,1},{17,25},{25,17},{2,10},{10... | collective-permute-start | bytes 907784 | tf_op jit(solution)/shard_map/ppermute | solution.py:430
  130.0 18.1 %collective-permute-start.32 = (bf16[192,768]{1,0:T(8,128)(2,1)S(1)}, bf16[192,768]{1,0:T(8,128)(2,1)S(1)}, u32[]{:S(2)}, u32[]{:S(2)}) collective-permute-start(bf16[192,768]{1,0:T(8,128)(2,1)S(1)} %shard_map.223.own), channel_id=1, source_target_pairs={{0,4},{2,6},{4,0},{6,2},{1,5},{3,7},{5,1},{7,3},{8,12},{10,14},{12... | collective-permute-start | bytes 884744 | tf_op jit(solution)/shard_map/ppermute | solution.py:433
  131.9 23.0 %collective-permute-start.38 = (bf16[512,768]{1,0:T(8,128)(2,1)S(1)}, bf16[512,768]{1,0:T(8,128)(2,1)S(1)}, u32[]{:S(2)}, u32[]{:S(2)}) collective-permute-start(bf16[512,768]{1,0:T(8,128)(2,1)S(1)} %get-tuple-element.224), channel_id=1, source_target_pairs={{0,1},{1,0},{2,3},{3,2},{4,5},{5,4},{6,7},{7,6},{8,9},{9,8},{10,11... | collective-permute-start | bytes 2359304 | tf_op jit(solution)/shard_map/ppermute | solution.py:436
  135.8 13.0 %collective-permute-start.36 = (f32[16,768]{1,0:T(8,128)S(1)}, f32[16,768]{1,0:T(8,128)S(1)}, u32[]{:S(2)}, u32[]{:S(2)}) collective-permute-start(f32[16,768]{1,0:T(8,128)S(1)} %get-tuple-element.218.small), channel_id=1, source_target_pairs={{0,4},{2,6},{4,0},{6,2},{1,5},{3,7},{5,1},{7,3},{8,12},{10,14},{12... | collective-permute-start | bytes 147464 | tf_op jit(solution)/shard_map/ppermute | solution.py:433
  139.3 13.2 %copy-start.3 = (f32[394,768]{1,0:T(8,128)S(1)}, f32[394,768]{1,0:T(8,128)}, u32[]{:S(2)}) copy-start(f32[394,768]{1,0:T(8,128)} %copy-done.2) | copy-start | bytes 3631108
  148.9 3.7 %collective-permute-start.37 = (bf16[400,384]{1,0:T(8,128)(2,1)}, bf16[400,384]{1,0:T(8,128)(2,1)}, u32[]{:S(2)}, u32[]{:S(2)}) collective-permute-start(bf16[400,384]{1,0:T(8,128)(2,1)} %add_convert_fusion.4), channel_id=1, source_target_pairs={{0,8},{8,0},{16,24},{24,16},{1,9},{9,1},{17,25},{25,17},{2,10},{10... | collective-permute-start | bytes 921608 | tf_op jit(solution)/shard_map/ppermute | solution.py:430
  149.0 5.9 %copy-start.18 = (f32[768,768]{1,0:T(8,128)S(1)}, f32[768,768]{1,0:T(8,128)}, u32[]{:S(2)}) copy-start(f32[768,768]{1,0:T(8,128)} %copy-done.17) | copy-start | bytes 7077892
  149.0 11.4 %collective-permute-start.39 = (bf16[208,768]{1,0:T(8,128)(2,1)S(1)}, bf16[208,768]{1,0:T(8,128)(2,1)S(1)}, u32[]{:S(2)}, u32[]{:S(2)}) collective-permute-start(bf16[208,768]{1,0:T(8,128)(2,1)S(1)} %shard_map.225.refs_0_), channel_id=1, source_target_pairs={{0,3},{1,2},{2,1},{3,0},{4,7},{5,6},{6,5},{7,4},{8,11},{9,10},{10,... | collective-permute-start | bytes 958472 | tf_op jit(solution)/shard_map/ppermute | solution.py:440
  149.1 16.8 %collective-permute-start.40 = (bf16[208,768]{1,0:T(8,128)(2,1)S(1)}, bf16[208,768]{1,0:T(8,128)(2,1)S(1)}, u32[]{:S(2)}, u32[]{:S(2)}) collective-permute-start(bf16[208,768]{1,0:T(8,128)(2,1)S(1)} %shard_map.225.refs_0_), channel_id=1, source_target_pairs={{0,1},{1,0},{2,3},{3,2},{4,5},{5,4},{6,7},{7,6},{8,9},{9,8},{10,11... | collective-permute-start | bytes 958472 | tf_op jit(solution)/shard_map/ppermute | solution.py:440
  149.9 16.1 %collective-permute-start.41 = (bf16[208,768]{1,0:T(8,128)(2,1)S(1)}, bf16[208,768]{1,0:T(8,128)(2,1)S(1)}, u32[]{:S(2)}, u32[]{:S(2)}) collective-permute-start(bf16[208,768]{1,0:T(8,128)(2,1)S(1)} %shard_map.225.refs_0_), channel_id=1, source_target_pairs={{0,2},{1,3},{2,0},{3,1},{4,6},{5,7},{6,4},{7,5},{8,10},{9,11},{10,... | collective-permute-start | bytes 958472 | tf_op jit(solution)/shard_map/ppermute | solution.py:440

commit v8 on v7

--- a/solution.py
+++ b/solution.py
@@ -517,7 +517,7 @@
             + [((LANES, width), BF16)]
             + [(shape, BF16) for shape in cot_shapes],
             [ids, after(routes.T, head_out), cotangent, w_router.T],
-            micros=2,
+            micros=0.01,
         )
         head_x = after(head_x, table)
         if small_slice:
@@ -535,7 +535,7 @@
                 ((n_tensor, inner, width), BF16),
                 ((rows, width), BF16),
             ],
-            micros=3,
+            micros=0.01,
         )
         if small_slice:
             *row_blocks, far_2, far_3 = lax.optimization_barrier((*row_blocks, *d_rows_in[2:]))
@@ -616,7 +616,7 @@
                 [((quarter, width), BF16)] * 2,
                 [gated[1][0], tensor_swap(gated[1][1], 2)],
             )
-            gated_blocks = [gated[0][0][0], expert_swap(gated[0][0][1], 1), *far_blocks]
+            gated_blocks = [gated[0][0][0], gated[0][0][1], *far_blocks]
         else:
             gated_blocks = [gated[0][0][k] for k in range(experts)]
 
@@ -628,11 +628,13 @@
         chip = (kept.astype(F32) + tensor_swap(sent, 1).astype(F32)).astype(BF16)
         own = (chip.astype(F32) + tensor_swap(chip, 2).astype(F32)).astype(BF16)
         if small_slice:
-            gated_home = gated_blocks[:2] + [expert_swap(gated_blocks[k], k) for k in (3, 2)][::-1]
+            home = {k: expert_swap(gated_blocks[k], k) for k in (2, 3, 1)}
+            gated_home = [gated_blocks[0], home[1], home[2], home[3]]
         else:
             gated_home = exchange(list(gated_blocks))
         came_first = dp_swap(sent_first)
-        own, *gated_home, came_first = lax.optimization_barrier((own, *gated_home, came_first))
+        own, *gated_home, came_first = lax.optimization_barrier((own, *gated_home[::-1], came_first))
+        gated_home = gated_home[::-1]
         other = tensor_swap(own, 1)
 
         parts = 4 if small_slice else 1

time: 169 us -> 173 us (1.024)
  local copies, waits for them, and re-layouts: 3.81 us -> 12.9 us
  waiting for transfers between devices: 77 us -> 73.4 us
  starting transfers between devices: 45 us -> 42.1 us
    unnamed x38 -> x68, local copies, waits for them, and re-layouts: 3.69 us -> 12.8 us
    ppermute x6, waiting for transfers between devices: 20.3 us -> 16.4 us  [quarter_swap(): return lax.ppermute(value, ('expert', 'dp'), pairs)]
    ppermute x20, starting transfers between devices: 12 us -> 9.53 us  [tensor_swap(): lax.ppermute(value, 'tensor', [(i, i ^ mask) for i in range(n_tensor)])]
    ppermute x14, waiting for transfers between devices: 38.3 us -> 40.2 us  [expert_swap(): lax.ppermute(value, 'expert', [(i, i ^ mask) for i in range(n_expert)])]
where the time goes in v8:
time: 173 us
  waiting for transfers between devices  73.4 us (42%)
  starting transfers between devices  42.1 us (24%)
  Pallas kernels  38.8 us (22%)
  local copies, waits for them, and re-layouts  12.9 us (7%)
  other arithmetic  3.51 us (2%)
  between operations  1.78 us (1%)
    ppermute x14, waiting for transfers between devices, expert_swap(): lax.ppermute(value, 'expert', [(i, i ^ mask) for i in range(n_expert)])  40.2 us
    pallas_call x16, Pallas kernels, run(): pl.pallas_call(kernel, out_shape=[jax.ShapeDtypeStruct(shape, kind) for s...  38.8 us
    ppermute x14, starting transfers between devices, expert_swap(): lax.ppermute(value, 'expert', [(i, i ^ mask) for i in range(n_expert)])  22.9 us
    ppermute x20, waiting for transfers between devices, tensor_swap(): lax.ppermute(value, 'tensor', [(i, i ^ mask) for i in range(n_tensor)])  16.9 us
    ppermute x6, waiting for transfers between devices, quarter_swap(): return lax.ppermute(value, ('expert', 'dp'), pairs)  16.4 us
    unnamed x68, local copies, waits for them, and re-layouts  12.8 us
    ppermute x20, starting transfers between devices, tensor_swap(): lax.ppermute(value, 'tensor', [(i, i ^ mask) for i in range(n_tensor)])  9.53 us
    ppermute x6, starting transfers between devices, quarter_swap(): return lax.ppermute(value, ('expert', 'dp'), pairs)  7.05 us
  transfers between devices with their start and end apart: 42, of which 21 were waited for; matrix products, arithmetic and copies ran while one was open for 2% of the time, Pallas kernels for 13%

profile of v8, /device:TPU:0, one launch (start us, length us, event | category | flops | bytes accessed | tf_op | source)
XLA Modules:
  0.0 172.6 jit_solution(665430859069157899)
XLA Ops:
  1.2 2.9 %collective-permute-start = (bf16[192,768]{1,0:T(8,128)(2,1)}, bf16[192,768]{1,0:T(8,128)(2,1)}, u32[]{:S(2)}, u32[]{:S(2)}) collective-permute-start(bf16[192,768]{1,0:T(8,128)(2,1)} %w_out.1), channel_id=1, source_target_pairs={{0,16},{8,24},{16,0},{24,8},{1,17},{9,25},{17,1},{25,9},{2,18},{10... | collective-permute-start | bytes 884744 | tf_op jit(solution)/shard_map/ppermute | solution.py:430
  4.2 1.1 copy-done.2
  5.2 0.7 copy-done.15
  5.9 1.2 copy-done.17
  7.1 0.7 copy-done.21
  7.8 2.5 %shard_map.212 = (bf16[394,768]{1,0:T(8,128)(2,1)S(1)}, bf16[394,192]{1,0:T(8,128)(2,1)S(1)}, bf16[394,192]{1,0:T(8,128)(2,1)S(1)}, bf16[394,192]{1,0:T(8,128)(2...) custom-call(bf16[394,768]{1,0:T(8,128)(2,1)S(1)} %copy-done.2, f32[768]{0:T(1024)S(1)} %copy-done.15, ...), custom_call_target="tpu_custom_call" | custom-call | flops 4600000000 | bytes 1024 | tf_op jit(solution)/shard_map/pallas_call | solution.py:413
  10.3 1.0 copy-done.24
  11.4 0.8 copy-done.26
  12.9 0.7 copy-done.30
  13.6 0.7 copy-done.32
  14.3 0.7 copy-done.9
  16.4 1.1 copy-done.6
  17.4 1.4 shard_map.213
  18.8 3.8 %collective-permute-done.5.rest_2_ = bf16[394,192]{1,0:T(8,128)(2,1)} collective-permute-done((bf16[394,192]{1,0:T(8,128)(2,1)S(1)}, bf16[394,192]{1,0:T(8,128)(2,1)}, u32[]{:S(2)}, u32[]{:S(2)}) %collective-permute-start.5) | collective-permute-done | bytes 151328 | tf_op jit(solution)/shard_map/ppermute | solution.py:430
  22.6 2.6 %collective-permute-start.8 = (bf16[72,768]{1,0:T(8,128)(2,1)S(1)}, bf16[72,768]{1,0:T(8,128)(2,1)S(1)}, u32[]{:S(2)}, u32[]{:S(2)}) collective-permute-start(bf16[72,768]{1,0:T(8,128)(2,1)S(1)} %get-tuple-element.142), channel_id=1, source_target_pairs={{0,4},{2,6},{4,0},{6,2},{1,5},{3,7},{5,1},{7,3},{8,12},{10,14},{12... | collective-permute-start | bytes 331784 | tf_op jit(solution)/shard_map/ppermute | solution.py:433
  25.2 1.4 collective-permute-start.9
  26.6 1.0 copy-done.10
  27.5 3.4 %shard_map.214 = (f32[394,768]{1,0:T(8,128)S(1)}, bf16[144,768]{1,0:T(8,128)(2,1)S(1)}, bf16[144,768]{1,0:T(8,128)(2,1)S(1)}, bf16[144,768]{1,0:T(8,128)(2,1)S(1)}, bf16[144,768]{1,0:T(8,128)(2,1)S(1)}) custom-call(s32[8]{0:T(128)S(1)} %stack.38.ids, bf16[394,768]{1,0:T(8,128)(2,1)S(1)} %copy-done.3, f32[768]{0:T(1024)S(1)} %copy-done.14, ...), custom_call_target="tpu_custom_call" | custom-call | flops 11500000 | bytes 1024 | tf_op jit(solution)/shard_map/pallas_call | solution.py:413
  30.9 3.2 %collective-permute-done.8.refs_2_ = bf16[72,768]{1,0:T(8,128)(2,1)S(1)} collective-permute-done((bf16[72,768]{1,0:T(8,128)(2,1)S(1)}, bf16[72,768]{1,0:T(8,128)(2,1)S(1)}, u32[]{:S(2)}, u32[]{:S(2)}) %collective-permute-start.8) | collective-permute-done | bytes 110624 | tf_op jit(solution)/shard_map/ppermute | solution.py:433
  34.1 2.7 %collective-permute-start.10 = (bf16[144,768]{1,0:T(8,128)(2,1)S(1)}, bf16[144,768]{1,0:T(8,128)(2,1)S(1)}, u32[]{:S(2)}, u32[]{:S(2)}) collective-permute-start(bf16[144,768]{1,0:T(8,128)(2,1)S(1)} %get-tuple-element.145), channel_id=1, source_target_pairs={{0,2},{2,0},{4,6},{6,4},{1,3},{3,1},{5,7},{7,5},{8,10},{10,8},{12,... | collective-permute-start | bytes 663560 | tf_op jit(solution)/shard_map/ppermute | solution.py:433
  36.8 3.9 %collective-permute-start.12 = (bf16[144,768]{1,0:T(8,128)(2,1)S(1)}, bf16[144,768]{1,0:T(8,128)(2,1)S(1)}, u32[]{:S(2)}, u32[]{:S(2)}) collective-permute-start(bf16[144,768]{1,0:T(8,128)(2,1)S(1)} %get-tuple-element.150), channel_id=1, source_target_pairs={{0,4},{2,6},{4,0},{6,2},{1,5},{3,7},{5,1},{7,3},{8,12},{10,14},{12... | collective-permute-start | bytes 663560 | tf_op jit(solution)/shard_map/ppermute | solution.py:433
  41.8 5.9 %collective-permute-done.10.refs_1_ = bf16[144,768]{1,0:T(8,128)(2,1)S(1)} collective-permute-done((bf16[144,768]{1,0:T(8,128)(2,1)S(1)}, bf16[144,768]{1,0:T(8,128)(2,1)S(1)}, u32[]{:S(2)}, u32[]{:S(2)}) %collective-permute-start.10) | collective-permute-done | bytes 221216 | tf_op jit(solution)/shard_map/ppermute | solution.py:433
  47.7 4.2 %collective-permute-done.11.refs_3_ = bf16[144,768]{1,0:T(8,128)(2,1)S(1)} collective-permute-done((bf16[144,768]{1,0:T(8,128)(2,1)S(1)}, bf16[144,768]{1,0:T(8,128)(2,1)S(1)}, u32[]{:S(2)}, u32[]{:S(2)}) %collective-permute-start.11) | collective-permute-done | bytes 221216 | tf_op jit(solution)/shard_map/ppermute | solution.py:433
  51.9 7.0 %shard_map.215 = (bf16[144,768]{1,0:T(8,128)(2,1)S(1)}, bf16[144,768]{1,0:T(8,128)(2,1)S(1)}, bf16[2,144,768]{2,1,0:T(8,128)(2,1)S(1)}, bf16[2,144,768]{2,1,0:T(...) custom-call(s32[8]{0:T(128)S(1)} %stack.38.ids, ...), custom_call_target="tpu_custom_call" | custom-call | flops 57500000 | bytes 1024 | tf_op jit(solution)/shard_map/pallas_call | solution.py:413
  58.9 0.9 collective-permute-done.13.refs_1_
  59.8 4.8 %shard_map.216 = (bf16[144,768]{1,0:T(8,128)(2,1)S(1)}, bf16[144,768]{1,0:T(8,128)(2,1)S(1)}, bf16[2,72,768]{2,1,0:T(8,128)(2,1)S(1)}, bf16[2,72,768]{2,1,0:T(8,...) custom-call(s32[8]{0:T(128)S(1)} %stack.38.ids, ...), custom_call_target="tpu_custom_call" | custom-call | flops 57500000 | bytes 1024 | tf_op jit(solution)/shard_map/pallas_call | solution.py:413
  64.6 2.7 %shard_map.218 = (bf16[1536,768]{1,0:T(8,128)(2,1)S(1)}, bf16[1536,768]{1,0:T(8,128)(2,1)S(1)}) custom-call(bf16[288,768]{1,0:T(8,128)(2,1)S(1)} %get-tuple-element.165.refs_0_, bf16[288,768]{1,0:T(8,128)(2,1)S(1)} %get-tuple-element.166.refs_1_, bf16[288,768]{1,0:T(8,128)(2,1)S(1)} %get-tuple-element.167.refs_2_, ...), custom_call_target="tpu_custom_call" | custom-call | flops 4600000000 | bytes 1024 | tf_op jit(solution)/shard_map/pallas_call | solution.py:413
  67.3 3.2 %collective-permute-start.15 = (bf16[144,768]{1,0:T(8,128)(2,1)S(1)}, bf16[144,768]{1,0:T(8,128)(2,1)S(1)}, u32[]{:S(2)}, u32[]{:S(2)}) collective-permute-start(bf16[144,768]{1,0:T(8,128)(2,1)S(1)} %get-tuple-element.154), channel_id=1, source_target_pairs={{0,6},{2,4},{4,2},{6,0},{1,7},{3,5},{5,3},{7,1},{8,14},{10,12},{12... | collective-permute-start | bytes 663560 | tf_op jit(solution)/shard_map/ppermute | solution.py:433
  70.5 1.2 collective-permute-start.17
  72.3 6.4 %collective-permute-done.18.came = bf16[2,72,768]{2,1,0:T(8,128)(2,1)S(1)} collective-permute-done((bf16[2,72,768]{2,1,0:T(8,128)(2,1)S(1)}, bf16[2,72,768]{2,1,0:T(8,128)(2,1)S(1)}, u32[]{:S(2)}, u32[]{:S(2)}) %collective-permute-start.18) | collective-permute-done | bytes 221216 | tf_op jit(solution)/shard_map/ppermute | solution.py:430
  78.8 1.6 shard_map.219
  80.5 9.2 %collective-permute-done.16.refs_2_ = bf16[144,768]{1,0:T(8,128)(2,1)S(1)} collective-permute-done((bf16[144,768]{1,0:T(8,128)(2,1)S(1)}, bf16[144,768]{1,0:T(8,128)(2,1)S(1)}, u32[]{:S(2)}, u32[]{:S(2)}) %collective-permute-start.16) | collective-permute-done | bytes 221216 | tf_op jit(solution)/shard_map/ppermute | solution.py:433
  89.6 1.5 shard_map.220
  91.2 1.6 collective-permute-done.20
  93.5 1.5 collective-permute-start.25
  95.1 2.4 %collective-permute-start.22 = (bf16[72,768]{1,0:T(8,128)(2,1)S(1)}, bf16[72,768]{1,0:T(8,128)(2,1)S(1)}, u32[]{:S(2)}, u32[]{:S(2)}) collective-permute-start(bf16[72,768]{1,0:T(8,128)(2,1)S(1)} %get-tuple-element.184), channel_id=1, source_target_pairs={{0,6},{2,4},{4,2},{6,0},{1,7},{3,5},{5,3},{7,1},{8,14},{10,12},{12... | collective-permute-start | bytes 331784 | tf_op jit(solution)/shard_map/ppermute | solution.py:433
  97.4 2.0 %collective-permute-start.24 = (bf16[144,768]{1,0:T(8,128)(2,1)S(1)}, bf16[144,768]{1,0:T(8,128)(2,1)S(1)}, u32[]{:S(2)}, u32[]{:S(2)}) collective-permute-start(bf16[144,768]{1,0:T(8,128)(2,1)S(1)} %get-tuple-element.186), channel_id=1, source_target_pairs={{0,2},{2,0},{4,6},{6,4},{1,3},{3,1},{5,7},{7,5},{8,10},{10,8},{12,... | collective-permute-start | bytes 663560 | tf_op jit(solution)/shard_map/ppermute | solution.py:433
  99.4 3.1 %collective-permute-done.21 = bf16[416,384]{1,0:T(8,128)(2,1)S(1)} collective-permute-done((bf16[416,384]{1,0:T(8,128)(2,1)S(1)}, bf16[416,384]{1,0:T(8,128)(2,1)S(1)}, u32[]{:S(2)}, u32[]{:S(2)}) %collective-permute-start.21) | collective-permute-done | bytes 319520 | tf_op jit(solution)/shard_map/ppermute | solution.py:430
  102.9 3.3 %collective-permute-done.23.refs_2_ = bf16[72,768]{1,0:T(8,128)(2,1)S(1)} collective-permute-done((bf16[72,768]{1,0:T(8,128)(2,1)S(1)}, bf16[72,768]{1,0:T(8,128)(2,1)S(1)}, u32[]{:S(2)}, u32[]{:S(2)}) %collective-permute-start.23) | collective-permute-done | bytes 110624 | tf_op jit(solution)/shard_map/ppermute | solution.py:433
  106.2 2.3 %collective-permute-done.24.refs_3_ = bf16[144,768]{1,0:T(8,128)(2,1)S(1)} collective-permute-done((bf16[144,768]{1,0:T(8,128)(2,1)S(1)}, bf16[144,768]{1,0:T(8,128)(2,1)S(1)}, u32[]{:S(2)}, u32[]{:S(2)}) %collective-permute-start.24) | collective-permute-done | bytes 221216 | tf_op jit(solution)/shard_map/ppermute | solution.py:433
  108.5 0.7 copy-done.19
  109.3 1.6 collective-permute-done.26.other
  110.9 5.0 %shard_map.221 = (f32[394,768]{1,0:T(8,128)S(1)}, bf16[394,384]{1,0:T(8,128)(2,1)S(1)}, bf16[394,384]{1,0:T(8,128)(2,1)S(1)}, f32[16,768]{1,0:T(8,128)S(1)}, bf1...) custom-call(s32[8]{0:T(128)S(1)} %stack.38.ids, ...), custom_call_target="tpu_custom_call" | custom-call | flops 6899999744 | bytes 1024 | tf_op jit(solution)/shard_map/pallas_call | solution.py:413
  116.7 1.5 collective-permute-start.30
  118.2 1.4 collective-permute-start.31
  119.6 1.4 shard_map.222
  121.2 1.6 collective-permute-start.34
  122.8 4.1 %collective-permute-done.29.refs_1_ = bf16[192,768]{1,0:T(8,128)(2,1)S(1)} collective-permute-done((bf16[192,768]{1,0:T(8,128)(2,1)S(1)}, bf16[192,768]{1,0:T(8,128)(2,1)S(1)}, u32[]{:S(2)}, u32[]{:S(2)}) %collective-permute-start.29) | collective-permute-done | bytes 294944 | tf_op jit(solution)/shard_map/ppermute | solution.py:440
  126.9 5.1 %collective-permute-done.30.refs_2_ = bf16[192,768]{1,0:T(8,128)(2,1)S(1)} collective-permute-done((bf16[192,768]{1,0:T(8,128)(2,1)S(1)}, bf16[192,768]{1,0:T(8,128)(2,1)S(1)}, u32[]{:S(2)}, u32[]{:S(2)}) %collective-permute-start.30) | collective-permute-done | bytes 294944 | tf_op jit(solution)/shard_map/ppermute | solution.py:440
  132.3 1.6 collective-permute-start.28
  134.0 1.3 collective-permute-start.32
  135.3 1.2 collective-permute-start.38
  136.5 2.4 %shard_map.224 = (bf16[394,768]{1,0:T(8,128)(2,1)}, f32[16,768]{1,0:T(8,128)S(1)}) custom-call(s32[8]{0:T(128)S(1)} %stack.38.ids, bf16[394,384]{1,0:T(8,128)(2,1)S(1)} %add_convert_fusion.2.own, bf16[394,384]{1,0:T(8,128)(2,1)S(1)} %collective-permute-done.35.other, bf16[394,768]{1,0:T(8,128)(2,1)S(1)} %copy-done.3, ...), custom_call_target="tpu_custom_call" | custom-call | flops 11500000 | bytes 1024 | tf_op jit(solution)/shard_map/pallas_call | solution.py:413
  138.9 1.8 %collective-permute-start.36 = (f32[16,768]{1,0:T(8,128)S(1)}, f32[16,768]{1,0:T(8,128)S(1)}, u32[]{:S(2)}, u32[]{:S(2)}) collective-permute-start(f32[16,768]{1,0:T(8,128)S(1)} %get-tuple-element.218.small), channel_id=1, source_target_pairs={{0,4},{2,6},{4,0},{6,2},{1,5},{3,7},{5,1},{7,3},{8,12},{10,14},{12... | collective-permute-start | bytes 147464 | tf_op jit(solution)/shard_map/ppermute | solution.py:433
  141.0 0.8 add_convert_fusion.4
  141.8 10.4 %collective-permute-done.32.came = bf16[192,768]{1,0:T(8,128)(2,1)S(1)} collective-permute-done((bf16[192,768]{1,0:T(8,128)(2,1)S(1)}, bf16[192,768]{1,0:T(8,128)(2,1)S(1)}, u32[]{:S(2)}, u32[]{:S(2)}) %collective-permute-start.32) | collective-permute-done | bytes 294944 | tf_op jit(solution)/shard_map/ppermute | solution.py:433
  153.0 1.3 collective-permute-start.40
  154.3 2.2 %collective-permute-start.41 = (bf16[208,768]{1,0:T(8,128)(2,1)S(1)}, bf16[208,768]{1,0:T(8,128)(2,1)S(1)}, u32[]{:S(2)}, u32[]{:S(2)}) collective-permute-start(bf16[208,768]{1,0:T(8,128)(2,1)S(1)} %shard_map.225.refs_0_), channel_id=1, source_target_pairs={{0,2},{1,3},{2,0},{3,1},{4,6},{5,7},{6,4},{7,5},{8,10},{9,11},{10,... | collective-permute-start | bytes 958472 | tf_op jit(solution)/shard_map/ppermute | solution.py:440
  156.5 2.3 %select_convert_fusion = bf16[394,768]{1,0:T(8,128)(2,1)} fusion(f32[394,768]{1,0:T(8,128)S(1)} %copy-done.5, bf16[400,384]{1,0:T(8,128)(2,1)} %collective-permute-done.37, bf16[400,384]{1,0:T(8,128)(2,1)} %add_convert_fusion.4, pred[394]{0:T(512)(128)(4,1)S(1)} %iota_compare_fusion, pred[]{:T(512)S(6)} %eq.7), kind=kLoop, calls=%fused_computation | loop fusion | flops 3933696 | bytes 2430347 | tf_op jit(solution)/shard_map/convert_element_type | solution.py:718
  158.8 1.7 copy-done.23
  160.5 2.8 %shard_map.226 = (f32[384,768]{1,0:T(8,128)}, f32[768,384]{1,0:T(8,128)}) custom-call(f32[768,768]{1,0:T(8,128)S(1)} %copy-done.23, bf16[256,768]{1,0:T(8,128)(2,1)S(1)} %copy-done.20, bf16[512,768]{1,0:T(8,128)(2,1)} %collective-permute-done.38.came_rest), custom_call_target="tpu_custom_call" | custom-call | flops 2300000000 | bytes 1024 | tf_op jit(solution)/shard_map/pallas_call | solution.py:413
  163.3 1.0 collective-permute-done.39.refs_1_
  164.3 5.5 %collective-permute-done.40.refs_2_ = bf16[208,768]{1,0:T(8,128)(2,1)S(1)} collective-permute-done((bf16[208,768]{1,0:T(8,128)(2,1)S(1)}, bf16[208,768]{1,0:T(8,128)(2,1)S(1)}, u32[]{:S(2)}, u32[]{:S(2)}) %collective-permute-start.40) | collective-permute-done | bytes 319520 | tf_op jit(solution)/shard_map/ppermute | solution.py:440
  170.4 2.2 %shard_map.227 = (f32[576,768]{1,0:T(8,128)}, f32[192,768]{1,0:T(8,128)}, f32[768]{0:T(1024)}, f32[768]{0:T(1024)}, f32[768]{0:T(1024)}, /*index=5*/f32[768]{0:T(1024)}, f32[4,768]{1,0:T(4,128)}) custom-call(s32[8]{0:T(128)S(1)} %stack.38.ids, bf16[208,768]{1,0:T(8,128)(2,1)S(1)} %shard_map.225.refs_0_, ...), custom_call_target="tpu_custom_call" | custom-call | flops 3449999872 | bytes 1024 | tf_op jit(solution)/shard_map/pallas_call | solution.py:413
  (115 shorter events, 8.2 us)
Async XLA Ops:
  0.6 14.3 %collective-permute-start.2 = (bf16[768,768]{1,0:T(8,128)(2,1)}, bf16[768,768]{1,0:T(8,128)(2,1)S(1)}, u32[]{:S(2)}, u32[]{:S(2)}) collective-permute-start(bf16[768,768]{1,0:T(8,128)(2,1)} %bitcast.26), channel_id=1, source_target_pairs={{0,8},{8,0},{16,24},{24,16},{1,9},{9,1},{17,25},{25,17},{2,10},{10... | collective-permute-start | bytes 3538952 | tf_op jit(solution)/shard_map/ppermute | solution.py:430
  1.2 13.8 %collective-permute-start.3 = (bf16[768,768]{1,0:T(8,128)(2,1)}, bf16[768,768]{1,0:T(8,128)(2,1)S(1)}, u32[]{:S(2)}, u32[]{:S(2)}) collective-permute-start(bf16[768,768]{1,0:T(8,128)(2,1)} %bitcast.29), channel_id=1, source_target_pairs={{0,8},{8,0},{16,24},{24,16},{1,9},{9,1},{17,25},{25,17},{2,10},{10... | collective-permute-start | bytes 3538952 | tf_op jit(solution)/shard_map/ppermute | solution.py:430
  1.2 13.0 %collective-permute-start = (bf16[192,768]{1,0:T(8,128)(2,1)}, bf16[192,768]{1,0:T(8,128)(2,1)}, u32[]{:S(2)}, u32[]{:S(2)}) collective-permute-start(bf16[192,768]{1,0:T(8,128)(2,1)} %w_out.1), channel_id=1, source_target_pairs={{0,16},{8,24},{16,0},{24,8},{1,17},{9,25},{17,1},{25,9},{2,18},{10... | collective-permute-start | bytes 884744 | tf_op jit(solution)/shard_map/ppermute | solution.py:430
  4.2 10.1 %collective-permute-start.1 = (bf16[192,768]{1,0:T(8,128)(2,1)}, bf16[192,768]{1,0:T(8,128)(2,1)S(1)}, u32[]{:S(2)}, u32[]{:S(2)}) collective-permute-start(bf16[192,768]{1,0:T(8,128)(2,1)} %w_out.1), channel_id=1, source_target_pairs={{0,8},{8,0},{16,24},{24,16},{1,9},{9,1},{17,25},{25,17},{2,10},{10... | collective-permute-start | bytes 884744 | tf_op jit(solution)/shard_map/ppermute | solution.py:430
  5.9 1.2 copy-start.17
  7.8 8.6 %copy-start.11 = (bf16[768,4]{0,1:T(4,128)(2,1)S(1)}, bf16[768,4]{0,1:T(4,128)(2,1)}, u32[]{:S(2)}) copy-start(bf16[768,4]{0,1:T(4,128)(2,1)} %param.22) | copy-start | bytes 18436
  7.8 8.6 %copy-start.12 = (s32[394,2]{0,1:T(2,128)S(1)}, s32[394,2]{0,1:T(2,128)}, u32[]{:S(2)}) copy-start(s32[394,2]{0,1:T(2,128)} %param.14) | copy-start | bytes 9460
  7.8 18.8 %copy-start.3 = (bf16[394,768]{1,0:T(8,128)(2,1)S(1)}, bf16[394,768]{1,0:T(8,128)(2,1)}, u32[]{:S(2)}) copy-start(bf16[394,768]{1,0:T(8,128)(2,1)} %tokens.5) | copy-start | bytes 1815556
  7.8 18.8 %copy-start.8 = (bf16[192,768]{1,0:T(8,128)(2,1)S(1)}, bf16[192,768]{1,0:T(8,128)(2,1)}, u32[]{:S(2)}) copy-start(bf16[192,768]{1,0:T(8,128)(2,1)} %w_out.1) | copy-start | bytes 884740
  7.8 18.8 %copy-start.13 = (f32[768]{0:T(1024)S(1)}, f32[768]{0:T(1024)}, u32[]{:S(2)}) copy-start(f32[768]{0:T(1024)} %bias.3) | copy-start | bytes 9220
  7.8 18.8 %copy-start.14 = (f32[768]{0:T(1024)S(1)}, f32[768]{0:T(1024)}, u32[]{:S(2)}) copy-start(f32[768]{0:T(1024)} %gain.6) | copy-start | bytes 9220
  15.0 7.6 %collective-permute-start.5 = (bf16[394,192]{1,0:T(8,128)(2,1)S(1)}, bf16[394,192]{1,0:T(8,128)(2,1)}, u32[]{:S(2)}, u32[]{:S(2)}) collective-permute-start(bf16[394,192]{1,0:T(8,128)(2,1)S(1)} %get-tuple-element.125.rest_0_.head_out), channel_id=1, source_target_pairs={{0,16},{8,24},{16,0},{24,8},{1,17},{9,25},{17,1},{25,9},{2,18},{10... | collective-permute-start | bytes 453896 | tf_op jit(solution)/shard_map/ppermute | solution.py:430
  15.1 11.5 %collective-permute-start.7 = (bf16[192,768]{1,0:T(8,128)(2,1)}, bf16[192,768]{1,0:T(8,128)(2,1)}, u32[]{:S(2)}, u32[]{:S(2)}) collective-permute-start(bf16[192,768]{1,0:T(8,128)(2,1)} %collective-permute-done.rest_6_), channel_id=1, source_target_pairs={{0,8},{8,0},{16,24},{24,16},{1,9},{9,1},{17,25},{25,17},{2,10},{10... | collective-permute-start | bytes 884744 | tf_op jit(solution)/shard_map/ppermute | solution.py:430
  16.3 10.2 %collective-permute-start.4 = (bf16[394,192]{1,0:T(8,128)(2,1)S(1)}, bf16[394,192]{1,0:T(8,128)(2,1)S(1)}, u32[]{:S(2)}, u32[]{:S(2)}) collective-permute-start(bf16[394,192]{1,0:T(8,128)(2,1)S(1)} %get-tuple-element.125.rest_0_.head_out), channel_id=1, source_target_pairs={{0,8},{8,0},{16,24},{24,16},{1,9},{9,1},{17,25},{25,17},{2,10},{10... | collective-permute-start | bytes 453896 | tf_op jit(solution)/shard_map/ppermute | solution.py:430
  22.6 4.0 %collective-permute-start.6 = (bf16[394,192]{1,0:T(8,128)(2,1)}, bf16[394,192]{1,0:T(8,128)(2,1)S(1)}, u32[]{:S(2)}, u32[]{:S(2)}) collective-permute-start(bf16[394,192]{1,0:T(8,128)(2,1)} %collective-permute-done.5.rest_2_), channel_id=1, source_target_pairs={{0,8},{8,0},{16,24},{24,16},{1,9},{9,1},{17,25},{25,17},{2,10},{10... | collective-permute-start | bytes 453896 | tf_op jit(solution)/shard_map/ppermute | solution.py:430
  22.6 11.5 %collective-permute-start.8 = (bf16[72,768]{1,0:T(8,128)(2,1)S(1)}, bf16[72,768]{1,0:T(8,128)(2,1)S(1)}, u32[]{:S(2)}, u32[]{:S(2)}) collective-permute-start(bf16[72,768]{1,0:T(8,128)(2,1)S(1)} %get-tuple-element.142), channel_id=1, source_target_pairs={{0,4},{2,6},{4,0},{6,2},{1,5},{3,7},{5,1},{7,3},{8,12},{10,14},{12... | collective-permute-start | bytes 331784 | tf_op jit(solution)/shard_map/ppermute | solution.py:433
  25.2 26.7 %copy-start = (bf16[1,768,768]{2,1,0:T(8,128)(2,1)S(1)}, bf16[1,768,768]{2,1,0:T(8,128)(2,1)}, u32[]{:S(2)}) copy-start(bf16[1,768,768]{2,1,0:T(8,128)(2,1)} %param.23) | copy-start | bytes 3538948
  25.2 26.7 %copy-start.1 = (bf16[1,768,768]{2,1,0:T(8,128)(2,1)S(1)}, bf16[1,768,768]{2,1,0:T(8,128)(2,1)}, u32[]{:S(2)}) copy-start(bf16[1,768,768]{2,1,0:T(8,128)(2,1)} %param.24) | copy-start | bytes 3538948
  25.2 8.9 %collective-permute-start.9 = (bf16[72,768]{1,0:T(8,128)(2,1)S(1)}, bf16[72,768]{1,0:T(8,128)(2,1)S(1)}, u32[]{:S(2)}, u32[]{:S(2)}) collective-permute-start(bf16[72,768]{1,0:T(8,128)(2,1)S(1)} %get-tuple-element.143), channel_id=1, source_target_pairs={{0,6},{2,4},{4,2},{6,0},{1,7},{3,5},{5,3},{7,1},{8,14},{10,12},{12... | collective-permute-start | bytes 331784 | tf_op jit(solution)/shard_map/ppermute | solution.py:433
  30.9 80.0 %copy-start.4 = (f32[394,768]{1,0:T(8,128)}, f32[394,768]{1,0:T(8,128)S(1)}, u32[]{:S(2)}) copy-start(f32[394,768]{1,0:T(8,128)S(1)} %get-tuple-element.133.middle) | copy-start | bytes 3631108
  34.1 13.6 %collective-permute-start.10 = (bf16[144,768]{1,0:T(8,128)(2,1)S(1)}, bf16[144,768]{1,0:T(8,128)(2,1)S(1)}, u32[]{:S(2)}, u32[]{:S(2)}) collective-permute-start(bf16[144,768]{1,0:T(8,128)(2,1)S(1)} %get-tuple-element.145), channel_id=1, source_target_pairs={{0,2},{2,0},{4,6},{6,4},{1,3},{3,1},{5,7},{7,5},{8,10},{10,8},{12,... | collective-permute-start | bytes 663560 | tf_op jit(solution)/shard_map/ppermute | solution.py:433
  36.8 15.1 %collective-permute-start.11 = (bf16[144,768]{1,0:T(8,128)(2,1)S(1)}, bf16[144,768]{1,0:T(8,128)(2,1)S(1)}, u32[]{:S(2)}, u32[]{:S(2)}) collective-permute-start(bf16[144,768]{1,0:T(8,128)(2,1)S(1)} %get-tuple-element.147), channel_id=1, source_target_pairs={{0,2},{2,0},{4,6},{6,4},{1,3},{3,1},{5,7},{7,5},{8,10},{10,8},{12,... | collective-permute-start | bytes 663560 | tf_op jit(solution)/shard_map/ppermute | solution.py:433
  36.8 22.1 %collective-permute-start.12 = (bf16[144,768]{1,0:T(8,128)(2,1)S(1)}, bf16[144,768]{1,0:T(8,128)(2,1)S(1)}, u32[]{:S(2)}, u32[]{:S(2)}) collective-permute-start(bf16[144,768]{1,0:T(8,128)(2,1)S(1)} %get-tuple-element.150), channel_id=1, source_target_pairs={{0,4},{2,6},{4,0},{6,2},{1,5},{3,7},{5,1},{7,3},{8,12},{10,14},{12... | collective-permute-start | bytes 663560 | tf_op jit(solution)/shard_map/ppermute | solution.py:433
  40.7 19.1 %collective-permute-start.13 = (bf16[144,768]{1,0:T(8,128)(2,1)S(1)}, bf16[144,768]{1,0:T(8,128)(2,1)S(1)}, u32[]{:S(2)}, u32[]{:S(2)}) collective-permute-start(bf16[144,768]{1,0:T(8,128)(2,1)S(1)} %get-tuple-element.151), channel_id=1, source_target_pairs={{0,6},{2,4},{4,2},{6,0},{1,7},{3,5},{5,3},{7,1},{8,14},{10,12},{12... | collective-permute-start | bytes 663560 | tf_op jit(solution)/shard_map/ppermute | solution.py:433
  41.2 18.7 %collective-permute-start.14 = (bf16[2,72,768]{2,1,0:T(8,128)(2,1)S(1)}, bf16[2,72,768]{2,1,0:T(8,128)(2,1)S(1)}, u32[]{:S(2)}, u32[]{:S(2)}) collective-permute-start(bf16[2,72,768]{2,1,0:T(8,128)(2,1)S(1)} %pad_maximum_fusion.2), channel_id=1, source_target_pairs={{0,16},{8,24},{16,0},{24,8},{1,17},{9,25},{17,1},{25,9},{2,18},{10... | collective-permute-start | bytes 663560 | tf_op jit(solution)/shard_map/ppermute | solution.py:430
  67.2 11.5 %collective-permute-start.19 = (bf16[1536,768]{1,0:T(8,128)(2,1)S(1)}, bf16[1536,768]{1,0:T(8,128)(2,1)S(1)}, u32[]{:S(2)}, u32[]{:S(2)}) collective-permute-start(bf16[1536,768]{1,0:T(8,128)(2,1)S(1)} %get-tuple-element.174), channel_id=1, source_target_pairs={{0,8},{8,0},{16,24},{24,16},{1,9},{9,1},{17,25},{25,17},{2,10},{10... | collective-permute-start | bytes 7077896 | tf_op jit(solution)/shard_map/ppermute | solution.py:430
  67.3 13.1 %collective-permute-start.15 = (bf16[144,768]{1,0:T(8,128)(2,1)S(1)}, bf16[144,768]{1,0:T(8,128)(2,1)S(1)}, u32[]{:S(2)}, u32[]{:S(2)}) collective-permute-start(bf16[144,768]{1,0:T(8,128)(2,1)S(1)} %get-tuple-element.154), channel_id=1, source_target_pairs={{0,6},{2,4},{4,2},{6,0},{1,7},{3,5},{5,3},{7,1},{8,14},{10,12},{12... | collective-permute-start | bytes 663560 | tf_op jit(solution)/shard_map/ppermute | solution.py:433
  70.5 19.1 %collective-permute-start.16 = (bf16[144,768]{1,0:T(8,128)(2,1)S(1)}, bf16[144,768]{1,0:T(8,128)(2,1)S(1)}, u32[]{:S(2)}, u32[]{:S(2)}) collective-permute-start(bf16[144,768]{1,0:T(8,128)(2,1)S(1)} %get-tuple-element.157), channel_id=1, source_target_pairs={{0,4},{2,6},{4,0},{6,2},{1,5},{3,7},{5,1},{7,3},{8,12},{10,14},{12... | collective-permute-start | bytes 663560 | tf_op jit(solution)/shard_map/ppermute | solution.py:433
  70.5 19.1 %collective-permute-start.17 = (bf16[144,768]{1,0:T(8,128)(2,1)S(1)}, bf16[144,768]{1,0:T(8,128)(2,1)S(1)}, u32[]{:S(2)}, u32[]{:S(2)}) collective-permute-start(bf16[144,768]{1,0:T(8,128)(2,1)S(1)} %get-tuple-element.158), channel_id=1, source_target_pairs={{0,2},{2,0},{4,6},{6,4},{1,3},{3,1},{5,7},{7,5},{8,10},{10,8},{12,... | collective-permute-start | bytes 663560 | tf_op jit(solution)/shard_map/ppermute | solution.py:433
  71.8 6.9 %collective-permute-start.18 = (bf16[2,72,768]{2,1,0:T(8,128)(2,1)S(1)}, bf16[2,72,768]{2,1,0:T(8,128)(2,1)S(1)}, u32[]{:S(2)}, u32[]{:S(2)}) collective-permute-start(bf16[2,72,768]{2,1,0:T(8,128)(2,1)S(1)} %get-tuple-element.162), channel_id=1, source_target_pairs={{0,16},{8,24},{16,0},{24,8},{1,17},{9,25},{17,1},{25,9},{2,18},{10... | collective-permute-start | bytes 663560 | tf_op jit(solution)/shard_map/ppermute | solution.py:430
  80.4 10.7 %copy-start.22 = (f32[768,768]{1,0:T(8,128)}, f32[768,768]{1,0:T(8,128)S(1)}, u32[]{:S(2)}) copy-start(f32[768,768]{1,0:T(8,128)S(1)} %get-tuple-element.222.kept) | copy-start | bytes 7077892
  89.6 21.3 %copy-start.25 = (bf16[3,394,394]{2,1,0:T(8,128)(2,1)S(1)}, bf16[3,394,394]{2,1,0:T(8,128)(2,1)}, u32[]{:S(2)}) copy-start(bf16[3,394,394]{2,1,0:T(8,128)(2,1)} %copy-done.24) | copy-start | bytes 2794252
  89.6 21.3 %copy-start.27 = (bf16[394,768]{1,0:T(8,128)(2,1)S(1)}, bf16[394,768]{1,0:T(8,128)(2,1)}, u32[]{:S(2)}) copy-start(bf16[394,768]{1,0:T(8,128)(2,1)} %copy-done.26) | copy-start | bytes 1815556
  89.6 21.3 %copy-start.33 = (bf16[394,192]{1,0:T(8,128)(2,1)S(1)}, bf16[394,192]{1,0:T(8,128)(2,1)}, u32[]{:S(2)}) copy-start(bf16[394,192]{1,0:T(8,128)(2,1)} %copy-done.32) | copy-start | bytes 453892
  91.1 19.8 %copy-start.7 = (bf16[394,768]{1,0:T(8,128)(2,1)S(1)}, bf16[394,768]{1,0:T(8,128)(2,1)}, u32[]{:S(2)}) copy-start(bf16[394,768]{1,0:T(8,128)(2,1)} %cot.3) | copy-start | bytes 1815556
  91.1 19.8 %copy-start.18 = (bf16[768,3,192]{0,2,1:T(8,128)(2,1)S(1)}, bf16[768,3,192]{0,2,1:T(8,128)(2,1)}, u32[]{:S(2)}) copy-start(bf16[768,3,192]{0,2,1:T(8,128)(2,1)} %param.18) | copy-start | bytes 2654212
  91.1 19.8 %copy-start.29 = (bf16[394,192]{1,0:T(8,128)(2,1)S(1)}, bf16[394,192]{1,0:T(8,128)(2,1)}, u32[]{:S(2)}) copy-start(bf16[394,192]{1,0:T(8,128)(2,1)} %copy-done.28) | copy-start | bytes 453892
  91.2 19.8 %copy-start.31 = (bf16[394,192]{1,0:T(8,128)(2,1)S(1)}, bf16[394,192]{1,0:T(8,128)(2,1)}, u32[]{:S(2)}) copy-start(bf16[394,192]{1,0:T(8,128)(2,1)} %copy-done.30) | copy-start | bytes 453892
  91.2 1.7 collective-permute-start.20
  92.9 9.6 %collective-permute-start.21 = (bf16[416,384]{1,0:T(8,128)(2,1)S(1)}, bf16[416,384]{1,0:T(8,128)(2,1)S(1)}, u32[]{:S(2)}, u32[]{:S(2)}) collective-permute-start(bf16[416,384]{1,0:T(8,128)(2,1)S(1)} %add_convert_fusion.1), channel_id=1, source_target_pairs={{0,16},{8,24},{16,0},{24,8},{1,17},{9,25},{17,1},{25,9},{2,18},{10... | collective-permute-start | bytes 958472 | tf_op jit(solution)/shard_map/ppermute | solution.py:430
  93.5 15.0 %collective-permute-start.25 = (bf16[256,768]{1,0:T(8,128)(2,1)S(1)}, bf16[256,768]{1,0:T(8,128)(2,1)S(1)}, u32[]{:S(2)}, u32[]{:S(2)}) collective-permute-start(bf16[256,768]{1,0:T(8,128)(2,1)S(1)} %get-tuple-element.188), channel_id=1, source_target_pairs={{0,1},{1,0},{2,3},{3,2},{4,5},{5,4},{6,7},{7,6},{8,9},{9,8},{10,11... | collective-permute-start | bytes 1179656 | tf_op jit(solution)/shard_map/ppermute | solution.py:436
  95.1 7.9 %collective-permute-start.22 = (bf16[72,768]{1,0:T(8,128)(2,1)S(1)}, bf16[72,768]{1,0:T(8,128)(2,1)S(1)}, u32[]{:S(2)}, u32[]{:S(2)}) collective-permute-start(bf16[72,768]{1,0:T(8,128)(2,1)S(1)} %get-tuple-element.184), channel_id=1, source_target_pairs={{0,6},{2,4},{4,2},{6,0},{1,7},{3,5},{5,3},{7,1},{8,14},{10,12},{12... | collective-permute-start | bytes 331784 | tf_op jit(solution)/shard_map/ppermute | solution.py:433
  97.4 8.7 %collective-permute-start.23 = (bf16[72,768]{1,0:T(8,128)(2,1)S(1)}, bf16[72,768]{1,0:T(8,128)(2,1)S(1)}, u32[]{:S(2)}, u32[]{:S(2)}) collective-permute-start(bf16[72,768]{1,0:T(8,128)(2,1)S(1)} %get-tuple-element.185), channel_id=1, source_target_pairs={{0,4},{2,6},{4,0},{6,2},{1,5},{3,7},{5,1},{7,3},{8,12},{10,14},{12... | collective-permute-start | bytes 331784 | tf_op jit(solution)/shard_map/ppermute | solution.py:433
  97.4 11.1 %collective-permute-start.24 = (bf16[144,768]{1,0:T(8,128)(2,1)S(1)}, bf16[144,768]{1,0:T(8,128)(2,1)S(1)}, u32[]{:S(2)}, u32[]{:S(2)}) collective-permute-start(bf16[144,768]{1,0:T(8,128)(2,1)S(1)} %get-tuple-element.186), channel_id=1, source_target_pairs={{0,2},{2,0},{4,6},{6,4},{1,3},{3,1},{5,7},{7,5},{8,10},{10,8},{12,... | collective-permute-start | bytes 663560 | tf_op jit(solution)/shard_map/ppermute | solution.py:433
  109.2 1.6 collective-permute-start.26
  115.9 5.2 %collective-permute-start.33 = (bf16[394,384]{1,0:T(8,128)(2,1)S(1)}, bf16[394,384]{1,0:T(8,128)(2,1)S(1)}, u32[]{:S(2)}, u32[]{:S(2)}) collective-permute-start(bf16[394,384]{1,0:T(8,128)(2,1)S(1)} %get-tuple-element.215), channel_id=1, source_target_pairs={{0,8},{8,0},{16,24},{24,16},{1,9},{9,1},{17,25},{25,17},{2,10},{10... | collective-permute-start | bytes 907784 | tf_op jit(solution)/shard_map/ppermute | solution.py:430
  116.1 10.8 %collective-permute-start.29 = (bf16[192,768]{1,0:T(8,128)(2,1)S(1)}, bf16[192,768]{1,0:T(8,128)(2,1)S(1)}, u32[]{:S(2)}, u32[]{:S(2)}) collective-permute-start(bf16[192,768]{1,0:T(8,128)(2,1)S(1)} %get-tuple-element.210), channel_id=1, source_target_pairs={{0,3},{1,2},{2,1},{3,0},{4,7},{5,6},{6,5},{7,4},{8,11},{9,10},{10,... | collective-permute-start | bytes 884744 | tf_op jit(solution)/shard_map/ppermute | solution.py:440
  116.7 15.3 %collective-permute-start.30 = (bf16[192,768]{1,0:T(8,128)(2,1)S(1)}, bf16[192,768]{1,0:T(8,128)(2,1)S(1)}, u32[]{:S(2)}, u32[]{:S(2)}) collective-permute-start(bf16[192,768]{1,0:T(8,128)(2,1)S(1)} %get-tuple-element.211), channel_id=1, source_target_pairs={{0,1},{1,0},{2,3},{3,2},{4,5},{5,4},{6,7},{7,6},{8,9},{9,8},{10,11... | collective-permute-start | bytes 884744 | tf_op jit(solution)/shard_map/ppermute | solution.py:440
  118.2 13.8 %collective-permute-start.31 = (bf16[192,768]{1,0:T(8,128)(2,1)S(1)}, bf16[192,768]{1,0:T(8,128)(2,1)S(1)}, u32[]{:S(2)}, u32[]{:S(2)}) collective-permute-start(bf16[192,768]{1,0:T(8,128)(2,1)S(1)} %get-tuple-element.212), channel_id=1, source_target_pairs={{0,2},{1,3},{2,0},{3,1},{4,6},{5,7},{6,4},{7,5},{8,10},{9,11},{10,... | collective-permute-start | bytes 884744 | tf_op jit(solution)/shard_map/ppermute | solution.py:440
  121.1 11.1 %collective-permute-start.27 = (bf16[400,384]{1,0:T(8,128)(2,1)S(1)}, bf16[400,384]{1,0:T(8,128)(2,1)S(1)}, u32[]{:S(2)}, u32[]{:S(2)}) collective-permute-start(bf16[400,384]{1,0:T(8,128)(2,1)S(1)} %get-tuple-element.208), channel_id=1, source_target_pairs={{0,8},{8,0},{16,24},{24,16},{1,9},{9,1},{17,25},{25,17},{2,10},{10... | collective-permute-start | bytes 921608 | tf_op jit(solution)/shard_map/ppermute | solution.py:430
  121.2 12.6 %collective-permute-start.34 = (bf16[394,384]{1,0:T(8,128)(2,1)S(1)}, bf16[394,384]{1,0:T(8,128)(2,1)S(1)}, u32[]{:S(2)}, u32[]{:S(2)}) collective-permute-start(bf16[394,384]{1,0:T(8,128)(2,1)S(1)} %add_convert_fusion.3), channel_id=1, source_target_pairs={{0,16},{8,24},{16,0},{24,8},{1,17},{9,25},{17,1},{25,9},{2,18},{10... | collective-permute-start | bytes 907784 | tf_op jit(solution)/shard_map/ppermute | solution.py:430
  132.2 4.3 %copy-start.16 = (f32[768]{0:T(1024)S(1)}, f32[768]{0:T(1024)}, u32[]{:S(2)}) copy-start(f32[768]{0:T(1024)} %gain.7) | copy-start | bytes 9220
  132.3 8.7 %collective-permute-start.28 = (bf16[400,384]{1,0:T(8,128)(2,1)S(1)}, bf16[400,384]{1,0:T(8,128)(2,1)S(1)}, u32[]{:S(2)}, u32[]{:S(2)}) collective-permute-start(bf16[400,384]{1,0:T(8,128)(2,1)S(1)} %add_convert_fusion.5), channel_id=1, source_target_pairs={{0,16},{8,24},{16,0},{24,8},{1,17},{9,25},{17,1},{25,9},{2,18},{10... | collective-permute-start | bytes 921608 | tf_op jit(solution)/shard_map/ppermute | solution.py:430
  133.9 2.5 %collective-permute-start.35 = (bf16[394,384]{1,0:T(8,128)(2,1)S(1)}, bf16[394,384]{1,0:T(8,128)(2,1)S(1)}, u32[]{:S(2)}, u32[]{:S(2)}) collective-permute-start(bf16[394,384]{1,0:T(8,128)(2,1)S(1)} %add_convert_fusion.2.own), channel_id=1, source_target_pairs={{0,8},{8,0},{16,24},{24,16},{1,9},{9,1},{17,25},{25,17},{2,10},{10... | collective-permute-start | bytes 907784 | tf_op jit(solution)/shard_map/ppermute | solution.py:430
  134.0 18.1 %collective-permute-start.32 = (bf16[192,768]{1,0:T(8,128)(2,1)S(1)}, bf16[192,768]{1,0:T(8,128)(2,1)S(1)}, u32[]{:S(2)}, u32[]{:S(2)}) collective-permute-start(bf16[192,768]{1,0:T(8,128)(2,1)S(1)} %shard_map.223.own), channel_id=1, source_target_pairs={{0,4},{2,6},{4,0},{6,2},{1,5},{3,7},{5,1},{7,3},{8,12},{10,14},{12... | collective-permute-start | bytes 884744 | tf_op jit(solution)/shard_map/ppermute | solution.py:433
  135.3 23.5 %collective-permute-start.38 = (bf16[512,768]{1,0:T(8,128)(2,1)S(1)}, bf16[512,768]{1,0:T(8,128)(2,1)}, u32[]{:S(2)}, u32[]{:S(2)}) collective-permute-start(bf16[512,768]{1,0:T(8,128)(2,1)S(1)} %get-tuple-element.224), channel_id=1, source_target_pairs={{0,1},{1,0},{2,3},{3,2},{4,5},{5,4},{6,7},{7,6},{8,9},{9,8},{10,11... | collective-permute-start | bytes 2359304 | tf_op jit(solution)/shard_map/ppermute | solution.py:436
  138.9 13.9 %collective-permute-start.36 = (f32[16,768]{1,0:T(8,128)S(1)}, f32[16,768]{1,0:T(8,128)S(1)}, u32[]{:S(2)}, u32[]{:S(2)}) collective-permute-start(f32[16,768]{1,0:T(8,128)S(1)} %get-tuple-element.218.small), channel_id=1, source_target_pairs={{0,4},{2,6},{4,0},{6,2},{1,5},{3,7},{5,1},{7,3},{8,12},{10,14},{12... | collective-permute-start | bytes 147464 | tf_op jit(solution)/shard_map/ppermute | solution.py:433
  141.8 14.7 %copy-start.5 = (f32[394,768]{1,0:T(8,128)S(1)}, f32[394,768]{1,0:T(8,128)}, u32[]{:S(2)}) copy-start(f32[394,768]{1,0:T(8,128)} %copy-done.4) | copy-start | bytes 3631108
  152.8 3.7 %collective-permute-start.37 = (bf16[400,384]{1,0:T(8,128)(2,1)}, bf16[400,384]{1,0:T(8,128)(2,1)}, u32[]{:S(2)}, u32[]{:S(2)}) collective-permute-start(bf16[400,384]{1,0:T(8,128)(2,1)} %add_convert_fusion.4), channel_id=1, source_target_pairs={{0,8},{8,0},{16,24},{24,16},{1,9},{9,1},{17,25},{25,17},{2,10},{10... | collective-permute-start | bytes 921608 | tf_op jit(solution)/shard_map/ppermute | solution.py:430
  152.9 5.9 %copy-start.20 = (bf16[256,768]{1,0:T(8,128)(2,1)S(1)}, bf16[256,768]{1,0:T(8,128)(2,1)}, u32[]{:S(2)}) copy-start(bf16[256,768]{1,0:T(8,128)(2,1)} %copy-done.19) | copy-start | bytes 1179652
  153.0 11.4 %collective-permute-start.39 = (bf16[208,768]{1,0:T(8,128)(2,1)S(1)}, bf16[208,768]{1,0:T(8,128)(2,1)S(1)}, u32[]{:S(2)}, u32[]{:S(2)}) collective-permute-start(bf16[208,768]{1,0:T(8,128)(2,1)S(1)} %shard_map.225.refs_0_), channel_id=1, source_target_pairs={{0,3},{1,2},{2,1},{3,0},{4,7},{5,6},{6,5},{7,4},{8,11},{9,10},{10,... | collective-permute-start | bytes 958472 | tf_op jit(solution)/shard_map/ppermute | solution.py:440
  153.0 16.8 %collective-permute-start.40 = (bf16[208,768]{1,0:T(8,128)(2,1)S(1)}, bf16[208,768]{1,0:T(8,128)(2,1)S(1)}, u32[]{:S(2)}, u32[]{:S(2)}) collective-permute-start(bf16[208,768]{1,0:T(8,128)(2,1)S(1)} %shard_map.225.refs_0_), channel_id=1, source_target_pairs={{0,1},{1,0},{2,3},{3,2},{4,5},{5,4},{6,7},{7,6},{8,9},{9,8},{10,11... | collective-permute-start | bytes 958472 | tf_op jit(solution)/shard_map/ppermute | solution.py:440
  154.3 16.1 %collective-permute-start.41 = (bf16[208,768]{1,0:T(8,128)(2,1)S(1)}, bf16[208,768]{1,0:T(8,128)(2,1)S(1)}, u32[]{:S(2)}, u32[]{:S(2)}) collective-permute-start(bf16[208,768]{1,0:T(8,128)(2,1)S(1)} %shard_map.225.refs_0_), channel_id=1, source_target_pairs={{0,2},{1,3},{2,0},{3,1},{4,6},{5,7},{6,4},{7,5},{8,10},{9,11},{10,... | collective-permute-start | bytes 958472 | tf_op jit(solution)/shard_map/ppermute | solution.py:440
  158.8 1.7 copy-start.23
  (12 other events, 9.9 us)

commit v9 on v8

--- a/solution.py
+++ b/solution.py
@@ -517,7 +517,7 @@
             + [((LANES, width), BF16)]
             + [(shape, BF16) for shape in cot_shapes],
             [ids, after(routes.T, head_out), cotangent, w_router.T],
-            micros=0.01,
+            micros=2,
         )
         head_x = after(head_x, table)
         if small_slice:
@@ -535,7 +535,7 @@
                 ((n_tensor, inner, width), BF16),
                 ((rows, width), BF16),
             ],
-            micros=0.01,
+            micros=3,
         )
         if small_slice:
             *row_blocks, far_2, far_3 = lax.optimization_barrier((*row_blocks, *d_rows_in[2:]))
@@ -633,8 +633,7 @@
         else:
             gated_home = exchange(list(gated_blocks))
         came_first = dp_swap(sent_first)
-        own, *gated_home, came_first = lax.optimization_barrier((own, *gated_home[::-1], came_first))
-        gated_home = gated_home[::-1]
+        own, came_first, *gated_home = lax.optimization_barrier((own, came_first, *gated_home))
         other = tensor_swap(own, 1)
 
         parts = 4 if small_slice else 1

time: 173 us -> 168 us (0.971)
  local copies, waits for them, and re-layouts: 12.9 us -> 3.81 us
  waiting for transfers between devices: 73.4 us -> 76.6 us
  starting transfers between devices: 42.1 us -> 44.8 us
    unnamed x68 -> x38, local copies, waits for them, and re-layouts: 12.8 us -> 3.69 us
    ppermute x6, waiting for transfers between devices: 16.4 us -> 20.1 us  [quarter_swap(): return lax.ppermute(value, ('expert', 'dp'), pairs)]
    ppermute x20, starting transfers between devices: 9.53 us -> 11.9 us  [tensor_swap(): lax.ppermute(value, 'tensor', [(i, i ^ mask) for i in range(n_tensor)])]
where the time goes in v9:
time: 168 us
  waiting for transfers between devices  76.6 us (46%)
  starting transfers between devices  44.8 us (27%)
  Pallas kernels  37.2 us (22%)
  local copies, waits for them, and re-layouts  3.81 us (2%)
  other arithmetic  3.56 us (2%)
  between operations  1.7 us (1%)
    ppermute x14, waiting for transfers between devices, expert_swap(): lax.ppermute(value, 'expert', [(i, i ^ mask) for i in range(n_expert)])  39.5 us
    pallas_call x16, Pallas kernels, run(): pl.pallas_call(kernel, out_shape=[jax.ShapeDtypeStruct(shape, kind) for s...  37.2 us
    ppermute x14, starting transfers between devices, expert_swap(): lax.ppermute(value, 'expert', [(i, i ^ mask) for i in range(n_expert)])  23 us
    ppermute x6, waiting for transfers between devices, quarter_swap(): return lax.ppermute(value, ('expert', 'dp'), pairs)  20.1 us
    ppermute x20, waiting for transfers between devices, tensor_swap(): lax.ppermute(value, 'tensor', [(i, i ^ mask) for i in range(n_tensor)])  17.1 us
    ppermute x20, starting transfers between devices, tensor_swap(): lax.ppermute(value, 'tensor', [(i, i ^ mask) for i in range(n_tensor)])  11.9 us
    ppermute x6, starting transfers between devices, quarter_swap(): return lax.ppermute(value, ('expert', 'dp'), pairs)  7.05 us
    unnamed x38, local copies, waits for them, and re-layouts  3.69 us
  transfers between devices with their start and end apart: 42, of which 21 were waited for; matrix products, arithmetic and copies ran while one was open for 2% of the time, Pallas kernels for 13%

profile of v9, /device:TPU:0, one launch (start us, length us, event | category | flops | bytes accessed | tf_op | source)
XLA Modules:
  0.0 167.6 jit_solution(2524083321584492377)
XLA Ops:
  0.6 0.5 collective-permute-start.2
  1.2 2.9 %collective-permute-start = (bf16[192,768]{1,0:T(8,128)(2,1)}, bf16[192,768]{1,0:T(8,128)(2,1)S(1)}, u32[]{:S(2)}, u32[]{:S(2)}) collective-permute-start(bf16[192,768]{1,0:T(8,128)(2,1)} %w_out.1), channel_id=1, source_target_pairs={{0,16},{8,24},{16,0},{24,8},{1,17},{9,25},{17,1},{25,9},{2,18},{10... | collective-permute-start | bytes 884744 | tf_op jit(solution)/shard_map/ppermute | solution.py:430
  4.9 1.1 copy-done.4
  6.0 0.7 copy-done.6
  6.7 1.2 copy-done.8
  7.8 0.7 copy-done.13
  8.5 2.5 %shard_map.212 = (bf16[394,768]{1,0:T(8,128)(2,1)S(1)}, bf16[394,192]{1,0:T(8,128)(2,1)S(1)}, bf16[394,192]{1,0:T(8,128)(2,1)S(1)}, bf16[394,192]{1,0:T(8,128)(2...) custom-call(bf16[394,768]{1,0:T(8,128)(2,1)S(1)} %copy-done.4, f32[768]{0:T(1024)S(1)} %copy-done.6, ...), custom_call_target="tpu_custom_call" | custom-call | flops 4600000000 | bytes 1024 | tf_op jit(solution)/shard_map/pallas_call | solution.py:413
  11.1 0.6 collective-permute-done.rest_6_
  11.7 1.8 %collective-permute-start.5 = (bf16[394,192]{1,0:T(8,128)(2,1)S(1)}, bf16[394,192]{1,0:T(8,128)(2,1)S(1)}, u32[]{:S(2)}, u32[]{:S(2)}) collective-permute-start(bf16[394,192]{1,0:T(8,128)(2,1)S(1)} %get-tuple-element.125.rest_0_.head_out), channel_id=1, source_target_pairs={{0,16},{8,24},{16,0},{24,8},{1,17},{9,25},{17,1},{25,9},{2,18},{10... | collective-permute-start | bytes 453896 | tf_op jit(solution)/shard_map/ppermute | solution.py:430
  13.7 1.4 shard_map.213
  15.1 4.1 %collective-permute-done.5.rest_2_ = bf16[394,192]{1,0:T(8,128)(2,1)S(1)} collective-permute-done((bf16[394,192]{1,0:T(8,128)(2,1)S(1)}, bf16[394,192]{1,0:T(8,128)(2,1)S(1)}, u32[]{:S(2)}, u32[]{:S(2)}) %collective-permute-start.5) | collective-permute-done | bytes 151328 | tf_op jit(solution)/shard_map/ppermute | solution.py:430
  19.2 2.8 %collective-permute-start.8 = (bf16[72,768]{1,0:T(8,128)(2,1)S(1)}, bf16[72,768]{1,0:T(8,128)(2,1)S(1)}, u32[]{:S(2)}, u32[]{:S(2)}) collective-permute-start(bf16[72,768]{1,0:T(8,128)(2,1)S(1)} %get-tuple-element.142), channel_id=1, source_target_pairs={{0,4},{2,6},{4,0},{6,2},{1,5},{3,7},{5,1},{7,3},{8,12},{10,14},{12... | collective-permute-start | bytes 331784 | tf_op jit(solution)/shard_map/ppermute | solution.py:433
  22.0 1.3 collective-permute-start.9
  23.5 2.7 %shard_map.214 = (f32[394,768]{1,0:T(8,128)S(1)}, bf16[144,768]{1,0:T(8,128)(2,1)S(1)}, bf16[144,768]{1,0:T(8,128)(2,1)S(1)}, bf16[144,768]{1,0:T(8,128)(2,1)S(1)}, bf16[144,768]{1,0:T(8,128)(2,1)S(1)}) custom-call(s32[8]{0:T(128)S(1)} %stack.38.ids, bf16[394,768]{1,0:T(8,128)(2,1)S(1)} %copy-done.5, f32[768]{0:T(1024)S(1)} %copy-done.16, ...), custom_call_target="tpu_custom_call" | custom-call | flops 3449999872 | bytes 1024 | tf_op jit(solution)/shard_map/pallas_call | solution.py:413
  26.2 4.6 %collective-permute-done.8.refs_2_ = bf16[72,768]{1,0:T(8,128)(2,1)S(1)} collective-permute-done((bf16[72,768]{1,0:T(8,128)(2,1)S(1)}, bf16[72,768]{1,0:T(8,128)(2,1)S(1)}, u32[]{:S(2)}, u32[]{:S(2)}) %collective-permute-start.8) | collective-permute-done | bytes 110624 | tf_op jit(solution)/shard_map/ppermute | solution.py:433
  30.8 2.9 %collective-permute-start.10 = (bf16[144,768]{1,0:T(8,128)(2,1)S(1)}, bf16[144,768]{1,0:T(8,128)(2,1)S(1)}, u32[]{:S(2)}, u32[]{:S(2)}) collective-permute-start(bf16[144,768]{1,0:T(8,128)(2,1)S(1)} %get-tuple-element.145), channel_id=1, source_target_pairs={{0,2},{2,0},{4,6},{6,4},{1,3},{3,1},{5,7},{7,5},{8,10},{10,8},{12,... | collective-permute-start | bytes 663560 | tf_op jit(solution)/shard_map/ppermute | solution.py:433
  33.7 3.9 %collective-permute-start.12 = (bf16[144,768]{1,0:T(8,128)(2,1)S(1)}, bf16[144,768]{1,0:T(8,128)(2,1)S(1)}, u32[]{:S(2)}, u32[]{:S(2)}) collective-permute-start(bf16[144,768]{1,0:T(8,128)(2,1)S(1)} %get-tuple-element.150), channel_id=1, source_target_pairs={{0,4},{2,6},{4,0},{6,2},{1,5},{3,7},{5,1},{7,3},{8,12},{10,14},{12... | collective-permute-start | bytes 663560 | tf_op jit(solution)/shard_map/ppermute | solution.py:433
  38.0 1.6 collective-permute-start.14
  39.6 5.0 %collective-permute-done.10.refs_1_ = bf16[144,768]{1,0:T(8,128)(2,1)S(1)} collective-permute-done((bf16[144,768]{1,0:T(8,128)(2,1)S(1)}, bf16[144,768]{1,0:T(8,128)(2,1)S(1)}, u32[]{:S(2)}, u32[]{:S(2)}) %collective-permute-start.10) | collective-permute-done | bytes 221216 | tf_op jit(solution)/shard_map/ppermute | solution.py:433
  44.6 4.2 %collective-permute-done.11.refs_3_ = bf16[144,768]{1,0:T(8,128)(2,1)S(1)} collective-permute-done((bf16[144,768]{1,0:T(8,128)(2,1)S(1)}, bf16[144,768]{1,0:T(8,128)(2,1)S(1)}, u32[]{:S(2)}, u32[]{:S(2)}) %collective-permute-start.11) | collective-permute-done | bytes 221216 | tf_op jit(solution)/shard_map/ppermute | solution.py:433
  48.8 7.0 %shard_map.215 = (bf16[144,768]{1,0:T(8,128)(2,1)S(1)}, bf16[144,768]{1,0:T(8,128)(2,1)S(1)}, bf16[2,144,768]{2,1,0:T(8,128)(2,1)S(1)}, bf16[2,144,768]{2,1,0:T(...) custom-call(s32[8]{0:T(128)S(1)} %stack.38.ids, ...), custom_call_target="tpu_custom_call" | custom-call | flops 57500000 | bytes 1024 | tf_op jit(solution)/shard_map/pallas_call | solution.py:413
  55.8 0.9 collective-permute-done.13.refs_1_
  56.7 4.8 %shard_map.216 = (bf16[144,768]{1,0:T(8,128)(2,1)S(1)}, bf16[144,768]{1,0:T(8,128)(2,1)S(1)}, bf16[2,72,768]{2,1,0:T(8,128)(2,1)S(1)}, bf16[2,72,768]{2,1,0:T(8,...) custom-call(s32[8]{0:T(128)S(1)} %stack.38.ids, ...), custom_call_target="tpu_custom_call" | custom-call | flops 57500000 | bytes 1024 | tf_op jit(solution)/shard_map/pallas_call | solution.py:413
  61.5 2.7 %shard_map.218 = (bf16[1536,768]{1,0:T(8,128)(2,1)S(1)}, bf16[1536,768]{1,0:T(8,128)(2,1)S(1)}) custom-call(bf16[288,768]{1,0:T(8,128)(2,1)S(1)} %get-tuple-element.165.refs_0_, bf16[288,768]{1,0:T(8,128)(2,1)S(1)} %get-tuple-element.166.refs_1_, bf16[288,768]{1,0:T(8,128)(2,1)S(1)} %get-tuple-element.167.refs_2_, ...), custom_call_target="tpu_custom_call" | custom-call | flops 4600000000 | bytes 1024 | tf_op jit(solution)/shard_map/pallas_call | solution.py:413
  64.3 3.2 %collective-permute-start.15 = (bf16[144,768]{1,0:T(8,128)(2,1)S(1)}, bf16[144,768]{1,0:T(8,128)(2,1)S(1)}, u32[]{:S(2)}, u32[]{:S(2)}) collective-permute-start(bf16[144,768]{1,0:T(8,128)(2,1)S(1)} %get-tuple-element.154), channel_id=1, source_target_pairs={{0,6},{2,4},{4,2},{6,0},{1,7},{3,5},{5,3},{7,1},{8,14},{10,12},{12... | collective-permute-start | bytes 663560 | tf_op jit(solution)/shard_map/ppermute | solution.py:433
  67.5 1.2 collective-permute-start.17
  68.7 1.5 collective-permute-start.18
  70.3 5.4 %collective-permute-done.18.came = bf16[2,72,768]{2,1,0:T(8,128)(2,1)S(1)} collective-permute-done((bf16[2,72,768]{2,1,0:T(8,128)(2,1)S(1)}, bf16[2,72,768]{2,1,0:T(8,128)(2,1)S(1)}, u32[]{:S(2)}, u32[]{:S(2)}) %collective-permute-start.18) | collective-permute-done | bytes 221216 | tf_op jit(solution)/shard_map/ppermute | solution.py:430
  75.7 1.6 shard_map.219
  77.4 9.2 %collective-permute-done.16.refs_2_ = bf16[144,768]{1,0:T(8,128)(2,1)S(1)} collective-permute-done((bf16[144,768]{1,0:T(8,128)(2,1)S(1)}, bf16[144,768]{1,0:T(8,128)(2,1)S(1)}, u32[]{:S(2)}, u32[]{:S(2)}) %collective-permute-start.16) | collective-permute-done | bytes 221216 | tf_op jit(solution)/shard_map/ppermute | solution.py:433
  86.6 1.5 shard_map.220
  88.2 1.6 collective-permute-done.20
  89.8 1.6 collective-permute-start.21
  91.4 1.5 collective-permute-start.22
  92.9 3.0 %collective-permute-start.24 = (bf16[72,768]{1,0:T(8,128)(2,1)S(1)}, bf16[72,768]{1,0:T(8,128)(2,1)S(1)}, u32[]{:S(2)}, u32[]{:S(2)}) collective-permute-start(bf16[72,768]{1,0:T(8,128)(2,1)S(1)} %get-tuple-element.187), channel_id=1, source_target_pairs={{0,4},{2,6},{4,0},{6,2},{1,5},{3,7},{5,1},{7,3},{8,12},{10,14},{12... | collective-permute-start | bytes 331784 | tf_op jit(solution)/shard_map/ppermute | solution.py:433
  95.9 1.4 collective-permute-start.25
  97.3 2.2 %collective-permute-done.21 = bf16[416,384]{1,0:T(8,128)(2,1)S(1)} collective-permute-done((bf16[416,384]{1,0:T(8,128)(2,1)S(1)}, bf16[416,384]{1,0:T(8,128)(2,1)S(1)}, u32[]{:S(2)}, u32[]{:S(2)}) %collective-permute-start.21) | collective-permute-done | bytes 319520 | tf_op jit(solution)/shard_map/ppermute | solution.py:430
  99.6 1.6 collective-permute-done.24.refs_2_
  101.2 4.2 %collective-permute-done.25.refs_1_ = bf16[72,768]{1,0:T(8,128)(2,1)S(1)} collective-permute-done((bf16[72,768]{1,0:T(8,128)(2,1)S(1)}, bf16[72,768]{1,0:T(8,128)(2,1)S(1)}, u32[]{:S(2)}, u32[]{:S(2)}) %collective-permute-start.25) | collective-permute-done | bytes 110624 | tf_op jit(solution)/shard_map/ppermute | solution.py:433
  105.3 1.6 collective-permute-done.26.other
  107.0 5.0 %shard_map.221 = (f32[394,768]{1,0:T(8,128)S(1)}, bf16[394,384]{1,0:T(8,128)(2,1)S(1)}, bf16[394,384]{1,0:T(8,128)(2,1)S(1)}, f32[16,768]{1,0:T(8,128)S(1)}, bf1...) custom-call(s32[8]{0:T(128)S(1)} %stack.38.ids, ...), custom_call_target="tpu_custom_call" | custom-call | flops 6899999744 | bytes 1024 | tf_op jit(solution)/shard_map/pallas_call | solution.py:413
  112.1 0.7 collective-permute-start.29
  112.9 1.5 collective-permute-start.30
  114.4 1.2 collective-permute-start.31
  115.6 1.4 shard_map.222
  117.3 0.6 collective-permute-start.34
  117.8 5.1 %collective-permute-done.29.refs_1_ = bf16[192,768]{1,0:T(8,128)(2,1)S(1)} collective-permute-done((bf16[192,768]{1,0:T(8,128)(2,1)S(1)}, bf16[192,768]{1,0:T(8,128)(2,1)S(1)}, u32[]{:S(2)}, u32[]{:S(2)}) %collective-permute-start.29) | collective-permute-done | bytes 294944 | tf_op jit(solution)/shard_map/ppermute | solution.py:440
  122.9 5.3 %collective-permute-done.30.refs_2_ = bf16[192,768]{1,0:T(8,128)(2,1)S(1)} collective-permute-done((bf16[192,768]{1,0:T(8,128)(2,1)S(1)}, bf16[192,768]{1,0:T(8,128)(2,1)S(1)}, u32[]{:S(2)}, u32[]{:S(2)}) %collective-permute-start.30) | collective-permute-done | bytes 294944 | tf_op jit(solution)/shard_map/ppermute | solution.py:440
  128.4 0.6 collective-permute-start.28
  129.2 1.5 collective-permute-start.32
  130.7 1.3 collective-permute-start.38
  132.0 2.4 %shard_map.224 = (bf16[394,768]{1,0:T(8,128)(2,1)}, f32[16,768]{1,0:T(8,128)S(1)}) custom-call(s32[8]{0:T(128)S(1)} %stack.38.ids, bf16[394,384]{1,0:T(8,128)(2,1)S(1)} %add_convert_fusion.2.own, bf16[394,384]{1,0:T(8,128)(2,1)S(1)} %collective-permute-done.35.other, bf16[394,768]{1,0:T(8,128)(2,1)S(1)} %copy-done.5, ...), custom_call_target="tpu_custom_call" | custom-call | flops 11500000 | bytes 1024 | tf_op jit(solution)/shard_map/pallas_call | solution.py:413
  134.4 1.2 collective-permute-start.36
  135.7 1.6 collective-permute-done.28
  137.3 0.8 add_convert_fusion.4
  138.1 9.3 %collective-permute-done.32.came = bf16[192,768]{1,0:T(8,128)(2,1)S(1)} collective-permute-done((bf16[192,768]{1,0:T(8,128)(2,1)S(1)}, bf16[192,768]{1,0:T(8,128)(2,1)S(1)}, u32[]{:S(2)}, u32[]{:S(2)}) %collective-permute-start.32) | collective-permute-done | bytes 294944 | tf_op jit(solution)/shard_map/ppermute | solution.py:433
  147.4 0.6 collective-permute-done.36.small_came
  148.2 1.1 collective-permute-start.40
  149.3 2.4 %collective-permute-start.41 = (bf16[208,768]{1,0:T(8,128)(2,1)S(1)}, bf16[208,768]{1,0:T(8,128)(2,1)S(1)}, u32[]{:S(2)}, u32[]{:S(2)}) collective-permute-start(bf16[208,768]{1,0:T(8,128)(2,1)S(1)} %shard_map.225.refs_0_), channel_id=1, source_target_pairs={{0,2},{1,3},{2,0},{3,1},{4,6},{5,7},{6,4},{7,5},{8,10},{9,11},{10,... | collective-permute-start | bytes 958472 | tf_op jit(solution)/shard_map/ppermute | solution.py:440
  151.7 2.3 %select_convert_fusion = bf16[394,768]{1,0:T(8,128)(2,1)} fusion(f32[394,768]{1,0:T(8,128)S(1)} %copy-done.3, bf16[400,384]{1,0:T(8,128)(2,1)} %collective-permute-done.37, bf16[400,384]{1,0:T(8,128)(2,1)} %add_convert_fusion.4, pred[394]{0:T(512)(128)(4,1)S(1)} %iota_compare_fusion, pred[]{:T(512)S(6)} %eq.7), kind=kLoop, calls=%fused_computation | loop fusion | flops 3933696 | bytes 2430347 | tf_op jit(solution)/shard_map/convert_element_type | solution.py:717
  154.1 1.7 %shard_map.226 = (f32[384,768]{1,0:T(8,128)}, f32[768,384]{1,0:T(8,128)}) custom-call(f32[768,768]{1,0:T(8,128)S(1)} %copy-done.18, bf16[256,768]{1,0:T(8,128)(2,1)S(1)} %collective-permute-done.22.came_first, bf16[512,768]{1,0:T(8,128)(2,1)S(1)} %collective-permute-done.38.came_rest), custom_call_target="tpu_custom_call" | custom-call | flops 2300000000 | bytes 1024 | tf_op jit(solution)/shard_map/pallas_call | solution.py:413
  155.7 3.8 %collective-permute-done.39.refs_1_ = bf16[208,768]{1,0:T(8,128)(2,1)S(1)} collective-permute-done((bf16[208,768]{1,0:T(8,128)(2,1)S(1)}, bf16[208,768]{1,0:T(8,128)(2,1)S(1)}, u32[]{:S(2)}, u32[]{:S(2)}) %collective-permute-start.39) | collective-permute-done | bytes 319520 | tf_op jit(solution)/shard_map/ppermute | solution.py:440
  159.5 5.5 %collective-permute-done.40.refs_2_ = bf16[208,768]{1,0:T(8,128)(2,1)S(1)} collective-permute-done((bf16[208,768]{1,0:T(8,128)(2,1)S(1)}, bf16[208,768]{1,0:T(8,128)(2,1)S(1)}, u32[]{:S(2)}, u32[]{:S(2)}) %collective-permute-start.40) | collective-permute-done | bytes 319520 | tf_op jit(solution)/shard_map/ppermute | solution.py:440
  165.5 2.2 %shard_map.227 = (f32[576,768]{1,0:T(8,128)}, f32[192,768]{1,0:T(8,128)}, f32[768]{0:T(1024)}, f32[768]{0:T(1024)}, f32[768]{0:T(1024)}, /*index=5*/f32[768]{0:T(1024)}, f32[4,768]{1,0:T(4,128)}) custom-call(s32[8]{0:T(128)S(1)} %stack.38.ids, bf16[208,768]{1,0:T(8,128)(2,1)S(1)} %shard_map.225.refs_0_, ...), custom_call_target="tpu_custom_call" | custom-call | flops 3449999872 | bytes 1024 | tf_op jit(solution)/shard_map/pallas_call | solution.py:413
  (85 shorter events, 2.9 us)
Async XLA Ops:
  0.6 11.0 %collective-permute-start.2 = (bf16[768,768]{1,0:T(8,128)(2,1)}, bf16[768,768]{1,0:T(8,128)(2,1)S(1)}, u32[]{:S(2)}, u32[]{:S(2)}) collective-permute-start(bf16[768,768]{1,0:T(8,128)(2,1)} %bitcast.26), channel_id=1, source_target_pairs={{0,8},{8,0},{16,24},{24,16},{1,9},{9,1},{17,25},{25,17},{2,10},{10... | collective-permute-start | bytes 3538952 | tf_op jit(solution)/shard_map/ppermute | solution.py:430
  1.2 10.5 %collective-permute-start.3 = (bf16[768,768]{1,0:T(8,128)(2,1)}, bf16[768,768]{1,0:T(8,128)(2,1)S(1)}, u32[]{:S(2)}, u32[]{:S(2)}) collective-permute-start(bf16[768,768]{1,0:T(8,128)(2,1)} %bitcast.29), channel_id=1, source_target_pairs={{0,8},{8,0},{16,24},{24,16},{1,9},{9,1},{17,25},{25,17},{2,10},{10... | collective-permute-start | bytes 3538952 | tf_op jit(solution)/shard_map/ppermute | solution.py:430
  1.2 10.4 %collective-permute-start = (bf16[192,768]{1,0:T(8,128)(2,1)}, bf16[192,768]{1,0:T(8,128)(2,1)S(1)}, u32[]{:S(2)}, u32[]{:S(2)}) collective-permute-start(bf16[192,768]{1,0:T(8,128)(2,1)} %w_out.1), channel_id=1, source_target_pairs={{0,16},{8,24},{16,0},{24,8},{1,17},{9,25},{17,1},{25,9},{2,18},{10... | collective-permute-start | bytes 884744 | tf_op jit(solution)/shard_map/ppermute | solution.py:430
  4.2 7.5 %collective-permute-start.1 = (bf16[192,768]{1,0:T(8,128)(2,1)}, bf16[192,768]{1,0:T(8,128)(2,1)S(1)}, u32[]{:S(2)}, u32[]{:S(2)}) collective-permute-start(bf16[192,768]{1,0:T(8,128)(2,1)} %w_out.1), channel_id=1, source_target_pairs={{0,8},{8,0},{16,24},{24,16},{1,9},{9,1},{17,25},{25,17},{2,10},{10... | collective-permute-start | bytes 884744 | tf_op jit(solution)/shard_map/ppermute | solution.py:430
  4.9 1.1 copy-start.4
  6.0 0.7 copy-start.6
  6.7 1.2 copy-start.8
  7.8 0.7 copy-start.13
  8.5 5.2 %copy-start.10 = (bf16[394,768]{1,0:T(8,128)(2,1)S(1)}, bf16[394,768]{1,0:T(8,128)(2,1)}, u32[]{:S(2)}) copy-start(bf16[394,768]{1,0:T(8,128)(2,1)} %cot.3) | copy-start | bytes 1815556
  8.5 5.2 %copy-start.12 = (bf16[768,4]{0,1:T(4,128)(2,1)S(1)}, bf16[768,4]{0,1:T(4,128)(2,1)}, u32[]{:S(2)}) copy-start(bf16[768,4]{0,1:T(4,128)(2,1)} %param.22) | copy-start | bytes 18436
  8.5 5.2 %copy-start.14 = (s32[394,2]{0,1:T(2,128)S(1)}, s32[394,2]{0,1:T(2,128)}, u32[]{:S(2)}) copy-start(s32[394,2]{0,1:T(2,128)} %param.14) | copy-start | bytes 9460
  11.6 11.8 %collective-permute-start.4 = (bf16[394,192]{1,0:T(8,128)(2,1)S(1)}, bf16[394,192]{1,0:T(8,128)(2,1)S(1)}, u32[]{:S(2)}, u32[]{:S(2)}) collective-permute-start(bf16[394,192]{1,0:T(8,128)(2,1)S(1)} %get-tuple-element.125.rest_0_.head_out), channel_id=1, source_target_pairs={{0,8},{8,0},{16,24},{24,16},{1,9},{9,1},{17,25},{25,17},{2,10},{10... | collective-permute-start | bytes 453896 | tf_op jit(solution)/shard_map/ppermute | solution.py:430
  11.7 7.5 %collective-permute-start.5 = (bf16[394,192]{1,0:T(8,128)(2,1)S(1)}, bf16[394,192]{1,0:T(8,128)(2,1)S(1)}, u32[]{:S(2)}, u32[]{:S(2)}) collective-permute-start(bf16[394,192]{1,0:T(8,128)(2,1)S(1)} %get-tuple-element.125.rest_0_.head_out), channel_id=1, source_target_pairs={{0,16},{8,24},{16,0},{24,8},{1,17},{9,25},{17,1},{25,9},{2,18},{10... | collective-permute-start | bytes 453896 | tf_op jit(solution)/shard_map/ppermute | solution.py:430
  13.5 9.9 %collective-permute-start.7 = (bf16[192,768]{1,0:T(8,128)(2,1)S(1)}, bf16[192,768]{1,0:T(8,128)(2,1)S(1)}, u32[]{:S(2)}, u32[]{:S(2)}) collective-permute-start(bf16[192,768]{1,0:T(8,128)(2,1)S(1)} %collective-permute-done.rest_6_), channel_id=1, source_target_pairs={{0,8},{8,0},{16,24},{24,16},{1,9},{9,1},{17,25},{25,17},{2,10},{10... | collective-permute-start | bytes 884744 | tf_op jit(solution)/shard_map/ppermute | solution.py:430
  13.7 9.7 %copy-start.5 = (bf16[394,768]{1,0:T(8,128)(2,1)S(1)}, bf16[394,768]{1,0:T(8,128)(2,1)}, u32[]{:S(2)}) copy-start(bf16[394,768]{1,0:T(8,128)(2,1)} %tokens.5) | copy-start | bytes 1815556
  13.7 9.7 %copy-start.11 = (bf16[192,768]{1,0:T(8,128)(2,1)S(1)}, bf16[192,768]{1,0:T(8,128)(2,1)}, u32[]{:S(2)}) copy-start(bf16[192,768]{1,0:T(8,128)(2,1)} %w_out.1) | copy-start | bytes 884740
  13.7 9.7 %copy-start.15 = (f32[768]{0:T(1024)S(1)}, f32[768]{0:T(1024)}, u32[]{:S(2)}) copy-start(f32[768]{0:T(1024)} %bias.3) | copy-start | bytes 9220
  13.7 9.7 %copy-start.16 = (f32[768]{0:T(1024)S(1)}, f32[768]{0:T(1024)}, u32[]{:S(2)}) copy-start(f32[768]{0:T(1024)} %gain.6) | copy-start | bytes 9220
  19.2 4.2 %collective-permute-start.6 = (bf16[394,192]{1,0:T(8,128)(2,1)S(1)}, bf16[394,192]{1,0:T(8,128)(2,1)S(1)}, u32[]{:S(2)}, u32[]{:S(2)}) collective-permute-start(bf16[394,192]{1,0:T(8,128)(2,1)S(1)} %collective-permute-done.5.rest_2_), channel_id=1, source_target_pairs={{0,8},{8,0},{16,24},{24,16},{1,9},{9,1},{17,25},{25,17},{2,10},{10... | collective-permute-start | bytes 453896 | tf_op jit(solution)/shard_map/ppermute | solution.py:430
  19.2 11.6 %collective-permute-start.8 = (bf16[72,768]{1,0:T(8,128)(2,1)S(1)}, bf16[72,768]{1,0:T(8,128)(2,1)S(1)}, u32[]{:S(2)}, u32[]{:S(2)}) collective-permute-start(bf16[72,768]{1,0:T(8,128)(2,1)S(1)} %get-tuple-element.142), channel_id=1, source_target_pairs={{0,4},{2,6},{4,0},{6,2},{1,5},{3,7},{5,1},{7,3},{8,12},{10,14},{12... | collective-permute-start | bytes 331784 | tf_op jit(solution)/shard_map/ppermute | solution.py:433
  22.0 8.7 %collective-permute-start.9 = (bf16[72,768]{1,0:T(8,128)(2,1)S(1)}, bf16[72,768]{1,0:T(8,128)(2,1)S(1)}, u32[]{:S(2)}, u32[]{:S(2)}) collective-permute-start(bf16[72,768]{1,0:T(8,128)(2,1)S(1)} %get-tuple-element.143), channel_id=1, source_target_pairs={{0,6},{2,4},{4,2},{6,0},{1,7},{3,5},{5,3},{7,1},{8,14},{10,12},{12... | collective-permute-start | bytes 331784 | tf_op jit(solution)/shard_map/ppermute | solution.py:433
  23.4 25.3 %copy-start = (bf16[1,768,768]{2,1,0:T(8,128)(2,1)S(1)}, bf16[1,768,768]{2,1,0:T(8,128)(2,1)}, u32[]{:S(2)}) copy-start(bf16[1,768,768]{2,1,0:T(8,128)(2,1)} %param.23) | copy-start | bytes 3538948
  23.5 25.3 %copy-start.1 = (bf16[1,768,768]{2,1,0:T(8,128)(2,1)S(1)}, bf16[1,768,768]{2,1,0:T(8,128)(2,1)}, u32[]{:S(2)}) copy-start(bf16[1,768,768]{2,1,0:T(8,128)(2,1)} %param.24) | copy-start | bytes 3538948
  26.2 80.7 %copy-start.2 = (f32[394,768]{1,0:T(8,128)}, f32[394,768]{1,0:T(8,128)S(1)}, u32[]{:S(2)}) copy-start(f32[394,768]{1,0:T(8,128)S(1)} %get-tuple-element.133.middle) | copy-start | bytes 3631108
  30.8 13.8 %collective-permute-start.10 = (bf16[144,768]{1,0:T(8,128)(2,1)S(1)}, bf16[144,768]{1,0:T(8,128)(2,1)S(1)}, u32[]{:S(2)}, u32[]{:S(2)}) collective-permute-start(bf16[144,768]{1,0:T(8,128)(2,1)S(1)} %get-tuple-element.145), channel_id=1, source_target_pairs={{0,2},{2,0},{4,6},{6,4},{1,3},{3,1},{5,7},{7,5},{8,10},{10,8},{12,... | collective-permute-start | bytes 663560 | tf_op jit(solution)/shard_map/ppermute | solution.py:433
  33.6 15.1 %collective-permute-start.11 = (bf16[144,768]{1,0:T(8,128)(2,1)S(1)}, bf16[144,768]{1,0:T(8,128)(2,1)S(1)}, u32[]{:S(2)}, u32[]{:S(2)}) collective-permute-start(bf16[144,768]{1,0:T(8,128)(2,1)S(1)} %get-tuple-element.147), channel_id=1, source_target_pairs={{0,2},{2,0},{4,6},{6,4},{1,3},{3,1},{5,7},{7,5},{8,10},{10,8},{12,... | collective-permute-start | bytes 663560 | tf_op jit(solution)/shard_map/ppermute | solution.py:433
  33.7 22.1 %collective-permute-start.12 = (bf16[144,768]{1,0:T(8,128)(2,1)S(1)}, bf16[144,768]{1,0:T(8,128)(2,1)S(1)}, u32[]{:S(2)}, u32[]{:S(2)}) collective-permute-start(bf16[144,768]{1,0:T(8,128)(2,1)S(1)} %get-tuple-element.150), channel_id=1, source_target_pairs={{0,4},{2,6},{4,0},{6,2},{1,5},{3,7},{5,1},{7,3},{8,12},{10,14},{12... | collective-permute-start | bytes 663560 | tf_op jit(solution)/shard_map/ppermute | solution.py:433
  37.6 19.1 %collective-permute-start.13 = (bf16[144,768]{1,0:T(8,128)(2,1)S(1)}, bf16[144,768]{1,0:T(8,128)(2,1)S(1)}, u32[]{:S(2)}, u32[]{:S(2)}) collective-permute-start(bf16[144,768]{1,0:T(8,128)(2,1)S(1)} %get-tuple-element.151), channel_id=1, source_target_pairs={{0,6},{2,4},{4,2},{6,0},{1,7},{3,5},{5,3},{7,1},{8,14},{10,12},{12... | collective-permute-start | bytes 663560 | tf_op jit(solution)/shard_map/ppermute | solution.py:433
  38.0 18.7 %collective-permute-start.14 = (bf16[2,72,768]{2,1,0:T(8,128)(2,1)S(1)}, bf16[2,72,768]{2,1,0:T(8,128)(2,1)S(1)}, u32[]{:S(2)}, u32[]{:S(2)}) collective-permute-start(bf16[2,72,768]{2,1,0:T(8,128)(2,1)S(1)} %pad_maximum_fusion.2), channel_id=1, source_target_pairs={{0,16},{8,24},{16,0},{24,8},{1,17},{9,25},{17,1},{25,9},{2,18},{10... | collective-permute-start | bytes 663560 | tf_op jit(solution)/shard_map/ppermute | solution.py:430
  64.2 11.5 %collective-permute-start.19 = (bf16[1536,768]{1,0:T(8,128)(2,1)S(1)}, bf16[1536,768]{1,0:T(8,128)(2,1)S(1)}, u32[]{:S(2)}, u32[]{:S(2)}) collective-permute-start(bf16[1536,768]{1,0:T(8,128)(2,1)S(1)} %get-tuple-element.174), channel_id=1, source_target_pairs={{0,8},{8,0},{16,24},{24,16},{1,9},{9,1},{17,25},{25,17},{2,10},{10... | collective-permute-start | bytes 7077896 | tf_op jit(solution)/shard_map/ppermute | solution.py:430
  64.3 13.1 %collective-permute-start.15 = (bf16[144,768]{1,0:T(8,128)(2,1)S(1)}, bf16[144,768]{1,0:T(8,128)(2,1)S(1)}, u32[]{:S(2)}, u32[]{:S(2)}) collective-permute-start(bf16[144,768]{1,0:T(8,128)(2,1)S(1)} %get-tuple-element.154), channel_id=1, source_target_pairs={{0,6},{2,4},{4,2},{6,0},{1,7},{3,5},{5,3},{7,1},{8,14},{10,12},{12... | collective-permute-start | bytes 663560 | tf_op jit(solution)/shard_map/ppermute | solution.py:433
  67.5 19.1 %collective-permute-start.16 = (bf16[144,768]{1,0:T(8,128)(2,1)S(1)}, bf16[144,768]{1,0:T(8,128)(2,1)S(1)}, u32[]{:S(2)}, u32[]{:S(2)}) collective-permute-start(bf16[144,768]{1,0:T(8,128)(2,1)S(1)} %get-tuple-element.157), channel_id=1, source_target_pairs={{0,4},{2,6},{4,0},{6,2},{1,5},{3,7},{5,1},{7,3},{8,12},{10,14},{12... | collective-permute-start | bytes 663560 | tf_op jit(solution)/shard_map/ppermute | solution.py:433
  67.5 19.1 %collective-permute-start.17 = (bf16[144,768]{1,0:T(8,128)(2,1)S(1)}, bf16[144,768]{1,0:T(8,128)(2,1)S(1)}, u32[]{:S(2)}, u32[]{:S(2)}) collective-permute-start(bf16[144,768]{1,0:T(8,128)(2,1)S(1)} %get-tuple-element.158), channel_id=1, source_target_pairs={{0,2},{2,0},{4,6},{6,4},{1,3},{3,1},{5,7},{7,5},{8,10},{10,8},{12,... | collective-permute-start | bytes 663560 | tf_op jit(solution)/shard_map/ppermute | solution.py:433
  68.7 6.9 %collective-permute-start.18 = (bf16[2,72,768]{2,1,0:T(8,128)(2,1)S(1)}, bf16[2,72,768]{2,1,0:T(8,128)(2,1)S(1)}, u32[]{:S(2)}, u32[]{:S(2)}) collective-permute-start(bf16[2,72,768]{2,1,0:T(8,128)(2,1)S(1)} %get-tuple-element.162), channel_id=1, source_target_pairs={{0,16},{8,24},{16,0},{24,8},{1,17},{9,25},{17,1},{25,9},{2,18},{10... | collective-permute-start | bytes 663560 | tf_op jit(solution)/shard_map/ppermute | solution.py:430
  77.4 10.7 %copy-start.17 = (f32[768,768]{1,0:T(8,128)}, f32[768,768]{1,0:T(8,128)S(1)}, u32[]{:S(2)}) copy-start(f32[768,768]{1,0:T(8,128)S(1)} %get-tuple-element.222.kept) | copy-start | bytes 7077892
  88.1 18.9 %copy-start.9 = (bf16[768,3,192]{0,2,1:T(8,128)(2,1)S(1)}, bf16[768,3,192]{0,2,1:T(8,128)(2,1)}, u32[]{:S(2)}) copy-start(bf16[768,3,192]{0,2,1:T(8,128)(2,1)} %param.18) | copy-start | bytes 2654212
  88.1 1.7 %collective-permute-start.20 = (bf16[416,384]{1,0:T(8,128)(2,1)S(1)}, bf16[416,384]{1,0:T(8,128)(2,1)S(1)}, u32[]{:S(2)}, u32[]{:S(2)}) collective-permute-start(bf16[416,384]{1,0:T(8,128)(2,1)S(1)} %get-tuple-element.183), channel_id=1, source_target_pairs={{0,8},{8,0},{16,24},{24,16},{1,9},{9,1},{17,25},{25,17},{2,10},{10... | collective-permute-start | bytes 958472 | tf_op jit(solution)/shard_map/ppermute | solution.py:430
  89.8 9.6 %collective-permute-start.21 = (bf16[416,384]{1,0:T(8,128)(2,1)S(1)}, bf16[416,384]{1,0:T(8,128)(2,1)S(1)}, u32[]{:S(2)}, u32[]{:S(2)}) collective-permute-start(bf16[416,384]{1,0:T(8,128)(2,1)S(1)} %add_convert_fusion.1), channel_id=1, source_target_pairs={{0,16},{8,24},{16,0},{24,8},{1,17},{9,25},{17,1},{25,9},{2,18},{10... | collective-permute-start | bytes 958472 | tf_op jit(solution)/shard_map/ppermute | solution.py:430
  91.4 13.9 %collective-permute-start.22 = (bf16[256,768]{1,0:T(8,128)(2,1)S(1)}, bf16[256,768]{1,0:T(8,128)(2,1)S(1)}, u32[]{:S(2)}, u32[]{:S(2)}) collective-permute-start(bf16[256,768]{1,0:T(8,128)(2,1)S(1)} %get-tuple-element.184), channel_id=1, source_target_pairs={{0,1},{1,0},{2,3},{3,2},{4,5},{5,4},{6,7},{7,6},{8,9},{9,8},{10,11... | collective-permute-start | bytes 1179656 | tf_op jit(solution)/shard_map/ppermute | solution.py:436
  92.9 12.4 %collective-permute-start.23 = (bf16[144,768]{1,0:T(8,128)(2,1)S(1)}, bf16[144,768]{1,0:T(8,128)(2,1)S(1)}, u32[]{:S(2)}, u32[]{:S(2)}) collective-permute-start(bf16[144,768]{1,0:T(8,128)(2,1)S(1)} %get-tuple-element.186), channel_id=1, source_target_pairs={{0,2},{2,0},{4,6},{6,4},{1,3},{3,1},{5,7},{7,5},{8,10},{10,8},{12,... | collective-permute-start | bytes 663560 | tf_op jit(solution)/shard_map/ppermute | solution.py:433
  92.9 8.2 %collective-permute-start.24 = (bf16[72,768]{1,0:T(8,128)(2,1)S(1)}, bf16[72,768]{1,0:T(8,128)(2,1)S(1)}, u32[]{:S(2)}, u32[]{:S(2)}) collective-permute-start(bf16[72,768]{1,0:T(8,128)(2,1)S(1)} %get-tuple-element.187), channel_id=1, source_target_pairs={{0,4},{2,6},{4,0},{6,2},{1,5},{3,7},{5,1},{7,3},{8,12},{10,14},{12... | collective-permute-start | bytes 331784 | tf_op jit(solution)/shard_map/ppermute | solution.py:433
  95.9 9.4 %collective-permute-start.25 = (bf16[72,768]{1,0:T(8,128)(2,1)S(1)}, bf16[72,768]{1,0:T(8,128)(2,1)S(1)}, u32[]{:S(2)}, u32[]{:S(2)}) collective-permute-start(bf16[72,768]{1,0:T(8,128)(2,1)S(1)} %get-tuple-element.188), channel_id=1, source_target_pairs={{0,6},{2,4},{4,2},{6,0},{1,7},{3,5},{5,3},{7,1},{8,14},{10,12},{12... | collective-permute-start | bytes 331784 | tf_op jit(solution)/shard_map/ppermute | solution.py:433
  105.3 1.6 collective-permute-start.26
  111.9 5.2 %collective-permute-start.33 = (bf16[394,384]{1,0:T(8,128)(2,1)S(1)}, bf16[394,384]{1,0:T(8,128)(2,1)S(1)}, u32[]{:S(2)}, u32[]{:S(2)}) collective-permute-start(bf16[394,384]{1,0:T(8,128)(2,1)S(1)} %get-tuple-element.215), channel_id=1, source_target_pairs={{0,8},{8,0},{16,24},{24,16},{1,9},{9,1},{17,25},{25,17},{2,10},{10... | collective-permute-start | bytes 907784 | tf_op jit(solution)/shard_map/ppermute | solution.py:430
  112.1 10.8 %collective-permute-start.29 = (bf16[192,768]{1,0:T(8,128)(2,1)S(1)}, bf16[192,768]{1,0:T(8,128)(2,1)S(1)}, u32[]{:S(2)}, u32[]{:S(2)}) collective-permute-start(bf16[192,768]{1,0:T(8,128)(2,1)S(1)} %get-tuple-element.210), channel_id=1, source_target_pairs={{0,3},{1,2},{2,1},{3,0},{4,7},{5,6},{6,5},{7,4},{8,11},{9,10},{10,... | collective-permute-start | bytes 884744 | tf_op jit(solution)/shard_map/ppermute | solution.py:440
  112.9 15.3 %collective-permute-start.30 = (bf16[192,768]{1,0:T(8,128)(2,1)S(1)}, bf16[192,768]{1,0:T(8,128)(2,1)S(1)}, u32[]{:S(2)}, u32[]{:S(2)}) collective-permute-start(bf16[192,768]{1,0:T(8,128)(2,1)S(1)} %get-tuple-element.211), channel_id=1, source_target_pairs={{0,1},{1,0},{2,3},{3,2},{4,5},{5,4},{6,7},{7,6},{8,9},{9,8},{10,11... | collective-permute-start | bytes 884744 | tf_op jit(solution)/shard_map/ppermute | solution.py:440
  114.4 13.8 %collective-permute-start.31 = (bf16[192,768]{1,0:T(8,128)(2,1)S(1)}, bf16[192,768]{1,0:T(8,128)(2,1)S(1)}, u32[]{:S(2)}, u32[]{:S(2)}) collective-permute-start(bf16[192,768]{1,0:T(8,128)(2,1)S(1)} %get-tuple-element.212), channel_id=1, source_target_pairs={{0,2},{1,3},{2,0},{3,1},{4,6},{5,7},{6,4},{7,5},{8,10},{9,11},{10,... | collective-permute-start | bytes 884744 | tf_op jit(solution)/shard_map/ppermute | solution.py:440
  117.1 11.3 %collective-permute-start.27 = (bf16[400,384]{1,0:T(8,128)(2,1)S(1)}, bf16[400,384]{1,0:T(8,128)(2,1)S(1)}, u32[]{:S(2)}, u32[]{:S(2)}) collective-permute-start(bf16[400,384]{1,0:T(8,128)(2,1)S(1)} %get-tuple-element.208), channel_id=1, source_target_pairs={{0,8},{8,0},{16,24},{24,16},{1,9},{9,1},{17,25},{25,17},{2,10},{10... | collective-permute-start | bytes 921608 | tf_op jit(solution)/shard_map/ppermute | solution.py:430
  117.3 11.8 %collective-permute-start.34 = (bf16[394,384]{1,0:T(8,128)(2,1)S(1)}, bf16[394,384]{1,0:T(8,128)(2,1)S(1)}, u32[]{:S(2)}, u32[]{:S(2)}) collective-permute-start(bf16[394,384]{1,0:T(8,128)(2,1)S(1)} %add_convert_fusion.3), channel_id=1, source_target_pairs={{0,16},{8,24},{16,0},{24,8},{1,17},{9,25},{17,1},{25,9},{2,18},{10... | collective-permute-start | bytes 907784 | tf_op jit(solution)/shard_map/ppermute | solution.py:430
  128.3 3.7 %copy-start.7 = (f32[768]{0:T(1024)S(1)}, f32[768]{0:T(1024)}, u32[]{:S(2)}) copy-start(f32[768]{0:T(1024)} %gain.7) | copy-start | bytes 9220
  128.4 8.8 %collective-permute-start.28 = (bf16[400,384]{1,0:T(8,128)(2,1)S(1)}, bf16[400,384]{1,0:T(8,128)(2,1)S(1)}, u32[]{:S(2)}, u32[]{:S(2)}) collective-permute-start(bf16[400,384]{1,0:T(8,128)(2,1)S(1)} %add_convert_fusion.5), channel_id=1, source_target_pairs={{0,16},{8,24},{16,0},{24,8},{1,17},{9,25},{17,1},{25,9},{2,18},{10... | collective-permute-start | bytes 921608 | tf_op jit(solution)/shard_map/ppermute | solution.py:430
  129.1 2.9 %collective-permute-start.35 = (bf16[394,384]{1,0:T(8,128)(2,1)S(1)}, bf16[394,384]{1,0:T(8,128)(2,1)S(1)}, u32[]{:S(2)}, u32[]{:S(2)}) collective-permute-start(bf16[394,384]{1,0:T(8,128)(2,1)S(1)} %add_convert_fusion.2.own), channel_id=1, source_target_pairs={{0,8},{8,0},{16,24},{24,16},{1,9},{9,1},{17,25},{25,17},{2,10},{10... | collective-permute-start | bytes 907784 | tf_op jit(solution)/shard_map/ppermute | solution.py:430
  129.2 18.1 %collective-permute-start.32 = (bf16[192,768]{1,0:T(8,128)(2,1)S(1)}, bf16[192,768]{1,0:T(8,128)(2,1)S(1)}, u32[]{:S(2)}, u32[]{:S(2)}) collective-permute-start(bf16[192,768]{1,0:T(8,128)(2,1)S(1)} %shard_map.223.own), channel_id=1, source_target_pairs={{0,4},{2,6},{4,0},{6,2},{1,5},{3,7},{5,1},{7,3},{8,12},{10,14},{12... | collective-permute-start | bytes 884744 | tf_op jit(solution)/shard_map/ppermute | solution.py:433
  130.7 23.4 %collective-permute-start.38 = (bf16[512,768]{1,0:T(8,128)(2,1)S(1)}, bf16[512,768]{1,0:T(8,128)(2,1)S(1)}, u32[]{:S(2)}, u32[]{:S(2)}) collective-permute-start(bf16[512,768]{1,0:T(8,128)(2,1)S(1)} %get-tuple-element.224), channel_id=1, source_target_pairs={{0,1},{1,0},{2,3},{3,2},{4,5},{5,4},{6,7},{7,6},{8,9},{9,8},{10,11... | collective-permute-start | bytes 2359304 | tf_op jit(solution)/shard_map/ppermute | solution.py:436
  134.4 13.5 %collective-permute-start.36 = (f32[16,768]{1,0:T(8,128)S(1)}, f32[16,768]{1,0:T(8,128)S(1)}, u32[]{:S(2)}, u32[]{:S(2)}) collective-permute-start(f32[16,768]{1,0:T(8,128)S(1)} %get-tuple-element.218.small), channel_id=1, source_target_pairs={{0,4},{2,6},{4,0},{6,2},{1,5},{3,7},{5,1},{7,3},{8,12},{10,14},{12... | collective-permute-start | bytes 147464 | tf_op jit(solution)/shard_map/ppermute | solution.py:433
  138.0 13.7 %copy-start.3 = (f32[394,768]{1,0:T(8,128)S(1)}, f32[394,768]{1,0:T(8,128)}, u32[]{:S(2)}) copy-start(f32[394,768]{1,0:T(8,128)} %copy-done.2) | copy-start | bytes 3631108
  148.0 3.7 %collective-permute-start.37 = (bf16[400,384]{1,0:T(8,128)(2,1)}, bf16[400,384]{1,0:T(8,128)(2,1)}, u32[]{:S(2)}, u32[]{:S(2)}) collective-permute-start(bf16[400,384]{1,0:T(8,128)(2,1)} %add_convert_fusion.4), channel_id=1, source_target_pairs={{0,8},{8,0},{16,24},{24,16},{1,9},{9,1},{17,25},{25,17},{2,10},{10... | collective-permute-start | bytes 921608 | tf_op jit(solution)/shard_map/ppermute | solution.py:430
  148.1 5.9 %copy-start.18 = (f32[768,768]{1,0:T(8,128)S(1)}, f32[768,768]{1,0:T(8,128)}, u32[]{:S(2)}) copy-start(f32[768,768]{1,0:T(8,128)} %copy-done.17) | copy-start | bytes 7077892
  148.1 11.4 %collective-permute-start.39 = (bf16[208,768]{1,0:T(8,128)(2,1)S(1)}, bf16[208,768]{1,0:T(8,128)(2,1)S(1)}, u32[]{:S(2)}, u32[]{:S(2)}) collective-permute-start(bf16[208,768]{1,0:T(8,128)(2,1)S(1)} %shard_map.225.refs_0_), channel_id=1, source_target_pairs={{0,3},{1,2},{2,1},{3,0},{4,7},{5,6},{6,5},{7,4},{8,11},{9,10},{10,... | collective-permute-start | bytes 958472 | tf_op jit(solution)/shard_map/ppermute | solution.py:440
  148.2 16.8 %collective-permute-start.40 = (bf16[208,768]{1,0:T(8,128)(2,1)S(1)}, bf16[208,768]{1,0:T(8,128)(2,1)S(1)}, u32[]{:S(2)}, u32[]{:S(2)}) collective-permute-start(bf16[208,768]{1,0:T(8,128)(2,1)S(1)} %shard_map.225.refs_0_), channel_id=1, source_target_pairs={{0,1},{1,0},{2,3},{3,2},{4,5},{5,4},{6,7},{7,6},{8,9},{9,8},{10,11... | collective-permute-start | bytes 958472 | tf_op jit(solution)/shard_map/ppermute | solution.py:440
  149.3 16.1 %collective-permute-start.41 = (bf16[208,768]{1,0:T(8,128)(2,1)S(1)}, bf16[208,768]{1,0:T(8,128)(2,1)S(1)}, u32[]{:S(2)}, u32[]{:S(2)}) collective-permute-start(bf16[208,768]{1,0:T(8,128)(2,1)S(1)} %shard_map.225.refs_0_), channel_id=1, source_target_pairs={{0,2},{1,3},{2,0},{3,1},{4,6},{5,7},{6,4},{7,5},{8,10},{9,11},{10,... | collective-permute-start | bytes 958472 | tf_op jit(solution)/shard_map/ppermute | solution.py:440

commit v10 on v9

--- a/solution.py
+++ b/solution.py
@@ -600,7 +600,7 @@
             micros=4,
             limit=24,
         )
-        third = width // 48 * 16
+        third = width // 96 * 16
         grad_kept, sent_first, sent_rest = run(
             split_grad_kernel,
             [((width, width), F32), ((third, width), BF16), ((width - third, width), BF16)],
@@ -620,8 +620,9 @@
         else:
             gated_blocks = [gated[0][0][k] for k in range(experts)]
 
-        *gated_blocks, sent_first = lax.optimization_barrier(
-            (*d_home[::-1], *gated_blocks, sent_first)
+        came_first = dp_swap(sent_first)
+        *gated_blocks, came_first = lax.optimization_barrier(
+            (*d_home[::-1], *gated_blocks, came_first)
         )
         d_home, gated_blocks = gated_blocks[:experts][::-1], gated_blocks[experts:]
         kept, sent = combine(list(d_home), [one[6] for one in worked])
@@ -632,8 +633,7 @@
             gated_home = [gated_blocks[0], home[1], home[2], home[3]]
         else:
             gated_home = exchange(list(gated_blocks))
-        came_first = dp_swap(sent_first)
-        own, came_first, *gated_home = lax.optimization_barrier((own, came_first, *gated_home))
+        own, *gated_home = lax.optimization_barrier((own, *gated_home))
         other = tensor_swap(own, 1)
 
         parts = 4 if small_slice else 1

time: 168 us -> 169 us (level)
    ppermute x2, waiting for transfers between devices: 0.01 us -> 4.98 us  [dp_swap(): return lax.ppermute(value, 'dp', [(i, i ^ 1) for i in range(n_dp)])]
    ppermute x6, waiting for transfers between devices: 20.1 us -> 16 us  [quarter_swap(): return lax.ppermute(value, ('expert', 'dp'), pairs)]
    unnamed x38 -> x42, local copies, waits for them, and re-layouts: 3.69 us -> 4.41 us
  transfers between devices with their start and end apart: 42 -> 42, of which waited for: 21 -> 20; matrix products, arithmetic and copies ran while one was open for 2% -> 2% of each run, Pallas kernels for 13% -> 13%
where the time goes in v10:
time: 169 us
  waiting for transfers between devices  76.9 us (46%)
  starting transfers between devices  44.7 us (26%)
  Pallas kernels  37.2 us (22%)
  local copies, waits for them, and re-layouts  4.53 us (3%)
  other arithmetic  3.54 us (2%)
    ppermute x14, waiting for transfers between devices, expert_swap(): lax.ppermute(value, 'expert', [(i, i ^ mask) for i in range(n_expert)])  40.2 us
    pallas_call x16, Pallas kernels, run(): pl.pallas_call(kernel, out_shape=[jax.ShapeDtypeStruct(shape, kind) for s...  37.2 us
    ppermute x14, starting transfers between devices, expert_swap(): lax.ppermute(value, 'expert', [(i, i ^ mask) for i in range(n_expert)])  23.2 us
    ppermute x6, waiting for transfers between devices, quarter_swap(): return lax.ppermute(value, ('expert', 'dp'), pairs)  16 us
    ppermute x20, waiting for transfers between devices, tensor_swap(): lax.ppermute(value, 'tensor', [(i, i ^ mask) for i in range(n_tensor)])  15.8 us
    ppermute x20, starting transfers between devices, tensor_swap(): lax.ppermute(value, 'tensor', [(i, i ^ mask) for i in range(n_tensor)])  11.9 us
    ppermute x6, starting transfers between devices, quarter_swap(): return lax.ppermute(value, ('expert', 'dp'), pairs)  7.05 us
    ppermute x2, waiting for transfers between devices, dp_swap(): return lax.ppermute(value, 'dp', [(i, i ^ 1) for i in range(n_dp)])  4.98 us
  transfers between devices with their start and end apart: 42, of which 20 were waited for; matrix products, arithmetic and copies ran while one was open for 2% of the time, Pallas kernels for 13%

profile of v10, /device:TPU:0, one launch (start us, length us, event | category | flops | bytes accessed | tf_op | source)
XLA Modules:
  0.0 168.6 jit_solution(16937162426322415527)
XLA Ops:
  0.6 0.5 collective-permute-start.2
  1.2 2.9 %collective-permute-start = (bf16[192,768]{1,0:T(8,128)(2,1)}, bf16[192,768]{1,0:T(8,128)(2,1)S(1)}, u32[]{:S(2)}, u32[]{:S(2)}) collective-permute-start(bf16[192,768]{1,0:T(8,128)(2,1)} %w_out.1), channel_id=1, source_target_pairs={{0,16},{8,24},{16,0},{24,8},{1,17},{9,25},{17,1},{25,9},{2,18},{10... | collective-permute-start | bytes 884744 | tf_op jit(solution)/shard_map/ppermute | solution.py:430
  4.9 1.1 copy-done.4
  6.0 0.7 copy-done.6
  6.7 1.2 copy-done.8
  7.8 0.7 copy-done.15
  8.5 2.5 %shard_map.212 = (bf16[394,768]{1,0:T(8,128)(2,1)S(1)}, bf16[394,192]{1,0:T(8,128)(2,1)S(1)}, bf16[394,192]{1,0:T(8,128)(2,1)S(1)}, bf16[394,192]{1,0:T(8,128)(2...) custom-call(bf16[394,768]{1,0:T(8,128)(2,1)S(1)} %copy-done.4, f32[768]{0:T(1024)S(1)} %copy-done.6, ...), custom_call_target="tpu_custom_call" | custom-call | flops 4600000000 | bytes 1024 | tf_op jit(solution)/shard_map/pallas_call | solution.py:413
  11.1 0.6 collective-permute-done.rest_6_
  11.7 1.8 %collective-permute-start.5 = (bf16[394,192]{1,0:T(8,128)(2,1)S(1)}, bf16[394,192]{1,0:T(8,128)(2,1)S(1)}, u32[]{:S(2)}, u32[]{:S(2)}) collective-permute-start(bf16[394,192]{1,0:T(8,128)(2,1)S(1)} %get-tuple-element.124.rest_0_.head_out), channel_id=1, source_target_pairs={{0,16},{8,24},{16,0},{24,8},{1,17},{9,25},{17,1},{25,9},{2,18},{10... | collective-permute-start | bytes 453896 | tf_op jit(solution)/shard_map/ppermute | solution.py:430
  13.7 1.4 shard_map.213
  15.1 4.1 %collective-permute-done.5.rest_2_ = bf16[394,192]{1,0:T(8,128)(2,1)S(1)} collective-permute-done((bf16[394,192]{1,0:T(8,128)(2,1)S(1)}, bf16[394,192]{1,0:T(8,128)(2,1)S(1)}, u32[]{:S(2)}, u32[]{:S(2)}) %collective-permute-start.5) | collective-permute-done | bytes 151328 | tf_op jit(solution)/shard_map/ppermute | solution.py:430
  19.2 2.8 %collective-permute-start.8 = (bf16[72,768]{1,0:T(8,128)(2,1)S(1)}, bf16[72,768]{1,0:T(8,128)(2,1)S(1)}, u32[]{:S(2)}, u32[]{:S(2)}) collective-permute-start(bf16[72,768]{1,0:T(8,128)(2,1)S(1)} %get-tuple-element.141), channel_id=1, source_target_pairs={{0,4},{2,6},{4,0},{6,2},{1,5},{3,7},{5,1},{7,3},{8,12},{10,14},{12... | collective-permute-start | bytes 331784 | tf_op jit(solution)/shard_map/ppermute | solution.py:433
  22.0 1.3 collective-permute-start.9
  23.5 2.7 %shard_map.214 = (f32[394,768]{1,0:T(8,128)S(1)}, bf16[144,768]{1,0:T(8,128)(2,1)S(1)}, bf16[144,768]{1,0:T(8,128)(2,1)S(1)}, bf16[144,768]{1,0:T(8,128)(2,1)S(1)}, bf16[144,768]{1,0:T(8,128)(2,1)S(1)}) custom-call(s32[8]{0:T(128)S(1)} %stack.38.ids, bf16[394,768]{1,0:T(8,128)(2,1)S(1)} %copy-done.5, f32[768]{0:T(1024)S(1)} %copy-done.18, ...), custom_call_target="tpu_custom_call" | custom-call | flops 3449999872 | bytes 1024 | tf_op jit(solution)/shard_map/pallas_call | solution.py:413
  26.2 4.5 %collective-permute-done.8.refs_2_ = bf16[72,768]{1,0:T(8,128)(2,1)S(1)} collective-permute-done((bf16[72,768]{1,0:T(8,128)(2,1)S(1)}, bf16[72,768]{1,0:T(8,128)(2,1)S(1)}, u32[]{:S(2)}, u32[]{:S(2)}) %collective-permute-start.8) | collective-permute-done | bytes 110624 | tf_op jit(solution)/shard_map/ppermute | solution.py:433
  30.8 2.9 %collective-permute-start.10 = (bf16[144,768]{1,0:T(8,128)(2,1)S(1)}, bf16[144,768]{1,0:T(8,128)(2,1)S(1)}, u32[]{:S(2)}, u32[]{:S(2)}) collective-permute-start(bf16[144,768]{1,0:T(8,128)(2,1)S(1)} %get-tuple-element.144), channel_id=1, source_target_pairs={{0,2},{2,0},{4,6},{6,4},{1,3},{3,1},{5,7},{7,5},{8,10},{10,8},{12,... | collective-permute-start | bytes 663560 | tf_op jit(solution)/shard_map/ppermute | solution.py:433
  33.7 3.9 %collective-permute-start.12 = (bf16[144,768]{1,0:T(8,128)(2,1)S(1)}, bf16[144,768]{1,0:T(8,128)(2,1)S(1)}, u32[]{:S(2)}, u32[]{:S(2)}) collective-permute-start(bf16[144,768]{1,0:T(8,128)(2,1)S(1)} %get-tuple-element.149), channel_id=1, source_target_pairs={{0,4},{2,6},{4,0},{6,2},{1,5},{3,7},{5,1},{7,3},{8,12},{10,14},{12... | collective-permute-start | bytes 663560 | tf_op jit(solution)/shard_map/ppermute | solution.py:433
  38.0 1.6 collective-permute-start.14
  39.6 5.0 %collective-permute-done.10.refs_1_ = bf16[144,768]{1,0:T(8,128)(2,1)S(1)} collective-permute-done((bf16[144,768]{1,0:T(8,128)(2,1)S(1)}, bf16[144,768]{1,0:T(8,128)(2,1)S(1)}, u32[]{:S(2)}, u32[]{:S(2)}) %collective-permute-start.10) | collective-permute-done | bytes 221216 | tf_op jit(solution)/shard_map/ppermute | solution.py:433
  44.6 4.2 %collective-permute-done.11.refs_3_ = bf16[144,768]{1,0:T(8,128)(2,1)S(1)} collective-permute-done((bf16[144,768]{1,0:T(8,128)(2,1)S(1)}, bf16[144,768]{1,0:T(8,128)(2,1)S(1)}, u32[]{:S(2)}, u32[]{:S(2)}) %collective-permute-start.11) | collective-permute-done | bytes 221216 | tf_op jit(solution)/shard_map/ppermute | solution.py:433
  48.8 7.0 %shard_map.215 = (bf16[144,768]{1,0:T(8,128)(2,1)S(1)}, bf16[144,768]{1,0:T(8,128)(2,1)S(1)}, bf16[2,144,768]{2,1,0:T(8,128)(2,1)S(1)}, bf16[2,144,768]{2,1,0:T(...) custom-call(s32[8]{0:T(128)S(1)} %stack.38.ids, ...), custom_call_target="tpu_custom_call" | custom-call | flops 57500000 | bytes 1024 | tf_op jit(solution)/shard_map/pallas_call | solution.py:413
  55.8 0.9 collective-permute-done.13.refs_1_
  56.7 4.8 %shard_map.216 = (bf16[144,768]{1,0:T(8,128)(2,1)S(1)}, bf16[144,768]{1,0:T(8,128)(2,1)S(1)}, bf16[2,72,768]{2,1,0:T(8,128)(2,1)S(1)}, bf16[2,72,768]{2,1,0:T(8,...) custom-call(s32[8]{0:T(128)S(1)} %stack.38.ids, ...), custom_call_target="tpu_custom_call" | custom-call | flops 57500000 | bytes 1024 | tf_op jit(solution)/shard_map/pallas_call | solution.py:413
  61.5 2.7 %shard_map.218 = (bf16[1536,768]{1,0:T(8,128)(2,1)S(1)}, bf16[1536,768]{1,0:T(8,128)(2,1)S(1)}) custom-call(bf16[288,768]{1,0:T(8,128)(2,1)S(1)} %get-tuple-element.164.refs_0_, bf16[288,768]{1,0:T(8,128)(2,1)S(1)} %get-tuple-element.165.refs_1_, bf16[288,768]{1,0:T(8,128)(2,1)S(1)} %get-tuple-element.166.refs_2_, ...), custom_call_target="tpu_custom_call" | custom-call | flops 4600000000 | bytes 1024 | tf_op jit(solution)/shard_map/pallas_call | solution.py:413
  64.3 3.2 %collective-permute-start.15 = (bf16[144,768]{1,0:T(8,128)(2,1)S(1)}, bf16[144,768]{1,0:T(8,128)(2,1)S(1)}, u32[]{:S(2)}, u32[]{:S(2)}) collective-permute-start(bf16[144,768]{1,0:T(8,128)(2,1)S(1)} %get-tuple-element.153), channel_id=1, source_target_pairs={{0,6},{2,4},{4,2},{6,0},{1,7},{3,5},{5,3},{7,1},{8,14},{10,12},{12... | collective-permute-start | bytes 663560 | tf_op jit(solution)/shard_map/ppermute | solution.py:433
  67.5 1.2 collective-permute-start.17
  68.7 1.5 collective-permute-start.18
  70.2 1.6 shard_map.219
  71.9 1.6 collective-permute-start.20
  73.5 2.2 %collective-permute-done.18.came = bf16[2,72,768]{2,1,0:T(8,128)(2,1)S(1)} collective-permute-done((bf16[2,72,768]{2,1,0:T(8,128)(2,1)S(1)}, bf16[2,72,768]{2,1,0:T(8,128)(2,1)S(1)}, u32[]{:S(2)}, u32[]{:S(2)}) %collective-permute-start.18) | collective-permute-done | bytes 221216 | tf_op jit(solution)/shard_map/ppermute | solution.py:430
  75.7 10.8 %collective-permute-done.16.refs_2_ = bf16[144,768]{1,0:T(8,128)(2,1)S(1)} collective-permute-done((bf16[144,768]{1,0:T(8,128)(2,1)S(1)}, bf16[144,768]{1,0:T(8,128)(2,1)S(1)}, u32[]{:S(2)}, u32[]{:S(2)}) %collective-permute-start.16) | collective-permute-done | bytes 221216 | tf_op jit(solution)/shard_map/ppermute | solution.py:433
  86.6 1.5 shard_map.220
  88.2 1.6 collective-permute-done.21
  89.8 1.6 collective-permute-start.22
  91.4 2.9 %collective-permute-start.24 = (bf16[72,768]{1,0:T(8,128)(2,1)S(1)}, bf16[72,768]{1,0:T(8,128)(2,1)S(1)}, u32[]{:S(2)}, u32[]{:S(2)}) collective-permute-start(bf16[72,768]{1,0:T(8,128)(2,1)S(1)} %get-tuple-element.185), channel_id=1, source_target_pairs={{0,4},{2,6},{4,0},{6,2},{1,5},{3,7},{5,1},{7,3},{8,12},{10,14},{12... | collective-permute-start | bytes 331784 | tf_op jit(solution)/shard_map/ppermute | solution.py:433
  94.4 1.4 collective-permute-start.25
  95.8 3.7 %collective-permute-done.22 = bf16[416,384]{1,0:T(8,128)(2,1)S(1)} collective-permute-done((bf16[416,384]{1,0:T(8,128)(2,1)S(1)}, bf16[416,384]{1,0:T(8,128)(2,1)S(1)}, u32[]{:S(2)}, u32[]{:S(2)}) %collective-permute-start.22) | collective-permute-done | bytes 319520 | tf_op jit(solution)/shard_map/ppermute | solution.py:430
  99.6 4.5 %collective-permute-done.25.refs_1_ = bf16[72,768]{1,0:T(8,128)(2,1)S(1)} collective-permute-done((bf16[72,768]{1,0:T(8,128)(2,1)S(1)}, bf16[72,768]{1,0:T(8,128)(2,1)S(1)}, u32[]{:S(2)}, u32[]{:S(2)}) %collective-permute-start.25) | collective-permute-done | bytes 110624 | tf_op jit(solution)/shard_map/ppermute | solution.py:433
  104.1 1.6 collective-permute-done.26.other
  105.7 5.0 %shard_map.221 = (f32[394,768]{1,0:T(8,128)S(1)}, bf16[394,384]{1,0:T(8,128)(2,1)S(1)}, bf16[394,384]{1,0:T(8,128)(2,1)S(1)}, f32[16,768]{1,0:T(8,128)S(1)}, bf1...) custom-call(s32[8]{0:T(128)S(1)} %stack.38.ids, ...), custom_call_target="tpu_custom_call" | custom-call | flops 6899999744 | bytes 1024 | tf_op jit(solution)/shard_map/pallas_call | solution.py:413
  110.9 1.8 %collective-permute-start.29 = (bf16[192,768]{1,0:T(8,128)(2,1)S(1)}, bf16[192,768]{1,0:T(8,128)(2,1)S(1)}, u32[]{:S(2)}, u32[]{:S(2)}) collective-permute-start(bf16[192,768]{1,0:T(8,128)(2,1)S(1)} %get-tuple-element.208), channel_id=1, source_target_pairs={{0,3},{1,2},{2,1},{3,0},{4,7},{5,6},{6,5},{7,4},{8,11},{9,10},{10,... | collective-permute-start | bytes 884744 | tf_op jit(solution)/shard_map/ppermute | solution.py:440
  112.7 0.5 collective-permute-start.30
  113.2 1.2 collective-permute-start.31
  114.4 1.4 shard_map.222
  116.0 0.6 collective-permute-start.34
  116.6 5.1 %collective-permute-done.29.refs_1_ = bf16[192,768]{1,0:T(8,128)(2,1)S(1)} collective-permute-done((bf16[192,768]{1,0:T(8,128)(2,1)S(1)}, bf16[192,768]{1,0:T(8,128)(2,1)S(1)}, u32[]{:S(2)}, u32[]{:S(2)}) %collective-permute-start.29) | collective-permute-done | bytes 294944 | tf_op jit(solution)/shard_map/ppermute | solution.py:440
  121.7 5.7 %collective-permute-done.30.refs_2_ = bf16[192,768]{1,0:T(8,128)(2,1)S(1)} collective-permute-done((bf16[192,768]{1,0:T(8,128)(2,1)S(1)}, bf16[192,768]{1,0:T(8,128)(2,1)S(1)}, u32[]{:S(2)}, u32[]{:S(2)}) %collective-permute-start.30) | collective-permute-done | bytes 294944 | tf_op jit(solution)/shard_map/ppermute | solution.py:440
  127.8 0.6 collective-permute-start.28
  128.5 1.0 collective-permute-start.38
  129.6 1.4 collective-permute-start.32
  131.0 2.4 %shard_map.224 = (bf16[394,768]{1,0:T(8,128)(2,1)}, f32[16,768]{1,0:T(8,128)S(1)}) custom-call(s32[8]{0:T(128)S(1)} %stack.38.ids, bf16[394,384]{1,0:T(8,128)(2,1)S(1)} %add_convert_fusion.2.own, bf16[394,384]{1,0:T(8,128)(2,1)S(1)} %collective-permute-done.35.other, bf16[394,768]{1,0:T(8,128)(2,1)S(1)} %copy-done.5, ...), custom_call_target="tpu_custom_call" | custom-call | flops 11500000 | bytes 1024 | tf_op jit(solution)/shard_map/pallas_call | solution.py:413
  133.4 1.5 collective-permute-start.36
  134.9 2.0 %collective-permute-done.28 = bf16[400,384]{1,0:T(8,128)(2,1)S(1)} collective-permute-done((bf16[400,384]{1,0:T(8,128)(2,1)S(1)}, bf16[400,384]{1,0:T(8,128)(2,1)S(1)}, u32[]{:S(2)}, u32[]{:S(2)}) %collective-permute-start.28) | collective-permute-done | bytes 307232 | tf_op jit(solution)/shard_map/ppermute | solution.py:430
  136.9 0.8 add_convert_fusion.4
  137.7 9.7 %collective-permute-done.32.came = bf16[192,768]{1,0:T(8,128)(2,1)S(1)} collective-permute-done((bf16[192,768]{1,0:T(8,128)(2,1)S(1)}, bf16[192,768]{1,0:T(8,128)(2,1)S(1)}, u32[]{:S(2)}, u32[]{:S(2)}) %collective-permute-start.32) | collective-permute-done | bytes 294944 | tf_op jit(solution)/shard_map/ppermute | solution.py:433
  147.4 0.5 collective-permute-done.36.small_came
  148.1 0.7 copy-done.11
  148.9 1.1 collective-permute-start.40
  150.0 2.4 %collective-permute-start.41 = (bf16[208,768]{1,0:T(8,128)(2,1)}, bf16[208,768]{1,0:T(8,128)(2,1)S(1)}, u32[]{:S(2)}, u32[]{:S(2)}) collective-permute-start(bf16[208,768]{1,0:T(8,128)(2,1)} %copy-done.11), channel_id=1, source_target_pairs={{0,2},{1,3},{2,0},{3,1},{4,6},{5,7},{6,4},{7,5},{8,10},{9,11},{10,... | collective-permute-start | bytes 958472 | tf_op jit(solution)/shard_map/ppermute | solution.py:440
  152.3 2.3 %select_convert_fusion = bf16[394,768]{1,0:T(8,128)(2,1)} fusion(f32[394,768]{1,0:T(8,128)S(1)} %copy-done.3, bf16[400,384]{1,0:T(8,128)(2,1)} %collective-permute-done.37, bf16[400,384]{1,0:T(8,128)(2,1)} %add_convert_fusion.4, pred[394]{0:T(512)(128)(4,1)S(1)} %iota_compare_fusion, pred[]{:T(512)S(6)} %eq.7), kind=kLoop, calls=%fused_computation | loop fusion | flops 3933696 | bytes 2430347 | tf_op jit(solution)/shard_map/convert_element_type | solution.py:717
  154.6 5.0 %collective-permute-done.38.came_rest = bf16[640,768]{1,0:T(8,128)(2,1)S(1)} collective-permute-done((bf16[640,768]{1,0:T(8,128)(2,1)S(1)}, bf16[640,768]{1,0:T(8,128)(2,1)S(1)}, u32[]{:S(2)}, u32[]{:S(2)}) %collective-permute-start.38) | collective-permute-done | bytes 983072 | tf_op jit(solution)/shard_map/ppermute | solution.py:436
  159.6 1.7 shard_map.226
  161.3 5.1 %collective-permute-done.40.refs_2_ = bf16[208,768]{1,0:T(8,128)(2,1)S(1)} collective-permute-done((bf16[208,768]{1,0:T(8,128)(2,1)}, bf16[208,768]{1,0:T(8,128)(2,1)S(1)}, u32[]{:S(2)}, u32[]{:S(2)}) %collective-permute-start.40) | collective-permute-done | bytes 319520 | tf_op jit(solution)/shard_map/ppermute | solution.py:440
  166.4 2.2 %shard_map.227 = (f32[576,768]{1,0:T(8,128)}, f32[192,768]{1,0:T(8,128)}, f32[768]{0:T(1024)}, f32[768]{0:T(1024)}, f32[768]{0:T(1024)}, /*index=5*/f32[768]{0:T(1024)}, f32[4,768]{1,0:T(4,128)}) custom-call(s32[8]{0:T(128)S(1)} %stack.38.ids, bf16[208,768]{1,0:T(8,128)(2,1)S(1)} %copy-done.12, bf16[208,768]{1,0:T(8,128)(2,1)S(1)} %collective-permute-done.39.refs_1_, ...), custom_call_target="tpu_custom_call" | custom-call | flops 3449999872 | bytes 1024 | tf_op jit(solution)/shard_map/pallas_call | solution.py:413
  (89 shorter events, 2.5 us)
Async XLA Ops:
  0.6 11.0 %collective-permute-start.2 = (bf16[768,768]{1,0:T(8,128)(2,1)}, bf16[768,768]{1,0:T(8,128)(2,1)S(1)}, u32[]{:S(2)}, u32[]{:S(2)}) collective-permute-start(bf16[768,768]{1,0:T(8,128)(2,1)} %bitcast.26), channel_id=1, source_target_pairs={{0,8},{8,0},{16,24},{24,16},{1,9},{9,1},{17,25},{25,17},{2,10},{10... | collective-permute-start | bytes 3538952 | tf_op jit(solution)/shard_map/ppermute | solution.py:430
  1.2 10.5 %collective-permute-start.3 = (bf16[768,768]{1,0:T(8,128)(2,1)}, bf16[768,768]{1,0:T(8,128)(2,1)S(1)}, u32[]{:S(2)}, u32[]{:S(2)}) collective-permute-start(bf16[768,768]{1,0:T(8,128)(2,1)} %bitcast.29), channel_id=1, source_target_pairs={{0,8},{8,0},{16,24},{24,16},{1,9},{9,1},{17,25},{25,17},{2,10},{10... | collective-permute-start | bytes 3538952 | tf_op jit(solution)/shard_map/ppermute | solution.py:430
  1.2 10.4 %collective-permute-start = (bf16[192,768]{1,0:T(8,128)(2,1)}, bf16[192,768]{1,0:T(8,128)(2,1)S(1)}, u32[]{:S(2)}, u32[]{:S(2)}) collective-permute-start(bf16[192,768]{1,0:T(8,128)(2,1)} %w_out.1), channel_id=1, source_target_pairs={{0,16},{8,24},{16,0},{24,8},{1,17},{9,25},{17,1},{25,9},{2,18},{10... | collective-permute-start | bytes 884744 | tf_op jit(solution)/shard_map/ppermute | solution.py:430
  4.2 7.5 %collective-permute-start.1 = (bf16[192,768]{1,0:T(8,128)(2,1)}, bf16[192,768]{1,0:T(8,128)(2,1)S(1)}, u32[]{:S(2)}, u32[]{:S(2)}) collective-permute-start(bf16[192,768]{1,0:T(8,128)(2,1)} %w_out.1), channel_id=1, source_target_pairs={{0,8},{8,0},{16,24},{24,16},{1,9},{9,1},{17,25},{25,17},{2,10},{10... | collective-permute-start | bytes 884744 | tf_op jit(solution)/shard_map/ppermute | solution.py:430
  4.9 1.1 copy-start.4
  6.0 0.7 copy-start.6
  6.7 1.2 copy-start.8
  7.8 0.7 copy-start.15
  8.5 5.2 %copy-start.10 = (bf16[394,768]{1,0:T(8,128)(2,1)S(1)}, bf16[394,768]{1,0:T(8,128)(2,1)}, u32[]{:S(2)}) copy-start(bf16[394,768]{1,0:T(8,128)(2,1)} %cot.3) | copy-start | bytes 1815556
  8.5 5.2 %copy-start.14 = (bf16[768,4]{0,1:T(4,128)(2,1)S(1)}, bf16[768,4]{0,1:T(4,128)(2,1)}, u32[]{:S(2)}) copy-start(bf16[768,4]{0,1:T(4,128)(2,1)} %param.22) | copy-start | bytes 18436
  8.5 5.2 %copy-start.16 = (s32[394,2]{0,1:T(2,128)S(1)}, s32[394,2]{0,1:T(2,128)}, u32[]{:S(2)}) copy-start(s32[394,2]{0,1:T(2,128)} %param.14) | copy-start | bytes 9460
  11.6 11.8 %collective-permute-start.4 = (bf16[394,192]{1,0:T(8,128)(2,1)S(1)}, bf16[394,192]{1,0:T(8,128)(2,1)S(1)}, u32[]{:S(2)}, u32[]{:S(2)}) collective-permute-start(bf16[394,192]{1,0:T(8,128)(2,1)S(1)} %get-tuple-element.124.rest_0_.head_out), channel_id=1, source_target_pairs={{0,8},{8,0},{16,24},{24,16},{1,9},{9,1},{17,25},{25,17},{2,10},{10... | collective-permute-start | bytes 453896 | tf_op jit(solution)/shard_map/ppermute | solution.py:430
  11.7 7.5 %collective-permute-start.5 = (bf16[394,192]{1,0:T(8,128)(2,1)S(1)}, bf16[394,192]{1,0:T(8,128)(2,1)S(1)}, u32[]{:S(2)}, u32[]{:S(2)}) collective-permute-start(bf16[394,192]{1,0:T(8,128)(2,1)S(1)} %get-tuple-element.124.rest_0_.head_out), channel_id=1, source_target_pairs={{0,16},{8,24},{16,0},{24,8},{1,17},{9,25},{17,1},{25,9},{2,18},{10... | collective-permute-start | bytes 453896 | tf_op jit(solution)/shard_map/ppermute | solution.py:430
  13.5 9.9 %collective-permute-start.7 = (bf16[192,768]{1,0:T(8,128)(2,1)S(1)}, bf16[192,768]{1,0:T(8,128)(2,1)S(1)}, u32[]{:S(2)}, u32[]{:S(2)}) collective-permute-start(bf16[192,768]{1,0:T(8,128)(2,1)S(1)} %collective-permute-done.rest_6_), channel_id=1, source_target_pairs={{0,8},{8,0},{16,24},{24,16},{1,9},{9,1},{17,25},{25,17},{2,10},{10... | collective-permute-start | bytes 884744 | tf_op jit(solution)/shard_map/ppermute | solution.py:430
  13.7 9.7 %copy-start.5 = (bf16[394,768]{1,0:T(8,128)(2,1)S(1)}, bf16[394,768]{1,0:T(8,128)(2,1)}, u32[]{:S(2)}) copy-start(bf16[394,768]{1,0:T(8,128)(2,1)} %tokens.5) | copy-start | bytes 1815556
  13.7 9.7 %copy-start.13 = (bf16[192,768]{1,0:T(8,128)(2,1)S(1)}, bf16[192,768]{1,0:T(8,128)(2,1)}, u32[]{:S(2)}) copy-start(bf16[192,768]{1,0:T(8,128)(2,1)} %w_out.1) | copy-start | bytes 884740
  13.7 9.7 %copy-start.17 = (f32[768]{0:T(1024)S(1)}, f32[768]{0:T(1024)}, u32[]{:S(2)}) copy-start(f32[768]{0:T(1024)} %bias.3) | copy-start | bytes 9220
  13.7 9.7 %copy-start.18 = (f32[768]{0:T(1024)S(1)}, f32[768]{0:T(1024)}, u32[]{:S(2)}) copy-start(f32[768]{0:T(1024)} %gain.6) | copy-start | bytes 9220
  19.2 4.2 %collective-permute-start.6 = (bf16[394,192]{1,0:T(8,128)(2,1)S(1)}, bf16[394,192]{1,0:T(8,128)(2,1)S(1)}, u32[]{:S(2)}, u32[]{:S(2)}) collective-permute-start(bf16[394,192]{1,0:T(8,128)(2,1)S(1)} %collective-permute-done.5.rest_2_), channel_id=1, source_target_pairs={{0,8},{8,0},{16,24},{24,16},{1,9},{9,1},{17,25},{25,17},{2,10},{10... | collective-permute-start | bytes 453896 | tf_op jit(solution)/shard_map/ppermute | solution.py:430
  19.2 11.6 %collective-permute-start.8 = (bf16[72,768]{1,0:T(8,128)(2,1)S(1)}, bf16[72,768]{1,0:T(8,128)(2,1)S(1)}, u32[]{:S(2)}, u32[]{:S(2)}) collective-permute-start(bf16[72,768]{1,0:T(8,128)(2,1)S(1)} %get-tuple-element.141), channel_id=1, source_target_pairs={{0,4},{2,6},{4,0},{6,2},{1,5},{3,7},{5,1},{7,3},{8,12},{10,14},{12... | collective-permute-start | bytes 331784 | tf_op jit(solution)/shard_map/ppermute | solution.py:433
  22.0 8.7 %collective-permute-start.9 = (bf16[72,768]{1,0:T(8,128)(2,1)S(1)}, bf16[72,768]{1,0:T(8,128)(2,1)S(1)}, u32[]{:S(2)}, u32[]{:S(2)}) collective-permute-start(bf16[72,768]{1,0:T(8,128)(2,1)S(1)} %get-tuple-element.142), channel_id=1, source_target_pairs={{0,6},{2,4},{4,2},{6,0},{1,7},{3,5},{5,3},{7,1},{8,14},{10,12},{12... | collective-permute-start | bytes 331784 | tf_op jit(solution)/shard_map/ppermute | solution.py:433
  23.4 25.3 %copy-start = (bf16[1,768,768]{2,1,0:T(8,128)(2,1)S(1)}, bf16[1,768,768]{2,1,0:T(8,128)(2,1)}, u32[]{:S(2)}) copy-start(bf16[1,768,768]{2,1,0:T(8,128)(2,1)} %param.23) | copy-start | bytes 3538948
  23.5 25.3 %copy-start.1 = (bf16[1,768,768]{2,1,0:T(8,128)(2,1)S(1)}, bf16[1,768,768]{2,1,0:T(8,128)(2,1)}, u32[]{:S(2)}) copy-start(bf16[1,768,768]{2,1,0:T(8,128)(2,1)} %param.24) | copy-start | bytes 3538948
  26.2 79.5 %copy-start.2 = (f32[394,768]{1,0:T(8,128)}, f32[394,768]{1,0:T(8,128)S(1)}, u32[]{:S(2)}) copy-start(f32[394,768]{1,0:T(8,128)S(1)} %get-tuple-element.132.middle) | copy-start | bytes 3631108
  30.8 13.8 %collective-permute-start.10 = (bf16[144,768]{1,0:T(8,128)(2,1)S(1)}, bf16[144,768]{1,0:T(8,128)(2,1)S(1)}, u32[]{:S(2)}, u32[]{:S(2)}) collective-permute-start(bf16[144,768]{1,0:T(8,128)(2,1)S(1)} %get-tuple-element.144), channel_id=1, source_target_pairs={{0,2},{2,0},{4,6},{6,4},{1,3},{3,1},{5,7},{7,5},{8,10},{10,8},{12,... | collective-permute-start | bytes 663560 | tf_op jit(solution)/shard_map/ppermute | solution.py:433
  33.6 15.1 %collective-permute-start.11 = (bf16[144,768]{1,0:T(8,128)(2,1)S(1)}, bf16[144,768]{1,0:T(8,128)(2,1)S(1)}, u32[]{:S(2)}, u32[]{:S(2)}) collective-permute-start(bf16[144,768]{1,0:T(8,128)(2,1)S(1)} %get-tuple-element.146), channel_id=1, source_target_pairs={{0,2},{2,0},{4,6},{6,4},{1,3},{3,1},{5,7},{7,5},{8,10},{10,8},{12,... | collective-permute-start | bytes 663560 | tf_op jit(solution)/shard_map/ppermute | solution.py:433
  33.7 22.1 %collective-permute-start.12 = (bf16[144,768]{1,0:T(8,128)(2,1)S(1)}, bf16[144,768]{1,0:T(8,128)(2,1)S(1)}, u32[]{:S(2)}, u32[]{:S(2)}) collective-permute-start(bf16[144,768]{1,0:T(8,128)(2,1)S(1)} %get-tuple-element.149), channel_id=1, source_target_pairs={{0,4},{2,6},{4,0},{6,2},{1,5},{3,7},{5,1},{7,3},{8,12},{10,14},{12... | collective-permute-start | bytes 663560 | tf_op jit(solution)/shard_map/ppermute | solution.py:433
  37.6 19.1 %collective-permute-start.13 = (bf16[144,768]{1,0:T(8,128)(2,1)S(1)}, bf16[144,768]{1,0:T(8,128)(2,1)S(1)}, u32[]{:S(2)}, u32[]{:S(2)}) collective-permute-start(bf16[144,768]{1,0:T(8,128)(2,1)S(1)} %get-tuple-element.150), channel_id=1, source_target_pairs={{0,6},{2,4},{4,2},{6,0},{1,7},{3,5},{5,3},{7,1},{8,14},{10,12},{12... | collective-permute-start | bytes 663560 | tf_op jit(solution)/shard_map/ppermute | solution.py:433
  38.0 18.7 %collective-permute-start.14 = (bf16[2,72,768]{2,1,0:T(8,128)(2,1)S(1)}, bf16[2,72,768]{2,1,0:T(8,128)(2,1)S(1)}, u32[]{:S(2)}, u32[]{:S(2)}) collective-permute-start(bf16[2,72,768]{2,1,0:T(8,128)(2,1)S(1)} %pad_maximum_fusion.2), channel_id=1, source_target_pairs={{0,16},{8,24},{16,0},{24,8},{1,17},{9,25},{17,1},{25,9},{2,18},{10... | collective-permute-start | bytes 663560 | tf_op jit(solution)/shard_map/ppermute | solution.py:430
  64.2 6.0 %collective-permute-start.19 = (bf16[1536,768]{1,0:T(8,128)(2,1)S(1)}, bf16[1536,768]{1,0:T(8,128)(2,1)S(1)}, u32[]{:S(2)}, u32[]{:S(2)}) collective-permute-start(bf16[1536,768]{1,0:T(8,128)(2,1)S(1)} %get-tuple-element.173), channel_id=1, source_target_pairs={{0,8},{8,0},{16,24},{24,16},{1,9},{9,1},{17,25},{25,17},{2,10},{10... | collective-permute-start | bytes 7077896 | tf_op jit(solution)/shard_map/ppermute | solution.py:430
  64.3 11.5 %collective-permute-start.15 = (bf16[144,768]{1,0:T(8,128)(2,1)S(1)}, bf16[144,768]{1,0:T(8,128)(2,1)S(1)}, u32[]{:S(2)}, u32[]{:S(2)}) collective-permute-start(bf16[144,768]{1,0:T(8,128)(2,1)S(1)} %get-tuple-element.153), channel_id=1, source_target_pairs={{0,6},{2,4},{4,2},{6,0},{1,7},{3,5},{5,3},{7,1},{8,14},{10,12},{12... | collective-permute-start | bytes 663560 | tf_op jit(solution)/shard_map/ppermute | solution.py:433
  67.5 19.1 %collective-permute-start.16 = (bf16[144,768]{1,0:T(8,128)(2,1)S(1)}, bf16[144,768]{1,0:T(8,128)(2,1)S(1)}, u32[]{:S(2)}, u32[]{:S(2)}) collective-permute-start(bf16[144,768]{1,0:T(8,128)(2,1)S(1)} %get-tuple-element.156), channel_id=1, source_target_pairs={{0,4},{2,6},{4,0},{6,2},{1,5},{3,7},{5,1},{7,3},{8,12},{10,14},{12... | collective-permute-start | bytes 663560 | tf_op jit(solution)/shard_map/ppermute | solution.py:433
  67.5 19.1 %collective-permute-start.17 = (bf16[144,768]{1,0:T(8,128)(2,1)S(1)}, bf16[144,768]{1,0:T(8,128)(2,1)S(1)}, u32[]{:S(2)}, u32[]{:S(2)}) collective-permute-start(bf16[144,768]{1,0:T(8,128)(2,1)S(1)} %get-tuple-element.157), channel_id=1, source_target_pairs={{0,2},{2,0},{4,6},{6,4},{1,3},{3,1},{5,7},{7,5},{8,10},{10,8},{12,... | collective-permute-start | bytes 663560 | tf_op jit(solution)/shard_map/ppermute | solution.py:433
  68.7 6.9 %collective-permute-start.18 = (bf16[2,72,768]{2,1,0:T(8,128)(2,1)S(1)}, bf16[2,72,768]{2,1,0:T(8,128)(2,1)S(1)}, u32[]{:S(2)}, u32[]{:S(2)}) collective-permute-start(bf16[2,72,768]{2,1,0:T(8,128)(2,1)S(1)} %get-tuple-element.161), channel_id=1, source_target_pairs={{0,16},{8,24},{16,0},{24,8},{1,17},{9,25},{17,1},{25,9},{2,18},{10... | collective-permute-start | bytes 663560 | tf_op jit(solution)/shard_map/ppermute | solution.py:430
  71.9 3.8 %copy-start.19 = (f32[768,768]{1,0:T(8,128)}, f32[768,768]{1,0:T(8,128)S(1)}, u32[]{:S(2)}) copy-start(f32[768,768]{1,0:T(8,128)S(1)} %get-tuple-element.220.kept) | copy-start | bytes 7077892
  71.9 14.7 %collective-permute-start.20 = (bf16[128,768]{1,0:T(8,128)(2,1)S(1)}, bf16[128,768]{1,0:T(8,128)(2,1)S(1)}, u32[]{:S(2)}, u32[]{:S(2)}) collective-permute-start(bf16[128,768]{1,0:T(8,128)(2,1)S(1)} %get-tuple-element.174), channel_id=1, source_target_pairs={{0,1},{1,0},{2,3},{3,2},{4,5},{5,4},{6,7},{7,6},{8,9},{9,8},{10,11... | collective-permute-start | bytes 589832 | tf_op jit(solution)/shard_map/ppermute | solution.py:436
  88.1 17.6 %copy-start.9 = (bf16[768,3,192]{0,2,1:T(8,128)(2,1)S(1)}, bf16[768,3,192]{0,2,1:T(8,128)(2,1)}, u32[]{:S(2)}) copy-start(bf16[768,3,192]{0,2,1:T(8,128)(2,1)} %param.18) | copy-start | bytes 2654212
  88.1 1.7 collective-permute-start.21
  89.8 9.6 %collective-permute-start.22 = (bf16[416,384]{1,0:T(8,128)(2,1)S(1)}, bf16[416,384]{1,0:T(8,128)(2,1)S(1)}, u32[]{:S(2)}, u32[]{:S(2)}) collective-permute-start(bf16[416,384]{1,0:T(8,128)(2,1)S(1)} %add_convert_fusion.1), channel_id=1, source_target_pairs={{0,16},{8,24},{16,0},{24,8},{1,17},{9,25},{17,1},{25,9},{2,18},{10... | collective-permute-start | bytes 958472 | tf_op jit(solution)/shard_map/ppermute | solution.py:430
  91.4 12.7 %collective-permute-start.23 = (bf16[144,768]{1,0:T(8,128)(2,1)S(1)}, bf16[144,768]{1,0:T(8,128)(2,1)S(1)}, u32[]{:S(2)}, u32[]{:S(2)}) collective-permute-start(bf16[144,768]{1,0:T(8,128)(2,1)S(1)} %get-tuple-element.184), channel_id=1, source_target_pairs={{0,2},{2,0},{4,6},{6,4},{1,3},{3,1},{5,7},{7,5},{8,10},{10,8},{12,... | collective-permute-start | bytes 663560 | tf_op jit(solution)/shard_map/ppermute | solution.py:433
  91.4 8.2 %collective-permute-start.24 = (bf16[72,768]{1,0:T(8,128)(2,1)S(1)}, bf16[72,768]{1,0:T(8,128)(2,1)S(1)}, u32[]{:S(2)}, u32[]{:S(2)}) collective-permute-start(bf16[72,768]{1,0:T(8,128)(2,1)S(1)} %get-tuple-element.185), channel_id=1, source_target_pairs={{0,4},{2,6},{4,0},{6,2},{1,5},{3,7},{5,1},{7,3},{8,12},{10,14},{12... | collective-permute-start | bytes 331784 | tf_op jit(solution)/shard_map/ppermute | solution.py:433
  94.4 9.7 %collective-permute-start.25 = (bf16[72,768]{1,0:T(8,128)(2,1)S(1)}, bf16[72,768]{1,0:T(8,128)(2,1)S(1)}, u32[]{:S(2)}, u32[]{:S(2)}) collective-permute-start(bf16[72,768]{1,0:T(8,128)(2,1)S(1)} %get-tuple-element.186), channel_id=1, source_target_pairs={{0,6},{2,4},{4,2},{6,0},{1,7},{3,5},{5,3},{7,1},{8,14},{10,12},{12... | collective-permute-start | bytes 331784 | tf_op jit(solution)/shard_map/ppermute | solution.py:433
  104.1 1.6 collective-permute-start.26
  110.7 5.2 %collective-permute-start.33 = (bf16[394,384]{1,0:T(8,128)(2,1)S(1)}, bf16[394,384]{1,0:T(8,128)(2,1)S(1)}, u32[]{:S(2)}, u32[]{:S(2)}) collective-permute-start(bf16[394,384]{1,0:T(8,128)(2,1)S(1)} %get-tuple-element.213), channel_id=1, source_target_pairs={{0,8},{8,0},{16,24},{24,16},{1,9},{9,1},{17,25},{25,17},{2,10},{10... | collective-permute-start | bytes 907784 | tf_op jit(solution)/shard_map/ppermute | solution.py:430
  110.9 10.8 %collective-permute-start.29 = (bf16[192,768]{1,0:T(8,128)(2,1)S(1)}, bf16[192,768]{1,0:T(8,128)(2,1)S(1)}, u32[]{:S(2)}, u32[]{:S(2)}) collective-permute-start(bf16[192,768]{1,0:T(8,128)(2,1)S(1)} %get-tuple-element.208), channel_id=1, source_target_pairs={{0,3},{1,2},{2,1},{3,0},{4,7},{5,6},{6,5},{7,4},{8,11},{9,10},{10,... | collective-permute-start | bytes 884744 | tf_op jit(solution)/shard_map/ppermute | solution.py:440
  112.7 14.7 %collective-permute-start.30 = (bf16[192,768]{1,0:T(8,128)(2,1)S(1)}, bf16[192,768]{1,0:T(8,128)(2,1)S(1)}, u32[]{:S(2)}, u32[]{:S(2)}) collective-permute-start(bf16[192,768]{1,0:T(8,128)(2,1)S(1)} %get-tuple-element.209), channel_id=1, source_target_pairs={{0,1},{1,0},{2,3},{3,2},{4,5},{5,4},{6,7},{7,6},{8,9},{9,8},{10,11... | collective-permute-start | bytes 884744 | tf_op jit(solution)/shard_map/ppermute | solution.py:440
  113.2 14.3 %collective-permute-start.31 = (bf16[192,768]{1,0:T(8,128)(2,1)S(1)}, bf16[192,768]{1,0:T(8,128)(2,1)S(1)}, u32[]{:S(2)}, u32[]{:S(2)}) collective-permute-start(bf16[192,768]{1,0:T(8,128)(2,1)S(1)} %get-tuple-element.210), channel_id=1, source_target_pairs={{0,2},{1,3},{2,0},{3,1},{4,6},{5,7},{6,4},{7,5},{8,10},{9,11},{10,... | collective-permute-start | bytes 884744 | tf_op jit(solution)/shard_map/ppermute | solution.py:440
  115.8 11.8 %collective-permute-start.27 = (bf16[400,384]{1,0:T(8,128)(2,1)S(1)}, bf16[400,384]{1,0:T(8,128)(2,1)S(1)}, u32[]{:S(2)}, u32[]{:S(2)}) collective-permute-start(bf16[400,384]{1,0:T(8,128)(2,1)S(1)} %get-tuple-element.206), channel_id=1, source_target_pairs={{0,8},{8,0},{16,24},{24,16},{1,9},{9,1},{17,25},{25,17},{2,10},{10... | collective-permute-start | bytes 921608 | tf_op jit(solution)/shard_map/ppermute | solution.py:430
  116.0 12.3 %collective-permute-start.34 = (bf16[394,384]{1,0:T(8,128)(2,1)S(1)}, bf16[394,384]{1,0:T(8,128)(2,1)S(1)}, u32[]{:S(2)}, u32[]{:S(2)}) collective-permute-start(bf16[394,384]{1,0:T(8,128)(2,1)S(1)} %add_convert_fusion.3), channel_id=1, source_target_pairs={{0,16},{8,24},{16,0},{24,8},{1,17},{9,25},{17,1},{25,9},{2,18},{10... | collective-permute-start | bytes 907784 | tf_op jit(solution)/shard_map/ppermute | solution.py:430
  127.7 3.3 %copy-start.7 = (f32[768]{0:T(1024)S(1)}, f32[768]{0:T(1024)}, u32[]{:S(2)}) copy-start(f32[768]{0:T(1024)} %gain.7) | copy-start | bytes 9220
  127.8 9.2 %collective-permute-start.28 = (bf16[400,384]{1,0:T(8,128)(2,1)S(1)}, bf16[400,384]{1,0:T(8,128)(2,1)S(1)}, u32[]{:S(2)}, u32[]{:S(2)}) collective-permute-start(bf16[400,384]{1,0:T(8,128)(2,1)S(1)} %add_convert_fusion.5), channel_id=1, source_target_pairs={{0,16},{8,24},{16,0},{24,8},{1,17},{9,25},{17,1},{25,9},{2,18},{10... | collective-permute-start | bytes 921608 | tf_op jit(solution)/shard_map/ppermute | solution.py:430
  128.4 2.5 %collective-permute-start.35 = (bf16[394,384]{1,0:T(8,128)(2,1)S(1)}, bf16[394,384]{1,0:T(8,128)(2,1)S(1)}, u32[]{:S(2)}, u32[]{:S(2)}) collective-permute-start(bf16[394,384]{1,0:T(8,128)(2,1)S(1)} %add_convert_fusion.2.own), channel_id=1, source_target_pairs={{0,8},{8,0},{16,24},{24,16},{1,9},{9,1},{17,25},{25,17},{2,10},{10... | collective-permute-start | bytes 907784 | tf_op jit(solution)/shard_map/ppermute | solution.py:430
  128.5 31.1 %collective-permute-start.38 = (bf16[640,768]{1,0:T(8,128)(2,1)S(1)}, bf16[640,768]{1,0:T(8,128)(2,1)S(1)}, u32[]{:S(2)}, u32[]{:S(2)}) collective-permute-start(bf16[640,768]{1,0:T(8,128)(2,1)S(1)} %get-tuple-element.222), channel_id=1, source_target_pairs={{0,1},{1,0},{2,3},{3,2},{4,5},{5,4},{6,7},{7,6},{8,9},{9,8},{10,11... | collective-permute-start | bytes 2949128 | tf_op jit(solution)/shard_map/ppermute | solution.py:436
  129.6 17.9 %collective-permute-start.32 = (bf16[192,768]{1,0:T(8,128)(2,1)S(1)}, bf16[192,768]{1,0:T(8,128)(2,1)S(1)}, u32[]{:S(2)}, u32[]{:S(2)}) collective-permute-start(bf16[192,768]{1,0:T(8,128)(2,1)S(1)} %shard_map.223.own), channel_id=1, source_target_pairs={{0,4},{2,6},{4,0},{6,2},{1,5},{3,7},{5,1},{7,3},{8,12},{10,14},{12... | collective-permute-start | bytes 884744 | tf_op jit(solution)/shard_map/ppermute | solution.py:433
  133.4 14.6 %collective-permute-start.36 = (f32[16,768]{1,0:T(8,128)S(1)}, f32[16,768]{1,0:T(8,128)S(1)}, u32[]{:S(2)}, u32[]{:S(2)}) collective-permute-start(f32[16,768]{1,0:T(8,128)S(1)} %get-tuple-element.216.small), channel_id=1, source_target_pairs={{0,4},{2,6},{4,0},{6,2},{1,5},{3,7},{5,1},{7,3},{8,12},{10,14},{12... | collective-permute-start | bytes 147464 | tf_op jit(solution)/shard_map/ppermute | solution.py:433
  137.7 14.6 %copy-start.3 = (f32[394,768]{1,0:T(8,128)S(1)}, f32[394,768]{1,0:T(8,128)}, u32[]{:S(2)}) copy-start(f32[394,768]{1,0:T(8,128)} %copy-done.2) | copy-start | bytes 3631108
  148.1 0.7 copy-start.11
  148.8 3.6 %collective-permute-start.37 = (bf16[400,384]{1,0:T(8,128)(2,1)}, bf16[400,384]{1,0:T(8,128)(2,1)}, u32[]{:S(2)}, u32[]{:S(2)}) collective-permute-start(bf16[400,384]{1,0:T(8,128)(2,1)} %add_convert_fusion.4), channel_id=1, source_target_pairs={{0,8},{8,0},{16,24},{24,16},{1,9},{9,1},{17,25},{25,17},{2,10},{10... | collective-permute-start | bytes 921608 | tf_op jit(solution)/shard_map/ppermute | solution.py:430
  148.8 10.8 %copy-start.20 = (f32[768,768]{1,0:T(8,128)S(1)}, f32[768,768]{1,0:T(8,128)}, u32[]{:S(2)}) copy-start(f32[768,768]{1,0:T(8,128)} %copy-done.19) | copy-start | bytes 7077892
  148.8 12.5 %collective-permute-start.39 = (bf16[208,768]{1,0:T(8,128)(2,1)}, bf16[208,768]{1,0:T(8,128)(2,1)S(1)}, u32[]{:S(2)}, u32[]{:S(2)}) collective-permute-start(bf16[208,768]{1,0:T(8,128)(2,1)} %copy-done.11), channel_id=1, source_target_pairs={{0,3},{1,2},{2,1},{3,0},{4,7},{5,6},{6,5},{7,4},{8,11},{9,10},{10,... | collective-permute-start | bytes 958472 | tf_op jit(solution)/shard_map/ppermute | solution.py:440
  148.9 17.5 %collective-permute-start.40 = (bf16[208,768]{1,0:T(8,128)(2,1)}, bf16[208,768]{1,0:T(8,128)(2,1)S(1)}, u32[]{:S(2)}, u32[]{:S(2)}) collective-permute-start(bf16[208,768]{1,0:T(8,128)(2,1)} %copy-done.11), channel_id=1, source_target_pairs={{0,1},{1,0},{2,3},{3,2},{4,5},{5,4},{6,7},{7,6},{8,9},{9,8},{10,11... | collective-permute-start | bytes 958472 | tf_op jit(solution)/shard_map/ppermute | solution.py:440
  150.0 16.4 %collective-permute-start.41 = (bf16[208,768]{1,0:T(8,128)(2,1)}, bf16[208,768]{1,0:T(8,128)(2,1)S(1)}, u32[]{:S(2)}, u32[]{:S(2)}) collective-permute-start(bf16[208,768]{1,0:T(8,128)(2,1)} %copy-done.11), channel_id=1, source_target_pairs={{0,2},{1,3},{2,0},{3,1},{4,6},{5,7},{6,4},{7,5},{8,10},{9,11},{10,... | collective-permute-start | bytes 958472 | tf_op jit(solution)/shard_map/ppermute | solution.py:440
  159.6 6.8 %copy-start.12 = (bf16[208,768]{1,0:T(8,128)(2,1)S(1)}, bf16[208,768]{1,0:T(8,128)(2,1)}, u32[]{:S(2)}) copy-start(bf16[208,768]{1,0:T(8,128)(2,1)} %copy-done.11) | copy-start | bytes 958468

commit v11 on v10

--- a/solution.py
+++ b/solution.py
@@ -246,7 +246,7 @@
     )
 
 
-def split_grad_kernel(ids, own, came, kept, sent_first, sent_rest, total, sent):
+def split_grad_kernel(ids, own, came, kept, sent_first, sent_next, sent_rest, total, sent):
     total[...] = own[...].astype(F32) + came[...].astype(F32)
     width = own.shape[1]
     half = width // 2
@@ -261,13 +261,15 @@
     sent[half:, half:] = total[width + half :, column].astype(BF16)
     first = sent_first.shape[0]
     sent_first[...] = sent[:first, :]
-    sent_rest[...] = sent[first:, :]
-
-
-def join_grad_kernel(kept, came_first, came_rest, grad_up, grad_down, came):
+    sent_next[...] = sent[first : 2 * first, :]
+    sent_rest[...] = sent[2 * first :, :]
+
+
+def join_grad_kernel(kept, came_first, came_next, came_rest, grad_up, grad_down, came):
     first = came_first.shape[0]
     came[:first, :] = came_first[...]
-    came[first:, :] = came_rest[...]
+    came[first : 2 * first, :] = came_next[...]
+    came[2 * first :, :] = came_rest[...]
     half = kept.shape[1] // 2
     grad_up[...] = kept[:half, :] + came[:half, :].astype(F32)
     grad_down[:half, :] = kept[half:, :half] + came[half:, :half].astype(F32)
@@ -600,10 +602,12 @@
             micros=4,
             limit=24,
         )
-        third = width // 96 * 16
-        grad_kept, sent_first, sent_rest = run(
+        sixth = width // 96 * 16
+        grad_kept, sent_first, sent_next, sent_rest = run(
             split_grad_kernel,
-            [((width, width), F32), ((third, width), BF16), ((width - third, width), BF16)],
+            [((width, width), F32)]
+            + [((sixth, width), BF16)] * 2
+            + [((width - 2 * sixth, width), BF16)],
             [ids, grad_own, tensor_swap(grad_pair, 1)],
             scratch=[((2 * width, width), F32), ((width, width), BF16)],
             micros=2,
@@ -620,9 +624,9 @@
         else:
             gated_blocks = [gated[0][0][k] for k in range(experts)]
 
-        came_first = dp_swap(sent_first)
-        *gated_blocks, came_first = lax.optimization_barrier(
-            (*d_home[::-1], *gated_blocks, came_first)
+        came_first, came_next = dp_swap(sent_first), dp_swap(sent_next)
+        *gated_blocks, came_first, came_next = lax.optimization_barrier(
+            (*d_home[::-1], *gated_blocks, came_first, came_next)
         )
         d_home, gated_blocks = gated_blocks[:experts][::-1], gated_blocks[experts:]
         kept, sent = combine(list(d_home), [one[6] for one in worked])
@@ -677,7 +681,7 @@
         grad_up, grad_down = run(
             join_grad_kernel,
             [((half, hidden_width), F32), ((hidden_width, half), F32)],
-            [grad_kept, came_first, dp_swap(sent_rest)],
+            [grad_kept, came_first, came_next, dp_swap(sent_rest)],
             scratch=[((width, width), BF16)],
             micros=2,
         )

time: 169 us -> 168 us (level)
    ppermute x2 -> x3, waiting for transfers between devices: 4.98 us -> 0.01 us  [dp_swap(): return lax.ppermute(value, 'dp', [(i, i ^ 1) for i in range(n_dp)])]
    ppermute x6, waiting for transfers between devices: 16 us -> 19.6 us  [quarter_swap(): return lax.ppermute(value, ('expert', 'dp'), pairs)]
    ppermute x14, waiting for transfers between devices: 40.2 us -> 42.4 us  [expert_swap(): lax.ppermute(value, 'expert', [(i, i ^ mask) for i in range(n_expert)])]
    ppermute x20, waiting for transfers between devices: 15.8 us -> 13.6 us  [tensor_swap(): lax.ppermute(value, 'tensor', [(i, i ^ mask) for i in range(n_tensor)])]
    unnamed x42 -> x38, local copies, waits for them, and re-layouts: 4.41 us -> 3.69 us
  transfers between devices with their start and end apart: 42 -> 43, of which waited for: 20 -> 21; matrix products, arithmetic and copies ran while one was open for 2% -> 2% of each run, Pallas kernels for 13% -> 13%
where the time goes in v11:
time: 168 us
  waiting for transfers between devices  75.6 us (45%)
  starting transfers between devices  46.3 us (28%)
  Pallas kernels  37.2 us (22%)
  local copies, waits for them, and re-layouts  3.81 us (2%)
  other arithmetic  3.55 us (2%)
  between operations  1.7 us (1%)
    ppermute x14, waiting for transfers between devices, expert_swap(): lax.ppermute(value, 'expert', [(i, i ^ mask) for i in range(n_expert)])  42.4 us
    pallas_call x16, Pallas kernels, run(): pl.pallas_call(kernel, out_shape=[jax.ShapeDtypeStruct(shape, kind) for s...  37.2 us
    ppermute x14, starting transfers between devices, expert_swap(): lax.ppermute(value, 'expert', [(i, i ^ mask) for i in range(n_expert)])  23.5 us
    ppermute x6, waiting for transfers between devices, quarter_swap(): return lax.ppermute(value, ('expert', 'dp'), pairs)  19.6 us
    ppermute x20, waiting for transfers between devices, tensor_swap(): lax.ppermute(value, 'tensor', [(i, i ^ mask) for i in range(n_tensor)])  13.6 us
    ppermute x20, starting transfers between devices, tensor_swap(): lax.ppermute(value, 'tensor', [(i, i ^ mask) for i in range(n_tensor)])  13 us
    ppermute x6, starting transfers between devices, quarter_swap(): return lax.ppermute(value, ('expert', 'dp'), pairs)  7.05 us
    unnamed x38, local copies, waits for them, and re-layouts  3.69 us
  transfers between devices with their start and end apart: 43, of which 21 were waited for; matrix products, arithmetic and copies ran while one was open for 2% of the time, Pallas kernels for 13%

profile of v11, /device:TPU:0, one launch (start us, length us, event | category | flops | bytes accessed | tf_op | source)
XLA Modules:
  0.0 168.1 jit_solution(16873337811177601402)
XLA Ops:
  0.6 0.5 collective-permute-start.2
  1.2 2.9 %collective-permute-start = (bf16[192,768]{1,0:T(8,128)(2,1)}, bf16[192,768]{1,0:T(8,128)(2,1)S(1)}, u32[]{:S(2)}, u32[]{:S(2)}) collective-permute-start(bf16[192,768]{1,0:T(8,128)(2,1)} %w_out.1), channel_id=1, source_target_pairs={{0,16},{8,24},{16,0},{24,8},{1,17},{9,25},{17,1},{25,9},{2,18},{10... | collective-permute-start | bytes 884744 | tf_op jit(solution)/shard_map/ppermute | solution.py:432
  4.9 1.1 copy-done.4
  6.0 0.7 copy-done.6
  6.7 1.2 copy-done.8
  7.8 0.7 copy-done.13
  8.5 2.5 %shard_map.212 = (bf16[394,768]{1,0:T(8,128)(2,1)S(1)}, bf16[394,192]{1,0:T(8,128)(2,1)S(1)}, bf16[394,192]{1,0:T(8,128)(2,1)S(1)}, bf16[394,192]{1,0:T(8,128)(2...) custom-call(bf16[394,768]{1,0:T(8,128)(2,1)S(1)} %copy-done.4, f32[768]{0:T(1024)S(1)} %copy-done.6, ...), custom_call_target="tpu_custom_call" | custom-call | flops 4600000000 | bytes 1024 | tf_op jit(solution)/shard_map/pallas_call | solution.py:415
  11.1 0.6 collective-permute-done.rest_6_
  11.7 1.8 %collective-permute-start.5 = (bf16[394,192]{1,0:T(8,128)(2,1)S(1)}, bf16[394,192]{1,0:T(8,128)(2,1)S(1)}, u32[]{:S(2)}, u32[]{:S(2)}) collective-permute-start(bf16[394,192]{1,0:T(8,128)(2,1)S(1)} %get-tuple-element.126.rest_0_.head_out), channel_id=1, source_target_pairs={{0,16},{8,24},{16,0},{24,8},{1,17},{9,25},{17,1},{25,9},{2,18},{10... | collective-permute-start | bytes 453896 | tf_op jit(solution)/shard_map/ppermute | solution.py:432
  13.7 1.4 shard_map.213
  15.1 4.1 %collective-permute-done.5.rest_2_ = bf16[394,192]{1,0:T(8,128)(2,1)S(1)} collective-permute-done((bf16[394,192]{1,0:T(8,128)(2,1)S(1)}, bf16[394,192]{1,0:T(8,128)(2,1)S(1)}, u32[]{:S(2)}, u32[]{:S(2)}) %collective-permute-start.5) | collective-permute-done | bytes 151328 | tf_op jit(solution)/shard_map/ppermute | solution.py:432
  19.2 2.8 %collective-permute-start.8 = (bf16[72,768]{1,0:T(8,128)(2,1)S(1)}, bf16[72,768]{1,0:T(8,128)(2,1)S(1)}, u32[]{:S(2)}, u32[]{:S(2)}) collective-permute-start(bf16[72,768]{1,0:T(8,128)(2,1)S(1)} %get-tuple-element.143), channel_id=1, source_target_pairs={{0,4},{2,6},{4,0},{6,2},{1,5},{3,7},{5,1},{7,3},{8,12},{10,14},{12... | collective-permute-start | bytes 331784 | tf_op jit(solution)/shard_map/ppermute | solution.py:435
  22.0 1.3 collective-permute-start.9
  23.5 2.7 %shard_map.214 = (f32[394,768]{1,0:T(8,128)S(1)}, bf16[144,768]{1,0:T(8,128)(2,1)S(1)}, bf16[144,768]{1,0:T(8,128)(2,1)S(1)}, bf16[144,768]{1,0:T(8,128)(2,1)S(1)}, bf16[144,768]{1,0:T(8,128)(2,1)S(1)}) custom-call(s32[8]{0:T(128)S(1)} %stack.38.ids, bf16[394,768]{1,0:T(8,128)(2,1)S(1)} %copy-done.5, f32[768]{0:T(1024)S(1)} %copy-done.16, ...), custom_call_target="tpu_custom_call" | custom-call | flops 3449999872 | bytes 1024 | tf_op jit(solution)/shard_map/pallas_call | solution.py:415
  26.2 4.5 %collective-permute-done.8.refs_2_ = bf16[72,768]{1,0:T(8,128)(2,1)S(1)} collective-permute-done((bf16[72,768]{1,0:T(8,128)(2,1)S(1)}, bf16[72,768]{1,0:T(8,128)(2,1)S(1)}, u32[]{:S(2)}, u32[]{:S(2)}) %collective-permute-start.8) | collective-permute-done | bytes 110624 | tf_op jit(solution)/shard_map/ppermute | solution.py:435
  30.8 2.9 %collective-permute-start.10 = (bf16[144,768]{1,0:T(8,128)(2,1)S(1)}, bf16[144,768]{1,0:T(8,128)(2,1)S(1)}, u32[]{:S(2)}, u32[]{:S(2)}) collective-permute-start(bf16[144,768]{1,0:T(8,128)(2,1)S(1)} %get-tuple-element.146), channel_id=1, source_target_pairs={{0,2},{2,0},{4,6},{6,4},{1,3},{3,1},{5,7},{7,5},{8,10},{10,8},{12,... | collective-permute-start | bytes 663560 | tf_op jit(solution)/shard_map/ppermute | solution.py:435
  33.7 3.9 %collective-permute-start.12 = (bf16[144,768]{1,0:T(8,128)(2,1)S(1)}, bf16[144,768]{1,0:T(8,128)(2,1)S(1)}, u32[]{:S(2)}, u32[]{:S(2)}) collective-permute-start(bf16[144,768]{1,0:T(8,128)(2,1)S(1)} %get-tuple-element.151), channel_id=1, source_target_pairs={{0,4},{2,6},{4,0},{6,2},{1,5},{3,7},{5,1},{7,3},{8,12},{10,14},{12... | collective-permute-start | bytes 663560 | tf_op jit(solution)/shard_map/ppermute | solution.py:435
  38.0 1.6 collective-permute-start.14
  39.6 5.0 %collective-permute-done.10.refs_1_ = bf16[144,768]{1,0:T(8,128)(2,1)S(1)} collective-permute-done((bf16[144,768]{1,0:T(8,128)(2,1)S(1)}, bf16[144,768]{1,0:T(8,128)(2,1)S(1)}, u32[]{:S(2)}, u32[]{:S(2)}) %collective-permute-start.10) | collective-permute-done | bytes 221216 | tf_op jit(solution)/shard_map/ppermute | solution.py:435
  44.6 4.2 %collective-permute-done.11.refs_3_ = bf16[144,768]{1,0:T(8,128)(2,1)S(1)} collective-permute-done((bf16[144,768]{1,0:T(8,128)(2,1)S(1)}, bf16[144,768]{1,0:T(8,128)(2,1)S(1)}, u32[]{:S(2)}, u32[]{:S(2)}) %collective-permute-start.11) | collective-permute-done | bytes 221216 | tf_op jit(solution)/shard_map/ppermute | solution.py:435
  48.8 7.0 %shard_map.215 = (bf16[144,768]{1,0:T(8,128)(2,1)S(1)}, bf16[144,768]{1,0:T(8,128)(2,1)S(1)}, bf16[2,144,768]{2,1,0:T(8,128)(2,1)S(1)}, bf16[2,144,768]{2,1,0:T(...) custom-call(s32[8]{0:T(128)S(1)} %stack.38.ids, ...), custom_call_target="tpu_custom_call" | custom-call | flops 57500000 | bytes 1024 | tf_op jit(solution)/shard_map/pallas_call | solution.py:415
  55.8 0.9 collective-permute-done.13.refs_1_
  56.7 4.8 %shard_map.216 = (bf16[144,768]{1,0:T(8,128)(2,1)S(1)}, bf16[144,768]{1,0:T(8,128)(2,1)S(1)}, bf16[2,72,768]{2,1,0:T(8,128)(2,1)S(1)}, bf16[2,72,768]{2,1,0:T(8,...) custom-call(s32[8]{0:T(128)S(1)} %stack.38.ids, ...), custom_call_target="tpu_custom_call" | custom-call | flops 57500000 | bytes 1024 | tf_op jit(solution)/shard_map/pallas_call | solution.py:415
  61.5 2.7 %shard_map.218 = (bf16[1536,768]{1,0:T(8,128)(2,1)S(1)}, bf16[1536,768]{1,0:T(8,128)(2,1)S(1)}) custom-call(bf16[288,768]{1,0:T(8,128)(2,1)S(1)} %get-tuple-element.166.refs_0_, bf16[288,768]{1,0:T(8,128)(2,1)S(1)} %get-tuple-element.167.refs_1_, bf16[288,768]{1,0:T(8,128)(2,1)S(1)} %get-tuple-element.168.refs_2_, ...), custom_call_target="tpu_custom_call" | custom-call | flops 4600000000 | bytes 1024 | tf_op jit(solution)/shard_map/pallas_call | solution.py:415
  64.3 1.6 collective-permute-start.18
  65.8 3.1 %collective-permute-start.15 = (bf16[144,768]{1,0:T(8,128)(2,1)S(1)}, bf16[144,768]{1,0:T(8,128)(2,1)S(1)}, u32[]{:S(2)}, u32[]{:S(2)}) collective-permute-start(bf16[144,768]{1,0:T(8,128)(2,1)S(1)} %get-tuple-element.155), channel_id=1, source_target_pairs={{0,6},{2,4},{4,2},{6,0},{1,7},{3,5},{5,3},{7,1},{8,14},{10,12},{12... | collective-permute-start | bytes 663560 | tf_op jit(solution)/shard_map/ppermute | solution.py:435
  69.0 1.2 collective-permute-start.17
  70.2 1.6 shard_map.219
  71.9 1.6 collective-permute-start.20
  73.5 0.5 collective-permute-start.21
  74.1 2.0 %collective-permute-done.15.refs_1_ = bf16[144,768]{1,0:T(8,128)(2,1)S(1)} collective-permute-done((bf16[144,768]{1,0:T(8,128)(2,1)S(1)}, bf16[144,768]{1,0:T(8,128)(2,1)S(1)}, u32[]{:S(2)}, u32[]{:S(2)}) %collective-permute-start.15) | collective-permute-done | bytes 221216 | tf_op jit(solution)/shard_map/ppermute | solution.py:435
  76.1 11.7 %collective-permute-done.16.refs_2_ = bf16[144,768]{1,0:T(8,128)(2,1)S(1)} collective-permute-done((bf16[144,768]{1,0:T(8,128)(2,1)S(1)}, bf16[144,768]{1,0:T(8,128)(2,1)S(1)}, u32[]{:S(2)}, u32[]{:S(2)}) %collective-permute-start.16) | collective-permute-done | bytes 221216 | tf_op jit(solution)/shard_map/ppermute | solution.py:435
  87.8 1.5 shard_map.220
  89.4 1.6 collective-permute-done.22
  91.1 0.6 collective-permute-start.23
  91.7 3.0 %collective-permute-start.25 = (bf16[72,768]{1,0:T(8,128)(2,1)S(1)}, bf16[72,768]{1,0:T(8,128)(2,1)S(1)}, u32[]{:S(2)}, u32[]{:S(2)}) collective-permute-start(bf16[72,768]{1,0:T(8,128)(2,1)S(1)} %get-tuple-element.188), channel_id=1, source_target_pairs={{0,4},{2,6},{4,0},{6,2},{1,5},{3,7},{5,1},{7,3},{8,12},{10,14},{12... | collective-permute-start | bytes 331784 | tf_op jit(solution)/shard_map/ppermute | solution.py:435
  94.6 1.4 collective-permute-start.26
  96.0 4.7 %collective-permute-done.23 = bf16[416,384]{1,0:T(8,128)(2,1)S(1)} collective-permute-done((bf16[416,384]{1,0:T(8,128)(2,1)S(1)}, bf16[416,384]{1,0:T(8,128)(2,1)S(1)}, u32[]{:S(2)}, u32[]{:S(2)}) %collective-permute-start.23) | collective-permute-done | bytes 319520 | tf_op jit(solution)/shard_map/ppermute | solution.py:432
  100.8 3.5 %collective-permute-done.26.refs_1_ = bf16[72,768]{1,0:T(8,128)(2,1)S(1)} collective-permute-done((bf16[72,768]{1,0:T(8,128)(2,1)S(1)}, bf16[72,768]{1,0:T(8,128)(2,1)S(1)}, u32[]{:S(2)}, u32[]{:S(2)}) %collective-permute-start.26) | collective-permute-done | bytes 110624 | tf_op jit(solution)/shard_map/ppermute | solution.py:435
  104.4 1.6 collective-permute-done.27.other
  106.0 5.0 %shard_map.221 = (f32[394,768]{1,0:T(8,128)S(1)}, bf16[394,384]{1,0:T(8,128)(2,1)S(1)}, bf16[394,384]{1,0:T(8,128)(2,1)S(1)}, f32[16,768]{1,0:T(8,128)S(1)}, bf1...) custom-call(s32[8]{0:T(128)S(1)} %stack.38.ids, ...), custom_call_target="tpu_custom_call" | custom-call | flops 6899999744 | bytes 1024 | tf_op jit(solution)/shard_map/pallas_call | solution.py:415
  111.1 1.8 %collective-permute-start.30 = (bf16[192,768]{1,0:T(8,128)(2,1)S(1)}, bf16[192,768]{1,0:T(8,128)(2,1)S(1)}, u32[]{:S(2)}, u32[]{:S(2)}) collective-permute-start(bf16[192,768]{1,0:T(8,128)(2,1)S(1)} %get-tuple-element.211), channel_id=1, source_target_pairs={{0,3},{1,2},{2,1},{3,0},{4,7},{5,6},{6,5},{7,4},{8,11},{9,10},{10,... | collective-permute-start | bytes 884744 | tf_op jit(solution)/shard_map/ppermute | solution.py:442
  112.9 0.5 collective-permute-start.31
  113.4 1.2 collective-permute-start.32
  114.6 1.4 shard_map.222
  116.3 1.6 collective-permute-start.35
  117.8 4.1 %collective-permute-done.30.refs_1_ = bf16[192,768]{1,0:T(8,128)(2,1)S(1)} collective-permute-done((bf16[192,768]{1,0:T(8,128)(2,1)S(1)}, bf16[192,768]{1,0:T(8,128)(2,1)S(1)}, u32[]{:S(2)}, u32[]{:S(2)}) %collective-permute-start.30) | collective-permute-done | bytes 294944 | tf_op jit(solution)/shard_map/ppermute | solution.py:442
  121.9 5.7 %collective-permute-done.31.refs_2_ = bf16[192,768]{1,0:T(8,128)(2,1)S(1)} collective-permute-done((bf16[192,768]{1,0:T(8,128)(2,1)S(1)}, bf16[192,768]{1,0:T(8,128)(2,1)S(1)}, u32[]{:S(2)}, u32[]{:S(2)}) %collective-permute-start.31) | collective-permute-done | bytes 294944 | tf_op jit(solution)/shard_map/ppermute | solution.py:442
  128.0 1.6 collective-permute-start.29
  129.7 1.8 %collective-permute-start.33 = (bf16[192,768]{1,0:T(8,128)(2,1)S(1)}, bf16[192,768]{1,0:T(8,128)(2,1)S(1)}, u32[]{:S(2)}, u32[]{:S(2)}) collective-permute-start(bf16[192,768]{1,0:T(8,128)(2,1)S(1)} %shard_map.223.own), channel_id=1, source_target_pairs={{0,4},{2,6},{4,0},{6,2},{1,5},{3,7},{5,1},{7,3},{8,12},{10,14},{12... | collective-permute-start | bytes 884744 | tf_op jit(solution)/shard_map/ppermute | solution.py:435
  131.5 0.7 collective-permute-start.39
  132.2 2.4 %shard_map.224 = (bf16[394,768]{1,0:T(8,128)(2,1)}, f32[16,768]{1,0:T(8,128)S(1)}) custom-call(s32[8]{0:T(128)S(1)} %stack.38.ids, bf16[394,384]{1,0:T(8,128)(2,1)S(1)} %add_convert_fusion.2.own, bf16[394,384]{1,0:T(8,128)(2,1)S(1)} %collective-permute-done.36.other, bf16[394,768]{1,0:T(8,128)(2,1)S(1)} %copy-done.5, ...), custom_call_target="tpu_custom_call" | custom-call | flops 11500000 | bytes 1024 | tf_op jit(solution)/shard_map/pallas_call | solution.py:415
  134.6 1.5 collective-permute-start.37
  136.1 1.1 collective-permute-done.29
  137.2 0.8 add_convert_fusion.4
  138.0 9.8 %collective-permute-done.33.came = bf16[192,768]{1,0:T(8,128)(2,1)S(1)} collective-permute-done((bf16[192,768]{1,0:T(8,128)(2,1)S(1)}, bf16[192,768]{1,0:T(8,128)(2,1)S(1)}, u32[]{:S(2)}, u32[]{:S(2)}) %collective-permute-start.33) | collective-permute-done | bytes 294944 | tf_op jit(solution)/shard_map/ppermute | solution.py:435
  147.8 0.7 collective-permute-done.37.small_came
  148.8 1.0 collective-permute-start.41
  149.8 2.4 %collective-permute-start.42 = (bf16[208,768]{1,0:T(8,128)(2,1)S(1)}, bf16[208,768]{1,0:T(8,128)(2,1)S(1)}, u32[]{:S(2)}, u32[]{:S(2)}) collective-permute-start(bf16[208,768]{1,0:T(8,128)(2,1)S(1)} %shard_map.225.refs_0_), channel_id=1, source_target_pairs={{0,2},{1,3},{2,0},{3,1},{4,6},{5,7},{6,4},{7,5},{8,10},{9,11},{10,... | collective-permute-start | bytes 958472 | tf_op jit(solution)/shard_map/ppermute | solution.py:442
  152.2 2.3 %select_convert_fusion = bf16[394,768]{1,0:T(8,128)(2,1)} fusion(f32[394,768]{1,0:T(8,128)S(1)} %copy-done.3, bf16[400,384]{1,0:T(8,128)(2,1)} %collective-permute-done.38, bf16[400,384]{1,0:T(8,128)(2,1)} %add_convert_fusion.4, pred[394]{0:T(512)(128)(4,1)S(1)} %iota_compare_fusion, pred[]{:T(512)S(6)} %eq.7), kind=kLoop, calls=%fused_computation | loop fusion | flops 3933696 | bytes 2430347 | tf_op jit(solution)/shard_map/convert_element_type | solution.py:721
  154.6 1.7 %shard_map.226 = (f32[384,768]{1,0:T(8,128)}, f32[768,384]{1,0:T(8,128)}) custom-call(f32[768,768]{1,0:T(8,128)S(1)} %copy-done.18, bf16[128,768]{1,0:T(8,128)(2,1)S(1)} %collective-permute-done.20.came_first, bf16[128,768]{1,0:T(8,128)(2,1)S(1)} %collective-permute-done.21.came_next, bf16[512,768]{1,0:T(8,128)(2,1)S(1)} %collective-permute-done.39.came_rest), custom_call_target="tpu_custom_call" | custom-call | flops 2300000000 | bytes 1024 | tf_op jit(solution)/shard_map/pallas_call | solution.py:415
  156.3 3.8 %collective-permute-done.40.refs_1_ = bf16[208,768]{1,0:T(8,128)(2,1)S(1)} collective-permute-done((bf16[208,768]{1,0:T(8,128)(2,1)S(1)}, bf16[208,768]{1,0:T(8,128)(2,1)S(1)}, u32[]{:S(2)}, u32[]{:S(2)}) %collective-permute-start.40) | collective-permute-done | bytes 319520 | tf_op jit(solution)/shard_map/ppermute | solution.py:442
  160.0 5.5 %collective-permute-done.41.refs_2_ = bf16[208,768]{1,0:T(8,128)(2,1)S(1)} collective-permute-done((bf16[208,768]{1,0:T(8,128)(2,1)S(1)}, bf16[208,768]{1,0:T(8,128)(2,1)S(1)}, u32[]{:S(2)}, u32[]{:S(2)}) %collective-permute-start.41) | collective-permute-done | bytes 319520 | tf_op jit(solution)/shard_map/ppermute | solution.py:442
  165.9 2.2 %shard_map.227 = (f32[576,768]{1,0:T(8,128)}, f32[192,768]{1,0:T(8,128)}, f32[768]{0:T(1024)}, f32[768]{0:T(1024)}, f32[768]{0:T(1024)}, /*index=5*/f32[768]{0:T(1024)}, f32[4,768]{1,0:T(4,128)}) custom-call(s32[8]{0:T(128)S(1)} %stack.38.ids, bf16[208,768]{1,0:T(8,128)(2,1)S(1)} %shard_map.225.refs_0_, ...), custom_call_target="tpu_custom_call" | custom-call | flops 3449999872 | bytes 1024 | tf_op jit(solution)/shard_map/pallas_call | solution.py:415
  (87 shorter events, 2.9 us)
Async XLA Ops:
  0.6 11.0 %collective-permute-start.2 = (bf16[768,768]{1,0:T(8,128)(2,1)}, bf16[768,768]{1,0:T(8,128)(2,1)S(1)}, u32[]{:S(2)}, u32[]{:S(2)}) collective-permute-start(bf16[768,768]{1,0:T(8,128)(2,1)} %bitcast.26), channel_id=1, source_target_pairs={{0,8},{8,0},{16,24},{24,16},{1,9},{9,1},{17,25},{25,17},{2,10},{10... | collective-permute-start | bytes 3538952 | tf_op jit(solution)/shard_map/ppermute | solution.py:432
  1.2 10.5 %collective-permute-start.3 = (bf16[768,768]{1,0:T(8,128)(2,1)}, bf16[768,768]{1,0:T(8,128)(2,1)S(1)}, u32[]{:S(2)}, u32[]{:S(2)}) collective-permute-start(bf16[768,768]{1,0:T(8,128)(2,1)} %bitcast.29), channel_id=1, source_target_pairs={{0,8},{8,0},{16,24},{24,16},{1,9},{9,1},{17,25},{25,17},{2,10},{10... | collective-permute-start | bytes 3538952 | tf_op jit(solution)/shard_map/ppermute | solution.py:432
  1.2 10.4 %collective-permute-start = (bf16[192,768]{1,0:T(8,128)(2,1)}, bf16[192,768]{1,0:T(8,128)(2,1)S(1)}, u32[]{:S(2)}, u32[]{:S(2)}) collective-permute-start(bf16[192,768]{1,0:T(8,128)(2,1)} %w_out.1), channel_id=1, source_target_pairs={{0,16},{8,24},{16,0},{24,8},{1,17},{9,25},{17,1},{25,9},{2,18},{10... | collective-permute-start | bytes 884744 | tf_op jit(solution)/shard_map/ppermute | solution.py:432
  4.2 7.5 %collective-permute-start.1 = (bf16[192,768]{1,0:T(8,128)(2,1)}, bf16[192,768]{1,0:T(8,128)(2,1)S(1)}, u32[]{:S(2)}, u32[]{:S(2)}) collective-permute-start(bf16[192,768]{1,0:T(8,128)(2,1)} %w_out.1), channel_id=1, source_target_pairs={{0,8},{8,0},{16,24},{24,16},{1,9},{9,1},{17,25},{25,17},{2,10},{10... | collective-permute-start | bytes 884744 | tf_op jit(solution)/shard_map/ppermute | solution.py:432
  4.9 1.1 copy-start.4
  6.0 0.7 copy-start.6
  6.7 1.2 copy-start.8
  7.8 0.7 copy-start.13
  8.5 5.2 %copy-start.10 = (bf16[394,768]{1,0:T(8,128)(2,1)S(1)}, bf16[394,768]{1,0:T(8,128)(2,1)}, u32[]{:S(2)}) copy-start(bf16[394,768]{1,0:T(8,128)(2,1)} %cot.3) | copy-start | bytes 1815556
  8.5 5.2 %copy-start.12 = (bf16[768,4]{0,1:T(4,128)(2,1)S(1)}, bf16[768,4]{0,1:T(4,128)(2,1)}, u32[]{:S(2)}) copy-start(bf16[768,4]{0,1:T(4,128)(2,1)} %param.22) | copy-start | bytes 18436
  8.5 5.2 %copy-start.14 = (s32[394,2]{0,1:T(2,128)S(1)}, s32[394,2]{0,1:T(2,128)}, u32[]{:S(2)}) copy-start(s32[394,2]{0,1:T(2,128)} %param.14) | copy-start | bytes 9460
  11.6 11.8 %collective-permute-start.4 = (bf16[394,192]{1,0:T(8,128)(2,1)S(1)}, bf16[394,192]{1,0:T(8,128)(2,1)S(1)}, u32[]{:S(2)}, u32[]{:S(2)}) collective-permute-start(bf16[394,192]{1,0:T(8,128)(2,1)S(1)} %get-tuple-element.126.rest_0_.head_out), channel_id=1, source_target_pairs={{0,8},{8,0},{16,24},{24,16},{1,9},{9,1},{17,25},{25,17},{2,10},{10... | collective-permute-start | bytes 453896 | tf_op jit(solution)/shard_map/ppermute | solution.py:432
  11.7 7.5 %collective-permute-start.5 = (bf16[394,192]{1,0:T(8,128)(2,1)S(1)}, bf16[394,192]{1,0:T(8,128)(2,1)S(1)}, u32[]{:S(2)}, u32[]{:S(2)}) collective-permute-start(bf16[394,192]{1,0:T(8,128)(2,1)S(1)} %get-tuple-element.126.rest_0_.head_out), channel_id=1, source_target_pairs={{0,16},{8,24},{16,0},{24,8},{1,17},{9,25},{17,1},{25,9},{2,18},{10... | collective-permute-start | bytes 453896 | tf_op jit(solution)/shard_map/ppermute | solution.py:432
  13.5 9.9 %collective-permute-start.7 = (bf16[192,768]{1,0:T(8,128)(2,1)S(1)}, bf16[192,768]{1,0:T(8,128)(2,1)S(1)}, u32[]{:S(2)}, u32[]{:S(2)}) collective-permute-start(bf16[192,768]{1,0:T(8,128)(2,1)S(1)} %collective-permute-done.rest_6_), channel_id=1, source_target_pairs={{0,8},{8,0},{16,24},{24,16},{1,9},{9,1},{17,25},{25,17},{2,10},{10... | collective-permute-start | bytes 884744 | tf_op jit(solution)/shard_map/ppermute | solution.py:432
  13.7 9.7 %copy-start.5 = (bf16[394,768]{1,0:T(8,128)(2,1)S(1)}, bf16[394,768]{1,0:T(8,128)(2,1)}, u32[]{:S(2)}) copy-start(bf16[394,768]{1,0:T(8,128)(2,1)} %tokens.5) | copy-start | bytes 1815556
  13.7 9.7 %copy-start.11 = (bf16[192,768]{1,0:T(8,128)(2,1)S(1)}, bf16[192,768]{1,0:T(8,128)(2,1)}, u32[]{:S(2)}) copy-start(bf16[192,768]{1,0:T(8,128)(2,1)} %w_out.1) | copy-start | bytes 884740
  13.7 9.7 %copy-start.15 = (f32[768]{0:T(1024)S(1)}, f32[768]{0:T(1024)}, u32[]{:S(2)}) copy-start(f32[768]{0:T(1024)} %bias.3) | copy-start | bytes 9220
  13.7 9.7 %copy-start.16 = (f32[768]{0:T(1024)S(1)}, f32[768]{0:T(1024)}, u32[]{:S(2)}) copy-start(f32[768]{0:T(1024)} %gain.6) | copy-start | bytes 9220
  19.2 4.2 %collective-permute-start.6 = (bf16[394,192]{1,0:T(8,128)(2,1)S(1)}, bf16[394,192]{1,0:T(8,128)(2,1)S(1)}, u32[]{:S(2)}, u32[]{:S(2)}) collective-permute-start(bf16[394,192]{1,0:T(8,128)(2,1)S(1)} %collective-permute-done.5.rest_2_), channel_id=1, source_target_pairs={{0,8},{8,0},{16,24},{24,16},{1,9},{9,1},{17,25},{25,17},{2,10},{10... | collective-permute-start | bytes 453896 | tf_op jit(solution)/shard_map/ppermute | solution.py:432
  19.2 11.6 %collective-permute-start.8 = (bf16[72,768]{1,0:T(8,128)(2,1)S(1)}, bf16[72,768]{1,0:T(8,128)(2,1)S(1)}, u32[]{:S(2)}, u32[]{:S(2)}) collective-permute-start(bf16[72,768]{1,0:T(8,128)(2,1)S(1)} %get-tuple-element.143), channel_id=1, source_target_pairs={{0,4},{2,6},{4,0},{6,2},{1,5},{3,7},{5,1},{7,3},{8,12},{10,14},{12... | collective-permute-start | bytes 331784 | tf_op jit(solution)/shard_map/ppermute | solution.py:435
  22.0 8.7 %collective-permute-start.9 = (bf16[72,768]{1,0:T(8,128)(2,1)S(1)}, bf16[72,768]{1,0:T(8,128)(2,1)S(1)}, u32[]{:S(2)}, u32[]{:S(2)}) collective-permute-start(bf16[72,768]{1,0:T(8,128)(2,1)S(1)} %get-tuple-element.144), channel_id=1, source_target_pairs={{0,6},{2,4},{4,2},{6,0},{1,7},{3,5},{5,3},{7,1},{8,14},{10,12},{12... | collective-permute-start | bytes 331784 | tf_op jit(solution)/shard_map/ppermute | solution.py:435
  23.4 25.3 %copy-start = (bf16[1,768,768]{2,1,0:T(8,128)(2,1)S(1)}, bf16[1,768,768]{2,1,0:T(8,128)(2,1)}, u32[]{:S(2)}) copy-start(bf16[1,768,768]{2,1,0:T(8,128)(2,1)} %param.23) | copy-start | bytes 3538948
  23.5 25.3 %copy-start.1 = (bf16[1,768,768]{2,1,0:T(8,128)(2,1)S(1)}, bf16[1,768,768]{2,1,0:T(8,128)(2,1)}, u32[]{:S(2)}) copy-start(bf16[1,768,768]{2,1,0:T(8,128)(2,1)} %param.24) | copy-start | bytes 3538948
  26.2 79.7 %copy-start.2 = (f32[394,768]{1,0:T(8,128)}, f32[394,768]{1,0:T(8,128)S(1)}, u32[]{:S(2)}) copy-start(f32[394,768]{1,0:T(8,128)S(1)} %get-tuple-element.134.middle) | copy-start | bytes 3631108
  30.8 13.8 %collective-permute-start.10 = (bf16[144,768]{1,0:T(8,128)(2,1)S(1)}, bf16[144,768]{1,0:T(8,128)(2,1)S(1)}, u32[]{:S(2)}, u32[]{:S(2)}) collective-permute-start(bf16[144,768]{1,0:T(8,128)(2,1)S(1)} %get-tuple-element.146), channel_id=1, source_target_pairs={{0,2},{2,0},{4,6},{6,4},{1,3},{3,1},{5,7},{7,5},{8,10},{10,8},{12,... | collective-permute-start | bytes 663560 | tf_op jit(solution)/shard_map/ppermute | solution.py:435
  33.6 15.1 %collective-permute-start.11 = (bf16[144,768]{1,0:T(8,128)(2,1)S(1)}, bf16[144,768]{1,0:T(8,128)(2,1)S(1)}, u32[]{:S(2)}, u32[]{:S(2)}) collective-permute-start(bf16[144,768]{1,0:T(8,128)(2,1)S(1)} %get-tuple-element.148), channel_id=1, source_target_pairs={{0,2},{2,0},{4,6},{6,4},{1,3},{3,1},{5,7},{7,5},{8,10},{10,8},{12,... | collective-permute-start | bytes 663560 | tf_op jit(solution)/shard_map/ppermute | solution.py:435
  33.7 22.1 %collective-permute-start.12 = (bf16[144,768]{1,0:T(8,128)(2,1)S(1)}, bf16[144,768]{1,0:T(8,128)(2,1)S(1)}, u32[]{:S(2)}, u32[]{:S(2)}) collective-permute-start(bf16[144,768]{1,0:T(8,128)(2,1)S(1)} %get-tuple-element.151), channel_id=1, source_target_pairs={{0,4},{2,6},{4,0},{6,2},{1,5},{3,7},{5,1},{7,3},{8,12},{10,14},{12... | collective-permute-start | bytes 663560 | tf_op jit(solution)/shard_map/ppermute | solution.py:435
  37.6 19.1 %collective-permute-start.13 = (bf16[144,768]{1,0:T(8,128)(2,1)S(1)}, bf16[144,768]{1,0:T(8,128)(2,1)S(1)}, u32[]{:S(2)}, u32[]{:S(2)}) collective-permute-start(bf16[144,768]{1,0:T(8,128)(2,1)S(1)} %get-tuple-element.152), channel_id=1, source_target_pairs={{0,6},{2,4},{4,2},{6,0},{1,7},{3,5},{5,3},{7,1},{8,14},{10,12},{12... | collective-permute-start | bytes 663560 | tf_op jit(solution)/shard_map/ppermute | solution.py:435
  38.0 18.7 %collective-permute-start.14 = (bf16[2,72,768]{2,1,0:T(8,128)(2,1)S(1)}, bf16[2,72,768]{2,1,0:T(8,128)(2,1)S(1)}, u32[]{:S(2)}, u32[]{:S(2)}) collective-permute-start(bf16[2,72,768]{2,1,0:T(8,128)(2,1)S(1)} %pad_maximum_fusion.2), channel_id=1, source_target_pairs={{0,16},{8,24},{16,0},{24,8},{1,17},{9,25},{17,1},{25,9},{2,18},{10... | collective-permute-start | bytes 663560 | tf_op jit(solution)/shard_map/ppermute | solution.py:432
  64.2 6.0 %collective-permute-start.19 = (bf16[1536,768]{1,0:T(8,128)(2,1)S(1)}, bf16[1536,768]{1,0:T(8,128)(2,1)S(1)}, u32[]{:S(2)}, u32[]{:S(2)}) collective-permute-start(bf16[1536,768]{1,0:T(8,128)(2,1)S(1)} %get-tuple-element.175), channel_id=1, source_target_pairs={{0,8},{8,0},{16,24},{24,16},{1,9},{9,1},{17,25},{25,17},{2,10},{10... | collective-permute-start | bytes 7077896 | tf_op jit(solution)/shard_map/ppermute | solution.py:432
  64.3 9.2 %collective-permute-start.18 = (bf16[2,72,768]{2,1,0:T(8,128)(2,1)S(1)}, bf16[2,72,768]{2,1,0:T(8,128)(2,1)S(1)}, u32[]{:S(2)}, u32[]{:S(2)}) collective-permute-start(bf16[2,72,768]{2,1,0:T(8,128)(2,1)S(1)} %get-tuple-element.163), channel_id=1, source_target_pairs={{0,16},{8,24},{16,0},{24,8},{1,17},{9,25},{17,1},{25,9},{2,18},{10... | collective-permute-start | bytes 663560 | tf_op jit(solution)/shard_map/ppermute | solution.py:432
  65.8 10.2 %collective-permute-start.15 = (bf16[144,768]{1,0:T(8,128)(2,1)S(1)}, bf16[144,768]{1,0:T(8,128)(2,1)S(1)}, u32[]{:S(2)}, u32[]{:S(2)}) collective-permute-start(bf16[144,768]{1,0:T(8,128)(2,1)S(1)} %get-tuple-element.155), channel_id=1, source_target_pairs={{0,6},{2,4},{4,2},{6,0},{1,7},{3,5},{5,3},{7,1},{8,14},{10,12},{12... | collective-permute-start | bytes 663560 | tf_op jit(solution)/shard_map/ppermute | solution.py:435
  69.0 18.8 %collective-permute-start.16 = (bf16[144,768]{1,0:T(8,128)(2,1)S(1)}, bf16[144,768]{1,0:T(8,128)(2,1)S(1)}, u32[]{:S(2)}, u32[]{:S(2)}) collective-permute-start(bf16[144,768]{1,0:T(8,128)(2,1)S(1)} %get-tuple-element.158), channel_id=1, source_target_pairs={{0,4},{2,6},{4,0},{6,2},{1,5},{3,7},{5,1},{7,3},{8,12},{10,14},{12... | collective-permute-start | bytes 663560 | tf_op jit(solution)/shard_map/ppermute | solution.py:435
  69.0 18.8 %collective-permute-start.17 = (bf16[144,768]{1,0:T(8,128)(2,1)S(1)}, bf16[144,768]{1,0:T(8,128)(2,1)S(1)}, u32[]{:S(2)}, u32[]{:S(2)}) collective-permute-start(bf16[144,768]{1,0:T(8,128)(2,1)S(1)} %get-tuple-element.159), channel_id=1, source_target_pairs={{0,2},{2,0},{4,6},{6,4},{1,3},{3,1},{5,7},{7,5},{8,10},{10,8},{12,... | collective-permute-start | bytes 663560 | tf_op jit(solution)/shard_map/ppermute | solution.py:435
  71.9 2.2 %copy-start.17 = (f32[768,768]{1,0:T(8,128)}, f32[768,768]{1,0:T(8,128)S(1)}, u32[]{:S(2)}) copy-start(f32[768,768]{1,0:T(8,128)S(1)} %get-tuple-element.223.kept) | copy-start | bytes 7077892
  71.9 15.9 %collective-permute-start.20 = (bf16[128,768]{1,0:T(8,128)(2,1)S(1)}, bf16[128,768]{1,0:T(8,128)(2,1)S(1)}, u32[]{:S(2)}, u32[]{:S(2)}) collective-permute-start(bf16[128,768]{1,0:T(8,128)(2,1)S(1)} %get-tuple-element.176), channel_id=1, source_target_pairs={{0,1},{1,0},{2,3},{3,2},{4,5},{5,4},{6,7},{7,6},{8,9},{9,8},{10,11... | collective-permute-start | bytes 589832 | tf_op jit(solution)/shard_map/ppermute | solution.py:438
  73.5 14.3 %collective-permute-start.21 = (bf16[128,768]{1,0:T(8,128)(2,1)S(1)}, bf16[128,768]{1,0:T(8,128)(2,1)S(1)}, u32[]{:S(2)}, u32[]{:S(2)}) collective-permute-start(bf16[128,768]{1,0:T(8,128)(2,1)S(1)} %get-tuple-element.177), channel_id=1, source_target_pairs={{0,1},{1,0},{2,3},{3,2},{4,5},{5,4},{6,7},{7,6},{8,9},{9,8},{10,11... | collective-permute-start | bytes 589832 | tf_op jit(solution)/shard_map/ppermute | solution.py:438
  89.3 16.7 %copy-start.9 = (bf16[768,3,192]{0,2,1:T(8,128)(2,1)S(1)}, bf16[768,3,192]{0,2,1:T(8,128)(2,1)}, u32[]{:S(2)}) copy-start(bf16[768,3,192]{0,2,1:T(8,128)(2,1)} %param.18) | copy-start | bytes 2654212
  89.3 1.7 %collective-permute-start.22 = (bf16[416,384]{1,0:T(8,128)(2,1)S(1)}, bf16[416,384]{1,0:T(8,128)(2,1)S(1)}, u32[]{:S(2)}, u32[]{:S(2)}) collective-permute-start(bf16[416,384]{1,0:T(8,128)(2,1)S(1)} %get-tuple-element.185), channel_id=1, source_target_pairs={{0,8},{8,0},{16,24},{24,16},{1,9},{9,1},{17,25},{25,17},{2,10},{10... | collective-permute-start | bytes 958472 | tf_op jit(solution)/shard_map/ppermute | solution.py:432
  91.1 9.6 %collective-permute-start.23 = (bf16[416,384]{1,0:T(8,128)(2,1)S(1)}, bf16[416,384]{1,0:T(8,128)(2,1)S(1)}, u32[]{:S(2)}, u32[]{:S(2)}) collective-permute-start(bf16[416,384]{1,0:T(8,128)(2,1)S(1)} %add_convert_fusion.1), channel_id=1, source_target_pairs={{0,16},{8,24},{16,0},{24,8},{1,17},{9,25},{17,1},{25,9},{2,18},{10... | collective-permute-start | bytes 958472 | tf_op jit(solution)/shard_map/ppermute | solution.py:432
  91.7 12.7 %collective-permute-start.24 = (bf16[144,768]{1,0:T(8,128)(2,1)S(1)}, bf16[144,768]{1,0:T(8,128)(2,1)S(1)}, u32[]{:S(2)}, u32[]{:S(2)}) collective-permute-start(bf16[144,768]{1,0:T(8,128)(2,1)S(1)} %get-tuple-element.187), channel_id=1, source_target_pairs={{0,2},{2,0},{4,6},{6,4},{1,3},{3,1},{5,7},{7,5},{8,10},{10,8},{12,... | collective-permute-start | bytes 663560 | tf_op jit(solution)/shard_map/ppermute | solution.py:435
  91.7 9.1 %collective-permute-start.25 = (bf16[72,768]{1,0:T(8,128)(2,1)S(1)}, bf16[72,768]{1,0:T(8,128)(2,1)S(1)}, u32[]{:S(2)}, u32[]{:S(2)}) collective-permute-start(bf16[72,768]{1,0:T(8,128)(2,1)S(1)} %get-tuple-element.188), channel_id=1, source_target_pairs={{0,4},{2,6},{4,0},{6,2},{1,5},{3,7},{5,1},{7,3},{8,12},{10,14},{12... | collective-permute-start | bytes 331784 | tf_op jit(solution)/shard_map/ppermute | solution.py:435
  94.6 9.7 %collective-permute-start.26 = (bf16[72,768]{1,0:T(8,128)(2,1)S(1)}, bf16[72,768]{1,0:T(8,128)(2,1)S(1)}, u32[]{:S(2)}, u32[]{:S(2)}) collective-permute-start(bf16[72,768]{1,0:T(8,128)(2,1)S(1)} %get-tuple-element.189), channel_id=1, source_target_pairs={{0,6},{2,4},{4,2},{6,0},{1,7},{3,5},{5,3},{7,1},{8,14},{10,12},{12... | collective-permute-start | bytes 331784 | tf_op jit(solution)/shard_map/ppermute | solution.py:435
  104.3 1.6 collective-permute-start.27
  110.9 5.2 %collective-permute-start.34 = (bf16[394,384]{1,0:T(8,128)(2,1)S(1)}, bf16[394,384]{1,0:T(8,128)(2,1)S(1)}, u32[]{:S(2)}, u32[]{:S(2)}) collective-permute-start(bf16[394,384]{1,0:T(8,128)(2,1)S(1)} %get-tuple-element.216), channel_id=1, source_target_pairs={{0,8},{8,0},{16,24},{24,16},{1,9},{9,1},{17,25},{25,17},{2,10},{10... | collective-permute-start | bytes 907784 | tf_op jit(solution)/shard_map/ppermute | solution.py:432
  111.1 10.8 %collective-permute-start.30 = (bf16[192,768]{1,0:T(8,128)(2,1)S(1)}, bf16[192,768]{1,0:T(8,128)(2,1)S(1)}, u32[]{:S(2)}, u32[]{:S(2)}) collective-permute-start(bf16[192,768]{1,0:T(8,128)(2,1)S(1)} %get-tuple-element.211), channel_id=1, source_target_pairs={{0,3},{1,2},{2,1},{3,0},{4,7},{5,6},{6,5},{7,4},{8,11},{9,10},{10,... | collective-permute-start | bytes 884744 | tf_op jit(solution)/shard_map/ppermute | solution.py:442
  112.9 14.7 %collective-permute-start.31 = (bf16[192,768]{1,0:T(8,128)(2,1)S(1)}, bf16[192,768]{1,0:T(8,128)(2,1)S(1)}, u32[]{:S(2)}, u32[]{:S(2)}) collective-permute-start(bf16[192,768]{1,0:T(8,128)(2,1)S(1)} %get-tuple-element.212), channel_id=1, source_target_pairs={{0,1},{1,0},{2,3},{3,2},{4,5},{5,4},{6,7},{7,6},{8,9},{9,8},{10,11... | collective-permute-start | bytes 884744 | tf_op jit(solution)/shard_map/ppermute | solution.py:442
  113.4 14.3 %collective-permute-start.32 = (bf16[192,768]{1,0:T(8,128)(2,1)S(1)}, bf16[192,768]{1,0:T(8,128)(2,1)S(1)}, u32[]{:S(2)}, u32[]{:S(2)}) collective-permute-start(bf16[192,768]{1,0:T(8,128)(2,1)S(1)} %get-tuple-element.213), channel_id=1, source_target_pairs={{0,2},{1,3},{2,0},{3,1},{4,6},{5,7},{6,4},{7,5},{8,10},{9,11},{10,... | collective-permute-start | bytes 884744 | tf_op jit(solution)/shard_map/ppermute | solution.py:442
  116.1 11.8 %collective-permute-start.28 = (bf16[400,384]{1,0:T(8,128)(2,1)S(1)}, bf16[400,384]{1,0:T(8,128)(2,1)S(1)}, u32[]{:S(2)}, u32[]{:S(2)}) collective-permute-start(bf16[400,384]{1,0:T(8,128)(2,1)S(1)} %get-tuple-element.209), channel_id=1, source_target_pairs={{0,8},{8,0},{16,24},{24,16},{1,9},{9,1},{17,25},{25,17},{2,10},{10... | collective-permute-start | bytes 921608 | tf_op jit(solution)/shard_map/ppermute | solution.py:432
  116.3 13.3 %collective-permute-start.35 = (bf16[394,384]{1,0:T(8,128)(2,1)S(1)}, bf16[394,384]{1,0:T(8,128)(2,1)S(1)}, u32[]{:S(2)}, u32[]{:S(2)}) collective-permute-start(bf16[394,384]{1,0:T(8,128)(2,1)S(1)} %add_convert_fusion.3), channel_id=1, source_target_pairs={{0,16},{8,24},{16,0},{24,8},{1,17},{9,25},{17,1},{25,9},{2,18},{10... | collective-permute-start | bytes 907784 | tf_op jit(solution)/shard_map/ppermute | solution.py:432
  127.9 4.3 %copy-start.7 = (f32[768]{0:T(1024)S(1)}, f32[768]{0:T(1024)}, u32[]{:S(2)}) copy-start(f32[768]{0:T(1024)} %gain.7) | copy-start | bytes 9220
  128.0 9.2 %collective-permute-start.29 = (bf16[400,384]{1,0:T(8,128)(2,1)S(1)}, bf16[400,384]{1,0:T(8,128)(2,1)S(1)}, u32[]{:S(2)}, u32[]{:S(2)}) collective-permute-start(bf16[400,384]{1,0:T(8,128)(2,1)S(1)} %add_convert_fusion.5), channel_id=1, source_target_pairs={{0,16},{8,24},{16,0},{24,8},{1,17},{9,25},{17,1},{25,9},{2,18},{10... | collective-permute-start | bytes 921608 | tf_op jit(solution)/shard_map/ppermute | solution.py:432
  129.7 2.5 %collective-permute-start.36 = (bf16[394,384]{1,0:T(8,128)(2,1)S(1)}, bf16[394,384]{1,0:T(8,128)(2,1)S(1)}, u32[]{:S(2)}, u32[]{:S(2)}) collective-permute-start(bf16[394,384]{1,0:T(8,128)(2,1)S(1)} %add_convert_fusion.2.own), channel_id=1, source_target_pairs={{0,8},{8,0},{16,24},{24,16},{1,9},{9,1},{17,25},{25,17},{2,10},{10... | collective-permute-start | bytes 907784 | tf_op jit(solution)/shard_map/ppermute | solution.py:432
  129.7 18.0 %collective-permute-start.33 = (bf16[192,768]{1,0:T(8,128)(2,1)S(1)}, bf16[192,768]{1,0:T(8,128)(2,1)S(1)}, u32[]{:S(2)}, u32[]{:S(2)}) collective-permute-start(bf16[192,768]{1,0:T(8,128)(2,1)S(1)} %shard_map.223.own), channel_id=1, source_target_pairs={{0,4},{2,6},{4,0},{6,2},{1,5},{3,7},{5,1},{7,3},{8,12},{10,14},{12... | collective-permute-start | bytes 884744 | tf_op jit(solution)/shard_map/ppermute | solution.py:435
  131.5 23.1 %collective-permute-start.39 = (bf16[512,768]{1,0:T(8,128)(2,1)S(1)}, bf16[512,768]{1,0:T(8,128)(2,1)S(1)}, u32[]{:S(2)}, u32[]{:S(2)}) collective-permute-start(bf16[512,768]{1,0:T(8,128)(2,1)S(1)} %get-tuple-element.226), channel_id=1, source_target_pairs={{0,1},{1,0},{2,3},{3,2},{4,5},{5,4},{6,7},{7,6},{8,9},{9,8},{10,11... | collective-permute-start | bytes 2359304 | tf_op jit(solution)/shard_map/ppermute | solution.py:438
  134.6 13.9 %collective-permute-start.37 = (f32[16,768]{1,0:T(8,128)S(1)}, f32[16,768]{1,0:T(8,128)S(1)}, u32[]{:S(2)}, u32[]{:S(2)}) collective-permute-start(f32[16,768]{1,0:T(8,128)S(1)} %get-tuple-element.219.small), channel_id=1, source_target_pairs={{0,4},{2,6},{4,0},{6,2},{1,5},{3,7},{5,1},{7,3},{8,12},{10,14},{12... | collective-permute-start | bytes 147464 | tf_op jit(solution)/shard_map/ppermute | solution.py:435
  138.0 14.3 %copy-start.3 = (f32[394,768]{1,0:T(8,128)S(1)}, f32[394,768]{1,0:T(8,128)}, u32[]{:S(2)}) copy-start(f32[394,768]{1,0:T(8,128)} %copy-done.2) | copy-start | bytes 3631108
  148.6 3.7 %collective-permute-start.38 = (bf16[400,384]{1,0:T(8,128)(2,1)}, bf16[400,384]{1,0:T(8,128)(2,1)}, u32[]{:S(2)}, u32[]{:S(2)}) collective-permute-start(bf16[400,384]{1,0:T(8,128)(2,1)} %add_convert_fusion.4), channel_id=1, source_target_pairs={{0,8},{8,0},{16,24},{24,16},{1,9},{9,1},{17,25},{25,17},{2,10},{10... | collective-permute-start | bytes 921608 | tf_op jit(solution)/shard_map/ppermute | solution.py:432
  148.7 5.9 %copy-start.18 = (f32[768,768]{1,0:T(8,128)S(1)}, f32[768,768]{1,0:T(8,128)}, u32[]{:S(2)}) copy-start(f32[768,768]{1,0:T(8,128)} %copy-done.17) | copy-start | bytes 7077892
  148.7 11.4 %collective-permute-start.40 = (bf16[208,768]{1,0:T(8,128)(2,1)S(1)}, bf16[208,768]{1,0:T(8,128)(2,1)S(1)}, u32[]{:S(2)}, u32[]{:S(2)}) collective-permute-start(bf16[208,768]{1,0:T(8,128)(2,1)S(1)} %shard_map.225.refs_0_), channel_id=1, source_target_pairs={{0,3},{1,2},{2,1},{3,0},{4,7},{5,6},{6,5},{7,4},{8,11},{9,10},{10,... | collective-permute-start | bytes 958472 | tf_op jit(solution)/shard_map/ppermute | solution.py:442
  148.8 16.8 %collective-permute-start.41 = (bf16[208,768]{1,0:T(8,128)(2,1)S(1)}, bf16[208,768]{1,0:T(8,128)(2,1)S(1)}, u32[]{:S(2)}, u32[]{:S(2)}) collective-permute-start(bf16[208,768]{1,0:T(8,128)(2,1)S(1)} %shard_map.225.refs_0_), channel_id=1, source_target_pairs={{0,1},{1,0},{2,3},{3,2},{4,5},{5,4},{6,7},{7,6},{8,9},{9,8},{10,11... | collective-permute-start | bytes 958472 | tf_op jit(solution)/shard_map/ppermute | solution.py:442
  149.8 16.1 %collective-permute-start.42 = (bf16[208,768]{1,0:T(8,128)(2,1)S(1)}, bf16[208,768]{1,0:T(8,128)(2,1)S(1)}, u32[]{:S(2)}, u32[]{:S(2)}) collective-permute-start(bf16[208,768]{1,0:T(8,128)(2,1)S(1)} %shard_map.225.refs_0_), channel_id=1, source_target_pairs={{0,2},{1,3},{2,0},{3,1},{4,6},{5,7},{6,4},{7,5},{8,10},{9,11},{10,... | collective-permute-start | bytes 958472 | tf_op jit(solution)/shard_map/ppermute | solution.py:442

commit v12 on v11

--- a/solution.py
+++ b/solution.py
@@ -692,7 +692,6 @@
                 [summed, expert_swap(summed, 2), small, expert_swap(small, 2)],
                 micros=1,
             )
-            own_y, ready = lax.optimization_barrier((own_y, ready))
             everything = [quarter_swap(ready, m) for m in (3, 1, 2)]
             ready, grad_up, grad_down = lax.optimization_barrier((ready, grad_up, grad_down))
             everything = [ready] + everything

time: 168 us -> 168 us (level)
    ppermute x3, waiting for transfers between devices: 0.01 us -> 4.64 us  [dp_swap(): return lax.ppermute(value, 'dp', [(i, i ^ 1) for i in range(n_dp)])]
    ppermute x6, waiting for transfers between devices: 19.6 us -> 15.8 us  [quarter_swap(): return lax.ppermute(value, ('expert', 'dp'), pairs)]
  transfers between devices with their start and end apart: 43 -> 43, of which waited for: 21 -> 20; matrix products, arithmetic and copies ran while one was open for 2% -> 2% of each run, Pallas kernels for 13% -> 13%
where the time goes in v12:
time: 168 us; the launch traced here: 167 us
  waiting for transfers between devices  76.4 us (45%)
  starting transfers between devices  45.6 us (27%)
  Pallas kernels  37.2 us (22%)
  local copies, waits for them, and re-layouts  3.81 us (2%)
  other arithmetic  2.61 us (2%)
    ppermute x14, waiting for transfers between devices, expert_swap(): lax.ppermute(value, 'expert', [(i, i ^ mask) for i in range(n_expert)])  42.9 us
    pallas_call x16, Pallas kernels, run(): pl.pallas_call(kernel, out_shape=[jax.ShapeDtypeStruct(shape, kind) for s...  37.2 us
    ppermute x14, starting transfers between devices, expert_swap(): lax.ppermute(value, 'expert', [(i, i ^ mask) for i in range(n_expert)])  23.2 us
    ppermute x6, waiting for transfers between devices, quarter_swap(): return lax.ppermute(value, ('expert', 'dp'), pairs)  15.8 us
    ppermute x20, waiting for transfers between devices, tensor_swap(): lax.ppermute(value, 'tensor', [(i, i ^ mask) for i in range(n_tensor)])  13.1 us
    ppermute x20, starting transfers between devices, tensor_swap(): lax.ppermute(value, 'tensor', [(i, i ^ mask) for i in range(n_tensor)])  12.5 us
    ppermute x6, starting transfers between devices, quarter_swap(): return lax.ppermute(value, ('expert', 'dp'), pairs)  7.03 us
    ppermute x3, waiting for transfers between devices, dp_swap(): return lax.ppermute(value, 'dp', [(i, i ^ 1) for i in range(n_dp)])  4.64 us
  transfers between devices with their start and end apart: 43, of which 20 were waited for; matrix products, arithmetic and copies ran while one was open for 2% of the time, Pallas kernels for 13%

profile of v12, /device:TPU:0, one launch (start us, length us, event | category | flops | bytes accessed | tf_op | source)
XLA Modules:
  0.0 167.3 jit_solution(13004934747231076263)
XLA Ops:
  0.6 0.5 collective-permute-start.2
  1.2 2.9 %collective-permute-start = (bf16[192,768]{1,0:T(8,128)(2,1)}, bf16[192,768]{1,0:T(8,128)(2,1)S(1)}, u32[]{:S(2)}, u32[]{:S(2)}) collective-permute-start(bf16[192,768]{1,0:T(8,128)(2,1)} %w_out.1), channel_id=1, source_target_pairs={{0,16},{8,24},{16,0},{24,8},{1,17},{9,25},{17,1},{25,9},{2,18},{10... | collective-permute-start | bytes 884744 | tf_op jit(solution)/shard_map/ppermute | solution.py:432
  4.9 1.1 copy-done.4
  6.0 0.7 copy-done.6
  6.7 1.2 copy-done.8
  7.8 0.7 copy-done.13
  8.5 2.5 %shard_map.212 = (bf16[394,768]{1,0:T(8,128)(2,1)S(1)}, bf16[394,192]{1,0:T(8,128)(2,1)S(1)}, bf16[394,192]{1,0:T(8,128)(2,1)S(1)}, bf16[394,192]{1,0:T(8,128)(2...) custom-call(bf16[394,768]{1,0:T(8,128)(2,1)S(1)} %copy-done.4, f32[768]{0:T(1024)S(1)} %copy-done.6, ...), custom_call_target="tpu_custom_call" | custom-call | flops 4600000000 | bytes 1024 | tf_op jit(solution)/shard_map/pallas_call | solution.py:415
  11.1 0.6 collective-permute-done.rest_6_
  11.7 1.8 %collective-permute-start.5 = (bf16[394,192]{1,0:T(8,128)(2,1)S(1)}, bf16[394,192]{1,0:T(8,128)(2,1)S(1)}, u32[]{:S(2)}, u32[]{:S(2)}) collective-permute-start(bf16[394,192]{1,0:T(8,128)(2,1)S(1)} %get-tuple-element.124.rest_0_.head_out), channel_id=1, source_target_pairs={{0,16},{8,24},{16,0},{24,8},{1,17},{9,25},{17,1},{25,9},{2,18},{10... | collective-permute-start | bytes 453896 | tf_op jit(solution)/shard_map/ppermute | solution.py:432
  13.7 1.4 shard_map.213
  15.1 4.1 %collective-permute-done.5.rest_2_ = bf16[394,192]{1,0:T(8,128)(2,1)S(1)} collective-permute-done((bf16[394,192]{1,0:T(8,128)(2,1)S(1)}, bf16[394,192]{1,0:T(8,128)(2,1)S(1)}, u32[]{:S(2)}, u32[]{:S(2)}) %collective-permute-start.5) | collective-permute-done | bytes 151328 | tf_op jit(solution)/shard_map/ppermute | solution.py:432
  19.2 2.8 %collective-permute-start.8 = (bf16[72,768]{1,0:T(8,128)(2,1)S(1)}, bf16[72,768]{1,0:T(8,128)(2,1)S(1)}, u32[]{:S(2)}, u32[]{:S(2)}) collective-permute-start(bf16[72,768]{1,0:T(8,128)(2,1)S(1)} %get-tuple-element.141), channel_id=1, source_target_pairs={{0,4},{2,6},{4,0},{6,2},{1,5},{3,7},{5,1},{7,3},{8,12},{10,14},{12... | collective-permute-start | bytes 331784 | tf_op jit(solution)/shard_map/ppermute | solution.py:435
  22.0 1.3 collective-permute-start.9
  23.5 2.7 %shard_map.214 = (f32[394,768]{1,0:T(8,128)S(1)}, bf16[144,768]{1,0:T(8,128)(2,1)S(1)}, bf16[144,768]{1,0:T(8,128)(2,1)S(1)}, bf16[144,768]{1,0:T(8,128)(2,1)S(1)}, bf16[144,768]{1,0:T(8,128)(2,1)S(1)}) custom-call(s32[8]{0:T(128)S(1)} %stack.38.ids, bf16[394,768]{1,0:T(8,128)(2,1)S(1)} %copy-done.5, f32[768]{0:T(1024)S(1)} %copy-done.16, ...), custom_call_target="tpu_custom_call" | custom-call | flops 3449999872 | bytes 1024 | tf_op jit(solution)/shard_map/pallas_call | solution.py:415
  26.2 4.5 %collective-permute-done.8.refs_2_ = bf16[72,768]{1,0:T(8,128)(2,1)S(1)} collective-permute-done((bf16[72,768]{1,0:T(8,128)(2,1)S(1)}, bf16[72,768]{1,0:T(8,128)(2,1)S(1)}, u32[]{:S(2)}, u32[]{:S(2)}) %collective-permute-start.8) | collective-permute-done | bytes 110624 | tf_op jit(solution)/shard_map/ppermute | solution.py:435
  30.8 2.9 %collective-permute-start.10 = (bf16[144,768]{1,0:T(8,128)(2,1)S(1)}, bf16[144,768]{1,0:T(8,128)(2,1)S(1)}, u32[]{:S(2)}, u32[]{:S(2)}) collective-permute-start(bf16[144,768]{1,0:T(8,128)(2,1)S(1)} %get-tuple-element.144), channel_id=1, source_target_pairs={{0,2},{2,0},{4,6},{6,4},{1,3},{3,1},{5,7},{7,5},{8,10},{10,8},{12,... | collective-permute-start | bytes 663560 | tf_op jit(solution)/shard_map/ppermute | solution.py:435
  33.7 3.9 %collective-permute-start.12 = (bf16[144,768]{1,0:T(8,128)(2,1)S(1)}, bf16[144,768]{1,0:T(8,128)(2,1)S(1)}, u32[]{:S(2)}, u32[]{:S(2)}) collective-permute-start(bf16[144,768]{1,0:T(8,128)(2,1)S(1)} %get-tuple-element.149), channel_id=1, source_target_pairs={{0,4},{2,6},{4,0},{6,2},{1,5},{3,7},{5,1},{7,3},{8,12},{10,14},{12... | collective-permute-start | bytes 663560 | tf_op jit(solution)/shard_map/ppermute | solution.py:435
  37.6 0.5 collective-permute-start.13
  38.0 1.6 collective-permute-start.14
  39.6 5.0 %collective-permute-done.10.refs_1_ = bf16[144,768]{1,0:T(8,128)(2,1)S(1)} collective-permute-done((bf16[144,768]{1,0:T(8,128)(2,1)S(1)}, bf16[144,768]{1,0:T(8,128)(2,1)S(1)}, u32[]{:S(2)}, u32[]{:S(2)}) %collective-permute-start.10) | collective-permute-done | bytes 221216 | tf_op jit(solution)/shard_map/ppermute | solution.py:435
  44.6 4.2 %collective-permute-done.11.refs_3_ = bf16[144,768]{1,0:T(8,128)(2,1)S(1)} collective-permute-done((bf16[144,768]{1,0:T(8,128)(2,1)S(1)}, bf16[144,768]{1,0:T(8,128)(2,1)S(1)}, u32[]{:S(2)}, u32[]{:S(2)}) %collective-permute-start.11) | collective-permute-done | bytes 221216 | tf_op jit(solution)/shard_map/ppermute | solution.py:435
  48.8 7.0 %shard_map.215 = (bf16[144,768]{1,0:T(8,128)(2,1)S(1)}, bf16[144,768]{1,0:T(8,128)(2,1)S(1)}, bf16[2,144,768]{2,1,0:T(8,128)(2,1)S(1)}, bf16[2,144,768]{2,1,0:T(...) custom-call(s32[8]{0:T(128)S(1)} %stack.38.ids, ...), custom_call_target="tpu_custom_call" | custom-call | flops 57500000 | bytes 1024 | tf_op jit(solution)/shard_map/pallas_call | solution.py:415
  55.8 0.9 collective-permute-done.13.refs_1_
  56.7 4.8 %shard_map.216 = (bf16[144,768]{1,0:T(8,128)(2,1)S(1)}, bf16[144,768]{1,0:T(8,128)(2,1)S(1)}, bf16[2,72,768]{2,1,0:T(8,128)(2,1)S(1)}, bf16[2,72,768]{2,1,0:T(8,...) custom-call(s32[8]{0:T(128)S(1)} %stack.38.ids, ...), custom_call_target="tpu_custom_call" | custom-call | flops 57500000 | bytes 1024 | tf_op jit(solution)/shard_map/pallas_call | solution.py:415
  61.5 2.7 %shard_map.218 = (bf16[1536,768]{1,0:T(8,128)(2,1)S(1)}, bf16[1536,768]{1,0:T(8,128)(2,1)S(1)}) custom-call(bf16[288,768]{1,0:T(8,128)(2,1)S(1)} %get-tuple-element.164.refs_0_, bf16[288,768]{1,0:T(8,128)(2,1)S(1)} %get-tuple-element.165.refs_1_, bf16[288,768]{1,0:T(8,128)(2,1)S(1)} %get-tuple-element.166.refs_2_, ...), custom_call_target="tpu_custom_call" | custom-call | flops 4600000000 | bytes 1024 | tf_op jit(solution)/shard_map/pallas_call | solution.py:415
  64.3 1.6 collective-permute-start.18
  65.8 3.1 %collective-permute-start.15 = (bf16[144,768]{1,0:T(8,128)(2,1)S(1)}, bf16[144,768]{1,0:T(8,128)(2,1)S(1)}, u32[]{:S(2)}, u32[]{:S(2)}) collective-permute-start(bf16[144,768]{1,0:T(8,128)(2,1)S(1)} %get-tuple-element.153), channel_id=1, source_target_pairs={{0,6},{2,4},{4,2},{6,0},{1,7},{3,5},{5,3},{7,1},{8,14},{10,12},{12... | collective-permute-start | bytes 663560 | tf_op jit(solution)/shard_map/ppermute | solution.py:435
  69.0 1.2 collective-permute-start.17
  70.2 1.6 shard_map.219
  71.9 1.6 collective-permute-start.20
  73.5 0.5 collective-permute-start.21
  74.1 2.0 %collective-permute-done.15.refs_1_ = bf16[144,768]{1,0:T(8,128)(2,1)S(1)} collective-permute-done((bf16[144,768]{1,0:T(8,128)(2,1)S(1)}, bf16[144,768]{1,0:T(8,128)(2,1)S(1)}, u32[]{:S(2)}, u32[]{:S(2)}) %collective-permute-start.15) | collective-permute-done | bytes 221216 | tf_op jit(solution)/shard_map/ppermute | solution.py:435
  76.1 11.7 %collective-permute-done.16.refs_2_ = bf16[144,768]{1,0:T(8,128)(2,1)S(1)} collective-permute-done((bf16[144,768]{1,0:T(8,128)(2,1)S(1)}, bf16[144,768]{1,0:T(8,128)(2,1)S(1)}, u32[]{:S(2)}, u32[]{:S(2)}) %collective-permute-start.16) | collective-permute-done | bytes 221216 | tf_op jit(solution)/shard_map/ppermute | solution.py:435
  87.8 1.5 shard_map.220
  89.4 1.6 collective-permute-done.22
  91.1 0.6 collective-permute-start.23
  91.7 3.0 %collective-permute-start.25 = (bf16[72,768]{1,0:T(8,128)(2,1)S(1)}, bf16[72,768]{1,0:T(8,128)(2,1)S(1)}, u32[]{:S(2)}, u32[]{:S(2)}) collective-permute-start(bf16[72,768]{1,0:T(8,128)(2,1)S(1)} %get-tuple-element.186), channel_id=1, source_target_pairs={{0,4},{2,6},{4,0},{6,2},{1,5},{3,7},{5,1},{7,3},{8,12},{10,14},{12... | collective-permute-start | bytes 331784 | tf_op jit(solution)/shard_map/ppermute | solution.py:435
  94.6 1.4 collective-permute-start.26
  96.0 4.7 %collective-permute-done.23 = bf16[416,384]{1,0:T(8,128)(2,1)S(1)} collective-permute-done((bf16[416,384]{1,0:T(8,128)(2,1)S(1)}, bf16[416,384]{1,0:T(8,128)(2,1)S(1)}, u32[]{:S(2)}, u32[]{:S(2)}) %collective-permute-start.23) | collective-permute-done | bytes 319520 | tf_op jit(solution)/shard_map/ppermute | solution.py:432
  100.8 3.5 %collective-permute-done.26.refs_1_ = bf16[72,768]{1,0:T(8,128)(2,1)S(1)} collective-permute-done((bf16[72,768]{1,0:T(8,128)(2,1)S(1)}, bf16[72,768]{1,0:T(8,128)(2,1)S(1)}, u32[]{:S(2)}, u32[]{:S(2)}) %collective-permute-start.26) | collective-permute-done | bytes 110624 | tf_op jit(solution)/shard_map/ppermute | solution.py:435
  104.4 1.6 collective-permute-done.27.other
  106.0 5.0 %shard_map.221 = (f32[394,768]{1,0:T(8,128)S(1)}, bf16[394,384]{1,0:T(8,128)(2,1)S(1)}, bf16[394,384]{1,0:T(8,128)(2,1)S(1)}, f32[16,768]{1,0:T(8,128)S(1)}, bf1...) custom-call(s32[8]{0:T(128)S(1)} %stack.38.ids, ...), custom_call_target="tpu_custom_call" | custom-call | flops 6899999744 | bytes 1024 | tf_op jit(solution)/shard_map/pallas_call | solution.py:415
  111.1 1.4 shard_map.222
  113.0 1.7 %collective-permute-start.33 = (bf16[192,768]{1,0:T(8,128)(2,1)S(1)}, bf16[192,768]{1,0:T(8,128)(2,1)S(1)}, u32[]{:S(2)}, u32[]{:S(2)}) collective-permute-start(bf16[192,768]{1,0:T(8,128)(2,1)S(1)} %get-tuple-element.212), channel_id=1, source_target_pairs={{0,3},{1,2},{2,1},{3,0},{4,7},{5,6},{6,5},{7,4},{8,11},{9,10},{10,... | collective-permute-start | bytes 884744 | tf_op jit(solution)/shard_map/ppermute | solution.py:442
  114.8 0.5 collective-permute-start.34
  115.3 1.2 collective-permute-start.35
  116.6 1.5 collective-permute-start.32
  118.2 0.6 collective-permute-start.29
  118.8 5.0 %collective-permute-done.33.refs_1_ = bf16[192,768]{1,0:T(8,128)(2,1)S(1)} collective-permute-done((bf16[192,768]{1,0:T(8,128)(2,1)S(1)}, bf16[192,768]{1,0:T(8,128)(2,1)S(1)}, u32[]{:S(2)}, u32[]{:S(2)}) %collective-permute-start.33) | collective-permute-done | bytes 294944 | tf_op jit(solution)/shard_map/ppermute | solution.py:442
  123.8 5.5 %collective-permute-done.34.refs_2_ = bf16[192,768]{1,0:T(8,128)(2,1)S(1)} collective-permute-done((bf16[192,768]{1,0:T(8,128)(2,1)S(1)}, bf16[192,768]{1,0:T(8,128)(2,1)S(1)}, u32[]{:S(2)}, u32[]{:S(2)}) %collective-permute-start.34) | collective-permute-done | bytes 294944 | tf_op jit(solution)/shard_map/ppermute | solution.py:442
  129.6 1.8 %collective-permute-start.37 = (bf16[192,768]{1,0:T(8,128)(2,1)S(1)}, bf16[192,768]{1,0:T(8,128)(2,1)S(1)}, u32[]{:S(2)}, u32[]{:S(2)}) collective-permute-start(bf16[192,768]{1,0:T(8,128)(2,1)S(1)} %shard_map.223.own), channel_id=1, source_target_pairs={{0,4},{2,6},{4,0},{6,2},{1,5},{3,7},{5,1},{7,3},{8,12},{10,14},{12... | collective-permute-start | bytes 884744 | tf_op jit(solution)/shard_map/ppermute | solution.py:435
  131.5 0.8 collective-permute-start.39
  132.6 0.5 collective-permute-done.36.other
  133.1 2.4 %shard_map.224 = (bf16[394,768]{1,0:T(8,128)(2,1)}, f32[16,768]{1,0:T(8,128)S(1)}) custom-call(s32[8]{0:T(128)S(1)} %stack.38.ids, bf16[394,384]{1,0:T(8,128)(2,1)S(1)} %add_convert_fusion.2.own, bf16[394,384]{1,0:T(8,128)(2,1)S(1)} %collective-permute-done.36.other, bf16[394,768]{1,0:T(8,128)(2,1)S(1)} %copy-done.5, ...), custom_call_target="tpu_custom_call" | custom-call | flops 11500000 | bytes 1024 | tf_op jit(solution)/shard_map/pallas_call | solution.py:415
  135.5 1.2 collective-permute-start.38
  136.7 10.3 %collective-permute-done.37.came = bf16[192,768]{1,0:T(8,128)(2,1)S(1)} collective-permute-done((bf16[192,768]{1,0:T(8,128)(2,1)S(1)}, bf16[192,768]{1,0:T(8,128)(2,1)S(1)}, u32[]{:S(2)}, u32[]{:S(2)}) %collective-permute-start.37) | collective-permute-done | bytes 294944 | tf_op jit(solution)/shard_map/ppermute | solution.py:435
  147.1 0.7 collective-permute-done.38.small_came
  147.9 0.7 collective-permute-start.41
  148.6 2.8 %collective-permute-start.42 = (bf16[208,768]{1,0:T(8,128)(2,1)S(1)}, bf16[208,768]{1,0:T(8,128)(2,1)S(1)}, u32[]{:S(2)}, u32[]{:S(2)}) collective-permute-start(bf16[208,768]{1,0:T(8,128)(2,1)S(1)} %shard_map.225.refs_0_), channel_id=1, source_target_pairs={{0,2},{1,3},{2,0},{3,1},{4,6},{5,7},{6,4},{7,5},{8,10},{9,11},{10,... | collective-permute-start | bytes 958472 | tf_op jit(solution)/shard_map/ppermute | solution.py:442
  151.4 2.1 %select_convert_fusion = bf16[394,768]{1,0:T(8,128)(2,1)} fusion(f32[394,768]{1,0:T(8,128)S(1)} %copy-done.3, bf16[400,384]{1,0:T(8,128)(2,1)} %collective-permute-done.30, bf16[400,384]{1,0:T(8,128)(2,1)S(1)} %add_convert_fusion.4, pred[394]{0:T(512)(128)(4,1)S(1)} %iota_compare_fusion, pred[]{:T(512)S(6)} %eq.7), kind=kLoop, calls=%fused_computation | loop fusion | flops 3933696 | bytes 2430347 | tf_op jit(solution)/shard_map/convert_element_type | solution.py:720
  153.6 4.6 %collective-permute-done.39.came_rest = bf16[512,768]{1,0:T(8,128)(2,1)S(1)} collective-permute-done((bf16[512,768]{1,0:T(8,128)(2,1)S(1)}, bf16[512,768]{1,0:T(8,128)(2,1)S(1)}, u32[]{:S(2)}, u32[]{:S(2)}) %collective-permute-start.39) | collective-permute-done | bytes 786464 | tf_op jit(solution)/shard_map/ppermute | solution.py:438
  158.2 1.7 shard_map.226
  159.9 5.3 %collective-permute-done.41.refs_2_ = bf16[208,768]{1,0:T(8,128)(2,1)S(1)} collective-permute-done((bf16[208,768]{1,0:T(8,128)(2,1)S(1)}, bf16[208,768]{1,0:T(8,128)(2,1)S(1)}, u32[]{:S(2)}, u32[]{:S(2)}) %collective-permute-start.41) | collective-permute-done | bytes 319520 | tf_op jit(solution)/shard_map/ppermute | solution.py:442
  165.1 2.2 %shard_map.227 = (f32[576,768]{1,0:T(8,128)}, f32[192,768]{1,0:T(8,128)}, f32[768]{0:T(1024)}, f32[768]{0:T(1024)}, f32[768]{0:T(1024)}, /*index=5*/f32[768]{0:T(1024)}, f32[4,768]{1,0:T(4,128)}) custom-call(s32[8]{0:T(128)S(1)} %stack.38.ids, bf16[208,768]{1,0:T(8,128)(2,1)S(1)} %shard_map.225.refs_0_, ...), custom_call_target="tpu_custom_call" | custom-call | flops 3449999872 | bytes 1024 | tf_op jit(solution)/shard_map/pallas_call | solution.py:415
  (87 shorter events, 2.6 us)
Async XLA Ops:
  0.6 11.0 %collective-permute-start.2 = (bf16[768,768]{1,0:T(8,128)(2,1)}, bf16[768,768]{1,0:T(8,128)(2,1)S(1)}, u32[]{:S(2)}, u32[]{:S(2)}) collective-permute-start(bf16[768,768]{1,0:T(8,128)(2,1)} %bitcast.26), channel_id=1, source_target_pairs={{0,8},{8,0},{16,24},{24,16},{1,9},{9,1},{17,25},{25,17},{2,10},{10... | collective-permute-start | bytes 3538952 | tf_op jit(solution)/shard_map/ppermute | solution.py:432
  1.2 10.5 %collective-permute-start.3 = (bf16[768,768]{1,0:T(8,128)(2,1)}, bf16[768,768]{1,0:T(8,128)(2,1)S(1)}, u32[]{:S(2)}, u32[]{:S(2)}) collective-permute-start(bf16[768,768]{1,0:T(8,128)(2,1)} %bitcast.29), channel_id=1, source_target_pairs={{0,8},{8,0},{16,24},{24,16},{1,9},{9,1},{17,25},{25,17},{2,10},{10... | collective-permute-start | bytes 3538952 | tf_op jit(solution)/shard_map/ppermute | solution.py:432
  1.2 10.4 %collective-permute-start = (bf16[192,768]{1,0:T(8,128)(2,1)}, bf16[192,768]{1,0:T(8,128)(2,1)S(1)}, u32[]{:S(2)}, u32[]{:S(2)}) collective-permute-start(bf16[192,768]{1,0:T(8,128)(2,1)} %w_out.1), channel_id=1, source_target_pairs={{0,16},{8,24},{16,0},{24,8},{1,17},{9,25},{17,1},{25,9},{2,18},{10... | collective-permute-start | bytes 884744 | tf_op jit(solution)/shard_map/ppermute | solution.py:432
  4.2 7.5 %collective-permute-start.1 = (bf16[192,768]{1,0:T(8,128)(2,1)}, bf16[192,768]{1,0:T(8,128)(2,1)S(1)}, u32[]{:S(2)}, u32[]{:S(2)}) collective-permute-start(bf16[192,768]{1,0:T(8,128)(2,1)} %w_out.1), channel_id=1, source_target_pairs={{0,8},{8,0},{16,24},{24,16},{1,9},{9,1},{17,25},{25,17},{2,10},{10... | collective-permute-start | bytes 884744 | tf_op jit(solution)/shard_map/ppermute | solution.py:432
  4.9 1.1 copy-start.4
  6.0 0.7 copy-start.6
  6.7 1.2 copy-start.8
  7.8 0.7 copy-start.13
  8.5 5.2 %copy-start.10 = (bf16[394,768]{1,0:T(8,128)(2,1)S(1)}, bf16[394,768]{1,0:T(8,128)(2,1)}, u32[]{:S(2)}) copy-start(bf16[394,768]{1,0:T(8,128)(2,1)} %cot.3) | copy-start | bytes 1815556
  8.5 5.2 %copy-start.12 = (bf16[768,4]{0,1:T(4,128)(2,1)S(1)}, bf16[768,4]{0,1:T(4,128)(2,1)}, u32[]{:S(2)}) copy-start(bf16[768,4]{0,1:T(4,128)(2,1)} %param.22) | copy-start | bytes 18436
  8.5 5.2 %copy-start.14 = (s32[394,2]{0,1:T(2,128)S(1)}, s32[394,2]{0,1:T(2,128)}, u32[]{:S(2)}) copy-start(s32[394,2]{0,1:T(2,128)} %param.14) | copy-start | bytes 9460
  11.6 11.8 %collective-permute-start.4 = (bf16[394,192]{1,0:T(8,128)(2,1)S(1)}, bf16[394,192]{1,0:T(8,128)(2,1)S(1)}, u32[]{:S(2)}, u32[]{:S(2)}) collective-permute-start(bf16[394,192]{1,0:T(8,128)(2,1)S(1)} %get-tuple-element.124.rest_0_.head_out), channel_id=1, source_target_pairs={{0,8},{8,0},{16,24},{24,16},{1,9},{9,1},{17,25},{25,17},{2,10},{10... | collective-permute-start | bytes 453896 | tf_op jit(solution)/shard_map/ppermute | solution.py:432
  11.7 7.5 %collective-permute-start.5 = (bf16[394,192]{1,0:T(8,128)(2,1)S(1)}, bf16[394,192]{1,0:T(8,128)(2,1)S(1)}, u32[]{:S(2)}, u32[]{:S(2)}) collective-permute-start(bf16[394,192]{1,0:T(8,128)(2,1)S(1)} %get-tuple-element.124.rest_0_.head_out), channel_id=1, source_target_pairs={{0,16},{8,24},{16,0},{24,8},{1,17},{9,25},{17,1},{25,9},{2,18},{10... | collective-permute-start | bytes 453896 | tf_op jit(solution)/shard_map/ppermute | solution.py:432
  13.5 9.9 %collective-permute-start.7 = (bf16[192,768]{1,0:T(8,128)(2,1)S(1)}, bf16[192,768]{1,0:T(8,128)(2,1)S(1)}, u32[]{:S(2)}, u32[]{:S(2)}) collective-permute-start(bf16[192,768]{1,0:T(8,128)(2,1)S(1)} %collective-permute-done.rest_6_), channel_id=1, source_target_pairs={{0,8},{8,0},{16,24},{24,16},{1,9},{9,1},{17,25},{25,17},{2,10},{10... | collective-permute-start | bytes 884744 | tf_op jit(solution)/shard_map/ppermute | solution.py:432
  13.7 9.7 %copy-start.5 = (bf16[394,768]{1,0:T(8,128)(2,1)S(1)}, bf16[394,768]{1,0:T(8,128)(2,1)}, u32[]{:S(2)}) copy-start(bf16[394,768]{1,0:T(8,128)(2,1)} %tokens.5) | copy-start | bytes 1815556
  13.7 9.7 %copy-start.11 = (bf16[192,768]{1,0:T(8,128)(2,1)S(1)}, bf16[192,768]{1,0:T(8,128)(2,1)}, u32[]{:S(2)}) copy-start(bf16[192,768]{1,0:T(8,128)(2,1)} %w_out.1) | copy-start | bytes 884740
  13.7 9.7 %copy-start.15 = (f32[768]{0:T(1024)S(1)}, f32[768]{0:T(1024)}, u32[]{:S(2)}) copy-start(f32[768]{0:T(1024)} %bias.3) | copy-start | bytes 9220
  13.7 9.7 %copy-start.16 = (f32[768]{0:T(1024)S(1)}, f32[768]{0:T(1024)}, u32[]{:S(2)}) copy-start(f32[768]{0:T(1024)} %gain.6) | copy-start | bytes 9220
  19.2 4.2 %collective-permute-start.6 = (bf16[394,192]{1,0:T(8,128)(2,1)S(1)}, bf16[394,192]{1,0:T(8,128)(2,1)S(1)}, u32[]{:S(2)}, u32[]{:S(2)}) collective-permute-start(bf16[394,192]{1,0:T(8,128)(2,1)S(1)} %collective-permute-done.5.rest_2_), channel_id=1, source_target_pairs={{0,8},{8,0},{16,24},{24,16},{1,9},{9,1},{17,25},{25,17},{2,10},{10... | collective-permute-start | bytes 453896 | tf_op jit(solution)/shard_map/ppermute | solution.py:432
  19.2 11.6 %collective-permute-start.8 = (bf16[72,768]{1,0:T(8,128)(2,1)S(1)}, bf16[72,768]{1,0:T(8,128)(2,1)S(1)}, u32[]{:S(2)}, u32[]{:S(2)}) collective-permute-start(bf16[72,768]{1,0:T(8,128)(2,1)S(1)} %get-tuple-element.141), channel_id=1, source_target_pairs={{0,4},{2,6},{4,0},{6,2},{1,5},{3,7},{5,1},{7,3},{8,12},{10,14},{12... | collective-permute-start | bytes 331784 | tf_op jit(solution)/shard_map/ppermute | solution.py:435
  22.0 8.7 %collective-permute-start.9 = (bf16[72,768]{1,0:T(8,128)(2,1)S(1)}, bf16[72,768]{1,0:T(8,128)(2,1)S(1)}, u32[]{:S(2)}, u32[]{:S(2)}) collective-permute-start(bf16[72,768]{1,0:T(8,128)(2,1)S(1)} %get-tuple-element.142), channel_id=1, source_target_pairs={{0,6},{2,4},{4,2},{6,0},{1,7},{3,5},{5,3},{7,1},{8,14},{10,12},{12... | collective-permute-start | bytes 331784 | tf_op jit(solution)/shard_map/ppermute | solution.py:435
  23.4 25.3 %copy-start = (bf16[1,768,768]{2,1,0:T(8,128)(2,1)S(1)}, bf16[1,768,768]{2,1,0:T(8,128)(2,1)}, u32[]{:S(2)}) copy-start(bf16[1,768,768]{2,1,0:T(8,128)(2,1)} %param.23) | copy-start | bytes 3538948
  23.5 25.3 %copy-start.1 = (bf16[1,768,768]{2,1,0:T(8,128)(2,1)S(1)}, bf16[1,768,768]{2,1,0:T(8,128)(2,1)}, u32[]{:S(2)}) copy-start(bf16[1,768,768]{2,1,0:T(8,128)(2,1)} %param.24) | copy-start | bytes 3538948
  26.2 79.7 %copy-start.2 = (f32[394,768]{1,0:T(8,128)}, f32[394,768]{1,0:T(8,128)S(1)}, u32[]{:S(2)}) copy-start(f32[394,768]{1,0:T(8,128)S(1)} %get-tuple-element.132.middle) | copy-start | bytes 3631108
  30.8 13.8 %collective-permute-start.10 = (bf16[144,768]{1,0:T(8,128)(2,1)S(1)}, bf16[144,768]{1,0:T(8,128)(2,1)S(1)}, u32[]{:S(2)}, u32[]{:S(2)}) collective-permute-start(bf16[144,768]{1,0:T(8,128)(2,1)S(1)} %get-tuple-element.144), channel_id=1, source_target_pairs={{0,2},{2,0},{4,6},{6,4},{1,3},{3,1},{5,7},{7,5},{8,10},{10,8},{12,... | collective-permute-start | bytes 663560 | tf_op jit(solution)/shard_map/ppermute | solution.py:435
  33.6 15.1 %collective-permute-start.11 = (bf16[144,768]{1,0:T(8,128)(2,1)S(1)}, bf16[144,768]{1,0:T(8,128)(2,1)S(1)}, u32[]{:S(2)}, u32[]{:S(2)}) collective-permute-start(bf16[144,768]{1,0:T(8,128)(2,1)S(1)} %get-tuple-element.146), channel_id=1, source_target_pairs={{0,2},{2,0},{4,6},{6,4},{1,3},{3,1},{5,7},{7,5},{8,10},{10,8},{12,... | collective-permute-start | bytes 663560 | tf_op jit(solution)/shard_map/ppermute | solution.py:435
  33.7 22.1 %collective-permute-start.12 = (bf16[144,768]{1,0:T(8,128)(2,1)S(1)}, bf16[144,768]{1,0:T(8,128)(2,1)S(1)}, u32[]{:S(2)}, u32[]{:S(2)}) collective-permute-start(bf16[144,768]{1,0:T(8,128)(2,1)S(1)} %get-tuple-element.149), channel_id=1, source_target_pairs={{0,4},{2,6},{4,0},{6,2},{1,5},{3,7},{5,1},{7,3},{8,12},{10,14},{12... | collective-permute-start | bytes 663560 | tf_op jit(solution)/shard_map/ppermute | solution.py:435
  37.6 19.1 %collective-permute-start.13 = (bf16[144,768]{1,0:T(8,128)(2,1)S(1)}, bf16[144,768]{1,0:T(8,128)(2,1)S(1)}, u32[]{:S(2)}, u32[]{:S(2)}) collective-permute-start(bf16[144,768]{1,0:T(8,128)(2,1)S(1)} %get-tuple-element.150), channel_id=1, source_target_pairs={{0,6},{2,4},{4,2},{6,0},{1,7},{3,5},{5,3},{7,1},{8,14},{10,12},{12... | collective-permute-start | bytes 663560 | tf_op jit(solution)/shard_map/ppermute | solution.py:435
  38.0 18.7 %collective-permute-start.14 = (bf16[2,72,768]{2,1,0:T(8,128)(2,1)S(1)}, bf16[2,72,768]{2,1,0:T(8,128)(2,1)S(1)}, u32[]{:S(2)}, u32[]{:S(2)}) collective-permute-start(bf16[2,72,768]{2,1,0:T(8,128)(2,1)S(1)} %pad_maximum_fusion.2), channel_id=1, source_target_pairs={{0,16},{8,24},{16,0},{24,8},{1,17},{9,25},{17,1},{25,9},{2,18},{10... | collective-permute-start | bytes 663560 | tf_op jit(solution)/shard_map/ppermute | solution.py:432
  64.2 6.0 %collective-permute-start.19 = (bf16[1536,768]{1,0:T(8,128)(2,1)S(1)}, bf16[1536,768]{1,0:T(8,128)(2,1)S(1)}, u32[]{:S(2)}, u32[]{:S(2)}) collective-permute-start(bf16[1536,768]{1,0:T(8,128)(2,1)S(1)} %get-tuple-element.173), channel_id=1, source_target_pairs={{0,8},{8,0},{16,24},{24,16},{1,9},{9,1},{17,25},{25,17},{2,10},{10... | collective-permute-start | bytes 7077896 | tf_op jit(solution)/shard_map/ppermute | solution.py:432
  64.3 9.2 %collective-permute-start.18 = (bf16[2,72,768]{2,1,0:T(8,128)(2,1)S(1)}, bf16[2,72,768]{2,1,0:T(8,128)(2,1)S(1)}, u32[]{:S(2)}, u32[]{:S(2)}) collective-permute-start(bf16[2,72,768]{2,1,0:T(8,128)(2,1)S(1)} %get-tuple-element.161), channel_id=1, source_target_pairs={{0,16},{8,24},{16,0},{24,8},{1,17},{9,25},{17,1},{25,9},{2,18},{10... | collective-permute-start | bytes 663560 | tf_op jit(solution)/shard_map/ppermute | solution.py:432
  65.8 10.2 %collective-permute-start.15 = (bf16[144,768]{1,0:T(8,128)(2,1)S(1)}, bf16[144,768]{1,0:T(8,128)(2,1)S(1)}, u32[]{:S(2)}, u32[]{:S(2)}) collective-permute-start(bf16[144,768]{1,0:T(8,128)(2,1)S(1)} %get-tuple-element.153), channel_id=1, source_target_pairs={{0,6},{2,4},{4,2},{6,0},{1,7},{3,5},{5,3},{7,1},{8,14},{10,12},{12... | collective-permute-start | bytes 663560 | tf_op jit(solution)/shard_map/ppermute | solution.py:435
  69.0 18.8 %collective-permute-start.16 = (bf16[144,768]{1,0:T(8,128)(2,1)S(1)}, bf16[144,768]{1,0:T(8,128)(2,1)S(1)}, u32[]{:S(2)}, u32[]{:S(2)}) collective-permute-start(bf16[144,768]{1,0:T(8,128)(2,1)S(1)} %get-tuple-element.156), channel_id=1, source_target_pairs={{0,4},{2,6},{4,0},{6,2},{1,5},{3,7},{5,1},{7,3},{8,12},{10,14},{12... | collective-permute-start | bytes 663560 | tf_op jit(solution)/shard_map/ppermute | solution.py:435
  69.0 18.8 %collective-permute-start.17 = (bf16[144,768]{1,0:T(8,128)(2,1)S(1)}, bf16[144,768]{1,0:T(8,128)(2,1)S(1)}, u32[]{:S(2)}, u32[]{:S(2)}) collective-permute-start(bf16[144,768]{1,0:T(8,128)(2,1)S(1)} %get-tuple-element.157), channel_id=1, source_target_pairs={{0,2},{2,0},{4,6},{6,4},{1,3},{3,1},{5,7},{7,5},{8,10},{10,8},{12,... | collective-permute-start | bytes 663560 | tf_op jit(solution)/shard_map/ppermute | solution.py:435
  71.9 2.2 %copy-start.17 = (f32[768,768]{1,0:T(8,128)}, f32[768,768]{1,0:T(8,128)S(1)}, u32[]{:S(2)}) copy-start(f32[768,768]{1,0:T(8,128)S(1)} %get-tuple-element.219.kept) | copy-start | bytes 7077892
  71.9 15.9 %collective-permute-start.20 = (bf16[128,768]{1,0:T(8,128)(2,1)S(1)}, bf16[128,768]{1,0:T(8,128)(2,1)S(1)}, u32[]{:S(2)}, u32[]{:S(2)}) collective-permute-start(bf16[128,768]{1,0:T(8,128)(2,1)S(1)} %get-tuple-element.174), channel_id=1, source_target_pairs={{0,1},{1,0},{2,3},{3,2},{4,5},{5,4},{6,7},{7,6},{8,9},{9,8},{10,11... | collective-permute-start | bytes 589832 | tf_op jit(solution)/shard_map/ppermute | solution.py:438
  73.5 14.3 %collective-permute-start.21 = (bf16[128,768]{1,0:T(8,128)(2,1)S(1)}, bf16[128,768]{1,0:T(8,128)(2,1)S(1)}, u32[]{:S(2)}, u32[]{:S(2)}) collective-permute-start(bf16[128,768]{1,0:T(8,128)(2,1)S(1)} %get-tuple-element.175), channel_id=1, source_target_pairs={{0,1},{1,0},{2,3},{3,2},{4,5},{5,4},{6,7},{7,6},{8,9},{9,8},{10,11... | collective-permute-start | bytes 589832 | tf_op jit(solution)/shard_map/ppermute | solution.py:438
  89.3 16.7 %copy-start.9 = (bf16[768,3,192]{0,2,1:T(8,128)(2,1)S(1)}, bf16[768,3,192]{0,2,1:T(8,128)(2,1)}, u32[]{:S(2)}) copy-start(bf16[768,3,192]{0,2,1:T(8,128)(2,1)} %param.18) | copy-start | bytes 2654212
  89.3 1.7 %collective-permute-start.22 = (bf16[416,384]{1,0:T(8,128)(2,1)S(1)}, bf16[416,384]{1,0:T(8,128)(2,1)S(1)}, u32[]{:S(2)}, u32[]{:S(2)}) collective-permute-start(bf16[416,384]{1,0:T(8,128)(2,1)S(1)} %get-tuple-element.183), channel_id=1, source_target_pairs={{0,8},{8,0},{16,24},{24,16},{1,9},{9,1},{17,25},{25,17},{2,10},{10... | collective-permute-start | bytes 958472 | tf_op jit(solution)/shard_map/ppermute | solution.py:432
  91.1 9.6 %collective-permute-start.23 = (bf16[416,384]{1,0:T(8,128)(2,1)S(1)}, bf16[416,384]{1,0:T(8,128)(2,1)S(1)}, u32[]{:S(2)}, u32[]{:S(2)}) collective-permute-start(bf16[416,384]{1,0:T(8,128)(2,1)S(1)} %add_convert_fusion.1), channel_id=1, source_target_pairs={{0,16},{8,24},{16,0},{24,8},{1,17},{9,25},{17,1},{25,9},{2,18},{10... | collective-permute-start | bytes 958472 | tf_op jit(solution)/shard_map/ppermute | solution.py:432
  91.7 12.7 %collective-permute-start.24 = (bf16[144,768]{1,0:T(8,128)(2,1)S(1)}, bf16[144,768]{1,0:T(8,128)(2,1)S(1)}, u32[]{:S(2)}, u32[]{:S(2)}) collective-permute-start(bf16[144,768]{1,0:T(8,128)(2,1)S(1)} %get-tuple-element.185), channel_id=1, source_target_pairs={{0,2},{2,0},{4,6},{6,4},{1,3},{3,1},{5,7},{7,5},{8,10},{10,8},{12,... | collective-permute-start | bytes 663560 | tf_op jit(solution)/shard_map/ppermute | solution.py:435
  91.7 9.1 %collective-permute-start.25 = (bf16[72,768]{1,0:T(8,128)(2,1)S(1)}, bf16[72,768]{1,0:T(8,128)(2,1)S(1)}, u32[]{:S(2)}, u32[]{:S(2)}) collective-permute-start(bf16[72,768]{1,0:T(8,128)(2,1)S(1)} %get-tuple-element.186), channel_id=1, source_target_pairs={{0,4},{2,6},{4,0},{6,2},{1,5},{3,7},{5,1},{7,3},{8,12},{10,14},{12... | collective-permute-start | bytes 331784 | tf_op jit(solution)/shard_map/ppermute | solution.py:435
  94.6 9.7 %collective-permute-start.26 = (bf16[72,768]{1,0:T(8,128)(2,1)S(1)}, bf16[72,768]{1,0:T(8,128)(2,1)S(1)}, u32[]{:S(2)}, u32[]{:S(2)}) collective-permute-start(bf16[72,768]{1,0:T(8,128)(2,1)S(1)} %get-tuple-element.187), channel_id=1, source_target_pairs={{0,6},{2,4},{4,2},{6,0},{1,7},{3,5},{5,3},{7,1},{8,14},{10,12},{12... | collective-permute-start | bytes 331784 | tf_op jit(solution)/shard_map/ppermute | solution.py:435
  104.3 1.6 collective-permute-start.27
  110.9 5.6 %collective-permute-start.31 = (bf16[394,384]{1,0:T(8,128)(2,1)S(1)}, bf16[394,384]{1,0:T(8,128)(2,1)S(1)}, u32[]{:S(2)}, u32[]{:S(2)}) collective-permute-start(bf16[394,384]{1,0:T(8,128)(2,1)S(1)} %get-tuple-element.210), channel_id=1, source_target_pairs={{0,8},{8,0},{16,24},{24,16},{1,9},{9,1},{17,25},{25,17},{2,10},{10... | collective-permute-start | bytes 907784 | tf_op jit(solution)/shard_map/ppermute | solution.py:432
  112.6 5.6 %collective-permute-start.28 = (bf16[400,384]{1,0:T(8,128)(2,1)S(1)}, bf16[400,384]{1,0:T(8,128)(2,1)S(1)}, u32[]{:S(2)}, u32[]{:S(2)}) collective-permute-start(bf16[400,384]{1,0:T(8,128)(2,1)S(1)} %get-tuple-element.207), channel_id=1, source_target_pairs={{0,8},{8,0},{16,24},{24,16},{1,9},{9,1},{17,25},{25,17},{2,10},{10... | collective-permute-start | bytes 921608 | tf_op jit(solution)/shard_map/ppermute | solution.py:432
  113.0 10.8 %collective-permute-start.33 = (bf16[192,768]{1,0:T(8,128)(2,1)S(1)}, bf16[192,768]{1,0:T(8,128)(2,1)S(1)}, u32[]{:S(2)}, u32[]{:S(2)}) collective-permute-start(bf16[192,768]{1,0:T(8,128)(2,1)S(1)} %get-tuple-element.212), channel_id=1, source_target_pairs={{0,3},{1,2},{2,1},{3,0},{4,7},{5,6},{6,5},{7,4},{8,11},{9,10},{10,... | collective-permute-start | bytes 884744 | tf_op jit(solution)/shard_map/ppermute | solution.py:442
  114.8 14.5 %collective-permute-start.34 = (bf16[192,768]{1,0:T(8,128)(2,1)S(1)}, bf16[192,768]{1,0:T(8,128)(2,1)S(1)}, u32[]{:S(2)}, u32[]{:S(2)}) collective-permute-start(bf16[192,768]{1,0:T(8,128)(2,1)S(1)} %get-tuple-element.213), channel_id=1, source_target_pairs={{0,1},{1,0},{2,3},{3,2},{4,5},{5,4},{6,7},{7,6},{8,9},{9,8},{10,11... | collective-permute-start | bytes 884744 | tf_op jit(solution)/shard_map/ppermute | solution.py:442
  115.3 14.1 %collective-permute-start.35 = (bf16[192,768]{1,0:T(8,128)(2,1)S(1)}, bf16[192,768]{1,0:T(8,128)(2,1)S(1)}, u32[]{:S(2)}, u32[]{:S(2)}) collective-permute-start(bf16[192,768]{1,0:T(8,128)(2,1)S(1)} %get-tuple-element.214), channel_id=1, source_target_pairs={{0,2},{1,3},{2,0},{3,1},{4,6},{5,7},{6,4},{7,5},{8,10},{9,11},{10,... | collective-permute-start | bytes 884744 | tf_op jit(solution)/shard_map/ppermute | solution.py:442
  116.6 14.7 %collective-permute-start.32 = (bf16[394,384]{1,0:T(8,128)(2,1)S(1)}, bf16[394,384]{1,0:T(8,128)(2,1)S(1)}, u32[]{:S(2)}, u32[]{:S(2)}) collective-permute-start(bf16[394,384]{1,0:T(8,128)(2,1)S(1)} %add_convert_fusion.3), channel_id=1, source_target_pairs={{0,16},{8,24},{16,0},{24,8},{1,17},{9,25},{17,1},{25,9},{2,18},{10... | collective-permute-start | bytes 907784 | tf_op jit(solution)/shard_map/ppermute | solution.py:432
  118.2 14.0 %collective-permute-start.29 = (bf16[400,384]{1,0:T(8,128)(2,1)S(1)}, bf16[400,384]{1,0:T(8,128)(2,1)S(1)}, u32[]{:S(2)}, u32[]{:S(2)}) collective-permute-start(bf16[400,384]{1,0:T(8,128)(2,1)S(1)} %add_convert_fusion.5), channel_id=1, source_target_pairs={{0,16},{8,24},{16,0},{24,8},{1,17},{9,25},{17,1},{25,9},{2,18},{10... | collective-permute-start | bytes 921608 | tf_op jit(solution)/shard_map/ppermute | solution.py:432
  129.6 3.5 %copy-start.7 = (f32[768]{0:T(1024)S(1)}, f32[768]{0:T(1024)}, u32[]{:S(2)}) copy-start(f32[768]{0:T(1024)} %gain.7) | copy-start | bytes 9220
  129.6 17.5 %collective-permute-start.37 = (bf16[192,768]{1,0:T(8,128)(2,1)S(1)}, bf16[192,768]{1,0:T(8,128)(2,1)S(1)}, u32[]{:S(2)}, u32[]{:S(2)}) collective-permute-start(bf16[192,768]{1,0:T(8,128)(2,1)S(1)} %shard_map.223.own), channel_id=1, source_target_pairs={{0,4},{2,6},{4,0},{6,2},{1,5},{3,7},{5,1},{7,3},{8,12},{10,14},{12... | collective-permute-start | bytes 884744 | tf_op jit(solution)/shard_map/ppermute | solution.py:435
  131.4 1.7 collective-permute-start.36
  131.5 26.7 %collective-permute-start.39 = (bf16[512,768]{1,0:T(8,128)(2,1)S(1)}, bf16[512,768]{1,0:T(8,128)(2,1)S(1)}, u32[]{:S(2)}, u32[]{:S(2)}) collective-permute-start(bf16[512,768]{1,0:T(8,128)(2,1)S(1)} %get-tuple-element.222), channel_id=1, source_target_pairs={{0,1},{1,0},{2,3},{3,2},{4,5},{5,4},{6,7},{7,6},{8,9},{9,8},{10,11... | collective-permute-start | bytes 2359304 | tf_op jit(solution)/shard_map/ppermute | solution.py:438
  132.3 19.1 %collective-permute-start.30 = (bf16[400,384]{1,0:T(8,128)(2,1)S(1)}, bf16[400,384]{1,0:T(8,128)(2,1)}, u32[]{:S(2)}, u32[]{:S(2)}) collective-permute-start(bf16[400,384]{1,0:T(8,128)(2,1)S(1)} %add_convert_fusion.4), channel_id=1, source_target_pairs={{0,8},{8,0},{16,24},{24,16},{1,9},{9,1},{17,25},{25,17},{2,10},{10... | collective-permute-start | bytes 921608 | tf_op jit(solution)/shard_map/ppermute | solution.py:432
  135.5 12.3 %collective-permute-start.38 = (f32[16,768]{1,0:T(8,128)S(1)}, f32[16,768]{1,0:T(8,128)S(1)}, u32[]{:S(2)}, u32[]{:S(2)}) collective-permute-start(f32[16,768]{1,0:T(8,128)S(1)} %get-tuple-element.218.small), channel_id=1, source_target_pairs={{0,4},{2,6},{4,0},{6,2},{1,5},{3,7},{5,1},{7,3},{8,12},{10,14},{12... | collective-permute-start | bytes 147464 | tf_op jit(solution)/shard_map/ppermute | solution.py:435
  136.7 14.7 %copy-start.3 = (f32[394,768]{1,0:T(8,128)S(1)}, f32[394,768]{1,0:T(8,128)}, u32[]{:S(2)}) copy-start(f32[394,768]{1,0:T(8,128)} %copy-done.2) | copy-start | bytes 3631108
  147.9 10.3 %copy-start.18 = (f32[768,768]{1,0:T(8,128)S(1)}, f32[768,768]{1,0:T(8,128)}, u32[]{:S(2)}) copy-start(f32[768,768]{1,0:T(8,128)} %copy-done.17) | copy-start | bytes 7077892
  147.9 12.0 %collective-permute-start.40 = (bf16[208,768]{1,0:T(8,128)(2,1)S(1)}, bf16[208,768]{1,0:T(8,128)(2,1)S(1)}, u32[]{:S(2)}, u32[]{:S(2)}) collective-permute-start(bf16[208,768]{1,0:T(8,128)(2,1)S(1)} %shard_map.225.refs_0_), channel_id=1, source_target_pairs={{0,3},{1,2},{2,1},{3,0},{4,7},{5,6},{6,5},{7,4},{8,11},{9,10},{10,... | collective-permute-start | bytes 958472 | tf_op jit(solution)/shard_map/ppermute | solution.py:442
  147.9 17.2 %collective-permute-start.41 = (bf16[208,768]{1,0:T(8,128)(2,1)S(1)}, bf16[208,768]{1,0:T(8,128)(2,1)S(1)}, u32[]{:S(2)}, u32[]{:S(2)}) collective-permute-start(bf16[208,768]{1,0:T(8,128)(2,1)S(1)} %shard_map.225.refs_0_), channel_id=1, source_target_pairs={{0,1},{1,0},{2,3},{3,2},{4,5},{5,4},{6,7},{7,6},{8,9},{9,8},{10,11... | collective-permute-start | bytes 958472 | tf_op jit(solution)/shard_map/ppermute | solution.py:442
  148.6 16.5 %collective-permute-start.42 = (bf16[208,768]{1,0:T(8,128)(2,1)S(1)}, bf16[208,768]{1,0:T(8,128)(2,1)S(1)}, u32[]{:S(2)}, u32[]{:S(2)}) collective-permute-start(bf16[208,768]{1,0:T(8,128)(2,1)S(1)} %shard_map.225.refs_0_), channel_id=1, source_target_pairs={{0,2},{1,3},{2,0},{3,1},{4,6},{5,7},{6,4},{7,5},{8,10},{9,11},{10,... | collective-permute-start | bytes 958472 | tf_op jit(solution)/shard_map/ppermute | solution.py:442
